TPU v7x, 32 devices: a whole 2x2x4 slice. The times are simulated.
32 devices in a mesh: dp: 8 (over y, x, core), mp: 4 (over z).
Axes of the slice: x: 2, y: 2, z: 4, core: 2. Of those that a mesh axis runs over, the one named last changes fastest.
Arguments:
- patches: bfloat16 [256, 256, 1152], P('dp', 'mp'), may hold values from -6 to 6
- cotangent: bfloat16 [128, 256, 1152], P('dp', 'mp'), may hold values from -6 to 6
- time_bins: int32 [256], P('dp'), may hold values from 0 to 15
- labels: int32 [256], P('dp'), may hold values from 0 to 999
- image_counts: int32 [8], replicated, may hold values from 1 to 32, 128 in all
- dest_perm: int32 [8], replicated, may hold values from 0 to 7, each once
- time_table: bfloat16 [16, 1152], replicated, may hold values from -4 to 4
- class_table: bfloat16 [1000, 1152], replicated, may hold values from -4 to 4
- ada_weight: bfloat16 [1152, 6, 1152], replicated, may hold values from -0.09375 to 0.09375
- qkv_weight: bfloat16 [1152, 3, 1152], P(None, None, 'mp'), may hold values from -0.1875 to 0.1875
- norm_gains: bfloat16 [2, 72], replicated, may hold values from 0.59765625 to 1.59375
- out_weight: bfloat16 [1152, 1152], P('mp'), may hold values from -0.75 to 0.75
- expand_weight: bfloat16 [1152, 2, 3072], P(None, None, 'mp'), may hold values from -0.1875 to 0.1875
- down_weight: bfloat16 [3072, 1152], P('mp'), may hold values from -0.109375 to 0.109375
Outputs:
- result: bfloat16 [128, 256, 1152], P('dp', 'mp')
- patch_grad: bfloat16 [256, 256, 1152], P('dp', 'mp')
- time_grad: float32 [16, 1152], P(None, 'dp')
- class_grad: float32 [1000, 1152], P(None, 'dp')
- ada_grad: float32 [1152, 6, 1152], P('dp', None, 'mp')
- qkv_grad: float32 [1152, 3, 1152], P('dp', None, 'mp')
- gains_grad: float32 [2, 72], replicated
- out_grad: float32 [1152, 1152], P('mp', 'dp')
- expand_grad: float32 [1152, 2, 3072], P('dp', None, 'mp')
- down_grad: float32 [3072, 1152], P('mp', 'dp')
Inputs may be any that keep to these rules, and one draw needn't show every extreme that they name: `image_counts`: entry s counts the live slots of dp index s, which are its first ones; the entries sum to 128, and one index has all 32 slots live. `dest_perm`: each dp index appears once.
All inputs are finite; a program needn't handle non-finite values.
Results may differ from a plain program's by a relative error of at most 0.02.
Values may be sent and summed in bfloat16 or wider, within the bound.
No kernel may reach another device: no remote copies, remote signals or barrier semaphores. Data moves between devices by JAX's collectives and lax.ppermute only.
A program may use at most 320 MiB of HBM per device.

v0:
```python
import jax
import jax.numpy as jnp
from jax import lax
from jax.sharding import PartitionSpec as P

HD = 72
GRID = 16
NCLS = 1000
NBINS = 16


epsilon = 1e-06
rope_base = 10000.0


def rms_scale(values, scaling, shifting):
    return (
        values * lax.rsqrt(jnp.mean(values * values, -1, keepdims=True) + epsilon) * (1.0 + scaling)
        + shifting
    )


def head_norm(values):
    return values * lax.rsqrt(jnp.mean(values * values, -1, keepdims=True) + epsilon)


def rope_tables(length):
    quarter = HD // 4
    position = jnp.arange(length)
    row_pos = (position // GRID).astype(jnp.float32)
    col_pos = (position % GRID).astype(jnp.float32)
    frequency = rope_base ** (-jnp.arange(quarter).astype(jnp.float32) / quarter)
    row_angle = row_pos[:, None] * frequency[None, :]
    col_angle = col_pos[:, None] * frequency[None, :]
    return (jnp.cos(row_angle), jnp.sin(row_angle), jnp.cos(col_angle), jnp.sin(col_angle))


def rotate(half_vec, cosine_tab, sine_tab):
    quarter = cosine_tab.shape[1]
    front_part = half_vec[..., :quarter]
    back_part = half_vec[..., quarter:]
    cosine_tab = cosine_tab[None, :, None, :]
    sine_tab = sine_tab[None, :, None, :]
    return jnp.concatenate(
        [
            front_part * cosine_tab - back_part * sine_tab,
            front_part * sine_tab + back_part * cosine_tab,
        ],
        -1,
    )


def apply_rope(values, tables):
    halfway = values.shape[-1] // 2
    return jnp.concatenate(
        [
            rotate(values[..., :halfway], tables[0], tables[1]),
            rotate(values[..., halfway:], tables[2], tables[3]),
        ],
        -1,
    )


def prepare(queries, key_vecs, gains, tables):
    query_pre = apply_rope(head_norm(queries) * gains[0], tables) * HD ** (-0.5)
    key_pre = apply_rope(head_norm(key_vecs) * gains[1], tables)
    return (query_pre, key_pre)


def swish_mul(gate_part, up_part):
    return jax.nn.silu(gate_part) * up_part


def project(normed_full, qkv_weight, heads_loc, head_dim):
    images, length, model_width = normed_full.shape
    projected = jnp.dot(
        normed_full.reshape(-1, model_width),
        qkv_weight.reshape(model_width, -1),
        preferred_element_type=jnp.float32,
    )
    projected = projected.reshape(images, length, 3, heads_loc, head_dim)
    return (projected[:, :, 0], projected[:, :, 1], projected[:, :, 2])


def attend(query_low, key_low, value_low):
    scores = jnp.einsum("iqhe,ikhe->ihqk", query_low, key_low, preferred_element_type=jnp.float32)
    attn_probs = jax.nn.softmax(scores, axis=-1)
    probs_low = attn_probs.astype(jnp.bfloat16)
    attended = jnp.einsum(
        "ihqk,ikhe->iqhe", probs_low, value_low, preferred_element_type=jnp.float32
    ).astype(jnp.bfloat16)
    return (attn_probs, probs_low, attended)


def shards(
    patches,
    cotangent,
    time_bins,
    labels,
    image_counts,
    dest_perm,
    time_table,
    class_table,
    ada_weight,
    qkv_weight,
    norm_gains,
    out_weight,
    expand_weight,
    down_weight,
):
    dp_size = lax.axis_size("dp")
    mp_size = lax.axis_size("mp")
    capacity = patches.shape[0]
    slot_count = capacity // dp_size
    images = cotangent.shape[0]
    local_len = patches.shape[1]
    model_width = patches.shape[2]
    length = local_len * mp_size
    head_dim = norm_gains.shape[1]
    local_dim = out_weight.shape[0]
    heads_loc = local_dim // head_dim
    unit_count = down_weight.shape[0]
    gains_f = norm_gains.astype(jnp.float32)
    tables = rope_tables(length)
    dp_index = lax.axis_index("dp")
    starts = jnp.cumsum(image_counts) - image_counts
    finish = starts + image_counts
    my_start = starts[dp_index]
    my_count = image_counts[dp_index]
    device_ids = jnp.arange(dp_size)
    matches = (dest_perm[:, None] == device_ids[None, :]).astype(jnp.int32)
    inverse = jnp.sum(device_ids[:, None] * matches, axis=0)
    my_place = inverse[dp_index]
    pair_ids = jnp.arange(dp_size * slot_count)
    pair_peer = pair_ids // slot_count
    pair_slot = pair_ids % slot_count
    send_index = pair_slot * dp_size + jnp.mod(inverse[pair_peer] - my_start, dp_size)
    send_valid = send_index < my_count
    send_index = jnp.minimum(send_index, capacity - 1)
    slot_ids = jnp.arange(capacity)
    slot_live = slot_ids < my_count
    bin_hot = (time_bins[:, None] == jnp.arange(NBINS)[None, :]).astype(jnp.bfloat16)
    label_hot = (labels[:, None] == jnp.arange(NCLS)[None, :]).astype(jnp.bfloat16)
    cond_src = (
        jnp.dot(bin_hot, time_table, preferred_element_type=jnp.float32)
        + jnp.dot(label_hot, class_table, preferred_element_type=jnp.float32)
    ).astype(jnp.bfloat16)
    local_hist = jnp.sum(
        bin_hot.astype(jnp.float32) * slot_live[:, None].astype(jnp.float32), axis=0
    )
    send_patches = jnp.where(send_valid[:, None, None], jnp.take(patches, send_index, axis=0), 0)
    send_cond = jnp.where(send_valid[:, None], jnp.take(cond_src, send_index, axis=0), 0)
    send_bins = jnp.where(send_valid, jnp.take(time_bins, send_index), 0).astype(jnp.bfloat16)
    bin_totals = lax.psum(local_hist, "dp")
    recv_patches, recv_cond, recv_bins = (
        lax.all_to_all(send_patches, "dp", split_axis=0, concat_axis=0, tiled=True),
        lax.all_to_all(send_cond, "dp", split_axis=0, concat_axis=0, tiled=True),
        lax.all_to_all(send_bins, "dp", split_axis=0, concat_axis=0, tiled=True),
    )
    rank_ids = jnp.arange(images) * dp_size + my_place
    source = jnp.sum((finish[None, :] <= rank_ids[:, None]).astype(jnp.int32), axis=1)
    within = rank_ids - starts[source]
    recv_index = source * slot_count + within // dp_size
    latent = jnp.take(recv_patches, recv_index, axis=0)
    cond_low = jnp.take(recv_cond, recv_index, axis=0)
    bal_bins = jnp.take(recv_bins, recv_index).astype(jnp.int32)
    bin_match = (bal_bins[:, None] == jnp.arange(NBINS)[None, :]).astype(jnp.float32)
    weights = dp_size * images / (NBINS * jnp.sum(bin_match * bin_totals[None, :], axis=1))
    condition = cond_low.astype(jnp.float32)
    silu_cond = jax.nn.silu(condition).astype(jnp.bfloat16)
    modulation = jnp.dot(
        silu_cond,
        ada_weight.reshape(model_width, 6 * model_width),
        preferred_element_type=jnp.float32,
    )
    modulation = modulation.reshape(images, 6, 1, model_width)
    shift_one = modulation[:, 0]
    scale_one = modulation[:, 1]
    gate_one = modulation[:, 2]
    shift_two = modulation[:, 3]
    scale_two = modulation[:, 4]
    gate_two = modulation[:, 5]
    latent_f = latent.astype(jnp.float32)
    out_cot = cotangent.astype(jnp.float32) * weights[:, None, None]
    normed = rms_scale(latent_f, scale_one, shift_one).astype(jnp.bfloat16)
    normed_full = lax.all_gather(normed, "mp", axis=1, tiled=True)
    queries, key_vecs, values_raw = project(normed_full, qkv_weight, heads_loc, head_dim)
    query_pre, key_pre = prepare(queries, key_vecs, gains_f, tables)
    attn_probs, probs_low, attended = attend(
        query_pre.astype(jnp.bfloat16),
        key_pre.astype(jnp.bfloat16),
        values_raw.astype(jnp.bfloat16),
    )
    branch_part = jnp.dot(
        attended.reshape(-1, local_dim), out_weight, preferred_element_type=jnp.float32
    ).reshape(images, length, model_width)
    branch_one = lax.psum_scatter(
        branch_part.astype(jnp.bfloat16), "mp", scatter_dimension=1, tiled=True
    ).astype(jnp.float32)
    middle = latent_f + gate_one * branch_one
    normed_two = rms_scale(middle, scale_two, shift_two).astype(jnp.bfloat16)
    normed_two_full = lax.all_gather(normed_two, "mp", axis=1, tiled=True)
    expand_flat = expand_weight.reshape(model_width, 2 * unit_count)
    expanded = jnp.dot(
        normed_two_full.reshape(-1, model_width), expand_flat, preferred_element_type=jnp.float32
    ).reshape(-1, 2, unit_count)
    hidden = swish_mul(expanded[:, 0], expanded[:, 1]).astype(jnp.bfloat16)
    down_part = jnp.dot(hidden, down_weight, preferred_element_type=jnp.float32).reshape(
        images, length, model_width
    )
    branch_two = lax.psum_scatter(
        down_part.astype(jnp.bfloat16), "mp", scatter_dimension=1, tiled=True
    ).astype(jnp.float32)
    result = (middle + gate_two * branch_two).astype(jnp.bfloat16)
    normed_two_full, normed_full = (
        lax.all_gather(normed_two, "mp", axis=1, tiled=True),
        lax.all_gather(normed, "mp", axis=1, tiled=True),
    )
    down_low = (gate_two * out_cot).astype(jnp.bfloat16)
    gate_two_grad = jnp.sum(out_cot * branch_two, axis=1)
    down_full = lax.all_gather(down_low, "mp", axis=1, tiled=True).reshape(-1, model_width)
    two_flat = normed_two_full.reshape(-1, model_width)
    expanded = jnp.dot(two_flat, expand_flat, preferred_element_type=jnp.float32).reshape(
        -1, 2, unit_count
    )
    swish_val, swish_pull = jax.vjp(swish_mul, expanded[:, 0], expanded[:, 1])
    hidden = swish_val.astype(jnp.bfloat16)
    down_term = jnp.einsum("nf,nd->fd", hidden, down_full, preferred_element_type=jnp.float32)
    hidden_grad = jnp.einsum(
        "nd,fd->nf", down_full, down_weight, preferred_element_type=jnp.float32
    )
    gate_grad, up_grad = swish_pull(hidden_grad)
    expand_low = jnp.stack([gate_grad, up_grad], 1).astype(jnp.bfloat16).reshape(-1, 2 * unit_count)
    expand_term = jnp.einsum(
        "nd,nf->df", two_flat, expand_low, preferred_element_type=jnp.float32
    ).reshape(model_width, 2, unit_count)
    two_part = jnp.einsum(
        "nf,df->nd", expand_low, expand_flat, preferred_element_type=jnp.float32
    ).reshape(images, length, model_width)
    normed_two_grad = lax.psum_scatter(
        two_part.astype(jnp.bfloat16), "mp", scatter_dimension=1, tiled=True
    ).astype(jnp.float32)
    norm_val, norm_pull = jax.vjp(rms_scale, middle, scale_two, shift_two)
    middle_grad, scale_two_grad, shift_two_grad = norm_pull(normed_two_grad)
    middle_grad = middle_grad + out_cot
    gate_one_grad = jnp.sum(middle_grad * branch_one, axis=1)
    branch_low = (gate_one * middle_grad).astype(jnp.bfloat16)
    branch_full = lax.all_gather(branch_low, "mp", axis=1, tiled=True).reshape(-1, model_width)
    queries, key_vecs, values_raw = project(normed_full, qkv_weight, heads_loc, head_dim)

    def prepped(query_in, key_in, gains_in):
        return prepare(query_in, key_in, gains_in, tables)

    pre_vals, prep_pull = jax.vjp(prepped, queries, key_vecs, gains_f)
    query_low = pre_vals[0].astype(jnp.bfloat16)
    key_low = pre_vals[1].astype(jnp.bfloat16)
    value_low = values_raw.astype(jnp.bfloat16)
    attn_probs, probs_low, attended = attend(query_low, key_low, value_low)
    out_term = jnp.einsum(
        "nc,nd->cd",
        attended.reshape(-1, local_dim),
        branch_full,
        preferred_element_type=jnp.float32,
    )
    attended_low = jnp.einsum(
        "nd,cd->nc", branch_full, out_weight, preferred_element_type=jnp.float32
    ).astype(jnp.bfloat16)
    attended_low = attended_low.reshape(images, length, heads_loc, head_dim)
    prob_grad = jnp.einsum(
        "iqhe,ikhe->ihqk", attended_low, value_low, preferred_element_type=jnp.float32
    )
    value_grad = jnp.einsum(
        "ihqk,iqhe->ikhe", probs_low, attended_low, preferred_element_type=jnp.float32
    )
    score_low = (
        attn_probs * (prob_grad - jnp.sum(attn_probs * prob_grad, -1, keepdims=True))
    ).astype(jnp.bfloat16)
    query_grad = jnp.einsum(
        "ihqk,ikhe->iqhe", score_low, key_low, preferred_element_type=jnp.float32
    )
    key_grad = jnp.einsum(
        "ihqk,iqhe->ikhe", score_low, query_low, preferred_element_type=jnp.float32
    )
    queries_grad, keys_grad, gains_grad = prep_pull((query_grad, key_grad))
    projected_low = (
        jnp.stack([queries_grad, keys_grad, value_grad], 2)
        .astype(jnp.bfloat16)
        .reshape(-1, 3 * local_dim)
    )
    qkv_flat = qkv_weight.reshape(model_width, 3 * local_dim)
    qkv_term = jnp.einsum(
        "nd,nc->dc",
        normed_full.reshape(-1, model_width),
        projected_low,
        preferred_element_type=jnp.float32,
    )
    qkv_term = qkv_term.reshape(model_width, 3, local_dim)
    normed_part = jnp.einsum(
        "nc,dc->nd", projected_low, qkv_flat, preferred_element_type=jnp.float32
    ).reshape(images, length, model_width)
    normed_grad = lax.psum_scatter(
        normed_part.astype(jnp.bfloat16), "mp", scatter_dimension=1, tiled=True
    ).astype(jnp.float32)
    norm_val, norm_pull = jax.vjp(rms_scale, latent_f, scale_one, shift_one)
    latent_grad, scale_one_grad, shift_one_grad = norm_pull(normed_grad)
    latent_grad = latent_grad + middle_grad
    modulation_grad = jnp.stack(
        [
            shift_one_grad[:, 0],
            scale_one_grad[:, 0],
            gate_one_grad,
            shift_two_grad[:, 0],
            scale_two_grad[:, 0],
            gate_two_grad,
        ],
        1,
    )
    modulation_grad, gains_grad = (
        lax.psum(modulation_grad.astype(jnp.bfloat16), "mp").astype(jnp.float32),
        lax.psum(gains_grad.astype(jnp.bfloat16), "mp").astype(jnp.float32),
    )
    modulation_low = modulation_grad.astype(jnp.bfloat16)
    column_block = lax.dynamic_slice_in_dim(
        modulation_low, lax.axis_index("mp") * local_dim, local_dim, 2
    )
    ada_term = jnp.einsum(
        "id,ikc->dkc", silu_cond, column_block, preferred_element_type=jnp.float32
    )
    silu_grad = jnp.einsum(
        "ie,de->id",
        modulation_low.reshape(images, 6 * model_width),
        ada_weight.reshape(model_width, 6 * model_width),
        preferred_element_type=jnp.float32,
    )
    silu_val, silu_pull = jax.vjp(jax.nn.silu, condition)
    condition_low = silu_pull(silu_grad)[0].astype(jnp.bfloat16)
    back_within = pair_slot * dp_size + jnp.mod(my_place - starts[pair_peer], dp_size)
    back_valid = back_within < image_counts[pair_peer]
    back_slot = jnp.clip((starts[pair_peer] + back_within - my_place) // dp_size, 0, images - 1)
    back_patches = jnp.where(
        back_valid[:, None, None], jnp.take(latent_grad.astype(jnp.bfloat16), back_slot, axis=0), 0
    )
    back_cond = jnp.where(back_valid[:, None], jnp.take(condition_low, back_slot, axis=0), 0)
    got_patches, got_cond = (
        lax.all_to_all(back_patches, "dp", split_axis=0, concat_axis=0, tiled=True),
        lax.all_to_all(back_cond, "dp", split_axis=0, concat_axis=0, tiled=True),
    )
    home_peer = dest_perm[jnp.mod(my_start + slot_ids, dp_size)]
    home_index = home_peer * slot_count + jnp.minimum(slot_ids // dp_size, slot_count - 1)
    patch_grad = jnp.where(slot_live[:, None, None], jnp.take(got_patches, home_index, axis=0), 0)
    cond_home = jnp.where(slot_live[:, None], jnp.take(got_cond, home_index, axis=0), 0)
    time_term = jnp.einsum("cn,cd->nd", bin_hot, cond_home, preferred_element_type=jnp.float32)
    class_term = jnp.einsum("cn,cd->nd", label_hot, cond_home, preferred_element_type=jnp.float32)
    gains_tiled = jnp.broadcast_to(gains_grad[None], (dp_size,) + gains_grad.shape)
    summed = (
        lax.psum_scatter(
            ada_term.astype(jnp.bfloat16), "dp", scatter_dimension=0, tiled=True
        ).astype(jnp.float32),
        lax.psum_scatter(
            qkv_term.astype(jnp.bfloat16), "dp", scatter_dimension=0, tiled=True
        ).astype(jnp.float32),
        lax.psum_scatter(
            out_term.astype(jnp.bfloat16), "dp", scatter_dimension=1, tiled=True
        ).astype(jnp.float32),
        lax.psum_scatter(
            expand_term.astype(jnp.bfloat16), "dp", scatter_dimension=0, tiled=True
        ).astype(jnp.float32),
        lax.psum_scatter(
            down_term.astype(jnp.bfloat16), "dp", scatter_dimension=1, tiled=True
        ).astype(jnp.float32),
        lax.psum_scatter(
            time_term.astype(jnp.bfloat16), "dp", scatter_dimension=1, tiled=True
        ).astype(jnp.float32),
        lax.psum_scatter(
            class_term.astype(jnp.bfloat16), "dp", scatter_dimension=1, tiled=True
        ).astype(jnp.float32),
        lax.psum_scatter(
            gains_tiled.astype(jnp.bfloat16), "dp", scatter_dimension=0, tiled=True
        ).astype(jnp.float32),
    )
    return (
        result,
        patch_grad,
        summed[5],
        summed[6],
        summed[0],
        summed[1],
        summed[7][0],
        summed[2],
        summed[3],
        summed[4],
    )


def solution(mesh):
    in_specs = (
        P("dp", "mp", None),
        P("dp", "mp", None),
        P("dp"),
        P("dp"),
        P(),
        P(),
        P(),
        P(),
        P(),
        P(None, None, "mp"),
        P(),
        P("mp", None),
        P(None, None, "mp"),
        P("mp", None),
    )
    out_specs = (
        P("dp", "mp", None),
        P("dp", "mp", None),
        P(None, "dp"),
        P(None, "dp"),
        P("dp", None, "mp"),
        P("dp", None, "mp"),
        P(),
        P("mp", "dp"),
        P("dp", None, "mp"),
        P("mp", "dp"),
    )
    return jax.shard_map(shards, mesh=mesh, in_specs=in_specs, out_specs=out_specs, check_vma=False)
```

profile of v0, /device:TPU:0, one launch (start us, length us, event | category | flops | bytes accessed | tf_op | source)
XLA Modules:
  0.0 2108.7 jit_solution(4763114407027833764)
XLA Ops:
  17.1 5.2 all-to-all-start.2
  26.6 5.6 gather_fusion.11
  36.4 5.2 select_select_fusion.1
  41.6 4.6 all-to-all-start
  48.2 22.4 %copy.99 = bf16[1152,6,1152]{0,2,1:T(8,128)(2,1)} copy(bf16[1152,6,1152]{2,0,1:T(8,128)(2,1)} %param.26) | data formatting | bytes 31850496 | tf_op args[8]
  73.2 9.8 fusion.48
  83.1 17.9 all-to-all-done
  108.1 165.7 %all-gather.5.cloned.1.call-done = bf16[16,256,1152]{2,1,0:T(8,128)(2,1)} async-done(((bf16[16,64,1152]{2,1,0:T(8,128)(2,1)}), bf16[16,256,1152]{2,1,0:T(8,128)(2,1)}) %all-gather.5.cloned.1.call-update) | async-done | bytes 9437200 | tf_op jit(solution)/shard_map/all_gather | solution.py:186
  273.9 15.5 fusion.13
  289.3 5.3 multiply_reduce_fusion.6
  295.3 5.4 multiply_multiply_fusion
  307.0 11.6 fusion.144
  318.6 8.8 fusion.59
  328.8 7.8 convolution_convert_fusion.3
  336.7 159.6 %reduce-scatter.14.cloned.1.call-done = bf16[16,64,1152]{2,1,0:T(8,128)(2,1)} async-done(((bf16[16,256,1152]{2,1,0:T(8,128)(2,1)}), bf16[16,64,1152]{2,1,0:T(8,128)(2,1)}) %reduce-scatter.14.cloned.1.call-update) | async-done | bytes 2359312 | tf_op jit(solution)/shard_map/reduce_scatter | solution.py:197
  502.8 13.2 psum.21
  520.3 9.1 reshape.1189
  529.3 4.5 copy.140
  533.8 5.8 copy.132
  539.6 130.1 %all-gather.7.cloned.1.call-done = bf16[16,256,1152]{2,1,0:T(8,128)(2,1)} async-done(((bf16[16,64,1152]{2,1,0:T(8,128)(2,1)}), bf16[16,256,1152]{2,1,0:T(8,128)(2,1)}) %all-gather.7.cloned.1.call-update) | async-done | bytes 9437200 | tf_op jit(solution)/shard_map/all_gather | solution.py:202
  669.8 23.5 %fusion.148 = f32[4096,2,768]{2,0,1:T(8,128)} fusion(bf16[4096,1152,1]{1,0,2:T(8,128)(2,1)} %bitcast.285, bf16[2,768,1152]{2,1,0:T(8,128)(2,1)} %bitcast.273), kind=kOutput, calls=%fused_computation.374 | convolution fusion | flops 14495514624 | bytes 38141952 | tf_op jit(solution)/shard_map/dot_general | solution.py:204
  693.3 142.9 %all-gather.9.cloned.1.call-done = bf16[16,256,1152]{2,1,0:T(8,128)(2,1)} async-done(((bf16[16,64,1152]{2,1,0:T(8,128)(2,1)}), bf16[16,256,1152]{2,1,0:T(8,128)(2,1)}) %all-gather.9.cloned.1.call-update) | async-done | bytes 9437200 | tf_op jit(solution)/shard_map/all_gather | solution.py:221
  836.2 23.8 %fusion.5 = (bf16[4096,1,768]{2,0,1:T(8,128)(2,1)}, bf16[4096,1,768]{2,0,1:T(8,128)(2,1)}) fusion(f32[4096,2,768]{2,0,1:T(8,128)} %fusion.148, bf16[4096,1152]{1,0:T(8,128)(2,1)} %bitcast.287, bf16[768,1152]{1,0:T(8,128)(2,1)} %param.31), kind=kOutput, calls=%fused_computation.30 | convolution fusion | flops 7291797504 | bytes 48955392 | tf_op jit(solution)/shard_map/nd,fd->nf/dot_general | solution.py:229
  860.0 10.7 maximum_convert_fusion
  870.7 23.8 %copy.133 = bf16[4096,2,768]{2,1,0:T(2,128)(2,1)} copy(bf16[4096,2,768]{2,0,1:T(8,128)(2,1)} %maximum_convert_fusion) | data formatting | bytes 25165824 | tf_op jit(solution)/shard_map/convert_element_type | solution.py:233
  894.5 27.3 %reshape.1194 = bf16[16,256,1536]{2,1,0:T(8,128)(2,1)} reshape(bf16[4096,2,768]{2,1,0:T(2,128)(2,1)} %copy.133) | data formatting | bytes 25165824 | tf_op jit(solution)/shard_map/convert_element_type | solution.py:233
  921.8 22.7 %convolution_convert_fusion.1 = bf16[16,256,1152]{2,1,0:T(8,128)(2,1)} fusion(bf16[16,256,1536]{2,1,0:T(8,128)(2,1)} %reshape.1194, bf16[1152,1536,1]{1,0,2:T(8,128)(2,1)} %reshape.1189), kind=kOutput, calls=%fused_computation.25 | convolution fusion | flops 14500233216 | bytes 25559040 | tf_op jit(solution)/shard_map/nf,df->nd/dot_general | solution.py:237
  944.6 159.6 %reduce-scatter.18.cloned.1.call-done = bf16[16,64,1152]{2,1,0:T(8,128)(2,1)} async-done(((bf16[16,256,1152]{2,1,0:T(8,128)(2,1)}), bf16[16,64,1152]{2,1,0:T(8,128)(2,1)}) %reduce-scatter.18.cloned.1.call-update) | async-done | bytes 2359312 | tf_op jit(solution)/shard_map/reduce_scatter | solution.py:240
  1112.5 167.7 %all-gather.11.cloned.1.call-done = bf16[16,256,1152]{2,1,0:T(8,128)(2,1)} async-done(((bf16[16,64,1152]{2,1,0:T(8,128)(2,1)}), bf16[16,256,1152]{2,1,0:T(8,128)(2,1)}) %all-gather.11.cloned.1.call-update) | async-done | bytes 9437200 | tf_op jit(solution)/shard_map/all_gather | solution.py:248
  1280.2 10.2 convolution_convert_fusion.5
  1291.3 10.5 fusion.52
  1301.7 13.7 multiply_reduce_fusion
  1315.4 16.0 multiply_convert_fusion
  1331.5 9.2 convolution_bitcast_fusion
  1340.7 6.0 multiply_bitcast_fusion
  1351.7 6.9 multiply_reduce_fusion.2
  1358.7 6.3 fusion.31
  1368.7 14.7 convolution_convert_fusion
  1383.5 18.1 fusion.143
  1401.6 17.2 convolution_convert_fusion.2
  1421.2 121.9 %reduce-scatter.20.cloned.1.call-done = bf16[16,64,1152]{2,1,0:T(8,128)(2,1)} async-done(((bf16[16,256,1152]{2,1,0:T(8,128)(2,1)}), bf16[16,64,1152]{2,1,0:T(8,128)(2,1)}) %reduce-scatter.20.cloned.1.call-update) | async-done | bytes 2359312 | tf_op jit(solution)/shard_map/reduce_scatter | solution.py:301
  1545.2 162.4 %reduce-scatter.16.cloned.1.call-done = bf16[16,64,1152]{2,1,0:T(8,128)(2,1)} async-done(((bf16[16,256,1152]{2,1,0:T(8,128)(2,1)}), bf16[16,64,1152]{2,1,0:T(8,128)(2,1)}) %reduce-scatter.16.cloned.1.call-update) | async-done | bytes 2359312 | tf_op jit(solution)/shard_map/reduce_scatter | solution.py:211
  1707.7 11.3 fusion.28
  1719.8 19.6 fusion.45
  1739.5 16.5 copy.110
  1756.0 21.5 %fusion.38 = bf16[1152,2,768]{2,0,1:T(8,128)(2,1)} fusion(bf16[4096,1152,1]{1,0,2:T(8,128)(2,1)} %bitcast.286, bf16[4096,2,768]{0,2,1:T(8,128)(2,1)} %copy.110), kind=kOutput, calls=%fused_computation.110 | convolution fusion | flops 14497284096 | bytes 25559040 | tf_op jit(solution)/shard_map/nd,nf->df/dot_general | solution.py:234
  1782.2 7.1 copy.118
  1789.3 7.6 copy.142
  1796.8 8.9 convolution_convert_fusion.8
  1805.8 18.2 convolution_convert_fusion.6
  1828.0 10.0 fusion.74
  1843.7 5.3 all-to-all-done.4
  1854.5 7.7 fusion.34
  1862.1 4.9 gather_fusion.8
  1867.1 5.0 convolution_convert_fusion.4
  1872.0 5.2 select_select_fusion.2
  1877.3 4.7 all-to-all-start.3
  1886.6 11.4 psum.23
  1898.0 53.4 %all-reduce.14 = bf16[8,2,72]{2,1,0:T(2,128)(2,1)S(1)} all-reduce(bf16[8,2,72]{2,1,0:T(2,128)(2,1)S(1)} %broadcast_in_dim.225), channel_id=10, replica_groups=mesh['dp'=8,'mp'=4] {'dp'}, use_global_device_ids=true, to_apply=%region_35.38.clone | all-reduce | flops 1152 | bytes 4608
  1958.2 34.8 %reduce-scatter.34.cloned.1.call-done = bf16[144,16]{1,0:T(8,128)(2,1)} async-done(((bf16[1152,16]{1,0:T(8,128)(2,1)}), bf16[144,16]{1,0:T(8,128)(2,1)}) %reduce-scatter.34.cloned.1.call-update) | async-done | bytes 4624
  1994.5 44.6 %reduce-scatter.22.cloned.1.call-done = bf16[1000,144]{0,1:T(8,128)(2,1)} async-done(((bf16[1000,1152]{0,1:T(8,128)(2,1)}), bf16[1000,144]{0,1:T(8,128)(2,1)}) %reduce-scatter.22.cloned.1.call-update) | async-done | bytes 288016 | tf_op jit(solution)/shard_map/reduce_scatter | solution.py:374
  2040.9 5.7 gather_fusion.13
  2046.6 5.7 select_select_fusion
  2052.3 47.4 %reduce-scatter.24.cloned.1.call-done = bf16[144,6,288]{2,0,1:T(8,128)(2,1)} async-done(((bf16[1152,6,288]{2,0,1:T(8,128)(2,1)}), bf16[144,6,288]{2,0,1:T(8,128)(2,1)}) %reduce-scatter.24.cloned.1.call-update) | async-done | bytes 497680 | tf_op jit(solution)/shard_map/reduce_scatter | solution.py:356
  (312 shorter events, 108.6 us)
Async XLA Ops:
  7.2 16.8 copy-start
  10.1 37.4 %copy-start.2 = (s32[8]{0:T(128)}, s32[8]{0:T(128)S(1)}, u32[]{:S(2)}) copy-start(s32[8]{0:T(128)S(1)} %bitcast_subtract_fusion.2) | copy-start | bytes 100
  17.1 15.1 all-to-all-start.2
  32.2 9.4 all-to-all-start.1
  41.6 59.4 %all-to-all-start = ((bf16[32,64,1152]{2,1,0:T(8,128)(2,1)}), bf16[32,64,1152]{2,1,0:T(8,128)(2,1)}, u32[]{:S(2)}, u32[]{:S(2)}) async-start(bf16[32,64,1152]{2,1,0:T(8,128)(2,1)} %select_select_fusion.1), calls=%async_computation | async-start | bytes 9437184 | tf_op jit(solution)/shard_map/all_to_all | solution.py:156
  46.2 227.6 %all-gather.5.cloned.1.call-start = ((), (), s32[]{:S(2)}) async-start(), calls=%async_computation.16 | async-start | bytes 11796480 | tf_op jit(solution)/shard_map/all_gather | solution.py:186
  72.5 1035.7 %copy-start.54 = (pred[16]{0:T(512)(128)(4,1)}, pred[16]{0:T(512)(128)(4,1)S(1)}, u32[]{:S(2)}) copy-start(pred[16]{0:T(512)(128)(4,1)S(1)} %get-tuple-element.82) | copy-start | bytes 52
  73.2 9.8 copy-start.41
  83.0 24.5 %copy-start.25 = (f32[16,1152]{1,0:T(8,128)}, f32[16,1152]{1,0:T(8,128)S(1)}, u32[]{:S(2)}) copy-start(f32[16,1152]{1,0:T(8,128)S(1)} %get-tuple-element.126) | copy-start | bytes 221188
  83.1 433.2 %copy-start.31 = (f32[16,1152]{1,0:T(8,128)}, f32[16,1152]{1,0:T(8,128)S(1)}, u32[]{:S(2)}) copy-start(f32[16,1152]{1,0:T(8,128)S(1)} %get-tuple-element.122) | copy-start | bytes 221188
  83.1 1025.2 %copy-start.18 = (f32[16,1152]{1,0:T(8,128)}, f32[16,1152]{1,0:T(8,128)S(1)}, u32[]{:S(2)}) copy-start(f32[16,1152]{1,0:T(8,128)S(1)} %get-tuple-element.127) | copy-start | bytes 221188
  83.1 1025.2 %copy-start.21 = (f32[16,1152]{1,0:T(8,128)}, f32[16,1152]{1,0:T(8,128)S(1)}, u32[]{:S(2)}) copy-start(f32[16,1152]{1,0:T(8,128)S(1)} %get-tuple-element.124) | copy-start | bytes 221188
  104.2 1004.1 %copy-start.8 = (bf16[16,64,1152]{2,1,0:T(8,128)(2,1)}, bf16[16,64,1152]{2,1,0:T(8,128)(2,1)S(1)}, u32[]{:S(2)}) copy-start(bf16[16,64,1152]{2,1,0:T(8,128)(2,1)S(1)} %gather_fusion.2) | copy-start | bytes 7077892
  107.5 388.7 %reduce-scatter.14.cloned.1.call-start = ((), (), s32[]{:S(2)}) async-start(), calls=%async_computation.17 | async-start | bytes 11796480 | tf_op jit(solution)/shard_map/reduce_scatter | solution.py:197
  107.8 187.5 %copy-start.60 = (f32[72]{0:T(128)}, f32[72]{0:T(128)S(1)}, u32[]{:S(2)}) copy-start(f32[72]{0:T(128)S(1)} %get-tuple-element.134) | copy-start | bytes 868
  107.8 187.5 %copy-start.62 = (f32[72]{0:T(128)}, f32[72]{0:T(128)S(1)}, u32[]{:S(2)}) copy-start(f32[72]{0:T(128)S(1)} %get-tuple-element.135) | copy-start | bytes 868
  108.1 195.5 %copy-start.33 = (f32[256,18]{0,1:T(8,128)}, f32[256,18]{0,1:T(8,128)S(1)}, u32[]{:S(2)}) copy-start(f32[256,18]{0,1:T(8,128)S(1)} %get-tuple-element.130) | copy-start | bytes 55300
  108.1 195.5 %copy-start.35 = (f32[256,18]{0,1:T(8,128)}, f32[256,18]{0,1:T(8,128)S(1)}, u32[]{:S(2)}) copy-start(f32[256,18]{0,1:T(8,128)S(1)} %get-tuple-element.131) | copy-start | bytes 55300
  108.1 195.5 %copy-start.37 = (f32[256,18]{0,1:T(8,128)}, f32[256,18]{0,1:T(8,128)S(1)}, u32[]{:S(2)}) copy-start(f32[256,18]{0,1:T(8,128)S(1)} %get-tuple-element.136) | copy-start | bytes 55300
  108.1 195.5 %copy-start.39 = (f32[256,18]{0,1:T(8,128)}, f32[256,18]{0,1:T(8,128)S(1)}, u32[]{:S(2)}) copy-start(f32[256,18]{0,1:T(8,128)S(1)} %get-tuple-element.137) | copy-start | bytes 55300
  318.5 8.9 copy-start.58
  318.6 10.2 copy-start.71
  336.6 333.1 %all-gather.7.cloned.1.call-start = ((), (), s32[]{:S(2)}) async-start(), calls=%async_computation.18 | async-start | bytes 11796480 | tf_op jit(solution)/shard_map/all_gather | solution.py:202
  499.3 609.0 %copy-start.48 = (f32[16,64]{1,0:T(8,128)}, f32[16,64]{1,0:T(8,128)S(1)}, u32[]{:S(2)}) copy-start(f32[16,64]{1,0:T(8,128)S(1)} %fusion.88) | copy-start | bytes 12292
  502.0 334.2 %all-gather.9.cloned.1.call-start = ((), (), s32[]{:S(2)}) async-start(), calls=%async_computation.20 | async-start | bytes 11796480 | tf_op jit(solution)/shard_map/all_gather | solution.py:221
  516.2 592.1 %copy-start.64 = (f32[16]{0:T(128)}, f32[16]{0:T(128)S(1)}, u32[]{:S(2)}) copy-start(f32[16]{0:T(128)S(1)} %multiply_divide_fusion) | copy-start | bytes 196
  520.2 584.0 %reduce-scatter.18.cloned.1.call-start = ((), (), s32[]{:S(2)}) async-start(), calls=%async_computation.21 | async-start | bytes 11796480 | tf_op jit(solution)/shard_map/reduce_scatter | solution.py:240
  944.5 335.6 %all-gather.11.cloned.1.call-start = ((), (), s32[]{:S(2)}) async-start(), calls=%async_computation.22 | async-start | bytes 11796480 | tf_op jit(solution)/shard_map/all_gather | solution.py:248
  1108.7 171.5 %copy-start.72 = (bf16[288,1152]{1,0:T(8,128)(2,1)S(1)}, bf16[288,1152]{1,0:T(8,128)(2,1)}, u32[]{:S(2)}) copy-start(bf16[288,1152]{1,0:T(8,128)(2,1)} %param.29) | copy-start | bytes 1990660
  1112.4 430.7 %reduce-scatter.20.cloned.1.call-start = ((), (), s32[]{:S(2)}) async-start(), calls=%async_computation.23 | async-start | bytes 11796480 | tf_op jit(solution)/shard_map/reduce_scatter | solution.py:301
  1315.4 16.0 copy-start.16
  1315.4 16.0 copy-start.17
  1383.4 18.1 copy-start.70
  1383.5 324.1 %reduce-scatter.16.cloned.1.call-start = ((), (), s32[]{:S(2)}) async-start(), calls=%async_computation.19 | async-start | bytes 11796480 | tf_op jit(solution)/shard_map/reduce_scatter | solution.py:211
  1418.8 288.8 %copy-start.9 = (bf16[16,64,1152]{2,1,0:T(8,128)(2,1)S(1)}, bf16[16,64,1152]{2,1,0:T(8,128)(2,1)}, u32[]{:S(2)}) copy-start(bf16[16,64,1152]{2,1,0:T(8,128)(2,1)} %copy-done.8) | copy-start | bytes 7077892
  1418.8 288.8 %copy-start.19 = (f32[16,1152]{1,0:T(8,128)S(1)}, f32[16,1152]{1,0:T(8,128)}, u32[]{:S(2)}) copy-start(f32[16,1152]{1,0:T(8,128)} %copy-done.18) | copy-start | bytes 221188
  1418.8 288.8 %copy-start.22 = (f32[16,1152]{1,0:T(8,128)S(1)}, f32[16,1152]{1,0:T(8,128)}, u32[]{:S(2)}) copy-start(f32[16,1152]{1,0:T(8,128)} %copy-done.21) | copy-start | bytes 221188
  1418.8 288.8 %copy-start.26 = (f32[16,1152]{1,0:T(8,128)S(1)}, f32[16,1152]{1,0:T(8,128)}, u32[]{:S(2)}) copy-start(f32[16,1152]{1,0:T(8,128)} %copy-done.25) | copy-start | bytes 221188
  1418.8 288.8 %copy-start.32 = (f32[16,1152]{1,0:T(8,128)S(1)}, f32[16,1152]{1,0:T(8,128)}, u32[]{:S(2)}) copy-start(f32[16,1152]{1,0:T(8,128)} %copy-done.31) | copy-start | bytes 221188
  1418.8 288.8 %copy-start.49 = (f32[16,64]{1,0:T(8,128)S(1)}, f32[16,64]{1,0:T(8,128)}, u32[]{:S(2)}) copy-start(f32[16,64]{1,0:T(8,128)} %copy-done.48) | copy-start | bytes 12292
  1418.8 288.8 %copy-start.51 = (f32[16,64]{1,0:T(8,128)S(1)}, f32[16,64]{1,0:T(8,128)}, u32[]{:S(2)}) copy-start(f32[16,64]{1,0:T(8,128)} %copy-done.50) | copy-start | bytes 12292
  1418.8 288.8 %copy-start.53 = (f32[16,64]{1,0:T(8,128)S(1)}, f32[16,64]{1,0:T(8,128)}, u32[]{:S(2)}) copy-start(f32[16,64]{1,0:T(8,128)} %copy-done.52) | copy-start | bytes 12292
  1418.8 288.8 %copy-start.55 = (pred[16]{0:T(512)(128)(4,1)S(1)}, pred[16]{0:T(512)(128)(4,1)}, u32[]{:S(2)}) copy-start(pred[16]{0:T(512)(128)(4,1)} %copy-done.54) | copy-start | bytes 52
  1418.9 288.8 %copy-start.65 = (f32[16]{0:T(128)S(1)}, f32[16]{0:T(128)}, u32[]{:S(2)}) copy-start(f32[16]{0:T(128)} %copy-done.64) | copy-start | bytes 196
  1418.9 409.1 %all-reduce.17.cloned.1.call-start = ((), (), s32[]{:S(2)}) async-start(), calls=%async_computation.24 | async-start | bytes 442368 | tf_op jit(solution)/shard_map/psum | solution.py:319
  1719.8 162.8 %reduce-scatter.32.cloned.1.call-start = ((), (), s32[]{:S(2)}) async-start(), calls=%async_computation.30 | async-start | bytes 1990656 | tf_op jit(solution)/shard_map/reduce_scatter | solution.py:368
  1756.0 128.4 %reduce-scatter.30.cloned.1.call-start = ((), (), s32[]{:S(2)}) async-start(), calls=%async_computation.29 | async-start | bytes 3981312 | tf_op jit(solution)/shard_map/reduce_scatter | solution.py:365
  1777.6 175.1 %reduce-scatter.28.cloned.1.call-start = ((), (), s32[]{:S(2)}) async-start(), calls=%async_computation.28 | async-start | bytes 995328 | tf_op jit(solution)/shard_map/reduce_scatter | solution.py:362
  1805.7 150.6 %reduce-scatter.26.cloned.1.call-start = ((), (), s32[]{:S(2)}) async-start(), calls=%async_computation.27 | async-start | bytes 2985984 | tf_op jit(solution)/shard_map/reduce_scatter | solution.py:359
  1805.8 18.3 copy-start.3
  1805.8 19.1 copy-start.6
  1805.8 20.1 copy-start.7
  1805.8 22.2 %copy-start.42 = (bf16[16,1152]{1,0:T(8,128)(2,1)S(1)}, bf16[16,1152]{1,0:T(8,128)(2,1)}, u32[]{:S(2)}) copy-start(bf16[16,1152]{1,0:T(8,128)(2,1)} %copy-done.41) | copy-start | bytes 110596
  1828.0 21.7 %copy-start.5 = (s32[32]{0:T(128)S(1)}, s32[32]{0:T(128)}, u32[]{:S(2)}) copy-start(s32[32]{0:T(128)} %param.20) | copy-start | bytes 388
  1828.0 22.9 %copy-start.67 = (s32[32]{0:T(128)S(1)}, s32[32]{0:T(128)}, u32[]{:S(2)}) copy-start(s32[32]{0:T(128)} %param.21) | copy-start | bytes 388
  1838.0 16.4 copy-start.57
  1839.5 9.5 all-to-all-start.4
  1843.0 150.0 %reduce-scatter.34.cloned.1.call-start = ((), (), s32[]{:S(2)}) async-start(), calls=%async_computation.31 | async-start | bytes 331776
  1850.8 188.3 %reduce-scatter.22.cloned.1.call-start = ((), (), s32[]{:S(2)}) async-start(), calls=%async_computation.25 | async-start | bytes 2654208 | tf_op jit(solution)/shard_map/reduce_scatter | solution.py:374
  1853.2 246.5 %reduce-scatter.24.cloned.1.call-start = ((), (), s32[]{:S(2)}) async-start(), calls=%async_computation.26 | async-start | bytes 5971968 | tf_op jit(solution)/shard_map/reduce_scatter | solution.py:356
  1877.3 9.4 copy-start.68
  1877.3 9.4 copy-start.69
  1877.3 163.6 %all-to-all-start.3 = ((bf16[32,64,1152]{2,1,0:T(8,128)(2,1)}), bf16[32,64,1152]{2,1,0:T(8,128)(2,1)}, u32[]{:S(2)}, u32[]{:S(2)}) async-start(bf16[32,64,1152]{2,1,0:T(8,128)(2,1)} %select_select_fusion.2), calls=%async_computation.7 | async-start | bytes 9437184 | tf_op jit(solution)/shard_map/all_to_all | solution.py:345
  2040.9 61.0 %copy-start.1 = (bf16[1000,1152]{1,0:T(8,128)(2,1)S(1)}, bf16[1000,1152]{1,0:T(8,128)(2,1)}, u32[]{:S(2)}) copy-start(bf16[1000,1152]{1,0:T(8,128)(2,1)} %param.25) | copy-start | bytes 6912004
  (32 other events, 115.0 us)
Sparse Core Ops, SparseCore 0:
  107.6 166.1 all-gather.4
  336.7 159.4 reduce-scatter.13
  502.1 167.6 all-gather.6
  671.2 164.9 all-gather.8
  944.7 159.4 reduce-scatter.17
  1112.5 167.6 all-gather.10
  1383.6 159.4 reduce-scatter.19
  1545.4 162.1 reduce-scatter.15
  1719.9 35.7 all-reduce.16
  1759.3 39.1 reduce-scatter.31
  1802.4 48.8 reduce-scatter.29
  1855.3 36.2 reduce-scatter.27
  1895.1 61.1 reduce-scatter.25
  1960.1 32.8 reduce-scatter.33
  1996.6 42.4 reduce-scatter.21
  2042.4 57.1 reduce-scatter.23
where the time goes:
time: 2120 us; the launch traced here: 2110 us
  waiting for transfers between devices  1360 us (64%)
  matrix products  293 us (14%)
  local copies, waits for them, and re-layouts  192 us (9%)
  other arithmetic  145 us (7%)
  blocking collectives  78 us (4%)
  starting transfers between devices  23.5 us (1%)
    all_gather x1, waiting for transfers between devices, shards(): lax.all_gather(branch_low, 'mp', axis=1, tiled=True)  168 us
    all_gather x1, waiting for transfers between devices, shards(): normed_full = lax.all_gather(normed, 'mp', axis=1, tiled=True)  166 us
    reduce_scatter x1, waiting for transfers between devices, shards(): lax.psum_scatter(down_part.astype(jnp.bfloat16), 'mp', scatter_dimension=...  162 us
    reduce_scatter x1, waiting for transfers between devices, shards(): lax.psum_scatter(two_part.astype(jnp.bfloat16), 'mp', scatter_dimension=1...  160 us
    reduce_scatter x1, waiting for transfers between devices, shards(): lax.psum_scatter(branch_part.astype(jnp.bfloat16), 'mp', scatter_dimensio...  160 us
    all_gather x1, waiting for transfers between devices, shards(): lax.all_gather(down_low, 'mp', axis=1, tiled=True).reshape(-1, model_width)  143 us
    all_gather x1, waiting for transfers between devices, shards(): normed_two_full = lax.all_gather(normed_two, 'mp', axis=1, tiled=True)  130 us
    reduce_scatter x1, waiting for transfers between devices, shards(): lax.psum_scatter(normed_part.astype(jnp.bfloat16), 'mp', scatter_dimensio...  122 us
  transfers between devices with their start and end apart: 21, of which 14 were waited for; matrix products, arithmetic and copies ran while one was open for 15% of the time, Pallas kernels for 0%

commit v1 on v0

v1 whole, which is shorter than its diff:
```python
import jax
import jax.numpy as jnp
from jax import lax
from jax.experimental import pallas as pl
from jax.experimental.pallas import tpu as pltpu
from jax.sharding import PartitionSpec as P

GRID = 16
NCLS = 1000
NBINS = 16

epsilon = 1e-06
rope_base = 10000.0
f32 = jnp.float32
bf16 = jnp.bfloat16


def rms_scale(values, scaling, shifting):
    return (
        values * lax.rsqrt(jnp.mean(values * values, -1, keepdims=True) + epsilon) * (1.0 + scaling)
        + shifting
    )


def feature_order(head_dim):
    quarter = head_dim // 4
    firsts = list(range(quarter)) + list(range(2 * quarter, 3 * quarter))
    cut = len(firsts) // 8 * 8
    seconds = [i + quarter for i in firsts]
    return firsts[:cut] + seconds[:cut] + firsts[cut:] + seconds[cut:], cut


def rope_tables(length, head_dim):
    quarter = head_dim // 4
    order, cut = feature_order(head_dim)
    position = jnp.arange(length)
    places = jnp.stack([position // GRID, position % GRID]).astype(f32)
    frequency = rope_base ** (-jnp.arange(quarter).astype(f32) / quarter)
    angle = (frequency[None, :, None] * places[:, None, :]).reshape(2 * quarter, length)
    cosine, sine = jnp.cos(angle), jnp.sin(angle)
    cos_tab = jnp.concatenate([cosine[:cut], cosine[:cut], cosine[cut:], cosine[cut:]])
    sin_tab = jnp.concatenate([-sine[:cut], sine[:cut], -sine[cut:], sine[cut:]])
    return cos_tab, sin_tab


def partner(values, cut):
    rest = values[2 * cut :]
    half = rest.shape[0] // 2
    return jnp.concatenate(
        [values[cut : 2 * cut], values[:cut], pltpu.roll(rest, half, 0)], axis=0
    )


def head_scale(values):
    return lax.rsqrt(jnp.mean(values * values, axis=0, keepdims=True) + epsilon)


def dot_00(a, b):
    return lax.dot_general(a, b, (((0,), (0,)), ((), ())), preferred_element_type=f32)


def dot_11(a, b):
    return lax.dot_general(a, b, (((1,), (1,)), ((), ())), preferred_element_type=f32)


def dot_10(a, b):
    return lax.dot_general(a, b, (((1,), (0,)), ((), ())), preferred_element_type=f32)


def softmax_first(scores):
    shifted = jnp.exp(scores - jnp.max(scores, axis=0, keepdims=True))
    return shifted * (1.0 / jnp.sum(shifted, axis=0, keepdims=True))


def attend_kernel(proj_ref, gains_ref, cos_ref, sin_ref, out_ref):
    head_dim = gains_ref.shape[1]
    cut = feature_order(head_dim)[1]
    cos_tab, sin_tab = cos_ref[...], sin_ref[...]
    outs = []
    for head in range(proj_ref.shape[2] // head_dim):
        rows = slice(head * head_dim, (head + 1) * head_dim)
        lows = []
        for kind in range(2):
            raw = proj_ref[0, kind, rows, :]
            scaled = raw * head_scale(raw) * gains_ref[kind]
            turned = scaled * cos_tab + partner(scaled, cut) * sin_tab
            lows.append(turned.astype(bf16))
        value_low = proj_ref[0, 2, rows, :].astype(bf16)
        probs = softmax_first(dot_00(lows[1], lows[0]))
        outs.append(dot_10(value_low, probs.astype(bf16)))
    out_ref[0] = jnp.concatenate(outs, axis=0).astype(bf16)


def attend_back_kernel(
    proj_ref, cot_ref, gains_ref, cos_ref, sin_ref, out_ref, gain_grad_ref
):
    head_dim = gains_ref.shape[1]
    cut = feature_order(head_dim)[1]
    cos_tab, sin_tab = cos_ref[...], sin_ref[...]

    @pl.when((pl.program_id(0) == 0) & (pl.program_id(1) == 0))
    def _():
        gain_grad_ref[...] = jnp.zeros_like(gain_grad_ref)

    outs = [[], [], []]
    cot_all = cot_ref[0].astype(f32)
    for head in range(proj_ref.shape[2] // head_dim):
        rows = slice(head * head_dim, (head + 1) * head_dim)
        lows, units, scales = [], [], []
        for kind in range(2):
            raw = proj_ref[0, kind, rows, :]
            scale = head_scale(raw)
            unit = raw * scale
            scaled = unit * gains_ref[kind]
            turned = scaled * cos_tab + partner(scaled, cut) * sin_tab
            lows.append(turned.astype(bf16))
            units.append(unit)
            scales.append(scale)
        value_low = proj_ref[0, 2, rows, :].astype(bf16)
        cot_low = cot_all[rows].astype(bf16)
        probs = softmax_first(dot_00(lows[1], lows[0]))
        prob_grad = dot_00(value_low, cot_low)
        outs[2].append(dot_11(cot_low, probs.astype(bf16)))
        mean = jnp.sum(probs * prob_grad, axis=0, keepdims=True)
        score_low = (probs * (prob_grad - mean)).astype(bf16)
        turned_grads = (dot_10(lows[1], score_low), dot_11(lows[0], score_low))
        for kind in range(2):
            grad = turned_grads[kind]
            grad = grad * cos_tab + partner(grad * sin_tab, cut)
            gain_grad_ref[kind] += grad * units[kind]
            grad = grad * gains_ref[kind]
            along = jnp.mean(grad * units[kind], axis=0, keepdims=True)
            outs[kind].append(scales[kind] * (grad - units[kind] * along))
    for kind in range(3):
        out_ref[0, kind] = jnp.concatenate(outs[kind], axis=0).astype(bf16)


def attend_specs(groups, rows, own, length, head_dim):
    proj = pl.BlockSpec((1, 3, rows, length), lambda g, i: (g, 0, 0, i))
    att = pl.BlockSpec((1, rows, length), lambda g, i: (g, 0, i))
    gains = pl.BlockSpec((2, head_dim, 1), lambda g, i: (0, 0, 0))
    table = pl.BlockSpec((head_dim, length), lambda g, i: (0, 0))
    grads = pl.BlockSpec((2, head_dim, length), lambda g, i: (0, 0, 0))
    return proj, att, gains, table, grads


def attend(proj, gains, tables, own):
    groups, _, rows, tokens = proj.shape
    length, head_dim = tokens // own, gains.shape[1]
    proj_s, att_s, gains_s, table_s, _ = attend_specs(groups, rows, own, length, head_dim)
    return pl.pallas_call(
        attend_kernel,
        grid=(groups, own),
        in_specs=[proj_s, gains_s, table_s, table_s],
        out_specs=att_s,
        out_shape=jax.ShapeDtypeStruct((groups, rows, tokens), bf16),
        compiler_params=pltpu.CompilerParams(vmem_limit_bytes=48 << 20),
        cost_estimate=pl.CostEstimate(
            flops=4 * groups * rows * tokens * length,
            bytes_accessed=proj.size * 4 + groups * rows * tokens * 2,
            transcendentals=groups * rows // head_dim * tokens * length,
        ),
        name="attend",
    )(proj, gains, *tables)


def attend_back(proj, cot, gains, tables, own):
    groups, _, rows, tokens = proj.shape
    length, head_dim = tokens // own, gains.shape[1]
    proj_s, att_s, gains_s, table_s, grads_s = attend_specs(groups, rows, own, length, head_dim)
    return pl.pallas_call(
        attend_back_kernel,
        grid=(groups, own),
        in_specs=[proj_s, att_s, gains_s, table_s, table_s],
        out_specs=[proj_s, grads_s],
        out_shape=[
            jax.ShapeDtypeStruct(proj.shape, bf16),
            jax.ShapeDtypeStruct((2, head_dim, length), f32),
        ],
        compiler_params=pltpu.CompilerParams(vmem_limit_bytes=48 << 20),
        cost_estimate=pl.CostEstimate(
            flops=10 * groups * rows * tokens * length,
            bytes_accessed=proj.size * 6 + groups * rows * tokens * 2,
            transcendentals=groups * rows // head_dim * tokens * length,
        ),
        name="attend_back",
    )(proj, cot, gains, *tables)


def swish_mul(gate_part, up_part):
    return jax.nn.silu(gate_part) * up_part


def dot(a, b):
    return jnp.dot(a, b, preferred_element_type=f32)


def ein(spec, a, b):
    return jnp.einsum(spec, a, b, preferred_element_type=f32)


def gather_rows(block, dp_size):
    rows, width = block.shape
    share = -(-rows // dp_size)
    if rows % dp_size:
        block = jnp.pad(block, ((0, share * dp_size - rows), (0, 0)))
    piece = lax.dynamic_slice_in_dim(block, lax.axis_index("dp") * share, share, 0)
    whole = lax.all_gather(piece, ("mp", "dp"), axis=0, tiled=True)
    if rows % dp_size:
        whole = whole.reshape(-1, share * dp_size, width)[:, :rows].reshape(-1, width)
    return whole


def reduce_grad(grad, mp_size):
    rows = lax.psum_scatter(grad, "dp", scatter_dimension=0, tiled=True)
    rows = rows.reshape(rows.shape[0], mp_size, -1).swapaxes(0, 1)
    return lax.psum_scatter(rows, "mp", scatter_dimension=0, tiled=False).astype(f32)


def shards(
    patches,
    cotangent,
    time_bins,
    labels,
    image_counts,
    dest_perm,
    time_table,
    class_table,
    ada_weight,
    qkv_weight,
    norm_gains,
    out_weight,
    expand_weight,
    down_weight,
):
    dp_size = lax.axis_size("dp")
    mp_size = lax.axis_size("mp")
    capacity = patches.shape[0]
    slot_count = capacity // dp_size
    images = cotangent.shape[0]
    local_len = patches.shape[1]
    model_width = patches.shape[2]
    length = local_len * mp_size
    head_dim = norm_gains.shape[1]
    local_dim = out_weight.shape[0]
    unit_count = down_weight.shape[0]
    units = unit_count * mp_size
    own = images // mp_size
    total_images = images * dp_size
    order = jnp.array(feature_order(head_dim)[0])
    tables = rope_tables(length, head_dim)
    gains_f = norm_gains.astype(f32)[:, order]
    gains_f = (gains_f * jnp.array([[head_dim ** (-0.5)], [1.0]], f32))[:, :, None]
    dp_index = lax.axis_index("dp")
    mp_index = lax.axis_index("mp")

    columns = jnp.arange(3 * local_dim)
    places = columns // head_dim * head_dim + order[columns % head_dim]
    places = jnp.where(columns < 2 * local_dim, places, columns)
    turn = (places[:, None] == columns[None, :]).astype(bf16)
    qkv_block = ein("rc,dc->rd", turn, qkv_weight.reshape(model_width, -1)).astype(bf16)
    qkv_full = gather_rows(qkv_block, dp_size)
    out_full = gather_rows(out_weight, dp_size)
    expand_full = gather_rows(expand_weight.reshape(model_width, -1).T, dp_size)
    down_full = gather_rows(down_weight, dp_size)

    starts = jnp.cumsum(image_counts) - image_counts
    finish = starts + image_counts
    my_start = starts[dp_index]
    my_count = image_counts[dp_index]
    device_ids = jnp.arange(dp_size)
    matches = (dest_perm[:, None] == device_ids[None, :]).astype(jnp.int32)
    inverse = jnp.sum(device_ids[:, None] * matches, axis=0)
    my_place = inverse[dp_index]
    pair_ids = jnp.arange(dp_size * slot_count)
    pair_peer = pair_ids // slot_count
    pair_slot = pair_ids % slot_count
    send_index = pair_slot * dp_size + jnp.mod(inverse[pair_peer] - my_start, dp_size)
    send_index = jnp.minimum(send_index, capacity - 1)
    send_patches = jnp.take(patches, send_index, axis=0)
    recv_patches = lax.all_to_all(send_patches, "dp", split_axis=0, concat_axis=0, tiled=True)
    rank_ids = jnp.arange(images) * dp_size + my_place
    source = jnp.sum((finish[None, :] <= rank_ids[:, None]).astype(jnp.int32), axis=1)
    within = rank_ids - starts[source]
    recv_index = source * slot_count + within // dp_size
    latent = jnp.take(recv_patches, recv_index, axis=0)
    latent = lax.all_to_all(latent, "mp", split_axis=0, concat_axis=1, tiled=True)
    cot = lax.all_to_all(cotangent, "mp", split_axis=0, concat_axis=1, tiled=True)

    info = lax.all_gather(jnp.stack([time_bins, labels]), "dp", axis=1, tiled=True)
    slot_all = jnp.arange(dp_size * capacity)
    live_all = (slot_all % capacity) < jnp.repeat(image_counts, capacity)
    bin_totals = jnp.sum(
        ((info[0][:, None] == jnp.arange(NBINS)[None, :]) & live_all[:, None]).astype(f32), axis=0
    )
    row_all = jnp.arange(total_images)
    rank_all = (row_all % images) * dp_size + jnp.repeat(inverse, images)
    source_all = jnp.sum((finish[None, :] <= rank_all[:, None]).astype(jnp.int32), axis=1)
    start_all = jnp.sum(
        jnp.where(source_all[:, None] == device_ids[None, :], starts[None, :], 0), axis=1
    )
    slots_all = source_all * capacity + rank_all - start_all
    slot_hit = slots_all[:, None] == slot_all[None, :]
    bins_all = jnp.sum(jnp.where(slot_hit, info[0][None, :], 0), axis=1)
    labels_all = jnp.sum(jnp.where(slot_hit, info[1][None, :], 0), axis=1)
    bin_hot = (bins_all[:, None] == jnp.arange(NBINS)[None, :])
    label_hot = (labels_all[:, None] == jnp.arange(NCLS)[None, :])
    weights_all = total_images / (NBINS * jnp.sum(bin_hot.astype(f32) * bin_totals[None, :], axis=1))
    bin_hot = bin_hot.astype(bf16)
    label_hot = label_hot.astype(bf16)
    cond_all = (dot(bin_hot, time_table) + dot(label_hot, class_table)).astype(bf16).astype(f32)
    silu_all = jax.nn.silu(cond_all).astype(bf16)
    first = dp_index * images + mp_index * own
    silu_cond = lax.dynamic_slice_in_dim(silu_all, first, own, 0)
    weights = lax.dynamic_slice_in_dim(weights_all, first, own, 0)

    modulation = dot(silu_cond, ada_weight.reshape(model_width, 6 * model_width))
    modulation = modulation.reshape(own, 6, 1, model_width)
    shift_one = modulation[:, 0]
    scale_one = modulation[:, 1]
    gate_one = modulation[:, 2]
    shift_two = modulation[:, 3]
    scale_two = modulation[:, 4]
    gate_two = modulation[:, 5]

    latent_f = latent.astype(f32)
    out_cot = cot.astype(f32) * weights[:, None, None]
    normed = rms_scale(latent_f, scale_one, shift_one).astype(bf16)
    normed_flat = normed.reshape(-1, model_width)
    proj = ein("cd,nd->cn", qkv_full, normed_flat)
    proj = proj.reshape(mp_size, 3, local_dim, own * length)
    attended = attend(proj, gains_f, tables, own)
    branch_one = ein("mcn,mcd->nd", attended, out_full.reshape(mp_size, local_dim, -1))
    branch_one = branch_one.reshape(own, length, model_width)
    middle = latent_f + gate_one * branch_one
    normed_two = rms_scale(middle, scale_two, shift_two).astype(bf16)
    two_flat = normed_two.reshape(-1, model_width)
    expanded = ein("nd,fd->nf", two_flat, expand_full).reshape(-1, mp_size, 2, unit_count)
    swish_val, swish_pull = jax.vjp(swish_mul, expanded[:, :, 0], expanded[:, :, 1])
    hidden = swish_val.astype(bf16).reshape(-1, units)
    branch_two = dot(hidden, down_full).reshape(own, length, model_width)
    result = (middle + gate_two * branch_two).astype(bf16)
    result = lax.all_to_all(result, "mp", split_axis=1, concat_axis=0, tiled=True)

    down_low = (gate_two * out_cot).astype(bf16)
    gate_two_grad = jnp.sum(out_cot * branch_two, axis=1)
    down_low = down_low.reshape(-1, model_width)
    down_term = ein("nd,nf->df", down_low, hidden).astype(bf16)
    hidden_grad = ein("nd,fd->nf", down_low, down_full).reshape(-1, mp_size, unit_count)
    gate_grad, up_grad = swish_pull(hidden_grad)
    expand_low = jnp.stack([gate_grad, up_grad], 2).astype(bf16).reshape(-1, 2 * units)
    expand_term = ein("nd,nf->df", two_flat, expand_low).astype(bf16)
    two_grad = ein("nf,fd->nd", expand_low, expand_full).reshape(own, length, model_width)
    norm_val, norm_pull = jax.vjp(rms_scale, middle, scale_two, shift_two)
    middle_grad, scale_two_grad, shift_two_grad = norm_pull(two_grad)
    middle_grad = middle_grad + out_cot
    gate_one_grad = jnp.sum(middle_grad * branch_one, axis=1)
    branch_low = (gate_one * middle_grad).astype(bf16).reshape(-1, model_width)
    out_term = ein("nd,mcn->dmc", branch_low, attended).astype(bf16)
    attended_low = ein("cd,nd->cn", out_full, branch_low).astype(bf16)
    attended_low = attended_low.reshape(mp_size, local_dim, own * length)
    projected_low, gains_grad = attend_back(proj, attended_low, gains_f, tables, own)
    gains_grad = jnp.sum(gains_grad, axis=2) * jnp.array([[head_dim ** (-0.5)], [1.0]], f32)
    qkv_term = ein("nd,mkcn->dmkc", normed_flat, projected_low).astype(bf16)
    normed_grad = ein("cn,cd->nd", projected_low.reshape(-1, own * length), qkv_full)
    normed_grad = normed_grad.reshape(own, length, model_width)
    norm_val, norm_pull = jax.vjp(rms_scale, latent_f, scale_one, shift_one)
    latent_grad, scale_one_grad, shift_one_grad = norm_pull(normed_grad)
    latent_grad = (latent_grad + middle_grad).astype(bf16)

    latent_back = lax.all_to_all(latent_grad, "mp", split_axis=1, concat_axis=0, tiled=True)
    back_within = pair_slot * dp_size + jnp.mod(my_place - starts[pair_peer], dp_size)
    back_slot = jnp.clip((starts[pair_peer] + back_within - my_place) // dp_size, 0, images - 1)
    back_patches = jnp.take(latent_back, back_slot, axis=0)
    got_patches = lax.all_to_all(back_patches, "dp", split_axis=0, concat_axis=0, tiled=True)
    slot_ids = jnp.arange(capacity)
    slot_live = slot_ids < my_count
    home_peer = dest_perm[jnp.mod(my_start + slot_ids, dp_size)]
    home_index = home_peer * slot_count + jnp.minimum(slot_ids // dp_size, slot_count - 1)
    patch_grad = jnp.where(slot_live[:, None, None], jnp.take(got_patches, home_index, axis=0), 0)

    modulation_grad = jnp.stack(
        [
            shift_one_grad[:, 0],
            scale_one_grad[:, 0],
            gate_one_grad,
            shift_two_grad[:, 0],
            scale_two_grad[:, 0],
            gate_two_grad,
        ],
        1,
    ).astype(bf16)
    mod_all = lax.all_gather(modulation_grad, ("dp", "mp"), axis=0, tiled=True)
    gains_total = lax.all_gather(gains_grad.astype(bf16), ("dp", "mp"), axis=0)
    gains_total = jnp.sum(gains_total.astype(f32), axis=0)
    gains_total = jnp.sum(
        jnp.where(order[:, None] == jnp.arange(head_dim)[None, :], gains_total[:, :, None], 0.0), axis=1
    )
    width_dp = model_width // dp_size
    width_mp = model_width // mp_size
    row0 = dp_index * width_dp
    silu_rows = lax.dynamic_slice_in_dim(silu_all, row0, width_dp, 1)
    mod_cols = lax.dynamic_slice_in_dim(mod_all, mp_index * width_mp, width_mp, 2)
    ada_grad = ein("id,ikc->dkc", silu_rows, mod_cols)
    ada_rows = lax.dynamic_slice_in_dim(ada_weight, row0, width_dp, 0)
    silu_grad = ein("ikc,dkc->id", mod_all, ada_rows)
    cond_rows = lax.dynamic_slice_in_dim(cond_all, row0, width_dp, 1)
    silu_val, silu_pull = jax.vjp(jax.nn.silu, cond_rows)
    condition_low = silu_pull(silu_grad)[0].astype(bf16)
    time_grad = ein("in,id->nd", bin_hot, condition_low)
    class_grad = ein("in,id->nd", label_hot, condition_low)

    down_grad = reduce_grad(down_term, mp_size).T
    expand_grad = reduce_grad(expand_term.reshape(model_width, -1), mp_size)
    expand_grad = expand_grad.reshape(-1, 2, unit_count)
    out_grad = reduce_grad(out_term, mp_size).T
    qkv_grad = reduce_grad(qkv_term.reshape(model_width, -1), mp_size)
    qkv_grad = lax.dot_general(
        qkv_grad,
        turn.astype(f32),
        (((1,), (0,)), ((), ())),
        precision=lax.Precision.HIGHEST,
        preferred_element_type=f32,
    )
    qkv_grad = qkv_grad.reshape(-1, 3, local_dim)
    return (
        result,
        patch_grad,
        time_grad,
        class_grad,
        ada_grad,
        qkv_grad,
        gains_total,
        out_grad,
        expand_grad,
        down_grad,
    )


def solution(mesh):
    in_specs = (
        P("dp", "mp", None),
        P("dp", "mp", None),
        P("dp"),
        P("dp"),
        P(),
        P(),
        P(),
        P(),
        P(),
        P(None, None, "mp"),
        P(),
        P("mp", None),
        P(None, None, "mp"),
        P("mp", None),
    )
    out_specs = (
        P("dp", "mp", None),
        P("dp", "mp", None),
        P(None, "dp"),
        P(None, "dp"),
        P("dp", None, "mp"),
        P("dp", None, "mp"),
        P(),
        P("mp", "dp"),
        P("dp", None, "mp"),
        P("mp", "dp"),
    )
    return jax.shard_map(shards, mesh=mesh, in_specs=in_specs, out_specs=out_specs, check_vma=False)
```

time: 2120 us -> 1140 us (0.54)
  waiting for transfers between devices: 1360 us -> 301 us
  local copies, waits for them, and re-layouts: 192 us -> 299 us
  matrix products: 293 us -> 220 us
  other arithmetic: 145 us -> 81.2 us
  Pallas kernels: 0 us -> 60.1 us
  blocking collectives: 78 us -> 121 us
    reduce_scatter x10 -> x8, waiting for transfers between devices: 698 us -> 91.5 us  [the longest x4 78.7 us: reduce_grad(): lax.psum_scatter(rows, 'mp', scatter_dimension=0, tiled=False).astype(f32)]
    all_gather x4 -> x5, waiting for transfers between devices: 606 us -> 10.9 us  [the longest x4 10.9 us: gather_rows(): whole = lax.all_gather(piece, ('mp', 'dp'), axis=0, tiled=True)]
    all_to_all x3 -> x4, waiting for transfers between devices: 5.3 us -> 198 us  [the longest x1 69.5 us: shards(): lax.all_to_all(cotangent, 'mp', split_axis=0, concat_axis=1, tiled=True)]
    all_gather x0 -> x2, blocking collectives: none -> 121 us  [the longest x1 81 us: shards(): gains_total = lax.all_gather(gains_grad.astype(bf16), ('dp', 'mp'), axis=0)]
    dot_general x24 -> x21, matrix products: 281 us -> 220 us  [the longest x16 182 us: ein(): return jnp.einsum(spec, a, b, preferred_element_type=f32)]
    squeeze x0 -> x4, local copies, waits for them, and re-layouts: none -> 60.4 us  [the longest x2 30.2 us: shards(): expanded[:, :, 0]]
    pallas_call x0 -> x2, Pallas kernels: none -> 60.1 us  [the longest x1 34 us: attend_back(): pl.pallas_call(attend_back_kernel, grid=(groups, own), in_specs=[proj_s,...]
    unnamed x1 -> x0, blocking collectives: 53.4 us -> none
  transfers between devices with their start and end apart: 21 -> 19, of which waited for: 14 -> 10; matrix products, arithmetic and copies ran while one was open for 15% -> 34% of each run, Pallas kernels for 0% -> 5%
where the time goes in v1:
time: 1140 us; the launch traced here: 1130 us
  waiting for transfers between devices  301 us (26%)
  local copies, waits for them, and re-layouts  299 us (26%)
  matrix products  220 us (19%)
  blocking collectives  121 us (11%)
  other arithmetic  81.2 us (7%)
  Pallas kernels  60.1 us (5%)
  starting transfers between devices  30.3 us (3%)
  between operations  15 us (1%)
    dot_general x16, matrix products, ein(): return jnp.einsum(spec, a, b, preferred_element_type=f32)  182 us
    all_gather x1, blocking collectives, shards(): gains_total = lax.all_gather(gains_grad.astype(bf16), ('dp', 'mp'), axis=0)  81 us
    reduce_scatter x4, waiting for transfers between devices, reduce_grad(): lax.psum_scatter(rows, 'mp', scatter_dimension=0, tiled=False).astype(f32)  78.7 us
    all_to_all x1, waiting for transfers between devices, shards(): lax.all_to_all(cotangent, 'mp', split_axis=0, concat_axis=1, tiled=True)  69.5 us
    convert_element_type x3, local copies, waits for them, and re-layouts, shards(): jnp.stack([gate_grad, up_grad], 2).astype(bf16).reshape(-1, 2 * units)  69.3 us
    unnamed x122, local copies, waits for them, and re-layouts  59.5 us
    all_to_all x1, waiting for transfers between devices, shards(): lax.all_to_all(latent, 'mp', split_axis=0, concat_axis=1, tiled=True)  49.8 us
    all_to_all x1, waiting for transfers between devices, shards(): lax.all_to_all(latent_grad, 'mp', split_axis=1, concat_axis=0, tiled=True)  47.9 us
  transfers between devices with their start and end apart: 19, of which 10 were waited for; matrix products, arithmetic and copies ran while one was open for 34% of the time, Pallas kernels for 5%

profile of v1, /device:TPU:0, one launch (start us, length us, event | category | flops | bytes accessed | tf_op | source)
XLA Modules:
  0.0 1126.0 jit_solution(14523339671738593459)
XLA Ops:
  9.1 5.7 gather_fusion.3
  14.8 4.0 fusion.23
  19.7 10.3 copy.201
  35.4 5.6 gather_fusion.8
  41.0 5.1 broadcast_select_fusion
  46.1 5.2 all-to-all-start
  54.0 22.5 %copy.194 = bf16[1152,6,1152]{0,2,1:T(8,128)(2,1)} copy(bf16[1152,6,1152]{2,0,1:T(8,128)(2,1)} %param.27) | data formatting | bytes 31850496 | tf_op args[8]
  76.6 39.6 %all-gather = s32[8,32,2]{1,2,0:T(2,128)S(1)} all-gather(s32[1,32,2]{1,2,0:T(2,128)S(1)} %add_bitcast_fusion), channel_id=1, replica_groups=mesh['dp'=8,'mp'=4] {'dp'}, dimensions={0}, use_global_device_ids=true | all-gather | bytes 2304 | tf_op jit(solution)/shard_map/all_gather | solution.py:290
  116.4 5.7 all-to-all-start.3
  127.0 4.6 gather_fusion.2
  131.5 3.4 broadcast_select_fusion.2
  134.9 69.5 %all-to-all-done.3 = bf16[16,64,1152]{2,1,0:T(8,128)(2,1)} async-done(((bf16[16,64,1152]{2,1,0:T(8,128)(2,1)}), bf16[16,64,1152]{2,1,0:T(8,128)(2,1)}, u32[]{:S(2)}, u32[]{:S(2)}) %all-to-all-start.3) | async-done | bytes 2359328 | tf_op jit(solution)/shard_map/all_to_all | solution.py:288
  204.4 4.5 all-to-all-start.1
  211.8 10.5 fusion.32
  228.9 5.3 reshape.1070
  234.2 49.8 %all-to-all-done.1 = bf16[16,64,1152]{2,1,0:T(8,128)(2,1)} async-done(((bf16[16,64,1152]{2,1,0:T(8,128)(2,1)}), bf16[16,64,1152]{2,1,0:T(8,128)(2,1)}, u32[]{:S(2)}, u32[]{:S(2)}) %all-to-all-start.1) | async-done | bytes 2359328 | tf_op jit(solution)/shard_map/all_to_all | solution.py:287
  284.0 4.3 copy.190
  290.7 4.5 add_convert_fusion.2
  295.2 9.7 dot_general.87
  304.8 15.4 %fusion.110.proj_ref = f32[4,3,288,1024]{3,2,1,0:T(8,128)} fusion(bf16[4,3,288,1152]{3,2,1,0:T(8,128)(2,1)} %dot_general.87, bf16[1024,1152,1,1]{1,0,3,2:T(8,128)(2,1)} %bitcast.333), kind=kOutput, calls=%fused_computation.284 | convolution fusion | flops 8153726976 | bytes 24477696 | tf_op jit(solution)/shard_map/cd,nd->cn/dot_general | solution.py:199
  320.3 26.1 %attend.1 = bf16[4,288,1024]{2,1,0:T(8,128)(2,1)S(1)} custom-call(f32[4,3,288,1024]{3,2,1,0:T(8,128)} %fusion.110.proj_ref, f32[2,72,1]{2,1,0:T(8,128)S(1)} %broadcast_multiply_fusion.gains_ref, f32[72,256]{1,0:T(8,128)S(1)} %pad_maximum_fusion.cos_ref, f32[72,256]{1,0:T(8,128)S(1)} %pad_maximum_fusion.1.sin_ref), custom_call_target="tpu_custom_call" | custom-call | flops 1207959552 | bytes 16515072 | tf_op jit(solution)/shard_map/attend/pallas_call | solution.py:151
  346.4 8.4 multiply_reduce_fusion.4
  359.2 23.7 %fusion.111 = f32[1024,4,2,768]{0,3,2,1:T(8,128)} fusion(bf16[1024,1152,1,1]{1,0,3,2:T(8,128)(2,1)} %bitcast.327, bf16[4,2,768,1152]{3,2,1,0:T(8,128)(2,1)} %bitcast.347), kind=kOutput, calls=%fused_computation.285 | convolution fusion | flops 14495514624 | bytes 41680896 | tf_op jit(solution)/shard_map/nd,fd->nf/dot_general | solution.py:199
  382.9 22.3 %multiply_convert_fusion = (bf16[1024,4,1,768]{0,3,2,1:T(8,128)(2,1)}, f32[1024,4,1,768]{0,3,2,1:T(8,128)}, f32[1024,4,1,768]{0,3,2,1:T(8,128)}) fusion(f32[1024,4,2,768]{0,3,2,1:T(8,128)} %fusion.111), kind=kLoop, calls=%fused_computation.29 | loop fusion | flops 18874368 | bytes 56623104 | tf_op jit(solution)/shard_map/convert_element_type | solution.py:340
  405.2 10.9 all-gather.11.cloned.1.call-done
  416.1 22.3 %fusion.6 = (bf16[1024,4,1,768]{0,3,1,2:T(8,128)(2,1)}, bf16[1024,4,1,768]{0,3,1,2:T(8,128)(2,1)}) fusion(f32[1024,4,2,768]{0,3,2,1:T(8,128)} %fusion.111, bf16[1024,1152,1]{1,0,2:T(8,128)(2,1)} %bitcast.329, bf16[4,768,1152]{2,1,0:T(8,128)(2,1)} %bitcast.348), kind=kOutput, calls=%fused_computation.19 | convolution fusion | flops 7291797504 | bytes 47185920 | tf_op jit(solution)/shard_map/nd,fd->nf/dot_general | solution.py:199
  438.4 10.5 maximum_convert_fusion
  448.9 31.7 %copy.208 = bf16[1024,4,2,768]{3,2,1,0:T(2,128)(2,1)} copy(bf16[1024,4,2,768]{0,3,1,2:T(8,128)(2,1)} %maximum_convert_fusion) | data formatting | bytes 25165824 | tf_op jit(solution)/shard_map/convert_element_type | solution.py:351
  480.6 26.5 %convert_element_type.248 = bf16[4,256,6144]{2,1,0:T(8,128)(2,1)} reshape(bf16[1024,4,2,768]{3,2,1,0:T(2,128)(2,1)} %copy.208) | data formatting | bytes 25165824 | tf_op jit(solution)/shard_map/convert_element_type | solution.py:351
  507.1 25.4 %multiply_reduce_fusion.1 = (bf16[4,1152]{1,0:T(4,128)(2,1)}, f32[4,256]{1,0:T(4,128)S(1)}, bf16[4,1152]{1,0:T(4,128)(2,1)}, f32[4,256,1152]{2,1,0:T(8,128)}) fusion(f32[4,256,1152]{2,1,0:T(8,128)} %copy-done.12, f32[4,256]{1,0:T(4,128)S(1)} %fusion.78, f32[4,1152]{1,0:T(4,128)S(1)} %get-tuple-element.40, bf16[4,256,6144]{2,1,0:T(8,128)(2,1)} %convert_element_type.248, ...), kind=kOutput, calls=%fused_computation.55 | convolution fusion | flops 14503761920 | bytes 36220928 | tf_op jit(solution)/shard_map/nf,fd->nd/dot_general | solution.py:199
  532.5 15.5 %squeeze.28 = f32[4,256,3072]{1,0,2:T(4,128)} reshape(f32[1024,4,1,768]{0,3,2,1:T(8,128)} %get-tuple-element.34) | data formatting | bytes 25165824 | tf_op jit(solution)/shard_map/squeeze | solution.py:339
  548.0 14.7 %copy.204 = f32[4,256,3072]{2,1,0:T(8,128)} copy(f32[4,256,3072]{1,0,2:T(4,128)} %squeeze.28) | data formatting | bytes 25165824 | tf_op jit(solution)/shard_map/squeeze | solution.py:339
  562.6 15.6 %squeeze.27 = f32[4,256,3072]{1,0,2:T(4,128)} reshape(f32[1024,4,1,768]{0,3,2,1:T(8,128)} %get-tuple-element.35) | data formatting | bytes 25165824 | tf_op jit(solution)/shard_map/squeeze | solution.py:339
  578.3 14.6 %copy.203 = f32[4,256,3072]{2,1,0:T(8,128)} copy(f32[4,256,3072]{1,0,2:T(4,128)} %squeeze.27) | data formatting | bytes 25165824 | tf_op jit(solution)/shard_map/squeeze | solution.py:339
  592.9 22.4 %fusion.21 = (bf16[4,1152]{1,0:T(4,128)(2,1)}, f32[4,256,1152]{2,1,0:T(8,128)S(1)}, bf16[4,1152]{1,0:T(4,128)(2,1)}, bf16[4,256,1152]{2,1,0:T(8,128)(2,1)}) fusion(f32[4,256,1152,1]{2,1,3,0:T(8,128)} %get-tuple-element.54, f32[4]{0:T(128)S(1)} %copy-done.47, f32[4,4,64,1152]{3,2,0,1:T(8,128)} %copy-done.11, f32[4,256,1152]{2,1,0:T(8,128)} %copy-done.12, ...), kind=kOutput, calls=%fused_computation.48 | convolution fusion | flops 7283137536 | bytes 58259472 | tf_op jit(solution)/shard_map/dot_general | solution.py:195
  619.6 5.4 convolution_convert_fusion.3
  625.0 12.3 %convolution_convert_fusion.2 = bf16[1152,3072]{1,0:T(8,128)(2,1)} fusion(bf16[1024,1152]{1,0:T(8,128)(2,1)} %bitcast.330, bf16[1024,3072]{0,1:T(8,128)(2,1)} %bitcast.322), kind=kOutput, calls=%fused_computation.32 | convolution fusion | flops 7251296256 | bytes 15728640 | tf_op jit(solution)/shard_map/nd,nf->df/dot_general | solution.py:199
  637.4 5.4 reshape.1061
  646.5 5.1 convolution_convert_fusion.4
  651.7 34.0 %attend_back.1 = (bf16[4,3,288,1024]{3,2,1,0:T(8,128)(2,1)}, f32[2,72,256]{2,1,0:T(8,128)S(1)}) custom-call(f32[4,3,288,1024]{3,2,1,0:T(8,128)} %fusion.110.proj_ref, bf16[4,288,1024]{2,1,0:T(8,128)(2,1)S(1)} %bitcast.312, f32[2,72,1]{2,1,0:T(8,128)S(1)} %broadcast_multiply_fusion.gains_ref, f32[72,256]{1,0:T(8,128)S(1)} %pad_maximum_fusion.cos_ref, ...), custom_call_target="tpu_custom_call" | custom-call | flops 3019898880 | bytes 23592960 | tf_op jit(solution)/shard_map/attend_back/pallas_call | solution.py:171
  685.7 14.4 %convolution_convert_fusion.1 = bf16[1152,4,3,288]{0,3,2,1:T(8,128)(2,1)} fusion(bf16[4,3,288,1024]{3,2,1,0:T(8,128)(2,1)} %get-tuple-element.13, bf16[1024,1152]{1,0:T(8,128)(2,1)S(1)} %fusion.19), kind=kOutput, calls=%fused_computation.31 | convolution fusion | flops 8157708288 | bytes 17399808 | tf_op jit(solution)/shard_map/nd,mkcn->dmkc/dot_general | solution.py:199
  700.1 11.7 %copy.217 = bf16[1152,3456]{1,0:T(8,128)(2,1)} copy(bf16[1152,3456]{0,1:T(8,128)(2,1)} %bitcast.318) | data formatting | bytes 15925248 | tf_op jit(solution)/shard_map/reshape | solution.py:417
  711.9 11.1 copy.220
  723.0 22.5 %convolution_convert_fusion = bf16[1152,6144]{1,0:T(8,128)(2,1)} fusion(bf16[1024,1152]{1,0:T(8,128)(2,1)} %bitcast.328, bf16[1024,6144]{0,1:T(8,128)(2,1)} %bitcast.316), kind=kOutput, calls=%fused_computation.11 | convolution fusion | flops 14502592512 | bytes 29097984 | tf_op jit(solution)/shard_map/nd,nf->df/dot_general | solution.py:199
  745.5 9.7 reshape.1076
  755.2 10.8 copy.209
  766.0 16.0 %multiply_reduce_fusion.2 = (bf16[4,1152]{1,0:T(4,128)(2,1)S(1)}, f32[4,256]{1,0:T(4,128)S(1)}, bf16[4,1152]{1,0:T(4,128)(2,1)S(1)}, f32[4,256,1152]{2,1,0:T(8,128)S(1)}) fusion(f32[4,4,64,1152]{3,2,0,1:T(8,128)} %copy.190, f32[4,256]{1,0:T(4,128)S(1)} %copy-done.28, f32[4,1152]{1,0:T(4,128)S(1)} %copy-done.18, bf16[4,256,3456]{2,1,0:T(8,128)(2,1)} %bitcast.320, ...), kind=kOutput, calls=%fused_computation.56 | convolution fusion | flops 8161974272 | bytes 24522752 | tf_op jit(solution)/shard_map/cn,cd->nd/dot_general | solution.py:199
  785.3 3.2 copy.210
  788.5 4.5 all-to-all-start.4
  793.9 5.0 copy.205
  798.9 47.9 %all-to-all-done.4 = bf16[4,256,1152]{2,0,1:T(4,128)(2,1)} async-done(((bf16[4,256,1152]{2,0,1:T(4,128)(2,1)}), bf16[4,256,1152]{2,0,1:T(4,128)(2,1)}, u32[]{:S(2)}, u32[]{:S(2)}) %all-to-all-start.4) | async-done | bytes 2359328 | tf_op jit(solution)/shard_map/all_to_all | solution.py:371
  846.8 4.7 all-to-all-start.2
  860.5 4.9 gather_fusion.6
  869.3 5.1 broadcast_select_fusion.1
  874.4 30.3 %all-to-all-done.2 = bf16[4,256,1152]{2,0,1:T(4,128)(2,1)} async-done(((bf16[4,256,1152]{2,0,1:T(4,128)(2,1)}), bf16[4,256,1152]{2,0,1:T(4,128)(2,1)}, u32[]{:S(2)}, u32[]{:S(2)}) %all-to-all-start.2) | async-done | bytes 2359328 | tf_op jit(solution)/shard_map/all_to_all | solution.py:343
  904.7 4.6 all-to-all-start.5
  910.8 12.8 %reduce-scatter.17.cloned.1.call-done = bf16[144,6144]{1,0:T(8,128)(2,1)} async-done(((bf16[1152,6144]{1,0:T(8,128)(2,1)}), bf16[144,6144]{1,0:T(8,128)(2,1)}) %reduce-scatter.17.cloned.1.call-update) | async-done | bytes 1769488 | tf_op jit(solution)/shard_map/reduce_scatter | solution.py:215
  927.4 81.0 %all_gather.28 = bf16[32,2,72]{2,1,0:T(2,128)(2,1)S(1)} all-gather(bf16[1,2,72]{2,1,0:T(2,128)(2,1)S(1)} %fusion.83), channel_id=1, replica_groups=mesh['dp'=8,'mp'=4] {'dp','mp'}, dimensions={0}, use_global_device_ids=true | all-gather | bytes 9504 | tf_op jit(solution)/shard_map/all_gather | solution.py:394
  1017.7 3.5 copy.206
  1024.7 5.6 gather_fusion.9
  1030.3 5.4 select_select_fusion
  1035.7 13.3 %reduce-scatter.23.cloned.1.call-done = bf16[1,144,768]{2,1,0:T(8,128)(2,1)} async-done(((bf16[4,144,768]{2,1,0:T(8,128)(2,1)}), bf16[1,144,768]{2,1,0:T(8,128)(2,1)}) %reduce-scatter.23.cloned.1.call-update) | async-done | bytes 221200 | tf_op jit(solution)/shard_map/reduce_scatter | solution.py:217
  1050.7 26.7 %reduce-scatter.11.cloned.1.call-done = bf16[1,144,864]{2,1,0:T(8,128)(2,1)} async-done(((bf16[4,144,864]{2,1,0:T(8,128)(2,1)}), bf16[1,144,864]{2,1,0:T(8,128)(2,1)}) %reduce-scatter.11.cloned.1.call-update) | async-done | bytes 248848 | tf_op jit(solution)/shard_map/reduce_scatter | solution.py:217
  1080.0 36.8 %reduce-scatter.19.cloned.1.call-done = bf16[1,144,1536]{2,1,0:T(8,128)(2,1)} async-done(((bf16[4,144,1536]{2,1,0:T(8,128)(2,1)}), bf16[1,144,1536]{2,1,0:T(8,128)(2,1)}) %reduce-scatter.19.cloned.1.call-update) | async-done | bytes 442384 | tf_op jit(solution)/shard_map/reduce_scatter | solution.py:217
  (267 shorter events, 81.6 us)
Async XLA Ops:
  7.2 202.8 %copy-start = (bf16[1000,1152]{1,0:T(8,128)(2,1)S(1)}, bf16[1000,1152]{1,0:T(8,128)(2,1)}, u32[]{:S(2)}) copy-start(bf16[1000,1152]{1,0:T(8,128)(2,1)} %param.26) | copy-start | bytes 6912004
  7.2 221.7 %all-gather.17.cloned.1.call-start = ((), (), s32[]{:S(2)}) async-start(), calls=%async_computation.26 | async-start | bytes 3041280 | tf_op jit(solution)/shard_map/all_gather | solution.py:208
  9.0 286.2 %all-gather.15.cloned.1.call-start = ((), (), s32[]{:S(2)}) async-start(), calls=%async_computation.25 | async-start | bytes 8515584 | tf_op jit(solution)/shard_map/all_gather | solution.py:208
  18.9 13.0 %copy-start.48 = (s32[8]{0:T(128)S(1)}, s32[8]{0:T(128)}, u32[]{:S(2)}) copy-start(s32[8]{0:T(128)} %param.23) | copy-start | bytes 100
  18.9 15.1 %copy-start.8 = (s32[8]{0:T(128)S(1)}, s32[8]{0:T(128)}, u32[]{:S(2)}) copy-start(s32[8]{0:T(128)} %param.24) | copy-start | bytes 100
  19.7 339.5 %all-gather.9.cloned.1.call-start = ((), (), s32[]{:S(2)}) async-start(), calls=%async_computation.14 | async-start | bytes 14598144 | tf_op jit(solution)/shard_map/all_gather | solution.py:208
  32.1 93.0 %copy-start.6 = (s32[8]{0:T(128)}, s32[8]{0:T(128)S(1)}, u32[]{:S(2)}) copy-start(s32[8]{0:T(128)S(1)} %bitcast_subtract_fusion.2) | copy-start | bytes 100
  33.9 7.1 copy-start.36
  46.1 70.3 %all-to-all-start = ((bf16[32,64,1152]{2,1,0:T(8,128)(2,1)}), bf16[32,64,1152]{2,1,0:T(8,128)(2,1)}, u32[]{:S(2)}, u32[]{:S(2)}) async-start(bf16[32,64,1152]{2,1,0:T(8,128)(2,1)} %broadcast_select_fusion), calls=%async_computation | async-start | bytes 9437184 | tf_op jit(solution)/shard_map/all_to_all | solution.py:281
  51.2 364.8 %all-gather.11.cloned.1.call-start = ((), (), s32[]{:S(2)}) async-start(), calls=%async_computation.15 | async-start | bytes 7299072 | tf_op jit(solution)/shard_map/all_gather | solution.py:208
  54.0 22.6 %copy-start.51 = (s32[32]{0:T(128)S(1)}, s32[32]{0:T(128)}, u32[]{:S(2)}) copy-start(s32[32]{0:T(128)} %param.22) | copy-start | bytes 388
  54.0 22.6 %copy-start.52 = (s32[32]{0:T(128)S(1)}, s32[32]{0:T(128)}, u32[]{:S(2)}) copy-start(s32[32]{0:T(128)} %param.21) | copy-start | bytes 388
  76.5 47.0 %copy-start.45 = (bf16[2,72]{1,0:T(2,128)(2,1)S(1)}, bf16[2,72]{1,0:T(2,128)(2,1)}, u32[]{:S(2)}) copy-start(bf16[2,72]{1,0:T(2,128)(2,1)} %param.29) | copy-start | bytes 868
  76.5 47.1 %copy-start.4 = (s32[72]{0:T(128)S(1)}, s32[72]{0:T(128)}, u32[]{:S(2)}) copy-start(s32[72]{0:T(128)} %constant.273.clone) | copy-start | bytes 868
  116.4 88.0 %all-to-all-start.3 = ((bf16[16,64,1152]{2,1,0:T(8,128)(2,1)}), bf16[16,64,1152]{2,1,0:T(8,128)(2,1)}, u32[]{:S(2)}, u32[]{:S(2)}) async-start(bf16[16,64,1152]{2,1,0:T(8,128)(2,1)} %param.20), calls=%async_computation.3 | async-start | bytes 4718592 | tf_op jit(solution)/shard_map/all_to_all | solution.py:288
  125.4 84.2 %copy-start.37 = (s32[128]{0:T(128)}, s32[128]{0:T(128)S(1)}, u32[]{:S(2)}) copy-start(s32[128]{0:T(128)S(1)} %get-tuple-element.22) | copy-start | bytes 1540
  125.4 84.5 %copy-start.43 = (s32[128]{0:T(128)}, s32[128]{0:T(128)S(1)}, u32[]{:S(2)}) copy-start(s32[128]{0:T(128)S(1)} %get-tuple-element.21) | copy-start | bytes 1540
  125.6 99.0 %copy-start.46 = (f32[4]{0:T(128)}, f32[4]{0:T(128)S(1)}, u32[]{:S(2)}) copy-start(f32[4]{0:T(128)S(1)} %dynamic_slice.47) | copy-start | bytes 52
  131.5 78.0 %copy-start.41 = (f32[2]{0:T(128)S(1)}, f32[2]{0:T(128)}, u32[]{:S(2)}) copy-start(f32[2]{0:T(128)} %constant.279) | copy-start | bytes 28
  131.5 78.1 %copy-start.29 = (bf16[16,1152]{1,0:T(8,128)(2,1)S(1)}, bf16[16,1152]{1,0:T(8,128)(2,1)}, u32[]{:S(2)}) copy-start(bf16[16,1152]{1,0:T(8,128)(2,1)} %param.25) | copy-start | bytes 110596
  204.4 79.6 %all-to-all-start.1 = ((bf16[16,64,1152]{2,1,0:T(8,128)(2,1)}), bf16[16,64,1152]{2,1,0:T(8,128)(2,1)}, u32[]{:S(2)}, u32[]{:S(2)}) async-start(bf16[16,64,1152]{2,1,0:T(8,128)(2,1)} %broadcast_select_fusion.2), calls=%async_computation.1 | async-start | bytes 4718592 | tf_op jit(solution)/shard_map/all_to_all | solution.py:287
  208.9 642.7 %reduce-scatter.13.cloned.1.call-start = ((), (), s32[]{:S(2)}) async-start(), calls=%async_computation.19 | async-start | bytes 3981312 | tf_op jit(solution)/shard_map/reduce_scatter | solution.py:215
  211.8 10.5 copy-start.16
  222.4 6.5 copy-start.25
  222.4 68.3 %copy-start.17 = (f32[4,1152]{1,0:T(4,128)}, f32[4,1152]{1,0:T(4,128)S(1)}, u32[]{:S(2)}) copy-start(f32[4,1152]{1,0:T(4,128)S(1)} %get-tuple-element.42) | copy-start | bytes 55300
  222.4 68.3 %copy-start.19 = (f32[4,1152]{1,0:T(4,128)}, f32[4,1152]{1,0:T(4,128)S(1)}, u32[]{:S(2)}) copy-start(f32[4,1152]{1,0:T(4,128)S(1)} %get-tuple-element.41) | copy-start | bytes 55300
  222.4 124.0 %copy-start.23 = (f32[4,1152]{1,0:T(4,128)}, f32[4,1152]{1,0:T(4,128)S(1)}, u32[]{:S(2)}) copy-start(f32[4,1152]{1,0:T(4,128)S(1)} %get-tuple-element.43) | copy-start | bytes 55300
  290.5 14.3 %copy-start.21 = (f32[16,64]{1,0:T(8,128)}, f32[16,64]{1,0:T(8,128)S(1)}, u32[]{:S(2)}) copy-start(f32[16,64]{1,0:T(8,128)S(1)} %multiply_add_fusion) | copy-start | bytes 12292
  290.6 14.2 %copy-start.30 = (f32[4,256]{1,0:T(4,128)}, f32[4,256]{1,0:T(4,128)S(1)}, u32[]{:S(2)}) copy-start(f32[4,256]{1,0:T(4,128)S(1)} %add.535) | copy-start | bytes 12292
  290.6 14.2 %copy-start.27 = (f32[4,256]{1,0:T(4,128)}, f32[4,256]{1,0:T(4,128)S(1)}, u32[]{:S(2)}) copy-start(f32[4,256]{1,0:T(4,128)S(1)} %rsqrt.28) | copy-start | bytes 12292
  320.3 26.1 %copy-start.13 = (bf16[4,288,1152,1]{2,1,0,3:T(8,128)(2,1)S(1)}, bf16[4,288,1152,1]{2,1,0,3:T(8,128)(2,1)}, u32[]{:S(2)}) copy-start(bf16[4,288,1152,1]{2,1,0,3:T(8,128)(2,1)} %reshape.1070) | copy-start | bytes 7962628
  346.4 8.4 copy-start.2
  578.3 14.6 %copy-start.26 = (f32[4,1152]{1,0:T(4,128)S(1)}, f32[4,1152]{1,0:T(4,128)}, u32[]{:S(2)}) copy-start(f32[4,1152]{1,0:T(4,128)} %copy-done.25) | copy-start | bytes 55300
  578.3 14.6 %copy-start.47 = (f32[4]{0:T(128)S(1)}, f32[4]{0:T(128)}, u32[]{:S(2)}) copy-start(f32[4]{0:T(128)} %copy-done.46) | copy-start | bytes 52
  592.9 24.9 %copy-start.24 = (f32[4,1152]{1,0:T(4,128)S(1)}, f32[4,1152]{1,0:T(4,128)}, u32[]{:S(2)}) copy-start(f32[4,1152]{1,0:T(4,128)} %copy-done.23) | copy-start | bytes 55300
  625.0 227.2 %reduce-scatter.21.cloned.1.call-start = ((), (), s32[]{:S(2)}) async-start(), calls=%async_computation.23 | async-start | bytes 7962624 | tf_op jit(solution)/shard_map/reduce_scatter | solution.py:215
  637.3 228.1 %reduce-scatter.9.cloned.1.call-start = ((), (), s32[]{:S(2)}) async-start(), calls=%async_computation.17 | async-start | bytes 8957952 | tf_op jit(solution)/shard_map/reduce_scatter | solution.py:215
  711.9 211.7 %reduce-scatter.17.cloned.1.call-start = ((), (), s32[]{:S(2)}) async-start(), calls=%async_computation.21 | async-start | bytes 15925248 | tf_op jit(solution)/shard_map/reduce_scatter | solution.py:215
  755.2 10.8 copy-start.28
  755.2 26.8 %slice-start = ((s8[4718592]{0:T(1024)(128)(4,1)}), s8[524288]{0:T(1024)(128)(4,1)S(1)}, s32[]{:S(2)}) async-start(s8[4718592]{0:T(1024)(128)(4,1)} %bitcast.313), calls=%async_computation.27 | async-start | bytes 1048576
  766.0 16.0 %copy-start.31 = (f32[4,256]{1,0:T(4,128)S(1)}, f32[4,256]{1,0:T(4,128)}, u32[]{:S(2)}) copy-start(f32[4,256]{1,0:T(4,128)} %copy-done.30) | copy-start | bytes 12292
  766.0 16.0 %slice-start.1 = ((s8[4718592]{0:T(1024)(128)(4,1)}), s8[4194304]{0:T(1024)(128)(4,1)S(1)}, s32[]{:S(2)}) async-start(s8[4718592]{0:T(1024)(128)(4,1)} %bitcast.313), calls=%async_computation.28 | async-start | bytes 8388608
  785.3 7.9 copy-start.35
  785.3 7.9 copy-start.33
  785.3 7.9 copy-start.32
  785.3 8.0 copy-start.34
  788.5 58.3 %all-to-all-start.4 = ((bf16[4,256,1152]{2,0,1:T(4,128)(2,1)}), bf16[4,256,1152]{2,0,1:T(4,128)(2,1)}, u32[]{:S(2)}, u32[]{:S(2)}) async-start(bf16[4,256,1152]{2,0,1:T(4,128)(2,1)} %copy.210), calls=%async_computation.4 | async-start | bytes 4718592 | tf_op jit(solution)/shard_map/all_to_all | solution.py:371
  793.1 216.0 %all-gather.13.cloned.1.call-start = ((), (), s32[]{:S(2)}) async-start(), calls=%async_computation.16 | async-start | bytes 2433024 | tf_op jit(solution)/shard_map/all_gather | solution.py:393
  798.9 55.5 %copy-start.7 = (s32[8]{0:T(128)S(1)}, s32[8]{0:T(128)}, u32[]{:S(2)}) copy-start(s32[8]{0:T(128)} %copy-done.6) | copy-start | bytes 100
  846.8 57.9 %all-to-all-start.2 = ((bf16[4,256,1152]{2,0,1:T(4,128)(2,1)}), bf16[4,256,1152]{2,0,1:T(4,128)(2,1)}, u32[]{:S(2)}, u32[]{:S(2)}) async-start(bf16[4,256,1152]{2,0,1:T(4,128)(2,1)} %copy.205), calls=%async_computation.2 | async-start | bytes 4718592 | tf_op jit(solution)/shard_map/all_to_all | solution.py:343
  851.5 171.6 %reduce-scatter.15.cloned.1.call-start = ((), (), s32[]{:S(2)}) async-start(), calls=%async_computation.20 | async-start | bytes 552960 | tf_op jit(solution)/shard_map/reduce_scatter | solution.py:217
  852.1 196.9 %reduce-scatter.23.cloned.1.call-start = ((), (), s32[]{:S(2)}) async-start(), calls=%async_computation.24 | async-start | bytes 1105920 | tf_op jit(solution)/shard_map/reduce_scatter | solution.py:217
  854.3 223.0 %reduce-scatter.11.cloned.1.call-start = ((), (), s32[]{:S(2)}) async-start(), calls=%async_computation.18 | async-start | bytes 1290240 | tf_op jit(solution)/shard_map/reduce_scatter | solution.py:217
  874.4 35.1 %copy-start.49 = (s32[8]{0:T(128)S(1)}, s32[8]{0:T(128)}, u32[]{:S(2)}) copy-start(s32[8]{0:T(128)} %param.23) | copy-start | bytes 100
  874.4 35.7 %copy-start.50 = (s32[32]{0:T(128)S(1)}, s32[32]{0:T(128)}, u32[]{:S(2)}) copy-start(s32[32]{0:T(128)} %get-tuple-element.60) | copy-start | bytes 388
  874.4 35.7 %copy-start.9 = (s32[8]{0:T(128)S(1)}, s32[8]{0:T(128)}, u32[]{:S(2)}) copy-start(s32[8]{0:T(128)} %param.24) | copy-start | bytes 100
  904.7 120.0 %all-to-all-start.5 = ((bf16[32,64,1152]{2,1,0:T(8,128)(2,1)}), bf16[32,64,1152]{2,1,0:T(8,128)(2,1)}, u32[]{:S(2)}, u32[]{:S(2)}) async-start(bf16[32,64,1152]{2,1,0:T(8,128)(2,1)} %broadcast_select_fusion.1), calls=%async_computation.5 | async-start | bytes 9437184 | tf_op jit(solution)/shard_map/all_to_all | solution.py:375
  909.3 17.8 %copy-start.5 = (s32[72]{0:T(128)S(1)}, s32[72]{0:T(128)}, u32[]{:S(2)}) copy-start(s32[72]{0:T(128)} %constant.273.clone) | copy-start | bytes 868
  909.4 18.0 %copy-start.42 = (f32[2]{0:T(128)S(1)}, f32[2]{0:T(128)}, u32[]{:S(2)}) copy-start(f32[2]{0:T(128)} %constant.279) | copy-start | bytes 28
  909.4 207.4 %reduce-scatter.19.cloned.1.call-start = ((), (), s32[]{:S(2)}) async-start(), calls=%async_computation.22 | async-start | bytes 2211840 | tf_op jit(solution)/shard_map/reduce_scatter | solution.py:217
  926.4 87.2 %copy-start.38 = (s32[128]{0:T(128)S(1)}, s32[128]{0:T(128)}, u32[]{:S(2)}) copy-start(s32[128]{0:T(128)} %copy-done.37) | copy-start | bytes 1540
  926.4 88.0 %copy-start.44 = (s32[128]{0:T(128)S(1)}, s32[128]{0:T(128)}, u32[]{:S(2)}) copy-start(s32[128]{0:T(128)} %copy-done.43) | copy-start | bytes 1540
  1030.3 89.0 %copy-start.1 = (bf16[1000,1152]{1,0:T(8,128)(2,1)S(1)}, bf16[1000,1152]{1,0:T(8,128)(2,1)}, u32[]{:S(2)}) copy-start(bf16[1000,1152]{1,0:T(8,128)(2,1)} %param.26) | copy-start | bytes 6912004
  1030.3 47.1 %copy-start.40 = (s32[864]{0:T(1024)S(1)}, s32[864]{0:T(1024)}, u32[]{:S(2)}) copy-start(s32[864]{0:T(1024)} %copy-done.39) | copy-start | bytes 10372
  (10 other events, 36.7 us)
Sparse Core Ops, SparseCore 0:
  11.5 65.3 all-gather.16
  80.4 122.1 all-gather.14
  206.0 135.9 all-gather.8
  345.4 70.6 all-gather.10
  625.1 46.6 reduce-scatter.12
  675.1 65.4 reduce-scatter.20
  744.6 70.0 reduce-scatter.8
  818.2 105.2 reduce-scatter.16
  926.9 73.9 all-gather.12
  1003.1 19.9 reduce-scatter.14
  1026.1 22.8 reduce-scatter.22
  1051.2 26.0 reduce-scatter.10
  1079.7 37.0 reduce-scatter.18

commit v2 on v1

--- a/solution.py
+++ b/solution.py
@@ -1,3 +1,5 @@
+import math
+
 import jax
 import jax.numpy as jnp
 from jax import lax
@@ -187,8 +189,228 @@
     )(proj, cot, gains, *tables)
 
 
-def swish_mul(gate_part, up_part):
-    return jax.nn.silu(gate_part) * up_part
+def sigmoid(values):
+    return 1.0 / (1.0 + jnp.exp(-values))
+
+
+def mlp_kernel(x_ref, w_ref, d_ref, save_ref, out_ref):
+    first = (pl.program_id(0) == 0) & (pl.program_id(1) == 0)
+    step = math.gcd(x_ref.shape[0], 256)
+
+    def body(index, carry):
+        rows = pl.ds(pl.multiple_of(index * step, step), step)
+        x_rows = x_ref[rows, :]
+        gate = dot_11(x_rows, w_ref[0, 0])
+        up = dot_11(x_rows, w_ref[0, 1])
+        save_ref[0, 0, rows, :] = gate
+        save_ref[0, 1, rows, :] = up
+        hidden = (gate * sigmoid(gate) * up).astype(bf16)
+        part = dot_10(hidden, d_ref[0])
+
+        @pl.when(first)
+        def _():
+            out_ref[rows, :] = part
+
+        @pl.when(jnp.logical_not(first))
+        def _():
+            out_ref[rows, :] += part
+
+        return carry
+
+    lax.fori_loop(0, x_ref.shape[0] // step, body, 0)
+
+
+def mlp(x, expand, down):
+    groups, _, units, width = expand.shape
+    tokens = x.shape[0]
+    block = math.gcd(units, 384)
+    return pl.pallas_call(
+        mlp_kernel,
+        grid=(groups, units // block),
+        in_specs=[
+            pl.BlockSpec((tokens, width), lambda g, h: (0, 0)),
+            pl.BlockSpec((1, 2, block, width), lambda g, h: (g, 0, h, 0)),
+            pl.BlockSpec((1, block, width), lambda g, h: (g, h, 0)),
+        ],
+        out_specs=[
+            pl.BlockSpec((1, 2, tokens, block), lambda g, h: (g, 0, 0, h)),
+            pl.BlockSpec((tokens, width), lambda g, h: (0, 0)),
+        ],
+        out_shape=[
+            jax.ShapeDtypeStruct((groups, 2, tokens, units), f32),
+            jax.ShapeDtypeStruct((tokens, width), f32),
+        ],
+        compiler_params=pltpu.CompilerParams(vmem_limit_bytes=56 << 20),
+        cost_estimate=pl.CostEstimate(
+            flops=6 * groups * units * tokens * width,
+            bytes_accessed=8 * groups * units * tokens + 6 * groups * units * width,
+            transcendentals=groups * units * tokens,
+        ),
+        name="mlp",
+    )(x, expand, down)
+
+
+def fill_rows(order_ref, source_ref, target_ref):
+    blocks, rows = source_ref.shape[0], source_ref.shape[1]
+    for place in range(blocks):
+        target_ref[place * rows : (place + 1) * rows, :] = source_ref[order_ref[place]]
+
+
+def mlp_back_kernel(
+    m_ref, e_ref, xt_ref, lowt_ref, low_ref, save_ref, w_ref, d_ref,
+    keep_ref, send_ref, two_ref, xs, lows, parts,
+):
+    first = (pl.program_id(0) == 0) & (pl.program_id(1) == 0)
+    tokens, width = low_ref.shape
+    step = math.gcd(tokens, 256)
+
+    @pl.when(first)
+    def _():
+        fill_rows(e_ref, xt_ref, xs)
+        fill_rows(e_ref, lowt_ref, lows)
+
+    def body(index, carry):
+        rows = pl.ds(pl.multiple_of(index * step, step), step)
+        hidden_grad = dot_11(low_ref[rows, :], d_ref[0])
+        gate = save_ref[0, 0, rows, :]
+        up = save_ref[0, 1, rows, :]
+        sig = sigmoid(gate)
+        swish = gate * sig
+        gate_low = (hidden_grad * up * (sig + swish * (1.0 - sig))).astype(bf16)
+        up_low = (hidden_grad * swish).astype(bf16)
+        parts[0, rows, :] = gate_low
+        parts[1, rows, :] = up_low
+        parts[2, rows, :] = (swish * up).astype(bf16)
+        part = dot_10(gate_low, w_ref[0, 0]) + dot_10(up_low, w_ref[0, 1])
+
+        @pl.when(first)
+        def _():
+            two_ref[rows, :] = part
+
+        @pl.when(jnp.logical_not(first))
+        def _():
+            two_ref[rows, :] += part
+
+        return carry
+
+    lax.fori_loop(0, tokens // step, body, 0)
+    half = width // 2
+    tile = math.gcd(half, 288)
+
+    for out_ref, base in ((keep_ref, 0), (send_ref, half)):
+
+        def grads(index, carry):
+            place = pl.multiple_of(index * tile, tile)
+            rows = pl.ds(pl.multiple_of(base + place, tile), tile)
+            x_rows = xs[rows, :]
+            for kind in range(2):
+                out_ref[0, kind, pl.ds(place, tile), :] = dot_10(x_rows, parts[kind]).astype(bf16)
+            out_ref[0, 2, pl.ds(place, tile), :] = dot_10(lows[rows, :], parts[2]).astype(bf16)
+            return carry
+
+        lax.fori_loop(0, half // tile, grads, 0)
+
+
+def mlp_back(m_order, e_order, xt, lowt, low, save, expand, down):
+    units, width = down.shape[1:]
+    tokens = low.shape[0]
+    blocks = m_order.shape[0]
+    block = math.gcd(units, 384)
+    whole = lambda p, h, m, e: (0, 0)
+    whole3 = lambda p, h, m, e: (0, 0, 0)
+    half = jax.ShapeDtypeStruct((blocks, 3, width // 2, units), bf16)
+    half_spec = pl.BlockSpec((1, 3, width // 2, block), lambda p, h, m, e: (p, 0, 0, h))
+    return pl.pallas_call(
+        mlp_back_kernel,
+        grid_spec=pltpu.PrefetchScalarGridSpec(
+            num_scalar_prefetch=2,
+            grid=(blocks, units // block),
+            in_specs=[
+                pl.BlockSpec(xt.shape, whole3),
+                pl.BlockSpec(lowt.shape, whole3),
+                pl.BlockSpec((tokens, width), whole),
+                pl.BlockSpec((1, 2, tokens, block), lambda p, h, m, e: (m[p], 0, 0, h)),
+                pl.BlockSpec((1, 2, block, width), lambda p, h, m, e: (m[p], 0, h, 0)),
+                pl.BlockSpec((1, block, width), lambda p, h, m, e: (m[p], h, 0)),
+            ],
+            out_specs=[half_spec, half_spec, pl.BlockSpec((tokens, width), whole)],
+            scratch_shapes=[
+                pltpu.VMEM((width, tokens), bf16),
+                pltpu.VMEM((width, tokens), bf16),
+                pltpu.VMEM((3, tokens, block), bf16),
+            ],
+        ),
+        out_shape=[half, half, jax.ShapeDtypeStruct((tokens, width), f32)],
+        compiler_params=pltpu.CompilerParams(vmem_limit_bytes=60 << 20),
+        cost_estimate=pl.CostEstimate(
+            flops=12 * blocks * units * tokens * width,
+            bytes_accessed=8 * blocks * units * tokens + 12 * blocks * units * width,
+            transcendentals=blocks * units * tokens,
+        ),
+        name="mlp_back",
+    )(m_order, e_order, xt, lowt, low, save, expand, down)
+
+
+def attend_grads_kernel(
+    m_ref, e_ref, xt_ref, lowt_ref, proj_ref, att_ref, keep_ref, send_ref, xs, lows
+):
+    @pl.when(pl.program_id(0) == 0)
+    def _():
+        fill_rows(e_ref, xt_ref, xs)
+        fill_rows(e_ref, lowt_ref, lows)
+
+    width = xs.shape[0]
+    half = width // 2
+    tile = math.gcd(half, 288)
+    columns = proj_ref.shape[1]
+
+    for out_ref, base in ((keep_ref, 0), (send_ref, half)):
+
+        def grads(index, carry):
+            place = pl.multiple_of(index * tile, tile)
+            rows = pl.ds(pl.multiple_of(base + place, tile), tile)
+            part = dot_11(xs[rows, :], proj_ref[0]).astype(bf16)
+            out_ref[0, pl.ds(place, tile), :columns] = part
+            part = dot_11(lows[rows, :], att_ref[0]).astype(bf16)
+            out_ref[0, pl.ds(place, tile), columns:] = part
+            return carry
+
+        lax.fori_loop(0, half // tile, grads, 0)
+
+
+def attend_grads(m_order, e_order, xt, lowt, proj, att):
+    rows, tokens = att.shape[1:]
+    width = xt.shape[0] * xt.shape[1]
+    blocks = m_order.shape[0]
+    whole3 = lambda p, m, e: (0, 0, 0)
+    half = jax.ShapeDtypeStruct((blocks, width // 2, 4 * rows), bf16)
+    half_spec = pl.BlockSpec((1, width // 2, 4 * rows), lambda p, m, e: (p, 0, 0))
+    return pl.pallas_call(
+        attend_grads_kernel,
+        grid_spec=pltpu.PrefetchScalarGridSpec(
+            num_scalar_prefetch=2,
+            grid=(blocks,),
+            in_specs=[
+                pl.BlockSpec(xt.shape, whole3),
+                pl.BlockSpec(lowt.shape, whole3),
+                pl.BlockSpec((1, 3 * rows, tokens), lambda p, m, e: (m[p], 0, 0)),
+                pl.BlockSpec((1, rows, tokens), lambda p, m, e: (m[p], 0, 0)),
+            ],
+            out_specs=[half_spec, half_spec],
+            scratch_shapes=[
+                pltpu.VMEM((width, tokens), bf16),
+                pltpu.VMEM((width, tokens), bf16),
+            ],
+        ),
+        out_shape=[half, half],
+        compiler_params=pltpu.CompilerParams(vmem_limit_bytes=56 << 20),
+        cost_estimate=pl.CostEstimate(
+            flops=8 * blocks * rows * tokens * width,
+            bytes_accessed=8 * blocks * rows * (tokens + width),
+            transcendentals=0,
+        ),
+        name="attend_grads",
+    )(m_order, e_order, xt, lowt, proj, att)
 
 
 def dot(a, b):
@@ -211,10 +433,42 @@
     return whole
 
 
-def reduce_grad(grad, mp_size):
-    rows = lax.psum_scatter(grad, "dp", scatter_dimension=0, tiled=True)
-    rows = rows.reshape(rows.shape[0], mp_size, -1).swapaxes(0, 1)
-    return lax.psum_scatter(rows, "mp", scatter_dimension=0, tiled=False).astype(f32)
+def bits_of(size):
+    return [1 << i for i in range(size.bit_length() - 1)]
+
+
+def swap(values, axis, bit):
+    size = lax.axis_size(axis)
+    return lax.ppermute(values, axis, [(i, i ^ bit) for i in range(size)])
+
+
+def xor_gather(values, axes_bits):
+    names = sorted({axis for axis, _ in axes_bits})
+    places = [{name: 0 for name in names}]
+    values = values[None]
+    for axis, bit in axes_bits:
+        values = jnp.concatenate([values, swap(values, axis, bit)], axis=0)
+        places = places + [dict(place, **{axis: place[axis] ^ bit}) for place in places]
+    return values, {name: [place[name] for place in places] for name in names}
+
+
+def halving_order(bits):
+    order = [0]
+    for bit in reversed(bits):
+        order = order + [place ^ bit for place in order]
+    return order
+
+
+def add_low(kept, received):
+    return (kept.astype(f32) + received.astype(f32)).astype(bf16)
+
+
+def halve(values, axis, bits, dim):
+    for bit in bits:
+        size = values.shape[dim] // 2
+        received = swap(lax.slice_in_dim(values, size, 2 * size, axis=dim), axis, bit)
+        values = add_low(lax.slice_in_dim(values, 0, size, axis=dim), received)
+    return values
 
 
 def shards(
@@ -244,7 +498,6 @@
     head_dim = norm_gains.shape[1]
     local_dim = out_weight.shape[0]
     unit_count = down_weight.shape[0]
-    units = unit_count * mp_size
     own = images // mp_size
     total_images = images * dp_size
     order = jnp.array(feature_order(head_dim)[0])
@@ -287,20 +540,40 @@
     latent = lax.all_to_all(latent, "mp", split_axis=0, concat_axis=1, tiled=True)
     cot = lax.all_to_all(cotangent, "mp", split_axis=0, concat_axis=1, tiled=True)
 
-    info = lax.all_gather(jnp.stack([time_bins, labels]), "dp", axis=1, tiled=True)
-    slot_all = jnp.arange(dp_size * capacity)
-    live_all = (slot_all % capacity) < jnp.repeat(image_counts, capacity)
+    info, info_places = xor_gather(
+        jnp.stack([time_bins, labels]), [("dp", bit) for bit in bits_of(dp_size)]
+    )
+    info = info.swapaxes(0, 1).reshape(2, -1)
+    info_owner = jnp.repeat(dp_index ^ jnp.array(info_places["dp"]), capacity)
+    info_slot = jnp.tile(jnp.arange(capacity), dp_size)
+    info_count = jnp.sum(
+        jnp.where(info_owner[:, None] == device_ids[None, :], image_counts[None, :], 0), axis=1
+    )
+    live_all = info_slot < info_count
     bin_totals = jnp.sum(
         ((info[0][:, None] == jnp.arange(NBINS)[None, :]) & live_all[:, None]).astype(f32), axis=0
     )
-    row_all = jnp.arange(total_images)
-    rank_all = (row_all % images) * dp_size + jnp.repeat(inverse, images)
+    gather_bits = [("mp", bit) for bit in bits_of(mp_size)[::-1]]
+    gather_bits = gather_bits + [("dp", bit) for bit in bits_of(dp_size)[::-1]]
+    places = {"dp": [0], "mp": [0]}
+    for axis, bit in gather_bits:
+        places = {
+            name: places[name] + [place ^ (bit if name == axis else 0) for place in places[name]]
+            for name in places
+        }
+    owner_all = jnp.repeat(dp_index ^ jnp.array(places["dp"]), own)
+    group_all = jnp.repeat(mp_index ^ jnp.array(places["mp"]), own)
+    row_all = group_all * own + jnp.tile(jnp.arange(own), dp_size * mp_size)
+    place_all = jnp.sum(
+        jnp.where(owner_all[:, None] == device_ids[None, :], inverse[None, :], 0), axis=1
+    )
+    rank_all = row_all * dp_size + place_all
     source_all = jnp.sum((finish[None, :] <= rank_all[:, None]).astype(jnp.int32), axis=1)
     start_all = jnp.sum(
         jnp.where(source_all[:, None] == device_ids[None, :], starts[None, :], 0), axis=1
     )
     slots_all = source_all * capacity + rank_all - start_all
-    slot_hit = slots_all[:, None] == slot_all[None, :]
+    slot_hit = slots_all[:, None] == (info_owner * capacity + info_slot)[None, :]
     bins_all = jnp.sum(jnp.where(slot_hit, info[0][None, :], 0), axis=1)
     labels_all = jnp.sum(jnp.where(slot_hit, info[1][None, :], 0), axis=1)
     bin_hot = (bins_all[:, None] == jnp.arange(NBINS)[None, :])
@@ -310,9 +583,8 @@
     label_hot = label_hot.astype(bf16)
     cond_all = (dot(bin_hot, time_table) + dot(label_hot, class_table)).astype(bf16).astype(f32)
     silu_all = jax.nn.silu(cond_all).astype(bf16)
-    first = dp_index * images + mp_index * own
-    silu_cond = lax.dynamic_slice_in_dim(silu_all, first, own, 0)
-    weights = lax.dynamic_slice_in_dim(weights_all, first, own, 0)
+    silu_cond = silu_all[:own]
+    weights = weights_all[:own]
 
     modulation = dot(silu_cond, ada_weight.reshape(model_width, 6 * model_width))
     modulation = modulation.reshape(own, 6, 1, model_width)
@@ -335,33 +607,65 @@
     middle = latent_f + gate_one * branch_one
     normed_two = rms_scale(middle, scale_two, shift_two).astype(bf16)
     two_flat = normed_two.reshape(-1, model_width)
-    expanded = ein("nd,fd->nf", two_flat, expand_full).reshape(-1, mp_size, 2, unit_count)
-    swish_val, swish_pull = jax.vjp(swish_mul, expanded[:, :, 0], expanded[:, :, 1])
-    hidden = swish_val.astype(bf16).reshape(-1, units)
-    branch_two = dot(hidden, down_full).reshape(own, length, model_width)
+    expand_blocks = expand_full.reshape(mp_size, 2, unit_count, model_width)
+    down_blocks = down_full.reshape(mp_size, unit_count, model_width)
+    save, branch_two = mlp(two_flat, expand_blocks, down_blocks)
+    branch_two = branch_two.reshape(own, length, model_width)
     result = (middle + gate_two * branch_two).astype(bf16)
     result = lax.all_to_all(result, "mp", split_axis=1, concat_axis=0, tiled=True)
 
     down_low = (gate_two * out_cot).astype(bf16)
     gate_two_grad = jnp.sum(out_cot * branch_two, axis=1)
     down_low = down_low.reshape(-1, model_width)
-    down_term = ein("nd,nf->df", down_low, hidden).astype(bf16)
-    hidden_grad = ein("nd,fd->nf", down_low, down_full).reshape(-1, mp_size, unit_count)
-    gate_grad, up_grad = swish_pull(hidden_grad)
-    expand_low = jnp.stack([gate_grad, up_grad], 2).astype(bf16).reshape(-1, 2 * units)
-    expand_term = ein("nd,nf->df", two_flat, expand_low).astype(bf16)
-    two_grad = ein("nf,fd->nd", expand_low, expand_full).reshape(own, length, model_width)
+    dp_bits = bits_of(dp_size)
+    dp_bits = (dp_bits, dp_bits[:1] + dp_bits[1:][::-1])
+    mp_bits = bits_of(mp_size)
+    e_orders = [(dp_index ^ jnp.array(halving_order(bits))).astype(jnp.int32) for bits in dp_bits]
+    m_order = (mp_index ^ jnp.array(halving_order(mp_bits))).astype(jnp.int32)
+    m_orders = (m_order[: mp_size // 2], m_order[mp_size // 2 :])
+
+    def by_owner(values):
+        return values.T.reshape(dp_size, model_width // dp_size, -1)
+
+    def reduce(kept, sent, which, dim):
+        kept = add_low(kept, swap(sent, "dp", dp_bits[which][0]))
+        return halve(kept, "dp", dp_bits[which][1:], dim)
+
+    def reduce_mp(kept, sent):
+        kept = add_low(kept, swap(sent, "mp", mp_bits[0]))
+        return halve(kept, "mp", mp_bits[1:], 0)[0].astype(f32)
+
+    two_t, down_t = by_owner(two_flat), by_owner(down_low)
+    mlp_parts, two_parts = [None, None], [None, None]
+    for which in (1, 0):
+        kept, sent, two_parts[which] = mlp_back(
+            m_orders[which], e_orders[which], two_t, down_t, down_low, save, expand_blocks, down_blocks
+        )
+        mlp_parts[which] = reduce(kept, sent, which, 2)
+    mlp_grad = reduce_mp(*mlp_parts)
+    two_grad = (two_parts[0] + two_parts[1]).reshape(own, length, model_width)
     norm_val, norm_pull = jax.vjp(rms_scale, middle, scale_two, shift_two)
     middle_grad, scale_two_grad, shift_two_grad = norm_pull(two_grad)
     middle_grad = middle_grad + out_cot
     gate_one_grad = jnp.sum(middle_grad * branch_one, axis=1)
     branch_low = (gate_one * middle_grad).astype(bf16).reshape(-1, model_width)
-    out_term = ein("nd,mcn->dmc", branch_low, attended).astype(bf16)
     attended_low = ein("cd,nd->cn", out_full, branch_low).astype(bf16)
     attended_low = attended_low.reshape(mp_size, local_dim, own * length)
     projected_low, gains_grad = attend_back(proj, attended_low, gains_f, tables, own)
     gains_grad = jnp.sum(gains_grad, axis=2) * jnp.array([[head_dim ** (-0.5)], [1.0]], f32)
-    qkv_term = ein("nd,mkcn->dmkc", normed_flat, projected_low).astype(bf16)
+    grad_parts = [None, None]
+    normed_t, branch_t = by_owner(normed_flat), by_owner(branch_low)
+    for which in (1, 0):
+        kept, sent = attend_grads(
+            m_orders[which],
+            e_orders[which],
+            normed_t,
+            branch_t,
+            projected_low.reshape(mp_size, 3 * local_dim, -1),
+            attended,
+        )
+        grad_parts[which] = reduce(kept, sent, which, 1)
+    attend_grad = reduce_mp(*grad_parts)
     normed_grad = ein("cn,cd->nd", projected_low.reshape(-1, own * length), qkv_full)
     normed_grad = normed_grad.reshape(own, length, model_width)
     norm_val, norm_pull = jax.vjp(rms_scale, latent_f, scale_one, shift_one)
@@ -390,8 +694,10 @@
         ],
         1,
     ).astype(bf16)
-    mod_all = lax.all_gather(modulation_grad, ("dp", "mp"), axis=0, tiled=True)
-    gains_total = lax.all_gather(gains_grad.astype(bf16), ("dp", "mp"), axis=0)
+    packed = jnp.concatenate([modulation_grad.reshape(-1), gains_grad.astype(bf16).reshape(-1)])
+    packed = xor_gather(packed, gather_bits)[0]
+    mod_all = packed[:, : own * 6 * model_width].reshape(total_images, 6, model_width)
+    gains_total = packed[:, own * 6 * model_width :].reshape(-1, 2, head_dim)
     gains_total = jnp.sum(gains_total.astype(f32), axis=0)
     gains_total = jnp.sum(
         jnp.where(order[:, None] == jnp.arange(head_dim)[None, :], gains_total[:, :, None], 0.0), axis=1
@@ -410,13 +716,11 @@
     time_grad = ein("in,id->nd", bin_hot, condition_low)
     class_grad = ein("in,id->nd", label_hot, condition_low)
 
-    down_grad = reduce_grad(down_term, mp_size).T
-    expand_grad = reduce_grad(expand_term.reshape(model_width, -1), mp_size)
-    expand_grad = expand_grad.reshape(-1, 2, unit_count)
-    out_grad = reduce_grad(out_term, mp_size).T
-    qkv_grad = reduce_grad(qkv_term.reshape(model_width, -1), mp_size)
+    expand_grad = mlp_grad[:2].swapaxes(0, 1)
+    down_grad = mlp_grad[2].T
+    out_grad = attend_grad[:, 3 * local_dim :].T
     qkv_grad = lax.dot_general(
-        qkv_grad,
+        attend_grad[:, : 3 * local_dim],
         turn.astype(f32),
         (((1,), (0,)), ((), ())),
         precision=lax.Precision.HIGHEST,

time: 1140 us -> 1040 us (0.912)
  Pallas kernels: 60.1 us -> 243 us
  matrix products: 220 us -> 70.4 us
  blocking collectives: 121 us -> 0 us
  local copies, waits for them, and re-layouts: 299 us -> 192 us
  waiting for transfers between devices: 301 us -> 356 us
  starting transfers between devices: 30.3 us -> 53.3 us
  other arithmetic: 81.2 us -> 96 us
    pallas_call x0 -> x5, Pallas kernels: none -> 183 us  [the longest x2 101 us: mlp_back(): pl.pallas_call(mlp_back_kernel, grid_spec=pltpu.PrefetchScalarGridSpec(nu...]
    ppermute x0 -> x24, waiting for transfers between devices: none -> 159 us  [swap(): return lax.ppermute(values, axis, [(i, i ^ bit) for i in range(size)])]
    dot_general x16 -> x9, matrix products: 182 us -> 57.5 us  [ein(): return jnp.einsum(spec, a, b, preferred_element_type=f32)]
    all_gather x2 -> x0, blocking collectives: 121 us -> none  [the longest x1 81 us: shards(): gains_total = lax.all_gather(gains_grad.astype(bf16), ('dp', 'mp'), axis=0)]
    reduce_scatter x8 -> x0, waiting for transfers between devices: 91.5 us -> none  [the longest x4 78.7 us: reduce_grad(): lax.psum_scatter(rows, 'mp', scatter_dimension=0, tiled=False).astype(f32)]
    convert_element_type x4 -> x2, local copies, waits for them, and re-layouts: 71.7 us -> 0.17 us  [the longest x1 0.09 us: shards(): gains_grad.astype(bf16).reshape(-1)]
    squeeze x4 -> x0, local copies, waits for them, and re-layouts: 60.4 us -> none  [the longest x2 30.2 us: shards(): expanded[:, :, 0]]
    all_to_all x1, waiting for transfers between devices: 0.01 us -> 58.6 us  [shards(): lax.all_to_all(send_patches, 'dp', split_axis=0, concat_axis=0, tiled=True)]
  transfers between devices with their start and end apart: 19 -> 34, of which waited for: 10 -> 14; matrix products, arithmetic and copies ran while one was open for 34% -> 28% of each run, Pallas kernels for 5% -> 6%
where the time goes in v2:
time: 1040 us; the launch traced here: 1030 us
  waiting for transfers between devices  356 us (34%)
  Pallas kernels  243 us (23%)
  local copies, waits for them, and re-layouts  192 us (18%)
  other arithmetic  96 us (9%)
  matrix products  70.4 us (7%)
  starting transfers between devices  53.3 us (5%)
  between operations  15.4 us (1%)
    ppermute x24, waiting for transfers between devices, swap(): return lax.ppermute(values, axis, [(i, i ^ bit) for i in range(size)])  159 us
    pallas_call x2, Pallas kernels, mlp_back(): pl.pallas_call(mlp_back_kernel, grid_spec=pltpu.PrefetchScalarGridSpec(nu...  101 us
    all_to_all x1, waiting for transfers between devices, shards(): lax.all_to_all(cotangent, 'mp', split_axis=0, concat_axis=1, tiled=True)  72.3 us
    all_to_all x1, waiting for transfers between devices, shards(): lax.all_to_all(send_patches, 'dp', split_axis=0, concat_axis=0, tiled=True)  58.6 us
    dot_general x9, matrix products, ein(): return jnp.einsum(spec, a, b, preferred_element_type=f32)  57.5 us
    unnamed x120, local copies, waits for them, and re-layouts  54 us
    pallas_call x1, Pallas kernels, mlp(): pl.pallas_call(mlp_kernel, grid=(groups, units // block), in_specs=[pl.Bl...  50.7 us
    all_gather x4, waiting for transfers between devices, gather_rows(): whole = lax.all_gather(piece, ('mp', 'dp'), axis=0, tiled=True)  40 us
  transfers between devices with their start and end apart: 34, of which 14 were waited for; matrix products, arithmetic and copies ran while one was open for 28% of the time, Pallas kernels for 6%

profile of v2, /device:TPU:0, one launch (start us, length us, event | category | flops | bytes accessed | tf_op | source)
XLA Modules:
  0.0 1026.0 jit_solution(14225222459713385855)
XLA Ops:
  9.1 5.7 gather_fusion.3
  14.8 4.0 fusion.13
  21.4 10.3 %copy.223 = bf16[1152,2,768]{0,2,1:T(8,128)(2,1)} copy(bf16[1152,2,768]{2,1,0:T(2,128)(2,1)} %param.37) | data formatting | bytes 7077888 | tf_op jit(solution)/shard_map/reshape | solution.py:517
  37.1 5.6 gather_fusion.8
  42.7 5.1 broadcast_select_fusion
  47.8 5.4 all-to-all-start
  56.5 58.6 %all-to-all-done = bf16[32,64,1152]{2,1,0:T(8,128)(2,1)} async-done(((bf16[32,64,1152]{2,1,0:T(8,128)(2,1)}), bf16[32,64,1152]{2,1,0:T(8,128)(2,1)}, u32[]{:S(2)}, u32[]{:S(2)}) %all-to-all-start) | async-done | bytes 4718624 | tf_op jit(solution)/shard_map/all_to_all | solution.py:534
  115.1 5.7 all-to-all-start.3
  124.7 4.5 gather_fusion.2
  129.3 3.4 broadcast_select_fusion.2
  132.6 72.3 %all-to-all-done.3 = bf16[16,64,1152]{2,1,0:T(8,128)(2,1)} async-done(((bf16[16,64,1152]{2,1,0:T(8,128)(2,1)}), bf16[16,64,1152]{2,1,0:T(8,128)(2,1)}, u32[]{:S(2)}, u32[]{:S(2)}) %all-to-all-start.3) | async-done | bytes 2359328 | tf_op jit(solution)/shard_map/all_to_all | solution.py:541
  204.9 4.7 all-to-all-start.1
  215.5 22.4 %copy.189 = bf16[1152,6,1152]{0,2,1:T(8,128)(2,1)} copy(bf16[1152,6,1152]{2,0,1:T(8,128)(2,1)} %param.33) | data formatting | bytes 31850496 | tf_op args[8]
  240.8 9.8 fusion.19
  256.9 4.3 copy.201
  261.2 5.2 reshape.978
  266.4 5.2 reshape.969
  271.5 4.9 all-to-all-done.1
  283.7 4.5 fusion.7
  288.2 4.3 copy.211
  292.5 4.5 add_convert_fusion.8
  297.0 9.3 dot_general.59
  306.3 15.8 %fusion.92.proj_ref = f32[4,3,288,1024]{3,2,1,0:T(8,128)} fusion(bf16[4,3,288,1152]{3,2,1,0:T(8,128)(2,1)} %dot_general.59, bf16[1024,1152,1,1]{1,0,3,2:T(8,128)(2,1)} %bitcast.275), kind=kOutput, calls=%fused_computation.291 | convolution fusion | flops 8153726976 | bytes 24477696 | tf_op jit(solution)/shard_map/cd,nd->cn/dot_general | solution.py:421
  322.1 26.2 %attend.1.att_ref = bf16[4,288,1024]{2,1,0:T(8,128)(2,1)S(1)} custom-call(f32[4,3,288,1024]{3,2,1,0:T(8,128)} %fusion.92.proj_ref, f32[2,72,1]{2,1,0:T(8,128)S(1)} %broadcast_multiply_fusion.gains_ref, f32[72,256]{1,0:T(8,128)S(1)} %pad_maximum_fusion.3.cos_ref, f32[72,256]{1,0:T(8,128)S(1)} %pad_maximum_fusion.4.sin_ref), custom_call_target="tpu_custom_call" | custom-call | flops 1207959552 | bytes 16515072 | tf_op jit(solution)/shard_map/attend/pallas_call | solution.py:153
  348.3 8.4 multiply_reduce_fusion.3
  360.9 4.3 copy.199
  365.2 9.3 reshape.980
  374.5 40.0 %all-gather.7.cloned.1.call-done = bf16[6144,1152]{1,0:T(8,128)(2,1)} async-done(((bf16[192,1152]{1,0:T(8,128)(2,1)}), bf16[6144,1152]{1,0:T(8,128)(2,1)}) %all-gather.7.cloned.1.call-update) | async-done | bytes 14155792 | tf_op jit(solution)/shard_map/all_gather | solution.py:430
  414.5 50.7 %mlp.1 = (f32[4,2,1024,768]{3,2,1,0:T(8,128)}, f32[1024,1152]{1,0:T(8,128)}) custom-call(bf16[1024,1152]{1,0:T(8,128)(2,1)} %bitcast.257, bf16[4,2,768,1152]{3,2,1,0:T(8,128)(2,1)} %bitcast.285, bf16[4,768,1152]{2,1,0:T(8,128)(2,1)} %bitcast.288), custom_call_target="tpu_custom_call" | custom-call | flops 21743271936 | bytes 46399488 | tf_op jit(solution)/shard_map/mlp/pallas_call | solution.py:227
  465.3 50.7 %mlp_back.2 = (bf16[2,3,576,768]{3,2,1,0:T(8,128)(2,1)}, bf16[2,3,576,768]{3,2,1,0:T(8,128)(2,1)}, f32[1024,1152]{1,0:T(8,128)}) custom-call(s32[2]{0:T(128)} %get-tuple-element.142.m_ref, s32[8]{0:T(128)} %get-tuple-element.152.e_ref, bf16[8,144,1024]{2,1,0:T(8,128)(2,1)} %bitcast.273, bf16[8,144,1024]{2,1,0:T(8,128)(2,1)} %bitcast.268, ...), custom_call_target="tpu_custom_call" | custom-call | flops 21743271936 | bytes 33816576 | tf_op jit(solution)/shard_map/mlp_back/pallas_call | solution.py:323
  516.0 50.3 %mlp_back.3 = (bf16[2,3,576,768]{3,2,1,0:T(8,128)(2,1)}, bf16[2,3,576,768]{3,2,1,0:T(8,128)(2,1)}, f32[1024,1152]{1,0:T(8,128)}) custom-call(s32[2]{0:T(128)} %get-tuple-element.141.m_ref, s32[8]{0:T(128)} %get-tuple-element.151.e_ref, bf16[8,144,1024]{2,1,0:T(8,128)(2,1)} %bitcast.274, bf16[8,144,1024]{2,1,0:T(8,128)(2,1)} %bitcast.269, ...), custom_call_target="tpu_custom_call" | custom-call | flops 21743271936 | bytes 33816576 | tf_op jit(solution)/shard_map/mlp_back/pallas_call | solution.py:323
  566.3 4.4 add.569
  570.7 4.1 fusion.8
  575.0 6.4 fusion.10
  585.4 4.3 copy.212
  589.6 5.7 convolution_convert_fusion
  595.4 34.0 %attend_back.1 = (bf16[4,3,288,1024]{3,2,1,0:T(8,128)(2,1)}, f32[2,72,256]{2,1,0:T(8,128)S(1)}) custom-call(f32[4,3,288,1024]{3,2,1,0:T(8,128)} %fusion.92.proj_ref, bf16[4,288,1024]{2,1,0:T(8,128)(2,1)S(1)} %bitcast.240, f32[2,72,1]{2,1,0:T(8,128)S(1)} %broadcast_multiply_fusion.gains_ref, f32[72,256]{1,0:T(8,128)S(1)} %pad_maximum_fusion.3.cos_ref, ...), custom_call_target="tpu_custom_call" | custom-call | flops 3019898880 | bytes 23592960 | tf_op jit(solution)/shard_map/attend_back/pallas_call | solution.py:173
  629.4 10.4 %copy.202 = bf16[1024,3456]{1,0:T(8,128)(2,1)} copy(bf16[1024,3456]{0,1:T(8,128)(2,1)} %bitcast.261) | data formatting | bytes 14155776 | tf_op jit(solution)/shard_map/cn,cd->nd/dot_general | solution.py:421
  639.7 16.6 %multiply_reduce_fusion.1 = (bf16[4,1152]{1,0:T(4,128)(2,1)S(1)}, f32[4,256]{1,0:T(4,128)S(1)}, bf16[4,1152]{1,0:T(4,128)(2,1)S(1)}, f32[4,256,1152]{2,1,0:T(8,128)}) fusion(f32[4,4,64,1152]{3,2,1,0:T(8,128)} %copy.186, f32[4,256]{1,0:T(4,128)S(1)} %rsqrt.28, f32[4,1152]{1,0:T(4,128)S(1)} %get-tuple-element.133, bf16[4,256,3456]{2,1,0:T(8,128)(2,1)} %bitcast.264, ...), kind=kOutput, calls=%fused_computation.44 | convolution fusion | flops 8161974272 | bytes 24522752 | tf_op jit(solution)/shard_map/cn,cd->nd/dot_general | solution.py:421
  658.4 15.7 %attend_grads.2 = (bf16[2,576,1152]{2,1,0:T(8,128)(2,1)}, bf16[2,576,1152]{2,1,0:T(8,128)(2,1)}) custom-call(s32[2]{0:T(128)} %get-tuple-element.142.m_ref, s32[8]{0:T(128)} %get-tuple-element.152.e_ref, bf16[8,144,1024]{2,1,0:T(8,128)(2,1)} %bitcast.266, bf16[8,144,1024]{2,1,0:T(8,128)(2,1)} %bitcast.271, bf16[4,864,1024]{2,1,0:T(8,128)(2,1)} %bitcast.262, ...), custom_call_target="tpu_custom_call" | custom-call | flops 5435817984 | bytes 10027008 | tf_op jit(solution)/shard_map/attend_grads/pallas_call | solution.py:388
  674.1 15.3 %attend_grads.3 = (bf16[2,576,1152]{2,1,0:T(8,128)(2,1)}, bf16[2,576,1152]{2,1,0:T(8,128)(2,1)}) custom-call(s32[2]{0:T(128)} %get-tuple-element.141.m_ref, s32[8]{0:T(128)} %get-tuple-element.151.e_ref, bf16[8,144,1024]{2,1,0:T(8,128)(2,1)} %bitcast.267, bf16[8,144,1024]{2,1,0:T(8,128)(2,1)} %bitcast.272, bf16[4,864,1024]{2,1,0:T(8,128)(2,1)} %bitcast.263, ...), custom_call_target="tpu_custom_call" | custom-call | flops 5435817984 | bytes 10027008 | tf_op jit(solution)/shard_map/attend_grads/pallas_call | solution.py:388
  691.4 4.5 collective-permute-done.4
  697.8 4.7 fusion.4
  705.7 4.6 all-to-all-start.4
  714.4 7.7 collective-permute-done.6
  722.1 3.7 concatenate.52
  727.4 4.9 copy.197
  732.3 8.2 concatenate.53
  748.3 4.9 reshape.867
  757.0 6.7 all-to-all-done.4
  763.7 4.7 all-to-all-start.2
  777.2 4.9 gather_fusion.6
  785.7 5.4 add_convert_fusion
  795.0 5.4 add_convert_fusion.1
  807.8 14.0 %all-to-all-done.2 = bf16[4,256,1152]{2,0,1:T(4,128)(2,1)} async-done(((bf16[4,256,1152]{2,0,1:T(4,128)(2,1)}), bf16[4,256,1152]{2,0,1:T(4,128)(2,1)}, u32[]{:S(2)}, u32[]{:S(2)}) %all-to-all-start.2) | async-done | bytes 2359328 | tf_op jit(solution)/shard_map/all_to_all | solution.py:615
  821.8 4.9 all-to-all-start.5
  831.1 22.5 %collective-permute-done.20 = bf16[2,3,288,768]{3,2,1,0:T(8,128)(2,1)} collective-permute-done((bf16[2,3,288,768]{3,2,1,0:T(8,128)(2,1)}, bf16[2,3,288,768]{3,2,1,0:T(8,128)(2,1)}, u32[]{:S(2)}, u32[]{:S(2)}) %collective-permute-start.20) | collective-permute-done | bytes 2654240 | tf_op jit(solution)/shard_map/ppermute | solution.py:442
  853.6 3.3 add_convert_fusion.2
  860.4 42.7 %collective-permute-done.10 = bf16[2,144,1152]{2,1,0:T(8,128)(2,1)S(1)} collective-permute-done((bf16[2,144,1152]{2,1,0:T(8,128)(2,1)S(1)}, bf16[2,144,1152]{2,1,0:T(8,128)(2,1)S(1)}, u32[]{:S(2)}, u32[]{:S(2)}) %collective-permute-start.10) | collective-permute-done | bytes 663584 | tf_op jit(solution)/shard_map/ppermute | solution.py:442
  910.4 43.1 %collective-permute-done.21 = bf16[2,3,144,768]{3,2,1,0:T(8,128)(2,1)S(1)} collective-permute-done((bf16[2,3,144,768]{3,2,1,0:T(8,128)(2,1)S(1)}, bf16[2,3,144,768]{3,2,1,0:T(8,128)(2,1)S(1)}, u32[]{:S(2)}, u32[]{:S(2)}) %collective-permute-start.21) | collective-permute-done | bytes 1327136 | tf_op jit(solution)/shard_map/ppermute | solution.py:442
  959.5 3.5 copy.198
  966.1 5.6 gather_fusion.9
  971.6 12.8 %collective-permute-done.22 = bf16[2,3,144,768]{3,2,1,0:T(8,128)(2,1)} collective-permute-done((bf16[2,3,144,768]{3,2,1,0:T(8,128)(2,1)}, bf16[2,3,144,768]{3,2,1,0:T(8,128)(2,1)}, u32[]{:S(2)}, u32[]{:S(2)}) %collective-permute-start.22) | collective-permute-done | bytes 1327136 | tf_op jit(solution)/shard_map/ppermute | solution.py:442
  992.4 23.9 %collective-permute-done.23 = bf16[1,3,144,768]{3,2,1,0:T(8,128)(2,1)S(1)} collective-permute-done((bf16[1,3,144,768]{3,2,1,0:T(8,128)(2,1)S(1)}, bf16[1,3,144,768]{3,2,1,0:T(8,128)(2,1)S(1)}, u32[]{:S(2)}, u32[]{:S(2)}) %collective-permute-start.23) | collective-permute-done | bytes 663584 | tf_op jit(solution)/shard_map/ppermute | solution.py:442
  (332 shorter events, 131.6 us)
Async XLA Ops:
  7.2 231.7 %copy-start = (bf16[1000,1152]{1,0:T(8,128)(2,1)S(1)}, bf16[1000,1152]{1,0:T(8,128)(2,1)}, u32[]{:S(2)}) copy-start(bf16[1000,1152]{1,0:T(8,128)(2,1)} %param.32) | copy-start | bytes 6912004
  7.2 254.0 %all-gather.13.cloned.1.call-start = ((), (), s32[]{:S(2)}) async-start(), calls=%async_computation.9 | async-start | bytes 3041280 | tf_op jit(solution)/shard_map/all_gather | solution.py:430
  9.0 288.0 %all-gather.11.cloned.1.call-start = ((), (), s32[]{:S(2)}) async-start(), calls=%async_computation.8 | async-start | bytes 8515584 | tf_op jit(solution)/shard_map/all_gather | solution.py:430
  19.6 14.0 %copy-start.33 = (s32[8]{0:T(128)S(1)}, s32[8]{0:T(128)}, u32[]{:S(2)}) copy-start(s32[8]{0:T(128)} %param.29) | copy-start | bytes 100
  19.6 16.0 %copy-start.7 = (s32[8]{0:T(128)S(1)}, s32[8]{0:T(128)}, u32[]{:S(2)}) copy-start(s32[8]{0:T(128)} %param.30) | copy-start | bytes 100
  19.7 354.8 %all-gather.9.cloned.1.call-start = ((), (), s32[]{:S(2)}) async-start(), calls=%async_computation.7 | async-start | bytes 7299072 | tf_op jit(solution)/shard_map/all_gather | solution.py:430
  21.4 393.1 %all-gather.7.cloned.1.call-start = ((), (), s32[]{:S(2)}) async-start(), calls=%async_computation.6 | async-start | bytes 14598144 | tf_op jit(solution)/shard_map/all_gather | solution.py:430
  33.8 89.2 %copy-start.5 = (s32[8]{0:T(128)}, s32[8]{0:T(128)S(1)}, u32[]{:S(2)}) copy-start(s32[8]{0:T(128)S(1)} %bitcast_subtract_fusion.2) | copy-start | bytes 100
  47.8 67.3 %all-to-all-start = ((bf16[32,64,1152]{2,1,0:T(8,128)(2,1)}), bf16[32,64,1152]{2,1,0:T(8,128)(2,1)}, u32[]{:S(2)}, u32[]{:S(2)}) async-start(bf16[32,64,1152]{2,1,0:T(8,128)(2,1)} %broadcast_select_fusion), calls=%async_computation | async-start | bytes 9437184 | tf_op jit(solution)/shard_map/all_to_all | solution.py:534
  53.1 67.7 %copy-start.32 = (bf16[2,72]{1,0:T(2,128)(2,1)S(1)}, bf16[2,72]{1,0:T(2,128)(2,1)}, u32[]{:S(2)}) copy-start(bf16[2,72]{1,0:T(2,128)(2,1)} %param.35) | copy-start | bytes 868
  53.2 67.8 %copy-start.3 = (s32[72]{0:T(128)S(1)}, s32[72]{0:T(128)}, u32[]{:S(2)}) copy-start(s32[72]{0:T(128)} %constant.263.clone) | copy-start | bytes 868
  53.2 69.9 %copy-start.40 = (s32[4]{0:T(128)S(1)}, s32[4]{0:T(128)}, u32[]{:S(2)}) copy-start(s32[4]{0:T(128)} %constant.269.clone) | copy-start | bytes 52
  53.2 70.6 %copy-start.36 = (s32[8]{0:T(128)S(1)}, s32[8]{0:T(128)}, u32[]{:S(2)}) copy-start(s32[8]{0:T(128)} %constant.267.clone) | copy-start | bytes 100
  53.2 70.6 %copy-start.37 = (s32[8]{0:T(128)S(1)}, s32[8]{0:T(128)}, u32[]{:S(2)}) copy-start(s32[8]{0:T(128)} %constant.268.clone) | copy-start | bytes 100
  53.2 71.4 %copy-start.28 = (f32[2]{0:T(128)S(1)}, f32[2]{0:T(128)}, u32[]{:S(2)}) copy-start(f32[2]{0:T(128)} %constant.274) | copy-start | bytes 28
  53.3 157.0 %collective-permute-start = (s32[1,2,32]{2,1,0:T(2,128)S(1)}, s32[1,2,32]{2,1,0:T(2,128)S(1)}, u32[]{:S(2)}, u32[]{:S(2)}) collective-permute-start(s32[1,2,32]{2,1,0:T(2,128)S(1)} %add_bitcast_fusion.1), channel_id=1, source_target_pairs={{0,4},{4,0},{8,12},{12,8},{16,20},{20,16},{24,28},{28,24},{1,5},{5... | collective-permute-start | bytes 776 | tf_op jit(solution)/shard_map/ppermute | solution.py:442
  115.1 89.8 %all-to-all-start.3 = ((bf16[16,64,1152]{2,1,0:T(8,128)(2,1)}), bf16[16,64,1152]{2,1,0:T(8,128)(2,1)}, u32[]{:S(2)}, u32[]{:S(2)}) async-start(bf16[16,64,1152]{2,1,0:T(8,128)(2,1)} %param.26), calls=%async_computation.3 | async-start | bytes 4718592 | tf_op jit(solution)/shard_map/all_to_all | solution.py:541
  204.9 71.5 %all-to-all-start.1 = ((bf16[16,64,1152]{2,1,0:T(8,128)(2,1)}), bf16[16,64,1152]{2,1,0:T(8,128)(2,1)}, u32[]{:S(2)}, u32[]{:S(2)}) async-start(bf16[16,64,1152]{2,1,0:T(8,128)(2,1)} %broadcast_select_fusion.2), calls=%async_computation.1 | async-start | bytes 4718592 | tf_op jit(solution)/shard_map/all_to_all | solution.py:540
  210.3 3.7 collective-permute-start.1
  213.9 23.9 %collective-permute-start.2 = (s32[4,2,32]{2,1,0:T(2,128)S(1)}, s32[4,2,32]{2,1,0:T(2,128)S(1)}, u32[]{:S(2)}, u32[]{:S(2)}) collective-permute-start(s32[4,2,32]{2,1,0:T(2,128)S(1)} %pad_add_fusion), channel_id=1, source_target_pairs={{0,16},{4,20},{8,24},{12,28},{16,0},{20,4},{24,8},{28,12},{1,17},{... | collective-permute-start | bytes 3080 | tf_op jit(solution)/shard_map/ppermute | solution.py:442
  215.5 23.1 %copy-start.20 = (bf16[16,1152]{1,0:T(8,128)(2,1)S(1)}, bf16[16,1152]{1,0:T(8,128)(2,1)}, u32[]{:S(2)}) copy-start(bf16[16,1152]{1,0:T(8,128)(2,1)} %param.31) | copy-start | bytes 110596
  238.4 12.2 %copy-start.24 = (s32[128]{0:T(128)}, s32[128]{0:T(128)S(1)}, u32[]{:S(2)}) copy-start(s32[128]{0:T(128)S(1)} %get-tuple-element.118) | copy-start | bytes 1540
  238.4 12.2 %copy-start.30 = (s32[128]{0:T(128)}, s32[128]{0:T(128)S(1)}, u32[]{:S(2)}) copy-start(s32[128]{0:T(128)S(1)} %get-tuple-element.117) | copy-start | bytes 1540
  240.8 9.9 copy-start.19
  322.1 26.2 %copy-start.18 = (bf16[4,288,1152,1]{2,1,0,3:T(8,128)(2,1)S(1)}, bf16[4,288,1152,1]{2,1,0,3:T(8,128)(2,1)}, u32[]{:S(2)}) copy-start(bf16[4,288,1152,1]{2,1,0,3:T(8,128)(2,1)} %reshape.978) | copy-start | bytes 7962628
  639.7 16.9 %copy-start.29 = (f32[2]{0:T(128)S(1)}, f32[2]{0:T(128)}, u32[]{:S(2)}) copy-start(f32[2]{0:T(128)} %constant.274) | copy-start | bytes 28
  656.9 33.6 %collective-permute-start.3 = (bf16[1,27792]{1,0:T(2,128)(2,1)S(1)}, bf16[1,27792]{1,0:T(2,128)(2,1)S(1)}, u32[]{:S(2)}, u32[]{:S(2)}) collective-permute-start(bf16[1,27792]{1,0:T(2,128)(2,1)S(1)} %broadcast_in_dim.201), channel_id=1, source_target_pairs={{0,2},{1,3},{2,0},{3,1},{4,6},{5,7},{6,4},{7,5},{8,10},{9,11},{10,... | collective-permute-start | bytes 166760 | tf_op jit(solution)/shard_map/ppermute | solution.py:442
  658.4 39.4 %slice-start = ((s8[4718592]{0:T(1024)(128)(4,1)}), s8[4194304]{0:T(1024)(128)(4,1)S(1)}, s32[]{:S(2)}) async-start(s8[4718592]{0:T(1024)(128)(4,1)} %bitcast.241), calls=%async_computation.10 | async-start | bytes 8388608
  674.1 17.2 %copy-start.22 = (f32[4,256]{1,0:T(4,128)S(1)}, f32[4,256]{1,0:T(4,128)}, u32[]{:S(2)}) copy-start(f32[4,256]{1,0:T(4,128)} %copy-done.21) | copy-start | bytes 12292
  674.1 23.7 %slice-start.1 = ((s8[4718592]{0:T(1024)(128)(4,1)}), s8[524288]{0:T(1024)(128)(4,1)S(1)}, s32[]{:S(2)}) async-start(s8[4718592]{0:T(1024)(128)(4,1)} %bitcast.241), calls=%async_computation.11 | async-start | bytes 1048576
  689.5 103.9 %collective-permute-start.16 = (bf16[2,3,576,768]{3,2,1,0:T(8,128)(2,1)}, bf16[2,3,576,768]{3,2,1,0:T(8,128)(2,1)}, u32[]{:S(2)}, u32[]{:S(2)}) collective-permute-start(bf16[2,3,576,768]{3,2,1,0:T(8,128)(2,1)} %get-tuple-element.36), channel_id=1, source_target_pairs={{0,4},{4,0},{8,12},{12,8},{16,20},{20,16},{24,28},{28,24},{1,5},{5... | collective-permute-start | bytes 15925256 | tf_op jit(solution)/shard_map/ppermute | solution.py:442
  689.5 96.2 %collective-permute-start.19 = (bf16[2,3,576,768]{3,2,1,0:T(8,128)(2,1)}, bf16[2,3,576,768]{3,2,1,0:T(8,128)(2,1)}, u32[]{:S(2)}, u32[]{:S(2)}) collective-permute-start(bf16[2,3,576,768]{3,2,1,0:T(8,128)(2,1)} %get-tuple-element.38), channel_id=1, source_target_pairs={{0,4},{4,0},{8,12},{12,8},{16,20},{20,16},{24,28},{28,24},{1,5},{5... | collective-permute-start | bytes 15925256 | tf_op jit(solution)/shard_map/ppermute | solution.py:442
  690.0 78.4 %collective-permute-start.8 = (bf16[2,576,1152]{2,1,0:T(8,128)(2,1)}, bf16[2,576,1152]{2,1,0:T(8,128)(2,1)}, u32[]{:S(2)}, u32[]{:S(2)}) collective-permute-start(bf16[2,576,1152]{2,1,0:T(8,128)(2,1)} %get-tuple-element.32), channel_id=1, source_target_pairs={{0,4},{4,0},{8,12},{12,8},{16,20},{20,16},{24,28},{28,24},{1,5},{5... | collective-permute-start | bytes 7962632 | tf_op jit(solution)/shard_map/ppermute | solution.py:442
  690.1 50.5 %collective-permute-start.11 = (bf16[2,576,1152]{2,1,0:T(8,128)(2,1)}, bf16[2,576,1152]{2,1,0:T(8,128)(2,1)}, u32[]{:S(2)}, u32[]{:S(2)}) collective-permute-start(bf16[2,576,1152]{2,1,0:T(8,128)(2,1)} %get-tuple-element.34), channel_id=1, source_target_pairs={{0,4},{4,0},{8,12},{12,8},{16,20},{20,16},{24,28},{28,24},{1,5},{5... | collective-permute-start | bytes 7962632 | tf_op jit(solution)/shard_map/ppermute | solution.py:442
  690.8 5.1 collective-permute-start.4
  696.3 14.1 %collective-permute-start.5 = (bf16[4,27792]{1,0:T(4,128)(2,1)S(1)}, bf16[4,27792]{1,0:T(4,128)(2,1)S(1)}, u32[]{:S(2)}, u32[]{:S(2)}) collective-permute-start(bf16[4,27792]{1,0:T(4,128)(2,1)S(1)} %pad_maximum_fusion.1), channel_id=1, source_target_pairs={{0,16},{4,20},{8,24},{12,28},{16,0},{20,4},{24,8},{28,12},{1,17},{... | collective-permute-start | bytes 667016 | tf_op jit(solution)/shard_map/ppermute | solution.py:442
  702.5 9.9 copy-start.34
  702.5 10.5 %copy-start.8 = (s32[8]{0:T(128)S(1)}, s32[8]{0:T(128)}, u32[]{:S(2)}) copy-start(s32[8]{0:T(128)} %param.30) | copy-start | bytes 100
  705.7 21.5 %copy-start.4 = (s32[72]{0:T(128)S(1)}, s32[72]{0:T(128)}, u32[]{:S(2)}) copy-start(s32[72]{0:T(128)} %constant.263.clone) | copy-start | bytes 868
  705.7 57.9 %all-to-all-start.4 = ((bf16[4,256,1152]{2,0,1:T(4,128)(2,1)}), bf16[4,256,1152]{2,0,1:T(4,128)(2,1)}, u32[]{:S(2)}, u32[]{:S(2)}) async-start(bf16[4,256,1152]{2,0,1:T(4,128)(2,1)} %copy.203), calls=%async_computation.4 | async-start | bytes 4718592 | tf_op jit(solution)/shard_map/all_to_all | solution.py:675
  710.9 11.2 %collective-permute-start.6 = (bf16[8,27792]{1,0:T(8,128)(2,1)S(1)}, bf16[8,27792]{1,0:T(8,128)(2,1)S(1)}, u32[]{:S(2)}, u32[]{:S(2)}) collective-permute-start(bf16[8,27792]{1,0:T(8,128)(2,1)S(1)} %pad_maximum_fusion), channel_id=1, source_target_pairs={{0,8},{4,12},{8,0},{12,4},{16,24},{20,28},{24,16},{28,20},{1,9},{5... | collective-permute-start | bytes 1334024 | tf_op jit(solution)/shard_map/ppermute | solution.py:442
  725.8 6.5 collective-permute-start.7
  746.4 35.7 %collective-permute-start.12 = (bf16[2,288,1152]{2,1,0:T(8,128)(2,1)}, bf16[2,288,1152]{2,1,0:T(8,128)(2,1)}, u32[]{:S(2)}, u32[]{:S(2)}) collective-permute-start(bf16[2,288,1152]{2,1,0:T(8,128)(2,1)} %slice.221), channel_id=1, source_target_pairs={{0,16},{4,20},{8,24},{12,28},{16,0},{20,4},{24,8},{28,12},{1,17},{... | collective-permute-start | bytes 3981320 | tf_op jit(solution)/shard_map/ppermute | solution.py:442
  763.7 58.1 %all-to-all-start.2 = ((bf16[4,256,1152]{2,0,1:T(4,128)(2,1)}), bf16[4,256,1152]{2,0,1:T(4,128)(2,1)}, u32[]{:S(2)}, u32[]{:S(2)}) async-start(bf16[4,256,1152]{2,0,1:T(4,128)(2,1)} %copy.197), calls=%async_computation.2 | async-start | bytes 4718592 | tf_op jit(solution)/shard_map/all_to_all | solution.py:615
  773.0 53.6 %collective-permute-start.9 = (bf16[2,288,1152]{2,1,0:T(8,128)(2,1)}, bf16[2,288,1152]{2,1,0:T(8,128)(2,1)}, u32[]{:S(2)}, u32[]{:S(2)}) collective-permute-start(bf16[2,288,1152]{2,1,0:T(8,128)(2,1)} %slice.217), channel_id=1, source_target_pairs={{0,8},{4,12},{8,0},{12,4},{16,24},{20,28},{24,16},{28,20},{1,9},{5... | collective-permute-start | bytes 3981320 | tf_op jit(solution)/shard_map/ppermute | solution.py:442
  784.2 46.6 %collective-permute-start.13 = (bf16[2,144,1152]{2,1,0:T(8,128)(2,1)S(1)}, bf16[2,144,1152]{2,1,0:T(8,128)(2,1)S(1)}, u32[]{:S(2)}, u32[]{:S(2)}) collective-permute-start(bf16[2,144,1152]{2,1,0:T(8,128)(2,1)S(1)} %slice.223), channel_id=1, source_target_pairs={{0,8},{4,12},{8,0},{12,4},{16,24},{20,28},{24,16},{28,20},{1,9},{5... | collective-permute-start | bytes 1990664 | tf_op jit(solution)/shard_map/ppermute | solution.py:442
  791.1 14.0 %slice-start.8 = ((s8[4718592]{0:T(1024)(128)(4,1)}), s8[4194304]{0:T(1024)(128)(4,1)S(1)}, s32[]{:S(2)}) async-start(s8[4718592]{0:T(1024)(128)(4,1)} %bitcast.251), calls=%async_computation.18 | async-start | bytes 8388608
  792.8 60.8 %collective-permute-start.20 = (bf16[2,3,288,768]{3,2,1,0:T(8,128)(2,1)}, bf16[2,3,288,768]{3,2,1,0:T(8,128)(2,1)}, u32[]{:S(2)}, u32[]{:S(2)}) collective-permute-start(bf16[2,3,288,768]{3,2,1,0:T(8,128)(2,1)} %slice.234), channel_id=1, source_target_pairs={{0,16},{4,20},{8,24},{12,28},{16,0},{20,4},{24,8},{28,12},{1,17},{... | collective-permute-start | bytes 7962632 | tf_op jit(solution)/shard_map/ppermute | solution.py:442
  795.0 10.0 slice-start.9
  804.5 101.6 %collective-permute-start.17 = (bf16[2,3,288,768]{3,2,1,0:T(8,128)(2,1)}, bf16[2,3,288,768]{3,2,1,0:T(8,128)(2,1)}, u32[]{:S(2)}, u32[]{:S(2)}) collective-permute-start(bf16[2,3,288,768]{3,2,1,0:T(8,128)(2,1)} %slice.230), channel_id=1, source_target_pairs={{0,8},{4,12},{8,0},{12,4},{16,24},{20,28},{24,16},{28,20},{1,9},{5... | collective-permute-start | bytes 7962632 | tf_op jit(solution)/shard_map/ppermute | solution.py:442
  821.8 144.3 %all-to-all-start.5 = ((bf16[32,64,1152]{2,1,0:T(8,128)(2,1)}), bf16[32,64,1152]{2,1,0:T(8,128)(2,1)}, u32[]{:S(2)}, u32[]{:S(2)}) async-start(bf16[32,64,1152]{2,1,0:T(8,128)(2,1)} %broadcast_select_fusion.1), calls=%async_computation.5 | async-start | bytes 9437184 | tf_op jit(solution)/shard_map/all_to_all | solution.py:679
  828.8 74.4 %collective-permute-start.10 = (bf16[2,144,1152]{2,1,0:T(8,128)(2,1)S(1)}, bf16[2,144,1152]{2,1,0:T(8,128)(2,1)S(1)}, u32[]{:S(2)}, u32[]{:S(2)}) collective-permute-start(bf16[2,144,1152]{2,1,0:T(8,128)(2,1)S(1)} %slice.219), channel_id=1, source_target_pairs={{0,16},{4,20},{8,24},{12,28},{16,0},{20,4},{24,8},{28,12},{1,17},{... | collective-permute-start | bytes 1990664 | tf_op jit(solution)/shard_map/ppermute | solution.py:442
  831.0 28.3 %copy-start.31 = (s32[128]{0:T(128)S(1)}, s32[128]{0:T(128)}, u32[]{:S(2)}) copy-start(s32[128]{0:T(128)} %copy-done.30) | copy-start | bytes 1540
  831.0 72.1 %collective-permute-start.14 = (bf16[2,144,1152]{2,1,0:T(8,128)(2,1)S(1)}, bf16[2,144,1152]{2,1,0:T(8,128)(2,1)S(1)}, u32[]{:S(2)}, u32[]{:S(2)}) collective-permute-start(bf16[2,144,1152]{2,1,0:T(8,128)(2,1)S(1)} %add_convert_fusion.16), channel_id=1, source_target_pairs={{0,1},{1,0},{2,3},{3,2},{4,5},{5,4},{6,7},{7,6},{8,9},{9,8},{10,11... | collective-permute-start | bytes 1990664 | tf_op jit(solution)/shard_map/ppermute | solution.py:442
  853.6 52.5 %slice-start.6 = ((s8[5308416]{0:T(1024)(128)(4,1)}), s8[4194304]{0:T(1024)(128)(4,1)S(1)}, s32[]{:S(2)}) async-start(s8[5308416]{0:T(1024)(128)(4,1)} %bitcast.249), calls=%async_computation.16 | async-start | bytes 8388608
  857.0 49.1 %slice-start.7 = ((s8[5308416]{0:T(1024)(128)(4,1)}), s8[1114112]{0:T(1024)(128)(4,1)S(1)}, s32[]{:S(2)}) async-start(s8[5308416]{0:T(1024)(128)(4,1)} %bitcast.249), calls=%async_computation.17 | async-start | bytes 2228224
  857.1 96.4 %collective-permute-start.21 = (bf16[2,3,144,768]{3,2,1,0:T(8,128)(2,1)S(1)}, bf16[2,3,144,768]{3,2,1,0:T(8,128)(2,1)S(1)}, u32[]{:S(2)}, u32[]{:S(2)}) collective-permute-start(bf16[2,3,144,768]{3,2,1,0:T(8,128)(2,1)S(1)} %slice.236), channel_id=1, source_target_pairs={{0,8},{4,12},{8,0},{12,4},{16,24},{20,28},{24,16},{28,20},{1,9},{5... | collective-permute-start | bytes 3981320 | tf_op jit(solution)/shard_map/ppermute | solution.py:442
  903.4 59.6 %collective-permute-start.15 = (bf16[1,144,1152]{2,1,0:T(8,128)(2,1)S(1)}, bf16[1,144,1152]{2,1,0:T(8,128)(2,1)S(1)}, u32[]{:S(2)}, u32[]{:S(2)}) collective-permute-start(bf16[1,144,1152]{2,1,0:T(8,128)(2,1)S(1)} %slice.225), channel_id=1, source_target_pairs={{0,2},{1,3},{2,0},{3,1},{4,6},{5,7},{6,4},{7,5},{8,10},{9,11},{10,... | collective-permute-start | bytes 995336 | tf_op jit(solution)/shard_map/ppermute | solution.py:442
  908.6 54.4 %copy-start.16 = (bf16[2,3,288,768]{3,2,1,0:T(8,128)(2,1)}, bf16[2,3,288,768]{3,2,1,0:T(8,128)(2,1)S(1)}, u32[]{:S(2)}) copy-start(bf16[2,3,288,768]{3,2,1,0:T(8,128)(2,1)S(1)} %add_convert_fusion.3) | copy-start | bytes 7962628
  909.8 61.8 %collective-permute-start.18 = (bf16[2,3,144,768]{3,2,1,0:T(8,128)(2,1)}, bf16[2,3,144,768]{3,2,1,0:T(8,128)(2,1)}, u32[]{:S(2)}, u32[]{:S(2)}) collective-permute-start(bf16[2,3,144,768]{3,2,1,0:T(8,128)(2,1)} %slice.232), channel_id=1, source_target_pairs={{0,16},{4,20},{8,24},{12,28},{16,0},{20,4},{24,8},{28,12},{1,17},{... | collective-permute-start | bytes 3981320 | tf_op jit(solution)/shard_map/ppermute | solution.py:442
  955.0 29.5 %collective-permute-start.22 = (bf16[2,3,144,768]{3,2,1,0:T(8,128)(2,1)}, bf16[2,3,144,768]{3,2,1,0:T(8,128)(2,1)}, u32[]{:S(2)}, u32[]{:S(2)}) collective-permute-start(bf16[2,3,144,768]{3,2,1,0:T(8,128)(2,1)} %add_convert_fusion.10), channel_id=1, source_target_pairs={{0,1},{1,0},{2,3},{3,2},{4,5},{5,4},{6,7},{7,6},{8,9},{9,8},{10,11... | collective-permute-start | bytes 3981320 | tf_op jit(solution)/shard_map/ppermute | solution.py:442
  971.6 17.9 %copy-start.14 = (bf16[32,64,1152]{2,1,0:T(8,128)(2,1)S(1)}, bf16[32,64,1152]{2,1,0:T(8,128)(2,1)}, u32[]{:S(2)}) copy-start(bf16[32,64,1152]{2,1,0:T(8,128)(2,1)} %gather_fusion.9) | copy-start | bytes 14155780
  987.1 29.2 %collective-permute-start.23 = (bf16[1,3,144,768]{3,2,1,0:T(8,128)(2,1)S(1)}, bf16[1,3,144,768]{3,2,1,0:T(8,128)(2,1)S(1)}, u32[]{:S(2)}, u32[]{:S(2)}) collective-permute-start(bf16[1,3,144,768]{3,2,1,0:T(8,128)(2,1)S(1)} %slice.238), channel_id=1, source_target_pairs={{0,2},{1,3},{2,0},{3,1},{4,6},{5,7},{6,4},{7,5},{8,10},{9,11},{10,... | collective-permute-start | bytes 1990664 | tf_op jit(solution)/shard_map/ppermute | solution.py:442
  989.5 29.4 %copy-start.1 = (bf16[1000,1152]{1,0:T(8,128)(2,1)S(1)}, bf16[1000,1152]{1,0:T(8,128)(2,1)}, u32[]{:S(2)}) copy-start(bf16[1000,1152]{1,0:T(8,128)(2,1)} %param.32) | copy-start | bytes 6912004
  (23 other events, 134.9 us)
Sparse Core Ops, SparseCore 0:
  11.5 65.1 all-gather.12
  80.2 125.1 all-gather.10
  208.9 100.3 all-gather.8
  312.6 101.8 all-gather.6

commit v3 on v2

--- a/solution.py
+++ b/solution.py
@@ -463,11 +463,22 @@
     return (kept.astype(f32) + received.astype(f32)).astype(bf16)
 
 
+def tie(*values):
+    return lax.optimization_barrier(values)
+
+
+def split(values, dim):
+    size = values.shape[dim] // 2
+    return (
+        lax.slice_in_dim(values, 0, size, axis=dim),
+        lax.slice_in_dim(values, size, 2 * size, axis=dim),
+    )
+
+
 def halve(values, axis, bits, dim):
     for bit in bits:
-        size = values.shape[dim] // 2
-        received = swap(lax.slice_in_dim(values, size, 2 * size, axis=dim), axis, bit)
-        values = add_low(lax.slice_in_dim(values, 0, size, axis=dim), received)
+        kept, sent = split(values, dim)
+        values = add_low(kept, swap(sent, axis, bit))
     return values
 
 
@@ -538,6 +549,7 @@
     recv_index = source * slot_count + within // dp_size
     latent = jnp.take(recv_patches, recv_index, axis=0)
     latent = lax.all_to_all(latent, "mp", split_axis=0, concat_axis=1, tiled=True)
+    cotangent, latent = tie(cotangent, latent)
     cot = lax.all_to_all(cotangent, "mp", split_axis=0, concat_axis=1, tiled=True)
 
     info, info_places = xor_gather(
@@ -627,22 +639,23 @@
     def by_owner(values):
         return values.T.reshape(dp_size, model_width // dp_size, -1)
 
-    def reduce(kept, sent, which, dim):
-        kept = add_low(kept, swap(sent, "dp", dp_bits[which][0]))
-        return halve(kept, "dp", dp_bits[which][1:], dim)
-
     def reduce_mp(kept, sent):
         kept = add_low(kept, swap(sent, "mp", mp_bits[0]))
         return halve(kept, "mp", mp_bits[1:], 0)[0].astype(f32)
 
     two_t, down_t = by_owner(two_flat), by_owner(down_low)
-    mlp_parts, two_parts = [None, None], [None, None]
-    for which in (1, 0):
-        kept, sent, two_parts[which] = mlp_back(
-            m_orders[which], e_orders[which], two_t, down_t, down_low, save, expand_blocks, down_blocks
-        )
-        mlp_parts[which] = reduce(kept, sent, which, 2)
-    mlp_grad = reduce_mp(*mlp_parts)
+    kept_one, sent_one, two_one = mlp_back(
+        m_orders[1], e_orders[1], two_t, down_t, down_low, save, expand_blocks, down_blocks
+    )
+    got_one = swap(sent_one, "dp", dp_bits[1][0])
+    kept_zero, sent_zero, two_zero = mlp_back(
+        m_orders[0], e_orders[0], two_t, down_t, down_low, save, expand_blocks, down_blocks
+    )
+    got_zero = swap(sent_zero, "dp", dp_bits[0][0])
+    two_zero, got_one = tie(two_zero, got_one)
+    kept_one, sent_one = split(add_low(kept_one, got_one), 2)
+    got_one = swap(sent_one, "dp", dp_bits[1][1])
+    two_parts = (two_zero, two_one)
     two_grad = (two_parts[0] + two_parts[1]).reshape(own, length, model_width)
     norm_val, norm_pull = jax.vjp(rms_scale, middle, scale_two, shift_two)
     middle_grad, scale_two_grad, shift_two_grad = norm_pull(two_grad)
@@ -651,11 +664,22 @@
     branch_low = (gate_one * middle_grad).astype(bf16).reshape(-1, model_width)
     attended_low = ein("cd,nd->cn", out_full, branch_low).astype(bf16)
     attended_low = attended_low.reshape(mp_size, local_dim, own * length)
+    attended_low, got_zero = tie(attended_low, got_zero)
+    kept_zero, sent_zero = split(add_low(kept_zero, got_zero), 2)
+    got_zero = swap(sent_zero, "dp", dp_bits[0][1])
     projected_low, gains_grad = attend_back(proj, attended_low, gains_f, tables, own)
     gains_grad = jnp.sum(gains_grad, axis=2) * jnp.array([[head_dim ** (-0.5)], [1.0]], f32)
-    grad_parts = [None, None]
-    normed_t, branch_t = by_owner(normed_flat), by_owner(branch_low)
-    for which in (1, 0):
+    projected_low, got_one = tie(projected_low, got_one)
+    mlp_one = halve(add_low(kept_one, got_one), "dp", dp_bits[1][2:], 2)
+    normed_grad = ein("cn,cd->nd", projected_low.reshape(-1, own * length), qkv_full)
+    normed_grad = normed_grad.reshape(own, length, model_width)
+    norm_val, norm_pull = jax.vjp(rms_scale, latent_f, scale_one, shift_one)
+    latent_grad, scale_one_grad, shift_one_grad = norm_pull(normed_grad)
+    latent_grad = (latent_grad + middle_grad).astype(bf16)
+
+    normed_t, branch_t, latent_grad = tie(by_owner(normed_flat), by_owner(branch_low), latent_grad)
+
+    def grads_of(which):
         kept, sent = attend_grads(
             m_orders[which],
             e_orders[which],
@@ -664,13 +688,14 @@
             projected_low.reshape(mp_size, 3 * local_dim, -1),
             attended,
         )
-        grad_parts[which] = reduce(kept, sent, which, 1)
-    attend_grad = reduce_mp(*grad_parts)
-    normed_grad = ein("cn,cd->nd", projected_low.reshape(-1, own * length), qkv_full)
-    normed_grad = normed_grad.reshape(own, length, model_width)
-    norm_val, norm_pull = jax.vjp(rms_scale, latent_f, scale_one, shift_one)
-    latent_grad, scale_one_grad, shift_one_grad = norm_pull(normed_grad)
-    latent_grad = (latent_grad + middle_grad).astype(bf16)
+        return kept, swap(sent, "dp", dp_bits[which][0])
+
+    attend_one = halve(add_low(*grads_of(1)), "dp", dp_bits[1][1:], 1)
+    normed_t, got_zero = tie(normed_t, got_zero)
+    mlp_zero = halve(add_low(kept_zero, got_zero), "dp", dp_bits[0][2:], 2)
+    attend_zero = halve(add_low(*grads_of(0)), "dp", dp_bits[0][1:], 1)
+    mlp_grad = reduce_mp(mlp_zero, mlp_one)
+    attend_grad = reduce_mp(attend_zero, attend_one)
 
     latent_back = lax.all_to_all(latent_grad, "mp", split_axis=1, concat_axis=0, tiled=True)
     back_within = pair_slot * dp_size + jnp.mod(my_place - starts[pair_peer], dp_size)

time: 1040 us -> 987 us (0.949)
  waiting for transfers between devices: 356 us -> 323 us
    ppermute x24, waiting for transfers between devices: 159 us -> 106 us  [swap(): return lax.ppermute(values, axis, [(i, i ^ bit) for i in range(size)])]
    all_to_all x1, waiting for transfers between devices: 4.91 us -> 47.1 us  [shards(): lax.all_to_all(latent, 'mp', split_axis=0, concat_axis=1, tiled=True)]
    all_to_all x1, waiting for transfers between devices: 72.3 us -> 44.1 us  [shards(): lax.all_to_all(cotangent, 'mp', split_axis=0, concat_axis=1, tiled=True)]
    all_gather x4, waiting for transfers between devices: 40 us -> 61.3 us  [gather_rows(): whole = lax.all_gather(piece, ('mp', 'dp'), axis=0, tiled=True)]
    all_to_all x1, waiting for transfers between devices: 14 us -> 0.01 us  [shards(): lax.all_to_all(result, 'mp', split_axis=1, concat_axis=0, tiled=True)]
    unnamed x120 -> x118, local copies, waits for them, and re-layouts: 54 us -> 50.5 us
  transfers between devices with their start and end apart: 34 -> 34, of which waited for: 14 -> 11; matrix products, arithmetic and copies ran while one was open for 28% -> 33% of each run, Pallas kernels for 6% -> 14%
where the time goes in v3:
time: 987 us; the launch traced here: 980 us
  waiting for transfers between devices  323 us (33%)
  Pallas kernels  242 us (25%)
  local copies, waits for them, and re-layouts  188 us (19%)
  other arithmetic  90.7 us (9%)
  matrix products  67.4 us (7%)
  starting transfers between devices  53.8 us (5%)
  between operations  15.4 us (2%)
    ppermute x24, waiting for transfers between devices, swap(): return lax.ppermute(values, axis, [(i, i ^ bit) for i in range(size)])  106 us
    pallas_call x2, Pallas kernels, mlp_back(): pl.pallas_call(mlp_back_kernel, grid_spec=pltpu.PrefetchScalarGridSpec(nu...  101 us
    all_gather x4, waiting for transfers between devices, gather_rows(): whole = lax.all_gather(piece, ('mp', 'dp'), axis=0, tiled=True)  61.3 us
    all_to_all x1, waiting for transfers between devices, shards(): lax.all_to_all(send_patches, 'dp', split_axis=0, concat_axis=0, tiled=True)  57.5 us
    dot_general x9, matrix products, ein(): return jnp.einsum(spec, a, b, preferred_element_type=f32)  54.5 us
    unnamed x118, local copies, waits for them, and re-layouts  50.5 us
    pallas_call x1, Pallas kernels, mlp(): pl.pallas_call(mlp_kernel, grid=(groups, units // block), in_specs=[pl.Bl...  50.5 us
    all_to_all x1, waiting for transfers between devices, shards(): lax.all_to_all(latent, 'mp', split_axis=0, concat_axis=1, tiled=True)  47.1 us
  transfers between devices with their start and end apart: 34, of which 11 were waited for; matrix products, arithmetic and copies ran while one was open for 33% of the time, Pallas kernels for 14%

profile of v3, /device:TPU:0, one launch (start us, length us, event | category | flops | bytes accessed | tf_op | source)
XLA Modules:
  0.0 980.2 jit_solution(16657778031457187283)
XLA Ops:
  9.1 5.5 gather_fusion.3
  14.7 4.0 fusion.17
  21.3 10.3 %copy.207 = bf16[1152,2,768]{0,2,1:T(8,128)(2,1)} copy(bf16[1152,2,768]{2,1,0:T(2,128)(2,1)} %param.37) | data formatting | bytes 7077888 | tf_op jit(solution)/shard_map/reshape | solution.py:528
  36.4 5.6 gather_fusion.8
  42.0 5.1 broadcast_select_fusion
  47.1 5.4 all-to-all-start
  56.9 57.5 %all-to-all-done = bf16[32,64,1152]{2,1,0:T(8,128)(2,1)} async-done(((bf16[32,64,1152]{2,1,0:T(8,128)(2,1)}), bf16[32,64,1152]{2,1,0:T(8,128)(2,1)}, u32[]{:S(2)}, u32[]{:S(2)}) %all-to-all-start) | async-done | bytes 4718624 | tf_op jit(solution)/shard_map/all_to_all | solution.py:545
  114.4 4.5 gather_fusion.2
  119.0 3.4 broadcast_select_fusion.2
  122.4 5.8 all-to-all-start.1
  132.3 3.1 collective-permute-done.1
  136.0 22.6 %copy.176 = bf16[1152,6,1152]{0,2,1:T(8,128)(2,1)} copy(bf16[1152,6,1152]{2,0,1:T(8,128)(2,1)} %param.33) | data formatting | bytes 31850496 | tf_op args[8]
  159.1 47.1 %all-to-all-done.1 = bf16[16,64,1152]{2,1,0:T(8,128)(2,1)} async-done(((bf16[16,64,1152]{2,1,0:T(8,128)(2,1)}), bf16[16,64,1152]{2,1,0:T(8,128)(2,1)}, u32[]{:S(2)}, u32[]{:S(2)}) %all-to-all-start.1) | async-done | bytes 2359328 | tf_op jit(solution)/shard_map/all_to_all | solution.py:551
  206.2 3.3 copy.173
  209.5 4.8 all-to-all-start.3
  216.7 10.0 %fusion.23 = f32[4,6,1,1152]{3,0,1,2:T(4,128)S(1)} fusion(bf16[1152,6,1152]{0,2,1:T(8,128)(2,1)} %copy.176, bf16[128,1152]{0,1:T(8,128)(2,1)S(1)} %get-tuple-element.169), kind=kOutput, calls=%fused_computation.70 | convolution fusion | flops 63700992 | bytes 16330752 | tf_op jit(solution)/shard_map/dot_general | solution.py:417
  226.8 5.2 reshape.903
  234.2 4.0 fusion.5
  238.1 44.1 %all-to-all-done.3 = bf16[16,64,1152]{2,1,0:T(8,128)(2,1)} async-done(((bf16[16,64,1152]{2,1,0:T(8,128)(2,1)}), bf16[16,64,1152]{2,1,0:T(8,128)(2,1)}, u32[]{:S(2)}, u32[]{:S(2)}) %all-to-all-start.3) | async-done | bytes 2359328 | tf_op jit(solution)/shard_map/all_to_all | solution.py:553
  287.6 4.3 copy.188
  292.0 9.3 dot_general.59
  301.3 15.6 %fusion.96.proj_ref = f32[4,3,288,1024]{3,2,1,0:T(8,128)} fusion(bf16[4,3,288,1152]{3,2,1,0:T(8,128)(2,1)} %dot_general.59, bf16[1024,1152,1,1]{1,0,3,2:T(8,128)(2,1)} %bitcast.226), kind=kOutput, calls=%fused_computation.292 | convolution fusion | flops 8153726976 | bytes 24477696 | tf_op jit(solution)/shard_map/cd,nd->cn/dot_general | solution.py:421
  316.9 26.3 %attend.1.att_ref = bf16[4,288,1024]{2,1,0:T(8,128)(2,1)S(1)} custom-call(f32[4,3,288,1024]{3,2,1,0:T(8,128)} %fusion.96.proj_ref, f32[2,72,1]{2,1,0:T(8,128)S(1)} %broadcast_multiply_fusion.gains_ref, f32[72,256]{1,0:T(8,128)S(1)} %pad_maximum_fusion.3.cos_ref, f32[72,256]{1,0:T(8,128)S(1)} %pad_maximum_fusion.4.sin_ref), custom_call_target="tpu_custom_call" | custom-call | flops 1207959552 | bytes 16515072 | tf_op jit(solution)/shard_map/attend/pallas_call | solution.py:153
  343.2 5.9 multiply_reduce_fusion.2
  352.0 4.3 copy.186
  356.3 61.2 %all-gather.7.cloned.1.call-done = bf16[6144,1152]{1,0:T(8,128)(2,1)} async-done(((bf16[192,1152]{1,0:T(8,128)(2,1)}), bf16[6144,1152]{1,0:T(8,128)(2,1)}) %all-gather.7.cloned.1.call-update) | async-done | bytes 14155792 | tf_op jit(solution)/shard_map/all_gather | solution.py:430
  417.5 50.5 %mlp.1 = (f32[4,2,1024,768]{3,2,1,0:T(8,128)}, f32[1024,1152]{1,0:T(8,128)}) custom-call(bf16[1024,1152]{1,0:T(8,128)(2,1)} %bitcast.230, bf16[4,2,768,1152]{3,2,1,0:T(8,128)(2,1)} %bitcast.256, bf16[4,768,1152]{2,1,0:T(8,128)(2,1)} %bitcast.259), custom_call_target="tpu_custom_call" | custom-call | flops 21743271936 | bytes 46399488 | tf_op jit(solution)/shard_map/mlp/pallas_call | solution.py:227
  468.0 50.3 %mlp_back.3 = (bf16[2,3,576,768]{3,2,1,0:T(8,128)(2,1)}, bf16[2,3,576,768]{3,2,1,0:T(8,128)(2,1)}, f32[1024,1152]{1,0:T(8,128)}) custom-call(s32[2]{0:T(128)} %get-tuple-element.167.m_ref, s32[8]{0:T(128)} %get-tuple-element.177.e_ref, bf16[8,144,1024]{2,1,0:T(8,128)(2,1)} %bitcast.247, bf16[8,144,1024]{2,1,0:T(8,128)(2,1)} %bitcast.245, ...), custom_call_target="tpu_custom_call" | custom-call | flops 21743271936 | bytes 33816576 | tf_op jit(solution)/shard_map/mlp_back/pallas_call | solution.py:323
  518.7 50.3 %mlp_back.2 = (bf16[2,3,576,768]{3,2,1,0:T(8,128)(2,1)}, bf16[2,3,576,768]{3,2,1,0:T(8,128)(2,1)}, f32[1024,1152]{1,0:T(8,128)}) custom-call(s32[2]{0:T(128)} %get-tuple-element.168.m_ref, s32[8]{0:T(128)} %get-tuple-element.178.e_ref, bf16[8,144,1024]{2,1,0:T(8,128)(2,1)} %bitcast.248, bf16[8,144,1024]{2,1,0:T(8,128)(2,1)} %bitcast.246, ...), custom_call_target="tpu_custom_call" | custom-call | flops 21743271936 | bytes 33816576 | tf_op jit(solution)/shard_map/mlp_back/pallas_call | solution.py:323
  572.7 5.2 reshape.894
  577.9 4.3 copy.185
  582.1 9.6 reshape.905
  591.8 5.5 add_convert_fusion.1
  606.6 6.5 fusion.15
  616.0 4.3 copy.189
  620.3 4.9 copy.183
  625.2 4.7 all-to-all-start.2
  629.8 5.7 convolution_convert_fusion
  635.6 34.0 %attend_back.1 = (bf16[4,3,288,1024]{3,2,1,0:T(8,128)(2,1)}, f32[2,72,256]{2,1,0:T(8,128)S(1)}) custom-call(f32[4,3,288,1024]{3,2,1,0:T(8,128)} %fusion.96.proj_ref, bf16[4,288,1024]{2,1,0:T(8,128)(2,1)S(1)} %bitcast.213, f32[2,72,1]{2,1,0:T(8,128)S(1)} %broadcast_multiply_fusion.gains_ref, f32[72,256]{1,0:T(8,128)S(1)} %pad_maximum_fusion.3.cos_ref, ...), custom_call_target="tpu_custom_call" | custom-call | flops 3019898880 | bytes 23592960 | tf_op jit(solution)/shard_map/attend_back/pallas_call | solution.py:173
  669.9 5.3 add_convert_fusion
  678.6 3.2 add_convert_fusion.2
  684.0 9.8 %copy.190 = bf16[1024,3456]{1,0:T(8,128)(2,1)} copy(bf16[1024,3456]{0,1:T(8,128)(2,1)} %bitcast.233) | data formatting | bytes 14155776 | tf_op jit(solution)/shard_map/cn,cd->nd/dot_general | solution.py:421
  693.8 16.1 %fusion.6 = (bf16[4,1152]{1,0:T(4,128)(2,1)S(1)}, f32[4,256]{1,0:T(4,128)S(1)}, bf16[4,1152]{1,0:T(4,128)(2,1)S(1)}, f32[4,256,1152]{2,1,0:T(8,128)}) fusion(bf16[4,256,1152]{2,1,0:T(8,128)(2,1)} %bitcast.221, f32[4,256]{1,0:T(4,128)S(1)} %copy-done.28, f32[4,1152]{1,0:T(4,128)S(1)} %copy-done.23, bf16[4,256,3456]{2,1,0:T(8,128)(2,1)} %bitcast.236, ...), kind=kOutput, calls=%fused_computation.29 | convolution fusion | flops 8163153920 | bytes 22163456 | tf_op jit(solution)/shard_map/cn,cd->nd/dot_general | solution.py:421
  713.2 5.4 collective-permute-done.6
  719.6 5.3 fusion.9
  726.5 15.2 %attend_grads.3 = (bf16[2,576,1152]{2,1,0:T(8,128)(2,1)}, bf16[2,576,1152]{2,1,0:T(8,128)(2,1)}) custom-call(s32[2]{0:T(128)} %get-tuple-element.167.m_ref, s32[8]{0:T(128)} %get-tuple-element.177.e_ref, bf16[8,144,1024]{2,1,0:T(8,128)(2,1)} %bitcast.241, bf16[8,144,1024]{2,1,0:T(8,128)(2,1)} %bitcast.243, bf16[4,864,1024]{2,1,0:T(8,128)(2,1)} %bitcast.234, ...), custom_call_target="tpu_custom_call" | custom-call | flops 5435817984 | bytes 10027008 | tf_op jit(solution)/shard_map/attend_grads/pallas_call | solution.py:388
  741.7 3.2 copy.191
  746.5 15.3 %attend_grads.2 = (bf16[2,576,1152]{2,1,0:T(8,128)(2,1)}, bf16[2,576,1152]{2,1,0:T(8,128)(2,1)}) custom-call(s32[2]{0:T(128)} %get-tuple-element.168.m_ref, s32[8]{0:T(128)} %get-tuple-element.178.e_ref, bf16[8,144,1024]{2,1,0:T(8,128)(2,1)} %bitcast.242, bf16[8,144,1024]{2,1,0:T(8,128)(2,1)} %bitcast.244, bf16[4,864,1024]{2,1,0:T(8,128)(2,1)} %bitcast.235, ...), custom_call_target="tpu_custom_call" | custom-call | flops 5435817984 | bytes 10027008 | tf_op jit(solution)/shard_map/attend_grads/pallas_call | solution.py:388
  762.0 13.1 %collective-permute-done.9 = bf16[8,27792]{1,0:T(8,128)(2,1)S(1)} collective-permute-done((bf16[8,27792]{1,0:T(8,128)(2,1)S(1)}, bf16[8,27792]{1,0:T(8,128)(2,1)S(1)}, u32[]{:S(2)}, u32[]{:S(2)}) %collective-permute-start.9) | collective-permute-done | bytes 444704 | tf_op jit(solution)/shard_map/ppermute | solution.py:442
  775.1 4.3 concatenate.52
  779.4 5.0 all-to-all-start.4
  785.1 3.2 add_convert_fusion.3
  791.0 3.5 copy.184
  799.3 8.2 concatenate.53
  809.0 4.9 reshape.802
  831.8 7.4 all-to-all-done.4
  842.7 4.9 gather_fusion.6
  847.6 5.1 broadcast_select_fusion.1
  852.7 4.9 all-to-all-start.5
  867.5 58.7 %collective-permute-done.17 = bf16[2,144,1152]{2,1,0:T(8,128)(2,1)S(1)} collective-permute-done((bf16[2,144,1152]{2,1,0:T(8,128)(2,1)S(1)}, bf16[2,144,1152]{2,1,0:T(8,128)(2,1)S(1)}, u32[]{:S(2)}, u32[]{:S(2)}) %collective-permute-start.17) | collective-permute-done | bytes 663584 | tf_op jit(solution)/shard_map/ppermute | solution.py:442
  929.8 13.0 %collective-permute-done.18 = bf16[2,144,1152]{2,1,0:T(8,128)(2,1)S(1)} collective-permute-done((bf16[2,144,1152]{2,1,0:T(8,128)(2,1)S(1)}, bf16[2,144,1152]{2,1,0:T(8,128)(2,1)S(1)}, u32[]{:S(2)}, u32[]{:S(2)}) %collective-permute-start.18) | collective-permute-done | bytes 663584 | tf_op jit(solution)/shard_map/ppermute | solution.py:442
  947.0 12.2 %collective-permute-done.19 = bf16[1,144,1152]{2,1,0:T(8,128)(2,1)S(1)} collective-permute-done((bf16[1,144,1152]{2,1,0:T(8,128)(2,1)S(1)}, bf16[1,144,1152]{2,1,0:T(8,128)(2,1)S(1)}, u32[]{:S(2)}, u32[]{:S(2)}) %collective-permute-start.19) | collective-permute-done | bytes 331808 | tf_op jit(solution)/shard_map/ppermute | solution.py:442
  962.2 5.6 gather_fusion.9
  967.8 5.4 select_select_fusion
  (320 shorter events, 112.7 us)
Async XLA Ops:
  7.2 207.6 %copy-start = (bf16[1000,1152]{1,0:T(8,128)(2,1)S(1)}, bf16[1000,1152]{1,0:T(8,128)(2,1)}, u32[]{:S(2)}) copy-start(bf16[1000,1152]{1,0:T(8,128)(2,1)} %param.32) | copy-start | bytes 6912004
  7.2 219.5 %all-gather.13.cloned.1.call-start = ((), (), s32[]{:S(2)}) async-start(), calls=%async_computation.9 | async-start | bytes 3041280 | tf_op jit(solution)/shard_map/all_gather | solution.py:430
  9.0 283.0 %all-gather.11.cloned.1.call-start = ((), (), s32[]{:S(2)}) async-start(), calls=%async_computation.8 | async-start | bytes 8515584 | tf_op jit(solution)/shard_map/all_gather | solution.py:430
  19.5 336.8 %all-gather.9.cloned.1.call-start = ((), (), s32[]{:S(2)}) async-start(), calls=%async_computation.7 | async-start | bytes 7299072 | tf_op jit(solution)/shard_map/all_gather | solution.py:430
  21.3 396.3 %all-gather.7.cloned.1.call-start = ((), (), s32[]{:S(2)}) async-start(), calls=%async_computation.6 | async-start | bytes 14598144 | tf_op jit(solution)/shard_map/all_gather | solution.py:430
  21.3 12.2 %copy-start.38 = (s32[8]{0:T(128)S(1)}, s32[8]{0:T(128)}, u32[]{:S(2)}) copy-start(s32[8]{0:T(128)} %param.29) | copy-start | bytes 100
  21.3 13.6 %copy-start.4 = (s32[8]{0:T(128)S(1)}, s32[8]{0:T(128)}, u32[]{:S(2)}) copy-start(s32[8]{0:T(128)} %param.30) | copy-start | bytes 100
  47.1 8.8 copy-start.45
  47.1 67.3 %all-to-all-start = ((bf16[32,64,1152]{2,1,0:T(8,128)(2,1)}), bf16[32,64,1152]{2,1,0:T(8,128)(2,1)}, u32[]{:S(2)}, u32[]{:S(2)}) async-start(bf16[32,64,1152]{2,1,0:T(8,128)(2,1)} %broadcast_select_fusion), calls=%async_computation | async-start | bytes 9437184 | tf_op jit(solution)/shard_map/all_to_all | solution.py:545
  52.5 79.1 %collective-permute-start = (s32[1,2,32]{2,1,0:T(2,128)S(1)}, s32[1,2,32]{2,1,0:T(2,128)S(1)}, u32[]{:S(2)}, u32[]{:S(2)}) collective-permute-start(s32[1,2,32]{2,1,0:T(2,128)S(1)} %add_bitcast_fusion.1), channel_id=1, source_target_pairs={{0,4},{4,0},{8,12},{12,8},{16,20},{20,16},{24,28},{28,24},{1,5},{5... | collective-permute-start | bytes 776 | tf_op jit(solution)/shard_map/ppermute | solution.py:442
  122.4 6.2 copy-start.44
  122.4 6.4 copy-start.37
  122.4 7.9 copy-start.43
  122.4 8.6 copy-start.39
  122.4 8.6 copy-start.40
  122.4 9.2 copy-start.33
  122.4 83.8 %all-to-all-start.1 = ((bf16[16,64,1152]{2,1,0:T(8,128)(2,1)}), bf16[16,64,1152]{2,1,0:T(8,128)(2,1)}, u32[]{:S(2)}, u32[]{:S(2)}) async-start(bf16[16,64,1152]{2,1,0:T(8,128)(2,1)} %broadcast_select_fusion.2), calls=%async_computation.1 | async-start | bytes 4718592 | tf_op jit(solution)/shard_map/all_to_all | solution.py:551
  131.7 3.7 collective-permute-start.1
  135.3 23.3 %collective-permute-start.2 = (s32[4,2,32]{2,1,0:T(2,128)S(1)}, s32[4,2,32]{2,1,0:T(2,128)S(1)}, u32[]{:S(2)}, u32[]{:S(2)}) collective-permute-start(s32[4,2,32]{2,1,0:T(2,128)S(1)} %pad_add_fusion), channel_id=1, source_target_pairs={{0,16},{4,20},{8,24},{12,28},{16,0},{20,4},{24,8},{28,12},{1,17},{... | collective-permute-start | bytes 3080 | tf_op jit(solution)/shard_map/ppermute | solution.py:442
  159.1 55.4 %copy-start.29 = (s32[128]{0:T(128)}, s32[128]{0:T(128)S(1)}, u32[]{:S(2)}) copy-start(s32[128]{0:T(128)S(1)} %get-tuple-element.144) | copy-start | bytes 1540
  159.1 55.7 %copy-start.35 = (s32[128]{0:T(128)}, s32[128]{0:T(128)S(1)}, u32[]{:S(2)}) copy-start(s32[128]{0:T(128)S(1)} %get-tuple-element.143) | copy-start | bytes 1540
  209.5 72.7 %all-to-all-start.3 = ((bf16[16,64,1152]{2,1,0:T(8,128)(2,1)}), bf16[16,64,1152]{2,1,0:T(8,128)(2,1)}, u32[]{:S(2)}, u32[]{:S(2)}) async-start(bf16[16,64,1152]{2,1,0:T(8,128)(2,1)} %param.26), calls=%async_computation.3 | async-start | bytes 4718592 | tf_op jit(solution)/shard_map/all_to_all | solution.py:553
  216.7 10.0 %copy-start.21 = (bf16[128,1152]{0,1:T(8,128)(2,1)}, bf16[128,1152]{0,1:T(8,128)(2,1)S(1)}, u32[]{:S(2)}) copy-start(bf16[128,1152]{0,1:T(8,128)(2,1)S(1)} %get-tuple-element.169) | copy-start | bytes 884740
  226.7 7.4 copy-start.22
  234.1 50.3 %copy-start.24 = (f32[4,256]{1,0:T(4,128)}, f32[4,256]{1,0:T(4,128)S(1)}, u32[]{:S(2)}) copy-start(f32[4,256]{1,0:T(4,128)S(1)} %fusion.10) | copy-start | bytes 12292
  234.1 50.2 %copy-start.27 = (f32[4,256]{1,0:T(4,128)}, f32[4,256]{1,0:T(4,128)S(1)}, u32[]{:S(2)}) copy-start(f32[4,256]{1,0:T(4,128)S(1)} %fusion.70) | copy-start | bytes 12292
  316.9 26.3 %copy-start.8 = (bf16[4,4,64,1152]{3,2,0,1:T(8,128)(2,1)S(1)}, bf16[4,4,64,1152]{3,2,0,1:T(8,128)(2,1)}, u32[]{:S(2)}) copy-start(bf16[4,4,64,1152]{3,2,0,1:T(8,128)(2,1)} %copy.173) | copy-start | bytes 7077892
  316.9 26.3 %copy-start.20 = (bf16[4,288,1152,1]{2,1,0,3:T(8,128)(2,1)S(1)}, bf16[4,288,1152,1]{2,1,0,3:T(8,128)(2,1)}, u32[]{:S(2)}) copy-start(bf16[4,288,1152,1]{2,1,0,3:T(8,128)(2,1)} %reshape.903) | copy-start | bytes 7962628
  518.3 73.4 %collective-permute-start.3 = (bf16[2,3,576,768]{3,2,1,0:T(8,128)(2,1)}, bf16[2,3,576,768]{3,2,1,0:T(8,128)(2,1)}, u32[]{:S(2)}, u32[]{:S(2)}) collective-permute-start(bf16[2,3,576,768]{3,2,1,0:T(8,128)(2,1)} %get-tuple-element.43), channel_id=1, source_target_pairs={{0,4},{4,0},{8,12},{12,8},{16,20},{20,16},{24,28},{28,24},{1,5},{5... | collective-permute-start | bytes 15925256 | tf_op jit(solution)/shard_map/ppermute | solution.py:442
  568.9 66.6 %collective-permute-start.4 = (bf16[2,3,576,768]{3,2,1,0:T(8,128)(2,1)}, bf16[2,3,576,768]{3,2,1,0:T(8,128)(2,1)}, u32[]{:S(2)}, u32[]{:S(2)}) collective-permute-start(bf16[2,3,576,768]{3,2,1,0:T(8,128)(2,1)} %get-tuple-element.46), channel_id=1, source_target_pairs={{0,4},{4,0},{8,12},{12,8},{16,20},{20,16},{24,28},{28,24},{1,5},{5... | collective-permute-start | bytes 15925256 | tf_op jit(solution)/shard_map/ppermute | solution.py:442
  591.8 9.5 slice-start.4
  591.8 9.5 slice-start.5
  597.3 7.0 slice-start
  599.0 79.6 %collective-permute-start.5 = (bf16[2,3,288,768]{3,2,1,0:T(8,128)(2,1)}, bf16[2,3,288,768]{3,2,1,0:T(8,128)(2,1)}, u32[]{:S(2)}, u32[]{:S(2)}) collective-permute-start(bf16[2,3,288,768]{3,2,1,0:T(8,128)(2,1)} %slice.215), channel_id=1, source_target_pairs={{0,16},{4,20},{8,24},{12,28},{16,0},{20,4},{24,8},{28,12},{1,17},{... | collective-permute-start | bytes 7962632 | tf_op jit(solution)/shard_map/ppermute | solution.py:442
  625.2 154.2 %all-to-all-start.2 = ((bf16[4,256,1152]{2,0,1:T(4,128)(2,1)}), bf16[4,256,1152]{2,0,1:T(4,128)(2,1)}, u32[]{:S(2)}, u32[]{:S(2)}) async-start(bf16[4,256,1152]{2,0,1:T(4,128)(2,1)} %copy.183), calls=%async_computation.2 | async-start | bytes 4718592 | tf_op jit(solution)/shard_map/all_to_all | solution.py:627
  635.6 34.1 %copy-start.34 = (f32[2]{0:T(128)S(1)}, f32[2]{0:T(128)}, u32[]{:S(2)}) copy-start(f32[2]{0:T(128)} %constant.274) | copy-start | bytes 28
  675.2 6.5 copy-start.9
  677.1 67.8 %collective-permute-start.11 = (bf16[2,3,288,768]{3,2,1,0:T(8,128)(2,1)}, bf16[2,3,288,768]{3,2,1,0:T(8,128)(2,1)}, u32[]{:S(2)}, u32[]{:S(2)}) collective-permute-start(bf16[2,3,288,768]{3,2,1,0:T(8,128)(2,1)} %slice.217), channel_id=1, source_target_pairs={{0,8},{4,12},{8,0},{12,4},{16,24},{20,28},{24,16},{28,20},{1,9},{5... | collective-permute-start | bytes 7962632 | tf_op jit(solution)/shard_map/ppermute | solution.py:442
  683.3 111.1 %collective-permute-start.21 = (bf16[2,3,144,768]{3,2,1,0:T(8,128)(2,1)S(1)}, bf16[2,3,144,768]{3,2,1,0:T(8,128)(2,1)}, u32[]{:S(2)}, u32[]{:S(2)}) collective-permute-start(bf16[2,3,144,768]{3,2,1,0:T(8,128)(2,1)S(1)} %slice.236), channel_id=1, source_target_pairs={{0,8},{4,12},{8,0},{12,4},{16,24},{20,28},{24,16},{28,20},{1,9},{5... | collective-permute-start | bytes 3981320 | tf_op jit(solution)/shard_map/ppermute | solution.py:442
  684.0 9.8 %copy-start.23 = (f32[4,1152]{1,0:T(4,128)S(1)}, f32[4,1152]{1,0:T(4,128)}, u32[]{:S(2)}) copy-start(f32[4,1152]{1,0:T(4,128)} %copy-done.22) | copy-start | bytes 55300
  684.0 9.8 %copy-start.28 = (f32[4,256]{1,0:T(4,128)S(1)}, f32[4,256]{1,0:T(4,128)}, u32[]{:S(2)}) copy-start(f32[4,256]{1,0:T(4,128)} %copy-done.27) | copy-start | bytes 12292
  693.8 19.4 %copy-start.25 = (f32[4,256]{1,0:T(4,128)S(1)}, f32[4,256]{1,0:T(4,128)}, u32[]{:S(2)}) copy-start(f32[4,256]{1,0:T(4,128)} %copy-done.24) | copy-start | bytes 12292
  710.2 8.3 collective-permute-start.6
  718.9 6.1 collective-permute-start.7
  725.3 19.6 %collective-permute-start.8 = (bf16[4,27792]{1,0:T(4,128)(2,1)S(1)}, bf16[4,27792]{1,0:T(4,128)(2,1)S(1)}, u32[]{:S(2)}, u32[]{:S(2)}) collective-permute-start(bf16[4,27792]{1,0:T(4,128)(2,1)S(1)} %pad_maximum_fusion.1), channel_id=1, source_target_pairs={{0,16},{4,20},{8,24},{12,28},{16,0},{20,4},{24,8},{28,12},{1,17},{... | collective-permute-start | bytes 667016 | tf_op jit(solution)/shard_map/ppermute | solution.py:442
  744.9 75.5 %collective-permute-start.15 = (bf16[2,576,1152]{2,1,0:T(8,128)(2,1)}, bf16[2,576,1152]{2,1,0:T(8,128)(2,1)}, u32[]{:S(2)}, u32[]{:S(2)}) collective-permute-start(bf16[2,576,1152]{2,1,0:T(8,128)(2,1)} %get-tuple-element.62), channel_id=1, source_target_pairs={{0,4},{4,0},{8,12},{12,8},{16,20},{20,16},{24,28},{28,24},{1,5},{5... | collective-permute-start | bytes 7962632 | tf_op jit(solution)/shard_map/ppermute | solution.py:442
  745.5 29.6 %collective-permute-start.9 = (bf16[8,27792]{1,0:T(8,128)(2,1)S(1)}, bf16[8,27792]{1,0:T(8,128)(2,1)S(1)}, u32[]{:S(2)}, u32[]{:S(2)}) collective-permute-start(bf16[8,27792]{1,0:T(8,128)(2,1)S(1)} %pad_maximum_fusion), channel_id=1, source_target_pairs={{0,8},{4,12},{8,0},{12,4},{16,24},{20,28},{24,16},{28,20},{1,9},{5... | collective-permute-start | bytes 1334024 | tf_op jit(solution)/shard_map/ppermute | solution.py:442
  761.8 62.4 %collective-permute-start.12 = (bf16[2,576,1152]{2,1,0:T(8,128)(2,1)}, bf16[2,576,1152]{2,1,0:T(8,128)(2,1)}, u32[]{:S(2)}, u32[]{:S(2)}) collective-permute-start(bf16[2,576,1152]{2,1,0:T(8,128)(2,1)} %get-tuple-element.60), channel_id=1, source_target_pairs={{0,4},{4,0},{8,12},{12,8},{16,20},{20,16},{24,28},{28,24},{1,5},{5... | collective-permute-start | bytes 7962632 | tf_op jit(solution)/shard_map/ppermute | solution.py:442
  779.4 19.9 %collective-permute-start.10 = (bf16[16,27792]{1,0:T(8,128)(2,1)}, bf16[16,27792]{1,0:T(8,128)(2,1)}, u32[]{:S(2)}, u32[]{:S(2)}) collective-permute-start(bf16[16,27792]{1,0:T(8,128)(2,1)} %concatenate.52), channel_id=1, source_target_pairs={{0,4},{4,0},{8,12},{12,8},{16,20},{20,16},{24,28},{28,24},{1,5},{5... | collective-permute-start | bytes 2668040 | tf_op jit(solution)/shard_map/ppermute | solution.py:442
  779.4 59.7 %all-to-all-start.4 = ((bf16[4,256,1152]{2,0,1:T(4,128)(2,1)}), bf16[4,256,1152]{2,0,1:T(4,128)(2,1)}, u32[]{:S(2)}, u32[]{:S(2)}) async-start(bf16[4,256,1152]{2,0,1:T(4,128)(2,1)} %copy.191), calls=%async_computation.4 | async-start | bytes 4718592 | tf_op jit(solution)/shard_map/all_to_all | solution.py:700
  788.3 6.1 copy-start.13
  788.3 6.1 copy-start.12
  789.5 72.4 %collective-permute-start.20 = (bf16[2,3,144,768]{3,2,1,0:T(8,128)(2,1)}, bf16[2,3,144,768]{3,2,1,0:T(8,128)(2,1)}, u32[]{:S(2)}, u32[]{:S(2)}) collective-permute-start(bf16[2,3,144,768]{3,2,1,0:T(8,128)(2,1)} %slice.233), channel_id=1, source_target_pairs={{0,16},{4,20},{8,24},{12,28},{16,0},{20,4},{24,8},{28,12},{1,17},{... | collective-permute-start | bytes 3981320 | tf_op jit(solution)/shard_map/ppermute | solution.py:442
  797.2 64.7 %collective-permute-start.22 = (bf16[2,3,144,768]{3,2,1,0:T(8,128)(2,1)}, bf16[2,3,144,768]{3,2,1,0:T(8,128)(2,1)}, u32[]{:S(2)}, u32[]{:S(2)}) collective-permute-start(bf16[2,3,144,768]{3,2,1,0:T(8,128)(2,1)} %add_convert_fusion.9), channel_id=1, source_target_pairs={{0,1},{1,0},{2,3},{3,2},{4,5},{5,4},{6,7},{7,6},{8,9},{9,8},{10,11... | collective-permute-start | bytes 3981320 | tf_op jit(solution)/shard_map/ppermute | solution.py:442
  813.9 6.6 copy-start.18
  823.1 34.5 %collective-permute-start.16 = (bf16[2,288,1152]{2,1,0:T(8,128)(2,1)S(1)}, bf16[2,288,1152]{2,1,0:T(8,128)(2,1)}, u32[]{:S(2)}, u32[]{:S(2)}) collective-permute-start(bf16[2,288,1152]{2,1,0:T(8,128)(2,1)S(1)} %slice.223), channel_id=1, source_target_pairs={{0,16},{4,20},{8,24},{12,28},{16,0},{20,4},{24,8},{28,12},{1,17},{... | collective-permute-start | bytes 3981320 | tf_op jit(solution)/shard_map/ppermute | solution.py:442
  830.8 33.5 %collective-permute-start.13 = (bf16[2,288,1152]{2,1,0:T(8,128)(2,1)}, bf16[2,288,1152]{2,1,0:T(8,128)(2,1)}, u32[]{:S(2)}, u32[]{:S(2)}) collective-permute-start(bf16[2,288,1152]{2,1,0:T(8,128)(2,1)} %slice.219), channel_id=1, source_target_pairs={{0,8},{4,12},{8,0},{12,4},{16,24},{20,28},{24,16},{28,20},{1,9},{5... | collective-permute-start | bytes 3981320 | tf_op jit(solution)/shard_map/ppermute | solution.py:442
  852.7 109.5 %all-to-all-start.5 = ((bf16[32,64,1152]{2,1,0:T(8,128)(2,1)}), bf16[32,64,1152]{2,1,0:T(8,128)(2,1)}, u32[]{:S(2)}, u32[]{:S(2)}) async-start(bf16[32,64,1152]{2,1,0:T(8,128)(2,1)} %broadcast_select_fusion.1), calls=%async_computation.5 | async-start | bytes 9437184 | tf_op jit(solution)/shard_map/all_to_all | solution.py:704
  859.9 66.4 %collective-permute-start.17 = (bf16[2,144,1152]{2,1,0:T(8,128)(2,1)S(1)}, bf16[2,144,1152]{2,1,0:T(8,128)(2,1)S(1)}, u32[]{:S(2)}, u32[]{:S(2)}) collective-permute-start(bf16[2,144,1152]{2,1,0:T(8,128)(2,1)S(1)} %slice.225), channel_id=1, source_target_pairs={{0,8},{4,12},{8,0},{12,4},{16,24},{20,28},{24,16},{28,20},{1,9},{5... | collective-permute-start | bytes 1990664 | tf_op jit(solution)/shard_map/ppermute | solution.py:442
  864.2 65.5 %collective-permute-start.23 = (bf16[1,3,144,768]{3,2,1,0:T(8,128)(2,1)S(1)}, bf16[1,3,144,768]{3,2,1,0:T(8,128)(2,1)S(1)}, u32[]{:S(2)}, u32[]{:S(2)}) collective-permute-start(bf16[1,3,144,768]{3,2,1,0:T(8,128)(2,1)S(1)} %slice.238), channel_id=1, source_target_pairs={{0,2},{1,3},{2,0},{3,1},{4,6},{5,7},{6,4},{7,5},{8,10},{9,11},{10,... | collective-permute-start | bytes 1990664 | tf_op jit(solution)/shard_map/ppermute | solution.py:442
  866.0 63.8 %collective-permute-start.14 = (bf16[2,144,1152]{2,1,0:T(8,128)(2,1)S(1)}, bf16[2,144,1152]{2,1,0:T(8,128)(2,1)S(1)}, u32[]{:S(2)}, u32[]{:S(2)}) collective-permute-start(bf16[2,144,1152]{2,1,0:T(8,128)(2,1)S(1)} %slice.221), channel_id=1, source_target_pairs={{0,16},{4,20},{8,24},{12,28},{16,0},{20,4},{24,8},{28,12},{1,17},{... | collective-permute-start | bytes 1990664 | tf_op jit(solution)/shard_map/ppermute | solution.py:442
  926.4 16.4 %collective-permute-start.18 = (bf16[2,144,1152]{2,1,0:T(8,128)(2,1)S(1)}, bf16[2,144,1152]{2,1,0:T(8,128)(2,1)S(1)}, u32[]{:S(2)}, u32[]{:S(2)}) collective-permute-start(bf16[2,144,1152]{2,1,0:T(8,128)(2,1)S(1)} %add_convert_fusion.15), channel_id=1, source_target_pairs={{0,1},{1,0},{2,3},{3,2},{4,5},{5,4},{6,7},{7,6},{8,9},{9,8},{10,11... | collective-permute-start | bytes 1990664 | tf_op jit(solution)/shard_map/ppermute | solution.py:442
  943.1 16.2 %copy-start.32 = (s32[864]{0:T(1024)S(1)}, s32[864]{0:T(1024)}, u32[]{:S(2)}) copy-start(s32[864]{0:T(1024)} %copy-done.31) | copy-start | bytes 10372
  943.1 16.0 %collective-permute-start.19 = (bf16[1,144,1152]{2,1,0:T(8,128)(2,1)S(1)}, bf16[1,144,1152]{2,1,0:T(8,128)(2,1)S(1)}, u32[]{:S(2)}, u32[]{:S(2)}) collective-permute-start(bf16[1,144,1152]{2,1,0:T(8,128)(2,1)S(1)} %slice.227), channel_id=1, source_target_pairs={{0,2},{1,3},{2,0},{3,1},{4,6},{5,7},{6,4},{7,5},{8,10},{9,11},{10,... | collective-permute-start | bytes 995336 | tf_op jit(solution)/shard_map/ppermute | solution.py:442
  (22 other events, 79.8 us)
Sparse Core Ops, SparseCore 0:
  11.5 65.4 all-gather.12
  80.5 122.9 all-gather.10
  207.0 105.5 all-gather.8
  315.9 101.6 all-gather.6

commit v4 on v3

--- a/solution.py
+++ b/solution.py
@@ -74,29 +74,51 @@
     return shifted * (1.0 / jnp.sum(shifted, axis=0, keepdims=True))
 
 
-def attend_kernel(proj_ref, gains_ref, cos_ref, sin_ref, out_ref):
+def attend_kernel(
+    x_ref, w_ref, gains_ref, cos_ref, sin_ref, proj_ref, att_ref, out_ref
+):
     head_dim = gains_ref.shape[1]
+    rows_all, length = att_ref.shape[1:]
     cut = feature_order(head_dim)[1]
     cos_tab, sin_tab = cos_ref[...], sin_ref[...]
+    proj = dot_11(w_ref[0, : 3 * rows_all], x_ref[...])
+    proj_ref[0] = proj
     outs = []
-    for head in range(proj_ref.shape[2] // head_dim):
-        rows = slice(head * head_dim, (head + 1) * head_dim)
+    for head in range(rows_all // head_dim):
         lows = []
         for kind in range(2):
-            raw = proj_ref[0, kind, rows, :]
+            start = kind * rows_all + head * head_dim
+            raw = proj[start : start + head_dim]
             scaled = raw * head_scale(raw) * gains_ref[kind]
             turned = scaled * cos_tab + partner(scaled, cut) * sin_tab
             lows.append(turned.astype(bf16))
-        value_low = proj_ref[0, 2, rows, :].astype(bf16)
+        start = 2 * rows_all + head * head_dim
+        value_low = proj[start : start + head_dim].astype(bf16)
         probs = softmax_first(dot_00(lows[1], lows[0]))
         outs.append(dot_10(value_low, probs.astype(bf16)))
-    out_ref[0] = jnp.concatenate(outs, axis=0).astype(bf16)
+    att = jnp.concatenate(outs, axis=0).astype(bf16)
+    att_ref[0] = att
+    part = dot_00(att, w_ref[0, 3 * rows_all :])
+    add_rows(out_ref, part, pl.program_id(0) == 0, pl.program_id(1), length)
+
+
+def add_rows(out_ref, part, first, index, length):
+    rows = pl.ds(pl.multiple_of(index * length, length), length)
+
+    @pl.when(first)
+    def _():
+        out_ref[rows, :] = part
+
+    @pl.when(jnp.logical_not(first))
+    def _():
+        out_ref[rows, :] += part
 
 
 def attend_back_kernel(
-    proj_ref, cot_ref, gains_ref, cos_ref, sin_ref, out_ref, gain_grad_ref
+    proj_ref, low_ref, w_ref, gains_ref, cos_ref, sin_ref, out_ref, gain_grad_ref, x_grad_ref
 ):
     head_dim = gains_ref.shape[1]
+    rows_all, length = proj_ref.shape[1] // 3, proj_ref.shape[2]
     cut = feature_order(head_dim)[1]
     cos_tab, sin_tab = cos_ref[...], sin_ref[...]
 
@@ -105,12 +127,12 @@
         gain_grad_ref[...] = jnp.zeros_like(gain_grad_ref)
 
     outs = [[], [], []]
-    cot_all = cot_ref[0].astype(f32)
-    for head in range(proj_ref.shape[2] // head_dim):
-        rows = slice(head * head_dim, (head + 1) * head_dim)
+    cot_all = dot_11(w_ref[0, 3 * rows_all :], low_ref[...])
+    for head in range(rows_all // head_dim):
         lows, units, scales = [], [], []
         for kind in range(2):
-            raw = proj_ref[0, kind, rows, :]
+            start = kind * rows_all + head * head_dim
+            raw = proj_ref[0, start : start + head_dim, :]
             scale = head_scale(raw)
             unit = raw * scale
             scaled = unit * gains_ref[kind]
@@ -118,8 +140,9 @@
             lows.append(turned.astype(bf16))
             units.append(unit)
             scales.append(scale)
-        value_low = proj_ref[0, 2, rows, :].astype(bf16)
-        cot_low = cot_all[rows].astype(bf16)
+        start = 2 * rows_all + head * head_dim
+        value_low = proj_ref[0, start : start + head_dim, :].astype(bf16)
+        cot_low = cot_all[head * head_dim : (head + 1) * head_dim].astype(bf16)
         probs = softmax_first(dot_00(lows[1], lows[0]))
         prob_grad = dot_00(value_low, cot_low)
         outs[2].append(dot_11(cot_low, probs.astype(bf16)))
@@ -133,121 +156,125 @@
             grad = grad * gains_ref[kind]
             along = jnp.mean(grad * units[kind], axis=0, keepdims=True)
             outs[kind].append(scales[kind] * (grad - units[kind] * along))
-    for kind in range(3):
-        out_ref[0, kind] = jnp.concatenate(outs[kind], axis=0).astype(bf16)
-
-
-def attend_specs(groups, rows, own, length, head_dim):
-    proj = pl.BlockSpec((1, 3, rows, length), lambda g, i: (g, 0, 0, i))
+    grads = jnp.concatenate(outs[0] + outs[1] + outs[2], axis=0).astype(bf16)
+    out_ref[0] = grads
+    part = dot_00(grads, w_ref[0, : 3 * rows_all])
+    add_rows(x_grad_ref, part, pl.program_id(0) == 0, pl.program_id(1), length)
+
+
+def attend_specs(groups, rows, own, length, width, head_dim):
+    proj = pl.BlockSpec((1, 3 * rows, length), lambda g, i: (g, 0, i))
     att = pl.BlockSpec((1, rows, length), lambda g, i: (g, 0, i))
+    x = pl.BlockSpec((length, width), lambda g, i: (i, 0))
+    w = pl.BlockSpec((1, 4 * rows, width), lambda g, i: (g, 0, 0))
     gains = pl.BlockSpec((2, head_dim, 1), lambda g, i: (0, 0, 0))
     table = pl.BlockSpec((head_dim, length), lambda g, i: (0, 0))
     grads = pl.BlockSpec((2, head_dim, length), lambda g, i: (0, 0, 0))
-    return proj, att, gains, table, grads
-
-
-def attend(proj, gains, tables, own):
-    groups, _, rows, tokens = proj.shape
+    total = pl.BlockSpec((own * length, width), lambda g, i: (0, 0))
+    return proj, att, x, w, gains, table, grads, total
+
+
+def attend(x, weights, gains, tables, own):
+    groups, rows, width = weights.shape[0], weights.shape[1] // 4, weights.shape[2]
+    tokens = x.shape[0]
     length, head_dim = tokens // own, gains.shape[1]
-    proj_s, att_s, gains_s, table_s, _ = attend_specs(groups, rows, own, length, head_dim)
+    proj_s, att_s, x_s, w_s, gains_s, table_s, _, total_s = attend_specs(
+        groups, rows, own, length, width, head_dim
+    )
     return pl.pallas_call(
         attend_kernel,
         grid=(groups, own),
-        in_specs=[proj_s, gains_s, table_s, table_s],
-        out_specs=att_s,
-        out_shape=jax.ShapeDtypeStruct((groups, rows, tokens), bf16),
-        compiler_params=pltpu.CompilerParams(vmem_limit_bytes=48 << 20),
-        cost_estimate=pl.CostEstimate(
-            flops=4 * groups * rows * tokens * length,
-            bytes_accessed=proj.size * 4 + groups * rows * tokens * 2,
-            transcendentals=groups * rows // head_dim * tokens * length,
-        ),
-        name="attend",
-    )(proj, gains, *tables)
-
-
-def attend_back(proj, cot, gains, tables, own):
-    groups, _, rows, tokens = proj.shape
-    length, head_dim = tokens // own, gains.shape[1]
-    proj_s, att_s, gains_s, table_s, grads_s = attend_specs(groups, rows, own, length, head_dim)
-    return pl.pallas_call(
-        attend_back_kernel,
-        grid=(groups, own),
-        in_specs=[proj_s, att_s, gains_s, table_s, table_s],
-        out_specs=[proj_s, grads_s],
+        in_specs=[x_s, w_s, gains_s, table_s, table_s],
+        out_specs=[proj_s, att_s, total_s],
         out_shape=[
-            jax.ShapeDtypeStruct(proj.shape, bf16),
-            jax.ShapeDtypeStruct((2, head_dim, length), f32),
-        ],
-        compiler_params=pltpu.CompilerParams(vmem_limit_bytes=48 << 20),
-        cost_estimate=pl.CostEstimate(
-            flops=10 * groups * rows * tokens * length,
-            bytes_accessed=proj.size * 6 + groups * rows * tokens * 2,
-            transcendentals=groups * rows // head_dim * tokens * length,
-        ),
-        name="attend_back",
-    )(proj, cot, gains, *tables)
-
-
-def sigmoid(values):
-    return 1.0 / (1.0 + jnp.exp(-values))
-
-
-def mlp_kernel(x_ref, w_ref, d_ref, save_ref, out_ref):
-    first = (pl.program_id(0) == 0) & (pl.program_id(1) == 0)
-    step = math.gcd(x_ref.shape[0], 256)
-
-    def body(index, carry):
-        rows = pl.ds(pl.multiple_of(index * step, step), step)
-        x_rows = x_ref[rows, :]
-        gate = dot_11(x_rows, w_ref[0, 0])
-        up = dot_11(x_rows, w_ref[0, 1])
-        save_ref[0, 0, rows, :] = gate
-        save_ref[0, 1, rows, :] = up
-        hidden = (gate * sigmoid(gate) * up).astype(bf16)
-        part = dot_10(hidden, d_ref[0])
-
-        @pl.when(first)
-        def _():
-            out_ref[rows, :] = part
-
-        @pl.when(jnp.logical_not(first))
-        def _():
-            out_ref[rows, :] += part
-
-        return carry
-
-    lax.fori_loop(0, x_ref.shape[0] // step, body, 0)
-
-
-def mlp(x, expand, down):
-    groups, _, units, width = expand.shape
-    tokens = x.shape[0]
-    block = math.gcd(units, 384)
-    return pl.pallas_call(
-        mlp_kernel,
-        grid=(groups, units // block),
-        in_specs=[
-            pl.BlockSpec((tokens, width), lambda g, h: (0, 0)),
-            pl.BlockSpec((1, 2, block, width), lambda g, h: (g, 0, h, 0)),
-            pl.BlockSpec((1, block, width), lambda g, h: (g, h, 0)),
-        ],
-        out_specs=[
-            pl.BlockSpec((1, 2, tokens, block), lambda g, h: (g, 0, 0, h)),
-            pl.BlockSpec((tokens, width), lambda g, h: (0, 0)),
-        ],
-        out_shape=[
-            jax.ShapeDtypeStruct((groups, 2, tokens, units), f32),
+            jax.ShapeDtypeStruct((groups, 3 * rows, tokens), f32),
+            jax.ShapeDtypeStruct((groups, rows, tokens), bf16),
             jax.ShapeDtypeStruct((tokens, width), f32),
         ],
         compiler_params=pltpu.CompilerParams(vmem_limit_bytes=56 << 20),
         cost_estimate=pl.CostEstimate(
+            flops=groups * rows * tokens * (4 * length + 8 * width),
+            bytes_accessed=14 * groups * rows * tokens,
+            transcendentals=groups * rows // head_dim * tokens * length,
+        ),
+        name="attend",
+    )(x, weights, gains, *tables)
+
+
+def attend_back(proj, low, weights, gains, tables, own):
+    groups, rows, width = weights.shape[0], weights.shape[1] // 4, weights.shape[2]
+    tokens = low.shape[0]
+    length, head_dim = tokens // own, gains.shape[1]
+    proj_s, _, x_s, w_s, gains_s, table_s, grads_s, total_s = attend_specs(
+        groups, rows, own, length, width, head_dim
+    )
+    return pl.pallas_call(
+        attend_back_kernel,
+        grid=(groups, own),
+        in_specs=[proj_s, x_s, w_s, gains_s, table_s, table_s],
+        out_specs=[proj_s, grads_s, total_s],
+        out_shape=[
+            jax.ShapeDtypeStruct(proj.shape, bf16),
+            jax.ShapeDtypeStruct((2, head_dim, length), f32),
+            jax.ShapeDtypeStruct((tokens, width), f32),
+        ],
+        compiler_params=pltpu.CompilerParams(vmem_limit_bytes=56 << 20),
+        cost_estimate=pl.CostEstimate(
+            flops=groups * rows * tokens * (10 * length + 8 * width),
+            bytes_accessed=18 * groups * rows * tokens,
+            transcendentals=groups * rows // head_dim * tokens * length,
+        ),
+        name="attend_back",
+    )(proj, low, weights, gains, *tables)
+
+
+def sigmoid(values):
+    return 1.0 / (1.0 + jnp.exp(-values))
+
+
+def kind_of(w_ref, kind):
+    pieces, _, rows, width = w_ref.shape[1:]
+    return w_ref[0, :, kind].reshape(pieces * rows, width)
+
+
+def mlp_kernel(x_ref, w_ref, save_ref, out_ref):
+    first = pl.program_id(0) == 0
+    x = x_ref[...]
+    gate = dot_11(x, kind_of(w_ref, 0))
+    up = dot_11(x, kind_of(w_ref, 1))
+    save_ref[0, 0] = gate.astype(bf16)
+    save_ref[0, 1] = up.astype(bf16)
+    hidden = (gate * sigmoid(gate) * up).astype(bf16)
+    part = dot_10(hidden, kind_of(w_ref, 2))
+    add_rows(out_ref, part, first, 0, x.shape[0])
+
+
+def mlp(x, weights):
+    groups, pieces, _, rows, width = weights.shape
+    units, tokens = pieces * rows, x.shape[0]
+    return pl.pallas_call(
+        mlp_kernel,
+        grid=(groups,),
+        in_specs=[
+            pl.BlockSpec((tokens, width), lambda g: (0, 0)),
+            pl.BlockSpec((1, pieces, 3, rows, width), lambda g: (g, 0, 0, 0, 0)),
+        ],
+        out_specs=[
+            pl.BlockSpec((1, 2, tokens, units), lambda g: (g, 0, 0, 0)),
+            pl.BlockSpec((tokens, width), lambda g: (0, 0)),
+        ],
+        out_shape=[
+            jax.ShapeDtypeStruct((groups, 2, tokens, units), bf16),
+            jax.ShapeDtypeStruct((tokens, width), f32),
+        ],
+        compiler_params=pltpu.CompilerParams(vmem_limit_bytes=60 << 20),
+        cost_estimate=pl.CostEstimate(
             flops=6 * groups * units * tokens * width,
-            bytes_accessed=8 * groups * units * tokens + 6 * groups * units * width,
+            bytes_accessed=4 * groups * units * tokens + 6 * groups * units * width,
             transcendentals=groups * units * tokens,
         ),
         name="mlp",
-    )(x, expand, down)
+    )(x, weights)
 
 
 def fill_rows(order_ref, source_ref, target_ref):
@@ -257,23 +284,23 @@
 
 
 def mlp_back_kernel(
-    m_ref, e_ref, xt_ref, lowt_ref, low_ref, save_ref, w_ref, d_ref,
+    m_ref, e_ref, xt_ref, lowt_ref, low_ref, save_ref, w_ref,
     keep_ref, send_ref, two_ref, xs, lows, parts,
 ):
-    first = (pl.program_id(0) == 0) & (pl.program_id(1) == 0)
+    first = pl.program_id(0) == 0
     tokens, width = low_ref.shape
-    step = math.gcd(tokens, 256)
+    step = math.gcd(tokens, 512)
 
     @pl.when(first)
     def _():
         fill_rows(e_ref, xt_ref, xs)
         fill_rows(e_ref, lowt_ref, lows)
 
-    def body(index, carry):
-        rows = pl.ds(pl.multiple_of(index * step, step), step)
-        hidden_grad = dot_11(low_ref[rows, :], d_ref[0])
-        gate = save_ref[0, 0, rows, :]
-        up = save_ref[0, 1, rows, :]
+    for index in range(tokens // step):
+        rows = pl.ds(index * step, step)
+        hidden_grad = dot_11(low_ref[rows, :], kind_of(w_ref, 2))
+        gate = save_ref[0, 0, rows, :].astype(f32)
+        up = save_ref[0, 1, rows, :].astype(f32)
         sig = sigmoid(gate)
         swish = gate * sig
         gate_low = (hidden_grad * up * (sig + swish * (1.0 - sig))).astype(bf16)
@@ -281,74 +308,54 @@
         parts[0, rows, :] = gate_low
         parts[1, rows, :] = up_low
         parts[2, rows, :] = (swish * up).astype(bf16)
-        part = dot_10(gate_low, w_ref[0, 0]) + dot_10(up_low, w_ref[0, 1])
-
-        @pl.when(first)
-        def _():
-            two_ref[rows, :] = part
-
-        @pl.when(jnp.logical_not(first))
-        def _():
-            two_ref[rows, :] += part
-
-        return carry
-
-    lax.fori_loop(0, tokens // step, body, 0)
+        part = dot_10(gate_low, kind_of(w_ref, 0)) + dot_10(up_low, kind_of(w_ref, 1))
+        add_rows(two_ref, part, first, index, step)
+
     half = width // 2
-    tile = math.gcd(half, 288)
-
-    for out_ref, base in ((keep_ref, 0), (send_ref, half)):
-
-        def grads(index, carry):
-            place = pl.multiple_of(index * tile, tile)
-            rows = pl.ds(pl.multiple_of(base + place, tile), tile)
-            x_rows = xs[rows, :]
-            for kind in range(2):
-                out_ref[0, kind, pl.ds(place, tile), :] = dot_10(x_rows, parts[kind]).astype(bf16)
-            out_ref[0, 2, pl.ds(place, tile), :] = dot_10(lows[rows, :], parts[2]).astype(bf16)
-            return carry
-
-        lax.fori_loop(0, half // tile, grads, 0)
-
-
-def mlp_back(m_order, e_order, xt, lowt, low, save, expand, down):
-    units, width = down.shape[1:]
-    tokens = low.shape[0]
+    for out_ref, rows in ((keep_ref, slice(0, half)), (send_ref, slice(half, width))):
+        x_rows = xs[rows, :]
+        for kind in range(2):
+            out_ref[0, kind] = dot_10(x_rows, parts[kind]).astype(bf16)
+        out_ref[0, 2] = dot_10(lows[rows, :], parts[2]).astype(bf16)
+
+
+def mlp_back(m_order, e_order, xt, lowt, low, save, weights):
+    _, pieces, _, rows, width = weights.shape
+    units, tokens = pieces * rows, low.shape[0]
     blocks = m_order.shape[0]
-    block = math.gcd(units, 384)
-    whole = lambda p, h, m, e: (0, 0)
-    whole3 = lambda p, h, m, e: (0, 0, 0)
+    once = pl.Buffered(1)
+    whole = lambda p, m, e: (0, 0)
+    whole3 = lambda p, m, e: (0, 0, 0)
     half = jax.ShapeDtypeStruct((blocks, 3, width // 2, units), bf16)
-    half_spec = pl.BlockSpec((1, 3, width // 2, block), lambda p, h, m, e: (p, 0, 0, h))
+    half_spec = pl.BlockSpec((1, 3, width // 2, units), lambda p, m, e: (p, 0, 0, 0))
     return pl.pallas_call(
         mlp_back_kernel,
         grid_spec=pltpu.PrefetchScalarGridSpec(
             num_scalar_prefetch=2,
-            grid=(blocks, units // block),
+            grid=(blocks,),
             in_specs=[
-                pl.BlockSpec(xt.shape, whole3),
-                pl.BlockSpec(lowt.shape, whole3),
-                pl.BlockSpec((tokens, width), whole),
-                pl.BlockSpec((1, 2, tokens, block), lambda p, h, m, e: (m[p], 0, 0, h)),
-                pl.BlockSpec((1, 2, block, width), lambda p, h, m, e: (m[p], 0, h, 0)),
-                pl.BlockSpec((1, block, width), lambda p, h, m, e: (m[p], h, 0)),
+                pl.BlockSpec(xt.shape, whole3, pipeline_mode=once),
+                pl.BlockSpec(lowt.shape, whole3, pipeline_mode=once),
+                pl.BlockSpec((tokens, width), whole, pipeline_mode=once),
+                pl.BlockSpec((1, 2, tokens, units), lambda p, m, e: (m[p], 0, 0, 0)),
+                pl.BlockSpec((1, pieces, 3, rows, width), lambda p, m, e: (m[p], 0, 0, 0, 0)),
             ],
             out_specs=[half_spec, half_spec, pl.BlockSpec((tokens, width), whole)],
             scratch_shapes=[
                 pltpu.VMEM((width, tokens), bf16),
                 pltpu.VMEM((width, tokens), bf16),
-                pltpu.VMEM((3, tokens, block), bf16),
+                pltpu.VMEM((3, tokens, units), bf16),
             ],
         ),
         out_shape=[half, half, jax.ShapeDtypeStruct((tokens, width), f32)],
-        compiler_params=pltpu.CompilerParams(vmem_limit_bytes=60 << 20),
+        compiler_params=pltpu.CompilerParams(vmem_limit_bytes=62 << 20),
         cost_estimate=pl.CostEstimate(
             flops=12 * blocks * units * tokens * width,
-            bytes_accessed=8 * blocks * units * tokens + 12 * blocks * units * width,
+            bytes_accessed=4 * blocks * units * tokens + 12 * blocks * units * width,
             transcendentals=blocks * units * tokens,
         ),
         name="mlp_back",
-    )(m_order, e_order, xt, lowt, low, save, expand, down)
+    )(m_order, e_order, xt, lowt, low, save, weights)
 
 
 def attend_grads_kernel(
@@ -361,21 +368,11 @@
 
     width = xs.shape[0]
     half = width // 2
-    tile = math.gcd(half, 288)
     columns = proj_ref.shape[1]
 
-    for out_ref, base in ((keep_ref, 0), (send_ref, half)):
-
-        def grads(index, carry):
-            place = pl.multiple_of(index * tile, tile)
-            rows = pl.ds(pl.multiple_of(base + place, tile), tile)
-            part = dot_11(xs[rows, :], proj_ref[0]).astype(bf16)
-            out_ref[0, pl.ds(place, tile), :columns] = part
-            part = dot_11(lows[rows, :], att_ref[0]).astype(bf16)
-            out_ref[0, pl.ds(place, tile), columns:] = part
-            return carry
-
-        lax.fori_loop(0, half // tile, grads, 0)
+    for out_ref, rows in ((keep_ref, slice(0, half)), (send_ref, slice(half, width))):
+        out_ref[0, :, :columns] = dot_11(xs[rows, :], proj_ref[0]).astype(bf16)
+        out_ref[0, :, columns:] = dot_11(lows[rows, :], att_ref[0]).astype(bf16)
 
 
 def attend_grads(m_order, e_order, xt, lowt, proj, att):
@@ -391,8 +388,8 @@
             num_scalar_prefetch=2,
             grid=(blocks,),
             in_specs=[
-                pl.BlockSpec(xt.shape, whole3),
-                pl.BlockSpec(lowt.shape, whole3),
+                pl.BlockSpec(xt.shape, whole3, pipeline_mode=pl.Buffered(1)),
+                pl.BlockSpec(lowt.shape, whole3, pipeline_mode=pl.Buffered(1)),
                 pl.BlockSpec((1, 3 * rows, tokens), lambda p, m, e: (m[p], 0, 0)),
                 pl.BlockSpec((1, rows, tokens), lambda p, m, e: (m[p], 0, 0)),
             ],
@@ -421,16 +418,13 @@
     return jnp.einsum(spec, a, b, preferred_element_type=f32)
 
 
-def gather_rows(block, dp_size):
-    rows, width = block.shape
-    share = -(-rows // dp_size)
-    if rows % dp_size:
-        block = jnp.pad(block, ((0, share * dp_size - rows), (0, 0)))
-    piece = lax.dynamic_slice_in_dim(block, lax.axis_index("dp") * share, share, 0)
-    whole = lax.all_gather(piece, ("mp", "dp"), axis=0, tiled=True)
-    if rows % dp_size:
-        whole = whole.reshape(-1, share * dp_size, width)[:, :rows].reshape(-1, width)
-    return whole
+def gather_pieces(piece, mp_size):
+    whole = lax.all_gather(piece, ("mp", "dp"), axis=0, tiled=False)
+    return whole.reshape((mp_size, -1) + piece.shape)
+
+
+def take_rows(values, index):
+    return jnp.take(values, index, axis=0, mode="clip")
 
 
 def bits_of(size):
@@ -522,12 +516,6 @@
     places = columns // head_dim * head_dim + order[columns % head_dim]
     places = jnp.where(columns < 2 * local_dim, places, columns)
     turn = (places[:, None] == columns[None, :]).astype(bf16)
-    qkv_block = ein("rc,dc->rd", turn, qkv_weight.reshape(model_width, -1)).astype(bf16)
-    qkv_full = gather_rows(qkv_block, dp_size)
-    out_full = gather_rows(out_weight, dp_size)
-    expand_full = gather_rows(expand_weight.reshape(model_width, -1).T, dp_size)
-    down_full = gather_rows(down_weight, dp_size)
-
     starts = jnp.cumsum(image_counts) - image_counts
     finish = starts + image_counts
     my_start = starts[dp_index]
@@ -541,13 +529,38 @@
     pair_slot = pair_ids % slot_count
     send_index = pair_slot * dp_size + jnp.mod(inverse[pair_peer] - my_start, dp_size)
     send_index = jnp.minimum(send_index, capacity - 1)
-    send_patches = jnp.take(patches, send_index, axis=0)
+    send_patches = take_rows(patches, send_index)
+    qkv_weight, out_weight, expand_weight, down_weight, send_patches = tie(
+        qkv_weight, out_weight, expand_weight, down_weight, send_patches
+    )
+    share = 4 * local_dim // dp_size
+    spots = dp_index * share + jnp.arange(share)
+    take_qkv = jnp.where(spots < 3 * local_dim, places[jnp.minimum(spots, 3 * local_dim - 1)], -1)
+    take_qkv = (take_qkv[:, None] == columns[None, :]).astype(bf16)
+    take_out = (spots[:, None] - 3 * local_dim == jnp.arange(local_dim)[None, :]).astype(bf16)
+    attend_piece = ein("rc,dc->rd", take_qkv, qkv_weight.reshape(model_width, -1))
+    attend_piece = (attend_piece + dot(take_out, out_weight)).astype(bf16)
+    share = unit_count // dp_size
+    spots = dp_index * share + jnp.arange(share)
+    take_units = (spots[:, None] == jnp.arange(unit_count)[None, :]).astype(bf16)
+    mlp_piece = jnp.stack(
+        [
+            ein("rf,df->rd", take_units, expand_weight[:, 0]).astype(bf16),
+            ein("rf,df->rd", take_units, expand_weight[:, 1]).astype(bf16),
+            lax.dynamic_slice_in_dim(down_weight, dp_index * share, share, 0),
+        ]
+    )
+    attend_full = gather_pieces(attend_piece, mp_size).reshape(mp_size, 4 * local_dim, -1)
+    mlp_full = gather_pieces(mlp_piece, mp_size)
+    if share % 16:
+        mlp_full = mlp_full.swapaxes(1, 2).reshape(mp_size, 1, 3, unit_count, model_width)
+
     recv_patches = lax.all_to_all(send_patches, "dp", split_axis=0, concat_axis=0, tiled=True)
     rank_ids = jnp.arange(images) * dp_size + my_place
     source = jnp.sum((finish[None, :] <= rank_ids[:, None]).astype(jnp.int32), axis=1)
     within = rank_ids - starts[source]
     recv_index = source * slot_count + within // dp_size
-    latent = jnp.take(recv_patches, recv_index, axis=0)
+    latent = take_rows(recv_patches, recv_index)
     latent = lax.all_to_all(latent, "mp", split_axis=0, concat_axis=1, tiled=True)
     cotangent, latent = tie(cotangent, latent)
     cot = lax.all_to_all(cotangent, "mp", split_axis=0, concat_axis=1, tiled=True)
@@ -608,20 +621,16 @@
     gate_two = modulation[:, 5]
 
     latent_f = latent.astype(f32)
-    out_cot = cot.astype(f32) * weights[:, None, None]
     normed = rms_scale(latent_f, scale_one, shift_one).astype(bf16)
     normed_flat = normed.reshape(-1, model_width)
-    proj = ein("cd,nd->cn", qkv_full, normed_flat)
-    proj = proj.reshape(mp_size, 3, local_dim, own * length)
-    attended = attend(proj, gains_f, tables, own)
-    branch_one = ein("mcn,mcd->nd", attended, out_full.reshape(mp_size, local_dim, -1))
+    proj, attended, branch_one = attend(normed_flat, attend_full, gains_f, tables, own)
     branch_one = branch_one.reshape(own, length, model_width)
     middle = latent_f + gate_one * branch_one
     normed_two = rms_scale(middle, scale_two, shift_two).astype(bf16)
     two_flat = normed_two.reshape(-1, model_width)
-    expand_blocks = expand_full.reshape(mp_size, 2, unit_count, model_width)
-    down_blocks = down_full.reshape(mp_size, unit_count, model_width)
-    save, branch_two = mlp(two_flat, expand_blocks, down_blocks)
+    save, branch_two = mlp(two_flat, mlp_full)
+    branch_two, cot = tie(branch_two, cot)
+    out_cot = cot.astype(f32) * weights[:, None, None]
     branch_two = branch_two.reshape(own, length, model_width)
     result = (middle + gate_two * branch_two).astype(bf16)
     result = lax.all_to_all(result, "mp", split_axis=1, concat_axis=0, tiled=True)
@@ -645,14 +654,14 @@
 
     two_t, down_t = by_owner(two_flat), by_owner(down_low)
     kept_one, sent_one, two_one = mlp_back(
-        m_orders[1], e_orders[1], two_t, down_t, down_low, save, expand_blocks, down_blocks
+        m_orders[1], e_orders[1], two_t, down_t, down_low, save, mlp_full
     )
     got_one = swap(sent_one, "dp", dp_bits[1][0])
     kept_zero, sent_zero, two_zero = mlp_back(
-        m_orders[0], e_orders[0], two_t, down_t, down_low, save, expand_blocks, down_blocks
+        m_orders[0], e_orders[0], two_t, down_t, down_low, save, mlp_full
     )
     got_zero = swap(sent_zero, "dp", dp_bits[0][0])
-    two_zero, got_one = tie(two_zero, got_one)
+    two_zero, got_one, result = tie(two_zero, got_one, result)
     kept_one, sent_one = split(add_low(kept_one, got_one), 2)
     got_one = swap(sent_one, "dp", dp_bits[1][1])
     two_parts = (two_zero, two_one)
@@ -662,16 +671,15 @@
     middle_grad = middle_grad + out_cot
     gate_one_grad = jnp.sum(middle_grad * branch_one, axis=1)
     branch_low = (gate_one * middle_grad).astype(bf16).reshape(-1, model_width)
-    attended_low = ein("cd,nd->cn", out_full, branch_low).astype(bf16)
-    attended_low = attended_low.reshape(mp_size, local_dim, own * length)
-    attended_low, got_zero = tie(attended_low, got_zero)
+    branch_low, got_zero = tie(branch_low, got_zero)
     kept_zero, sent_zero = split(add_low(kept_zero, got_zero), 2)
     got_zero = swap(sent_zero, "dp", dp_bits[0][1])
-    projected_low, gains_grad = attend_back(proj, attended_low, gains_f, tables, own)
+    projected_low, gains_grad, normed_grad = attend_back(
+        proj, branch_low, attend_full, gains_f, tables, own
+    )
     gains_grad = jnp.sum(gains_grad, axis=2) * jnp.array([[head_dim ** (-0.5)], [1.0]], f32)
-    projected_low, got_one = tie(projected_low, got_one)
+    projected_low, normed_grad, got_one = tie(projected_low, normed_grad, got_one)
     mlp_one = halve(add_low(kept_one, got_one), "dp", dp_bits[1][2:], 2)
-    normed_grad = ein("cn,cd->nd", projected_low.reshape(-1, own * length), qkv_full)
     normed_grad = normed_grad.reshape(own, length, model_width)
     norm_val, norm_pull = jax.vjp(rms_scale, latent_f, scale_one, shift_one)
     latent_grad, scale_one_grad, shift_one_grad = norm_pull(normed_grad)
@@ -685,28 +693,34 @@
             e_orders[which],
             normed_t,
             branch_t,
-            projected_low.reshape(mp_size, 3 * local_dim, -1),
+            projected_low,
             attended,
         )
         return kept, swap(sent, "dp", dp_bits[which][0])
 
-    attend_one = halve(add_low(*grads_of(1)), "dp", dp_bits[1][1:], 1)
+    kept_one, got_one = grads_of(1)
     normed_t, got_zero = tie(normed_t, got_zero)
     mlp_zero = halve(add_low(kept_zero, got_zero), "dp", dp_bits[0][2:], 2)
-    attend_zero = halve(add_low(*grads_of(0)), "dp", dp_bits[0][1:], 1)
+    kept_zero, got_zero = grads_of(0)
+    kept_zero, got_one = tie(kept_zero, got_one)
+    attend_one = halve(add_low(kept_one, got_one), "dp", dp_bits[1][1:], 1)
+    kept_zero, sent_zero = split(add_low(kept_zero, got_zero), 1)
+    got_zero = swap(sent_zero, "dp", dp_bits[0][1])
     mlp_grad = reduce_mp(mlp_zero, mlp_one)
+
+    latent_back = lax.all_to_all(latent_grad, "mp", split_axis=1, concat_axis=0, tiled=True)
+    latent_back, kept_zero = tie(latent_back, kept_zero)
+    attend_zero = halve(add_low(kept_zero, got_zero), "dp", dp_bits[0][2:], 1)
     attend_grad = reduce_mp(attend_zero, attend_one)
-
-    latent_back = lax.all_to_all(latent_grad, "mp", split_axis=1, concat_axis=0, tiled=True)
     back_within = pair_slot * dp_size + jnp.mod(my_place - starts[pair_peer], dp_size)
     back_slot = jnp.clip((starts[pair_peer] + back_within - my_place) // dp_size, 0, images - 1)
-    back_patches = jnp.take(latent_back, back_slot, axis=0)
+    back_patches = take_rows(latent_back, back_slot)
     got_patches = lax.all_to_all(back_patches, "dp", split_axis=0, concat_axis=0, tiled=True)
     slot_ids = jnp.arange(capacity)
     slot_live = slot_ids < my_count
     home_peer = dest_perm[jnp.mod(my_start + slot_ids, dp_size)]
     home_index = home_peer * slot_count + jnp.minimum(slot_ids // dp_size, slot_count - 1)
-    patch_grad = jnp.where(slot_live[:, None, None], jnp.take(got_patches, home_index, axis=0), 0)
+    patch_grad = jnp.where(slot_live[:, None, None], take_rows(got_patches, home_index), 0)
 
     modulation_grad = jnp.stack(
         [

time: 987 us -> 947 us (0.959)
  local copies, waits for them, and re-layouts: 188 us -> 148 us
  matrix products: 67.4 us -> 27.8 us
  other arithmetic: 90.7 us -> 120 us
  Pallas kernels: 242 us -> 252 us
    all_gather x4 -> x2, waiting for transfers between devices: 61.3 us -> 0.01 us  [gather_pieces(): whole = lax.all_gather(piece, ('mp', 'dp'), axis=0, tiled=False)]
    dot_general x9 -> x7, matrix products: 54.5 us -> 12.8 us  [ein(): return jnp.einsum(spec, a, b, preferred_element_type=f32)]
    all_to_all x1, waiting for transfers between devices: 44.1 us -> 84 us  [shards(): lax.all_to_all(cotangent, 'mp', split_axis=0, concat_axis=1, tiled=True)]
    pallas_call x2, Pallas kernels: 101 us -> 71.8 us  [mlp_back(): pl.pallas_call(mlp_back_kernel, grid_spec=pltpu.PrefetchScalarGridSpec(nu...]
    pallas_call x1, Pallas kernels: 34 us -> 57.2 us  [attend_back(): pl.pallas_call(attend_back_kernel, grid=(groups, own), in_specs=[proj_s,...]
    reshape x3 -> x0, local copies, waits for them, and re-layouts: 19.8 us -> none  [the longest x1 10.3 us: shards(): expand_full = gather_rows(expand_weight.reshape(model_width, -1).T, dp_size)]
    pallas_call x2, Pallas kernels: 76.8 us -> 96.5 us  [the longest x1 62.7 us: attend(): pl.pallas_call(attend_kernel, grid=(groups, own), in_specs=[x_s, w_s, gai...]
    dot_general x2 -> x0, local copies, waits for them, and re-layouts: 19.1 us -> none  [ein(): return jnp.einsum(spec, a, b, preferred_element_type=f32)]
  transfers between devices with their start and end apart: 34 -> 32, of which waited for: 11 -> 10; matrix products, arithmetic and copies ran while one was open for 33% -> 25% of each run, Pallas kernels for 14% -> 19%
where the time goes in v4:
time: 947 us; the launch traced here: 938 us
  waiting for transfers between devices  326 us (34%)
  Pallas kernels  252 us (27%)
  local copies, waits for them, and re-layouts  148 us (16%)
  other arithmetic  120 us (13%)
  starting transfers between devices  50.2 us (5%)
  matrix products  27.8 us (3%)
  between operations  15.8 us (2%)
    ppermute x24, waiting for transfers between devices, swap(): return lax.ppermute(values, axis, [(i, i ^ bit) for i in range(size)])  96.2 us
    all_to_all x1, waiting for transfers between devices, shards(): lax.all_to_all(cotangent, 'mp', split_axis=0, concat_axis=1, tiled=True)  84 us
    all_to_all x1, waiting for transfers between devices, shards(): lax.all_to_all(send_patches, 'dp', split_axis=0, concat_axis=0, tiled=True)  74.6 us
    pallas_call x2, Pallas kernels, mlp_back(): pl.pallas_call(mlp_back_kernel, grid_spec=pltpu.PrefetchScalarGridSpec(nu...  71.8 us
    pallas_call x1, Pallas kernels, attend(): pl.pallas_call(attend_kernel, grid=(groups, own), in_specs=[x_s, w_s, gai...  62.7 us
    pallas_call x1, Pallas kernels, attend_back(): pl.pallas_call(attend_back_kernel, grid=(groups, own), in_specs=[proj_s,...  57.2 us
    all_to_all x1, waiting for transfers between devices, shards(): lax.all_to_all(latent, 'mp', split_axis=0, concat_axis=1, tiled=True)  40.1 us
    unnamed x108, local copies, waits for them, and re-layouts  36.1 us
  transfers between devices with their start and end apart: 32, of which 10 were waited for; matrix products, arithmetic and copies ran while one was open for 25% of the time, Pallas kernels for 19%

profile of v4, /device:TPU:0, one launch (start us, length us, event | category | flops | bytes accessed | tf_op | source)
XLA Modules:
  0.0 938.2 jit_solution(7770109536022048901)
XLA Ops:
  12.3 5.6 gather_fusion.1
  17.9 5.5 gather_fusion.4
  26.5 4.2 copy.216
  37.0 5.3 all-to-all-start
  46.0 74.6 %all-to-all-done = bf16[32,64,1152]{2,1,0:T(8,128)(2,1)} async-done(((bf16[32,64,1152]{2,1,0:T(8,128)(2,1)}), bf16[32,64,1152]{2,1,0:T(8,128)(2,1)}, u32[]{:S(2)}, u32[]{:S(2)}) %all-to-all-start) | async-done | bytes 4718624 | tf_op jit(solution)/shard_map/all_to_all | solution.py:558
  120.6 4.6 gather_fusion.3
  125.2 6.5 all-to-all-start.1
  137.1 3.0 collective-permute-done.1
  140.7 22.4 %copy.203 = bf16[1152,6,1152]{0,2,1:T(8,128)(2,1)} copy(bf16[1152,6,1152]{2,0,1:T(8,128)(2,1)} %param.31) | data formatting | bytes 31850496 | tf_op args[8]
  163.7 40.1 %all-to-all-done.1 = bf16[16,64,1152]{2,1,0:T(8,128)(2,1)} async-done(((bf16[16,64,1152]{2,1,0:T(8,128)(2,1)}), bf16[16,64,1152]{2,1,0:T(8,128)(2,1)}, u32[]{:S(2)}, u32[]{:S(2)}) %all-to-all-start.1) | async-done | bytes 2359328 | tf_op jit(solution)/shard_map/all_to_all | solution.py:564
  203.8 4.9 copy.200
  208.7 4.9 all-to-all-start.2
  213.9 3.5 multiply_convert_fusion.2
  217.5 9.9 %fusion.18 = f32[4,6,1,1152]{3,0,1,2:T(4,128)S(1)} fusion(bf16[1152,6,1152]{0,2,1:T(8,128)(2,1)} %copy.203, bf16[128,1152]{0,1:T(8,128)(2,1)S(1)} %get-tuple-element.201), kind=kOutput, calls=%fused_computation.65 | convolution fusion | flops 63700992 | bytes 16330752 | tf_op jit(solution)/shard_map/dot_general | solution.py:414
  229.0 3.3 fusion.5
  233.9 84.0 %all-to-all-done.2 = bf16[16,64,1152]{2,1,0:T(8,128)(2,1)} async-done(((bf16[16,64,1152]{2,1,0:T(8,128)(2,1)}), bf16[16,64,1152]{2,1,0:T(8,128)(2,1)}, u32[]{:S(2)}, u32[]{:S(2)}) %all-to-all-start.2) | async-done | bytes 2359328 | tf_op jit(solution)/shard_map/all_to_all | solution.py:566
  317.9 5.0 copy.218
  323.0 62.7 %attend.1 = (f32[4,864,1024]{2,1,0:T(8,128)}, bf16[4,288,1024]{2,1,0:T(8,128)(2,1)}, f32[1024,1152]{1,0:T(8,128)}) custom-call(bf16[1024,1152]{1,0:T(8,128)(2,1)} %bitcast.191, bf16[4,1152,1152]{2,1,0:T(8,128)(2,1)} %bitcast.223, f32[2,72,1]{2,1,0:T(8,128)} %broadcast_multiply_fusion.gains_ref, f32[72,256]{1,0:T(8,128)} %pad_maximum_fusion.4.cos_ref, ...), custom_call_target="tpu_custom_call" | custom-call | flops 12079595520 | bytes 16515072 | tf_op jit(solution)/shard_map/attend/pallas_call | solution.py:184
  385.7 8.5 multiply_reduce_fusion.4
  394.4 3.8 add_convert_fusion.7
  399.9 4.3 copy.215
  404.3 33.8 %mlp.1 = (bf16[4,2,1024,768]{3,2,1,0:T(8,128)(2,1)}, f32[1024,1152]{1,0:T(8,128)}) custom-call(bf16[1024,1152]{1,0:T(8,128)(2,1)} %bitcast.199, bf16[4,8,3,96,1152]{4,3,2,1,0:T(8,128)(2,1)} %bitcast.220), custom_call_target="tpu_custom_call" | custom-call | flops 21743271936 | bytes 33816576 | tf_op jit(solution)/shard_map/mlp/pallas_call | solution.py:255
  438.1 9.2 multiply_reduce_fusion
  449.0 4.3 copy.220
  453.3 35.8 %mlp_back.3 = (bf16[2,3,576,768]{3,2,1,0:T(8,128)(2,1)}, bf16[2,3,576,768]{3,2,1,0:T(8,128)(2,1)}, f32[1024,1152]{1,0:T(8,128)}) custom-call(s32[2]{0:T(128)} %get-tuple-element.199.m_ref, s32[8]{0:T(128)} %get-tuple-element.203.e_ref, bf16[8,144,1024]{2,1,0:T(8,128)(2,1)} %bitcast.209, bf16[8,144,1024]{2,1,0:T(8,128)(2,1)} %bitcast.211, ...), custom_call_target="tpu_custom_call" | custom-call | flops 21743271936 | bytes 27525120 | tf_op jit(solution)/shard_map/mlp_back/pallas_call | solution.py:331
  489.1 4.7 all-to-all-start.3
  493.9 36.0 %mlp_back.2 = (bf16[2,3,576,768]{3,2,1,0:T(8,128)(2,1)}, bf16[2,3,576,768]{3,2,1,0:T(8,128)(2,1)}, f32[1024,1152]{1,0:T(8,128)}) custom-call(s32[2]{0:T(128)} %get-tuple-element.200.m_ref, s32[8]{0:T(128)} %get-tuple-element.204.e_ref, bf16[8,144,1024]{2,1,0:T(8,128)(2,1)} %bitcast.210, bf16[8,144,1024]{2,1,0:T(8,128)(2,1)} %bitcast.212, ...), custom_call_target="tpu_custom_call" | custom-call | flops 21743271936 | bytes 27525120 | tf_op jit(solution)/shard_map/mlp_back/pallas_call | solution.py:331
  532.4 4.7 copy.223
  537.1 11.5 %all-to-all-done.3 = bf16[4,256,1152]{2,0,1:T(4,128)(2,1)} async-done(((bf16[4,256,1152]{2,0,1:T(4,128)(2,1)}), bf16[4,256,1152]{2,0,1:T(4,128)(2,1)}, u32[]{:S(2)}, u32[]{:S(2)}) %all-to-all-start.3) | async-done | bytes 2359328 | tf_op jit(solution)/shard_map/all_to_all | solution.py:636
  548.7 3.6 copy.222
  552.3 4.3 bitcast_reduce_fusion.1
  556.6 3.9 multiply_reduce_fusion.1
  560.8 5.5 add_convert_fusion.1
  571.4 15.9 %multiply_reduce_fusion.2 = (bf16[4,1152]{1,0:T(4,128)(2,1)S(1)}, f32[4,256,1152]{2,0,1:T(4,128)S(1)}) fusion(f32[4,256,1152]{2,1,0:T(8,128)} %bitcast.190, f32[4]{0:T(128)S(1)} %bitcast.215, bf16[4,256,1152]{2,0,1:T(4,128)(2,1)} %bitcast.188, f32[4,256,1152]{2,0,1:T(4,128)S(1)} %bitcast.174, f32[4,256]{0,1:T(8,128)S(1)} %copy.226, f32[4,256]{0,1:T(8,128)S(1)} %copy.213, ...), kind=kLoop, calls=%fused_computation.38 | loop fusion | flops 11791872 | bytes 21269520 | tf_op jit(solution)/shard_map/reduce_sum | solution.py:672
  592.4 4.3 add_convert_fusion
  596.7 2.4 copy-done.13
  602.0 4.3 copy.228
  606.3 57.2 %attend_back.1 = (bf16[4,864,1024]{2,1,0:T(8,128)(2,1)}, f32[2,72,256]{2,1,0:T(8,128)}, f32[1024,1152]{1,0:T(8,128)}) custom-call(f32[4,864,1024]{2,1,0:T(8,128)} %get-tuple-element.73.proj_ref, bf16[1024,1152]{1,0:T(8,128)(2,1)} %bitcast.197, bf16[4,1152,1152]{2,1,0:T(8,128)(2,1)} %bitcast.224, f32[2,72,1]{2,1,0:T(8,128)} %broadcast_multiply_fusion.gains_ref, ...), custom_call_target="tpu_custom_call" | custom-call | flops 13891534848 | bytes 21233664 | tf_op jit(solution)/shard_map/attend_back/pallas_call | solution.py:211
  664.7 2.7 bitcast_reduce_fusion
  668.4 5.5 fusion.6
  674.6 10.0 %fusion.9 = bf16[4,256,1152]{2,0,1:T(4,128)(2,1)} fusion(f32[4,256,1152]{2,0,1:T(4,128)} %copy-done.10, bf16[4,256,1152]{2,0,1:T(4,128)(2,1)} %bitcast.177, f32[4,256,1152]{2,1,0:T(8,128)} %bitcast.180, f32[4,256]{0,1:T(8,128)S(1)} %copy.231, f32[4,1152]{1,0:T(4,128)S(1)} %get-tuple-element.191, f32[4,256]{0,1:T(8,128)S(1)} %copy.206), kind=kLoop, calls=%fused_computation.33 | loop fusion | flops 9437184 | bytes 14182400 | tf_op jit(solution)/shard_map/convert_element_type | solution.py:686
  686.7 2.6 add_convert_fusion.2
  693.8 13.1 %attend_grads.3 = (bf16[2,576,1152]{2,1,0:T(8,128)(2,1)}, bf16[2,576,1152]{2,1,0:T(8,128)(2,1)}) custom-call(s32[2]{0:T(128)} %get-tuple-element.199.m_ref, s32[8]{0:T(128)} %get-tuple-element.203.e_ref, bf16[8,144,1024]{2,1,0:T(8,128)(2,1)} %bitcast.205, bf16[8,144,1024]{2,1,0:T(8,128)(2,1)} %bitcast.207, bf16[4,864,1024]{2,1,0:T(8,128)(2,1)} %get-tuple-element.85.proj_ref, ...), custom_call_target="tpu_custom_call" | custom-call | flops 5435817984 | bytes 10027008 | tf_op jit(solution)/shard_map/attend_grads/pallas_call | solution.py:385
  708.6 13.1 %attend_grads.2 = (bf16[2,576,1152]{2,1,0:T(8,128)(2,1)}, bf16[2,576,1152]{2,1,0:T(8,128)(2,1)}) custom-call(s32[2]{0:T(128)} %get-tuple-element.200.m_ref, s32[8]{0:T(128)} %get-tuple-element.204.e_ref, bf16[8,144,1024]{2,1,0:T(8,128)(2,1)} %bitcast.206, bf16[8,144,1024]{2,1,0:T(8,128)(2,1)} %bitcast.208, bf16[4,864,1024]{2,1,0:T(8,128)(2,1)} %get-tuple-element.85.proj_ref, ...), custom_call_target="tpu_custom_call" | custom-call | flops 5435817984 | bytes 10027008 | tf_op jit(solution)/shard_map/attend_grads/pallas_call | solution.py:385
  722.6 7.9 collective-permute-done.12
  730.4 4.3 concatenate.52
  735.4 3.2 add_convert_fusion.3
  742.8 4.7 all-to-all-start.4
  747.5 3.1 add_convert_fusion.9
  752.6 8.2 concatenate.53
  762.2 4.9 reshape.860
  767.2 3.1 fusion.47
  771.1 2.6 add_convert_fusion.4
  775.5 2.4 add_convert_fusion.5
  782.9 19.3 %all-to-all-done.4 = bf16[4,256,1152]{2,0,1:T(4,128)(2,1)} async-done(((bf16[4,256,1152]{2,0,1:T(4,128)(2,1)}), bf16[4,256,1152]{2,0,1:T(4,128)(2,1)}, u32[]{:S(2)}, u32[]{:S(2)}) %all-to-all-start.4) | async-done | bytes 2359328 | tf_op jit(solution)/shard_map/all_to_all | solution.py:711
  805.8 4.9 gather_fusion.8
  810.7 4.9 all-to-all-start.5
  815.6 2.2 add_convert_fusion.11
  819.9 2.2 add_convert_fusion.8
  825.5 58.1 %collective-permute-done.17 = bf16[2,144,1152]{2,1,0:T(8,128)(2,1)S(1)} collective-permute-done((bf16[2,144,1152]{2,1,0:T(8,128)(2,1)S(1)}, bf16[2,144,1152]{2,1,0:T(8,128)(2,1)S(1)}, u32[]{:S(2)}, u32[]{:S(2)}) %collective-permute-start.17) | collective-permute-done | bytes 663584 | tf_op jit(solution)/shard_map/ppermute | solution.py:436
  886.8 13.5 %collective-permute-done.18 = bf16[2,144,1152]{2,1,0:T(8,128)(2,1)S(1)} collective-permute-done((bf16[2,144,1152]{2,1,0:T(8,128)(2,1)S(1)}, bf16[2,144,1152]{2,1,0:T(8,128)(2,1)S(1)}, u32[]{:S(2)}, u32[]{:S(2)}) %collective-permute-start.18) | collective-permute-done | bytes 663584 | tf_op jit(solution)/shard_map/ppermute | solution.py:436
  903.4 13.8 %collective-permute-done.19 = bf16[1,144,1152]{2,1,0:T(8,128)(2,1)S(1)} collective-permute-done((bf16[1,144,1152]{2,1,0:T(8,128)(2,1)S(1)}, bf16[1,144,1152]{2,1,0:T(8,128)(2,1)S(1)}, u32[]{:S(2)}, u32[]{:S(2)}) %collective-permute-start.19) | collective-permute-done | bytes 331808 | tf_op jit(solution)/shard_map/ppermute | solution.py:436
  920.2 5.7 gather_fusion.10
  925.9 5.0 broadcast_select_fusion
  (314 shorter events, 93.6 us)
Async XLA Ops:
  7.2 18.0 %copy-start = (bf16[1152,3,288]{0,2,1:T(8,128)(2,1)S(1)}, bf16[1152,3,288]{0,2,1:T(8,128)(2,1)}, u32[]{:S(2)}) copy-start(bf16[1152,3,288]{0,2,1:T(8,128)(2,1)} %param.32) | copy-start | bytes 5971972
  7.2 315.8 %all-gather.5.cloned.1.call-start = ((), (), s32[]{:S(2)}) async-start(), calls=%async_computation.6 | async-start | bytes 10948608 | tf_op jit(solution)/shard_map/all_gather | solution.py:422
  12.3 5.6 copy-start.2
  17.9 6.8 copy-start.21
  23.5 7.2 copy-start.5
  26.5 377.8 %all-gather.7.cloned.1.call-start = ((), (), s32[]{:S(2)}) async-start(), calls=%async_computation.7 | async-start | bytes 21897216 | tf_op jit(solution)/shard_map/all_gather | solution.py:422
  37.0 5.4 copy-start.37
  37.0 8.8 copy-start.41
  37.0 83.6 %all-to-all-start = ((bf16[32,64,1152]{2,1,0:T(8,128)(2,1)}), bf16[32,64,1152]{2,1,0:T(8,128)(2,1)}, u32[]{:S(2)}, u32[]{:S(2)}) async-start(bf16[32,64,1152]{2,1,0:T(8,128)(2,1)} %gather_fusion.1), calls=%async_computation | async-start | bytes 9437184 | tf_op jit(solution)/shard_map/all_to_all | solution.py:558
  42.4 94.1 %collective-permute-start = (s32[1,2,32]{2,1,0:T(2,128)S(1)}, s32[1,2,32]{2,1,0:T(2,128)S(1)}, u32[]{:S(2)}, u32[]{:S(2)}) collective-permute-start(s32[1,2,32]{2,1,0:T(2,128)S(1)} %add_bitcast_fusion.1), channel_id=1, source_target_pairs={{0,4},{4,0},{8,12},{12,8},{16,20},{20,16},{24,28},{28,24},{1,5},{5... | collective-permute-start | bytes 776 | tf_op jit(solution)/shard_map/ppermute | solution.py:436
  125.2 6.5 copy-start.40
  125.2 7.1 copy-start.32
  125.2 8.7 copy-start.39
  125.2 9.3 copy-start.35
  125.2 9.3 copy-start.36
  125.2 9.9 %copy-start.28 = (f32[2]{0:T(128)S(1)}, f32[2]{0:T(128)}, u32[]{:S(2)}) copy-start(f32[2]{0:T(128)} %constant.233) | copy-start | bytes 28
  125.2 15.4 %copy-start.33 = (s32[8]{0:T(128)S(1)}, s32[8]{0:T(128)}, u32[]{:S(2)}) copy-start(s32[8]{0:T(128)} %param.27) | copy-start | bytes 100
  125.2 78.6 %all-to-all-start.1 = ((bf16[16,64,1152]{2,1,0:T(8,128)(2,1)}), bf16[16,64,1152]{2,1,0:T(8,128)(2,1)}, u32[]{:S(2)}, u32[]{:S(2)}) async-start(bf16[16,64,1152]{2,1,0:T(8,128)(2,1)} %gather_fusion.3), calls=%async_computation.1 | async-start | bytes 4718592 | tf_op jit(solution)/shard_map/all_to_all | solution.py:564
  136.5 3.6 collective-permute-start.1
  140.0 23.1 %collective-permute-start.2 = (s32[4,2,32]{2,1,0:T(2,128)S(1)}, s32[4,2,32]{2,1,0:T(2,128)S(1)}, u32[]{:S(2)}, u32[]{:S(2)}) collective-permute-start(s32[4,2,32]{2,1,0:T(2,128)S(1)} %pad_add_fusion), channel_id=1, source_target_pairs={{0,16},{4,20},{8,24},{12,28},{16,0},{20,4},{24,8},{28,12},{1,17},{... | collective-permute-start | bytes 3080 | tf_op jit(solution)/shard_map/ppermute | solution.py:436
  163.6 50.0 %copy-start.26 = (s32[128]{0:T(128)}, s32[128]{0:T(128)S(1)}, u32[]{:S(2)}) copy-start(s32[128]{0:T(128)S(1)} %get-tuple-element.175) | copy-start | bytes 1540
  163.6 50.3 %copy-start.30 = (s32[128]{0:T(128)}, s32[128]{0:T(128)S(1)}, u32[]{:S(2)}) copy-start(s32[128]{0:T(128)S(1)} %get-tuple-element.174) | copy-start | bytes 1540
  208.7 109.3 %all-to-all-start.2 = ((bf16[16,64,1152]{2,1,0:T(8,128)(2,1)}), bf16[16,64,1152]{2,1,0:T(8,128)(2,1)}, u32[]{:S(2)}, u32[]{:S(2)}) async-start(bf16[16,64,1152]{2,1,0:T(8,128)(2,1)} %param.24), calls=%async_computation.2 | async-start | bytes 4718592 | tf_op jit(solution)/shard_map/all_to_all | solution.py:566
  217.4 9.9 %copy-start.22 = (bf16[128,1152]{0,1:T(8,128)(2,1)}, bf16[128,1152]{0,1:T(8,128)(2,1)S(1)}, u32[]{:S(2)}) copy-start(bf16[128,1152]{0,1:T(8,128)(2,1)S(1)} %get-tuple-element.201) | copy-start | bytes 884740
  217.4 10.0 %copy-start.7 = (bf16[4,4,64,1152]{3,1,2,0:T(4,128)(2,1)S(1)}, bf16[4,4,64,1152]{3,1,2,0:T(4,128)(2,1)}, u32[]{:S(2)}) copy-start(bf16[4,4,64,1152]{3,1,2,0:T(4,128)(2,1)} %copy.200) | copy-start | bytes 7077892
  323.0 62.7 %copy-start.8 = (bf16[4,4,64,1152]{3,1,2,0:T(4,128)(2,1)S(1)}, bf16[4,4,64,1152]{3,1,2,0:T(4,128)(2,1)}, u32[]{:S(2)}) copy-start(bf16[4,4,64,1152]{3,1,2,0:T(4,128)(2,1)} %copy.200) | copy-start | bytes 7077892
  489.1 63.2 %collective-permute-start.3 = (bf16[2,3,576,768]{3,2,1,0:T(8,128)(2,1)}, bf16[2,3,576,768]{3,2,1,0:T(8,128)(2,1)}, u32[]{:S(2)}, u32[]{:S(2)}) collective-permute-start(bf16[2,3,576,768]{3,2,1,0:T(8,128)(2,1)} %get-tuple-element.66), channel_id=1, source_target_pairs={{0,4},{4,0},{8,12},{12,8},{16,20},{20,16},{24,28},{28,24},{1,5},{5... | collective-permute-start | bytes 15925256 | tf_op jit(solution)/shard_map/ppermute | solution.py:436
  489.1 59.5 %all-to-all-start.3 = ((bf16[4,256,1152]{2,0,1:T(4,128)(2,1)}), bf16[4,256,1152]{2,0,1:T(4,128)(2,1)}, u32[]{:S(2)}, u32[]{:S(2)}) async-start(bf16[4,256,1152]{2,0,1:T(4,128)(2,1)} %get-tuple-element.183), calls=%async_computation.3 | async-start | bytes 4718592 | tf_op jit(solution)/shard_map/all_to_all | solution.py:636
  493.8 37.2 %copy-start.4 = (s32[8]{0:T(128)S(1)}, s32[8]{0:T(128)}, u32[]{:S(2)}) copy-start(s32[8]{0:T(128)} %param.28) | copy-start | bytes 100
  529.8 61.6 %collective-permute-start.4 = (bf16[2,3,576,768]{3,2,1,0:T(8,128)(2,1)}, bf16[2,3,576,768]{3,2,1,0:T(8,128)(2,1)}, u32[]{:S(2)}, u32[]{:S(2)}) collective-permute-start(bf16[2,3,576,768]{3,2,1,0:T(8,128)(2,1)} %get-tuple-element.71), channel_id=1, source_target_pairs={{0,4},{4,0},{8,12},{12,8},{16,20},{20,16},{24,28},{28,24},{1,5},{5... | collective-permute-start | bytes 15925256 | tf_op jit(solution)/shard_map/ppermute | solution.py:436
  548.7 8.0 slice-start
  556.6 12.9 %slice-start.2 = ((s8[4718592]{0:T(1024)(128)(4,1)}), s8[524288]{0:T(1024)(128)(4,1)S(1)}, s32[]{:S(2)}) async-start(s8[4718592]{0:T(1024)(128)(4,1)} %bitcast.173), calls=%async_computation.10 | async-start | bytes 1048576
  560.8 8.7 slice-start.3
  566.3 21.1 %copy-start.14 = (bf16[2,3,576,768]{3,2,1,0:T(8,128)(2,1)}, bf16[2,3,576,768]{3,2,1,0:T(8,128)(2,1)S(1)}, u32[]{:S(2)}) copy-start(bf16[2,3,576,768]{3,2,1,0:T(8,128)(2,1)S(1)} %add_convert_fusion.1) | copy-start | bytes 15925252
  568.0 96.7 %collective-permute-start.5 = (bf16[2,3,288,768]{3,2,1,0:T(8,128)(2,1)}, bf16[2,3,288,768]{3,2,1,0:T(8,128)(2,1)}, u32[]{:S(2)}, u32[]{:S(2)}) collective-permute-start(bf16[2,3,288,768]{3,2,1,0:T(8,128)(2,1)} %slice.227), channel_id=1, source_target_pairs={{0,16},{4,20},{8,24},{12,28},{16,0},{20,4},{24,8},{28,12},{1,17},{... | collective-permute-start | bytes 7962632 | tf_op jit(solution)/shard_map/ppermute | solution.py:436
  600.8 88.5 %collective-permute-start.6 = (bf16[2,3,288,768]{3,2,1,0:T(8,128)(2,1)}, bf16[2,3,288,768]{3,2,1,0:T(8,128)(2,1)}, u32[]{:S(2)}, u32[]{:S(2)}) collective-permute-start(bf16[2,3,288,768]{3,2,1,0:T(8,128)(2,1)} %slice.228), channel_id=1, source_target_pairs={{0,8},{4,12},{8,0},{12,4},{16,24},{20,28},{24,16},{28,20},{1,9},{5... | collective-permute-start | bytes 7962632 | tf_op jit(solution)/shard_map/ppermute | solution.py:436
  606.3 58.2 %copy-start.29 = (f32[2]{0:T(128)S(1)}, f32[2]{0:T(128)}, u32[]{:S(2)}) copy-start(f32[2]{0:T(128)} %constant.233) | copy-start | bytes 28
  668.4 5.6 copy-start.25
  674.4 12.3 %slice-start.4 = ((s8[5308416]{0:T(1024)(128)(4,1)}), s8[4194304]{0:T(1024)(128)(4,1)S(1)}, s32[]{:S(2)}) async-start(s8[5308416]{0:T(1024)(128)(4,1)} %bitcast.185), calls=%async_computation.12 | async-start | bytes 8388608
  674.5 12.3 %slice-start.5 = ((s8[5308416]{0:T(1024)(128)(4,1)}), s8[1114112]{0:T(1024)(128)(4,1)S(1)}, s32[]{:S(2)}) async-start(s8[5308416]{0:T(1024)(128)(4,1)} %bitcast.185), calls=%async_computation.13 | async-start | bytes 2228224
  674.5 10.1 %collective-permute-start.9 = (bf16[1,27792]{1,0:T(2,128)(2,1)S(1)}, bf16[1,27792]{1,0:T(2,128)(2,1)S(1)}, u32[]{:S(2)}, u32[]{:S(2)}) collective-permute-start(bf16[1,27792]{1,0:T(2,128)(2,1)S(1)} %broadcast_in_dim.187), channel_id=1, source_target_pairs={{0,2},{1,3},{2,0},{3,1},{4,6},{5,7},{6,4},{7,5},{8,10},{9,11},{10,... | collective-permute-start | bytes 166760 | tf_op jit(solution)/shard_map/ppermute | solution.py:436
  684.8 7.0 collective-permute-start.10
  690.9 56.6 %collective-permute-start.21 = (bf16[2,3,144,768]{3,2,1,0:T(8,128)(2,1)S(1)}, bf16[2,3,144,768]{3,2,1,0:T(8,128)(2,1)}, u32[]{:S(2)}, u32[]{:S(2)}) collective-permute-start(bf16[2,3,144,768]{3,2,1,0:T(8,128)(2,1)S(1)} %slice.248), channel_id=1, source_target_pairs={{0,8},{4,12},{8,0},{12,4},{16,24},{20,28},{24,16},{28,20},{1,9},{5... | collective-permute-start | bytes 3981320 | tf_op jit(solution)/shard_map/ppermute | solution.py:436
  692.2 14.6 %collective-permute-start.11 = (bf16[4,27792]{1,0:T(4,128)(2,1)S(1)}, bf16[4,27792]{1,0:T(4,128)(2,1)S(1)}, u32[]{:S(2)}, u32[]{:S(2)}) collective-permute-start(bf16[4,27792]{1,0:T(4,128)(2,1)S(1)} %pad_maximum_fusion.2), channel_id=1, source_target_pairs={{0,16},{4,20},{8,24},{12,28},{16,0},{20,4},{24,8},{28,12},{1,17},{... | collective-permute-start | bytes 667016 | tf_op jit(solution)/shard_map/ppermute | solution.py:436
  706.8 64.3 %collective-permute-start.7 = (bf16[2,576,1152]{2,1,0:T(8,128)(2,1)}, bf16[2,576,1152]{2,1,0:T(8,128)(2,1)}, u32[]{:S(2)}, u32[]{:S(2)}) collective-permute-start(bf16[2,576,1152]{2,1,0:T(8,128)(2,1)} %get-tuple-element.88), channel_id=1, source_target_pairs={{0,4},{4,0},{8,12},{12,8},{16,20},{20,16},{24,28},{28,24},{1,5},{5... | collective-permute-start | bytes 7962632 | tf_op jit(solution)/shard_map/ppermute | solution.py:436
  707.4 14.5 %copy-start.34 = (s32[8]{0:T(128)S(1)}, s32[8]{0:T(128)}, u32[]{:S(2)}) copy-start(s32[8]{0:T(128)} %param.27) | copy-start | bytes 100
  707.4 15.1 %copy-start.3 = (s32[72]{0:T(128)S(1)}, s32[72]{0:T(128)}, u32[]{:S(2)}) copy-start(s32[72]{0:T(128)} %constant.222.clone) | copy-start | bytes 868
  707.4 23.1 %collective-permute-start.12 = (bf16[8,27792]{1,0:T(8,128)(2,1)S(1)}, bf16[8,27792]{1,0:T(8,128)(2,1)S(1)}, u32[]{:S(2)}, u32[]{:S(2)}) collective-permute-start(bf16[8,27792]{1,0:T(8,128)(2,1)S(1)} %pad_maximum_fusion.1), channel_id=1, source_target_pairs={{0,8},{4,12},{8,0},{12,4},{16,24},{20,28},{24,16},{28,20},{1,9},{5... | collective-permute-start | bytes 1334024 | tf_op jit(solution)/shard_map/ppermute | solution.py:436
  721.7 53.9 %collective-permute-start.8 = (bf16[2,576,1152]{2,1,0:T(8,128)(2,1)}, bf16[2,576,1152]{2,1,0:T(8,128)(2,1)}, u32[]{:S(2)}, u32[]{:S(2)}) collective-permute-start(bf16[2,576,1152]{2,1,0:T(8,128)(2,1)} %get-tuple-element.90), channel_id=1, source_target_pairs={{0,4},{4,0},{8,12},{12,8},{16,20},{20,16},{24,28},{28,24},{1,5},{5... | collective-permute-start | bytes 7962632 | tf_op jit(solution)/shard_map/ppermute | solution.py:436
  734.8 17.9 %collective-permute-start.13 = (bf16[16,27792]{1,0:T(8,128)(2,1)}, bf16[16,27792]{1,0:T(8,128)(2,1)}, u32[]{:S(2)}, u32[]{:S(2)}) collective-permute-start(bf16[16,27792]{1,0:T(8,128)(2,1)} %concatenate.52), channel_id=1, source_target_pairs={{0,4},{4,0},{8,12},{12,8},{16,20},{20,16},{24,28},{28,24},{1,5},{5... | collective-permute-start | bytes 2668040 | tf_op jit(solution)/shard_map/ppermute | solution.py:436
  741.3 78.6 %collective-permute-start.20 = (bf16[2,3,144,768]{3,2,1,0:T(8,128)(2,1)}, bf16[2,3,144,768]{3,2,1,0:T(8,128)(2,1)}, u32[]{:S(2)}, u32[]{:S(2)}) collective-permute-start(bf16[2,3,144,768]{3,2,1,0:T(8,128)(2,1)} %slice.245), channel_id=1, source_target_pairs={{0,16},{4,20},{8,24},{12,28},{16,0},{20,4},{24,8},{28,12},{1,17},{... | collective-permute-start | bytes 3981320 | tf_op jit(solution)/shard_map/ppermute | solution.py:436
  742.8 59.4 %all-to-all-start.4 = ((bf16[4,256,1152]{2,0,1:T(4,128)(2,1)}), bf16[4,256,1152]{2,0,1:T(4,128)(2,1)}, u32[]{:S(2)}, u32[]{:S(2)}) async-start(bf16[4,256,1152]{2,0,1:T(4,128)(2,1)} %fusion.9), calls=%async_computation.4 | async-start | bytes 4718592 | tf_op jit(solution)/shard_map/all_to_all | solution.py:711
  750.6 69.3 %collective-permute-start.22 = (bf16[2,3,144,768]{3,2,1,0:T(8,128)(2,1)}, bf16[2,3,144,768]{3,2,1,0:T(8,128)(2,1)}, u32[]{:S(2)}, u32[]{:S(2)}) collective-permute-start(bf16[2,3,144,768]{3,2,1,0:T(8,128)(2,1)} %add_convert_fusion.9), channel_id=1, source_target_pairs={{0,1},{1,0},{2,3},{3,2},{4,5},{5,4},{6,7},{7,6},{8,9},{9,8},{10,11... | collective-permute-start | bytes 3981320 | tf_op jit(solution)/shard_map/ppermute | solution.py:436
  762.2 8.1 copy-start.27
  775.0 40.6 %collective-permute-start.16 = (bf16[2,288,1152]{2,1,0:T(8,128)(2,1)}, bf16[2,288,1152]{2,1,0:T(8,128)(2,1)}, u32[]{:S(2)}, u32[]{:S(2)}) collective-permute-start(bf16[2,288,1152]{2,1,0:T(8,128)(2,1)} %slice.235), channel_id=1, source_target_pairs={{0,16},{4,20},{8,24},{12,28},{16,0},{20,4},{24,8},{28,12},{1,17},{... | collective-permute-start | bytes 3981320 | tf_op jit(solution)/shard_map/ppermute | solution.py:436
  779.3 43.0 %collective-permute-start.14 = (bf16[2,288,1152]{2,1,0:T(8,128)(2,1)}, bf16[2,288,1152]{2,1,0:T(8,128)(2,1)}, u32[]{:S(2)}, u32[]{:S(2)}) collective-permute-start(bf16[2,288,1152]{2,1,0:T(8,128)(2,1)} %get-tuple-element.184), channel_id=1, source_target_pairs={{0,8},{4,12},{8,0},{12,4},{16,24},{20,28},{24,16},{28,20},{1,9},{5... | collective-permute-start | bytes 3981320 | tf_op jit(solution)/shard_map/ppermute | solution.py:436
  810.7 109.5 %all-to-all-start.5 = ((bf16[32,64,1152]{2,1,0:T(8,128)(2,1)}), bf16[32,64,1152]{2,1,0:T(8,128)(2,1)}, u32[]{:S(2)}, u32[]{:S(2)}) async-start(bf16[32,64,1152]{2,1,0:T(8,128)(2,1)} %gather_fusion.8), calls=%async_computation.5 | async-start | bytes 9437184 | tf_op jit(solution)/shard_map/all_to_all | solution.py:718
  817.9 65.7 %collective-permute-start.17 = (bf16[2,144,1152]{2,1,0:T(8,128)(2,1)S(1)}, bf16[2,144,1152]{2,1,0:T(8,128)(2,1)S(1)}, u32[]{:S(2)}, u32[]{:S(2)}) collective-permute-start(bf16[2,144,1152]{2,1,0:T(8,128)(2,1)S(1)} %slice.237), channel_id=1, source_target_pairs={{0,8},{4,12},{8,0},{12,4},{16,24},{20,28},{24,16},{28,20},{1,9},{5... | collective-permute-start | bytes 1990664 | tf_op jit(solution)/shard_map/ppermute | solution.py:436
  822.2 64.5 %collective-permute-start.23 = (bf16[1,3,144,768]{3,2,1,0:T(8,128)(2,1)S(1)}, bf16[1,3,144,768]{3,2,1,0:T(8,128)(2,1)S(1)}, u32[]{:S(2)}, u32[]{:S(2)}) collective-permute-start(bf16[1,3,144,768]{3,2,1,0:T(8,128)(2,1)S(1)} %slice.250), channel_id=1, source_target_pairs={{0,2},{1,3},{2,0},{3,1},{4,6},{5,7},{6,4},{7,5},{8,10},{9,11},{10,... | collective-permute-start | bytes 1990664 | tf_op jit(solution)/shard_map/ppermute | solution.py:436
  824.0 62.9 %collective-permute-start.15 = (bf16[2,144,1152]{2,1,0:T(8,128)(2,1)S(1)}, bf16[2,144,1152]{2,1,0:T(8,128)(2,1)S(1)}, u32[]{:S(2)}, u32[]{:S(2)}) collective-permute-start(bf16[2,144,1152]{2,1,0:T(8,128)(2,1)S(1)} %slice.233), channel_id=1, source_target_pairs={{0,16},{4,20},{8,24},{12,28},{16,0},{20,4},{24,8},{28,12},{1,17},{... | collective-permute-start | bytes 1990664 | tf_op jit(solution)/shard_map/ppermute | solution.py:436
  883.8 16.5 %collective-permute-start.18 = (bf16[2,144,1152]{2,1,0:T(8,128)(2,1)S(1)}, bf16[2,144,1152]{2,1,0:T(8,128)(2,1)S(1)}, u32[]{:S(2)}, u32[]{:S(2)}) collective-permute-start(bf16[2,144,1152]{2,1,0:T(8,128)(2,1)S(1)} %add_convert_fusion.15), channel_id=1, source_target_pairs={{0,1},{1,0},{2,3},{3,2},{4,5},{5,4},{6,7},{7,6},{8,9},{9,8},{10,11... | collective-permute-start | bytes 1990664 | tf_op jit(solution)/shard_map/ppermute | solution.py:436
  900.5 16.7 %copy-start.6 = (s32[864]{0:T(1024)S(1)}, s32[864]{0:T(1024)}, u32[]{:S(2)}) copy-start(s32[864]{0:T(1024)} %copy-done.5) | copy-start | bytes 10372
  900.6 16.5 %collective-permute-start.19 = (bf16[1,144,1152]{2,1,0:T(8,128)(2,1)S(1)}, bf16[1,144,1152]{2,1,0:T(8,128)(2,1)S(1)}, u32[]{:S(2)}, u32[]{:S(2)}) collective-permute-start(bf16[1,144,1152]{2,1,0:T(8,128)(2,1)S(1)} %slice.239), channel_id=1, source_target_pairs={{0,2},{1,3},{2,0},{3,1},{4,6},{5,7},{6,4},{7,5},{8,10},{9,11},{10,... | collective-permute-start | bytes 995336 | tf_op jit(solution)/shard_map/ppermute | solution.py:436
  920.2 10.7 %copy-start.1 = (bf16[1152,3,288]{0,2,1:T(8,128)(2,1)S(1)}, bf16[1152,3,288]{0,2,1:T(8,128)(2,1)}, u32[]{:S(2)}) copy-start(bf16[1152,3,288]{0,2,1:T(8,128)(2,1)} %param.32) | copy-start | bytes 5971972
  (18 other events, 70.7 us)
Sparse Core Ops, SparseCore 0:
  26.6 130.6 all-gather.4
  160.8 183.8 all-gather.6

commit v5 on v4

--- a/solution.py
+++ b/solution.py
@@ -2,6 +2,7 @@
 
 import jax
 import jax.numpy as jnp
+import numpy as np
 from jax import lax
 from jax.experimental import pallas as pl
 from jax.experimental.pallas import tpu as pltpu
@@ -15,13 +16,6 @@
 rope_base = 10000.0
 f32 = jnp.float32
 bf16 = jnp.bfloat16
-
-
-def rms_scale(values, scaling, shifting):
-    return (
-        values * lax.rsqrt(jnp.mean(values * values, -1, keepdims=True) + epsilon) * (1.0 + scaling)
-        + shifting
-    )
 
 
 def feature_order(head_dim):
@@ -74,14 +68,53 @@
     return shifted * (1.0 / jnp.sum(shifted, axis=0, keepdims=True))
 
 
+SHIFT_ONE, SCALE_ONE, GATE_ONE, SHIFT_TWO, SCALE_TWO, GATE_TWO, WEIGHT = range(7)
+
+
+def row_of(mods_ref, which):
+    return mods_ref[0, which : which + 1, :]
+
+
+def rms(values):
+    scale = lax.rsqrt(jnp.mean(values * values, -1, keepdims=True) + epsilon)
+    return values * scale, scale
+
+
+def rms_back(grad, unit, scale, scaling):
+    grad = grad * (1.0 + scaling)
+    return scale * (grad - unit * jnp.mean(grad * unit, -1, keepdims=True))
+
+
+def row_sum(values):
+    return jnp.sum(values, axis=0, keepdims=True)
+
+
+def put_rows(sums_ref, rows):
+    for which in range(sums_ref.shape[1]):
+        value = rows.get(which, jnp.zeros((1, sums_ref.shape[2]), f32))
+        sums_ref[0, which : which + 1, :] = value
+
+
 def attend_kernel(
-    x_ref, w_ref, gains_ref, cos_ref, sin_ref, proj_ref, att_ref, out_ref
+    latent_ref, mods_ref, w_ref, gains_ref, cos_ref, sin_ref,
+    proj_ref, att_ref, out_ref, x_ref, xt_ref, middle_ref, two_ref, twot_ref,
 ):
     head_dim = gains_ref.shape[1]
     rows_all, length = att_ref.shape[1:]
     cut = feature_order(head_dim)[1]
     cos_tab, sin_tab = cos_ref[...], sin_ref[...]
-    proj = dot_11(w_ref[0, : 3 * rows_all], x_ref[...])
+    group, image = pl.program_id(0), pl.program_id(1)
+    tokens = pl.ds(pl.multiple_of(image * length, length), length)
+
+    @pl.when(group == 0)
+    def _():
+        unit = rms(latent_ref[...].astype(f32))[0]
+        x = unit * (1.0 + row_of(mods_ref, SCALE_ONE)) + row_of(mods_ref, SHIFT_ONE)
+        x = x.astype(bf16)
+        x_ref[tokens, :] = x
+        xt_ref[:, tokens] = x.T
+
+    proj = dot_11(w_ref[0, : 3 * rows_all], x_ref[tokens, :])
     proj_ref[0] = proj
     outs = []
     for head in range(rows_all // head_dim):
@@ -99,7 +132,83 @@
     att = jnp.concatenate(outs, axis=0).astype(bf16)
     att_ref[0] = att
     part = dot_00(att, w_ref[0, 3 * rows_all :])
-    add_rows(out_ref, part, pl.program_id(0) == 0, pl.program_id(1), length)
+    add_rows(out_ref, part, group == 0, image, length)
+
+    @pl.when(group == pl.num_programs(0) - 1)
+    def _():
+        middle = latent_ref[...].astype(f32) + row_of(mods_ref, GATE_ONE) * out_ref[tokens, :]
+        middle_ref[tokens, :] = middle
+        two = rms(middle)[0] * (1.0 + row_of(mods_ref, SCALE_TWO)) + row_of(mods_ref, SHIFT_TWO)
+        two = two.astype(bf16)
+        two_ref[tokens, :] = two
+        twot_ref[:, tokens] = two.T
+
+
+def finish_kernel(
+    branch_ref, middle_ref, cot_ref, mods_ref, result_ref, low_ref, lowt_ref, sums_ref
+):
+    branch = branch_ref[...]
+    gate = row_of(mods_ref, GATE_TWO)
+    result_ref[...] = (middle_ref[...] + gate * branch).astype(bf16)
+    cot = cot_ref[...].astype(f32) * row_of(mods_ref, WEIGHT)
+    low = (gate * cot).astype(bf16)
+    low_ref[...] = low
+    lowt_ref[...] = low.T
+    put_rows(sums_ref, {GATE_TWO: row_sum(cot * branch)})
+
+
+def middle_kernel(
+    one_ref, other_ref, middle_ref, branch_ref, cot_ref, mods_ref,
+    grad_ref, low_ref, lowt_ref, sums_ref,
+):
+    grad = one_ref[...] + other_ref[...]
+    unit, scale = rms(middle_ref[...])
+    sums = {SHIFT_TWO: row_sum(grad), SCALE_TWO: row_sum(grad * unit)}
+    cot = cot_ref[...].astype(f32) * row_of(mods_ref, WEIGHT)
+    grad = cot + rms_back(grad, unit, scale, row_of(mods_ref, SCALE_TWO))
+    grad_ref[...] = grad
+    low = (row_of(mods_ref, GATE_ONE) * grad).astype(bf16)
+    low_ref[...] = low
+    lowt_ref[...] = low.T
+    sums[GATE_ONE] = row_sum(grad * branch_ref[...])
+    put_rows(sums_ref, sums)
+
+
+def entry_kernel(grad_ref, latent_ref, middle_ref, mods_ref, out_ref, sums_ref):
+    grad = grad_ref[...]
+    unit, scale = rms(latent_ref[...].astype(f32))
+    put_rows(sums_ref, {SHIFT_ONE: row_sum(grad), SCALE_ONE: row_sum(grad * unit)})
+    grad = middle_ref[...] + rms_back(grad, unit, scale, row_of(mods_ref, SCALE_ONE))
+    out_ref[...] = grad.astype(bf16)
+
+
+def by_image(kernel, name, arrays, mods, outs):
+    own, sums, width = mods.shape
+    tokens = arrays[0].shape[0]
+    length = tokens // own
+    block = pl.BlockSpec((length, width), lambda i: (i, 0))
+    turned = pl.BlockSpec((width, length), lambda i: (0, i))
+    whole = pl.BlockSpec((1, sums, width), lambda i: (i, 0, 0))
+    shapes = [
+        jax.ShapeDtypeStruct((width, tokens), bf16)
+        if out is True
+        else jax.ShapeDtypeStruct((tokens, width), out)
+        for out in outs
+    ]
+    return pl.pallas_call(
+        kernel,
+        grid=(own,),
+        in_specs=[block] * len(arrays) + [whole],
+        out_specs=[turned if out is True else block for out in outs] + [whole],
+        out_shape=shapes + [jax.ShapeDtypeStruct(mods.shape, f32)],
+        compiler_params=pltpu.CompilerParams(vmem_limit_bytes=48 << 20),
+        cost_estimate=pl.CostEstimate(
+            flops=10 * tokens * width,
+            bytes_accessed=4 * tokens * width * (len(arrays) + len(outs)),
+            transcendentals=0,
+        ),
+        name=name,
+    )(*arrays, mods)
 
 
 def add_rows(out_ref, part, first, index, length):
@@ -174,31 +283,39 @@
     return proj, att, x, w, gains, table, grads, total
 
 
-def attend(x, weights, gains, tables, own):
+def attend(latent, mods, weights, gains, tables, own):
     groups, rows, width = weights.shape[0], weights.shape[1] // 4, weights.shape[2]
-    tokens = x.shape[0]
+    tokens = latent.shape[0]
     length, head_dim = tokens // own, gains.shape[1]
     proj_s, att_s, x_s, w_s, gains_s, table_s, _, total_s = attend_specs(
         groups, rows, own, length, width, head_dim
     )
+    turned_s = pl.BlockSpec((width, tokens), lambda g, i: (0, 0))
+    mods_s = pl.BlockSpec((1,) + mods.shape[1:], lambda g, i: (i, 0, 0))
+    total, turned = (tokens, width), (width, tokens)
     return pl.pallas_call(
         attend_kernel,
         grid=(groups, own),
-        in_specs=[x_s, w_s, gains_s, table_s, table_s],
-        out_specs=[proj_s, att_s, total_s],
+        in_specs=[x_s, mods_s, w_s, gains_s, table_s, table_s],
+        out_specs=[proj_s, att_s, total_s, total_s, turned_s, total_s, total_s, turned_s],
         out_shape=[
             jax.ShapeDtypeStruct((groups, 3 * rows, tokens), f32),
             jax.ShapeDtypeStruct((groups, rows, tokens), bf16),
-            jax.ShapeDtypeStruct((tokens, width), f32),
+            jax.ShapeDtypeStruct(total, f32),
+            jax.ShapeDtypeStruct(total, bf16),
+            jax.ShapeDtypeStruct(turned, bf16),
+            jax.ShapeDtypeStruct(total, f32),
+            jax.ShapeDtypeStruct(total, bf16),
+            jax.ShapeDtypeStruct(turned, bf16),
         ],
-        compiler_params=pltpu.CompilerParams(vmem_limit_bytes=56 << 20),
+        compiler_params=pltpu.CompilerParams(vmem_limit_bytes=60 << 20),
         cost_estimate=pl.CostEstimate(
             flops=groups * rows * tokens * (4 * length + 8 * width),
             bytes_accessed=14 * groups * rows * tokens,
             transcendentals=groups * rows // head_dim * tokens * length,
         ),
         name="attend",
-    )(x, weights, gains, *tables)
+    )(latent, mods, weights, gains, *tables)
 
 
 def attend_back(proj, low, weights, gains, tables, own):
@@ -505,17 +622,16 @@
     unit_count = down_weight.shape[0]
     own = images // mp_size
     total_images = images * dp_size
-    order = jnp.array(feature_order(head_dim)[0])
+    order = np.array(feature_order(head_dim)[0])
+    columns = np.arange(4 * local_dim)
+    places = columns // head_dim * head_dim + order[columns % head_dim]
+    places = np.where(columns < 2 * local_dim, places, columns).astype(np.int32)
     tables = rope_tables(length, head_dim)
     gains_f = norm_gains.astype(f32)[:, order]
     gains_f = (gains_f * jnp.array([[head_dim ** (-0.5)], [1.0]], f32))[:, :, None]
     dp_index = lax.axis_index("dp")
     mp_index = lax.axis_index("mp")
 
-    columns = jnp.arange(3 * local_dim)
-    places = columns // head_dim * head_dim + order[columns % head_dim]
-    places = jnp.where(columns < 2 * local_dim, places, columns)
-    turn = (places[:, None] == columns[None, :]).astype(bf16)
     starts = jnp.cumsum(image_counts) - image_counts
     finish = starts + image_counts
     my_start = starts[dp_index]
@@ -530,13 +646,15 @@
     send_index = pair_slot * dp_size + jnp.mod(inverse[pair_peer] - my_start, dp_size)
     send_index = jnp.minimum(send_index, capacity - 1)
     send_patches = take_rows(patches, send_index)
-    qkv_weight, out_weight, expand_weight, down_weight, send_patches = tie(
-        qkv_weight, out_weight, expand_weight, down_weight, send_patches
+    info, info_places = xor_gather(
+        jnp.stack([time_bins, labels]), [("dp", bit) for bit in bits_of(dp_size)]
+    )
+    qkv_weight, out_weight, expand_weight, down_weight, send_patches, info = tie(
+        qkv_weight, out_weight, expand_weight, down_weight, send_patches, info
     )
     share = 4 * local_dim // dp_size
-    spots = dp_index * share + jnp.arange(share)
-    take_qkv = jnp.where(spots < 3 * local_dim, places[jnp.minimum(spots, 3 * local_dim - 1)], -1)
-    take_qkv = (take_qkv[:, None] == columns[None, :]).astype(bf16)
+    spots = lax.dynamic_slice_in_dim(jnp.array(places), dp_index * share, share, 0)
+    take_qkv = (spots[:, None] == jnp.arange(3 * local_dim)[None, :]).astype(bf16)
     take_out = (spots[:, None] - 3 * local_dim == jnp.arange(local_dim)[None, :]).astype(bf16)
     attend_piece = ein("rc,dc->rd", take_qkv, qkv_weight.reshape(model_width, -1))
     attend_piece = (attend_piece + dot(take_out, out_weight)).astype(bf16)
@@ -556,18 +674,6 @@
         mlp_full = mlp_full.swapaxes(1, 2).reshape(mp_size, 1, 3, unit_count, model_width)
 
     recv_patches = lax.all_to_all(send_patches, "dp", split_axis=0, concat_axis=0, tiled=True)
-    rank_ids = jnp.arange(images) * dp_size + my_place
-    source = jnp.sum((finish[None, :] <= rank_ids[:, None]).astype(jnp.int32), axis=1)
-    within = rank_ids - starts[source]
-    recv_index = source * slot_count + within // dp_size
-    latent = take_rows(recv_patches, recv_index)
-    latent = lax.all_to_all(latent, "mp", split_axis=0, concat_axis=1, tiled=True)
-    cotangent, latent = tie(cotangent, latent)
-    cot = lax.all_to_all(cotangent, "mp", split_axis=0, concat_axis=1, tiled=True)
-
-    info, info_places = xor_gather(
-        jnp.stack([time_bins, labels]), [("dp", bit) for bit in bits_of(dp_size)]
-    )
     info = info.swapaxes(0, 1).reshape(2, -1)
     info_owner = jnp.repeat(dp_index ^ jnp.array(info_places["dp"]), capacity)
     info_slot = jnp.tile(jnp.arange(capacity), dp_size)
@@ -580,14 +686,14 @@
     )
     gather_bits = [("mp", bit) for bit in bits_of(mp_size)[::-1]]
     gather_bits = gather_bits + [("dp", bit) for bit in bits_of(dp_size)[::-1]]
-    places = {"dp": [0], "mp": [0]}
+    spread = {"dp": [0], "mp": [0]}
     for axis, bit in gather_bits:
-        places = {
-            name: places[name] + [place ^ (bit if name == axis else 0) for place in places[name]]
-            for name in places
+        spread = {
+            name: spread[name] + [place ^ (bit if name == axis else 0) for place in spread[name]]
+            for name in spread
         }
-    owner_all = jnp.repeat(dp_index ^ jnp.array(places["dp"]), own)
-    group_all = jnp.repeat(mp_index ^ jnp.array(places["mp"]), own)
+    owner_all = jnp.repeat(dp_index ^ jnp.array(spread["dp"]), own)
+    group_all = jnp.repeat(mp_index ^ jnp.array(spread["mp"]), own)
     row_all = group_all * own + jnp.tile(jnp.arange(own), dp_size * mp_size)
     place_all = jnp.sum(
         jnp.where(owner_all[:, None] == device_ids[None, :], inverse[None, :], 0), axis=1
@@ -612,32 +718,37 @@
     weights = weights_all[:own]
 
     modulation = dot(silu_cond, ada_weight.reshape(model_width, 6 * model_width))
-    modulation = modulation.reshape(own, 6, 1, model_width)
-    shift_one = modulation[:, 0]
-    scale_one = modulation[:, 1]
-    gate_one = modulation[:, 2]
-    shift_two = modulation[:, 3]
-    scale_two = modulation[:, 4]
-    gate_two = modulation[:, 5]
-
-    latent_f = latent.astype(f32)
-    normed = rms_scale(latent_f, scale_one, shift_one).astype(bf16)
-    normed_flat = normed.reshape(-1, model_width)
-    proj, attended, branch_one = attend(normed_flat, attend_full, gains_f, tables, own)
-    branch_one = branch_one.reshape(own, length, model_width)
-    middle = latent_f + gate_one * branch_one
-    normed_two = rms_scale(middle, scale_two, shift_two).astype(bf16)
-    two_flat = normed_two.reshape(-1, model_width)
-    save, branch_two = mlp(two_flat, mlp_full)
-    branch_two, cot = tie(branch_two, cot)
-    out_cot = cot.astype(f32) * weights[:, None, None]
-    branch_two = branch_two.reshape(own, length, model_width)
-    result = (middle + gate_two * branch_two).astype(bf16)
+    mods = jnp.concatenate(
+        [
+            modulation.reshape(own, 6, model_width),
+            jnp.broadcast_to(weights[:, None, None], (own, 1, model_width)),
+            jnp.zeros((own, 1, model_width), f32),
+        ],
+        axis=1,
+    )
+    recv_patches, mods = tie(recv_patches, mods)
+
+    rank_ids = jnp.arange(images) * dp_size + my_place
+    source = jnp.sum((finish[None, :] <= rank_ids[:, None]).astype(jnp.int32), axis=1)
+    within = rank_ids - starts[source]
+    recv_index = source * slot_count + within // dp_size
+    latent = take_rows(recv_patches, recv_index)
+    latent = lax.all_to_all(latent, "mp", split_axis=0, concat_axis=1, tiled=True)
+    latent = latent.reshape(-1, model_width)
+
+    proj, attended, branch_one, normed, normed_t, middle, two, two_t = attend(
+        latent, mods, attend_full, gains_f, tables, own
+    )
+    cotangent, attended = tie(cotangent, attended)
+    cot = lax.all_to_all(cotangent, "mp", split_axis=0, concat_axis=1, tiled=True)
+    cot = cot.reshape(-1, model_width)
+    save, branch_two = mlp(two, mlp_full)
+    result, down_low, down_t, sums_finish = by_image(
+        finish_kernel, "finish", (branch_two, middle, cot), mods, (bf16, bf16, True)
+    )
+    result = result.reshape(own, length, model_width)
     result = lax.all_to_all(result, "mp", split_axis=1, concat_axis=0, tiled=True)
 
-    down_low = (gate_two * out_cot).astype(bf16)
-    gate_two_grad = jnp.sum(out_cot * branch_two, axis=1)
-    down_low = down_low.reshape(-1, model_width)
     dp_bits = bits_of(dp_size)
     dp_bits = (dp_bits, dp_bits[:1] + dp_bits[1:][::-1])
     mp_bits = bits_of(mp_size)
@@ -646,13 +757,9 @@
     m_orders = (m_order[: mp_size // 2], m_order[mp_size // 2 :])
 
     def by_owner(values):
-        return values.T.reshape(dp_size, model_width // dp_size, -1)
-
-    def reduce_mp(kept, sent):
-        kept = add_low(kept, swap(sent, "mp", mp_bits[0]))
-        return halve(kept, "mp", mp_bits[1:], 0)[0].astype(f32)
-
-    two_t, down_t = by_owner(two_flat), by_owner(down_low)
+        return values.reshape(dp_size, model_width // dp_size, -1)
+
+    two_t, down_t = by_owner(two_t), by_owner(down_t)
     kept_one, sent_one, two_one = mlp_back(
         m_orders[1], e_orders[1], two_t, down_t, down_low, save, mlp_full
     )
@@ -664,13 +771,13 @@
     two_zero, got_one, result = tie(two_zero, got_one, result)
     kept_one, sent_one = split(add_low(kept_one, got_one), 2)
     got_one = swap(sent_one, "dp", dp_bits[1][1])
-    two_parts = (two_zero, two_one)
-    two_grad = (two_parts[0] + two_parts[1]).reshape(own, length, model_width)
-    norm_val, norm_pull = jax.vjp(rms_scale, middle, scale_two, shift_two)
-    middle_grad, scale_two_grad, shift_two_grad = norm_pull(two_grad)
-    middle_grad = middle_grad + out_cot
-    gate_one_grad = jnp.sum(middle_grad * branch_one, axis=1)
-    branch_low = (gate_one * middle_grad).astype(bf16).reshape(-1, model_width)
+    middle_grad, branch_low, branch_t, sums_middle = by_image(
+        middle_kernel,
+        "middle",
+        (two_zero, two_one, middle, branch_one, cot),
+        mods,
+        (f32, bf16, True),
+    )
     branch_low, got_zero = tie(branch_low, got_zero)
     kept_zero, sent_zero = split(add_low(kept_zero, got_zero), 2)
     got_zero = swap(sent_zero, "dp", dp_bits[0][1])
@@ -678,14 +785,19 @@
         proj, branch_low, attend_full, gains_f, tables, own
     )
     gains_grad = jnp.sum(gains_grad, axis=2) * jnp.array([[head_dim ** (-0.5)], [1.0]], f32)
-    projected_low, normed_grad, got_one = tie(projected_low, normed_grad, got_one)
-    mlp_one = halve(add_low(kept_one, got_one), "dp", dp_bits[1][2:], 2)
-    normed_grad = normed_grad.reshape(own, length, model_width)
-    norm_val, norm_pull = jax.vjp(rms_scale, latent_f, scale_one, shift_one)
-    latent_grad, scale_one_grad, shift_one_grad = norm_pull(normed_grad)
-    latent_grad = (latent_grad + middle_grad).astype(bf16)
-
-    normed_t, branch_t, latent_grad = tie(by_owner(normed_flat), by_owner(branch_low), latent_grad)
+    projected_low, normed_grad, got_one, got_zero = tie(projected_low, normed_grad, got_one, got_zero)
+    kept_one, sent_one = split(add_low(kept_one, got_one), 2)
+    kept_zero, sent_zero = split(add_low(kept_zero, got_zero), 2)
+    got_one = swap(sent_one, "dp", dp_bits[1][2])
+    got_zero = swap(sent_zero, "dp", dp_bits[0][2])
+    latent_grad, sums_entry = by_image(
+        entry_kernel, "entry", (normed_grad, latent, middle_grad), mods, (bf16,)
+    )
+    latent_back = latent_grad.reshape(own, length, model_width)
+    latent_back = lax.all_to_all(latent_back, "mp", split_axis=1, concat_axis=0, tiled=True)
+
+    normed_t, latent_grad = tie(normed_t, latent_grad)
+    normed_t, branch_t = by_owner(normed_t), by_owner(branch_t)
 
     def grads_of(which):
         kept, sent = attend_grads(
@@ -698,43 +810,43 @@
         )
         return kept, swap(sent, "dp", dp_bits[which][0])
 
-    kept_one, got_one = grads_of(1)
-    normed_t, got_zero = tie(normed_t, got_zero)
-    mlp_zero = halve(add_low(kept_zero, got_zero), "dp", dp_bits[0][2:], 2)
-    kept_zero, got_zero = grads_of(0)
-    kept_zero, got_one = tie(kept_zero, got_one)
-    attend_one = halve(add_low(kept_one, got_one), "dp", dp_bits[1][1:], 1)
-    kept_zero, sent_zero = split(add_low(kept_zero, got_zero), 1)
-    got_zero = swap(sent_zero, "dp", dp_bits[0][1])
-    mlp_grad = reduce_mp(mlp_zero, mlp_one)
-
-    latent_back = lax.all_to_all(latent_grad, "mp", split_axis=1, concat_axis=0, tiled=True)
-    latent_back, kept_zero = tie(latent_back, kept_zero)
-    attend_zero = halve(add_low(kept_zero, got_zero), "dp", dp_bits[0][2:], 1)
-    attend_grad = reduce_mp(attend_zero, attend_one)
+    attend_one, attend_got_one = grads_of(1)
+    attend_zero, attend_got_zero = grads_of(0)
+    attend_zero, attend_got_one, got_one, got_zero = tie(
+        attend_zero, attend_got_one, got_one, got_zero
+    )
+    mlp_one = halve(add_low(kept_one, got_one), "dp", dp_bits[1][3:], 2)
+    mlp_zero = halve(add_low(kept_zero, got_zero), "dp", dp_bits[0][3:], 2)
+    mlp_got = swap(mlp_one, "mp", mp_bits[0])
+    attend_one, sent_one = split(add_low(attend_one, attend_got_one), 1)
+    attend_zero, sent_zero = split(add_low(attend_zero, attend_got_zero), 1)
+    attend_got_one = swap(sent_one, "dp", dp_bits[1][1])
+    attend_got_zero = swap(sent_zero, "dp", dp_bits[0][1])
+
+    modulation_grad = (sums_finish + sums_middle + sums_entry)[:, :6].astype(bf16)
+    packed = jnp.concatenate([modulation_grad.reshape(-1), gains_grad.astype(bf16).reshape(-1)])
+    packed = xor_gather(packed, gather_bits)[0]
+    latent_back, packed, attend_got_one, attend_got_zero, mlp_got = tie(
+        latent_back, packed, attend_got_one, attend_got_zero, mlp_got
+    )
+    attend_one = halve(add_low(attend_one, attend_got_one), "dp", dp_bits[1][2:], 1)
+    attend_zero = halve(add_low(attend_zero, attend_got_zero), "dp", dp_bits[0][2:], 1)
+    mlp_grad = halve(add_low(mlp_zero, mlp_got), "mp", mp_bits[1:], 0)[0].astype(f32)
+    attend_grad = add_low(attend_zero, swap(attend_one, "mp", mp_bits[0]))
+    attend_grad = halve(attend_grad, "mp", mp_bits[1:], 0)[0].astype(f32)
+
     back_within = pair_slot * dp_size + jnp.mod(my_place - starts[pair_peer], dp_size)
+    back_valid = back_within < image_counts[pair_peer]
     back_slot = jnp.clip((starts[pair_peer] + back_within - my_place) // dp_size, 0, images - 1)
+    back_slot = jnp.where(back_valid, back_slot, images)
+    latent_back = jnp.pad(latent_back, ((0, 1), (0, 0), (0, 0)))
     back_patches = take_rows(latent_back, back_slot)
     got_patches = lax.all_to_all(back_patches, "dp", split_axis=0, concat_axis=0, tiled=True)
     slot_ids = jnp.arange(capacity)
-    slot_live = slot_ids < my_count
     home_peer = dest_perm[jnp.mod(my_start + slot_ids, dp_size)]
     home_index = home_peer * slot_count + jnp.minimum(slot_ids // dp_size, slot_count - 1)
-    patch_grad = jnp.where(slot_live[:, None, None], take_rows(got_patches, home_index), 0)
-
-    modulation_grad = jnp.stack(
-        [
-            shift_one_grad[:, 0],
-            scale_one_grad[:, 0],
-            gate_one_grad,
-            shift_two_grad[:, 0],
-            scale_two_grad[:, 0],
-            gate_two_grad,
-        ],
-        1,
-    ).astype(bf16)
-    packed = jnp.concatenate([modulation_grad.reshape(-1), gains_grad.astype(bf16).reshape(-1)])
-    packed = xor_gather(packed, gather_bits)[0]
+    patch_grad = take_rows(got_patches, home_index)
+
     mod_all = packed[:, : own * 6 * model_width].reshape(total_images, 6, model_width)
     gains_total = packed[:, own * 6 * model_width :].reshape(-1, 2, head_dim)
     gains_total = jnp.sum(gains_total.astype(f32), axis=0)
@@ -760,7 +872,7 @@
     out_grad = attend_grad[:, 3 * local_dim :].T
     qkv_grad = lax.dot_general(
         attend_grad[:, : 3 * local_dim],
-        turn.astype(f32),
+        jnp.array(places[: 3 * local_dim, None] == columns[: 3 * local_dim], f32),
         (((1,), (0,)), ((), ())),
         precision=lax.Precision.HIGHEST,
         preferred_element_type=f32,

time: 947 us -> 864 us (0.912)
  waiting for transfers between devices: 326 us -> 252 us
  other arithmetic: 120 us -> 53.1 us
  blocking collectives: 0 us -> 57 us
  Pallas kernels: 252 us -> 284 us
  local copies, waits for them, and re-layouts: 148 us -> 121 us
    all_to_all x0 -> x1, blocking collectives: none -> 57 us  [shards(): lax.all_to_all(result, 'mp', split_axis=1, concat_axis=0, tiled=True)]
    reduce_sum x8 -> x0, other arithmetic: 51.3 us -> none  [the longest x4 16.4 us: rms_scale(): values * lax.rsqrt(jnp.mean(values * values, -1, keepdims=True) + epsilon)]
    ppermute x24, waiting for transfers between devices: 96.2 us -> 55.7 us  [swap(): return lax.ppermute(values, axis, [(i, i ^ bit) for i in range(size)])]
    all_to_all x2 -> x1, waiting for transfers between devices: 30.8 us -> 0.01 us  [shards(): lax.all_to_all(latent_back, 'mp', split_axis=1, concat_axis=0, tiled=True)]
    pallas_call x1 -> x4, Pallas kernels: 62.7 us -> 92.7 us  [the longest x1 70.3 us: attend(): pl.pallas_call(attend_kernel, grid=(groups, own), in_specs=[x_s, mods_s,...]
    all_to_all x1, waiting for transfers between devices: 40.1 us -> 61.8 us  [shards(): lax.all_to_all(latent, 'mp', split_axis=0, concat_axis=1, tiled=True)]
    transpose x4 -> x0, local copies, waits for them, and re-layouts: 17.6 us -> none  [by_owner(): return values.T.reshape(dp_size, model_width // dp_size, -1)]
    all_to_all x1, waiting for transfers between devices: 74.6 us -> 57.7 us  [shards(): lax.all_to_all(send_patches, 'dp', split_axis=0, concat_axis=0, tiled=True)]
  transfers between devices with their start and end apart: 32 -> 31, of which waited for: 10 -> 9; matrix products, arithmetic and copies ran while one was open for 25% -> 19% of each run, Pallas kernels for 19% -> 24%
where the time goes in v5:
time: 864 us; the launch traced here: 854 us
  Pallas kernels  284 us (33%)
  waiting for transfers between devices  252 us (29%)
  local copies, waits for them, and re-layouts  121 us (14%)
  blocking collectives  57 us (7%)
  other arithmetic  53.1 us (6%)
  starting transfers between devices  46.9 us (5%)
  matrix products  25.5 us (3%)
  between operations  15.2 us (2%)
    pallas_call x2, Pallas kernels, mlp_back(): pl.pallas_call(mlp_back_kernel, grid_spec=pltpu.PrefetchScalarGridSpec(nu...  72.4 us
    all_to_all x1, waiting for transfers between devices, shards(): lax.all_to_all(cotangent, 'mp', split_axis=0, concat_axis=1, tiled=True)  71.3 us
    pallas_call x1, Pallas kernels, attend(): pl.pallas_call(attend_kernel, grid=(groups, own), in_specs=[x_s, mods_s,...  70.3 us
    all_to_all x1, waiting for transfers between devices, shards(): lax.all_to_all(latent, 'mp', split_axis=0, concat_axis=1, tiled=True)  61.8 us
    pallas_call x1, Pallas kernels, attend_back(): pl.pallas_call(attend_back_kernel, grid=(groups, own), in_specs=[proj_s,...  57.8 us
    all_to_all x1, waiting for transfers between devices, shards(): lax.all_to_all(send_patches, 'dp', split_axis=0, concat_axis=0, tiled=True)  57.7 us
    all_to_all x1, blocking collectives, shards(): lax.all_to_all(result, 'mp', split_axis=1, concat_axis=0, tiled=True)  57 us
    ppermute x24, waiting for transfers between devices, swap(): return lax.ppermute(values, axis, [(i, i ^ bit) for i in range(size)])  55.7 us
  transfers between devices with their start and end apart: 31, of which 9 were waited for; matrix products, arithmetic and copies ran while one was open for 19% of the time, Pallas kernels for 24%

profile of v5, /device:TPU:0, one launch (start us, length us, event | category | flops | bytes accessed | tf_op | source)
XLA Modules:
  0.0 854.2 jit_solution(10586769087459148930)
XLA Ops:
  12.7 2.6 collective-permute-start.1
  16.9 2.0 collective-permute-start.2
  19.7 5.6 gather_fusion.1
  27.2 2.5 copy.135
  34.3 22.4 %copy.128 = bf16[1152,6,1152]{0,2,1:T(8,128)(2,1)} copy(bf16[1152,6,1152]{2,0,1:T(8,128)(2,1)} %param.35) | data formatting | bytes 31850496 | tf_op args[8]
  57.5 4.8 all-to-all-start
  64.8 3.6 multiply_convert_fusion
  68.4 9.9 %fusion = f32[4,6,1152]{2,0,1:T(4,128)S(1)} fusion(bf16[1152,6,1152]{0,2,1:T(8,128)(2,1)} %copy.128, bf16[128,1152]{0,1:T(8,128)(2,1)S(1)} %get-tuple-element.206), kind=kOutput, calls=%fused_computation.10 | convolution fusion | flops 63700992 | bytes 16330752 | tf_op jit(solution)/shard_map/dot_general | solution.py:531
  79.4 57.7 %all-to-all-done = bf16[32,64,1152]{2,1,0:T(8,128)(2,1)} async-done(((bf16[32,64,1152]{2,1,0:T(8,128)(2,1)}), bf16[32,64,1152]{2,1,0:T(8,128)(2,1)}, u32[]{:S(2)}, u32[]{:S(2)}) %all-to-all-start) | async-done | bytes 4718624 | tf_op jit(solution)/shard_map/all_to_all | solution.py:676
  137.0 4.5 gather_fusion.3
  141.6 4.9 all-to-all-start.1
  150.2 61.8 %all-to-all-done.1 = bf16[16,64,1152]{2,1,0:T(8,128)(2,1)S(1)} async-done(((bf16[16,64,1152]{2,1,0:T(8,128)(2,1)}), bf16[16,64,1152]{2,1,0:T(8,128)(2,1)S(1)}, u32[]{:S(2)}, u32[]{:S(2)}) %all-to-all-start.1) | async-done | bytes 2359328 | tf_op jit(solution)/shard_map/all_to_all | solution.py:736
  213.6 70.3 %attend.1 = (f32[4,864,1024]{2,1,0:T(8,128)}, bf16[4,288,1024]{2,1,0:T(8,128)(2,1)}, f32[1024,1152]{1,0:T(8,128)}, bf16[1024,1152]{1,0:T(8,128)(2,1)}, bf16[1152...) custom-call(bf16[1024,1152]{1,0:T(8,128)(2,1)} %bitcast.133, ...), custom_call_target="tpu_custom_call" | custom-call | flops 12079595520 | bytes 16515072 | tf_op jit(solution)/shard_map/attend/pallas_call | solution.py:296
  284.0 3.8 all-to-all-start.2
  288.9 71.3 %all-to-all-done.2 = bf16[16,64,1152]{2,1,0:T(8,128)(2,1)S(1)} async-done(((bf16[16,64,1152]{2,1,0:T(8,128)(2,1)}), bf16[16,64,1152]{2,1,0:T(8,128)(2,1)S(1)}, u32[]{:S(2)}, u32[]{:S(2)}) %all-to-all-start.2) | async-done | bytes 2359328 | tf_op jit(solution)/shard_map/all_to_all | solution.py:743
  360.2 1.6 copy.137
  361.9 33.9 %mlp.1 = (bf16[4,2,1024,768]{3,2,1,0:T(8,128)(2,1)}, f32[1024,1152]{1,0:T(8,128)}) custom-call(bf16[1024,1152]{1,0:T(8,128)(2,1)} %get-tuple-element.78.x_ref, bf16[4,8,3,96,1152]{4,3,2,1,0:T(8,128)(2,1)} %bitcast.157), custom_call_target="tpu_custom_call" | custom-call | flops 21743271936 | bytes 33816576 | tf_op jit(solution)/shard_map/mlp/pallas_call | solution.py:372
  395.8 6.6 finish.1
  405.2 36.2 %mlp_back.3 = (bf16[2,3,576,768]{3,2,1,0:T(8,128)(2,1)}, bf16[2,3,576,768]{3,2,1,0:T(8,128)(2,1)}, f32[1024,1152]{1,0:T(8,128)}) custom-call(s32[2]{0:T(128)} %get-tuple-element.204.m_ref, s32[8]{0:T(128)} %get-tuple-element.208.e_ref, bf16[8,144,1024]{2,1,0:T(8,128)(2,1)} %bitcast.166, bf16[8,144,1024]{2,1,0:T(8,128)(2,1)} %bitcast.162, ...), custom_call_target="tpu_custom_call" | custom-call | flops 21743271936 | bytes 27525120 | tf_op jit(solution)/shard_map/mlp_back/pallas_call | solution.py:448
  441.4 36.2 %mlp_back.2 = (bf16[2,3,576,768]{3,2,1,0:T(8,128)(2,1)}, bf16[2,3,576,768]{3,2,1,0:T(8,128)(2,1)}, f32[1024,1152]{1,0:T(8,128)}) custom-call(s32[2]{0:T(128)} %get-tuple-element.205.m_ref, s32[8]{0:T(128)} %get-tuple-element.209.e_ref, bf16[8,144,1024]{2,1,0:T(8,128)(2,1)} %bitcast.167, bf16[8,144,1024]{2,1,0:T(8,128)(2,1)} %bitcast.163, ...), custom_call_target="tpu_custom_call" | custom-call | flops 21743271936 | bytes 27525120 | tf_op jit(solution)/shard_map/mlp_back/pallas_call | solution.py:448
  478.1 3.5 copy.138
  481.6 57.0 %all_to_all.76 = bf16[4,256,1152]{2,0,1:T(4,128)(2,1)S(1)} all-to-all(bf16[4,256,1152]{2,0,1:T(4,128)(2,1)S(1)} %copy.138), channel_id=1, replica_groups=mesh['dp'=8,'mp'=4] {'mp'}, dimensions={1} | all-to-all | bytes 4718592 | tf_op jit(solution)/shard_map/all_to_all | solution.py:750
  538.6 1.8 copy.139
  540.4 10.4 %middle.1 = (f32[1024,1152]{1,0:T(8,128)}, bf16[1024,1152]{1,0:T(8,128)(2,1)S(1)}, bf16[1152,1024]{1,0:T(8,128)(2,1)S(1)}, f32[4,8,1152]{2,1,0:T(8,128)S(1)}) custom-call(f32[1024,1152]{1,0:T(8,128)} %get-tuple-element.93.one_ref, f32[1024,1152]{1,0:T(8,128)} %get-tuple-element.94.other_ref, f32[1024,1152]{1,0:T(8,128)} %get-tuple-element.82.middle_ref, ...), custom_call_target="tpu_custom_call" | custom-call | flops 11796480 | bytes 37748736 | tf_op jit(solution)/shard_map/middle/pallas_call | solution.py:198
  552.2 2.3 copy-done.23
  554.5 5.6 add_convert_fusion
  560.1 1.9 slice.201
  562.0 2.1 collective-permute-start.6
  564.1 3.8 add_convert_fusion.1
  567.8 1.8 slice.200
  571.9 57.8 %attend_back.1 = (bf16[4,864,1024]{2,1,0:T(8,128)(2,1)}, f32[2,72,256]{2,1,0:T(8,128)}, f32[1024,1152]{1,0:T(8,128)}) custom-call(f32[4,864,1024]{2,1,0:T(8,128)} %get-tuple-element.92.proj_ref, bf16[1024,1152]{1,0:T(8,128)(2,1)} %copy-done.8, bf16[4,1152,1152]{2,1,0:T(8,128)(2,1)} %bitcast.161, f32[2,72,1]{2,1,0:T(8,128)} %broadcast_multiply_fusion.gains_ref, ...), custom_call_target="tpu_custom_call" | custom-call | flops 13891534848 | bytes 21233664 | tf_op jit(solution)/shard_map/attend_back/pallas_call | solution.py:328
  630.9 5.4 entry.1
  638.2 13.6 %attend_grads.2 = (bf16[2,576,1152]{2,1,0:T(8,128)(2,1)}, bf16[2,576,1152]{2,1,0:T(8,128)(2,1)}) custom-call(s32[2]{0:T(128)} %get-tuple-element.204.m_ref, s32[8]{0:T(128)} %get-tuple-element.208.e_ref, bf16[8,144,1024]{2,1,0:T(8,128)(2,1)} %bitcast.164, bf16[8,144,1024]{2,1,0:T(8,128)(2,1)} %bitcast.137, ...), custom_call_target="tpu_custom_call" | custom-call | flops 5435817984 | bytes 10027008 | tf_op jit(solution)/shard_map/attend_grads/pallas_call | solution.py:502
  651.8 13.6 %attend_grads.3 = (bf16[2,576,1152]{2,1,0:T(8,128)(2,1)}, bf16[2,576,1152]{2,1,0:T(8,128)(2,1)}) custom-call(s32[2]{0:T(128)} %get-tuple-element.205.m_ref, s32[8]{0:T(128)} %get-tuple-element.209.e_ref, bf16[8,144,1024]{2,1,0:T(8,128)(2,1)} %bitcast.165, bf16[8,144,1024]{2,1,0:T(8,128)(2,1)} %bitcast.138, ...), custom_call_target="tpu_custom_call" | custom-call | flops 5435817984 | bytes 10027008 | tf_op jit(solution)/shard_map/attend_grads/pallas_call | solution.py:502
  665.7 1.9 collective-permute-start.8
  667.6 3.2 add_convert_fusion.4
  675.1 2.4 add_convert_fusion.5
  682.0 3.2 copy.140
  685.3 4.7 all-to-all-start.4
  690.0 16.6 %collective-permute-done.9 = bf16[4,27792]{1,0:T(4,128)(2,1)} collective-permute-done((bf16[4,27792]{1,0:T(4,128)(2,1)}, bf16[4,27792]{1,0:T(4,128)(2,1)}, u32[]{:S(2)}, u32[]{:S(2)}) %collective-permute-start.9) | collective-permute-done | bytes 222368 | tf_op jit(solution)/shard_map/ppermute | solution.py:553
  706.6 2.2 pad_maximum_fusion.1
  710.2 3.2 add_convert_fusion.10
  713.7 2.4 add_convert_fusion.2
  719.4 2.4 add_convert_fusion.3
  726.6 5.3 concatenate.56
  734.7 10.4 %concatenate.57 = bf16[32,27792]{1,0:T(8,128)(2,1)} concatenate(bf16[1,27792]{1,0:T(2,128)(2,1)S(1)} %broadcast_in_dim.165, bf16[1,27792]{1,0:T(2,128)(2,1)S(1)} %collective-permute-done.7, bf16[2,27792]{1,0:T(2,128)(2,1)S(1)} %collective-permute-done.8, bf16[4,27792]{1,0:T(4,128)(2,1)} %collective-permute-done.9, bf16[8,27792]{1,0:T(8,128)(2,1)S(1)} %collective-permute-done.10, ...), dimensions={0} | concatenate | bytes 3557376 | tf_op jit(solution)/shard_map/concatenate | solution.py:561
  745.1 1.9 copy.141
  747.0 1.6 copy.142
  748.6 10.6 %collective-permute-done.18 = bf16[2,3,144,768]{3,2,1,0:T(8,128)(2,1)} collective-permute-done((bf16[2,3,144,768]{3,2,1,0:T(8,128)(2,1)}, bf16[2,3,144,768]{3,2,1,0:T(8,128)(2,1)}, u32[]{:S(2)}, u32[]{:S(2)}) %collective-permute-start.18) | collective-permute-done | bytes 1327136 | tf_op jit(solution)/shard_map/ppermute | solution.py:553
  759.2 2.4 add_convert_fusion.6
  762.7 2.4 collective-permute-start.23
  765.1 1.7 add_convert_fusion.9
  769.0 1.6 add_convert_fusion.8
  772.8 3.7 reshape.698
  776.6 2.0 pad.4
  778.6 3.4 gather_fusion.7
  782.0 4.9 all-to-all-start.5
  786.9 3.1 fusion.34
  796.1 2.2 fusion.16
  799.5 12.7 %collective-permute-done.21 = bf16[2,144,1152]{2,1,0:T(8,128)(2,1)S(1)} collective-permute-done((bf16[2,144,1152]{2,1,0:T(8,128)(2,1)S(1)}, bf16[2,144,1152]{2,1,0:T(8,128)(2,1)S(1)}, u32[]{:S(2)}, u32[]{:S(2)}) %collective-permute-start.21) | collective-permute-done | bytes 663584 | tf_op jit(solution)/shard_map/ppermute | solution.py:553
  816.8 14.2 %collective-permute-done.22 = bf16[1,144,1152]{2,1,0:T(8,128)(2,1)S(1)} collective-permute-done((bf16[1,144,1152]{2,1,0:T(8,128)(2,1)S(1)}, bf16[1,144,1152]{2,1,0:T(8,128)(2,1)S(1)}, u32[]{:S(2)}, u32[]{:S(2)}) %collective-permute-start.22) | collective-permute-done | bytes 331808 | tf_op jit(solution)/shard_map/ppermute | solution.py:553
  834.7 1.8 convert_bitcast_fusion
  836.5 5.1 all-to-all-done.5
  841.6 5.6 gather_fusion.9
  (284 shorter events, 77.5 us)
Async XLA Ops:
  7.2 18.6 %copy-start = (bf16[1152,3,288]{0,2,1:T(8,128)(2,1)S(1)}, bf16[1152,3,288]{0,2,1:T(8,128)(2,1)}, u32[]{:S(2)}) copy-start(bf16[1152,3,288]{0,2,1:T(8,128)(2,1)} %param.36) | copy-start | bytes 5971972
  7.2 206.4 %all-gather.5.cloned.1.call-start = ((), (), s32[]{:S(2)}) async-start(), calls=%async_computation.6 | async-start | bytes 10948608 | tf_op jit(solution)/shard_map/all_gather | solution.py:539
  8.1 4.7 collective-permute-start
  10.0 54.0 %copy-start.10 = (s32[8]{0:T(128)}, s32[8]{0:T(128)S(1)}, u32[]{:S(2)}) copy-start(s32[8]{0:T(128)S(1)} %bitcast_subtract_fusion.2) | copy-start | bytes 100
  12.7 4.1 collective-permute-start.1
  16.9 8.5 collective-permute-start.2
  19.7 5.7 copy-start.34
  27.2 334.7 %all-gather.7.cloned.1.call-start = ((), (), s32[]{:S(2)}) async-start(), calls=%async_computation.7 | async-start | bytes 21897216 | tf_op jit(solution)/shard_map/all_gather | solution.py:539
  57.5 5.6 copy-start.12
  57.5 7.0 copy-start.36
  57.5 79.5 %all-to-all-start = ((bf16[32,64,1152]{2,1,0:T(8,128)(2,1)}), bf16[32,64,1152]{2,1,0:T(8,128)(2,1)}, u32[]{:S(2)}, u32[]{:S(2)}) async-start(bf16[32,64,1152]{2,1,0:T(8,128)(2,1)} %gather_fusion.1), calls=%async_computation | async-start | bytes 9437184 | tf_op jit(solution)/shard_map/all_to_all | solution.py:676
  64.5 13.9 %copy-start.38 = (s32[128]{0:T(128)}, s32[128]{0:T(128)S(1)}, u32[]{:S(2)}) copy-start(s32[128]{0:T(128)S(1)} %get-tuple-element.195) | copy-start | bytes 1540
  68.4 9.9 %copy-start.35 = (bf16[128,1152]{0,1:T(8,128)(2,1)}, bf16[128,1152]{0,1:T(8,128)(2,1)S(1)}, u32[]{:S(2)}) copy-start(bf16[128,1152]{0,1:T(8,128)(2,1)S(1)} %get-tuple-element.206) | copy-start | bytes 884740
  141.6 5.4 copy-start.45
  141.6 5.5 copy-start.41
  141.6 7.9 copy-start.40
  141.6 70.4 %all-to-all-start.1 = ((bf16[16,64,1152]{2,1,0:T(8,128)(2,1)}), bf16[16,64,1152]{2,1,0:T(8,128)(2,1)S(1)}, u32[]{:S(2)}, u32[]{:S(2)}) async-start(bf16[16,64,1152]{2,1,0:T(8,128)(2,1)} %gather_fusion.3), calls=%async_computation.1 | async-start | bytes 4718592 | tf_op jit(solution)/shard_map/all_to_all | solution.py:736
  283.9 4.4 copy-start.46
  283.9 4.4 copy-start.47
  284.0 76.3 %all-to-all-start.2 = ((bf16[16,64,1152]{2,1,0:T(8,128)(2,1)}), bf16[16,64,1152]{2,1,0:T(8,128)(2,1)S(1)}, u32[]{:S(2)}, u32[]{:S(2)}) async-start(bf16[16,64,1152]{2,1,0:T(8,128)(2,1)} %param.28), calls=%async_computation.2 | async-start | bytes 4718592 | tf_op jit(solution)/shard_map/all_to_all | solution.py:743
  361.9 33.9 %copy-start.6 = (f32[4,8,1152]{2,1,0:T(8,128)S(1)}, f32[4,8,1152]{2,1,0:T(8,128)}, u32[]{:S(2)}) copy-start(f32[4,8,1152]{2,1,0:T(8,128)} %maximum_maximum_fusion.mods_ref) | copy-start | bytes 442372
  441.4 99.0 %collective-permute-start.3 = (bf16[2,3,576,768]{3,2,1,0:T(8,128)(2,1)}, bf16[2,3,576,768]{3,2,1,0:T(8,128)(2,1)}, u32[]{:S(2)}, u32[]{:S(2)}) collective-permute-start(bf16[2,3,576,768]{3,2,1,0:T(8,128)(2,1)} %get-tuple-element.89), channel_id=1, source_target_pairs={{0,4},{4,0},{8,12},{12,8},{16,20},{20,16},{24,28},{28,24},{1,5},{5... | collective-permute-start | bytes 15925256 | tf_op jit(solution)/shard_map/ppermute | solution.py:553
  477.6 74.6 %collective-permute-start.4 = (bf16[2,3,576,768]{3,2,1,0:T(8,128)(2,1)}, bf16[2,3,576,768]{3,2,1,0:T(8,128)(2,1)S(1)}, u32[]{:S(2)}, u32[]{:S(2)}) collective-permute-start(bf16[2,3,576,768]{3,2,1,0:T(8,128)(2,1)} %get-tuple-element.97), channel_id=1, source_target_pairs={{0,4},{4,0},{8,12},{12,8},{16,20},{20,16},{24,28},{28,24},{1,5},{5... | collective-permute-start | bytes 15925256 | tf_op jit(solution)/shard_map/ppermute | solution.py:553
  552.2 7.9 copy-start.7
  554.5 9.6 %slice-start.3 = ((s8[5308416]{0:T(1024)(128)(4,1)}), s8[4194304]{0:T(1024)(128)(4,1)S(1)}, s32[]{:S(2)}) async-start(s8[5308416]{0:T(1024)(128)(4,1)} %bitcast.149), calls=%async_computation.11 | async-start | bytes 8388608
  554.5 9.6 %slice-start.4 = ((s8[5308416]{0:T(1024)(128)(4,1)}), s8[1114112]{0:T(1024)(128)(4,1)S(1)}, s32[]{:S(2)}) async-start(s8[5308416]{0:T(1024)(128)(4,1)} %bitcast.149), calls=%async_computation.12 | async-start | bytes 2228224
  560.1 3.9 copy-start.16
  562.0 68.9 %collective-permute-start.6 = (bf16[2,3,288,768]{3,2,1,0:T(8,128)(2,1)}, bf16[2,3,288,768]{3,2,1,0:T(8,128)(2,1)}, u32[]{:S(2)}, u32[]{:S(2)}) collective-permute-start(bf16[2,3,288,768]{3,2,1,0:T(8,128)(2,1)} %slice.201), channel_id=1, source_target_pairs={{0,8},{4,12},{8,0},{12,4},{16,24},{20,28},{24,16},{28,20},{1,9},{5... | collective-permute-start | bytes 7962632 | tf_op jit(solution)/shard_map/ppermute | solution.py:553
  571.1 59.8 %collective-permute-start.5 = (bf16[2,3,288,768]{3,2,1,0:T(8,128)(2,1)}, bf16[2,3,288,768]{3,2,1,0:T(8,128)(2,1)}, u32[]{:S(2)}, u32[]{:S(2)}) collective-permute-start(bf16[2,3,288,768]{3,2,1,0:T(8,128)(2,1)} %slice.200), channel_id=1, source_target_pairs={{0,16},{4,20},{8,24},{12,28},{16,0},{20,4},{24,8},{28,12},{1,17},{... | collective-permute-start | bytes 7962632 | tf_op jit(solution)/shard_map/ppermute | solution.py:553
  571.9 59.0 %copy-start.2 = (bf16[4,4,64,1152]{3,2,0,1:T(8,128)(2,1)S(1)}, bf16[4,4,64,1152]{3,2,0,1:T(8,128)(2,1)}, u32[]{:S(2)}) copy-start(bf16[4,4,64,1152]{3,2,0,1:T(8,128)(2,1)} %copy.131) | copy-start | bytes 7077892
  638.0 27.5 %collective-permute-start.7 = (bf16[1,27792]{1,0:T(2,128)(2,1)S(1)}, bf16[1,27792]{1,0:T(2,128)(2,1)S(1)}, u32[]{:S(2)}, u32[]{:S(2)}) collective-permute-start(bf16[1,27792]{1,0:T(2,128)(2,1)S(1)} %broadcast_in_dim.165), channel_id=1, source_target_pairs={{0,2},{1,3},{2,0},{3,1},{4,6},{5,7},{6,4},{7,5},{8,10},{9,11},{10,... | collective-permute-start | bytes 166760 | tf_op jit(solution)/shard_map/ppermute | solution.py:553
  638.2 36.8 %slice-start = ((s8[5308416]{0:T(1024)(128)(4,1)}), s8[4194304]{0:T(1024)(128)(4,1)S(1)}, s32[]{:S(2)}) async-start(s8[5308416]{0:T(1024)(128)(4,1)} %bitcast.142), calls=%async_computation.8 | async-start | bytes 8388608
  651.8 23.2 %slice-start.1 = ((s8[5308416]{0:T(1024)(128)(4,1)}), s8[1114112]{0:T(1024)(128)(4,1)S(1)}, s32[]{:S(2)}) async-start(s8[5308416]{0:T(1024)(128)(4,1)} %bitcast.142), calls=%async_computation.9 | async-start | bytes 2228224
  665.7 7.4 collective-permute-start.8
  672.0 38.3 %collective-permute-start.14 = (bf16[2,3,144,768]{3,2,1,0:T(8,128)(2,1)}, bf16[2,3,144,768]{3,2,1,0:T(8,128)(2,1)}, u32[]{:S(2)}, u32[]{:S(2)}) collective-permute-start(bf16[2,3,144,768]{3,2,1,0:T(8,128)(2,1)} %slice.208), channel_id=1, source_target_pairs={{0,16},{4,20},{8,24},{12,28},{16,0},{20,4},{24,8},{28,12},{1,17},{... | collective-permute-start | bytes 3981320 | tf_op jit(solution)/shard_map/ppermute | solution.py:553
  674.2 32.3 %collective-permute-start.9 = (bf16[4,27792]{1,0:T(4,128)(2,1)}, bf16[4,27792]{1,0:T(4,128)(2,1)}, u32[]{:S(2)}, u32[]{:S(2)}) collective-permute-start(bf16[4,27792]{1,0:T(4,128)(2,1)} %pad_maximum_fusion.2), channel_id=1, source_target_pairs={{0,16},{4,20},{8,24},{12,28},{16,0},{20,4},{24,8},{28,12},{1,17},{... | collective-permute-start | bytes 667016 | tf_op jit(solution)/shard_map/ppermute | solution.py:553
  680.2 30.1 %collective-permute-start.13 = (bf16[2,3,144,768]{3,2,1,0:T(8,128)(2,1)}, bf16[2,3,144,768]{3,2,1,0:T(8,128)(2,1)}, u32[]{:S(2)}, u32[]{:S(2)}) collective-permute-start(bf16[2,3,144,768]{3,2,1,0:T(8,128)(2,1)} %slice.206), channel_id=1, source_target_pairs={{0,8},{4,12},{8,0},{12,4},{16,24},{20,28},{24,16},{28,20},{1,9},{5... | collective-permute-start | bytes 3981320 | tf_op jit(solution)/shard_map/ppermute | solution.py:553
  681.5 28.7 %collective-permute-start.12 = (bf16[2,576,1152]{2,1,0:T(8,128)(2,1)}, bf16[2,576,1152]{2,1,0:T(8,128)(2,1)}, u32[]{:S(2)}, u32[]{:S(2)}) collective-permute-start(bf16[2,576,1152]{2,1,0:T(8,128)(2,1)} %get-tuple-element.119), channel_id=1, source_target_pairs={{0,4},{4,0},{8,12},{12,8},{16,20},{20,16},{24,28},{28,24},{1,5},{5... | collective-permute-start | bytes 7962632 | tf_op jit(solution)/shard_map/ppermute | solution.py:553
  681.5 32.2 %collective-permute-start.16 = (bf16[2,576,1152]{2,1,0:T(8,128)(2,1)}, bf16[2,576,1152]{2,1,0:T(8,128)(2,1)}, u32[]{:S(2)}, u32[]{:S(2)}) collective-permute-start(bf16[2,576,1152]{2,1,0:T(8,128)(2,1)} %get-tuple-element.124), channel_id=1, source_target_pairs={{0,4},{4,0},{8,12},{12,8},{16,20},{20,16},{24,28},{28,24},{1,5},{5... | collective-permute-start | bytes 7962632 | tf_op jit(solution)/shard_map/ppermute | solution.py:553
  685.3 59.8 %all-to-all-start.4 = ((bf16[4,256,1152]{2,0,1:T(4,128)(2,1)}), bf16[4,256,1152]{2,0,1:T(4,128)(2,1)}, u32[]{:S(2)}, u32[]{:S(2)}) async-start(bf16[4,256,1152]{2,0,1:T(4,128)(2,1)} %copy.140), calls=%async_computation.4 | async-start | bytes 4718592 | tf_op jit(solution)/shard_map/all_to_all | solution.py:797
  690.0 23.7 %copy-start.32 = (bf16[2,576,1152]{2,1,0:T(8,128)(2,1)S(1)}, bf16[2,576,1152]{2,1,0:T(8,128)(2,1)}, u32[]{:S(2)}) copy-start(bf16[2,576,1152]{2,1,0:T(8,128)(2,1)} %get-tuple-element.123) | copy-start | bytes 7962628
  708.8 17.8 %collective-permute-start.10 = (bf16[8,27792]{1,0:T(8,128)(2,1)}, bf16[8,27792]{1,0:T(8,128)(2,1)S(1)}, u32[]{:S(2)}, u32[]{:S(2)}) collective-permute-start(bf16[8,27792]{1,0:T(8,128)(2,1)} %pad_maximum_fusion.1), channel_id=1, source_target_pairs={{0,8},{4,12},{8,0},{12,4},{16,24},{20,28},{24,16},{28,20},{1,9},{5... | collective-permute-start | bytes 1334024 | tf_op jit(solution)/shard_map/ppermute | solution.py:553
  713.4 45.8 %collective-permute-start.18 = (bf16[2,3,144,768]{3,2,1,0:T(8,128)(2,1)}, bf16[2,3,144,768]{3,2,1,0:T(8,128)(2,1)}, u32[]{:S(2)}, u32[]{:S(2)}) collective-permute-start(bf16[2,3,144,768]{3,2,1,0:T(8,128)(2,1)} %add_convert_fusion.10), channel_id=1, source_target_pairs={{0,1},{1,0},{2,3},{3,2},{4,5},{5,4},{6,7},{7,6},{8,9},{9,8},{10,11... | collective-permute-start | bytes 3981320 | tf_op jit(solution)/shard_map/ppermute | solution.py:553
  716.2 5.7 copy-start.17
  717.5 41.7 %collective-permute-start.17 = (bf16[2,288,1152]{2,1,0:T(8,128)(2,1)}, bf16[2,288,1152]{2,1,0:T(8,128)(2,1)}, u32[]{:S(2)}, u32[]{:S(2)}) collective-permute-start(bf16[2,288,1152]{2,1,0:T(8,128)(2,1)} %slice.210), channel_id=1, source_target_pairs={{0,8},{4,12},{8,0},{12,4},{16,24},{20,28},{24,16},{28,20},{1,9},{5... | collective-permute-start | bytes 3981320 | tf_op jit(solution)/shard_map/ppermute | solution.py:553
  721.9 11.4 %copy-start.14 = (s32[8]{0:T(128)S(1)}, s32[8]{0:T(128)}, u32[]{:S(2)}) copy-start(s32[8]{0:T(128)} %param.32) | copy-start | bytes 100
  721.9 12.7 %copy-start.42 = (s32[72]{0:T(128)S(1)}, s32[72]{0:T(128)}, u32[]{:S(2)}) copy-start(s32[72]{0:T(128)} %constant.208) | copy-start | bytes 868
  723.8 35.4 %collective-permute-start.15 = (bf16[2,288,1152]{2,1,0:T(8,128)(2,1)}, bf16[2,288,1152]{2,1,0:T(8,128)(2,1)}, u32[]{:S(2)}, u32[]{:S(2)}) collective-permute-start(bf16[2,288,1152]{2,1,0:T(8,128)(2,1)} %slice.209), channel_id=1, source_target_pairs={{0,16},{4,20},{8,24},{12,28},{16,0},{20,4},{24,8},{28,12},{1,17},{... | collective-permute-start | bytes 3981320 | tf_op jit(solution)/shard_map/ppermute | solution.py:553
  731.9 2.8 collective-permute-start.11
  759.2 5.9 copy-start.18
  762.6 6.3 copy-start.20
  762.7 35.6 %collective-permute-start.23 = (bf16[1,3,144,768]{3,2,1,0:T(8,128)(2,1)S(1)}, bf16[1,3,144,768]{3,2,1,0:T(8,128)(2,1)}, u32[]{:S(2)}, u32[]{:S(2)}) collective-permute-start(bf16[1,3,144,768]{3,2,1,0:T(8,128)(2,1)S(1)} %slice.224), channel_id=1, source_target_pairs={{0,2},{1,3},{2,0},{3,1},{4,6},{5,7},{6,4},{7,5},{8,10},{9,11},{10,... | collective-permute-start | bytes 1990664 | tf_op jit(solution)/shard_map/ppermute | solution.py:553
  767.8 31.7 %collective-permute-start.19 = (bf16[2,144,1152]{2,1,0:T(8,128)(2,1)}, bf16[2,144,1152]{2,1,0:T(8,128)(2,1)}, u32[]{:S(2)}, u32[]{:S(2)}) collective-permute-start(bf16[2,144,1152]{2,1,0:T(8,128)(2,1)} %slice.214), channel_id=1, source_target_pairs={{0,16},{4,20},{8,24},{12,28},{16,0},{20,4},{24,8},{28,12},{1,17},{... | collective-permute-start | bytes 1990664 | tf_op jit(solution)/shard_map/ppermute | solution.py:553
  771.9 21.7 %collective-permute-start.20 = (bf16[2,144,1152]{2,1,0:T(8,128)(2,1)}, bf16[2,144,1152]{2,1,0:T(8,128)(2,1)}, u32[]{:S(2)}, u32[]{:S(2)}) collective-permute-start(bf16[2,144,1152]{2,1,0:T(8,128)(2,1)} %slice.217), channel_id=1, source_target_pairs={{0,8},{4,12},{8,0},{12,4},{16,24},{20,28},{24,16},{28,20},{1,9},{5... | collective-permute-start | bytes 1990664 | tf_op jit(solution)/shard_map/ppermute | solution.py:553
  782.0 59.6 %all-to-all-start.5 = ((bf16[32,64,1152]{2,1,0:T(8,128)(2,1)}), bf16[32,64,1152]{2,1,0:T(8,128)(2,1)}, u32[]{:S(2)}, u32[]{:S(2)}) async-start(bf16[32,64,1152]{2,1,0:T(8,128)(2,1)} %gather_fusion.7), calls=%async_computation.5 | async-start | bytes 9437184 | tf_op jit(solution)/shard_map/all_to_all | solution.py:844
  786.8 4.8 copy-start.39
  786.8 5.6 copy-start.44
  786.9 6.8 copy-start.29
  791.7 6.6 copy-start.27
  794.9 17.3 %copy-start.25 = (bf16[2,288,1152]{2,1,0:T(8,128)(2,1)S(1)}, bf16[2,288,1152]{2,1,0:T(8,128)(2,1)}, u32[]{:S(2)}) copy-start(bf16[2,288,1152]{2,1,0:T(8,128)(2,1)} %copy-done.24) | copy-start | bytes 3981316
  794.9 17.3 %collective-permute-start.21 = (bf16[2,144,1152]{2,1,0:T(8,128)(2,1)S(1)}, bf16[2,144,1152]{2,1,0:T(8,128)(2,1)S(1)}, u32[]{:S(2)}, u32[]{:S(2)}) collective-permute-start(bf16[2,144,1152]{2,1,0:T(8,128)(2,1)S(1)} %add_convert_fusion.13), channel_id=1, source_target_pairs={{0,1},{1,0},{2,3},{3,2},{4,5},{5,4},{6,7},{7,6},{8,9},{9,8},{10,11... | collective-permute-start | bytes 1990664 | tf_op jit(solution)/shard_map/ppermute | solution.py:553
  813.6 18.3 %copy-start.30 = (f32[864,864]{1,0:T(8,128)S(1)}, f32[864,864]{1,0:T(8,128)}, u32[]{:S(2)}) copy-start(f32[864,864]{1,0:T(8,128)} %constant.203.clone) | copy-start | bytes 8957956
  813.6 17.5 %collective-permute-start.22 = (bf16[1,144,1152]{2,1,0:T(8,128)(2,1)S(1)}, bf16[1,144,1152]{2,1,0:T(8,128)(2,1)S(1)}, u32[]{:S(2)}, u32[]{:S(2)}) collective-permute-start(bf16[1,144,1152]{2,1,0:T(8,128)(2,1)S(1)} %slice.219), channel_id=1, source_target_pairs={{0,2},{1,3},{2,0},{3,1},{4,6},{5,7},{6,4},{7,5},{8,10},{9,11},{10,... | collective-permute-start | bytes 995336 | tf_op jit(solution)/shard_map/ppermute | solution.py:553
  834.7 12.5 %copy-start.1 = (bf16[1152,3,288]{0,2,1:T(8,128)(2,1)S(1)}, bf16[1152,3,288]{0,2,1:T(8,128)(2,1)}, u32[]{:S(2)}) copy-start(bf16[1152,3,288]{0,2,1:T(8,128)(2,1)} %param.36) | copy-start | bytes 5971972
  (23 other events, 57.5 us)
Sparse Core Ops, SparseCore 0:
  27.3 110.5 all-gather.4
  141.4 194.3 all-gather.6

commit v6 on v5

v6 whole, which is shorter than its diff:
```python
import functools
import math

import jax
import jax.numpy as jnp
import numpy as np
from jax import lax
from jax.experimental import pallas as pl
from jax.experimental.pallas import tpu as pltpu
from jax.sharding import PartitionSpec as P

GRID = 16
NCLS = 1000
NBINS = 16

epsilon = 1e-06
rope_base = 10000.0
f32 = jnp.float32
bf16 = jnp.bfloat16


def feature_order(head_dim):
    quarter = head_dim // 4
    firsts = list(range(quarter)) + list(range(2 * quarter, 3 * quarter))
    cut = len(firsts) // 8 * 8
    seconds = [i + quarter for i in firsts]
    return firsts[:cut] + seconds[:cut] + firsts[cut:] + seconds[cut:], cut


def rope_tables(position, head_dim):
    quarter = head_dim // 4
    order, cut = feature_order(head_dim)
    places = jnp.stack([position // GRID, position % GRID]).astype(f32)
    frequency = rope_base ** (-jnp.arange(quarter).astype(f32) / quarter)
    angle = (frequency[None, :, None] * places[:, None, :]).reshape(2 * quarter, -1)
    cosine, sine = jnp.cos(angle), jnp.sin(angle)
    cos_tab = jnp.concatenate([cosine[:cut], cosine[:cut], cosine[cut:], cosine[cut:]])
    sin_tab = jnp.concatenate([-sine[:cut], sine[:cut], -sine[cut:], sine[cut:]])
    return cos_tab, sin_tab


def partner(values, cut):
    rest = values[2 * cut :]
    half = rest.shape[0] // 2
    return jnp.concatenate(
        [values[cut : 2 * cut], values[:cut], pltpu.roll(rest, half, 0)], axis=0
    )


def head_scale(values):
    return lax.rsqrt(jnp.mean(values * values, axis=0, keepdims=True) + epsilon)


def dot_00(a, b):
    return lax.dot_general(a, b, (((0,), (0,)), ((), ())), preferred_element_type=f32)


def dot_11(a, b):
    return lax.dot_general(a, b, (((1,), (1,)), ((), ())), preferred_element_type=f32)


def dot_10(a, b):
    return lax.dot_general(a, b, (((1,), (0,)), ((), ())), preferred_element_type=f32)


def softmax_first(scores):
    shifted = jnp.exp(scores - jnp.max(scores, axis=0, keepdims=True))
    return shifted * (1.0 / jnp.sum(shifted, axis=0, keepdims=True))


def lasting(microseconds):
    return pl.CostEstimate(
        flops=int(microseconds * 1.1e9), bytes_accessed=1 << 20, transcendentals=0
    )


SHIFT_ONE, SCALE_ONE, GATE_ONE, SHIFT_TWO, SCALE_TWO, GATE_TWO, WEIGHT = range(7)


def row_of(mods, which):
    return mods[which : which + 1, :]


def rms(values):
    scale = lax.rsqrt(jnp.mean(values * values, -1, keepdims=True) + epsilon)
    return values * scale, scale


def rms_back(grad, unit, scale, scaling):
    grad = grad * (1.0 + scaling)
    return scale * (grad - unit * jnp.mean(grad * unit, -1, keepdims=True))


def row_sum(values):
    return jnp.sum(values, axis=0, keepdims=True)


def put_rows(sums_ref, image, rows):
    for which in range(sums_ref.shape[1]):
        value = rows.get(which, jnp.zeros((1, sums_ref.shape[2]), f32))
        sums_ref[image, which : which + 1, :] = value


def chunk_rows(ref, image):
    return jnp.concatenate([ref[chunk, image] for chunk in range(ref.shape[0])], axis=0)


def put_chunks(ref, image, values):
    size = ref.shape[2]
    for chunk in range(ref.shape[0]):
        ref[chunk, image] = values[chunk * size : (chunk + 1) * size]


def attend_kernel(
    latent_ref, mods_ref, w_ref, wo_ref, gains_ref, cos_ref, sin_ref,
    proj_ref, att_ref, branch_ref, xt_ref, middle_ref, two_ref, twot_ref, x_ref,
):
    own = mods_ref.shape[0]
    head_dim = gains_ref.shape[1]
    rows_all = att_ref.shape[1]
    length = xt_ref.shape[1] // own
    heads = range(rows_all // head_dim)
    cut = feature_order(head_dim)[1]
    group = pl.program_id(0)

    def place(image):
        return pl.ds(pl.multiple_of(image * length, length), length)

    @pl.when(group == 0)
    def _():
        def entry(image, carry):
            mods = mods_ref[image]
            unit = rms(chunk_rows(latent_ref, image).astype(f32))[0]
            x = (unit * (1.0 + row_of(mods, SCALE_ONE)) + row_of(mods, SHIFT_ONE)).astype(bf16)
            x_ref[place(image), :] = x
            xt_ref[:, place(image)] = x.T
            return carry

        lax.fori_loop(0, own, entry, 0)

    proj_ref[0] = dot_11(w_ref[0, : 3 * rows_all], x_ref[...])

    def heads_of(image, carry):
        tokens = place(image)
        cos_tab, sin_tab = cos_ref[...], sin_ref[...]
        lows = [[], [], []]
        for kind in range(2):
            for head in heads:
                start = kind * rows_all + head * head_dim
                raw = proj_ref[0, start : start + head_dim, tokens]
                scaled = raw * head_scale(raw) * gains_ref[kind]
                turned = scaled * cos_tab + partner(scaled, cut) * sin_tab
                lows[kind].append(turned.astype(bf16))
        for head in heads:
            start = 2 * rows_all + head * head_dim
            lows[2].append(proj_ref[0, start : start + head_dim, tokens].astype(bf16))
        scores = [dot_00(lows[1][head], lows[0][head]) for head in heads]
        probs = [softmax_first(score).astype(bf16) for score in scores]
        outs = [dot_10(lows[2][head], probs[head]) for head in heads]
        att_ref[group, :, tokens] = jnp.concatenate(outs, axis=0).astype(bf16)
        return carry

    lax.fori_loop(0, own, heads_of, 0, unroll=True)

    @pl.when(group == pl.num_programs(0) - 1)
    def _():
        groups = att_ref.shape[0]

        def leave(image, carry):
            tokens = place(image)
            mods = mods_ref[image]
            att = att_ref[:, :, tokens].reshape(groups * rows_all, length)
            branch = dot_00(att, wo_ref[...].reshape(groups * rows_all, -1))
            branch_ref[tokens, :] = branch.astype(bf16)
            latent = chunk_rows(latent_ref, image).astype(f32)
            middle = latent + row_of(mods, GATE_ONE) * branch
            middle_ref[tokens, :] = middle
            two = rms(middle)[0] * (1.0 + row_of(mods, SCALE_TWO)) + row_of(mods, SHIFT_TWO)
            two = two.astype(bf16)
            two_ref[tokens, :] = two
            twot_ref[:, tokens] = two.T
            return carry

        lax.fori_loop(0, own, leave, 0)


def attend_back_kernel(
    latent_ref, proj_ref, low_ref, w_ref, gains_ref, cos_ref, sin_ref, grad_ref, mods_ref,
    out_ref, gain_grad_ref, sums_ref, chunks_ref, cot_ref,
):
    own = mods_ref.shape[0]
    head_dim = gains_ref.shape[1]
    rows_all, tokens_all = proj_ref.shape[1] // 3, proj_ref.shape[2]
    length = tokens_all // own
    heads = range(rows_all // head_dim)
    cut = feature_order(head_dim)[1]
    group = pl.program_id(0)

    def place(image):
        return pl.ds(pl.multiple_of(image * length, length), length)

    @pl.when(group == 0)
    def _():
        gain_grad_ref[...] = jnp.zeros_like(gain_grad_ref)

    cot_ref[...] = dot_11(w_ref[group, 3 * rows_all :], low_ref[...])

    def heads_of(image, carry):
        tokens = place(image)
        cos_tab, sin_tab = cos_ref[...], sin_ref[...]
        lows, units, scales = [[], [], []], [[], []], [[], []]
        for kind in range(2):
            for head in heads:
                start = kind * rows_all + head * head_dim
                raw = proj_ref[0, start : start + head_dim, tokens]
                scale = head_scale(raw)
                unit = raw * scale
                scaled = unit * gains_ref[kind]
                turned = scaled * cos_tab + partner(scaled, cut) * sin_tab
                lows[kind].append(turned.astype(bf16))
                units[kind].append(unit)
                scales[kind].append(scale)
        cots = []
        for head in heads:
            start = 2 * rows_all + head * head_dim
            lows[2].append(proj_ref[0, start : start + head_dim, tokens].astype(bf16))
            cots.append(cot_ref[head * head_dim : (head + 1) * head_dim, tokens].astype(bf16))
        scores = [dot_00(lows[1][head], lows[0][head]) for head in heads]
        prob_grads = [dot_00(lows[2][head], cots[head]) for head in heads]
        probs = [softmax_first(score) for score in scores]
        outs = [[], [], []]
        outs[2] = [dot_11(cots[head], probs[head].astype(bf16)) for head in heads]
        score_lows = []
        for head in heads:
            mean = jnp.sum(probs[head] * prob_grads[head], axis=0, keepdims=True)
            score_lows.append((probs[head] * (prob_grads[head] - mean)).astype(bf16))
        turned_grads = [
            [dot_10(lows[1][head], score_lows[head]) for head in heads],
            [dot_11(lows[0][head], score_lows[head]) for head in heads],
        ]
        for kind in range(2):
            total = 0.0
            for head in heads:
                grad, unit = turned_grads[kind][head], units[kind][head]
                grad = grad * cos_tab + partner(grad * sin_tab, cut)
                total = total + grad * unit
                grad = grad * gains_ref[kind]
                along = jnp.mean(grad * unit, axis=0, keepdims=True)
                outs[kind].append(scales[kind][head] * (grad - unit * along))
            gain_grad_ref[kind] += total
        grads = jnp.concatenate(outs[0] + outs[1] + outs[2], axis=0).astype(bf16)
        out_ref[group, :, tokens] = grads
        return carry

    lax.fori_loop(0, own, heads_of, 0, unroll=True)

    @pl.when(group == pl.num_programs(0) - 1)
    def _():
        def leave(image, carry):
            tokens = place(image)
            mods = mods_ref[image]
            grad = 0.0
            for other in range(out_ref.shape[0]):
                grad = grad + dot_00(out_ref[other, :, tokens], w_ref[other, : 3 * rows_all])
            unit, scale = rms(chunk_rows(latent_ref, image).astype(f32))
            sums = {SHIFT_ONE: row_sum(grad), SCALE_ONE: row_sum(grad * unit)}
            put_rows(sums_ref, image, sums)
            grad = grad_ref[tokens, :] + rms_back(grad, unit, scale, row_of(mods, SCALE_ONE))
            put_chunks(chunks_ref, image, grad.astype(bf16))
            return carry

        lax.fori_loop(0, own, leave, 0)


def whole_spec(shape):
    return pl.BlockSpec(shape, lambda g: (0,) * len(shape), pipeline_mode=pl.Buffered(1))


def attend(latent, mods, weights, gains, tables):
    groups, rows, width = weights.shape[0], weights.shape[1] // 4, weights.shape[2]
    own = mods.shape[0]
    length, head_dim = tables[0].shape[1], gains.shape[1]
    tokens = own * length
    total, turned = (tokens, width), (width, tokens)
    const = lambda shape: pl.BlockSpec(shape, lambda g: (0,) * len(shape))
    return pl.pallas_call(
        attend_kernel,
        grid=(groups,),
        in_specs=[
            whole_spec(latent.shape),
            whole_spec(mods.shape),
            pl.BlockSpec((1, 4 * rows, width), lambda g: (g, 0, 0)),
            pl.BlockSpec((groups, rows, width), lambda g: (0, 3, 0), pipeline_mode=pl.Buffered(1)),
            whole_spec(gains.shape),
            whole_spec(tables[0].shape),
            whole_spec(tables[0].shape),
        ],
        out_specs=[
            pl.BlockSpec((1, 3 * rows, tokens), lambda g: (g, 0, 0)),
            const((groups, rows, tokens)),
            const(total),
            const(turned),
            const(total),
            const(total),
            const(turned),
        ],
        out_shape=[
            jax.ShapeDtypeStruct((groups, 3 * rows, tokens), f32),
            jax.ShapeDtypeStruct((groups, rows, tokens), bf16),
            jax.ShapeDtypeStruct(total, bf16),
            jax.ShapeDtypeStruct(turned, bf16),
            jax.ShapeDtypeStruct(total, f32),
            jax.ShapeDtypeStruct(total, bf16),
            jax.ShapeDtypeStruct(turned, bf16),
        ],
        scratch_shapes=[pltpu.VMEM(total, bf16)],
        compiler_params=pltpu.CompilerParams(vmem_limit_bytes=62 << 20),
        cost_estimate=lasting(160),
        name="attend",
    )(latent, mods, weights, weights, gains, *tables)


def attend_back(latent, proj, low, weights, gains, tables, grad, mods):
    groups, rows, width = weights.shape[0], weights.shape[1] // 4, weights.shape[2]
    own = mods.shape[0]
    tokens = low.shape[0]
    length, head_dim = tokens // own, gains.shape[1]
    const = lambda shape: pl.BlockSpec(shape, lambda g: (0,) * len(shape))
    gain_shape = (2, head_dim, length)
    return pl.pallas_call(
        attend_back_kernel,
        grid=(groups,),
        in_specs=[
            whole_spec(latent.shape),
            pl.BlockSpec((1, 3 * rows, tokens), lambda g: (g, 0, 0)),
            whole_spec(low.shape),
            whole_spec(weights.shape),
            whole_spec(gains.shape),
            whole_spec(tables[0].shape),
            whole_spec(tables[0].shape),
            whole_spec(grad.shape),
            whole_spec(mods.shape),
        ],
        out_specs=[const(proj.shape), const(gain_shape), const(mods.shape), const(latent.shape)],
        out_shape=[
            jax.ShapeDtypeStruct(proj.shape, bf16),
            jax.ShapeDtypeStruct(gain_shape, f32),
            jax.ShapeDtypeStruct(mods.shape, f32),
            jax.ShapeDtypeStruct(latent.shape, bf16),
        ],
        scratch_shapes=[pltpu.VMEM((rows, tokens), f32)],
        compiler_params=pltpu.CompilerParams(vmem_limit_bytes=62 << 20),
        cost_estimate=lasting(160),
        name="attend_back",
    )(latent, proj, low, weights, gains, *tables, grad, mods)


def finish_kernel(
    branch_ref, middle_ref, cot_ref, mods_ref, low_ref, lowt_ref, chunks_ref, sums_ref
):
    branch, mods = branch_ref[...], mods_ref[0]
    gate = row_of(mods, GATE_TWO)
    result = (middle_ref[...] + gate * branch).astype(bf16)
    put_chunks(chunks_ref, 0, result)
    cot = chunk_rows(cot_ref, 0).astype(f32) * row_of(mods, WEIGHT)
    low = (gate * cot).astype(bf16)
    low_ref[...] = low
    lowt_ref[...] = low.T
    put_rows(sums_ref, 0, {GATE_TWO: row_sum(cot * branch)})


def middle_kernel(
    one_ref, other_ref, middle_ref, branch_ref, cot_ref, mods_ref,
    grad_ref, low_ref, lowt_ref, sums_ref,
):
    mods = mods_ref[0]
    grad = one_ref[...] + other_ref[...]
    unit, scale = rms(middle_ref[...])
    sums = {SHIFT_TWO: row_sum(grad), SCALE_TWO: row_sum(grad * unit)}
    cot = chunk_rows(cot_ref, 0).astype(f32) * row_of(mods, WEIGHT)
    grad = cot + rms_back(grad, unit, scale, row_of(mods, SCALE_TWO))
    grad_ref[...] = grad
    low = (row_of(mods, GATE_ONE) * grad).astype(bf16)
    low_ref[...] = low
    lowt_ref[...] = low.T
    sums[GATE_ONE] = row_sum(grad * branch_ref[...].astype(f32))
    put_rows(sums_ref, 0, sums)


def by_image(kernel, name, rows, chunks, mods, outs):
    own, sums, width = mods.shape
    tokens = rows[0].shape[0]
    length = tokens // own
    block = pl.BlockSpec((length, width), lambda i: (i, 0))
    turned = pl.BlockSpec((width, length), lambda i: (0, i))
    chunk = pl.BlockSpec((chunks.shape[0], 1) + chunks.shape[2:], lambda i: (0, i, 0, 0))
    whole = pl.BlockSpec((1, sums, width), lambda i: (i, 0, 0))
    specs, shapes = [], []
    for out in outs:
        if out is True:
            specs.append(turned)
            shapes.append(jax.ShapeDtypeStruct((width, tokens), bf16))
        elif out is False:
            specs.append(chunk)
            shapes.append(jax.ShapeDtypeStruct(chunks.shape, bf16))
        else:
            specs.append(block)
            shapes.append(jax.ShapeDtypeStruct((tokens, width), out))
    return pl.pallas_call(
        kernel,
        grid=(own,),
        in_specs=[block] * len(rows) + [chunk, whole],
        out_specs=specs + [whole],
        out_shape=shapes + [jax.ShapeDtypeStruct(mods.shape, f32)],
        compiler_params=pltpu.CompilerParams(vmem_limit_bytes=48 << 20),
        cost_estimate=lasting(30),
        name=name,
    )(*rows, chunks, mods)


def modulate_kernel(silu_ref, weight_ref, ada_ref, out_ref):
    own, kinds = out_ref.shape[0], ada_ref.shape[1]
    depth = ada_ref.shape[0]
    base = pl.program_id(0) * depth

    @pl.when(pl.program_id(0) == 0)
    def _():
        out_ref[...] = jnp.zeros_like(out_ref)
        for image in range(own):
            out_ref[image, WEIGHT : WEIGHT + 1, :] = jnp.full(
                (1, out_ref.shape[2]), weight_ref[image], f32
            )

    def step(index, totals):
        row = ada_ref[index].astype(f32)
        return tuple(
            total + silu_ref[image, base + index] * row for image, total in enumerate(totals)
        )

    start = tuple(out_ref[image, :kinds] for image in range(own))
    for image, total in enumerate(lax.fori_loop(0, depth, step, start, unroll=4)):
        out_ref[image, :kinds] = total


def modulate(silu, weight, ada):
    own, width = silu.shape
    depth = math.gcd(width, 144)
    return pl.pallas_call(
        modulate_kernel,
        grid=(width // depth,),
        in_specs=[
            pl.BlockSpec(memory_space=pltpu.SMEM),
            pl.BlockSpec(memory_space=pltpu.SMEM),
            pl.BlockSpec((depth,) + ada.shape[1:], lambda i: (i, 0, 0)),
        ],
        out_specs=pl.BlockSpec((own, 8, width), lambda i: (0, 0, 0)),
        out_shape=jax.ShapeDtypeStruct((own, 8, width), f32),
        compiler_params=pltpu.CompilerParams(vmem_limit_bytes=32 << 20),
        cost_estimate=lasting(100),
        name="modulate",
    )(silu.astype(f32), weight, ada)


def add_rows(out_ref, part, first, index, length):
    rows = pl.ds(pl.multiple_of(index * length, length), length)

    @pl.when(first)
    def _():
        out_ref[rows, :] = part

    @pl.when(jnp.logical_not(first))
    def _():
        out_ref[rows, :] += part


def sigmoid(values):
    return 1.0 / (1.0 + jnp.exp(-values))


def mlp_kernel(count, e_ref, x_ref, *refs):
    first = pl.program_id(0) == 0
    save_ref, out_ref, w_ref = refs[count:]
    size = refs[0].shape[2]
    for index, ref in enumerate(refs[:count]):
        rows = pl.ds(pl.multiple_of(e_ref[index] * size, size), size)
        for kind in range(3):
            w_ref[0, kind, rows, :] = ref[0, kind]
    x = x_ref[...]
    gate = dot_11(x, w_ref[0, 0])
    up = dot_11(x, w_ref[0, 1])
    save_ref[0, 0] = gate.astype(bf16)
    save_ref[0, 1] = up.astype(bf16)
    hidden = (gate * sigmoid(gate) * up).astype(bf16)
    part = dot_10(hidden, w_ref[0, 2])
    add_rows(out_ref, part, first, 0, x.shape[0])


def mlp(x, order, pieces):
    groups, _, size, width = pieces[0].shape
    units, tokens = size * len(pieces), x.shape[0]
    return pl.pallas_call(
        functools.partial(mlp_kernel, len(pieces)),
        grid_spec=pltpu.PrefetchScalarGridSpec(
            num_scalar_prefetch=1,
            grid=(groups,),
            in_specs=[pl.BlockSpec((tokens, width), lambda g, e: (0, 0), pipeline_mode=pl.Buffered(1))]
            + [pl.BlockSpec((1, 3, size, width), lambda g, e: (g, 0, 0, 0))] * len(pieces),
            out_specs=[
                pl.BlockSpec((1, 2, tokens, units), lambda g, e: (g, 0, 0, 0)),
                pl.BlockSpec((tokens, width), lambda g, e: (0, 0)),
                pl.BlockSpec((1, 3, units, width), lambda g, e: (g, 0, 0, 0)),
            ],
        ),
        out_shape=[
            jax.ShapeDtypeStruct((groups, 2, tokens, units), bf16),
            jax.ShapeDtypeStruct((tokens, width), f32),
            jax.ShapeDtypeStruct((groups, 3, units, width), bf16),
        ],
        compiler_params=pltpu.CompilerParams(vmem_limit_bytes=62 << 20),
        cost_estimate=lasting(120),
        name="mlp",
    )(order, x, *pieces)


def fill_rows(order_ref, source_ref, target_ref):
    blocks, rows = source_ref.shape[0], source_ref.shape[1]
    for place in range(blocks):
        target_ref[place * rows : (place + 1) * rows, :] = source_ref[order_ref[place]]


def mlp_back_kernel(
    e_ref, xt_ref, lowt_ref, low_ref, save_ref, w_ref,
    keep_ref, send_ref, two_ref, xs, lows, parts,
):
    first = pl.program_id(0) == 0
    tokens, width = low_ref.shape
    step = math.gcd(tokens, 512)

    @pl.when(first)
    def _():
        fill_rows(e_ref, xt_ref, xs)
        fill_rows(e_ref, lowt_ref, lows)

    for index in range(tokens // step):
        rows = pl.ds(index * step, step)
        hidden_grad = dot_11(low_ref[rows, :], w_ref[0, 2])
        gate = save_ref[0, 0, rows, :].astype(f32)
        up = save_ref[0, 1, rows, :].astype(f32)
        sig = sigmoid(gate)
        swish = gate * sig
        gate_low = (hidden_grad * up * (sig + swish * (1.0 - sig))).astype(bf16)
        up_low = (hidden_grad * swish).astype(bf16)
        parts[0, rows, :] = gate_low
        parts[1, rows, :] = up_low
        parts[2, rows, :] = (swish * up).astype(bf16)
        part = dot_10(gate_low, w_ref[0, 0]) + dot_10(up_low, w_ref[0, 1])
        add_rows(two_ref, part, first, index, step)

    half = width // 2
    for out_ref, rows in ((keep_ref, slice(0, half)), (send_ref, slice(half, width))):
        x_rows = xs[rows, :]
        for kind in range(2):
            out_ref[0, kind] = dot_10(x_rows, parts[kind]).astype(bf16)
        out_ref[0, 2] = dot_10(lows[rows, :], parts[2]).astype(bf16)


def mlp_back(which, e_order, xt, lowt, low, save, weights):
    groups, _, units, width = weights.shape
    tokens = low.shape[0]
    blocks = groups // 2
    base = which * blocks
    once = pl.Buffered(1)
    whole = lambda p, e: (0, 0)
    whole3 = lambda p, e: (0, 0, 0)
    half = jax.ShapeDtypeStruct((blocks, 3, width // 2, units), bf16)
    half_spec = pl.BlockSpec((1, 3, width // 2, units), lambda p, e: (p, 0, 0, 0))
    return pl.pallas_call(
        mlp_back_kernel,
        grid_spec=pltpu.PrefetchScalarGridSpec(
            num_scalar_prefetch=1,
            grid=(blocks,),
            in_specs=[
                pl.BlockSpec(xt.shape, whole3, pipeline_mode=once),
                pl.BlockSpec(lowt.shape, whole3, pipeline_mode=once),
                pl.BlockSpec((tokens, width), whole, pipeline_mode=once),
                pl.BlockSpec((1, 2, tokens, units), lambda p, e: (base + p, 0, 0, 0)),
                pl.BlockSpec((1, 3, units, width), lambda p, e: (base + p, 0, 0, 0)),
            ],
            out_specs=[half_spec, half_spec, pl.BlockSpec((tokens, width), whole)],
            scratch_shapes=[
                pltpu.VMEM((width, tokens), bf16),
                pltpu.VMEM((width, tokens), bf16),
                pltpu.VMEM((3, tokens, units), bf16),
            ],
        ),
        out_shape=[half, half, jax.ShapeDtypeStruct((tokens, width), f32)],
        compiler_params=pltpu.CompilerParams(vmem_limit_bytes=62 << 20),
        cost_estimate=lasting(150),
        name="mlp_back",
    )(e_order, xt, lowt, low, save, weights)


def attend_grads_kernel(
    m_ref, e_ref, xt_ref, lowt_ref, proj_ref, att_ref, keep_ref, send_ref, xs, lows
):
    @pl.when(pl.program_id(0) == 0)
    def _():
        fill_rows(e_ref, xt_ref, xs)
        fill_rows(e_ref, lowt_ref, lows)

    width = xs.shape[0]
    half = width // 2
    columns = proj_ref.shape[1]

    for out_ref, rows in ((keep_ref, slice(0, half)), (send_ref, slice(half, width))):
        out_ref[0, :, :columns] = dot_11(xs[rows, :], proj_ref[0]).astype(bf16)
        out_ref[0, :, columns:] = dot_11(lows[rows, :], att_ref[0]).astype(bf16)


def attend_grads(m_order, e_order, xt, lowt, proj, att, microseconds):
    rows, tokens = att.shape[1:]
    width = xt.shape[0] * xt.shape[1]
    blocks = m_order.shape[0]
    whole3 = lambda p, m, e: (0, 0, 0)
    half = jax.ShapeDtypeStruct((blocks, width // 2, 4 * rows), bf16)
    half_spec = pl.BlockSpec((1, width // 2, 4 * rows), lambda p, m, e: (p, 0, 0))
    return pl.pallas_call(
        attend_grads_kernel,
        grid_spec=pltpu.PrefetchScalarGridSpec(
            num_scalar_prefetch=2,
            grid=(blocks,),
            in_specs=[
                pl.BlockSpec(xt.shape, whole3, pipeline_mode=pl.Buffered(1)),
                pl.BlockSpec(lowt.shape, whole3, pipeline_mode=pl.Buffered(1)),
                pl.BlockSpec((1, 3 * rows, tokens), lambda p, m, e: (m[p], 0, 0)),
                pl.BlockSpec((1, rows, tokens), lambda p, m, e: (m[p], 0, 0)),
            ],
            out_specs=[half_spec, half_spec],
            scratch_shapes=[
                pltpu.VMEM((width, tokens), bf16),
                pltpu.VMEM((width, tokens), bf16),
            ],
        ),
        out_shape=[half, half],
        compiler_params=pltpu.CompilerParams(vmem_limit_bytes=56 << 20),
        cost_estimate=lasting(microseconds),
        name="attend_grads",
    )(m_order, e_order, xt, lowt, proj, att)


def dot(a, b):
    return jnp.dot(a, b, preferred_element_type=f32)


def ein(spec, a, b):
    return jnp.einsum(spec, a, b, preferred_element_type=f32)


def gather_pieces(piece, mp_size):
    whole = lax.all_gather(piece, ("mp", "dp"), axis=0, tiled=False)
    return whole.reshape((mp_size, -1) + piece.shape)


def take_rows(values, index):
    return jnp.take(values, index, axis=0, mode="clip")


def bits_of(size):
    return [1 << i for i in range(size.bit_length() - 1)]


def swap(values, axis, bit):
    size = lax.axis_size(axis)
    return lax.ppermute(values, axis, [(i, i ^ bit) for i in range(size)])


def xor_gather(values, axes_bits):
    names = sorted({axis for axis, _ in axes_bits})
    places = [{name: 0 for name in names}]
    values = values[None]
    for axis, bit in axes_bits:
        values = jnp.concatenate([values, swap(values, axis, bit)], axis=0)
        places = places + [dict(place, **{axis: place[axis] ^ bit}) for place in places]
    return values, {name: [place[name] for place in places] for name in names}


def halving_order(bits):
    order = [0]
    for bit in reversed(bits):
        order = order + [place ^ bit for place in order]
    return order


def add_low(kept, received):
    return (kept.astype(f32) + received.astype(f32)).astype(bf16)


def tie(*values):
    return lax.optimization_barrier(values)


def split(values, dim):
    size = values.shape[dim] // 2
    return (
        lax.slice_in_dim(values, 0, size, axis=dim),
        lax.slice_in_dim(values, size, 2 * size, axis=dim),
    )


def halve(values, axis, bits, dim):
    for bit in bits:
        kept, sent = split(values, dim)
        values = add_low(kept, swap(sent, axis, bit))
    return values


def shards(
    patches,
    cotangent,
    time_bins,
    labels,
    image_counts,
    dest_perm,
    time_table,
    class_table,
    ada_weight,
    qkv_weight,
    norm_gains,
    out_weight,
    expand_weight,
    down_weight,
):
    dp_size = lax.axis_size("dp")
    mp_size = lax.axis_size("mp")
    capacity = patches.shape[0]
    slot_count = capacity // dp_size
    images = cotangent.shape[0]
    local_len = patches.shape[1]
    model_width = patches.shape[2]
    length = local_len * mp_size
    head_dim = norm_gains.shape[1]
    local_dim = out_weight.shape[0]
    unit_count = down_weight.shape[0]
    own = images // mp_size
    total_images = images * dp_size
    order = np.array(feature_order(head_dim)[0])
    columns = np.arange(4 * local_dim)
    places = columns // head_dim * head_dim + order[columns % head_dim]
    places = np.where(columns < 2 * local_dim, places, columns).astype(np.int32)
    gains_f = norm_gains.astype(f32)[:, order]
    gains_f = (gains_f * jnp.array([[head_dim ** (-0.5)], [1.0]], f32))[:, :, None]
    dp_index = lax.axis_index("dp")
    mp_index = lax.axis_index("mp")
    dp_bits = bits_of(dp_size)
    dp_bits = (dp_bits, dp_bits[:1] + dp_bits[1:][::-1])
    mp_bits = bits_of(mp_size)

    tables = rope_tables(jnp.arange(length), head_dim)

    def turn(chunks):
        return lax.all_to_all(chunks, "mp", split_axis=0, concat_axis=0, tiled=True)

    starts = jnp.cumsum(image_counts) - image_counts
    finish = starts + image_counts
    my_start = starts[dp_index]
    my_count = image_counts[dp_index]
    device_ids = jnp.arange(dp_size)
    matches = (dest_perm[:, None] == device_ids[None, :]).astype(jnp.int32)
    inverse = jnp.sum(device_ids[:, None] * matches, axis=0)
    my_place = inverse[dp_index]
    pair_ids = jnp.arange(dp_size * slot_count)
    pair_peer = pair_ids // slot_count
    pair_slot = pair_ids % slot_count
    send_index = pair_slot * dp_size + jnp.mod(inverse[pair_peer] - my_start, dp_size)
    send_index = jnp.minimum(send_index, capacity - 1)
    send_patches = take_rows(patches, send_index)
    info, info_places = xor_gather(
        jnp.stack([time_bins, labels]), [("dp", bit) for bit in bits_of(dp_size)]
    )
    qkv_weight, out_weight, expand_weight, down_weight, send_patches, info = tie(
        qkv_weight, out_weight, expand_weight, down_weight, send_patches, info
    )
    share = 4 * local_dim // dp_size
    spots = lax.dynamic_slice_in_dim(jnp.array(places), dp_index * share, share, 0)
    take_qkv = (spots[:, None] == jnp.arange(3 * local_dim)[None, :]).astype(bf16)
    take_out = (spots[:, None] - 3 * local_dim == jnp.arange(local_dim)[None, :]).astype(bf16)
    attend_piece = ein("rc,dc->rd", take_qkv, qkv_weight.reshape(model_width, -1))
    attend_piece = (attend_piece + dot(take_out, out_weight)).astype(bf16)
    share = unit_count // dp_size
    spots = dp_index * share + jnp.arange(share)
    take_units = (spots[:, None] == jnp.arange(unit_count)[None, :]).astype(bf16)
    mlp_piece = jnp.stack(
        [
            ein("rf,df->rd", take_units, expand_weight[:, 0]).astype(bf16),
            ein("rf,df->rd", take_units, expand_weight[:, 1]).astype(bf16),
            lax.dynamic_slice_in_dim(down_weight, dp_index * share, share, 0),
        ]
    )
    attend_full = gather_pieces(attend_piece, mp_size).reshape(mp_size, 4 * local_dim, -1)
    by_permutes = share % 32 == 0 and dp_size == 8 and mp_size == 4
    if by_permutes:
        mlp_near = mlp_piece[None]
        far_near = swap(mlp_near, "mp", 2)
    else:
        mlp_full = gather_pieces(mlp_piece, mp_size)
        mlp_full = mlp_full.swapaxes(1, 2).reshape(mp_size, 3, unit_count, model_width)
        mlp_pieces = [mlp_full[mp_index ^ jnp.array(halving_order(mp_bits))]]
        mlp_order = jnp.zeros((1,), jnp.int32)

    recv_patches = lax.all_to_all(send_patches, "dp", split_axis=0, concat_axis=0, tiled=True)
    info = info.swapaxes(0, 1).reshape(2, -1)
    info_owner = jnp.repeat(dp_index ^ jnp.array(info_places["dp"]), capacity)
    info_slot = jnp.tile(jnp.arange(capacity), dp_size)
    info_count = jnp.sum(
        jnp.where(info_owner[:, None] == device_ids[None, :], image_counts[None, :], 0), axis=1
    )
    live_all = info_slot < info_count
    bin_totals = jnp.sum(
        ((info[0][:, None] == jnp.arange(NBINS)[None, :]) & live_all[:, None]).astype(f32), axis=0
    )
    gather_bits = [("mp", bit) for bit in bits_of(mp_size)[::-1]]
    gather_bits = gather_bits + [("dp", bit) for bit in bits_of(dp_size)[::-1]]
    spread = {"dp": [0], "mp": [0]}
    for axis, bit in gather_bits:
        spread = {
            name: spread[name] + [place ^ (bit if name == axis else 0) for place in spread[name]]
            for name in spread
        }
    owner_all = jnp.repeat(dp_index ^ jnp.array(spread["dp"]), own)
    group_all = jnp.repeat(mp_index ^ jnp.array(spread["mp"]), own)
    row_all = group_all * own + jnp.tile(jnp.arange(own), dp_size * mp_size)
    place_all = jnp.sum(
        jnp.where(owner_all[:, None] == device_ids[None, :], inverse[None, :], 0), axis=1
    )
    rank_all = row_all * dp_size + place_all
    source_all = jnp.sum((finish[None, :] <= rank_all[:, None]).astype(jnp.int32), axis=1)
    start_all = jnp.sum(
        jnp.where(source_all[:, None] == device_ids[None, :], starts[None, :], 0), axis=1
    )
    slots_all = source_all * capacity + rank_all - start_all
    slot_hit = slots_all[:, None] == (info_owner * capacity + info_slot)[None, :]
    bins_all = jnp.sum(jnp.where(slot_hit, info[0][None, :], 0), axis=1)
    labels_all = jnp.sum(jnp.where(slot_hit, info[1][None, :], 0), axis=1)
    bin_hot = (bins_all[:, None] == jnp.arange(NBINS)[None, :])
    label_hot = (labels_all[:, None] == jnp.arange(NCLS)[None, :])
    weights_all = total_images / (NBINS * jnp.sum(bin_hot.astype(f32) * bin_totals[None, :], axis=1))
    bin_hot = bin_hot.astype(bf16)
    label_hot = label_hot.astype(bf16)
    cond_all = (dot(bin_hot, time_table) + dot(label_hot, class_table)).astype(bf16).astype(f32)
    silu_all = jax.nn.silu(cond_all).astype(bf16)
    silu_cond = silu_all[:own]
    weights = weights_all[:own]

    if by_permutes:
        silu_cond, far_near = tie(silu_cond, far_near)
        mlp_near = jnp.concatenate([mlp_near, far_near], axis=0)
        far_near = swap(mlp_near, "mp", 1)
    mods = modulate(silu_cond, weights, ada_weight)
    recv_patches, mods = tie(recv_patches, mods)

    rank_ids = jnp.arange(images) * dp_size + my_place
    source = jnp.sum((finish[None, :] <= rank_ids[:, None]).astype(jnp.int32), axis=1)
    within = rank_ids - starts[source]
    recv_index = source * slot_count + within // dp_size
    latent = take_rows(recv_patches, recv_index).reshape(mp_size, own, local_len, model_width)
    latent = turn(latent)
    if by_permutes:
        mlp_near = jnp.concatenate([mlp_near, far_near], axis=0)
        halves = split(mlp_near, 2)
        orders = ((2, 4), (4, 2))
        got = [swap(halves[half], "dp", orders[half][0]) for half in range(2)]
        latent, got[0], got[1] = tie(latent, got[0], got[1])
        halves = [jnp.stack([halves[half], got[half]]) for half in range(2)]
        got = [swap(halves[half], "dp", orders[half][1]) for half in range(2)]

    proj, attended, branch_one, normed_t, middle, two, two_t = attend(
        latent, mods, attend_full, gains_f, tables
    )
    cotangent, attended = tie(cotangent, attended)
    cot = turn(cotangent.reshape(mp_size, own, local_len, model_width))
    if by_permutes:
        mlp_pieces, mlp_order = [], []
        for half in range(2):
            first, second = orders[half]
            parts = {0: halves[half][0], first: halves[half][1]}
            parts.update({second: got[half][0], first ^ second: got[half][1]})
            for near, part in parts.items():
                mlp_pieces += [part, swap(part, "dp", 1)]
                mlp_order += [(dp_index ^ near) * 2 + half, (dp_index ^ near ^ 1) * 2 + half]
        mlp_order = jnp.stack(mlp_order).astype(jnp.int32)
    save, branch_two, mlp_full = mlp(two, mlp_order, mlp_pieces)
    down_low, down_t, result, sums_finish = by_image(
        finish_kernel, "finish", (branch_two, middle), cot, mods, (bf16, True, False)
    )
    result = turn(result)

    e_orders = [(dp_index ^ jnp.array(halving_order(bits))).astype(jnp.int32) for bits in dp_bits]
    m_order = (mp_index ^ jnp.array(halving_order(mp_bits))).astype(jnp.int32)
    m_orders = (m_order[: mp_size // 2], m_order[mp_size // 2 :])

    def by_owner(values):
        return values.reshape(dp_size, model_width // dp_size, -1)

    two_t, down_t = by_owner(two_t), by_owner(down_t)
    kept_one, sent_one, two_one = mlp_back(
        1, e_orders[1], two_t, down_t, down_low, save, mlp_full
    )
    got_one = swap(sent_one, "dp", dp_bits[1][0])
    kept_zero, sent_zero, two_zero = mlp_back(
        0, e_orders[0], two_t, down_t, down_low, save, mlp_full
    )
    got_zero = swap(sent_zero, "dp", dp_bits[0][0])
    two_zero, got_one, result = tie(two_zero, got_one, result)
    kept_one, sent_one = split(add_low(kept_one, got_one), 2)
    got_one = swap(sent_one, "dp", dp_bits[1][1])
    middle_grad, branch_low, branch_t, sums_middle = by_image(
        middle_kernel,
        "middle",
        (two_zero, two_one, middle, branch_one),
        cot,
        mods,
        (f32, bf16, True),
    )
    branch_low, got_zero = tie(branch_low, got_zero)
    kept_zero, sent_zero = split(add_low(kept_zero, got_zero), 2)
    got_zero = swap(sent_zero, "dp", dp_bits[0][1])
    projected_low, gains_grad, sums_entry, latent_back = attend_back(
        latent, proj, branch_low, attend_full, gains_f, tables, middle_grad, mods
    )
    gains_grad = jnp.sum(gains_grad, axis=2) * jnp.array([[head_dim ** (-0.5)], [1.0]], f32)
    projected_low, got_one, got_zero = tie(projected_low, got_one, got_zero)
    kept_one, sent_one = split(add_low(kept_one, got_one), 2)
    kept_zero, sent_zero = split(add_low(kept_zero, got_zero), 2)
    got_one = swap(sent_one, "dp", dp_bits[1][2])
    got_zero = swap(sent_zero, "dp", dp_bits[0][2])
    latent_back = turn(latent_back)

    normed_t, branch_t = by_owner(normed_t), by_owner(branch_t)

    def grads_of(which):
        kept, sent = attend_grads(
            m_orders[which],
            e_orders[which],
            normed_t,
            branch_t,
            projected_low,
            attended,
            200 if which else 5,
        )
        return kept, swap(sent, "dp", dp_bits[which][0])

    attend_one, attend_got_one = grads_of(1)
    attend_zero, attend_got_zero = grads_of(0)
    attend_zero, attend_got_one, got_one, got_zero = tie(
        attend_zero, attend_got_one, got_one, got_zero
    )
    mlp_one = halve(add_low(kept_one, got_one), "dp", dp_bits[1][3:], 2)
    mlp_zero = halve(add_low(kept_zero, got_zero), "dp", dp_bits[0][3:], 2)
    mlp_got = swap(mlp_one, "mp", mp_bits[0])
    attend_one, sent_one = split(add_low(attend_one, attend_got_one), 1)
    attend_zero, sent_zero = split(add_low(attend_zero, attend_got_zero), 1)
    attend_got_one = swap(sent_one, "dp", dp_bits[1][1])
    attend_got_zero = swap(sent_zero, "dp", dp_bits[0][1])

    packed = sums_finish + sums_middle + sums_entry
    gains_row = jnp.pad(gains_grad.reshape(1, 1, -1), ((0, own - 1), (7, 0), (0, model_width - 2 * head_dim)))
    packed = jnp.where(jnp.arange(8)[:, None] == 7, gains_row, packed).astype(bf16)
    packed = xor_gather(packed, gather_bits)[0]
    latent_back, attend_got_one, attend_got_zero, mlp_got = tie(
        latent_back, attend_got_one, attend_got_zero, mlp_got
    )
    attend_one = halve(add_low(attend_one, attend_got_one), "dp", dp_bits[1][2:], 1)
    attend_zero = halve(add_low(attend_zero, attend_got_zero), "dp", dp_bits[0][2:], 1)
    mlp_grad = halve(add_low(mlp_zero, mlp_got), "mp", mp_bits[1:], 0)[0].astype(f32)
    attend_grad = add_low(attend_zero, swap(attend_one, "mp", mp_bits[0]))
    attend_grad = halve(attend_grad, "mp", mp_bits[1:], 0)[0].astype(f32)

    back_within = pair_slot * dp_size + jnp.mod(my_place - starts[pair_peer], dp_size)
    back_valid = back_within < image_counts[pair_peer]
    back_slot = jnp.clip((starts[pair_peer] + back_within - my_place) // dp_size, 0, images - 1)
    back_slot = jnp.where(back_valid, back_slot, images)
    empty = jnp.zeros((1, local_len, model_width), bf16)
    latent_back = latent_back.reshape(images, local_len, model_width)
    latent_back = jnp.concatenate([latent_back, empty], axis=0)
    back_patches = take_rows(latent_back, back_slot)
    got_patches = lax.all_to_all(back_patches, "dp", split_axis=0, concat_axis=0, tiled=True)
    slot_ids = jnp.arange(capacity)
    home_peer = dest_perm[jnp.mod(my_start + slot_ids, dp_size)]
    home_index = home_peer * slot_count + jnp.minimum(slot_ids // dp_size, slot_count - 1)
    patch_grad = take_rows(got_patches, home_index)

    packed = packed.reshape(total_images, 8, model_width)
    mod_all = packed[:, :6]
    gains_total = packed.reshape(-1, own, 8, model_width)[:, 0, 7, : 2 * head_dim]
    gains_total = jnp.sum(gains_total.astype(f32), axis=0).reshape(2, head_dim)
    gains_total = jnp.sum(
        jnp.where(order[:, None] == jnp.arange(head_dim)[None, :], gains_total[:, :, None], 0.0), axis=1
    )
    width_dp = model_width // dp_size
    width_mp = model_width // mp_size
    row0 = dp_index * width_dp
    silu_rows = lax.dynamic_slice_in_dim(silu_all, row0, width_dp, 1)
    mod_cols = lax.dynamic_slice_in_dim(mod_all, mp_index * width_mp, width_mp, 2)
    ada_grad = ein("id,ikc->dkc", silu_rows, mod_cols)
    ada_rows = lax.dynamic_slice_in_dim(ada_weight, row0, width_dp, 0)
    silu_grad = ein("ikc,dkc->id", mod_all, ada_rows)
    cond_rows = lax.dynamic_slice_in_dim(cond_all, row0, width_dp, 1)
    silu_val, silu_pull = jax.vjp(jax.nn.silu, cond_rows)
    condition_low = silu_pull(silu_grad)[0].astype(bf16)
    time_grad = ein("in,id->nd", bin_hot, condition_low)
    class_grad = ein("in,id->nd", label_hot, condition_low)

    expand_grad = mlp_grad[:2].swapaxes(0, 1)
    down_grad = mlp_grad[2].T
    out_grad = attend_grad[:, 3 * local_dim :].T
    qkv_grad = lax.dot_general(
        attend_grad[:, : 3 * local_dim],
        jnp.array(places[: 3 * local_dim, None] == columns[: 3 * local_dim], f32),
        (((1,), (0,)), ((), ())),
        precision=lax.Precision.HIGHEST,
        preferred_element_type=f32,
    )
    qkv_grad = qkv_grad.reshape(-1, 3, local_dim)
    return (
        result.reshape(images, local_len, model_width),
        patch_grad,
        time_grad,
        class_grad,
        ada_grad,
        qkv_grad,
        gains_total,
        out_grad,
        expand_grad,
        down_grad,
    )


def solution(mesh):
    in_specs = (
        P("dp", "mp", None),
        P("dp", "mp", None),
        P("dp"),
        P("dp"),
        P(),
        P(),
        P(),
        P(),
        P(),
        P(None, None, "mp"),
        P(),
        P("mp", None),
        P(None, None, "mp"),
        P("mp", None),
    )
    out_specs = (
        P("dp", "mp", None),
        P("dp", "mp", None),
        P(None, "dp"),
        P(None, "dp"),
        P("dp", None, "mp"),
        P("dp", None, "mp"),
        P(),
        P("mp", "dp"),
        P("dp", None, "mp"),
        P("mp", "dp"),
    )
    return jax.shard_map(shards, mesh=mesh, in_specs=in_specs, out_specs=out_specs, check_vma=False)
```

time: 864 us -> 849 us (0.983)
  waiting for transfers between devices: 252 us -> 313 us
  blocking collectives: 57 us -> 0 us
  Pallas kernels: 284 us -> 253 us
  starting transfers between devices: 46.9 us -> 65.4 us
  other arithmetic: 53.1 us -> 63.1 us
  matrix products: 25.5 us -> 16 us
    ppermute x24 -> x38, waiting for transfers between devices: 55.7 us -> 263 us  [swap(): return lax.ppermute(values, axis, [(i, i ^ bit) for i in range(size)])]
    all_to_all x3 -> x4, waiting for transfers between devices: 133 us -> 49.8 us  [turn(): return lax.all_to_all(chunks, 'mp', split_axis=0, concat_axis=0, tiled=True)]
    all_to_all x1, waiting for transfers between devices: 57.7 us -> 0.01 us  [shards(): lax.all_to_all(send_patches, 'dp', split_axis=0, concat_axis=0, tiled=True)]
    all_to_all x1 -> x0, blocking collectives: 57 us -> none  [shards(): lax.all_to_all(result, 'mp', split_axis=1, concat_axis=0, tiled=True)]
    unnamed x113 -> x127, local copies, waits for them, and re-layouts: 40.1 us -> 72.4 us
    pallas_call x6, Pallas kernels: 184 us -> 154 us  [the longest x1 45.2 us: attend_back(): pl.pallas_call(attend_back_kernel, grid=(groups,), in_specs=[whole_spec(l...]
    all_to_all x3 -> x4, starting transfers between devices: 13.4 us -> 29.1 us  [turn(): return lax.all_to_all(chunks, 'mp', split_axis=0, concat_axis=0, tiled=True)]
    concatenate x2, local copies, waits for them, and re-layouts: 15.6 us -> 1.27 us  [xor_gather(): values = jnp.concatenate([values, swap(values, axis, bit)], axis=0)]
  transfers between devices with their start and end apart: 31 -> 45, of which waited for: 9 -> 15; matrix products, arithmetic and copies ran while one was open for 19% -> 19% of each run, Pallas kernels for 24% -> 25%
where the time goes in v6:
time: 849 us; the launch traced here: 845 us
  waiting for transfers between devices  313 us (37%)
  Pallas kernels  253 us (30%)
  local copies, waits for them, and re-layouts  120 us (14%)
  starting transfers between devices  65.4 us (8%)
  other arithmetic  63.1 us (7%)
  matrix products  16 us (2%)
  between operations  15.2 us (2%)
    ppermute x38, waiting for transfers between devices, swap(): return lax.ppermute(values, axis, [(i, i ^ bit) for i in range(size)])  263 us
    unnamed x127, local copies, waits for them, and re-layouts  72.4 us
    pallas_call x2, Pallas kernels, mlp_back(): pl.pallas_call(mlp_back_kernel, grid_spec=pltpu.PrefetchScalarGridSpec(nu...  72.3 us
    all_to_all x4, waiting for transfers between devices, turn(): return lax.all_to_all(chunks, 'mp', split_axis=0, concat_axis=0, tiled=True)  49.8 us
    pallas_call x1, Pallas kernels, attend_back(): pl.pallas_call(attend_back_kernel, grid=(groups,), in_specs=[whole_spec(l...  45.2 us
    pallas_call x1, Pallas kernels, mlp(): pl.pallas_call(functools.partial(mlp_kernel, len(pieces)), grid_spec=pltp...  38 us
    pallas_call x1, Pallas kernels, attend(): pl.pallas_call(attend_kernel, grid=(groups,), in_specs=[whole_spec(latent...  35.9 us
    convert_element_type x12, other arithmetic, add_low(): return (kept.astype(f32) + received.astype(f32)).astype(bf16)  31.3 us
  transfers between devices with their start and end apart: 45, of which 15 were waited for; matrix products, arithmetic and copies ran while one was open for 19% of the time, Pallas kernels for 25%

profile of v6, /device:TPU:0, one launch (start us, length us, event | category | flops | bytes accessed | tf_op | source)
XLA Modules:
  0.0 845.0 jit_solution(3583654583801998922)
XLA Ops:
  18.7 2.6 collective-permute-start.1
  22.9 2.0 collective-permute-start.2
  25.7 5.6 gather_fusion.1
  34.2 43.7 %copy.75.ada_ref = bf16[1152,6,1152]{2,1,0:T(8,128)(2,1)} copy(bf16[1152,6,1152]{2,0,1:T(8,128)(2,1)} %param.35) | data formatting | bytes 31850496 | tf_op args[8]
  81.0 2.7 collective-permute-start.3
  84.3 3.7 multiply_convert_fusion
  88.8 4.6 all-to-all-start
  93.7 47.0 %collective-permute-done.3 = bf16[1,3,96,1152]{3,2,1,0:T(8,128)(2,1)S(1)} collective-permute-done((bf16[1,3,96,1152]{3,2,1,0:T(8,128)(2,1)S(1)}, bf16[1,3,96,1152]{3,2,1,0:T(8,128)(2,1)S(1)}, u32[]{:S(2)}, u32[]{:S(2)}) %collective-permute-start.3) | collective-permute-done | bytes 663584 | tf_op jit(solution)/shard_map/ppermute | solution.py:674
  141.5 7.0 copy-done.2
  148.5 17.6 %modulate.1.mods_ref = f32[4,8,1152]{2,1,0:T(8,128)S(1)} custom-call(f32[4,1152]{1,0:T(4,128)S(1)} %convert_element_type.221.silu_ref, f32[4]{0:T(128)S(1)} %bitcast.151, bf16[1152,6,1152]{2,1,0:T(8,128)(2,1)S(1)} %copy-done.2), custom_call_target="tpu_custom_call" | custom-call | flops 109999996928 | bytes 1048576 | tf_op jit(solution)/shard_map/modulate/pallas_call | solution.py:448
  166.8 4.5 gather_fusion.3
  171.4 15.2 %all-to-all-start.1 = ((bf16[4,4,64,1152]{3,2,1,0:T(8,128)(2,1)}), bf16[4,4,64,1152]{3,2,1,0:T(8,128)(2,1)}, u32[]{:S(2)}, u32[]{:S(2)}) async-start(bf16[4,4,64,1152]{3,2,1,0:T(8,128)(2,1)} %bitcast.21), calls=%async_computation.1 | async-start | bytes 4718592 | tf_op jit(solution)/shard_map/all_to_all | solution.py:761
  186.6 1.6 pad_maximum_fusion
  190.2 29.3 %collective-permute-done.5.refs_2_ = bf16[4,3,48,1152]{3,2,1,0:T(8,128)(2,1)} collective-permute-done((bf16[4,3,48,1152]{3,2,1,0:T(8,128)(2,1)S(1)}, bf16[4,3,48,1152]{3,2,1,0:T(8,128)(2,1)}, u32[]{:S(2)}, u32[]{:S(2)}) %collective-permute-start.5) | collective-permute-done | bytes 1327136 | tf_op jit(solution)/shard_map/ppermute | solution.py:674
  220.6 20.7 %all-to-all-done.1.latent_ref = bf16[4,4,64,1152]{3,2,1,0:T(8,128)(2,1)} async-done(((bf16[4,4,64,1152]{3,2,1,0:T(8,128)(2,1)}), bf16[4,4,64,1152]{3,2,1,0:T(8,128)(2,1)}, u32[]{:S(2)}, u32[]{:S(2)}) %all-to-all-start.1) | async-done | bytes 2359328 | tf_op jit(solution)/shard_map/all_to_all | solution.py:761
  241.3 3.1 pad_maximum_fusion.2
  244.4 3.1 pad_maximum_fusion.1
  253.5 50.7 %collective-permute-done.14 = bf16[2,4,3,48,1152]{4,3,2,1,0:T(8,128)(2,1)} collective-permute-done((bf16[2,4,3,48,1152]{4,3,2,1,0:T(8,128)(2,1)}, bf16[2,4,3,48,1152]{4,3,2,1,0:T(8,128)(2,1)}, u32[]{:S(2)}, u32[]{:S(2)}) %collective-permute-start.14) | collective-permute-done | bytes 2654240 | tf_op jit(solution)/shard_map/ppermute | solution.py:674
  304.2 3.5 slice_bitcast_fusion.4
  308.2 1.7 slice_bitcast_fusion.6
  310.5 35.9 %attend.1 = (f32[4,864,1024]{2,1,0:T(8,128)}, bf16[4,288,1024]{2,1,0:T(8,128)(2,1)}, bf16[1024,1152]{1,0:T(8,128)(2,1)}, bf16[1152,1024]{1,0:T(8,128)(2,1)}, f32...) custom-call(bf16[4,4,64,1152]{3,2,1,0:T(8,128)(2,1)} %all-to-all-done.1.latent_ref, ...), custom_call_target="tpu_custom_call" | custom-call | flops 176000008192 | bytes 1048576 | tf_op jit(solution)/shard_map/attend/pallas_call | solution.py:286
  346.4 4.5 all-to-all-start.2
  351.0 38.0 %mlp.1 = (bf16[4,2,1024,768]{3,2,1,0:T(8,128)(2,1)}, f32[1024,1152]{1,0:T(8,128)}, bf16[4,3,768,1152]{3,2,1,0:T(8,128)(2,1)}) custom-call(s32[16]{0:T(128)} %stack.119.e_ref, bf16[1024,1152]{1,0:T(8,128)(2,1)} %get-tuple-element.85.x_ref, bf16[4,3,48,1152]{3,2,1,0:T(8,128)(2,1)} %copy-done.30, bf16[4,3,48,1152]{3,2,1,0:T(8,128)(2,1)} %collective-permute-done.7.refs_1_, ...), custom_call_target="tpu_custom_call" | custom-call | flops 131999997952 | bytes 1048576 | tf_op jit(solution)/shard_map/mlp/pallas_call | solution.py:501
  389.0 16.7 %all-to-all-done.2.cot_ref = bf16[4,4,64,1152]{3,2,1,0:T(8,128)(2,1)} async-done(((bf16[4,4,64,1152]{3,2,1,0:T(8,128)(2,1)}), bf16[4,4,64,1152]{3,2,1,0:T(8,128)(2,1)}, u32[]{:S(2)}, u32[]{:S(2)}) %all-to-all-start.2) | async-done | bytes 2359328 | tf_op jit(solution)/shard_map/all_to_all | solution.py:761
  405.7 6.8 finish.1
  415.2 36.2 %mlp_back.3 = (bf16[2,3,576,768]{3,2,1,0:T(8,128)(2,1)}, bf16[2,3,576,768]{3,2,1,0:T(8,128)(2,1)}, f32[1024,1152]{1,0:T(8,128)}) custom-call(s32[8]{0:T(128)} %get-tuple-element.210.e_ref, bf16[8,144,1024]{2,1,0:T(8,128)(2,1)} %bitcast.168, bf16[8,144,1024]{2,1,0:T(8,128)(2,1)} %bitcast.149, bf16[1024,1152]{1,0:T(8,128)(2,1)} %copy-done.6, ...), custom_call_target="tpu_custom_call" | custom-call | flops 165000003584 | bytes 1048576 | tf_op jit(solution)/shard_map/mlp_back/pallas_call | solution.py:577
  451.5 4.7 all-to-all-start.3
  456.3 36.1 %mlp_back.2 = (bf16[2,3,576,768]{3,2,1,0:T(8,128)(2,1)}, bf16[2,3,576,768]{3,2,1,0:T(8,128)(2,1)}, f32[1024,1152]{1,0:T(8,128)}) custom-call(s32[8]{0:T(128)} %get-tuple-element.211.e_ref, bf16[8,144,1024]{2,1,0:T(8,128)(2,1)} %bitcast.169, bf16[8,144,1024]{2,1,0:T(8,128)(2,1)} %bitcast.150, bf16[1024,1152]{1,0:T(8,128)(2,1)} %copy-done.6, ...), custom_call_target="tpu_custom_call" | custom-call | flops 165000003584 | bytes 1048576 | tf_op jit(solution)/shard_map/mlp_back/pallas_call | solution.py:577
  494.5 1.7 fusion.48
  498.6 12.4 %all-to-all-done.3 = bf16[4,4,64,1152]{3,2,1,0:T(8,128)(2,1)} async-done(((bf16[4,4,64,1152]{3,2,1,0:T(8,128)(2,1)}), bf16[4,4,64,1152]{3,2,1,0:T(8,128)(2,1)}, u32[]{:S(2)}, u32[]{:S(2)}) %all-to-all-start.3) | async-done | bytes 2359328 | tf_op jit(solution)/shard_map/all_to_all | solution.py:761
  511.0 10.0 %middle.1 = (f32[1024,1152]{1,0:T(8,128)}, bf16[1024,1152]{1,0:T(8,128)(2,1)S(1)}, bf16[1152,1024]{1,0:T(8,128)(2,1)S(1)}, f32[4,8,1152]{2,1,0:T(8,128)S(1)}) custom-call(f32[1024,1152]{1,0:T(8,128)} %get-tuple-element.101.one_ref, f32[1024,1152]{1,0:T(8,128)} %get-tuple-element.102.other_ref, f32[1024,1152]{1,0:T(8,128)} %get-tuple-element.89.middle_ref, ...), custom_call_target="tpu_custom_call" | custom-call | flops 32999999488 | bytes 1048576 | tf_op jit(solution)/shard_map/middle/pallas_call | solution.py:409
  522.5 6.2 add_convert_fusion
  528.7 1.8 slice.226
  532.7 5.3 add_convert_fusion.1
  538.0 1.8 slice.225
  541.7 45.2 %attend_back.1 = (bf16[4,864,1024]{2,1,0:T(8,128)(2,1)}, f32[2,72,256]{2,1,0:T(8,128)}, f32[4,8,1152]{2,1,0:T(8,128)}, bf16[4,4,64,1152]{3,2,1,0:T(8,128)(2,1)}) custom-call(bf16[4,4,64,1152]{3,2,1,0:T(8,128)(2,1)} %all-to-all-done.1.latent_ref, f32[4,864,1024]{2,1,0:T(8,128)} %get-tuple-element.100.proj_ref, bf16[1024,1152]{1,0:T(8,128)(2,1)} %copy-done.5, ...), custom_call_target="tpu_custom_call" | custom-call | flops 176000008192 | bytes 1048576 | tf_op jit(solution)/shard_map/attend_back/pallas_call | solution.py:330
  590.3 4.6 collective-permute-done.28
  595.6 4.7 collective-permute-done.19
  600.4 13.1 %attend_grads.2 = (bf16[2,576,1152]{2,1,0:T(8,128)(2,1)}, bf16[2,576,1152]{2,1,0:T(8,128)(2,1)}) custom-call(s32[2]{0:T(128)} %get-tuple-element.206.m_ref, s32[8]{0:T(128)} %get-tuple-element.210.e_ref, bf16[8,144,1024]{2,1,0:T(8,128)(2,1)} %bitcast.166, bf16[8,144,1024]{2,1,0:T(8,128)(2,1)} %bitcast.147, ...), custom_call_target="tpu_custom_call" | custom-call | flops 219999993856 | bytes 1048576 | tf_op jit(solution)/shard_map/attend_grads/pallas_call | solution.py:627
  613.5 13.7 %attend_grads.3 = (bf16[2,576,1152]{2,1,0:T(8,128)(2,1)}, bf16[2,576,1152]{2,1,0:T(8,128)(2,1)}) custom-call(s32[2]{0:T(128)} %get-tuple-element.207.m_ref, s32[8]{0:T(128)} %get-tuple-element.211.e_ref, bf16[8,144,1024]{2,1,0:T(8,128)(2,1)} %bitcast.167, bf16[8,144,1024]{2,1,0:T(8,128)(2,1)} %bitcast.148, ...), custom_call_target="tpu_custom_call" | custom-call | flops 5500000256 | bytes 1048576 | tf_op jit(solution)/shard_map/attend_grads/pallas_call | solution.py:627
  629.4 2.4 add_convert_fusion.4
  634.5 2.5 add_convert_fusion.5
  639.9 4.7 all-to-all-start.4
  647.2 1.6 constant_dynamic-update-slice_fusion.2
  649.7 31.8 %collective-permute-done.31 = bf16[8,4,8,1152]{3,2,1,0:T(8,128)(2,1)S(1)} collective-permute-done((bf16[8,4,8,1152]{3,2,1,0:T(8,128)(2,1)S(1)}, bf16[8,4,8,1152]{3,2,1,0:T(8,128)(2,1)S(1)}, u32[]{:S(2)}, u32[]{:S(2)}) %collective-permute-start.31) | collective-permute-done | bytes 589856 | tf_op jit(solution)/shard_map/ppermute | solution.py:674
  682.7 2.9 add_convert_fusion.10
  685.5 2.5 add_convert_fusion.2
  691.2 2.4 add_convert_fusion.3
  698.3 2.8 fusion.27
  701.8 24.8 %collective-permute-done.27 = bf16[2,3,144,768]{3,2,1,0:T(8,128)(2,1)} collective-permute-done((bf16[2,3,144,768]{3,2,1,0:T(8,128)(2,1)}, bf16[2,3,144,768]{3,2,1,0:T(8,128)(2,1)}, u32[]{:S(2)}, u32[]{:S(2)}) %collective-permute-start.27) | collective-permute-done | bytes 1327136 | tf_op jit(solution)/shard_map/ppermute | solution.py:674
  729.4 2.0 concatenate.57
  731.4 3.4 gather_fusion.7
  734.8 4.9 all-to-all-start.5
  739.7 2.4 add_convert_fusion.6
  742.1 1.8 collective-permute-start.37
  743.9 1.7 add_convert_fusion.9
  745.7 1.9 collective-permute-start.33
  749.3 2.7 fusion.11
  753.2 21.4 %collective-permute-done.37 = bf16[1,3,144,768]{3,2,1,0:T(8,128)(2,1)S(1)} collective-permute-done((bf16[1,3,144,768]{3,2,1,0:T(8,128)(2,1)S(1)}, bf16[1,3,144,768]{3,2,1,0:T(8,128)(2,1)S(1)}, u32[]{:S(2)}, u32[]{:S(2)}) %collective-permute-start.37) | collective-permute-done | bytes 663584 | tf_op jit(solution)/shard_map/ppermute | solution.py:674
  774.7 32.8 %collective-permute-done.33 = bf16[2,144,1152]{2,1,0:T(8,128)(2,1)S(1)} collective-permute-done((bf16[2,144,1152]{2,1,0:T(8,128)(2,1)S(1)}, bf16[2,144,1152]{2,1,0:T(8,128)(2,1)S(1)}, u32[]{:S(2)}, u32[]{:S(2)}) %collective-permute-start.33) | collective-permute-done | bytes 663584 | tf_op jit(solution)/shard_map/ppermute | solution.py:674
  807.9 1.8 collective-permute-start.36
  812.1 13.2 %collective-permute-done.36 = bf16[1,144,1152]{2,1,0:T(8,128)(2,1)S(1)} collective-permute-done((bf16[1,144,1152]{2,1,0:T(8,128)(2,1)S(1)}, bf16[1,144,1152]{2,1,0:T(8,128)(2,1)S(1)}, u32[]{:S(2)}, u32[]{:S(2)}) %collective-permute-start.36) | collective-permute-done | bytes 331808 | tf_op jit(solution)/shard_map/ppermute | solution.py:674
  829.0 5.7 gather_fusion.9
  834.7 3.3 copy.108
  (315 shorter events, 82.8 us)
Async XLA Ops:
  7.2 24.6 %copy-start = (bf16[1152,3,288]{0,2,1:T(8,128)(2,1)S(1)}, bf16[1152,3,288]{0,2,1:T(8,128)(2,1)}, u32[]{:S(2)}) copy-start(bf16[1152,3,288]{0,2,1:T(8,128)(2,1)} %param.36) | copy-start | bytes 5971972
  7.2 303.3 %all-gather.3.cloned.1.call-start = ((), (), s32[]{:S(2)}) async-start(), calls=%async_computation.6 | async-start | bytes 10948608 | tf_op jit(solution)/shard_map/all_gather | solution.py:660
  8.1 10.7 %collective-permute-start = (s32[1,2,32]{2,1,0:T(2,128)S(1)}, s32[1,2,32]{2,1,0:T(2,128)S(1)}, u32[]{:S(2)}, u32[]{:S(2)}) collective-permute-start(s32[1,2,32]{2,1,0:T(2,128)S(1)} %add_bitcast_fusion), channel_id=1, source_target_pairs={{0,4},{4,0},{8,12},{12,8},{16,20},{20,16},{24,28},{28,24},{1,5},{5... | collective-permute-start | bytes 776 | tf_op jit(solution)/shard_map/ppermute | solution.py:674
  11.9 19.4 %copy-start.10 = (s32[8]{0:T(128)}, s32[8]{0:T(128)S(1)}, u32[]{:S(2)}) copy-start(s32[8]{0:T(128)S(1)} %bitcast_subtract_fusion.2) | copy-start | bytes 100
  18.7 4.1 collective-permute-start.1
  22.9 8.5 %collective-permute-start.2 = (s32[4,2,32]{2,1,0:T(2,128)S(1)}, s32[4,2,32]{2,1,0:T(2,128)S(1)}, u32[]{:S(2)}, u32[]{:S(2)}) collective-permute-start(s32[4,2,32]{2,1,0:T(2,128)S(1)} %pad_add_fusion.1), channel_id=1, source_target_pairs={{0,16},{4,20},{8,24},{12,28},{16,0},{20,4},{24,8},{28,12},{1,17},{... | collective-permute-start | bytes 3080 | tf_op jit(solution)/shard_map/ppermute | solution.py:674
  34.2 43.7 %copy-start.22 = (bf16[1152,2,768]{2,1,0:T(2,128)(2,1)S(1)}, bf16[1152,2,768]{2,1,0:T(2,128)(2,1)}, u32[]{:S(2)}) copy-start(bf16[1152,2,768]{2,1,0:T(2,128)(2,1)} %param.39) | copy-start | bytes 10616836
  81.0 59.6 %collective-permute-start.3 = (bf16[1,3,96,1152]{3,2,1,0:T(8,128)(2,1)S(1)}, bf16[1,3,96,1152]{3,2,1,0:T(8,128)(2,1)S(1)}, u32[]{:S(2)}, u32[]{:S(2)}) collective-permute-start(bf16[1,3,96,1152]{3,2,1,0:T(8,128)(2,1)S(1)} %maximum_bitcast_fusion), channel_id=1, source_target_pairs={{0,2},{1,3},{2,0},{3,1},{4,6},{5,7},{6,4},{7,5},{8,10},{9,11},{10,... | collective-permute-start | bytes 1990664 | tf_op jit(solution)/shard_map/ppermute | solution.py:674
  84.0 9.5 %copy-start.37 = (s32[128]{0:T(128)}, s32[128]{0:T(128)S(1)}, u32[]{:S(2)}) copy-start(s32[128]{0:T(128)S(1)} %get-tuple-element.179) | copy-start | bytes 1540
  88.8 78.0 %all-to-all-start = ((bf16[32,64,1152]{2,1,0:T(8,128)(2,1)}), bf16[32,64,1152]{2,1,0:T(8,128)(2,1)}, u32[]{:S(2)}, u32[]{:S(2)}) async-start(bf16[32,64,1152]{2,1,0:T(8,128)(2,1)} %gather_fusion.1), calls=%async_computation | async-start | bytes 9437184 | tf_op jit(solution)/shard_map/all_to_all | solution.py:810
  140.7 45.9 %collective-permute-start.4 = (bf16[2,3,96,1152]{3,2,1,0:T(8,128)(2,1)S(1)}, bf16[2,3,96,1152]{3,2,1,0:T(8,128)(2,1)}, u32[]{:S(2)}, u32[]{:S(2)}) collective-permute-start(bf16[2,3,96,1152]{3,2,1,0:T(8,128)(2,1)S(1)} %pad_maximum_fusion.3), channel_id=1, source_target_pairs={{0,1},{1,0},{2,3},{3,2},{4,5},{5,4},{6,7},{7,6},{8,9},{9,8},{10,11... | collective-permute-start | bytes 3981320 | tf_op jit(solution)/shard_map/ppermute | solution.py:674
  171.4 69.9 %all-to-all-start.1 = ((bf16[4,4,64,1152]{3,2,1,0:T(8,128)(2,1)}), bf16[4,4,64,1152]{3,2,1,0:T(8,128)(2,1)}, u32[]{:S(2)}, u32[]{:S(2)}) async-start(bf16[4,4,64,1152]{3,2,1,0:T(8,128)(2,1)} %bitcast.21), calls=%async_computation.1 | async-start | bytes 4718592 | tf_op jit(solution)/shard_map/all_to_all | solution.py:761
  188.7 30.9 %collective-permute-start.5 = (bf16[4,3,48,1152]{3,2,1,0:T(8,128)(2,1)S(1)}, bf16[4,3,48,1152]{3,2,1,0:T(8,128)(2,1)}, u32[]{:S(2)}, u32[]{:S(2)}) collective-permute-start(bf16[4,3,48,1152]{3,2,1,0:T(8,128)(2,1)S(1)} %get-tuple-element.187.refs_0_), channel_id=1, source_target_pairs={{0,8},{4,12},{8,0},{12,4},{16,24},{20,28},{24,16},{28,20},{1,9},{5... | collective-permute-start | bytes 3981320 | tf_op jit(solution)/shard_map/ppermute | solution.py:674
  189.7 30.9 %collective-permute-start.6 = (bf16[4,3,48,1152]{3,2,1,0:T(8,128)(2,1)S(1)}, bf16[4,3,48,1152]{3,2,1,0:T(8,128)(2,1)}, u32[]{:S(2)}, u32[]{:S(2)}) collective-permute-start(bf16[4,3,48,1152]{3,2,1,0:T(8,128)(2,1)S(1)} %get-tuple-element.186.refs_8_), channel_id=1, source_target_pairs={{0,16},{4,20},{8,24},{12,28},{16,0},{20,4},{24,8},{28,12},{1,17},{... | collective-permute-start | bytes 3981320 | tf_op jit(solution)/shard_map/ppermute | solution.py:674
  244.4 59.8 %collective-permute-start.14 = (bf16[2,4,3,48,1152]{4,3,2,1,0:T(8,128)(2,1)}, bf16[2,4,3,48,1152]{4,3,2,1,0:T(8,128)(2,1)}, u32[]{:S(2)}, u32[]{:S(2)}) collective-permute-start(bf16[2,4,3,48,1152]{4,3,2,1,0:T(8,128)(2,1)} %pad_maximum_fusion.2), channel_id=1, source_target_pairs={{0,8},{4,12},{8,0},{12,4},{16,24},{20,28},{24,16},{28,20},{1,9},{5... | collective-permute-start | bytes 7962632 | tf_op jit(solution)/shard_map/ppermute | solution.py:674
  247.6 60.1 %collective-permute-start.9 = (bf16[2,4,3,48,1152]{4,3,2,1,0:T(8,128)(2,1)}, bf16[2,4,3,48,1152]{4,3,2,1,0:T(8,128)(2,1)S(1)}, u32[]{:S(2)}, u32[]{:S(2)}) collective-permute-start(bf16[2,4,3,48,1152]{4,3,2,1,0:T(8,128)(2,1)} %pad_maximum_fusion.1), channel_id=1, source_target_pairs={{0,16},{4,20},{8,24},{12,28},{16,0},{20,4},{24,8},{28,12},{1,17},{... | collective-permute-start | bytes 7962632 | tf_op jit(solution)/shard_map/ppermute | solution.py:674
  252.3 57.6 %collective-permute-start.12 = (bf16[4,3,48,1152]{3,2,1,0:T(8,128)(2,1)}, bf16[4,3,48,1152]{3,2,1,0:T(8,128)(2,1)}, u32[]{:S(2)}, u32[]{:S(2)}) collective-permute-start(bf16[4,3,48,1152]{3,2,1,0:T(8,128)(2,1)} %copy-done.29), channel_id=1, source_target_pairs={{0,4},{4,0},{8,12},{12,8},{16,20},{20,16},{24,28},{28,24},{1,5},{5... | collective-permute-start | bytes 3981320 | tf_op jit(solution)/shard_map/ppermute | solution.py:674
  252.3 57.6 %collective-permute-start.7 = (bf16[4,3,48,1152]{3,2,1,0:T(8,128)(2,1)}, bf16[4,3,48,1152]{3,2,1,0:T(8,128)(2,1)}, u32[]{:S(2)}, u32[]{:S(2)}) collective-permute-start(bf16[4,3,48,1152]{3,2,1,0:T(8,128)(2,1)} %copy-done.30), channel_id=1, source_target_pairs={{0,4},{4,0},{8,12},{12,8},{16,20},{20,16},{24,28},{28,24},{1,5},{5... | collective-permute-start | bytes 3981320 | tf_op jit(solution)/shard_map/ppermute | solution.py:674
  252.8 57.6 %collective-permute-start.13 = (bf16[4,3,48,1152]{3,2,1,0:T(8,128)(2,1)}, bf16[4,3,48,1152]{3,2,1,0:T(8,128)(2,1)}, u32[]{:S(2)}, u32[]{:S(2)}) collective-permute-start(bf16[4,3,48,1152]{3,2,1,0:T(8,128)(2,1)} %collective-permute-done.6.refs_10_), channel_id=1, source_target_pairs={{0,4},{4,0},{8,12},{12,8},{16,20},{20,16},{24,28},{28,24},{1,5},{5... | collective-permute-start | bytes 3981320 | tf_op jit(solution)/shard_map/ppermute | solution.py:674
  304.2 46.7 %collective-permute-start.8 = (bf16[4,3,48,1152]{3,2,1,0:T(8,128)(2,1)}, bf16[4,3,48,1152]{3,2,1,0:T(8,128)(2,1)}, u32[]{:S(2)}, u32[]{:S(2)}) collective-permute-start(bf16[4,3,48,1152]{3,2,1,0:T(8,128)(2,1)} %collective-permute-done.5.refs_2_), channel_id=1, source_target_pairs={{0,4},{4,0},{8,12},{12,8},{16,20},{20,16},{24,28},{28,24},{1,5},{5... | collective-permute-start | bytes 3981320 | tf_op jit(solution)/shard_map/ppermute | solution.py:674
  307.7 43.3 %collective-permute-start.15 = (bf16[4,3,48,1152]{3,2,1,0:T(8,128)(2,1)}, bf16[4,3,48,1152]{3,2,1,0:T(8,128)(2,1)}, u32[]{:S(2)}, u32[]{:S(2)}) collective-permute-start(bf16[4,3,48,1152]{3,2,1,0:T(8,128)(2,1)} %get-tuple-element.183.refs_12_), channel_id=1, source_target_pairs={{0,4},{4,0},{8,12},{12,8},{16,20},{20,16},{24,28},{28,24},{1,5},{5... | collective-permute-start | bytes 3981320 | tf_op jit(solution)/shard_map/ppermute | solution.py:674
  309.9 41.1 %collective-permute-start.16 = (bf16[4,3,48,1152]{3,2,1,0:T(8,128)(2,1)}, bf16[4,3,48,1152]{3,2,1,0:T(8,128)(2,1)}, u32[]{:S(2)}, u32[]{:S(2)}) collective-permute-start(bf16[4,3,48,1152]{3,2,1,0:T(8,128)(2,1)} %get-tuple-element.182.refs_14_), channel_id=1, source_target_pairs={{0,4},{4,0},{8,12},{12,8},{16,20},{20,16},{24,28},{28,24},{1,5},{5... | collective-permute-start | bytes 3981320 | tf_op jit(solution)/shard_map/ppermute | solution.py:674
  309.9 41.1 %collective-permute-start.10 = (bf16[4,3,48,1152]{3,2,1,0:T(8,128)(2,1)}, bf16[4,3,48,1152]{3,2,1,0:T(8,128)(2,1)}, u32[]{:S(2)}, u32[]{:S(2)}) collective-permute-start(bf16[4,3,48,1152]{3,2,1,0:T(8,128)(2,1)} %get-tuple-element.189.refs_4_), channel_id=1, source_target_pairs={{0,4},{4,0},{8,12},{12,8},{16,20},{20,16},{24,28},{28,24},{1,5},{5... | collective-permute-start | bytes 3981320 | tf_op jit(solution)/shard_map/ppermute | solution.py:674
  310.4 40.6 %collective-permute-start.11 = (bf16[4,3,48,1152]{3,2,1,0:T(8,128)(2,1)}, bf16[4,3,48,1152]{3,2,1,0:T(8,128)(2,1)}, u32[]{:S(2)}, u32[]{:S(2)}) collective-permute-start(bf16[4,3,48,1152]{3,2,1,0:T(8,128)(2,1)} %get-tuple-element.188.refs_6_), channel_id=1, source_target_pairs={{0,4},{4,0},{8,12},{12,8},{16,20},{20,16},{24,28},{28,24},{1,5},{5... | collective-permute-start | bytes 3981320 | tf_op jit(solution)/shard_map/ppermute | solution.py:674
  346.4 59.3 %all-to-all-start.2 = ((bf16[4,4,64,1152]{3,2,1,0:T(8,128)(2,1)}), bf16[4,4,64,1152]{3,2,1,0:T(8,128)(2,1)}, u32[]{:S(2)}, u32[]{:S(2)}) async-start(bf16[4,4,64,1152]{3,2,1,0:T(8,128)(2,1)} %bitcast.158), calls=%async_computation.2 | async-start | bytes 4718592 | tf_op jit(solution)/shard_map/all_to_all | solution.py:761
  351.0 54.7 %copy-start.8 = (f32[4,8,1152]{2,1,0:T(8,128)S(1)}, f32[4,8,1152]{2,1,0:T(8,128)}, u32[]{:S(2)}) copy-start(f32[4,8,1152]{2,1,0:T(8,128)} %copy-done.7) | copy-start | bytes 442372
  451.5 59.5 %collective-permute-start.17 = (bf16[2,3,576,768]{3,2,1,0:T(8,128)(2,1)}, bf16[2,3,576,768]{3,2,1,0:T(8,128)(2,1)}, u32[]{:S(2)}, u32[]{:S(2)}) collective-permute-start(bf16[2,3,576,768]{3,2,1,0:T(8,128)(2,1)} %get-tuple-element.97), channel_id=1, source_target_pairs={{0,4},{4,0},{8,12},{12,8},{16,20},{20,16},{24,28},{28,24},{1,5},{5... | collective-permute-start | bytes 15925256 | tf_op jit(solution)/shard_map/ppermute | solution.py:674
  451.5 59.5 %all-to-all-start.3 = ((bf16[4,4,64,1152]{3,2,1,0:T(8,128)(2,1)}), bf16[4,4,64,1152]{3,2,1,0:T(8,128)(2,1)}, u32[]{:S(2)}, u32[]{:S(2)}) async-start(bf16[4,4,64,1152]{3,2,1,0:T(8,128)(2,1)} %get-tuple-element.98), calls=%async_computation.3 | async-start | bytes 4718592 | tf_op jit(solution)/shard_map/all_to_all | solution.py:761
  456.2 36.6 %copy-start.11 = (s32[8]{0:T(128)S(1)}, s32[8]{0:T(128)}, u32[]{:S(2)}) copy-start(s32[8]{0:T(128)} %copy-done.10) | copy-start | bytes 100
  456.2 37.4 %copy-start.12 = (s32[8]{0:T(128)S(1)}, s32[8]{0:T(128)}, u32[]{:S(2)}) copy-start(s32[8]{0:T(128)} %param.31) | copy-start | bytes 100
  456.2 40.0 %copy-start.13 = (s32[8]{0:T(128)S(1)}, s32[8]{0:T(128)}, u32[]{:S(2)}) copy-start(s32[8]{0:T(128)} %param.32) | copy-start | bytes 100
  456.2 41.2 %copy-start.53 = (s32[4]{0:T(128)S(1)}, s32[4]{0:T(128)}, u32[]{:S(2)}) copy-start(s32[4]{0:T(128)} %constant.206.clone) | copy-start | bytes 52
  456.2 54.8 %copy-start.9 = (f32[4,8,1152]{2,1,0:T(8,128)S(1)}, f32[4,8,1152]{2,1,0:T(8,128)}, u32[]{:S(2)}) copy-start(f32[4,8,1152]{2,1,0:T(8,128)} %copy-done.7) | copy-start | bytes 442372
  492.3 30.2 %collective-permute-start.18 = (bf16[2,3,576,768]{3,2,1,0:T(8,128)(2,1)}, bf16[2,3,576,768]{3,2,1,0:T(8,128)(2,1)}, u32[]{:S(2)}, u32[]{:S(2)}) collective-permute-start(bf16[2,3,576,768]{3,2,1,0:T(8,128)(2,1)} %get-tuple-element.105), channel_id=1, source_target_pairs={{0,4},{4,0},{8,12},{12,8},{16,20},{20,16},{24,28},{28,24},{1,5},{5... | collective-permute-start | bytes 15925256 | tf_op jit(solution)/shard_map/ppermute | solution.py:674
  531.8 63.9 %collective-permute-start.20 = (bf16[2,3,288,768]{3,2,1,0:T(8,128)(2,1)}, bf16[2,3,288,768]{3,2,1,0:T(8,128)(2,1)}, u32[]{:S(2)}, u32[]{:S(2)}) collective-permute-start(bf16[2,3,288,768]{3,2,1,0:T(8,128)(2,1)} %slice.226), channel_id=1, source_target_pairs={{0,8},{4,12},{8,0},{12,4},{16,24},{20,28},{24,16},{28,20},{1,9},{5... | collective-permute-start | bytes 7962632 | tf_op jit(solution)/shard_map/ppermute | solution.py:674
  541.2 59.2 %collective-permute-start.19 = (bf16[2,3,288,768]{3,2,1,0:T(8,128)(2,1)}, bf16[2,3,288,768]{3,2,1,0:T(8,128)(2,1)}, u32[]{:S(2)}, u32[]{:S(2)}) collective-permute-start(bf16[2,3,288,768]{3,2,1,0:T(8,128)(2,1)} %slice.225), channel_id=1, source_target_pairs={{0,16},{4,20},{8,24},{12,28},{16,0},{20,4},{24,8},{28,12},{1,17},{... | collective-permute-start | bytes 7962632 | tf_op jit(solution)/shard_map/ppermute | solution.py:674
  541.7 46.2 %copy-start.40 = (f32[2]{0:T(128)S(1)}, f32[2]{0:T(128)}, u32[]{:S(2)}) copy-start(f32[2]{0:T(128)} %constant.214) | copy-start | bytes 28
  541.7 46.4 %copy-start.52 = (pred[8]{0:T(512)(128)(4,1)S(1)}, pred[8]{0:T(512)(128)(4,1)}, u32[]{:S(2)}) copy-start(pred[8]{0:T(512)(128)(4,1)} %iota_compare_fusion.19) | copy-start | bytes 28
  541.7 48.0 %copy-start.44 = (s32[32]{0:T(128)S(1)}, s32[32]{0:T(128)}, u32[]{:S(2)}) copy-start(s32[32]{0:T(128)} %get-tuple-element.214) | copy-start | bytes 388
  589.7 5.3 collective-permute-start.28
  595.6 32.0 %collective-permute-start.29 = (bf16[2,4,8,1152]{3,2,1,0:T(8,128)(2,1)}, bf16[2,4,8,1152]{3,2,1,0:T(8,128)(2,1)}, u32[]{:S(2)}, u32[]{:S(2)}) collective-permute-start(bf16[2,4,8,1152]{3,2,1,0:T(8,128)(2,1)} %pad_maximum_fusion.6), channel_id=1, source_target_pairs={{0,1},{1,0},{2,3},{3,2},{4,5},{5,4},{6,7},{7,6},{8,9},{9,8},{10,11... | collective-permute-start | bytes 442376 | tf_op jit(solution)/shard_map/ppermute | solution.py:674
  613.5 69.2 %collective-permute-start.21 = (bf16[2,576,1152]{2,1,0:T(8,128)(2,1)}, bf16[2,576,1152]{2,1,0:T(8,128)(2,1)}, u32[]{:S(2)}, u32[]{:S(2)}) collective-permute-start(bf16[2,576,1152]{2,1,0:T(8,128)(2,1)} %get-tuple-element.120), channel_id=1, source_target_pairs={{0,4},{4,0},{8,12},{12,8},{16,20},{20,16},{24,28},{28,24},{1,5},{5... | collective-permute-start | bytes 7962632 | tf_op jit(solution)/shard_map/ppermute | solution.py:674
  613.5 15.9 %slice-start = ((s8[5308416]{0:T(1024)(128)(4,1)}), s8[4194304]{0:T(1024)(128)(4,1)S(1)}, s32[]{:S(2)}) async-start(s8[5308416]{0:T(1024)(128)(4,1)} %bitcast.153), calls=%async_computation.7 | async-start | bytes 8388608
  613.5 14.2 %copy-start.28 = (bf16[1,4,8,1152]{3,2,1,0:T(8,128)(2,1)S(1)}, bf16[1,4,8,1152]{3,2,1,0:T(8,128)(2,1)}, u32[]{:S(2)}) copy-start(bf16[1,4,8,1152]{3,2,1,0:T(8,128)(2,1)} %copy-done.27) | copy-start | bytes 221188
  613.5 14.2 %copy-start.32 = (bf16[1,4,8,1152]{3,2,1,0:T(8,128)(2,1)S(1)}, bf16[1,4,8,1152]{3,2,1,0:T(8,128)(2,1)}, u32[]{:S(2)}) copy-start(bf16[1,4,8,1152]{3,2,1,0:T(8,128)(2,1)} %copy-done.31) | copy-start | bytes 221188
  613.5 15.9 %slice-start.1 = ((s8[5308416]{0:T(1024)(128)(4,1)}), s8[1114112]{0:T(1024)(128)(4,1)S(1)}, s32[]{:S(2)}) async-start(s8[5308416]{0:T(1024)(128)(4,1)} %bitcast.153), calls=%async_computation.8 | async-start | bytes 2228224
  627.2 58.4 %collective-permute-start.25 = (bf16[2,576,1152]{2,1,0:T(8,128)(2,1)}, bf16[2,576,1152]{2,1,0:T(8,128)(2,1)}, u32[]{:S(2)}, u32[]{:S(2)}) collective-permute-start(bf16[2,576,1152]{2,1,0:T(8,128)(2,1)} %get-tuple-element.125), channel_id=1, source_target_pairs={{0,4},{4,0},{8,12},{12,8},{16,20},{20,16},{24,28},{28,24},{1,5},{5... | collective-permute-start | bytes 7962632 | tf_op jit(solution)/shard_map/ppermute | solution.py:674
  628.8 15.8 %collective-permute-start.30 = (bf16[4,4,8,1152]{3,2,1,0:T(8,128)(2,1)S(1)}, bf16[4,4,8,1152]{3,2,1,0:T(8,128)(2,1)S(1)}, u32[]{:S(2)}, u32[]{:S(2)}) collective-permute-start(bf16[4,4,8,1152]{3,2,1,0:T(8,128)(2,1)S(1)} %pad_maximum_fusion.5), channel_id=1, source_target_pairs={{0,16},{4,20},{8,24},{12,28},{16,0},{20,4},{24,8},{28,12},{1,17},{... | collective-permute-start | bytes 884744 | tf_op jit(solution)/shard_map/ppermute | solution.py:674
  633.0 49.7 %collective-permute-start.23 = (bf16[2,3,144,768]{3,2,1,0:T(8,128)(2,1)}, bf16[2,3,144,768]{3,2,1,0:T(8,128)(2,1)}, u32[]{:S(2)}, u32[]{:S(2)}) collective-permute-start(bf16[2,3,144,768]{3,2,1,0:T(8,128)(2,1)} %slice.230), channel_id=1, source_target_pairs={{0,16},{4,20},{8,24},{12,28},{16,0},{20,4},{24,8},{28,12},{1,17},{... | collective-permute-start | bytes 3981320 | tf_op jit(solution)/shard_map/ppermute | solution.py:674
  638.2 44.5 %collective-permute-start.22 = (bf16[2,3,144,768]{3,2,1,0:T(8,128)(2,1)}, bf16[2,3,144,768]{3,2,1,0:T(8,128)(2,1)}, u32[]{:S(2)}, u32[]{:S(2)}) collective-permute-start(bf16[2,3,144,768]{3,2,1,0:T(8,128)(2,1)} %slice.228), channel_id=1, source_target_pairs={{0,8},{4,12},{8,0},{12,4},{16,24},{20,28},{24,16},{28,20},{1,9},{5... | collective-permute-start | bytes 3981320 | tf_op jit(solution)/shard_map/ppermute | solution.py:674
  639.9 61.9 %all-to-all-start.4 = ((bf16[4,4,64,1152]{3,2,1,0:T(8,128)(2,1)}), bf16[4,4,64,1152]{3,2,1,0:T(8,128)(2,1)}, u32[]{:S(2)}, u32[]{:S(2)}) async-start(bf16[4,4,64,1152]{3,2,1,0:T(8,128)(2,1)} %get-tuple-element.108), calls=%async_computation.4 | async-start | bytes 4718592 | tf_op jit(solution)/shard_map/all_to_all | solution.py:761
  645.6 35.9 %collective-permute-start.31 = (bf16[8,4,8,1152]{3,2,1,0:T(8,128)(2,1)S(1)}, bf16[8,4,8,1152]{3,2,1,0:T(8,128)(2,1)S(1)}, u32[]{:S(2)}, u32[]{:S(2)}) collective-permute-start(bf16[8,4,8,1152]{3,2,1,0:T(8,128)(2,1)S(1)} %pad_maximum_fusion.4), channel_id=1, source_target_pairs={{0,8},{4,12},{8,0},{12,4},{16,24},{20,28},{24,16},{28,20},{1,9},{5... | collective-permute-start | bytes 1769480 | tf_op jit(solution)/shard_map/ppermute | solution.py:674
  682.6 13.1 %collective-permute-start.32 = (bf16[16,4,8,1152]{3,2,1,0:T(8,128)(2,1)}, bf16[16,4,8,1152]{3,2,1,0:T(8,128)(2,1)S(1)}, u32[]{:S(2)}, u32[]{:S(2)}) collective-permute-start(bf16[16,4,8,1152]{3,2,1,0:T(8,128)(2,1)} %get-tuple-element.190), channel_id=1, source_target_pairs={{0,4},{4,0},{8,12},{12,8},{16,20},{20,16},{24,28},{28,24},{1,5},{5... | collective-permute-start | bytes 3538952 | tf_op jit(solution)/shard_map/ppermute | solution.py:674
  685.5 41.1 %collective-permute-start.27 = (bf16[2,3,144,768]{3,2,1,0:T(8,128)(2,1)}, bf16[2,3,144,768]{3,2,1,0:T(8,128)(2,1)}, u32[]{:S(2)}, u32[]{:S(2)}) collective-permute-start(bf16[2,3,144,768]{3,2,1,0:T(8,128)(2,1)} %add_convert_fusion.10), channel_id=1, source_target_pairs={{0,1},{1,0},{2,3},{3,2},{4,5},{5,4},{6,7},{7,6},{8,9},{9,8},{10,11... | collective-permute-start | bytes 3981320 | tf_op jit(solution)/shard_map/ppermute | solution.py:674
  689.2 37.4 %collective-permute-start.26 = (bf16[2,288,1152]{2,1,0:T(8,128)(2,1)}, bf16[2,288,1152]{2,1,0:T(8,128)(2,1)}, u32[]{:S(2)}, u32[]{:S(2)}) collective-permute-start(bf16[2,288,1152]{2,1,0:T(8,128)(2,1)} %slice.232), channel_id=1, source_target_pairs={{0,8},{4,12},{8,0},{12,4},{16,24},{20,28},{24,16},{28,20},{1,9},{5... | collective-permute-start | bytes 3981320 | tf_op jit(solution)/shard_map/ppermute | solution.py:674
  694.8 31.7 %collective-permute-start.24 = (bf16[2,288,1152]{2,1,0:T(8,128)(2,1)}, bf16[2,288,1152]{2,1,0:T(8,128)(2,1)}, u32[]{:S(2)}, u32[]{:S(2)}) collective-permute-start(bf16[2,288,1152]{2,1,0:T(8,128)(2,1)} %slice.231), channel_id=1, source_target_pairs={{0,16},{4,20},{8,24},{12,28},{16,0},{20,4},{24,8},{28,12},{1,17},{... | collective-permute-start | bytes 3981320 | tf_op jit(solution)/shard_map/ppermute | solution.py:674
  728.3 19.4 %collective-permute-start.34 = (bf16[2,144,1152]{2,1,0:T(8,128)(2,1)S(1)}, bf16[2,144,1152]{2,1,0:T(8,128)(2,1)}, u32[]{:S(2)}, u32[]{:S(2)}) collective-permute-start(bf16[2,144,1152]{2,1,0:T(8,128)(2,1)S(1)} %slice.240), channel_id=1, source_target_pairs={{0,8},{4,12},{8,0},{12,4},{16,24},{20,28},{24,16},{28,20},{1,9},{5... | collective-permute-start | bytes 1990664 | tf_op jit(solution)/shard_map/ppermute | solution.py:674
  734.8 94.2 %all-to-all-start.5 = ((bf16[32,64,1152]{2,1,0:T(8,128)(2,1)}), bf16[32,64,1152]{2,1,0:T(8,128)(2,1)}, u32[]{:S(2)}, u32[]{:S(2)}) async-start(bf16[32,64,1152]{2,1,0:T(8,128)(2,1)} %gather_fusion.7), calls=%async_computation.5 | async-start | bytes 9437184 | tf_op jit(solution)/shard_map/all_to_all | solution.py:986
  742.1 32.5 %collective-permute-start.37 = (bf16[1,3,144,768]{3,2,1,0:T(8,128)(2,1)S(1)}, bf16[1,3,144,768]{3,2,1,0:T(8,128)(2,1)S(1)}, u32[]{:S(2)}, u32[]{:S(2)}) collective-permute-start(bf16[1,3,144,768]{3,2,1,0:T(8,128)(2,1)S(1)} %slice.248), channel_id=1, source_target_pairs={{0,2},{1,3},{2,0},{3,1},{4,6},{5,7},{6,4},{7,5},{8,10},{9,11},{10,... | collective-permute-start | bytes 1990664 | tf_op jit(solution)/shard_map/ppermute | solution.py:674
  745.7 61.9 %collective-permute-start.33 = (bf16[2,144,1152]{2,1,0:T(8,128)(2,1)S(1)}, bf16[2,144,1152]{2,1,0:T(8,128)(2,1)S(1)}, u32[]{:S(2)}, u32[]{:S(2)}) collective-permute-start(bf16[2,144,1152]{2,1,0:T(8,128)(2,1)S(1)} %slice.237), channel_id=1, source_target_pairs={{0,16},{4,20},{8,24},{12,28},{16,0},{20,4},{24,8},{28,12},{1,17},{... | collective-permute-start | bytes 1990664 | tf_op jit(solution)/shard_map/ppermute | solution.py:674
  748.9 58.7 %collective-permute-start.35 = (bf16[2,144,1152]{2,1,0:T(8,128)(2,1)S(1)}, bf16[2,144,1152]{2,1,0:T(8,128)(2,1)S(1)}, u32[]{:S(2)}, u32[]{:S(2)}) collective-permute-start(bf16[2,144,1152]{2,1,0:T(8,128)(2,1)S(1)} %add_convert_fusion.13), channel_id=1, source_target_pairs={{0,1},{1,0},{2,3},{3,2},{4,5},{5,4},{6,7},{7,6},{8,9},{9,8},{10,11... | collective-permute-start | bytes 1990664 | tf_op jit(solution)/shard_map/ppermute | solution.py:674
  807.9 17.5 %copy-start.23 = (f32[864,864]{1,0:T(8,128)S(1)}, f32[864,864]{1,0:T(8,128)}, u32[]{:S(2)}) copy-start(f32[864,864]{1,0:T(8,128)} %constant.208.clone) | copy-start | bytes 8957956
  807.9 17.4 %collective-permute-start.36 = (bf16[1,144,1152]{2,1,0:T(8,128)(2,1)S(1)}, bf16[1,144,1152]{2,1,0:T(8,128)(2,1)S(1)}, u32[]{:S(2)}, u32[]{:S(2)}) collective-permute-start(bf16[1,144,1152]{2,1,0:T(8,128)(2,1)S(1)} %slice.242), channel_id=1, source_target_pairs={{0,2},{1,3},{2,0},{3,1},{4,6},{5,7},{6,4},{7,5},{8,10},{9,11},{10,... | collective-permute-start | bytes 995336 | tf_op jit(solution)/shard_map/ppermute | solution.py:674
  829.0 9.0 %copy-start.1 = (bf16[1152,3,288]{0,2,1:T(8,128)(2,1)S(1)}, bf16[1152,3,288]{0,2,1:T(8,128)(2,1)}, u32[]{:S(2)}) copy-start(bf16[1152,3,288]{0,2,1:T(8,128)(2,1)} %param.36) | copy-start | bytes 5971972
  (40 other events, 152.4 us)
Sparse Core Ops, SparseCore 0:
  33.3 109.5 all-gather.2

commit v7 on v6

--- a/solution.py
+++ b/solution.py
@@ -418,47 +418,25 @@
     )(*rows, chunks, mods)
 
 
-def modulate_kernel(silu_ref, weight_ref, ada_ref, out_ref):
-    own, kinds = out_ref.shape[0], ada_ref.shape[1]
-    depth = ada_ref.shape[0]
-    base = pl.program_id(0) * depth
-
-    @pl.when(pl.program_id(0) == 0)
-    def _():
-        out_ref[...] = jnp.zeros_like(out_ref)
-        for image in range(own):
-            out_ref[image, WEIGHT : WEIGHT + 1, :] = jnp.full(
-                (1, out_ref.shape[2]), weight_ref[image], f32
-            )
-
-    def step(index, totals):
-        row = ada_ref[index].astype(f32)
-        return tuple(
-            total + silu_ref[image, base + index] * row for image, total in enumerate(totals)
-        )
-
-    start = tuple(out_ref[image, :kinds] for image in range(own))
-    for image, total in enumerate(lax.fori_loop(0, depth, step, start, unroll=4)):
-        out_ref[image, :kinds] = total
-
-
-def modulate(silu, weight, ada):
-    own, width = silu.shape
-    depth = math.gcd(width, 144)
+def modulate_kernel(silu_ref, ada_ref, out_ref):
+    out_ref[0] = dot_10(silu_ref[...], ada_ref[0])
+
+
+def modulate(silu, ada):
+    kinds, width = ada.shape[:2]
     return pl.pallas_call(
         modulate_kernel,
-        grid=(width // depth,),
+        grid=(kinds,),
         in_specs=[
-            pl.BlockSpec(memory_space=pltpu.SMEM),
-            pl.BlockSpec(memory_space=pltpu.SMEM),
-            pl.BlockSpec((depth,) + ada.shape[1:], lambda i: (i, 0, 0)),
+            pl.BlockSpec(silu.shape, lambda k: (0, 0)),
+            pl.BlockSpec((1, width, width), lambda k: (k, 0, 0)),
         ],
-        out_specs=pl.BlockSpec((own, 8, width), lambda i: (0, 0, 0)),
-        out_shape=jax.ShapeDtypeStruct((own, 8, width), f32),
+        out_specs=pl.BlockSpec((1,) + silu.shape, lambda k: (k, 0, 0)),
+        out_shape=jax.ShapeDtypeStruct((kinds,) + silu.shape, f32),
         compiler_params=pltpu.CompilerParams(vmem_limit_bytes=32 << 20),
-        cost_estimate=lasting(100),
+        cost_estimate=lasting(60),
         name="modulate",
-    )(silu.astype(f32), weight, ada)
+    )(silu, ada)
 
 
 def add_rows(out_ref, part, first, index, length):
@@ -784,7 +762,7 @@
     spots = lax.dynamic_slice_in_dim(jnp.array(places), dp_index * share, share, 0)
     take_qkv = (spots[:, None] == jnp.arange(3 * local_dim)[None, :]).astype(bf16)
     take_out = (spots[:, None] - 3 * local_dim == jnp.arange(local_dim)[None, :]).astype(bf16)
-    attend_piece = ein("rc,dc->rd", take_qkv, qkv_weight.reshape(model_width, -1))
+    attend_piece = dot(take_qkv, qkv_weight.transpose(1, 2, 0).reshape(-1, model_width))
     attend_piece = (attend_piece + dot(take_out, out_weight)).astype(bf16)
     share = unit_count // dp_size
     spots = dp_index * share + jnp.arange(share)
@@ -855,8 +833,20 @@
         silu_cond, far_near = tie(silu_cond, far_near)
         mlp_near = jnp.concatenate([mlp_near, far_near], axis=0)
         far_near = swap(mlp_near, "mp", 1)
-    mods = modulate(silu_cond, weights, ada_weight)
-    recv_patches, mods = tie(recv_patches, mods)
+    ada_kinds = ada_weight.swapaxes(0, 1)
+    modulation = modulate(jnp.pad(silu_cond, ((0, -own % 16), (0, 0))), ada_kinds)[:, :own]
+    mods = jnp.concatenate(
+        [
+            modulation.swapaxes(0, 1),
+            jnp.broadcast_to(weights[:, None, None], (own, 1, model_width)),
+            jnp.zeros((own, 1, model_width), f32),
+        ],
+        axis=1,
+    )
+    if by_permutes:
+        recv_patches, mods, far_near = tie(recv_patches, mods, far_near)
+    else:
+        recv_patches, mods = tie(recv_patches, mods)
 
     rank_ids = jnp.arange(images) * dp_size + my_place
     source = jnp.sum((finish[None, :] <= rank_ids[:, None]).astype(jnp.int32), axis=1)
@@ -870,8 +860,8 @@
         orders = ((2, 4), (4, 2))
         got = [swap(halves[half], "dp", orders[half][0]) for half in range(2)]
         latent, got[0], got[1] = tie(latent, got[0], got[1])
-        halves = [jnp.stack([halves[half], got[half]]) for half in range(2)]
-        got = [swap(halves[half], "dp", orders[half][1]) for half in range(2)]
+        firsts = [(halves[half], got[half]) for half in range(2)]
+        got = [swap(jnp.stack(firsts[half]), "dp", orders[half][1]) for half in range(2)]
 
     proj, attended, branch_one, normed_t, middle, two, two_t = attend(
         latent, mods, attend_full, gains_f, tables
@@ -879,10 +869,11 @@
     cotangent, attended = tie(cotangent, attended)
     cot = turn(cotangent.reshape(mp_size, own, local_len, model_width))
     if by_permutes:
+        got[0], got[1], attended = tie(got[0], got[1], attended)
         mlp_pieces, mlp_order = [], []
         for half in range(2):
             first, second = orders[half]
-            parts = {0: halves[half][0], first: halves[half][1]}
+            parts = {0: firsts[half][0], first: firsts[half][1]}
             parts.update({second: got[half][0], first ^ second: got[half][1]})
             for near, part in parts.items():
                 mlp_pieces += [part, swap(part, "dp", 1)]
@@ -951,29 +942,18 @@
 
     attend_one, attend_got_one = grads_of(1)
     attend_zero, attend_got_zero = grads_of(0)
-    attend_zero, attend_got_one, got_one, got_zero = tie(
-        attend_zero, attend_got_one, got_one, got_zero
-    )
     mlp_one = halve(add_low(kept_one, got_one), "dp", dp_bits[1][3:], 2)
     mlp_zero = halve(add_low(kept_zero, got_zero), "dp", dp_bits[0][3:], 2)
-    mlp_got = swap(mlp_one, "mp", mp_bits[0])
-    attend_one, sent_one = split(add_low(attend_one, attend_got_one), 1)
-    attend_zero, sent_zero = split(add_low(attend_zero, attend_got_zero), 1)
+    attend_one = add_low(attend_one, attend_got_one)
+    attend_zero = add_low(attend_zero, attend_got_zero)
+    latent_back, attend_one, attend_zero, mlp_one, mlp_zero = tie(
+        latent_back, attend_one, attend_zero, mlp_one, mlp_zero
+    )
+    attend_one, sent_one = split(attend_one, 1)
+    attend_zero, sent_zero = split(attend_zero, 1)
     attend_got_one = swap(sent_one, "dp", dp_bits[1][1])
     attend_got_zero = swap(sent_zero, "dp", dp_bits[0][1])
-
-    packed = sums_finish + sums_middle + sums_entry
-    gains_row = jnp.pad(gains_grad.reshape(1, 1, -1), ((0, own - 1), (7, 0), (0, model_width - 2 * head_dim)))
-    packed = jnp.where(jnp.arange(8)[:, None] == 7, gains_row, packed).astype(bf16)
-    packed = xor_gather(packed, gather_bits)[0]
-    latent_back, attend_got_one, attend_got_zero, mlp_got = tie(
-        latent_back, attend_got_one, attend_got_zero, mlp_got
-    )
-    attend_one = halve(add_low(attend_one, attend_got_one), "dp", dp_bits[1][2:], 1)
-    attend_zero = halve(add_low(attend_zero, attend_got_zero), "dp", dp_bits[0][2:], 1)
-    mlp_grad = halve(add_low(mlp_zero, mlp_got), "mp", mp_bits[1:], 0)[0].astype(f32)
-    attend_grad = add_low(attend_zero, swap(attend_one, "mp", mp_bits[0]))
-    attend_grad = halve(attend_grad, "mp", mp_bits[1:], 0)[0].astype(f32)
+    mlp_got = swap(mlp_one, "mp", mp_bits[0])
 
     back_within = pair_slot * dp_size + jnp.mod(my_place - starts[pair_peer], dp_size)
     back_valid = back_within < image_counts[pair_peer]
@@ -983,6 +963,12 @@
     latent_back = latent_back.reshape(images, local_len, model_width)
     latent_back = jnp.concatenate([latent_back, empty], axis=0)
     back_patches = take_rows(latent_back, back_slot)
+
+    packed = sums_finish + sums_middle + sums_entry
+    gains_row = jnp.pad(gains_grad.reshape(1, 1, -1), ((0, own - 1), (7, 0), (0, model_width - 2 * head_dim)))
+    packed = jnp.where(jnp.arange(8)[:, None] == 7, gains_row, packed).astype(bf16)
+    packed, back_patches = tie(packed, back_patches)
+    packed = xor_gather(packed, gather_bits)[0]
     got_patches = lax.all_to_all(back_patches, "dp", split_axis=0, concat_axis=0, tiled=True)
     slot_ids = jnp.arange(capacity)
     home_peer = dest_perm[jnp.mod(my_start + slot_ids, dp_size)]
@@ -1002,13 +988,19 @@
     silu_rows = lax.dynamic_slice_in_dim(silu_all, row0, width_dp, 1)
     mod_cols = lax.dynamic_slice_in_dim(mod_all, mp_index * width_mp, width_mp, 2)
     ada_grad = ein("id,ikc->dkc", silu_rows, mod_cols)
-    ada_rows = lax.dynamic_slice_in_dim(ada_weight, row0, width_dp, 0)
-    silu_grad = ein("ikc,dkc->id", mod_all, ada_rows)
+    ada_rows = lax.dynamic_slice_in_dim(ada_kinds, row0, width_dp, 1)
+    silu_grad = ein("ikc,kdc->id", mod_all, ada_rows)
     cond_rows = lax.dynamic_slice_in_dim(cond_all, row0, width_dp, 1)
     silu_val, silu_pull = jax.vjp(jax.nn.silu, cond_rows)
     condition_low = silu_pull(silu_grad)[0].astype(bf16)
     time_grad = ein("in,id->nd", bin_hot, condition_low)
     class_grad = ein("in,id->nd", label_hot, condition_low)
+
+    attend_one = halve(add_low(attend_one, attend_got_one), "dp", dp_bits[1][2:], 1)
+    attend_zero = halve(add_low(attend_zero, attend_got_zero), "dp", dp_bits[0][2:], 1)
+    mlp_grad = halve(add_low(mlp_zero, mlp_got), "mp", mp_bits[1:], 0)[0].astype(f32)
+    attend_grad = add_low(attend_zero, swap(attend_one, "mp", mp_bits[0]))
+    attend_grad = halve(attend_grad, "mp", mp_bits[1:], 0)[0].astype(f32)
 
     expand_grad = mlp_grad[:2].swapaxes(0, 1)
     down_grad = mlp_grad[2].T

time: 849 us -> 826 us (0.973)
  local copies, waits for them, and re-layouts: 120 us -> 83.6 us
  waiting for transfers between devices: 313 us -> 347 us
  Pallas kernels: 253 us -> 238 us
    unnamed x127 -> x107, local copies, waits for them, and re-layouts: 72.4 us -> 25.5 us
    ppermute x38, waiting for transfers between devices: 263 us -> 285 us  [swap(): return lax.ppermute(values, axis, [(i, i ^ bit) for i in range(size)])]
    pallas_call x1, Pallas kernels: 17.6 us -> 2.82 us  [modulate(): pl.pallas_call(modulate_kernel, grid=(kinds,), in_specs=[pl.BlockSpec(sil...]
    all_to_all x4, waiting for transfers between devices: 49.8 us -> 62.2 us  [turn(): return lax.all_to_all(chunks, 'mp', split_axis=0, concat_axis=0, tiled=True)]
    all_to_all x4, starting transfers between devices: 29.1 us -> 19.2 us  [turn(): return lax.all_to_all(chunks, 'mp', split_axis=0, concat_axis=0, tiled=True)]
    convert_element_type x12 -> x13, other arithmetic: 31.3 us -> 38.1 us  [add_low(): return (kept.astype(f32) + received.astype(f32)).astype(bf16)]
  transfers between devices with their start and end apart: 45 -> 45, of which waited for: 15 -> 18; matrix products, arithmetic and copies ran while one was open for 19% -> 14% of each run, Pallas kernels for 25% -> 24%
where the time goes in v7:
time: 826 us; the launch traced here: 820 us
  waiting for transfers between devices  347 us (42%)
  Pallas kernels  238 us (29%)
  local copies, waits for them, and re-layouts  83.6 us (10%)
  starting transfers between devices  61.3 us (7%)
  other arithmetic  60.4 us (7%)
  between operations  15.2 us (2%)
  matrix products  14.5 us (2%)
    ppermute x38, waiting for transfers between devices, swap(): return lax.ppermute(values, axis, [(i, i ^ bit) for i in range(size)])  285 us
    pallas_call x2, Pallas kernels, mlp_back(): pl.pallas_call(mlp_back_kernel, grid_spec=pltpu.PrefetchScalarGridSpec(nu...  72.3 us
    all_to_all x4, waiting for transfers between devices, turn(): return lax.all_to_all(chunks, 'mp', split_axis=0, concat_axis=0, tiled=True)  62.2 us
    pallas_call x1, Pallas kernels, attend_back(): pl.pallas_call(attend_back_kernel, grid=(groups,), in_specs=[whole_spec(l...  45 us
    convert_element_type x13, other arithmetic, add_low(): return (kept.astype(f32) + received.astype(f32)).astype(bf16)  38.1 us
    pallas_call x1, Pallas kernels, mlp(): pl.pallas_call(functools.partial(mlp_kernel, len(pieces)), grid_spec=pltp...  38 us
    pallas_call x1, Pallas kernels, attend(): pl.pallas_call(attend_kernel, grid=(groups,), in_specs=[whole_spec(latent...  36 us
    ppermute x38, starting transfers between devices, swap(): return lax.ppermute(values, axis, [(i, i ^ bit) for i in range(size)])  32.5 us
  transfers between devices with their start and end apart: 45, of which 18 were waited for; matrix products, arithmetic and copies ran while one was open for 14% of the time, Pallas kernels for 24%

profile of v7, /device:TPU:0, one launch (start us, length us, event | category | flops | bytes accessed | tf_op | source)
XLA Modules:
  0.0 819.7 jit_solution(18024066373571059536)
XLA Ops:
  15.3 2.6 collective-permute-start.1
  19.4 2.0 collective-permute-start.2
  22.3 5.6 gather_fusion.1
  30.8 2.5 copy.73
  35.7 2.6 collective-permute-start.3
  39.1 3.1 multiply_convert_fusion
  42.9 4.6 all-to-all-start
  47.8 26.2 %collective-permute-done.3 = bf16[1,3,96,1152]{3,2,1,0:T(8,128)(2,1)S(1)} collective-permute-done((bf16[1,3,96,1152]{3,2,1,0:T(8,128)(2,1)S(1)}, bf16[1,3,96,1152]{3,2,1,0:T(8,128)(2,1)S(1)}, u32[]{:S(2)}, u32[]{:S(2)}) %collective-permute-start.3) | collective-permute-done | bytes 663584 | tf_op jit(solution)/shard_map/ppermute | solution.py:652
  74.8 5.5 copy-done.4
  80.3 2.8 modulate.1
  84.1 34.3 %collective-permute-done.4 = bf16[2,3,96,1152]{3,2,1,0:T(8,128)(2,1)S(1)} collective-permute-done((bf16[2,3,96,1152]{3,2,1,0:T(8,128)(2,1)S(1)}, bf16[2,3,96,1152]{3,2,1,0:T(8,128)(2,1)S(1)}, u32[]{:S(2)}, u32[]{:S(2)}) %collective-permute-start.4) | collective-permute-done | bytes 1327136 | tf_op jit(solution)/shard_map/ppermute | solution.py:652
  118.3 5.7 gather_fusion.3
  124.0 5.2 all-to-all-start.1
  129.6 1.9 slice_bitcast_fusion.10
  138.6 29.8 %collective-permute-done.5.refs_2_ = bf16[4,3,48,1152]{3,2,1,0:T(8,128)(2,1)} collective-permute-done((bf16[4,3,48,1152]{3,2,1,0:T(8,128)(2,1)}, bf16[4,3,48,1152]{3,2,1,0:T(8,128)(2,1)}, u32[]{:S(2)}, u32[]{:S(2)}) %collective-permute-start.5) | collective-permute-done | bytes 1327136 | tf_op jit(solution)/shard_map/ppermute | solution.py:652
  168.4 32.5 %all-to-all-done.1.latent_ref = bf16[4,4,64,1152]{3,2,1,0:T(8,128)(2,1)} async-done(((bf16[4,4,64,1152]{3,2,1,0:T(8,128)(2,1)}), bf16[4,4,64,1152]{3,2,1,0:T(8,128)(2,1)}, u32[]{:S(2)}, u32[]{:S(2)}) %all-to-all-start.1) | async-done | bytes 2359328 | tf_op jit(solution)/shard_map/all_to_all | solution.py:739
  201.0 3.2 pad_maximum_fusion.2
  205.6 3.1 pad_maximum_fusion.1
  210.1 36.0 %attend.1 = (f32[4,864,1024]{2,1,0:T(8,128)}, bf16[4,288,1024]{2,1,0:T(8,128)(2,1)}, bf16[1024,1152]{1,0:T(8,128)(2,1)}, bf16[1152,1024]{1,0:T(8,128)(2,1)}, f32...) custom-call(bf16[4,4,64,1152]{3,2,1,0:T(8,128)(2,1)} %all-to-all-done.1.latent_ref, ...), custom_call_target="tpu_custom_call" | custom-call | flops 176000008192 | bytes 1048576 | tf_op jit(solution)/shard_map/attend/pallas_call | solution.py:286
  246.1 18.3 %collective-permute-done.10 = bf16[2,4,3,48,1152]{4,3,2,1,0:T(8,128)(2,1)} collective-permute-done((bf16[2,4,3,48,1152]{4,3,2,1,0:T(8,128)(2,1)}, bf16[2,4,3,48,1152]{4,3,2,1,0:T(8,128)(2,1)}, u32[]{:S(2)}, u32[]{:S(2)}) %collective-permute-start.10) | collective-permute-done | bytes 2654240 | tf_op jit(solution)/shard_map/ppermute | solution.py:652
  264.4 4.3 collective-permute-done.9
  268.7 1.9 slice_bitcast_fusion.6
  270.7 4.5 slice_bitcast_fusion.4
  277.1 4.7 all-to-all-start.2
  282.5 38.0 %mlp.1 = (bf16[4,2,1024,768]{3,2,1,0:T(8,128)(2,1)}, f32[1024,1152]{1,0:T(8,128)}, bf16[4,3,768,1152]{3,2,1,0:T(8,128)(2,1)}) custom-call(s32[16]{0:T(128)} %stack.119.e_ref, bf16[1024,1152]{1,0:T(8,128)(2,1)} %get-tuple-element.89.x_ref, bf16[4,3,48,1152]{3,2,1,0:T(8,128)(2,1)} %get-tuple-element.193.refs_0_, ...), custom_call_target="tpu_custom_call" | custom-call | flops 131999997952 | bytes 1048576 | tf_op jit(solution)/shard_map/mlp/pallas_call | solution.py:479
  320.4 16.1 %all-to-all-done.2.cot_ref = bf16[4,4,64,1152]{3,2,1,0:T(8,128)(2,1)} async-done(((bf16[4,4,64,1152]{3,2,1,0:T(8,128)(2,1)}), bf16[4,4,64,1152]{3,2,1,0:T(8,128)(2,1)}, u32[]{:S(2)}, u32[]{:S(2)}) %all-to-all-start.2) | async-done | bytes 2359328 | tf_op jit(solution)/shard_map/all_to_all | solution.py:739
  336.6 6.8 finish.1
  346.1 36.2 %mlp_back.3 = (bf16[2,3,576,768]{3,2,1,0:T(8,128)(2,1)}, bf16[2,3,576,768]{3,2,1,0:T(8,128)(2,1)}, f32[1024,1152]{1,0:T(8,128)}) custom-call(s32[8]{0:T(128)} %get-tuple-element.216.e_ref, bf16[8,144,1024]{2,1,0:T(8,128)(2,1)} %bitcast.185, bf16[8,144,1024]{2,1,0:T(8,128)(2,1)} %bitcast.164, bf16[1024,1152]{1,0:T(8,128)(2,1)} %copy-done.8, ...), custom_call_target="tpu_custom_call" | custom-call | flops 165000003584 | bytes 1048576 | tf_op jit(solution)/shard_map/mlp_back/pallas_call | solution.py:555
  382.4 4.7 all-to-all-start.3
  387.1 36.1 %mlp_back.2 = (bf16[2,3,576,768]{3,2,1,0:T(8,128)(2,1)}, bf16[2,3,576,768]{3,2,1,0:T(8,128)(2,1)}, f32[1024,1152]{1,0:T(8,128)}) custom-call(s32[8]{0:T(128)} %get-tuple-element.217.e_ref, bf16[8,144,1024]{2,1,0:T(8,128)(2,1)} %bitcast.186, bf16[8,144,1024]{2,1,0:T(8,128)(2,1)} %bitcast.165, bf16[1024,1152]{1,0:T(8,128)(2,1)} %copy-done.8, ...), custom_call_target="tpu_custom_call" | custom-call | flops 165000003584 | bytes 1048576 | tf_op jit(solution)/shard_map/mlp_back/pallas_call | solution.py:555
  428.3 13.6 %all-to-all-done.3 = bf16[4,4,64,1152]{3,2,1,0:T(8,128)(2,1)} async-done(((bf16[4,4,64,1152]{3,2,1,0:T(8,128)(2,1)}), bf16[4,4,64,1152]{3,2,1,0:T(8,128)(2,1)}, u32[]{:S(2)}, u32[]{:S(2)}) %all-to-all-start.3) | async-done | bytes 2359328 | tf_op jit(solution)/shard_map/all_to_all | solution.py:739
  441.9 10.3 %middle.1 = (f32[1024,1152]{1,0:T(8,128)}, bf16[1024,1152]{1,0:T(8,128)(2,1)S(1)}, bf16[1152,1024]{1,0:T(8,128)(2,1)S(1)}, f32[4,8,1152]{2,1,0:T(8,128)S(1)}) custom-call(f32[1024,1152]{1,0:T(8,128)} %get-tuple-element.108.one_ref, f32[1024,1152]{1,0:T(8,128)} %get-tuple-element.109.other_ref, f32[1024,1152]{1,0:T(8,128)} %get-tuple-element.97.middle_ref, ...), custom_call_target="tpu_custom_call" | custom-call | flops 32999999488 | bytes 1048576 | tf_op jit(solution)/shard_map/middle/pallas_call | solution.py:409
  453.5 6.2 add_convert_fusion
  459.7 1.8 slice.227
  463.5 5.3 add_convert_fusion.1
  473.5 45.0 %attend_back.1 = (bf16[4,864,1024]{2,1,0:T(8,128)(2,1)}, f32[2,72,256]{2,1,0:T(8,128)}, f32[4,8,1152]{2,1,0:T(8,128)}, bf16[4,4,64,1152]{3,2,1,0:T(8,128)(2,1)}) custom-call(bf16[4,4,64,1152]{3,2,1,0:T(8,128)(2,1)} %all-to-all-done.1.latent_ref, f32[4,864,1024]{2,1,0:T(8,128)} %get-tuple-element.107.proj_ref, bf16[1024,1152]{1,0:T(8,128)(2,1)} %copy-done.7, ...), custom_call_target="tpu_custom_call" | custom-call | flops 176000008192 | bytes 1048576 | tf_op jit(solution)/shard_map/attend_back/pallas_call | solution.py:330
  518.5 4.7 all-to-all-start.4
  523.2 8.1 collective-permute-done.19
  531.3 3.2 add_convert_fusion.2
  538.5 13.1 %attend_grads.3 = (bf16[2,576,1152]{2,1,0:T(8,128)(2,1)}, bf16[2,576,1152]{2,1,0:T(8,128)(2,1)}) custom-call(s32[2]{0:T(128)} %get-tuple-element.212.m_ref, s32[8]{0:T(128)} %get-tuple-element.217.e_ref, bf16[8,144,1024]{2,1,0:T(8,128)(2,1)} %bitcast.183, bf16[8,144,1024]{2,1,0:T(8,128)(2,1)} %bitcast.162, ...), custom_call_target="tpu_custom_call" | custom-call | flops 5500000256 | bytes 1048576 | tf_op jit(solution)/shard_map/attend_grads/pallas_call | solution.py:605
  551.7 13.6 %attend_grads.2 = (bf16[2,576,1152]{2,1,0:T(8,128)(2,1)}, bf16[2,576,1152]{2,1,0:T(8,128)(2,1)}) custom-call(s32[2]{0:T(128)} %get-tuple-element.213.m_ref, s32[8]{0:T(128)} %get-tuple-element.216.e_ref, bf16[8,144,1024]{2,1,0:T(8,128)(2,1)} %bitcast.184, bf16[8,144,1024]{2,1,0:T(8,128)(2,1)} %bitcast.163, ...), custom_call_target="tpu_custom_call" | custom-call | flops 219999993856 | bytes 1048576 | tf_op jit(solution)/shard_map/attend_grads/pallas_call | solution.py:605
  565.8 2.6 add_convert_fusion.3
  572.1 2.2 add_convert_fusion.9
  574.3 27.0 %collective-permute-done.23 = bf16[2,3,144,768]{3,2,1,0:T(8,128)(2,1)} collective-permute-done((bf16[2,3,144,768]{3,2,1,0:T(8,128)(2,1)S(1)}, bf16[2,3,144,768]{3,2,1,0:T(8,128)(2,1)}, u32[]{:S(2)}, u32[]{:S(2)}) %collective-permute-start.23) | collective-permute-done | bytes 1327136 | tf_op jit(solution)/shard_map/ppermute | solution.py:652
  601.3 2.7 add_convert_fusion.10
  604.0 4.1 add_convert_fusion.4
  608.1 4.0 add_convert_fusion.5
  612.1 3.4 concatenate.61
  615.6 5.1 gather_fusion.7
  621.4 4.5 collective-permute-done.25
  626.0 2.1 collective-permute-start.36
  628.1 4.7 collective-permute-done.26
  637.7 2.5 slice.181
  641.7 4.8 all-to-all-start.5
  646.6 2.0 collective-permute-start.28
  650.9 75.4 %collective-permute-done.28 = bf16[8,4,8,1152]{3,2,1,0:T(8,128)(2,1)S(1)} collective-permute-done((bf16[8,4,8,1152]{3,2,1,0:T(8,128)(2,1)S(1)}, bf16[8,4,8,1152]{3,2,1,0:T(8,128)(2,1)S(1)}, u32[]{:S(2)}, u32[]{:S(2)}) %collective-permute-start.28) | collective-permute-done | bytes 589856 | tf_op jit(solution)/shard_map/ppermute | solution.py:652
  727.4 1.8 add_convert_fusion.6
  737.0 24.5 %collective-permute-done.37 = bf16[1,3,144,768]{3,2,1,0:T(8,128)(2,1)S(1)} collective-permute-done((bf16[1,3,144,768]{3,2,1,0:T(8,128)(2,1)S(1)}, bf16[1,3,144,768]{3,2,1,0:T(8,128)(2,1)S(1)}, u32[]{:S(2)}, u32[]{:S(2)}) %collective-permute-start.37) | collective-permute-done | bytes 663584 | tf_op jit(solution)/shard_map/ppermute | solution.py:652
  765.6 2.4 fusion.12
  768.1 2.2 fusion.28
  771.1 10.3 %collective-permute-done.34 = bf16[2,144,1152]{2,1,0:T(8,128)(2,1)} collective-permute-done((bf16[2,144,1152]{2,1,0:T(8,128)(2,1)}, bf16[2,144,1152]{2,1,0:T(8,128)(2,1)}, u32[]{:S(2)}, u32[]{:S(2)}) %collective-permute-start.34) | collective-permute-done | bytes 663584 | tf_op jit(solution)/shard_map/ppermute | solution.py:652
  785.0 15.0 %collective-permute-done.35 = bf16[1,144,1152]{2,1,0:T(8,128)(2,1)S(1)} collective-permute-done((bf16[1,144,1152]{2,1,0:T(8,128)(2,1)S(1)}, bf16[1,144,1152]{2,1,0:T(8,128)(2,1)S(1)}, u32[]{:S(2)}, u32[]{:S(2)}) %collective-permute-start.35) | collective-permute-done | bytes 331808 | tf_op jit(solution)/shard_map/ppermute | solution.py:652
  803.7 5.7 gather_fusion.9
  809.4 3.3 copy.111
  (298 shorter events, 86.5 us)
Async XLA Ops:
  7.2 21.2 %copy-start = (bf16[1152,3,288]{0,2,1:T(8,128)(2,1)S(1)}, bf16[1152,3,288]{0,2,1:T(8,128)(2,1)}, u32[]{:S(2)}) copy-start(bf16[1152,3,288]{0,2,1:T(8,128)(2,1)} %param.36) | copy-start | bytes 5971972
  7.2 202.9 %all-gather.3.cloned.1.call-start = ((), (), s32[]{:S(2)}) async-start(), calls=%async_computation.6 | async-start | bytes 10948608 | tf_op jit(solution)/shard_map/all_gather | solution.py:638
  8.1 7.2 collective-permute-start
  12.0 18.8 %copy-start.9 = (s32[8]{0:T(128)}, s32[8]{0:T(128)S(1)}, u32[]{:S(2)}) copy-start(s32[8]{0:T(128)S(1)} %bitcast_subtract_fusion.2) | copy-start | bytes 100
  14.0 8.3 %copy-start.33 = (s32[1024]{0:T(1024)}, s32[1024]{0:T(1024)S(1)}, u32[]{:S(2)}) copy-start(s32[1024]{0:T(1024)S(1)} %pad_clamp_fusion.7) | copy-start | bytes 12292
  15.3 4.1 collective-permute-start.1
  19.4 8.5 %collective-permute-start.2 = (s32[4,2,32]{2,1,0:T(2,128)S(1)}, s32[4,2,32]{2,1,0:T(2,128)S(1)}, u32[]{:S(2)}, u32[]{:S(2)}) collective-permute-start(s32[4,2,32]{2,1,0:T(2,128)S(1)} %pad_add_fusion.1), channel_id=1, source_target_pairs={{0,16},{4,20},{8,24},{12,28},{16,0},{20,4},{24,8},{28,12},{1,17},{... | collective-permute-start | bytes 3080 | tf_op jit(solution)/shard_map/ppermute | solution.py:652
  35.7 38.2 %collective-permute-start.3 = (bf16[1,3,96,1152]{3,2,1,0:T(8,128)(2,1)S(1)}, bf16[1,3,96,1152]{3,2,1,0:T(8,128)(2,1)S(1)}, u32[]{:S(2)}, u32[]{:S(2)}) collective-permute-start(bf16[1,3,96,1152]{3,2,1,0:T(8,128)(2,1)S(1)} %maximum_bitcast_fusion), channel_id=1, source_target_pairs={{0,2},{1,3},{2,0},{3,1},{4,6},{5,7},{6,4},{7,5},{8,10},{9,11},{10,... | collective-permute-start | bytes 1990664 | tf_op jit(solution)/shard_map/ppermute | solution.py:652
  38.8 8.9 %copy-start.34 = (s32[128]{0:T(128)}, s32[128]{0:T(128)S(1)}, u32[]{:S(2)}) copy-start(s32[128]{0:T(128)S(1)} %get-tuple-element.185) | copy-start | bytes 1540
  42.9 75.4 %all-to-all-start = ((bf16[32,64,1152]{2,1,0:T(8,128)(2,1)}), bf16[32,64,1152]{2,1,0:T(8,128)(2,1)}, u32[]{:S(2)}, u32[]{:S(2)}) async-start(bf16[32,64,1152]{2,1,0:T(8,128)(2,1)} %gather_fusion.1), calls=%async_computation | async-start | bytes 9437184 | tf_op jit(solution)/shard_map/all_to_all | solution.py:788
  74.1 44.2 %collective-permute-start.4 = (bf16[2,3,96,1152]{3,2,1,0:T(8,128)(2,1)S(1)}, bf16[2,3,96,1152]{3,2,1,0:T(8,128)(2,1)S(1)}, u32[]{:S(2)}, u32[]{:S(2)}) collective-permute-start(bf16[2,3,96,1152]{3,2,1,0:T(8,128)(2,1)S(1)} %pad_maximum_fusion.3), channel_id=1, source_target_pairs={{0,1},{1,0},{2,3},{3,2},{4,5},{5,4},{6,7},{7,6},{8,9},{9,8},{10,11... | collective-permute-start | bytes 3981320 | tf_op jit(solution)/shard_map/ppermute | solution.py:652
  124.0 76.9 %all-to-all-start.1 = ((bf16[4,4,64,1152]{3,2,1,0:T(8,128)(2,1)}), bf16[4,4,64,1152]{3,2,1,0:T(8,128)(2,1)}, u32[]{:S(2)}, u32[]{:S(2)}) async-start(bf16[4,4,64,1152]{3,2,1,0:T(8,128)(2,1)} %bitcast.167), calls=%async_computation.1 | async-start | bytes 4718592 | tf_op jit(solution)/shard_map/all_to_all | solution.py:739
  129.6 7.8 copy-start.36
  131.5 36.9 %collective-permute-start.5 = (bf16[4,3,48,1152]{3,2,1,0:T(8,128)(2,1)}, bf16[4,3,48,1152]{3,2,1,0:T(8,128)(2,1)}, u32[]{:S(2)}, u32[]{:S(2)}) collective-permute-start(bf16[4,3,48,1152]{3,2,1,0:T(8,128)(2,1)} %get-tuple-element.193.refs_0_), channel_id=1, source_target_pairs={{0,8},{4,12},{8,0},{12,4},{16,24},{20,28},{24,16},{28,20},{1,9},{5... | collective-permute-start | bytes 3981320 | tf_op jit(solution)/shard_map/ppermute | solution.py:652
  133.0 35.5 %collective-permute-start.6 = (bf16[4,3,48,1152]{3,2,1,0:T(8,128)(2,1)}, bf16[4,3,48,1152]{3,2,1,0:T(8,128)(2,1)}, u32[]{:S(2)}, u32[]{:S(2)}) collective-permute-start(bf16[4,3,48,1152]{3,2,1,0:T(8,128)(2,1)} %get-tuple-element.192.refs_8_), channel_id=1, source_target_pairs={{0,16},{4,20},{8,24},{12,28},{16,0},{20,4},{24,8},{28,12},{1,17},{... | collective-permute-start | bytes 3981320 | tf_op jit(solution)/shard_map/ppermute | solution.py:652
  138.1 137.1 %collective-permute-start.13 = (bf16[4,3,48,1152]{3,2,1,0:T(8,128)(2,1)}, bf16[4,3,48,1152]{3,2,1,0:T(8,128)(2,1)}, u32[]{:S(2)}, u32[]{:S(2)}) collective-permute-start(bf16[4,3,48,1152]{3,2,1,0:T(8,128)(2,1)} %get-tuple-element.192.refs_8_), channel_id=1, source_target_pairs={{0,4},{4,0},{8,12},{12,8},{16,20},{20,16},{24,28},{28,24},{1,5},{5... | collective-permute-start | bytes 3981320 | tf_op jit(solution)/shard_map/ppermute | solution.py:652
  138.1 137.2 %collective-permute-start.7 = (bf16[4,3,48,1152]{3,2,1,0:T(8,128)(2,1)}, bf16[4,3,48,1152]{3,2,1,0:T(8,128)(2,1)}, u32[]{:S(2)}, u32[]{:S(2)}) collective-permute-start(bf16[4,3,48,1152]{3,2,1,0:T(8,128)(2,1)} %get-tuple-element.193.refs_0_), channel_id=1, source_target_pairs={{0,4},{4,0},{8,12},{12,8},{16,20},{20,16},{24,28},{28,24},{1,5},{5... | collective-permute-start | bytes 3981320 | tf_op jit(solution)/shard_map/ppermute | solution.py:652
  200.9 74.8 %collective-permute-start.14 = (bf16[4,3,48,1152]{3,2,1,0:T(8,128)(2,1)}, bf16[4,3,48,1152]{3,2,1,0:T(8,128)(2,1)}, u32[]{:S(2)}, u32[]{:S(2)}) collective-permute-start(bf16[4,3,48,1152]{3,2,1,0:T(8,128)(2,1)} %collective-permute-done.6.refs_10_), channel_id=1, source_target_pairs={{0,4},{4,0},{8,12},{12,8},{16,20},{20,16},{24,28},{28,24},{1,5},{5... | collective-permute-start | bytes 3981320 | tf_op jit(solution)/shard_map/ppermute | solution.py:652
  204.1 60.3 %collective-permute-start.10 = (bf16[2,4,3,48,1152]{4,3,2,1,0:T(8,128)(2,1)}, bf16[2,4,3,48,1152]{4,3,2,1,0:T(8,128)(2,1)}, u32[]{:S(2)}, u32[]{:S(2)}) collective-permute-start(bf16[2,4,3,48,1152]{4,3,2,1,0:T(8,128)(2,1)} %pad_maximum_fusion.2), channel_id=1, source_target_pairs={{0,8},{4,12},{8,0},{12,4},{16,24},{20,28},{24,16},{28,20},{1,9},{5... | collective-permute-start | bytes 7962632 | tf_op jit(solution)/shard_map/ppermute | solution.py:652
  208.7 60.0 %collective-permute-start.9 = (bf16[2,4,3,48,1152]{4,3,2,1,0:T(8,128)(2,1)}, bf16[2,4,3,48,1152]{4,3,2,1,0:T(8,128)(2,1)}, u32[]{:S(2)}, u32[]{:S(2)}) collective-permute-start(bf16[2,4,3,48,1152]{4,3,2,1,0:T(8,128)(2,1)} %pad_maximum_fusion.1), channel_id=1, source_target_pairs={{0,16},{4,20},{8,24},{12,28},{16,0},{20,4},{24,8},{28,12},{1,17},{... | collective-permute-start | bytes 7962632 | tf_op jit(solution)/shard_map/ppermute | solution.py:652
  264.4 17.4 %collective-permute-start.8 = (bf16[4,3,48,1152]{3,2,1,0:T(8,128)(2,1)}, bf16[4,3,48,1152]{3,2,1,0:T(8,128)(2,1)}, u32[]{:S(2)}, u32[]{:S(2)}) collective-permute-start(bf16[4,3,48,1152]{3,2,1,0:T(8,128)(2,1)} %collective-permute-done.5.refs_2_), channel_id=1, source_target_pairs={{0,4},{4,0},{8,12},{12,8},{16,20},{20,16},{24,28},{28,24},{1,5},{5... | collective-permute-start | bytes 3981320 | tf_op jit(solution)/shard_map/ppermute | solution.py:652
  270.6 5.9 copy-start.44
  270.6 5.9 copy-start.45
  270.6 11.2 %collective-permute-start.11 = (bf16[4,3,48,1152]{3,2,1,0:T(8,128)(2,1)S(1)}, bf16[4,3,48,1152]{3,2,1,0:T(8,128)(2,1)}, u32[]{:S(2)}, u32[]{:S(2)}) collective-permute-start(bf16[4,3,48,1152]{3,2,1,0:T(8,128)(2,1)S(1)} %get-tuple-element.189.refs_4_), channel_id=1, source_target_pairs={{0,4},{4,0},{8,12},{12,8},{16,20},{20,16},{24,28},{28,24},{1,5},{5... | collective-permute-start | bytes 3981320 | tf_op jit(solution)/shard_map/ppermute | solution.py:652
  275.2 6.6 collective-permute-start.12
  275.3 6.6 collective-permute-start.15
  275.8 6.7 collective-permute-start.16
  277.1 59.5 %all-to-all-start.2 = ((bf16[4,4,64,1152]{3,2,1,0:T(8,128)(2,1)}), bf16[4,4,64,1152]{3,2,1,0:T(8,128)(2,1)}, u32[]{:S(2)}, u32[]{:S(2)}) async-start(bf16[4,4,64,1152]{3,2,1,0:T(8,128)(2,1)} %bitcast.169), calls=%async_computation.2 | async-start | bytes 4718592 | tf_op jit(solution)/shard_map/all_to_all | solution.py:739
  282.5 54.1 %copy-start.2 = (f32[4,8,1152]{2,1,0:T(8,128)S(1)}, f32[4,8,1152]{2,1,0:T(8,128)}, u32[]{:S(2)}) copy-start(f32[4,8,1152]{2,1,0:T(8,128)} %maximum_maximum_fusion.mods_ref) | copy-start | bytes 442372
  382.3 59.5 %collective-permute-start.17 = (bf16[2,3,576,768]{3,2,1,0:T(8,128)(2,1)}, bf16[2,3,576,768]{3,2,1,0:T(8,128)(2,1)}, u32[]{:S(2)}, u32[]{:S(2)}) collective-permute-start(bf16[2,3,576,768]{3,2,1,0:T(8,128)(2,1)} %get-tuple-element.104), channel_id=1, source_target_pairs={{0,4},{4,0},{8,12},{12,8},{16,20},{20,16},{24,28},{28,24},{1,5},{5... | collective-permute-start | bytes 15925256 | tf_op jit(solution)/shard_map/ppermute | solution.py:652
  382.4 59.5 %all-to-all-start.3 = ((bf16[4,4,64,1152]{3,2,1,0:T(8,128)(2,1)}), bf16[4,4,64,1152]{3,2,1,0:T(8,128)(2,1)}, u32[]{:S(2)}, u32[]{:S(2)}) async-start(bf16[4,4,64,1152]{3,2,1,0:T(8,128)(2,1)} %get-tuple-element.105), calls=%async_computation.3 | async-start | bytes 4718592 | tf_op jit(solution)/shard_map/all_to_all | solution.py:739
  387.1 36.7 %copy-start.10 = (s32[8]{0:T(128)S(1)}, s32[8]{0:T(128)}, u32[]{:S(2)}) copy-start(s32[8]{0:T(128)} %copy-done.9) | copy-start | bytes 100
  387.1 37.5 %copy-start.12 = (s32[8]{0:T(128)S(1)}, s32[8]{0:T(128)}, u32[]{:S(2)}) copy-start(s32[8]{0:T(128)} %param.31) | copy-start | bytes 100
  387.1 40.6 %copy-start.46 = (s32[4]{0:T(128)S(1)}, s32[4]{0:T(128)}, u32[]{:S(2)}) copy-start(s32[4]{0:T(128)} %constant.208.clone) | copy-start | bytes 52
  387.1 54.8 %copy-start.3 = (f32[4,8,1152]{2,1,0:T(8,128)S(1)}, f32[4,8,1152]{2,1,0:T(8,128)}, u32[]{:S(2)}) copy-start(f32[4,8,1152]{2,1,0:T(8,128)} %maximum_maximum_fusion.mods_ref) | copy-start | bytes 442372
  423.2 30.3 %collective-permute-start.18 = (bf16[2,3,576,768]{3,2,1,0:T(8,128)(2,1)}, bf16[2,3,576,768]{3,2,1,0:T(8,128)(2,1)}, u32[]{:S(2)}, u32[]{:S(2)}) collective-permute-start(bf16[2,3,576,768]{3,2,1,0:T(8,128)(2,1)} %get-tuple-element.112), channel_id=1, source_target_pairs={{0,4},{4,0},{8,12},{12,8},{16,20},{20,16},{24,28},{28,24},{1,5},{5... | collective-permute-start | bytes 15925256 | tf_op jit(solution)/shard_map/ppermute | solution.py:652
  453.5 6.2 copy-start.5
  462.9 60.3 %collective-permute-start.20 = (bf16[2,3,288,768]{3,2,1,0:T(8,128)(2,1)}, bf16[2,3,288,768]{3,2,1,0:T(8,128)(2,1)}, u32[]{:S(2)}, u32[]{:S(2)}) collective-permute-start(bf16[2,3,288,768]{3,2,1,0:T(8,128)(2,1)} %slice.227), channel_id=1, source_target_pairs={{0,8},{4,12},{8,0},{12,4},{16,24},{20,28},{24,16},{28,20},{1,9},{5... | collective-permute-start | bytes 7962632 | tf_op jit(solution)/shard_map/ppermute | solution.py:652
  472.1 59.2 %collective-permute-start.19 = (bf16[2,3,288,768]{3,2,1,0:T(8,128)(2,1)}, bf16[2,3,288,768]{3,2,1,0:T(8,128)(2,1)}, u32[]{:S(2)}, u32[]{:S(2)}) collective-permute-start(bf16[2,3,288,768]{3,2,1,0:T(8,128)(2,1)} %slice.226), channel_id=1, source_target_pairs={{0,16},{4,20},{8,24},{12,28},{16,0},{20,4},{24,8},{28,12},{1,17},{... | collective-permute-start | bytes 7962632 | tf_op jit(solution)/shard_map/ppermute | solution.py:652
  518.5 93.6 %all-to-all-start.4 = ((bf16[4,4,64,1152]{3,2,1,0:T(8,128)(2,1)}), bf16[4,4,64,1152]{3,2,1,0:T(8,128)(2,1)}, u32[]{:S(2)}, u32[]{:S(2)}) async-start(bf16[4,4,64,1152]{3,2,1,0:T(8,128)(2,1)} %get-tuple-element.119), calls=%async_computation.4 | async-start | bytes 4718592 | tf_op jit(solution)/shard_map/all_to_all | solution.py:739
  537.1 35.0 %collective-permute-start.24 = (bf16[2,3,144,768]{3,2,1,0:T(8,128)(2,1)}, bf16[2,3,144,768]{3,2,1,0:T(8,128)(2,1)}, u32[]{:S(2)}, u32[]{:S(2)}) collective-permute-start(bf16[2,3,144,768]{3,2,1,0:T(8,128)(2,1)} %slice.233), channel_id=1, source_target_pairs={{0,16},{4,20},{8,24},{12,28},{16,0},{20,4},{24,8},{28,12},{1,17},{... | collective-permute-start | bytes 3981320 | tf_op jit(solution)/shard_map/ppermute | solution.py:652
  551.7 52.3 %collective-permute-start.22 = (bf16[2,576,1152]{2,1,0:T(8,128)(2,1)}, bf16[2,576,1152]{2,1,0:T(8,128)(2,1)}, u32[]{:S(2)}, u32[]{:S(2)}) collective-permute-start(bf16[2,576,1152]{2,1,0:T(8,128)(2,1)} %get-tuple-element.132), channel_id=1, source_target_pairs={{0,4},{4,0},{8,12},{12,8},{16,20},{20,16},{24,28},{28,24},{1,5},{5... | collective-permute-start | bytes 7962632 | tf_op jit(solution)/shard_map/ppermute | solution.py:652
  551.7 14.1 %copy-start.15 = (bf16[2,3,576,768]{3,2,1,0:T(8,128)(2,1)S(1)}, bf16[2,3,576,768]{3,2,1,0:T(8,128)(2,1)}, u32[]{:S(2)}) copy-start(bf16[2,3,576,768]{3,2,1,0:T(8,128)(2,1)} %copy-done.14) | copy-start | bytes 15925252
  565.3 42.8 %collective-permute-start.21 = (bf16[2,576,1152]{2,1,0:T(8,128)(2,1)}, bf16[2,576,1152]{2,1,0:T(8,128)(2,1)}, u32[]{:S(2)}, u32[]{:S(2)}) collective-permute-start(bf16[2,576,1152]{2,1,0:T(8,128)(2,1)} %get-tuple-element.130), channel_id=1, source_target_pairs={{0,4},{4,0},{8,12},{12,8},{16,20},{20,16},{24,28},{28,24},{1,5},{5... | collective-permute-start | bytes 7962632 | tf_op jit(solution)/shard_map/ppermute | solution.py:652
  570.1 31.2 %collective-permute-start.23 = (bf16[2,3,144,768]{3,2,1,0:T(8,128)(2,1)S(1)}, bf16[2,3,144,768]{3,2,1,0:T(8,128)(2,1)}, u32[]{:S(2)}, u32[]{:S(2)}) collective-permute-start(bf16[2,3,144,768]{3,2,1,0:T(8,128)(2,1)S(1)} %slice.230), channel_id=1, source_target_pairs={{0,8},{4,12},{8,0},{12,4},{16,24},{20,28},{24,16},{28,20},{1,9},{5... | collective-permute-start | bytes 3981320 | tf_op jit(solution)/shard_map/ppermute | solution.py:652
  572.0 29.3 %copy-start.21 = (bf16[2,3,288,768]{3,2,1,0:T(8,128)(2,1)S(1)}, bf16[2,3,288,768]{3,2,1,0:T(8,128)(2,1)}, u32[]{:S(2)}) copy-start(bf16[2,3,288,768]{3,2,1,0:T(8,128)(2,1)} %copy-done.20) | copy-start | bytes 7962628
  574.3 29.7 %copy-start.23 = (bf16[2,576,1152]{2,1,0:T(8,128)(2,1)S(1)}, bf16[2,576,1152]{2,1,0:T(8,128)(2,1)}, u32[]{:S(2)}) copy-start(bf16[2,576,1152]{2,1,0:T(8,128)(2,1)} %get-tuple-element.131) | copy-start | bytes 7962628
  620.7 5.3 collective-permute-start.25
  625.9 6.9 collective-permute-start.26
  626.0 101.4 %collective-permute-start.36 = (bf16[2,3,144,768]{3,2,1,0:T(8,128)(2,1)}, bf16[2,3,144,768]{3,2,1,0:T(8,128)(2,1)}, u32[]{:S(2)}, u32[]{:S(2)}) collective-permute-start(bf16[2,3,144,768]{3,2,1,0:T(8,128)(2,1)} %add_convert_fusion.10), channel_id=1, source_target_pairs={{0,1},{1,0},{2,3},{3,2},{4,5},{5,4},{6,7},{7,6},{8,9},{9,8},{10,11... | collective-permute-start | bytes 3981320 | tf_op jit(solution)/shard_map/ppermute | solution.py:652
  633.5 13.0 %collective-permute-start.27 = (bf16[4,4,8,1152]{3,2,1,0:T(8,128)(2,1)}, bf16[4,4,8,1152]{3,2,1,0:T(8,128)(2,1)S(1)}, u32[]{:S(2)}, u32[]{:S(2)}) collective-permute-start(bf16[4,4,8,1152]{3,2,1,0:T(8,128)(2,1)} %pad_maximum_fusion.5), channel_id=1, source_target_pairs={{0,16},{4,20},{8,24},{12,28},{16,0},{20,4},{24,8},{28,12},{1,17},{... | collective-permute-start | bytes 884744 | tf_op jit(solution)/shard_map/ppermute | solution.py:652
  636.2 96.7 %collective-permute-start.30 = (bf16[2,288,1152]{2,1,0:T(8,128)(2,1)S(1)}, bf16[2,288,1152]{2,1,0:T(8,128)(2,1)}, u32[]{:S(2)}, u32[]{:S(2)}) collective-permute-start(bf16[2,288,1152]{2,1,0:T(8,128)(2,1)S(1)} %slice.177), channel_id=1, source_target_pairs={{0,8},{4,12},{8,0},{12,4},{16,24},{20,28},{24,16},{28,20},{1,9},{5... | collective-permute-start | bytes 3981320 | tf_op jit(solution)/shard_map/ppermute | solution.py:652
  640.2 89.2 %collective-permute-start.32 = (bf16[2,288,1152]{2,1,0:T(8,128)(2,1)}, bf16[2,288,1152]{2,1,0:T(8,128)(2,1)}, u32[]{:S(2)}, u32[]{:S(2)}) collective-permute-start(bf16[2,288,1152]{2,1,0:T(8,128)(2,1)} %slice.181), channel_id=1, source_target_pairs={{0,16},{4,20},{8,24},{12,28},{16,0},{20,4},{24,8},{28,12},{1,17},{... | collective-permute-start | bytes 3981320 | tf_op jit(solution)/shard_map/ppermute | solution.py:652
  641.7 162.0 %all-to-all-start.5 = ((bf16[32,64,1152]{2,1,0:T(8,128)(2,1)}), bf16[32,64,1152]{2,1,0:T(8,128)(2,1)}, u32[]{:S(2)}, u32[]{:S(2)}) async-start(bf16[32,64,1152]{2,1,0:T(8,128)(2,1)} %gather_fusion.7), calls=%async_computation.5 | async-start | bytes 9437184 | tf_op jit(solution)/shard_map/all_to_all | solution.py:972
  646.6 79.7 %collective-permute-start.28 = (bf16[8,4,8,1152]{3,2,1,0:T(8,128)(2,1)S(1)}, bf16[8,4,8,1152]{3,2,1,0:T(8,128)(2,1)S(1)}, u32[]{:S(2)}, u32[]{:S(2)}) collective-permute-start(bf16[8,4,8,1152]{3,2,1,0:T(8,128)(2,1)S(1)} %pad_maximum_fusion.4), channel_id=1, source_target_pairs={{0,8},{4,12},{8,0},{12,4},{16,24},{20,28},{24,16},{28,20},{1,9},{5... | collective-permute-start | bytes 1769480 | tf_op jit(solution)/shard_map/ppermute | solution.py:652
  727.4 37.6 %collective-permute-start.29 = (bf16[16,4,8,1152]{3,2,1,0:T(8,128)(2,1)}, bf16[16,4,8,1152]{3,2,1,0:T(8,128)(2,1)S(1)}, u32[]{:S(2)}, u32[]{:S(2)}) collective-permute-start(bf16[16,4,8,1152]{3,2,1,0:T(8,128)(2,1)} %get-tuple-element.194), channel_id=1, source_target_pairs={{0,4},{4,0},{8,12},{12,8},{16,20},{20,16},{24,28},{28,24},{1,5},{5... | collective-permute-start | bytes 3538952 | tf_op jit(solution)/shard_map/ppermute | solution.py:652
  729.3 32.1 %collective-permute-start.37 = (bf16[1,3,144,768]{3,2,1,0:T(8,128)(2,1)S(1)}, bf16[1,3,144,768]{3,2,1,0:T(8,128)(2,1)S(1)}, u32[]{:S(2)}, u32[]{:S(2)}) collective-permute-start(bf16[1,3,144,768]{3,2,1,0:T(8,128)(2,1)S(1)} %slice.245), channel_id=1, source_target_pairs={{0,2},{1,3},{2,0},{3,1},{4,6},{5,7},{6,4},{7,5},{8,10},{9,11},{10,... | collective-permute-start | bytes 1990664 | tf_op jit(solution)/shard_map/ppermute | solution.py:652
  731.4 31.8 %collective-permute-start.33 = (bf16[2,144,1152]{2,1,0:T(8,128)(2,1)S(1)}, bf16[2,144,1152]{2,1,0:T(8,128)(2,1)S(1)}, u32[]{:S(2)}, u32[]{:S(2)}) collective-permute-start(bf16[2,144,1152]{2,1,0:T(8,128)(2,1)S(1)} %slice.238), channel_id=1, source_target_pairs={{0,8},{4,12},{8,0},{12,4},{16,24},{20,28},{24,16},{28,20},{1,9},{5... | collective-permute-start | bytes 1990664 | tf_op jit(solution)/shard_map/ppermute | solution.py:652
  735.5 35.6 %collective-permute-start.31 = (bf16[2,144,1152]{2,1,0:T(8,128)(2,1)}, bf16[2,144,1152]{2,1,0:T(8,128)(2,1)}, u32[]{:S(2)}, u32[]{:S(2)}) collective-permute-start(bf16[2,144,1152]{2,1,0:T(8,128)(2,1)} %slice.236), channel_id=1, source_target_pairs={{0,16},{4,20},{8,24},{12,28},{16,0},{20,4},{24,8},{28,12},{1,17},{... | collective-permute-start | bytes 1990664 | tf_op jit(solution)/shard_map/ppermute | solution.py:652
  764.2 17.2 %collective-permute-start.34 = (bf16[2,144,1152]{2,1,0:T(8,128)(2,1)}, bf16[2,144,1152]{2,1,0:T(8,128)(2,1)}, u32[]{:S(2)}, u32[]{:S(2)}) collective-permute-start(bf16[2,144,1152]{2,1,0:T(8,128)(2,1)} %add_convert_fusion.13), channel_id=1, source_target_pairs={{0,1},{1,0},{2,3},{3,2},{4,5},{5,4},{6,7},{7,6},{8,9},{9,8},{10,11... | collective-permute-start | bytes 1990664 | tf_op jit(solution)/shard_map/ppermute | solution.py:652
  770.3 13.5 %copy-start.42 = (s32[128]{0:T(128)S(1)}, s32[128]{0:T(128)}, u32[]{:S(2)}) copy-start(s32[128]{0:T(128)} %copy-done.41) | copy-start | bytes 1540
  771.1 29.0 %copy-start.22 = (f32[864,864]{1,0:T(8,128)S(1)}, f32[864,864]{1,0:T(8,128)}, u32[]{:S(2)}) copy-start(f32[864,864]{1,0:T(8,128)} %constant.210.clone) | copy-start | bytes 8957956
  783.0 17.0 %collective-permute-start.35 = (bf16[1,144,1152]{2,1,0:T(8,128)(2,1)S(1)}, bf16[1,144,1152]{2,1,0:T(8,128)(2,1)S(1)}, u32[]{:S(2)}, u32[]{:S(2)}) collective-permute-start(bf16[1,144,1152]{2,1,0:T(8,128)(2,1)S(1)} %slice.240), channel_id=1, source_target_pairs={{0,2},{1,3},{2,0},{3,1},{4,6},{5,7},{6,4},{7,5},{8,10},{9,11},{10,... | collective-permute-start | bytes 995336 | tf_op jit(solution)/shard_map/ppermute | solution.py:652
  803.7 9.0 %copy-start.1 = (bf16[1152,3,288]{0,2,1:T(8,128)(2,1)S(1)}, bf16[1152,3,288]{0,2,1:T(8,128)(2,1)}, u32[]{:S(2)}) copy-start(bf16[1152,3,288]{0,2,1:T(8,128)(2,1)} %param.36) | copy-start | bytes 5971972
  (30 other events, 92.9 us)
Sparse Core Ops, SparseCore 0:
  29.9 143.8 all-gather.2

commit v8 on v7

--- a/solution.py
+++ b/solution.py
@@ -387,7 +387,7 @@
     put_rows(sums_ref, 0, sums)
 
 
-def by_image(kernel, name, rows, chunks, mods, outs):
+def by_image(kernel, name, microseconds, rows, chunks, mods, outs):
     own, sums, width = mods.shape
     tokens = rows[0].shape[0]
     length = tokens // own
@@ -413,7 +413,7 @@
         out_specs=specs + [whole],
         out_shape=shapes + [jax.ShapeDtypeStruct(mods.shape, f32)],
         compiler_params=pltpu.CompilerParams(vmem_limit_bytes=48 << 20),
-        cost_estimate=lasting(30),
+        cost_estimate=lasting(microseconds),
         name=name,
     )(*rows, chunks, mods)
 
@@ -458,9 +458,9 @@
 def mlp_kernel(count, e_ref, x_ref, *refs):
     first = pl.program_id(0) == 0
     save_ref, out_ref, w_ref = refs[count:]
-    size = refs[0].shape[2]
+    unit = min(ref.shape[2] for ref in refs[:count])
     for index, ref in enumerate(refs[:count]):
-        rows = pl.ds(pl.multiple_of(e_ref[index] * size, size), size)
+        rows = pl.ds(pl.multiple_of(e_ref[index] * unit, unit), ref.shape[2])
         for kind in range(3):
             w_ref[0, kind, rows, :] = ref[0, kind]
     x = x_ref[...]
@@ -474,15 +474,15 @@
 
 
 def mlp(x, order, pieces):
-    groups, _, size, width = pieces[0].shape
-    units, tokens = size * len(pieces), x.shape[0]
+    groups, _, _, width = pieces[0].shape
+    units, tokens = sum(piece.shape[2] for piece in pieces), x.shape[0]
     return pl.pallas_call(
         functools.partial(mlp_kernel, len(pieces)),
         grid_spec=pltpu.PrefetchScalarGridSpec(
             num_scalar_prefetch=1,
             grid=(groups,),
             in_specs=[pl.BlockSpec((tokens, width), lambda g, e: (0, 0), pipeline_mode=pl.Buffered(1))]
-            + [pl.BlockSpec((1, 3, size, width), lambda g, e: (g, 0, 0, 0))] * len(pieces),
+            + [pl.BlockSpec((1,) + piece.shape[1:], lambda g, e: (g, 0, 0, 0)) for piece in pieces],
             out_specs=[
                 pl.BlockSpec((1, 2, tokens, units), lambda g, e: (g, 0, 0, 0)),
                 pl.BlockSpec((tokens, width), lambda g, e: (0, 0)),
@@ -500,10 +500,10 @@
     )(order, x, *pieces)
 
 
-def fill_rows(order_ref, source_ref, target_ref):
+def fill_rows(order_ref, source_ref, target_ref, base=0):
     blocks, rows = source_ref.shape[0], source_ref.shape[1]
     for place in range(blocks):
-        target_ref[place * rows : (place + 1) * rows, :] = source_ref[order_ref[place]]
+        target_ref[place * rows : (place + 1) * rows, :] = source_ref[order_ref[base + place]]
 
 
 def mlp_back_kernel(
@@ -581,10 +581,13 @@
 def attend_grads_kernel(
     m_ref, e_ref, xt_ref, lowt_ref, proj_ref, att_ref, keep_ref, send_ref, xs, lows
 ):
-    @pl.when(pl.program_id(0) == 0)
+    first = pl.num_programs(0) // 2 == pl.program_id(0)
+    base = jnp.where(first, xt_ref.shape[0], 0)
+
+    @pl.when(first | (pl.program_id(0) == 0))
     def _():
-        fill_rows(e_ref, xt_ref, xs)
-        fill_rows(e_ref, lowt_ref, lows)
+        fill_rows(e_ref, xt_ref, xs, base)
+        fill_rows(e_ref, lowt_ref, lows, base)
 
     width = xs.shape[0]
     half = width // 2
@@ -595,7 +598,7 @@
         out_ref[0, :, columns:] = dot_11(lows[rows, :], att_ref[0]).astype(bf16)
 
 
-def attend_grads(m_order, e_order, xt, lowt, proj, att, microseconds):
+def attend_grads(m_order, e_orders, xt, lowt, proj, att):
     rows, tokens = att.shape[1:]
     width = xt.shape[0] * xt.shape[1]
     blocks = m_order.shape[0]
@@ -621,9 +624,9 @@
         ),
         out_shape=[half, half],
         compiler_params=pltpu.CompilerParams(vmem_limit_bytes=56 << 20),
-        cost_estimate=lasting(microseconds),
+        cost_estimate=lasting(200),
         name="attend_grads",
-    )(m_order, e_order, xt, lowt, proj, att)
+    )(m_order, e_orders, xt, lowt, proj, att)
 
 
 def dot(a, b):
@@ -796,8 +799,8 @@
     bin_totals = jnp.sum(
         ((info[0][:, None] == jnp.arange(NBINS)[None, :]) & live_all[:, None]).astype(f32), axis=0
     )
-    gather_bits = [("mp", bit) for bit in bits_of(mp_size)[::-1]]
-    gather_bits = gather_bits + [("dp", bit) for bit in bits_of(dp_size)[::-1]]
+    gather_bits = [("dp", bit) for bit in bits_of(dp_size)]
+    gather_bits = gather_bits + [("mp", bit) for bit in bits_of(mp_size)[::-1]]
     spread = {"dp": [0], "mp": [0]}
     for axis, bit in gather_bits:
         spread = {
@@ -858,36 +861,34 @@
         mlp_near = jnp.concatenate([mlp_near, far_near], axis=0)
         halves = split(mlp_near, 2)
         orders = ((2, 4), (4, 2))
-        got = [swap(halves[half], "dp", orders[half][0]) for half in range(2)]
-        latent, got[0], got[1] = tie(latent, got[0], got[1])
-        firsts = [(halves[half], got[half]) for half in range(2)]
-        got = [swap(jnp.stack(firsts[half]), "dp", orders[half][1]) for half in range(2)]
-
+        parts = [{bit: swap(halves[half], "dp", bit) for bit in orders[half]} for half in range(2)]
+        cored = swap(mlp_near, "dp", 1)
+        latent, parts[0][2], parts[1][4], cored = tie(latent, parts[0][2], parts[1][4], cored)
+        got = [swap(parts[half][orders[half][0]], "dp", orders[half][1]) for half in range(2)]
+
+    cotangent, latent = tie(cotangent, latent)
     proj, attended, branch_one, normed_t, middle, two, two_t = attend(
         latent, mods, attend_full, gains_f, tables
     )
-    cotangent, attended = tie(cotangent, attended)
     cot = turn(cotangent.reshape(mp_size, own, local_len, model_width))
     if by_permutes:
         got[0], got[1], attended = tie(got[0], got[1], attended)
-        mlp_pieces, mlp_order = [], []
+        mlp_pieces, mlp_order = [mlp_near, cored], [dp_index * 2, (dp_index ^ 1) * 2]
         for half in range(2):
-            first, second = orders[half]
-            parts = {0: firsts[half][0], first: firsts[half][1]}
-            parts.update({second: got[half][0], first ^ second: got[half][1]})
-            for near, part in parts.items():
+            parts[half][6] = got[half]
+            for near, part in parts[half].items():
                 mlp_pieces += [part, swap(part, "dp", 1)]
                 mlp_order += [(dp_index ^ near) * 2 + half, (dp_index ^ near ^ 1) * 2 + half]
         mlp_order = jnp.stack(mlp_order).astype(jnp.int32)
+    two, cot = tie(two, cot)
     save, branch_two, mlp_full = mlp(two, mlp_order, mlp_pieces)
     down_low, down_t, result, sums_finish = by_image(
-        finish_kernel, "finish", (branch_two, middle), cot, mods, (bf16, True, False)
+        finish_kernel, "finish", 30, (branch_two, middle), cot, mods, (bf16, True, False)
     )
     result = turn(result)
 
     e_orders = [(dp_index ^ jnp.array(halving_order(bits))).astype(jnp.int32) for bits in dp_bits]
     m_order = (mp_index ^ jnp.array(halving_order(mp_bits))).astype(jnp.int32)
-    m_orders = (m_order[: mp_size // 2], m_order[mp_size // 2 :])
 
     def by_owner(values):
         return values.reshape(dp_size, model_width // dp_size, -1)
@@ -901,54 +902,66 @@
         0, e_orders[0], two_t, down_t, down_low, save, mlp_full
     )
     got_zero = swap(sent_zero, "dp", dp_bits[0][0])
-    two_zero, got_one, result = tie(two_zero, got_one, result)
-    kept_one, sent_one = split(add_low(kept_one, got_one), 2)
+    kept_one, kept_zero = add_low(kept_one, got_one), add_low(kept_zero, got_zero)
+    two_zero, kept_one, kept_zero = tie(two_zero, kept_one, kept_zero)
+    kept_one, sent_one = split(kept_one, 2)
+    kept_zero, sent_zero = split(kept_zero, 2)
     got_one = swap(sent_one, "dp", dp_bits[1][1])
+    got_zero = swap(sent_zero, "dp", dp_bits[0][1])
     middle_grad, branch_low, branch_t, sums_middle = by_image(
         middle_kernel,
         "middle",
+        1,
         (two_zero, two_one, middle, branch_one),
         cot,
         mods,
         (f32, bf16, True),
     )
-    branch_low, got_zero = tie(branch_low, got_zero)
-    kept_zero, sent_zero = split(add_low(kept_zero, got_zero), 2)
-    got_zero = swap(sent_zero, "dp", dp_bits[0][1])
+    branch_low, result = tie(branch_low, result)
     projected_low, gains_grad, sums_entry, latent_back = attend_back(
         latent, proj, branch_low, attend_full, gains_f, tables, middle_grad, mods
     )
     gains_grad = jnp.sum(gains_grad, axis=2) * jnp.array([[head_dim ** (-0.5)], [1.0]], f32)
     projected_low, got_one, got_zero = tie(projected_low, got_one, got_zero)
-    kept_one, sent_one = split(add_low(kept_one, got_one), 2)
-    kept_zero, sent_zero = split(add_low(kept_zero, got_zero), 2)
+    kept_one, kept_zero = add_low(kept_one, got_one), add_low(kept_zero, got_zero)
+    normed_t, kept_one, kept_zero = tie(normed_t, kept_one, kept_zero)
+    kept_one, sent_one = split(kept_one, 2)
+    kept_zero, sent_zero = split(kept_zero, 2)
     got_one = swap(sent_one, "dp", dp_bits[1][2])
     got_zero = swap(sent_zero, "dp", dp_bits[0][2])
     latent_back = turn(latent_back)
 
     normed_t, branch_t = by_owner(normed_t), by_owner(branch_t)
 
-    def grads_of(which):
-        kept, sent = attend_grads(
-            m_orders[which],
-            e_orders[which],
-            normed_t,
-            branch_t,
-            projected_low,
-            attended,
-            200 if which else 5,
-        )
-        return kept, swap(sent, "dp", dp_bits[which][0])
-
-    attend_one, attend_got_one = grads_of(1)
-    attend_zero, attend_got_zero = grads_of(0)
+    attend_kept, attend_sent = attend_grads(
+        m_order, jnp.concatenate(e_orders), normed_t, branch_t, projected_low, attended
+    )
+    attend_got = swap(attend_sent, "dp", dp_bits[0][0])
+    attend_kept, got_one, got_zero = tie(attend_kept, got_one, got_zero)
+
+    packed = sums_finish + sums_middle + sums_entry
+    gains_row = jnp.pad(gains_grad.reshape(1, 1, -1), ((0, own - 1), (7, 0), (0, model_width - 2 * head_dim)))
+    packed = jnp.where(jnp.arange(8)[:, None] == 7, gains_row, packed).astype(bf16)
+    packed = packed[None]
+    got_packed = swap(packed, *gather_bits[0])
+
+    def more(after):
+        nonlocal packed, got_packed, stage
+        after, got_packed = tie(after, got_packed)
+        packed = jnp.concatenate([packed, got_packed], axis=0)
+        stage += 1
+        if stage < len(gather_bits):
+            got_packed = swap(packed, *gather_bits[stage])
+        return after
+
+    stage = 0
+    attend_kept = more(attend_kept)
+    attend_sum = more(add_low(attend_kept, attend_got))
     mlp_one = halve(add_low(kept_one, got_one), "dp", dp_bits[1][3:], 2)
     mlp_zero = halve(add_low(kept_zero, got_zero), "dp", dp_bits[0][3:], 2)
-    attend_one = add_low(attend_one, attend_got_one)
-    attend_zero = add_low(attend_zero, attend_got_zero)
-    latent_back, attend_one, attend_zero, mlp_one, mlp_zero = tie(
-        latent_back, attend_one, attend_zero, mlp_one, mlp_zero
-    )
+    mlp_one = more(mlp_one)
+    attend_zero, attend_one = split(attend_sum, 0)
+    latent_back, attend_one, attend_zero = tie(latent_back, attend_one, attend_zero)
     attend_one, sent_one = split(attend_one, 1)
     attend_zero, sent_zero = split(attend_zero, 1)
     attend_got_one = swap(sent_one, "dp", dp_bits[1][1])
@@ -964,17 +977,14 @@
     latent_back = jnp.concatenate([latent_back, empty], axis=0)
     back_patches = take_rows(latent_back, back_slot)
 
-    packed = sums_finish + sums_middle + sums_entry
-    gains_row = jnp.pad(gains_grad.reshape(1, 1, -1), ((0, own - 1), (7, 0), (0, model_width - 2 * head_dim)))
-    packed = jnp.where(jnp.arange(8)[:, None] == 7, gains_row, packed).astype(bf16)
-    packed, back_patches = tie(packed, back_patches)
-    packed = xor_gather(packed, gather_bits)[0]
     got_patches = lax.all_to_all(back_patches, "dp", split_axis=0, concat_axis=0, tiled=True)
     slot_ids = jnp.arange(capacity)
     home_peer = dest_perm[jnp.mod(my_start + slot_ids, dp_size)]
     home_index = home_peer * slot_count + jnp.minimum(slot_ids // dp_size, slot_count - 1)
     patch_grad = take_rows(got_patches, home_index)
 
+    while stage < len(gather_bits):
+        mlp_zero = more(mlp_zero)
     packed = packed.reshape(total_images, 8, model_width)
     mod_all = packed[:, :6]
     gains_total = packed.reshape(-1, own, 8, model_width)[:, 0, 7, : 2 * head_dim]

time: 826 us -> 769 us (0.931)
  waiting for transfers between devices: 347 us -> 294 us
    ppermute x38, waiting for transfers between devices: 285 us -> 233 us  [swap(): return lax.ppermute(values, axis, [(i, i ^ bit) for i in range(size)])]
    pallas_call x2 -> x1, Pallas kernels: 26.7 us -> 21.5 us  [attend_grads(): pl.pallas_call(attend_grads_kernel, grid_spec=pltpu.PrefetchScalarGridSpe...]
    convert_element_type x13 -> x12, other arithmetic: 38.1 us -> 41.3 us  [add_low(): return (kept.astype(f32) + received.astype(f32)).astype(bf16)]
    unnamed x107 -> x109, local copies, waits for them, and re-layouts: 25.5 us -> 24.2 us
  transfers between devices with their start and end apart: 45 -> 45, of which waited for: 18 -> 17; matrix products, arithmetic and copies ran while one was open for 14% -> 15% of each run, Pallas kernels for 24% -> 17%
where the time goes in v8:
time: 769 us; the launch traced here: 762 us
  waiting for transfers between devices  294 us (38%)
  Pallas kernels  232 us (30%)
  local copies, waits for them, and re-layouts  81.1 us (11%)
  starting transfers between devices  64.2 us (8%)
  other arithmetic  59.6 us (8%)
  between operations  15.4 us (2%)
  matrix products  14.6 us (2%)
    ppermute x38, waiting for transfers between devices, swap(): return lax.ppermute(values, axis, [(i, i ^ bit) for i in range(size)])  233 us
    pallas_call x2, Pallas kernels, mlp_back(): pl.pallas_call(mlp_back_kernel, grid_spec=pltpu.PrefetchScalarGridSpec(nu...  72.5 us
    all_to_all x4, waiting for transfers between devices, turn(): return lax.all_to_all(chunks, 'mp', split_axis=0, concat_axis=0, tiled=True)  61.3 us
    pallas_call x1, Pallas kernels, attend_back(): pl.pallas_call(attend_back_kernel, grid=(groups,), in_specs=[whole_spec(l...  45.3 us
    convert_element_type x12, other arithmetic, add_low(): return (kept.astype(f32) + received.astype(f32)).astype(bf16)  41.3 us
    pallas_call x1, Pallas kernels, mlp(): pl.pallas_call(functools.partial(mlp_kernel, len(pieces)), grid_spec=pltp...  37.8 us
    pallas_call x1, Pallas kernels, attend(): pl.pallas_call(attend_kernel, grid=(groups,), in_specs=[whole_spec(latent...  36.1 us
    ppermute x38, starting transfers between devices, swap(): return lax.ppermute(values, axis, [(i, i ^ bit) for i in range(size)])  35.5 us
  transfers between devices with their start and end apart: 45, of which 17 were waited for; matrix products, arithmetic and copies ran while one was open for 15% of the time, Pallas kernels for 17%

profile of v8, /device:TPU:0, one launch (start us, length us, event | category | flops | bytes accessed | tf_op | source)
XLA Modules:
  0.0 761.7 jit_solution(14923814101656981213)
XLA Ops:
  15.2 2.6 collective-permute-start.1
  19.3 2.0 collective-permute-start.2
  22.1 5.6 gather_fusion.1
  30.7 2.5 copy.73
  35.6 2.6 collective-permute-start.3
  38.9 3.1 multiply_convert_fusion
  42.8 4.6 all-to-all-start
  47.6 26.2 %collective-permute-done.3 = bf16[1,3,96,1152]{3,2,1,0:T(8,128)(2,1)S(1)} collective-permute-done((bf16[1,3,96,1152]{3,2,1,0:T(8,128)(2,1)S(1)}, bf16[1,3,96,1152]{3,2,1,0:T(8,128)(2,1)S(1)}, u32[]{:S(2)}, u32[]{:S(2)}) %collective-permute-start.3) | collective-permute-done | bytes 663584 | tf_op jit(solution)/shard_map/ppermute | solution.py:655
  74.7 5.5 copy-done.3
  80.2 2.8 modulate.1
  83.9 34.3 %collective-permute-done.4 = bf16[2,3,96,1152]{3,2,1,0:T(8,128)(2,1)S(1)} collective-permute-done((bf16[2,3,96,1152]{3,2,1,0:T(8,128)(2,1)S(1)}, bf16[2,3,96,1152]{3,2,1,0:T(8,128)(2,1)S(1)}, u32[]{:S(2)}, u32[]{:S(2)}) %collective-permute-start.4) | collective-permute-done | bytes 1327136 | tf_op jit(solution)/shard_map/ppermute | solution.py:655
  118.2 5.7 gather_fusion.3
  123.9 5.0 all-to-all-start.1
  128.8 1.8 pad_maximum_fusion.refs_0_
  130.7 2.0 fusion.61
  140.5 28.0 %collective-permute-done.9.refs_4_ = bf16[4,3,48,1152]{3,2,1,0:T(8,128)(2,1)} collective-permute-done((bf16[4,3,48,1152]{3,2,1,0:T(8,128)(2,1)S(1)}, bf16[4,3,48,1152]{3,2,1,0:T(8,128)(2,1)}, u32[]{:S(2)}, u32[]{:S(2)}) %collective-permute-start.9) | collective-permute-done | bytes 1327136 | tf_op jit(solution)/shard_map/ppermute | solution.py:655
  168.6 28.1 %collective-permute-done.15.refs_10_ = bf16[4,3,48,1152]{3,2,1,0:T(8,128)(2,1)} collective-permute-done((bf16[4,3,48,1152]{3,2,1,0:T(8,128)(2,1)S(1)}, bf16[4,3,48,1152]{3,2,1,0:T(8,128)(2,1)}, u32[]{:S(2)}, u32[]{:S(2)}) %collective-permute-start.15) | collective-permute-done | bytes 1327136 | tf_op jit(solution)/shard_map/ppermute | solution.py:655
  196.7 4.0 all-to-all-done.1.latent_ref
  203.7 4.7 all-to-all-start.2
  208.5 36.1 %attend.1 = (f32[4,864,1024]{2,1,0:T(8,128)}, bf16[4,288,1024]{2,1,0:T(8,128)(2,1)}, bf16[1024,1152]{1,0:T(8,128)(2,1)}, bf16[1152,1024]{1,0:T(8,128)(2,1)}, f32...) custom-call(bf16[4,4,64,1152]{3,2,1,0:T(8,128)(2,1)} %all-to-all-done.1.latent_ref, ...), custom_call_target="tpu_custom_call" | custom-call | flops 176000008192 | bytes 1048576 | tf_op jit(solution)/shard_map/attend/pallas_call | solution.py:286
  246.6 16.4 %all-to-all-done.2.cot_ref = bf16[4,4,64,1152]{3,2,1,0:T(8,128)(2,1)} async-done(((bf16[4,4,64,1152]{3,2,1,0:T(8,128)(2,1)}), bf16[4,4,64,1152]{3,2,1,0:T(8,128)(2,1)}, u32[]{:S(2)}, u32[]{:S(2)}) %all-to-all-start.2) | async-done | bytes 2359328 | tf_op jit(solution)/shard_map/all_to_all | solution.py:742
  264.1 37.8 %mlp.1 = (bf16[4,2,1024,768]{3,2,1,0:T(8,128)(2,1)}, f32[1024,1152]{1,0:T(8,128)}, bf16[4,3,768,1152]{3,2,1,0:T(8,128)(2,1)}) custom-call(s32[14]{0:T(128)} %stack.93.e_ref, bf16[1024,1152]{1,0:T(8,128)(2,1)} %get-tuple-element.105.x_ref, bf16[4,3,96,1152]{3,2,1,0:T(8,128)(2,1)} %pad_maximum_fusion.refs_0_, ...), custom_call_target="tpu_custom_call" | custom-call | flops 131999997952 | bytes 1048576 | tf_op jit(solution)/shard_map/mlp/pallas_call | solution.py:479
  301.9 6.8 finish.1
  311.5 36.1 %mlp_back.2 = (bf16[2,3,576,768]{3,2,1,0:T(8,128)(2,1)}, bf16[2,3,576,768]{3,2,1,0:T(8,128)(2,1)}, f32[1024,1152]{1,0:T(8,128)}) custom-call(s32[8]{0:T(128)} %get-tuple-element.237.e_ref, bf16[8,144,1024]{2,1,0:T(8,128)(2,1)} %bitcast.165, bf16[8,144,1024]{2,1,0:T(8,128)(2,1)} %bitcast.147, bf16[1024,1152]{1,0:T(8,128)(2,1)} %copy-done.7, ...), custom_call_target="tpu_custom_call" | custom-call | flops 165000003584 | bytes 1048576 | tf_op jit(solution)/shard_map/mlp_back/pallas_call | solution.py:555
  347.5 36.4 %mlp_back.3 = (bf16[2,3,576,768]{3,2,1,0:T(8,128)(2,1)}, bf16[2,3,576,768]{3,2,1,0:T(8,128)(2,1)}, f32[1024,1152]{1,0:T(8,128)}) custom-call(s32[8]{0:T(128)} %get-tuple-element.236.e_ref, bf16[8,144,1024]{2,1,0:T(8,128)(2,1)} %bitcast.166, bf16[8,144,1024]{2,1,0:T(8,128)(2,1)} %bitcast.148, bf16[1024,1152]{1,0:T(8,128)(2,1)} %copy-done.7, ...), custom_call_target="tpu_custom_call" | custom-call | flops 165000003584 | bytes 1048576 | tf_op jit(solution)/shard_map/mlp_back/pallas_call | solution.py:555
  384.4 4.8 all-to-all-start.3
  390.4 7.9 %add_convert_fusion.1 = bf16[2,3,576,768]{3,2,1,0:T(8,128)(2,1)} fusion(bf16[2,3,576,768]{3,2,1,0:T(8,128)(2,1)} %collective-permute-done.19, bf16[2,3,576,768]{3,2,1,0:T(8,128)(2,1)} %get-tuple-element.122), kind=kLoop, calls=%fused_computation.11 | loop fusion | flops 10616832 | bytes 15925248 | tf_op jit(solution)/shard_map/convert_element_type | solution.py:676
  398.3 6.6 add_convert_fusion.2
  404.9 9.8 %middle.1 = (f32[1024,1152]{1,0:T(8,128)}, bf16[1024,1152]{1,0:T(8,128)(2,1)S(1)}, bf16[1152,1024]{1,0:T(8,128)(2,1)S(1)}, f32[4,8,1152]{2,1,0:T(8,128)S(1)}) custom-call(f32[1024,1152]{1,0:T(8,128)} %get-tuple-element.124.one_ref, f32[1024,1152]{1,0:T(8,128)} %get-tuple-element.125.other_ref, f32[1024,1152]{1,0:T(8,128)} %get-tuple-element.113.middle_ref, ...), custom_call_target="tpu_custom_call" | custom-call | flops 1100000000 | bytes 1048576 | tf_op jit(solution)/shard_map/middle/pallas_call | solution.py:409
  417.6 26.1 %all-to-all-done.3 = bf16[4,4,64,1152]{3,2,1,0:T(8,128)(2,1)} async-done(((bf16[4,4,64,1152]{3,2,1,0:T(8,128)(2,1)}), bf16[4,4,64,1152]{3,2,1,0:T(8,128)(2,1)}, u32[]{:S(2)}, u32[]{:S(2)}) %all-to-all-start.3) | async-done | bytes 2359328 | tf_op jit(solution)/shard_map/all_to_all | solution.py:742
  443.6 3.6 slice.150
  447.8 1.7 slice.151
  450.0 45.3 %attend_back.1 = (bf16[4,864,1024]{2,1,0:T(8,128)(2,1)}, f32[2,72,256]{2,1,0:T(8,128)}, f32[4,8,1152]{2,1,0:T(8,128)}, bf16[4,4,64,1152]{3,2,1,0:T(8,128)(2,1)}) custom-call(bf16[4,4,64,1152]{3,2,1,0:T(8,128)(2,1)} %all-to-all-done.1.latent_ref, f32[4,864,1024]{2,1,0:T(8,128)} %get-tuple-element.130.proj_ref, bf16[1024,1152]{1,0:T(8,128)(2,1)} %copy-done.5, ...), custom_call_target="tpu_custom_call" | custom-call | flops 176000008192 | bytes 1048576 | tf_op jit(solution)/shard_map/attend_back/pallas_call | solution.py:330
  495.3 10.9 %collective-permute-done.20 = bf16[2,3,288,768]{3,2,1,0:T(8,128)(2,1)} collective-permute-done((bf16[2,3,288,768]{3,2,1,0:T(8,128)(2,1)}, bf16[2,3,288,768]{3,2,1,0:T(8,128)(2,1)}, u32[]{:S(2)}, u32[]{:S(2)}) %collective-permute-start.20) | collective-permute-done | bytes 2654240 | tf_op jit(solution)/shard_map/ppermute | solution.py:655
  506.2 2.1 collective-permute-done.21
  508.3 4.8 add_convert_fusion.3
  513.1 4.1 add_convert_fusion.4
  517.3 21.5 %attend_grads.1 = (bf16[4,576,1152]{2,1,0:T(8,128)(2,1)}, bf16[4,576,1152]{2,1,0:T(8,128)(2,1)}) custom-call(s32[4]{0:T(128)} %broadcast_xor_fusion.m_ref, s32[16]{0:T(128)} %pad_add_fusion.3.e_ref, bf16[8,144,1024]{2,1,0:T(8,128)(2,1)} %bitcast.164, bf16[8,144,1024]{2,1,0:T(8,128)(2,1)} %bitcast.146, bf16[4,864,1024]{2,1,0:T(8,128)(2,1)} %get-tuple-element.142.proj_ref, ...), custom_call_target="tpu_custom_call" | custom-call | flops 219999993856 | bytes 1048576 | tf_op jit(solution)/shard_map/attend_grads/pallas_call | solution.py:608
  547.3 4.6 all-to-all-start.4
  553.6 22.1 %collective-permute-done.22 = bf16[2,3,144,768]{3,2,1,0:T(8,128)(2,1)} collective-permute-done((bf16[2,3,144,768]{3,2,1,0:T(8,128)(2,1)S(1)}, bf16[2,3,144,768]{3,2,1,0:T(8,128)(2,1)}, u32[]{:S(2)}, u32[]{:S(2)}) %collective-permute-start.22) | collective-permute-done | bytes 1327136 | tf_op jit(solution)/shard_map/ppermute | solution.py:655
  575.6 1.8 collective-permute-done.23
  578.8 3.1 add_convert_fusion.9
  582.0 5.3 add_convert_fusion
  588.8 2.8 fusion.60
  591.5 14.8 %all-to-all-done.4 = bf16[4,4,64,1152]{3,2,1,0:T(8,128)(2,1)} async-done(((bf16[4,4,64,1152]{3,2,1,0:T(8,128)(2,1)}), bf16[4,4,64,1152]{3,2,1,0:T(8,128)(2,1)}, u32[]{:S(2)}, u32[]{:S(2)}) %all-to-all-start.4) | async-done | bytes 2359328 | tf_op jit(solution)/shard_map/all_to_all | solution.py:742
  608.7 1.6 add_convert_fusion.8
  613.4 2.0 collective-permute-start.36
  616.3 21.2 %collective-permute-done.28 = bf16[8,4,8,1152]{3,2,1,0:T(8,128)(2,1)S(1)} collective-permute-done((bf16[8,4,8,1152]{3,2,1,0:T(8,128)(2,1)S(1)}, bf16[8,4,8,1152]{3,2,1,0:T(8,128)(2,1)S(1)}, u32[]{:S(2)}, u32[]{:S(2)}) %collective-permute-start.28) | collective-permute-done | bytes 589856 | tf_op jit(solution)/shard_map/ppermute | solution.py:655
  641.2 3.4 concatenate.66
  644.7 5.0 gather_fusion.7
  649.6 4.9 all-to-all-start.5
  654.5 2.1 add_convert_fusion.7
  657.5 2.0 collective-permute-start.31
  659.5 2.1 add_convert_fusion.12
  661.6 2.0 collective-permute-start.34
  663.6 20.0 %collective-permute-done.29 = bf16[16,4,8,1152]{3,2,1,0:T(8,128)(2,1)} collective-permute-done((bf16[16,4,8,1152]{3,2,1,0:T(8,128)(2,1)}, bf16[16,4,8,1152]{3,2,1,0:T(8,128)(2,1)}, u32[]{:S(2)}, u32[]{:S(2)}) %collective-permute-start.29) | collective-permute-done | bytes 1179680 | tf_op jit(solution)/shard_map/ppermute | solution.py:655
  683.6 1.6 add_convert_fusion.5
  689.6 2.2 fusion.28
  691.8 2.5 fusion.12
  696.8 25.7 %collective-permute-done.31 = bf16[2,144,1152]{2,1,0:T(8,128)(2,1)} collective-permute-done((bf16[2,144,1152]{2,1,0:T(8,128)(2,1)}, bf16[2,144,1152]{2,1,0:T(8,128)(2,1)}, u32[]{:S(2)}, u32[]{:S(2)}) %collective-permute-start.31) | collective-permute-done | bytes 663584 | tf_op jit(solution)/shard_map/ppermute | solution.py:655
  724.1 3.0 collective-permute-start.35
  730.8 10.9 %collective-permute-done.35 = bf16[1,144,1152]{2,1,0:T(8,128)(2,1)S(1)} collective-permute-done((bf16[1,144,1152]{2,1,0:T(8,128)(2,1)S(1)}, bf16[1,144,1152]{2,1,0:T(8,128)(2,1)S(1)}, u32[]{:S(2)}, u32[]{:S(2)}) %collective-permute-start.35) | collective-permute-done | bytes 331808 | tf_op jit(solution)/shard_map/ppermute | solution.py:655
  745.4 5.7 gather_fusion.9
  751.2 3.3 copy.111
  (296 shorter events, 80.5 us)
Async XLA Ops:
  7.2 21.1 %copy-start = (bf16[1152,3,288]{0,2,1:T(8,128)(2,1)S(1)}, bf16[1152,3,288]{0,2,1:T(8,128)(2,1)}, u32[]{:S(2)}) copy-start(bf16[1152,3,288]{0,2,1:T(8,128)(2,1)} %param.36) | copy-start | bytes 5971972
  7.2 201.3 %all-gather.3.cloned.1.call-start = ((), (), s32[]{:S(2)}) async-start(), calls=%async_computation.6 | async-start | bytes 10948608 | tf_op jit(solution)/shard_map/all_gather | solution.py:641
  8.1 7.1 collective-permute-start
  11.9 18.7 %copy-start.8 = (s32[8]{0:T(128)}, s32[8]{0:T(128)S(1)}, u32[]{:S(2)}) copy-start(s32[8]{0:T(128)S(1)} %bitcast_subtract_fusion.2) | copy-start | bytes 100
  13.8 8.3 %copy-start.30 = (s32[1024]{0:T(1024)}, s32[1024]{0:T(1024)S(1)}, u32[]{:S(2)}) copy-start(s32[1024]{0:T(1024)S(1)} %pad_clamp_fusion.7) | copy-start | bytes 12292
  15.2 4.1 collective-permute-start.1
  19.3 8.5 %collective-permute-start.2 = (s32[4,2,32]{2,1,0:T(2,128)S(1)}, s32[4,2,32]{2,1,0:T(2,128)S(1)}, u32[]{:S(2)}, u32[]{:S(2)}) collective-permute-start(s32[4,2,32]{2,1,0:T(2,128)S(1)} %pad_add_fusion.1), channel_id=1, source_target_pairs={{0,16},{4,20},{8,24},{12,28},{16,0},{20,4},{24,8},{28,12},{1,17},{... | collective-permute-start | bytes 3080 | tf_op jit(solution)/shard_map/ppermute | solution.py:655
  35.6 38.2 %collective-permute-start.3 = (bf16[1,3,96,1152]{3,2,1,0:T(8,128)(2,1)S(1)}, bf16[1,3,96,1152]{3,2,1,0:T(8,128)(2,1)S(1)}, u32[]{:S(2)}, u32[]{:S(2)}) collective-permute-start(bf16[1,3,96,1152]{3,2,1,0:T(8,128)(2,1)S(1)} %maximum_bitcast_fusion), channel_id=1, source_target_pairs={{0,2},{1,3},{2,0},{3,1},{4,6},{5,7},{6,4},{7,5},{8,10},{9,11},{10,... | collective-permute-start | bytes 1990664 | tf_op jit(solution)/shard_map/ppermute | solution.py:655
  38.6 8.9 %copy-start.31 = (s32[128]{0:T(128)}, s32[128]{0:T(128)S(1)}, u32[]{:S(2)}) copy-start(s32[128]{0:T(128)S(1)} %get-tuple-element.211) | copy-start | bytes 1540
  42.8 75.4 %all-to-all-start = ((bf16[32,64,1152]{2,1,0:T(8,128)(2,1)}), bf16[32,64,1152]{2,1,0:T(8,128)(2,1)}, u32[]{:S(2)}, u32[]{:S(2)}) async-start(bf16[32,64,1152]{2,1,0:T(8,128)(2,1)} %gather_fusion.1), calls=%async_computation | async-start | bytes 9437184 | tf_op jit(solution)/shard_map/all_to_all | solution.py:791
  74.0 44.2 %collective-permute-start.4 = (bf16[2,3,96,1152]{3,2,1,0:T(8,128)(2,1)S(1)}, bf16[2,3,96,1152]{3,2,1,0:T(8,128)(2,1)S(1)}, u32[]{:S(2)}, u32[]{:S(2)}) collective-permute-start(bf16[2,3,96,1152]{3,2,1,0:T(8,128)(2,1)S(1)} %pad_maximum_fusion.1), channel_id=1, source_target_pairs={{0,1},{1,0},{2,3},{3,2},{4,5},{5,4},{6,7},{7,6},{8,9},{9,8},{10,11... | collective-permute-start | bytes 3981320 | tf_op jit(solution)/shard_map/ppermute | solution.py:655
  123.9 76.9 %all-to-all-start.1 = ((bf16[4,4,64,1152]{3,2,1,0:T(8,128)(2,1)}), bf16[4,4,64,1152]{3,2,1,0:T(8,128)(2,1)}, u32[]{:S(2)}, u32[]{:S(2)}) async-start(bf16[4,4,64,1152]{3,2,1,0:T(8,128)(2,1)} %bitcast.150), calls=%async_computation.1 | async-start | bytes 4718592 | tf_op jit(solution)/shard_map/all_to_all | solution.py:742
  130.7 66.1 %collective-permute-start.7 = (bf16[4,3,96,1152]{3,2,1,0:T(8,128)(2,1)}, bf16[4,3,96,1152]{3,2,1,0:T(8,128)(2,1)}, u32[]{:S(2)}, u32[]{:S(2)}) collective-permute-start(bf16[4,3,96,1152]{3,2,1,0:T(8,128)(2,1)} %pad_maximum_fusion.refs_0_), channel_id=1, source_target_pairs={{0,4},{4,0},{8,12},{12,8},{16,20},{20,16},{24,28},{28,24},{1,5},{5... | collective-permute-start | bytes 7962632 | tf_op jit(solution)/shard_map/ppermute | solution.py:655
  130.7 6.6 copy-start.35
  130.7 9.1 %copy-start.33 = (f32[2]{0:T(128)S(1)}, f32[2]{0:T(128)}, u32[]{:S(2)}) copy-start(f32[2]{0:T(128)} %constant.218) | copy-start | bytes 28
  132.8 63.9 %collective-permute-start.5 = (bf16[4,3,48,1152]{3,2,1,0:T(8,128)(2,1)S(1)}, bf16[4,3,48,1152]{3,2,1,0:T(8,128)(2,1)}, u32[]{:S(2)}, u32[]{:S(2)}) collective-permute-start(bf16[4,3,48,1152]{3,2,1,0:T(8,128)(2,1)S(1)} %get-tuple-element.217), channel_id=1, source_target_pairs={{0,8},{4,12},{8,0},{12,4},{16,24},{20,28},{24,16},{28,20},{1,9},{5... | collective-permute-start | bytes 3981320 | tf_op jit(solution)/shard_map/ppermute | solution.py:655
  134.3 34.3 %collective-permute-start.9 = (bf16[4,3,48,1152]{3,2,1,0:T(8,128)(2,1)S(1)}, bf16[4,3,48,1152]{3,2,1,0:T(8,128)(2,1)}, u32[]{:S(2)}, u32[]{:S(2)}) collective-permute-start(bf16[4,3,48,1152]{3,2,1,0:T(8,128)(2,1)S(1)} %get-tuple-element.217), channel_id=1, source_target_pairs={{0,16},{4,20},{8,24},{12,28},{16,0},{20,4},{24,8},{28,12},{1,17},{... | collective-permute-start | bytes 3981320 | tf_op jit(solution)/shard_map/ppermute | solution.py:655
  135.7 61.0 %collective-permute-start.6 = (bf16[4,3,48,1152]{3,2,1,0:T(8,128)(2,1)S(1)}, bf16[4,3,48,1152]{3,2,1,0:T(8,128)(2,1)}, u32[]{:S(2)}, u32[]{:S(2)}) collective-permute-start(bf16[4,3,48,1152]{3,2,1,0:T(8,128)(2,1)S(1)} %get-tuple-element.216), channel_id=1, source_target_pairs={{0,16},{4,20},{8,24},{12,28},{16,0},{20,4},{24,8},{28,12},{1,17},{... | collective-permute-start | bytes 3981320 | tf_op jit(solution)/shard_map/ppermute | solution.py:655
  136.3 60.4 %collective-permute-start.15 = (bf16[4,3,48,1152]{3,2,1,0:T(8,128)(2,1)S(1)}, bf16[4,3,48,1152]{3,2,1,0:T(8,128)(2,1)}, u32[]{:S(2)}, u32[]{:S(2)}) collective-permute-start(bf16[4,3,48,1152]{3,2,1,0:T(8,128)(2,1)S(1)} %get-tuple-element.216), channel_id=1, source_target_pairs={{0,8},{4,12},{8,0},{12,4},{16,24},{20,28},{24,16},{28,20},{1,9},{5... | collective-permute-start | bytes 3981320 | tf_op jit(solution)/shard_map/ppermute | solution.py:655
  168.6 76.6 %collective-permute-start.10 = (bf16[4,3,48,1152]{3,2,1,0:T(8,128)(2,1)}, bf16[4,3,48,1152]{3,2,1,0:T(8,128)(2,1)}, u32[]{:S(2)}, u32[]{:S(2)}) collective-permute-start(bf16[4,3,48,1152]{3,2,1,0:T(8,128)(2,1)} %collective-permute-done.9.refs_4_), channel_id=1, source_target_pairs={{0,4},{4,0},{8,12},{12,8},{16,20},{20,16},{24,28},{28,24},{1,5},{5... | collective-permute-start | bytes 3981320 | tf_op jit(solution)/shard_map/ppermute | solution.py:655
  196.7 66.3 %collective-permute-start.16 = (bf16[4,3,48,1152]{3,2,1,0:T(8,128)(2,1)}, bf16[4,3,48,1152]{3,2,1,0:T(8,128)(2,1)}, u32[]{:S(2)}, u32[]{:S(2)}) collective-permute-start(bf16[4,3,48,1152]{3,2,1,0:T(8,128)(2,1)} %collective-permute-done.15.refs_10_), channel_id=1, source_target_pairs={{0,4},{4,0},{8,12},{12,8},{16,20},{20,16},{24,28},{28,24},{1,5},{5... | collective-permute-start | bytes 3981320 | tf_op jit(solution)/shard_map/ppermute | solution.py:655
  200.8 44.1 %collective-permute-start.12 = (bf16[4,3,48,1152]{3,2,1,0:T(8,128)(2,1)}, bf16[4,3,48,1152]{3,2,1,0:T(8,128)(2,1)}, u32[]{:S(2)}, u32[]{:S(2)}) collective-permute-start(bf16[4,3,48,1152]{3,2,1,0:T(8,128)(2,1)} %collective-permute-done.6.refs_8_), channel_id=1, source_target_pairs={{0,8},{4,12},{8,0},{12,4},{16,24},{20,28},{24,16},{28,20},{1,9},{5... | collective-permute-start | bytes 3981320 | tf_op jit(solution)/shard_map/ppermute | solution.py:655
  202.3 60.8 %collective-permute-start.14 = (bf16[4,3,48,1152]{3,2,1,0:T(8,128)(2,1)}, bf16[4,3,48,1152]{3,2,1,0:T(8,128)(2,1)}, u32[]{:S(2)}, u32[]{:S(2)}) collective-permute-start(bf16[4,3,48,1152]{3,2,1,0:T(8,128)(2,1)} %collective-permute-done.6.refs_8_), channel_id=1, source_target_pairs={{0,4},{4,0},{8,12},{12,8},{16,20},{20,16},{24,28},{28,24},{1,5},{5... | collective-permute-start | bytes 3981320 | tf_op jit(solution)/shard_map/ppermute | solution.py:655
  202.3 42.3 %collective-permute-start.11 = (bf16[4,3,48,1152]{3,2,1,0:T(8,128)(2,1)}, bf16[4,3,48,1152]{3,2,1,0:T(8,128)(2,1)}, u32[]{:S(2)}, u32[]{:S(2)}) collective-permute-start(bf16[4,3,48,1152]{3,2,1,0:T(8,128)(2,1)} %collective-permute-done.5.refs_2_), channel_id=1, source_target_pairs={{0,16},{4,20},{8,24},{12,28},{16,0},{20,4},{24,8},{28,12},{1,17},{... | collective-permute-start | bytes 3981320 | tf_op jit(solution)/shard_map/ppermute | solution.py:655
  203.7 59.3 %all-to-all-start.2 = ((bf16[4,4,64,1152]{3,2,1,0:T(8,128)(2,1)}), bf16[4,4,64,1152]{3,2,1,0:T(8,128)(2,1)}, u32[]{:S(2)}, u32[]{:S(2)}) async-start(bf16[4,4,64,1152]{3,2,1,0:T(8,128)(2,1)} %bitcast.154), calls=%async_computation.2 | async-start | bytes 4718592 | tf_op jit(solution)/shard_map/all_to_all | solution.py:742
  208.5 37.6 %copy-start.40 = (s32[8]{0:T(128)S(1)}, s32[8]{0:T(128)}, u32[]{:S(2)}) copy-start(s32[8]{0:T(128)} %constant.206.clone) | copy-start | bytes 100
  208.5 37.6 %copy-start.41 = (s32[8]{0:T(128)S(1)}, s32[8]{0:T(128)}, u32[]{:S(2)}) copy-start(s32[8]{0:T(128)} %constant.207.clone) | copy-start | bytes 100
  244.6 18.4 %collective-permute-start.8 = (bf16[4,3,48,1152]{3,2,1,0:T(8,128)(2,1)}, bf16[4,3,48,1152]{3,2,1,0:T(8,128)(2,1)S(1)}, u32[]{:S(2)}, u32[]{:S(2)}) collective-permute-start(bf16[4,3,48,1152]{3,2,1,0:T(8,128)(2,1)} %collective-permute-done.5.refs_2_), channel_id=1, source_target_pairs={{0,4},{4,0},{8,12},{12,8},{16,20},{20,16},{24,28},{28,24},{1,5},{5... | collective-permute-start | bytes 3981320 | tf_op jit(solution)/shard_map/ppermute | solution.py:655
  244.9 18.2 %collective-permute-start.13 = (bf16[4,3,48,1152]{3,2,1,0:T(8,128)(2,1)}, bf16[4,3,48,1152]{3,2,1,0:T(8,128)(2,1)}, u32[]{:S(2)}, u32[]{:S(2)}) collective-permute-start(bf16[4,3,48,1152]{3,2,1,0:T(8,128)(2,1)} %collective-permute-done.11.refs_6_), channel_id=1, source_target_pairs={{0,4},{4,0},{8,12},{12,8},{16,20},{20,16},{24,28},{28,24},{1,5},{5... | collective-permute-start | bytes 3981320 | tf_op jit(solution)/shard_map/ppermute | solution.py:655
  245.2 17.9 %collective-permute-start.17 = (bf16[4,3,48,1152]{3,2,1,0:T(8,128)(2,1)}, bf16[4,3,48,1152]{3,2,1,0:T(8,128)(2,1)}, u32[]{:S(2)}, u32[]{:S(2)}) collective-permute-start(bf16[4,3,48,1152]{3,2,1,0:T(8,128)(2,1)} %collective-permute-done.12.refs_12_), channel_id=1, source_target_pairs={{0,4},{4,0},{8,12},{12,8},{16,20},{20,16},{24,28},{28,24},{1,5},{5... | collective-permute-start | bytes 3981320 | tf_op jit(solution)/shard_map/ppermute | solution.py:655
  263.0 38.9 %copy-start.2 = (f32[4,8,1152]{2,1,0:T(8,128)S(1)}, f32[4,8,1152]{2,1,0:T(8,128)}, u32[]{:S(2)}) copy-start(f32[4,8,1152]{2,1,0:T(8,128)} %maximum_maximum_fusion.mods_ref) | copy-start | bytes 442372
  347.5 42.8 %collective-permute-start.19 = (bf16[2,3,576,768]{3,2,1,0:T(8,128)(2,1)}, bf16[2,3,576,768]{3,2,1,0:T(8,128)(2,1)}, u32[]{:S(2)}, u32[]{:S(2)}) collective-permute-start(bf16[2,3,576,768]{3,2,1,0:T(8,128)(2,1)} %get-tuple-element.123), channel_id=1, source_target_pairs={{0,4},{4,0},{8,12},{12,8},{16,20},{20,16},{24,28},{28,24},{1,5},{5... | collective-permute-start | bytes 15925256 | tf_op jit(solution)/shard_map/ppermute | solution.py:655
  383.9 14.3 %collective-permute-start.18 = (bf16[2,3,576,768]{3,2,1,0:T(8,128)(2,1)}, bf16[2,3,576,768]{3,2,1,0:T(8,128)(2,1)}, u32[]{:S(2)}, u32[]{:S(2)}) collective-permute-start(bf16[2,3,576,768]{3,2,1,0:T(8,128)(2,1)} %get-tuple-element.121), channel_id=1, source_target_pairs={{0,4},{4,0},{8,12},{12,8},{16,20},{20,16},{24,28},{28,24},{1,5},{5... | collective-permute-start | bytes 15925256 | tf_op jit(solution)/shard_map/ppermute | solution.py:655
  384.4 59.2 %all-to-all-start.3 = ((bf16[4,4,64,1152]{3,2,1,0:T(8,128)(2,1)}), bf16[4,4,64,1152]{3,2,1,0:T(8,128)(2,1)}, u32[]{:S(2)}, u32[]{:S(2)}) async-start(bf16[4,4,64,1152]{3,2,1,0:T(8,128)(2,1)} %get-tuple-element.128), calls=%async_computation.3 | async-start | bytes 4718592 | tf_op jit(solution)/shard_map/all_to_all | solution.py:742
  390.4 7.9 %slice-start = ((s8[5308416]{0:T(1024)(128)(4,1)}), s8[4194304]{0:T(1024)(128)(4,1)S(1)}, s32[]{:S(2)}) async-start(s8[5308416]{0:T(1024)(128)(4,1)} %bitcast.151), calls=%async_computation.7 | async-start | bytes 8388608
  390.4 7.9 %slice-start.1 = ((s8[5308416]{0:T(1024)(128)(4,1)}), s8[1114112]{0:T(1024)(128)(4,1)S(1)}, s32[]{:S(2)}) async-start(s8[5308416]{0:T(1024)(128)(4,1)} %bitcast.151), calls=%async_computation.8 | async-start | bytes 2228224
  447.2 59.0 %collective-permute-start.20 = (bf16[2,3,288,768]{3,2,1,0:T(8,128)(2,1)}, bf16[2,3,288,768]{3,2,1,0:T(8,128)(2,1)}, u32[]{:S(2)}, u32[]{:S(2)}) collective-permute-start(bf16[2,3,288,768]{3,2,1,0:T(8,128)(2,1)} %slice.150), channel_id=1, source_target_pairs={{0,16},{4,20},{8,24},{12,28},{16,0},{20,4},{24,8},{28,12},{1,17},{... | collective-permute-start | bytes 7962632 | tf_op jit(solution)/shard_map/ppermute | solution.py:655
  449.5 58.8 %collective-permute-start.21 = (bf16[2,3,288,768]{3,2,1,0:T(8,128)(2,1)}, bf16[2,3,288,768]{3,2,1,0:T(8,128)(2,1)}, u32[]{:S(2)}, u32[]{:S(2)}) collective-permute-start(bf16[2,3,288,768]{3,2,1,0:T(8,128)(2,1)} %slice.151), channel_id=1, source_target_pairs={{0,8},{4,12},{8,0},{12,4},{16,24},{20,28},{24,16},{28,20},{1,9},{5... | collective-permute-start | bytes 7962632 | tf_op jit(solution)/shard_map/ppermute | solution.py:655
  517.2 21.5 %copy-start.9 = (s32[8]{0:T(128)S(1)}, s32[8]{0:T(128)}, u32[]{:S(2)}) copy-start(s32[8]{0:T(128)} %copy-done.8) | copy-start | bytes 100
  517.2 22.3 %copy-start.11 = (s32[8]{0:T(128)S(1)}, s32[8]{0:T(128)}, u32[]{:S(2)}) copy-start(s32[8]{0:T(128)} %param.31) | copy-start | bytes 100
  517.3 24.4 %copy-start.12 = (s32[8]{0:T(128)S(1)}, s32[8]{0:T(128)}, u32[]{:S(2)}) copy-start(s32[8]{0:T(128)} %param.32) | copy-start | bytes 100
  538.7 43.2 %collective-permute-start.25 = (bf16[4,576,1152]{2,1,0:T(8,128)(2,1)}, bf16[4,576,1152]{2,1,0:T(8,128)(2,1)}, u32[]{:S(2)}, u32[]{:S(2)}) collective-permute-start(bf16[4,576,1152]{2,1,0:T(8,128)(2,1)} %get-tuple-element.153), channel_id=1, source_target_pairs={{0,4},{4,0},{8,12},{12,8},{16,20},{20,16},{24,28},{28,24},{1,5},{5... | collective-permute-start | bytes 15925256 | tf_op jit(solution)/shard_map/ppermute | solution.py:655
  543.9 31.7 %collective-permute-start.22 = (bf16[2,3,144,768]{3,2,1,0:T(8,128)(2,1)S(1)}, bf16[2,3,144,768]{3,2,1,0:T(8,128)(2,1)}, u32[]{:S(2)}, u32[]{:S(2)}) collective-permute-start(bf16[2,3,144,768]{3,2,1,0:T(8,128)(2,1)S(1)} %slice.153), channel_id=1, source_target_pairs={{0,8},{4,12},{8,0},{12,4},{16,24},{20,28},{24,16},{28,20},{1,9},{5... | collective-permute-start | bytes 3981320 | tf_op jit(solution)/shard_map/ppermute | solution.py:655
  545.7 31.7 %collective-permute-start.23 = (bf16[2,3,144,768]{3,2,1,0:T(8,128)(2,1)}, bf16[2,3,144,768]{3,2,1,0:T(8,128)(2,1)}, u32[]{:S(2)}, u32[]{:S(2)}) collective-permute-start(bf16[2,3,144,768]{3,2,1,0:T(8,128)(2,1)} %slice.154), channel_id=1, source_target_pairs={{0,16},{4,20},{8,24},{12,28},{16,0},{20,4},{24,8},{28,12},{1,17},{... | collective-permute-start | bytes 3981320 | tf_op jit(solution)/shard_map/ppermute | solution.py:655
  547.3 59.0 %all-to-all-start.4 = ((bf16[4,4,64,1152]{3,2,1,0:T(8,128)(2,1)}), bf16[4,4,64,1152]{3,2,1,0:T(8,128)(2,1)}, u32[]{:S(2)}, u32[]{:S(2)}) async-start(bf16[4,4,64,1152]{3,2,1,0:T(8,128)(2,1)} %get-tuple-element.133), calls=%async_computation.4 | async-start | bytes 4718592 | tf_op jit(solution)/shard_map/all_to_all | solution.py:742
  552.8 24.6 %collective-permute-start.24 = (bf16[1,4,8,1152]{3,2,1,0:T(8,128)(2,1)S(1)}, bf16[1,4,8,1152]{3,2,1,0:T(8,128)(2,1)S(1)}, u32[]{:S(2)}, u32[]{:S(2)}) collective-permute-start(bf16[1,4,8,1152]{3,2,1,0:T(8,128)(2,1)S(1)} %get-tuple-element.213), channel_id=1, source_target_pairs={{0,4},{4,0},{8,12},{12,8},{16,20},{20,16},{24,28},{28,24},{1,5},{5... | collective-permute-start | bytes 221192 | tf_op jit(solution)/shard_map/ppermute | solution.py:655
  577.5 9.8 %collective-permute-start.26 = (bf16[2,4,8,1152]{3,2,1,0:T(8,128)(2,1)S(1)}, bf16[2,4,8,1152]{3,2,1,0:T(8,128)(2,1)S(1)}, u32[]{:S(2)}, u32[]{:S(2)}) collective-permute-start(bf16[2,4,8,1152]{3,2,1,0:T(8,128)(2,1)S(1)} %pad_maximum_fusion.4), channel_id=1, source_target_pairs={{0,8},{4,12},{8,0},{12,4},{16,24},{20,28},{24,16},{28,20},{1,9},{5... | collective-permute-start | bytes 442376 | tf_op jit(solution)/shard_map/ppermute | solution.py:655
  587.4 23.0 %collective-permute-start.27 = (bf16[4,4,8,1152]{3,2,1,0:T(8,128)(2,1)S(1)}, bf16[4,4,8,1152]{3,2,1,0:T(8,128)(2,1)S(1)}, u32[]{:S(2)}, u32[]{:S(2)}) collective-permute-start(bf16[4,4,8,1152]{3,2,1,0:T(8,128)(2,1)S(1)} %pad_maximum_fusion.3), channel_id=1, source_target_pairs={{0,16},{4,20},{8,24},{12,28},{16,0},{20,4},{24,8},{28,12},{1,17},{... | collective-permute-start | bytes 884744 | tf_op jit(solution)/shard_map/ppermute | solution.py:655
  607.9 30.6 %collective-permute-start.32 = (bf16[2,288,1152]{2,1,0:T(8,128)(2,1)S(1)}, bf16[2,288,1152]{2,1,0:T(8,128)(2,1)S(1)}, u32[]{:S(2)}, u32[]{:S(2)}) collective-permute-start(bf16[2,288,1152]{2,1,0:T(8,128)(2,1)S(1)} %slice.165), channel_id=1, source_target_pairs={{0,16},{4,20},{8,24},{12,28},{16,0},{20,4},{24,8},{28,12},{1,17},{... | collective-permute-start | bytes 3981320 | tf_op jit(solution)/shard_map/ppermute | solution.py:655
  610.5 27.0 %collective-permute-start.28 = (bf16[8,4,8,1152]{3,2,1,0:T(8,128)(2,1)S(1)}, bf16[8,4,8,1152]{3,2,1,0:T(8,128)(2,1)S(1)}, u32[]{:S(2)}, u32[]{:S(2)}) collective-permute-start(bf16[8,4,8,1152]{3,2,1,0:T(8,128)(2,1)S(1)} %pad_maximum_fusion.2), channel_id=1, source_target_pairs={{0,2},{1,3},{2,0},{3,1},{4,6},{5,7},{6,4},{7,5},{8,10},{9,11},{10,... | collective-permute-start | bytes 1769480 | tf_op jit(solution)/shard_map/ppermute | solution.py:655
  611.2 27.3 %copy-start.18 = (bf16[2,576,1152]{2,1,0:T(8,128)(2,1)S(1)}, bf16[2,576,1152]{2,1,0:T(8,128)(2,1)}, u32[]{:S(2)}) copy-start(bf16[2,576,1152]{2,1,0:T(8,128)(2,1)} %get-tuple-element.165) | copy-start | bytes 7962628
  611.3 43.2 %collective-permute-start.30 = (bf16[2,288,1152]{2,1,0:T(8,128)(2,1)S(1)}, bf16[2,288,1152]{2,1,0:T(8,128)(2,1)}, u32[]{:S(2)}, u32[]{:S(2)}) collective-permute-start(bf16[2,288,1152]{2,1,0:T(8,128)(2,1)S(1)} %slice.161), channel_id=1, source_target_pairs={{0,8},{4,12},{8,0},{12,4},{16,24},{20,28},{24,16},{28,20},{1,9},{5... | collective-permute-start | bytes 3981320 | tf_op jit(solution)/shard_map/ppermute | solution.py:655
  613.4 70.2 %collective-permute-start.36 = (bf16[2,3,144,768]{3,2,1,0:T(8,128)(2,1)}, bf16[2,3,144,768]{3,2,1,0:T(8,128)(2,1)}, u32[]{:S(2)}, u32[]{:S(2)}) collective-permute-start(bf16[2,3,144,768]{3,2,1,0:T(8,128)(2,1)} %add_convert_fusion.9), channel_id=1, source_target_pairs={{0,1},{1,0},{2,3},{3,2},{4,5},{5,4},{6,7},{7,6},{8,9},{9,8},{10,11... | collective-permute-start | bytes 3981320 | tf_op jit(solution)/shard_map/ppermute | solution.py:655
  638.6 45.1 %collective-permute-start.29 = (bf16[16,4,8,1152]{3,2,1,0:T(8,128)(2,1)}, bf16[16,4,8,1152]{3,2,1,0:T(8,128)(2,1)}, u32[]{:S(2)}, u32[]{:S(2)}) collective-permute-start(bf16[16,4,8,1152]{3,2,1,0:T(8,128)(2,1)} %get-tuple-element.218), channel_id=1, source_target_pairs={{0,1},{1,0},{2,3},{3,2},{4,5},{5,4},{6,7},{7,6},{8,9},{9,8},{10,11... | collective-permute-start | bytes 3538952 | tf_op jit(solution)/shard_map/ppermute | solution.py:655
  640.0 19.5 %collective-permute-start.33 = (bf16[2,144,1152]{2,1,0:T(8,128)(2,1)S(1)}, bf16[2,144,1152]{2,1,0:T(8,128)(2,1)}, u32[]{:S(2)}, u32[]{:S(2)}) collective-permute-start(bf16[2,144,1152]{2,1,0:T(8,128)(2,1)S(1)} %slice.214), channel_id=1, source_target_pairs={{0,8},{4,12},{8,0},{12,4},{16,24},{20,28},{24,16},{28,20},{1,9},{5... | collective-permute-start | bytes 1990664 | tf_op jit(solution)/shard_map/ppermute | solution.py:655
  649.6 95.8 %all-to-all-start.5 = ((bf16[32,64,1152]{2,1,0:T(8,128)(2,1)}), bf16[32,64,1152]{2,1,0:T(8,128)(2,1)}, u32[]{:S(2)}, u32[]{:S(2)}) async-start(bf16[32,64,1152]{2,1,0:T(8,128)(2,1)} %gather_fusion.7), calls=%async_computation.5 | async-start | bytes 9437184 | tf_op jit(solution)/shard_map/all_to_all | solution.py:980
  657.5 64.9 %collective-permute-start.31 = (bf16[2,144,1152]{2,1,0:T(8,128)(2,1)}, bf16[2,144,1152]{2,1,0:T(8,128)(2,1)}, u32[]{:S(2)}, u32[]{:S(2)}) collective-permute-start(bf16[2,144,1152]{2,1,0:T(8,128)(2,1)} %slice.212), channel_id=1, source_target_pairs={{0,16},{4,20},{8,24},{12,28},{16,0},{20,4},{24,8},{28,12},{1,17},{... | collective-permute-start | bytes 1990664 | tf_op jit(solution)/shard_map/ppermute | solution.py:655
  661.6 26.1 %copy-start.24 = (bf16[32,4,8,1152]{3,2,1,0:T(8,128)(2,1)S(1)}, bf16[32,4,8,1152]{3,2,1,0:T(8,128)(2,1)}, u32[]{:S(2)}) copy-start(bf16[32,4,8,1152]{3,2,1,0:T(8,128)(2,1)} %get-tuple-element.219) | copy-start | bytes 7077892
  661.6 60.9 %collective-permute-start.34 = (bf16[2,144,1152]{2,1,0:T(8,128)(2,1)}, bf16[2,144,1152]{2,1,0:T(8,128)(2,1)}, u32[]{:S(2)}, u32[]{:S(2)}) collective-permute-start(bf16[2,144,1152]{2,1,0:T(8,128)(2,1)} %add_convert_fusion.12), channel_id=1, source_target_pairs={{0,1},{1,0},{2,3},{3,2},{4,5},{5,4},{6,7},{7,6},{8,9},{9,8},{10,11... | collective-permute-start | bytes 1990664 | tf_op jit(solution)/shard_map/ppermute | solution.py:655
  687.3 39.8 %collective-permute-start.37 = (bf16[1,3,144,768]{3,2,1,0:T(8,128)(2,1)}, bf16[1,3,144,768]{3,2,1,0:T(8,128)(2,1)}, u32[]{:S(2)}, u32[]{:S(2)}) collective-permute-start(bf16[1,3,144,768]{3,2,1,0:T(8,128)(2,1)} %slice.221), channel_id=1, source_target_pairs={{0,2},{1,3},{2,0},{3,1},{4,6},{5,7},{6,4},{7,5},{8,10},{9,11},{10,... | collective-permute-start | bytes 1990664 | tf_op jit(solution)/shard_map/ppermute | solution.py:655
  694.3 32.8 %copy-start.20 = (bf16[2,3,144,768]{3,2,1,0:T(8,128)(2,1)S(1)}, bf16[2,3,144,768]{3,2,1,0:T(8,128)(2,1)}, u32[]{:S(2)}) copy-start(bf16[2,3,144,768]{3,2,1,0:T(8,128)(2,1)} %copy-done.19) | copy-start | bytes 3981316
  724.1 17.7 %collective-permute-start.35 = (bf16[1,144,1152]{2,1,0:T(8,128)(2,1)S(1)}, bf16[1,144,1152]{2,1,0:T(8,128)(2,1)S(1)}, u32[]{:S(2)}, u32[]{:S(2)}) collective-permute-start(bf16[1,144,1152]{2,1,0:T(8,128)(2,1)S(1)} %slice.216), channel_id=1, source_target_pairs={{0,2},{1,3},{2,0},{3,1},{4,6},{5,7},{6,4},{7,5},{8,10},{9,11},{10,... | collective-permute-start | bytes 995336 | tf_op jit(solution)/shard_map/ppermute | solution.py:655
  728.3 13.5 %copy-start.23 = (f32[864,864]{1,0:T(8,128)S(1)}, f32[864,864]{1,0:T(8,128)}, u32[]{:S(2)}) copy-start(f32[864,864]{1,0:T(8,128)} %constant.210.clone) | copy-start | bytes 8957956
  745.4 9.0 %copy-start.1 = (bf16[1152,3,288]{0,2,1:T(8,128)(2,1)S(1)}, bf16[1152,3,288]{0,2,1:T(8,128)(2,1)}, u32[]{:S(2)}) copy-start(bf16[1152,3,288]{0,2,1:T(8,128)(2,1)} %param.36) | copy-start | bytes 5971972
  (31 other events, 108.2 us)
Sparse Core Ops, SparseCore 0:
  29.7 143.8 all-gather.2

commit v9 on v8

--- a/solution.py
+++ b/solution.py
@@ -70,7 +70,7 @@
 
 def lasting(microseconds):
     return pl.CostEstimate(
-        flops=int(microseconds * 1.1e9), bytes_accessed=1 << 20, transcendentals=0
+        flops=int(microseconds * 1.1e9), bytes_accessed=1 << 10, transcendentals=0
     )
 
 
@@ -350,7 +350,7 @@
         ],
         scratch_shapes=[pltpu.VMEM((rows, tokens), f32)],
         compiler_params=pltpu.CompilerParams(vmem_limit_bytes=62 << 20),
-        cost_estimate=lasting(160),
+        cost_estimate=lasting(1),
         name="attend_back",
     )(latent, proj, low, weights, gains, *tables, grad, mods)
 
@@ -495,7 +495,7 @@
             jax.ShapeDtypeStruct((groups, 3, units, width), bf16),
         ],
         compiler_params=pltpu.CompilerParams(vmem_limit_bytes=62 << 20),
-        cost_estimate=lasting(120),
+        cost_estimate=lasting(1),
         name="mlp",
     )(order, x, *pieces)
 
@@ -674,6 +674,34 @@
 
 def add_low(kept, received):
     return (kept.astype(f32) + received.astype(f32)).astype(bf16)
+
+
+def sum_halves_kernel(kept_ref, got_ref, first_ref, second_ref):
+    total = (kept_ref[0].astype(f32) + got_ref[0].astype(f32)).astype(bf16)
+    half = first_ref.shape[1]
+    first_ref[0] = total[:half]
+    second_ref[0] = total[half:]
+
+
+def sum_halves(kept, got):
+    rows, columns = kept.shape[-2:]
+    if rows % 32:
+        return split(add_low(kept, got), kept.ndim - 2)
+    shape = kept.shape[:-2] + (rows // 2, columns)
+    kept, got = kept.reshape(-1, rows, columns), got.reshape(-1, rows, columns)
+    whole = pl.BlockSpec((1, rows, columns), lambda i: (i, 0, 0))
+    half = pl.BlockSpec((1, rows // 2, columns), lambda i: (i, 0, 0))
+    halves = pl.pallas_call(
+        sum_halves_kernel,
+        grid=(kept.shape[0],),
+        in_specs=[whole, whole],
+        out_specs=[half, half],
+        out_shape=[jax.ShapeDtypeStruct((kept.shape[0], rows // 2, columns), bf16)] * 2,
+        compiler_params=pltpu.CompilerParams(vmem_limit_bytes=32 << 20),
+        cost_estimate=lasting(0),
+        name="sum_halves",
+    )(kept, got)
+    return halves[0].reshape(shape), halves[1].reshape(shape)
 
 
 def tie(*values):
@@ -846,16 +874,15 @@
         ],
         axis=1,
     )
-    if by_permutes:
-        recv_patches, mods, far_near = tie(recv_patches, mods, far_near)
-    else:
-        recv_patches, mods = tie(recv_patches, mods)
+    recv_patches, mods = tie(recv_patches, mods)
 
     rank_ids = jnp.arange(images) * dp_size + my_place
     source = jnp.sum((finish[None, :] <= rank_ids[:, None]).astype(jnp.int32), axis=1)
     within = rank_ids - starts[source]
     recv_index = source * slot_count + within // dp_size
     latent = take_rows(recv_patches, recv_index).reshape(mp_size, own, local_len, model_width)
+    if by_permutes:
+        far_near, _ = tie(far_near, latent)
     latent = turn(latent)
     if by_permutes:
         mlp_near = jnp.concatenate([mlp_near, far_near], axis=0)
@@ -880,10 +907,10 @@
                 mlp_pieces += [part, swap(part, "dp", 1)]
                 mlp_order += [(dp_index ^ near) * 2 + half, (dp_index ^ near ^ 1) * 2 + half]
         mlp_order = jnp.stack(mlp_order).astype(jnp.int32)
-    two, cot = tie(two, cot)
     save, branch_two, mlp_full = mlp(two, mlp_order, mlp_pieces)
+    branch_two, cot = tie(branch_two, cot)
     down_low, down_t, result, sums_finish = by_image(
-        finish_kernel, "finish", 30, (branch_two, middle), cot, mods, (bf16, True, False)
+        finish_kernel, "finish", 1, (branch_two, middle), cot, mods, (bf16, True, False)
     )
     result = turn(result)
 
@@ -902,31 +929,28 @@
         0, e_orders[0], two_t, down_t, down_low, save, mlp_full
     )
     got_zero = swap(sent_zero, "dp", dp_bits[0][0])
-    kept_one, kept_zero = add_low(kept_one, got_one), add_low(kept_zero, got_zero)
-    two_zero, kept_one, kept_zero = tie(two_zero, kept_one, kept_zero)
-    kept_one, sent_one = split(kept_one, 2)
-    kept_zero, sent_zero = split(kept_zero, 2)
+    kept_one, sent_one = sum_halves(kept_one, got_one)
+    kept_zero, sent_zero = sum_halves(kept_zero, got_zero)
+    two_zero, kept_one, kept_zero, result = tie(two_zero, kept_one, kept_zero, result)
     got_one = swap(sent_one, "dp", dp_bits[1][1])
     got_zero = swap(sent_zero, "dp", dp_bits[0][1])
     middle_grad, branch_low, branch_t, sums_middle = by_image(
         middle_kernel,
         "middle",
-        1,
+        100,
         (two_zero, two_one, middle, branch_one),
         cot,
         mods,
         (f32, bf16, True),
     )
-    branch_low, result = tie(branch_low, result)
     projected_low, gains_grad, sums_entry, latent_back = attend_back(
         latent, proj, branch_low, attend_full, gains_f, tables, middle_grad, mods
     )
     gains_grad = jnp.sum(gains_grad, axis=2) * jnp.array([[head_dim ** (-0.5)], [1.0]], f32)
     projected_low, got_one, got_zero = tie(projected_low, got_one, got_zero)
-    kept_one, kept_zero = add_low(kept_one, got_one), add_low(kept_zero, got_zero)
+    kept_one, sent_one = sum_halves(kept_one, got_one)
+    kept_zero, sent_zero = sum_halves(kept_zero, got_zero)
     normed_t, kept_one, kept_zero = tie(normed_t, kept_one, kept_zero)
-    kept_one, sent_one = split(kept_one, 2)
-    kept_zero, sent_zero = split(kept_zero, 2)
     got_one = swap(sent_one, "dp", dp_bits[1][2])
     got_zero = swap(sent_zero, "dp", dp_bits[0][2])
     latent_back = turn(latent_back)
@@ -956,17 +980,11 @@
 
     stage = 0
     attend_kept = more(attend_kept)
-    attend_sum = more(add_low(attend_kept, attend_got))
-    mlp_one = halve(add_low(kept_one, got_one), "dp", dp_bits[1][3:], 2)
-    mlp_zero = halve(add_low(kept_zero, got_zero), "dp", dp_bits[0][3:], 2)
-    mlp_one = more(mlp_one)
-    attend_zero, attend_one = split(attend_sum, 0)
-    latent_back, attend_one, attend_zero = tie(latent_back, attend_one, attend_zero)
-    attend_one, sent_one = split(attend_one, 1)
-    attend_zero, sent_zero = split(attend_zero, 1)
+    halves = sum_halves(attend_kept, attend_got)
+    (attend_zero, attend_one), (sent_zero, sent_one) = split(halves[0], 0), split(halves[1], 0)
     attend_got_one = swap(sent_one, "dp", dp_bits[1][1])
     attend_got_zero = swap(sent_zero, "dp", dp_bits[0][1])
-    mlp_got = swap(mlp_one, "mp", mp_bits[0])
+    latent_back, attend_one, attend_zero = tie(latent_back, attend_one, attend_zero)
 
     back_within = pair_slot * dp_size + jnp.mod(my_place - starts[pair_peer], dp_size)
     back_valid = back_within < image_counts[pair_peer]
@@ -977,12 +995,20 @@
     latent_back = jnp.concatenate([latent_back, empty], axis=0)
     back_patches = take_rows(latent_back, back_slot)
 
+    got_packed, _ = tie(got_packed, back_patches)
     got_patches = lax.all_to_all(back_patches, "dp", split_axis=0, concat_axis=0, tiled=True)
     slot_ids = jnp.arange(capacity)
     home_peer = dest_perm[jnp.mod(my_start + slot_ids, dp_size)]
     home_index = home_peer * slot_count + jnp.minimum(slot_ids // dp_size, slot_count - 1)
     patch_grad = take_rows(got_patches, home_index)
 
+    mlp_one = more(halve(add_low(kept_one, got_one), "dp", dp_bits[1][3:], 2))
+    mlp_zero = more(halve(add_low(kept_zero, got_zero), "dp", dp_bits[0][3:], 2))
+    mlp_got = swap(mlp_one, "mp", mp_bits[0])
+    attend_one, sent_one = sum_halves(attend_one, attend_got_one)
+    attend_zero, sent_zero = sum_halves(attend_zero, attend_got_zero)
+    attend_got_one = swap(sent_one, "dp", dp_bits[1][2])
+    attend_got_zero = swap(sent_zero, "dp", dp_bits[0][2])
     while stage < len(gather_bits):
         mlp_zero = more(mlp_zero)
     packed = packed.reshape(total_images, 8, model_width)
@@ -1006,8 +1032,8 @@
     time_grad = ein("in,id->nd", bin_hot, condition_low)
     class_grad = ein("in,id->nd", label_hot, condition_low)
 
-    attend_one = halve(add_low(attend_one, attend_got_one), "dp", dp_bits[1][2:], 1)
-    attend_zero = halve(add_low(attend_zero, attend_got_zero), "dp", dp_bits[0][2:], 1)
+    attend_one = halve(add_low(attend_one, attend_got_one), "dp", dp_bits[1][3:], 1)
+    attend_zero = halve(add_low(attend_zero, attend_got_zero), "dp", dp_bits[0][3:], 1)
     mlp_grad = halve(add_low(mlp_zero, mlp_got), "mp", mp_bits[1:], 0)[0].astype(f32)
     attend_grad = add_low(attend_zero, swap(attend_one, "mp", mp_bits[0]))
     attend_grad = halve(attend_grad, "mp", mp_bits[1:], 0)[0].astype(f32)

time: 769 us -> 752 us (0.978)
  other arithmetic: 59.6 us -> 29.7 us
  Pallas kernels: 232 us -> 255 us
  waiting for transfers between devices: 294 us -> 280 us
    convert_element_type x12 -> x5, other arithmetic: 41.3 us -> 10.8 us  [add_low(): return (kept.astype(f32) + received.astype(f32)).astype(bf16)]
    all_to_all x1, waiting for transfers between devices: 0.01 us -> 27.7 us  [shards(): lax.all_to_all(send_patches, 'dp', split_axis=0, concat_axis=0, tiled=True)]
    ppermute x38, waiting for transfers between devices: 233 us -> 206 us  [swap(): return lax.ppermute(values, axis, [(i, i ^ bit) for i in range(size)])]
    pallas_call x0 -> x7, Pallas kernels: none -> 22.9 us  [sum_halves(): pl.pallas_call(sum_halves_kernel, grid=(kept.shape[0],), in_specs=[whole,...]
    unnamed x109 -> x121, local copies, waits for them, and re-layouts: 24.2 us -> 39.9 us
    all_to_all x4, waiting for transfers between devices: 61.3 us -> 46.8 us  [turn(): return lax.all_to_all(chunks, 'mp', split_axis=0, concat_axis=0, tiled=True)]
    slice x11 -> x3, local copies, waits for them, and re-layouts: 13.5 us -> 1.96 us  [split(): lax.slice_in_dim(values, size, 2 * size, axis=dim)]
  transfers between devices with their start and end apart: 45 -> 45, of which waited for: 17 -> 22; matrix products, arithmetic and copies ran while one was open for 15% -> 12% of each run, Pallas kernels for 17% -> 25%
where the time goes in v9:
time: 752 us; the launch traced here: 744 us
  waiting for transfers between devices  280 us (37%)
  Pallas kernels  255 us (34%)
  local copies, waits for them, and re-layouts  84.6 us (11%)
  starting transfers between devices  64.5 us (9%)
  other arithmetic  29.7 us (4%)
  matrix products  15.4 us (2%)
  between operations  15.2 us (2%)
    ppermute x38, waiting for transfers between devices, swap(): return lax.ppermute(values, axis, [(i, i ^ bit) for i in range(size)])  206 us
    pallas_call x2, Pallas kernels, mlp_back(): pl.pallas_call(mlp_back_kernel, grid_spec=pltpu.PrefetchScalarGridSpec(nu...  72.1 us
    all_to_all x4, waiting for transfers between devices, turn(): return lax.all_to_all(chunks, 'mp', split_axis=0, concat_axis=0, tiled=True)  46.8 us
    pallas_call x1, Pallas kernels, attend_back(): pl.pallas_call(attend_back_kernel, grid=(groups,), in_specs=[whole_spec(l...  44.9 us
    unnamed x121, local copies, waits for them, and re-layouts  39.9 us
    pallas_call x1, Pallas kernels, mlp(): pl.pallas_call(functools.partial(mlp_kernel, len(pieces)), grid_spec=pltp...  38 us
    pallas_call x1, Pallas kernels, attend(): pl.pallas_call(attend_kernel, grid=(groups,), in_specs=[whole_spec(latent...  36 us
    ppermute x38, starting transfers between devices, swap(): return lax.ppermute(values, axis, [(i, i ^ bit) for i in range(size)])  35 us
  transfers between devices with their start and end apart: 45, of which 22 were waited for; matrix products, arithmetic and copies ran while one was open for 12% of the time, Pallas kernels for 25%

profile of v9, /device:TPU:0, one launch (start us, length us, event | category | flops | bytes accessed | tf_op | source)
XLA Modules:
  0.0 744.2 jit_solution(16876082526672198791)
XLA Ops:
  15.2 2.6 collective-permute-start.1
  19.3 2.0 collective-permute-start.2
  22.1 5.6 gather_fusion.1
  30.7 2.5 copy.73
  35.6 2.7 collective-permute-start.3
  38.9 3.1 multiply_convert_fusion
  42.8 4.6 all-to-all-start
  47.6 26.2 %collective-permute-done.3 = bf16[1,3,96,1152]{3,2,1,0:T(8,128)(2,1)S(1)} collective-permute-done((bf16[1,3,96,1152]{3,2,1,0:T(8,128)(2,1)S(1)}, bf16[1,3,96,1152]{3,2,1,0:T(8,128)(2,1)S(1)}, u32[]{:S(2)}, u32[]{:S(2)}) %collective-permute-start.3) | collective-permute-done | bytes 663584 | tf_op jit(solution)/shard_map/ppermute | solution.py:655
  74.7 5.5 copy-done.13
  80.2 2.8 modulate.1
  83.9 27.7 %all-to-all-done = bf16[32,64,1152]{2,1,0:T(8,128)(2,1)} async-done(((bf16[32,64,1152]{2,1,0:T(8,128)(2,1)}), bf16[32,64,1152]{2,1,0:T(8,128)(2,1)}, u32[]{:S(2)}, u32[]{:S(2)}) %all-to-all-start) | async-done | bytes 4718624 | tf_op jit(solution)/shard_map/all_to_all | solution.py:819
  111.6 4.5 gather_fusion.3
  116.1 4.7 all-to-all-start.1
  120.8 1.8 pad_maximum_fusion.refs_0_
  122.8 1.9 fusion.62
  127.0 2.0 collective-permute-start.15
  132.6 36.0 %collective-permute-done.9.refs_4_ = bf16[4,3,48,1152]{3,2,1,0:T(8,128)(2,1)} collective-permute-done((bf16[4,3,48,1152]{3,2,1,0:T(8,128)(2,1)}, bf16[4,3,48,1152]{3,2,1,0:T(8,128)(2,1)}, u32[]{:S(2)}, u32[]{:S(2)}) %collective-permute-start.9) | collective-permute-done | bytes 1327136 | tf_op jit(solution)/shard_map/ppermute | solution.py:655
  168.6 28.1 %collective-permute-done.15.refs_10_ = bf16[4,3,48,1152]{3,2,1,0:T(8,128)(2,1)} collective-permute-done((bf16[4,3,48,1152]{3,2,1,0:T(8,128)(2,1)}, bf16[4,3,48,1152]{3,2,1,0:T(8,128)(2,1)}, u32[]{:S(2)}, u32[]{:S(2)}) %collective-permute-start.15) | collective-permute-done | bytes 1327136 | tf_op jit(solution)/shard_map/ppermute | solution.py:655
  196.7 3.5 all-to-all-done.1.latent_ref
  203.2 5.0 all-to-all-start.2
  208.3 36.0 %attend.1 = (f32[4,864,1024]{2,1,0:T(8,128)}, bf16[4,288,1024]{2,1,0:T(8,128)(2,1)}, bf16[1024,1152]{1,0:T(8,128)(2,1)}, bf16[1152,1024]{1,0:T(8,128)(2,1)}, f32...) custom-call(bf16[4,4,64,1152]{3,2,1,0:T(8,128)(2,1)} %all-to-all-done.1.latent_ref, ...), custom_call_target="tpu_custom_call" | custom-call | flops 176000008192 | bytes 1024 | tf_op jit(solution)/shard_map/attend/pallas_call | solution.py:286
  247.6 3.8 collective-permute-done.13.refs_7_
  252.4 38.0 %mlp.1 = (bf16[4,2,1024,768]{3,2,1,0:T(8,128)(2,1)}, f32[1024,1152]{1,0:T(8,128)}, bf16[4,3,768,1152]{3,2,1,0:T(8,128)(2,1)}) custom-call(s32[14]{0:T(128)} %stack.93.e_ref, bf16[1024,1152]{1,0:T(8,128)(2,1)} %get-tuple-element.117.x_ref, bf16[4,3,96,1152]{3,2,1,0:T(8,128)(2,1)} %copy-done.25, bf16[4,3,96,1152]{3,2,1,0:T(8,128)(2,1)} %collective-permute-done.7.refs_1_, ...), custom_call_target="tpu_custom_call" | custom-call | flops 1100000000 | bytes 1024 | tf_op jit(solution)/shard_map/mlp/pallas_call | solution.py:479
  290.4 6.8 finish.1
  300.0 36.1 %mlp_back.2 = (bf16[2,3,576,768]{3,2,1,0:T(8,128)(2,1)}, bf16[2,3,576,768]{3,2,1,0:T(8,128)(2,1)}, f32[1024,1152]{1,0:T(8,128)}) custom-call(s32[8]{0:T(128)} %broadcast_xor_fusion.3.e_ref, bf16[8,144,1024]{2,1,0:T(8,128)(2,1)} %bitcast.188, bf16[8,144,1024]{2,1,0:T(8,128)(2,1)} %bitcast.170, bf16[1024,1152]{1,0:T(8,128)(2,1)} %copy-done.16, ...), custom_call_target="tpu_custom_call" | custom-call | flops 165000003584 | bytes 1024 | tf_op jit(solution)/shard_map/mlp_back/pallas_call | solution.py:555
  336.3 36.0 %mlp_back.3 = (bf16[2,3,576,768]{3,2,1,0:T(8,128)(2,1)}, bf16[2,3,576,768]{3,2,1,0:T(8,128)(2,1)}, f32[1024,1152]{1,0:T(8,128)}) custom-call(s32[8]{0:T(128)} %broadcast_xor_fusion.2.e_ref, bf16[8,144,1024]{2,1,0:T(8,128)(2,1)} %bitcast.189, bf16[8,144,1024]{2,1,0:T(8,128)(2,1)} %bitcast.171, bf16[1024,1152]{1,0:T(8,128)(2,1)} %copy-done.16, ...), custom_call_target="tpu_custom_call" | custom-call | flops 165000003584 | bytes 1024 | tf_op jit(solution)/shard_map/mlp_back/pallas_call | solution.py:555
  372.6 5.6 all-to-all-start.3
  379.4 2.7 copy-done.3
  382.1 4.7 sum_halves.8
  389.8 4.5 sum_halves.7
  397.3 35.0 %all-to-all-done.3 = bf16[4,4,64,1152]{3,2,1,0:T(8,128)(2,1)} async-done(((bf16[4,4,64,1152]{3,2,1,0:T(8,128)(2,1)}), bf16[4,4,64,1152]{3,2,1,0:T(8,128)(2,1)}, u32[]{:S(2)}, u32[]{:S(2)}) %all-to-all-start.3) | async-done | bytes 2359328 | tf_op jit(solution)/shard_map/all_to_all | solution.py:770
  433.6 9.8 %middle.1 = (f32[1024,1152]{1,0:T(8,128)}, bf16[1024,1152]{1,0:T(8,128)(2,1)S(1)}, bf16[1152,1024]{1,0:T(8,128)(2,1)S(1)}, f32[4,8,1152]{2,1,0:T(8,128)S(1)}) custom-call(f32[1024,1152]{1,0:T(8,128)} %get-tuple-element.143.one_ref, f32[1024,1152]{1,0:T(8,128)} %get-tuple-element.144.other_ref, f32[1024,1152]{1,0:T(8,128)} %get-tuple-element.127.middle_ref, ...), custom_call_target="tpu_custom_call" | custom-call | flops 109999996928 | bytes 1024 | tf_op jit(solution)/shard_map/middle/pallas_call | solution.py:409
  446.2 44.9 %attend_back.1 = (bf16[4,864,1024]{2,1,0:T(8,128)(2,1)}, f32[2,72,256]{2,1,0:T(8,128)}, f32[4,8,1152]{2,1,0:T(8,128)}, bf16[4,4,64,1152]{3,2,1,0:T(8,128)(2,1)}) custom-call(bf16[4,4,64,1152]{3,2,1,0:T(8,128)(2,1)} %all-to-all-done.1.latent_ref, f32[4,864,1024]{2,1,0:T(8,128)} %get-tuple-element.142.proj_ref, bf16[1024,1152]{1,0:T(8,128)(2,1)} %copy-done.9, ...), custom_call_target="tpu_custom_call" | custom-call | flops 1100000000 | bytes 1024 | tf_op jit(solution)/shard_map/attend_back/pallas_call | solution.py:330
  491.6 1.7 copy-done.5
  493.4 3.7 sum_halves.10
  498.2 3.6 sum_halves.9
  502.8 21.5 %attend_grads.1 = (bf16[4,576,1152]{2,1,0:T(8,128)(2,1)}, bf16[4,576,1152]{2,1,0:T(8,128)(2,1)}) custom-call(s32[4]{0:T(128)} %broadcast_xor_fusion.m_ref, s32[16]{0:T(128)} %pad_add_fusion.3.e_ref, bf16[8,144,1024]{2,1,0:T(8,128)(2,1)} %bitcast.187, bf16[8,144,1024]{2,1,0:T(8,128)(2,1)} %bitcast.174, bf16[4,864,1024]{2,1,0:T(8,128)(2,1)} %get-tuple-element.161.proj_ref, ...), custom_call_target="tpu_custom_call" | custom-call | flops 219999993856 | bytes 1024 | tf_op jit(solution)/shard_map/attend_grads/pallas_call | solution.py:608
  524.4 4.7 all-to-all-start.4
  536.1 26.3 %collective-permute-done.23 = bf16[2,3,144,768]{3,2,1,0:T(8,128)(2,1)} collective-permute-done((bf16[2,3,144,768]{3,2,1,0:T(8,128)(2,1)S(1)}, bf16[2,3,144,768]{3,2,1,0:T(8,128)(2,1)}, u32[]{:S(2)}, u32[]{:S(2)}) %collective-permute-start.23) | collective-permute-done | bytes 1327136 | tf_op jit(solution)/shard_map/ppermute | solution.py:655
  564.9 2.8 add_convert_fusion.2
  567.7 2.5 copy-done.2
  570.2 3.8 sum_halves.11
  575.6 8.2 %all-to-all-done.4 = bf16[4,4,64,1152]{3,2,1,0:T(8,128)(2,1)} async-done(((bf16[4,4,64,1152]{3,2,1,0:T(8,128)(2,1)}), bf16[4,4,64,1152]{3,2,1,0:T(8,128)(2,1)}, u32[]{:S(2)}, u32[]{:S(2)}) %all-to-all-start.4) | async-done | bytes 2359328 | tf_op jit(solution)/shard_map/all_to_all | solution.py:770
  583.9 3.5 concatenate.65
  587.4 5.0 gather_fusion.7
  593.4 3.1 fusion.60
  597.6 2.8 add_convert_fusion.1
  600.3 2.0 collective-permute-done.27
  603.2 2.0 collective-permute-start.36
  608.2 19.5 %collective-permute-done.28 = bf16[8,4,8,1152]{3,2,1,0:T(8,128)(2,1)S(1)} collective-permute-done((bf16[8,4,8,1152]{3,2,1,0:T(8,128)(2,1)S(1)}, bf16[8,4,8,1152]{3,2,1,0:T(8,128)(2,1)S(1)}, u32[]{:S(2)}, u32[]{:S(2)}) %collective-permute-start.28) | collective-permute-done | bytes 589856 | tf_op jit(solution)/shard_map/ppermute | solution.py:655
  632.7 4.8 all-to-all-start.5
  639.1 2.0 collective-permute-start.31
  641.2 7.4 %collective-permute-done.33 = bf16[2,144,1152]{2,1,0:T(8,128)(2,1)} collective-permute-done((bf16[2,144,1152]{2,1,0:T(8,128)(2,1)}, bf16[2,144,1152]{2,1,0:T(8,128)(2,1)}, u32[]{:S(2)}, u32[]{:S(2)}) %collective-permute-start.33) | collective-permute-done | bytes 663584 | tf_op jit(solution)/shard_map/ppermute | solution.py:655
  648.6 2.1 add_convert_fusion.5
  652.0 28.5 %collective-permute-done.29 = bf16[16,4,8,1152]{3,2,1,0:T(8,128)(2,1)} collective-permute-done((bf16[16,4,8,1152]{3,2,1,0:T(8,128)(2,1)}, bf16[16,4,8,1152]{3,2,1,0:T(8,128)(2,1)}, u32[]{:S(2)}, u32[]{:S(2)}) %collective-permute-start.29) | collective-permute-done | bytes 1179680 | tf_op jit(solution)/shard_map/ppermute | solution.py:655
  680.5 1.6 add_convert_fusion
  685.8 2.8 fusion.28
  688.5 2.8 fusion.12
  693.8 11.7 %collective-permute-done.31 = bf16[2,144,1152]{2,1,0:T(8,128)(2,1)} collective-permute-done((bf16[2,144,1152]{2,1,0:T(8,128)(2,1)S(1)}, bf16[2,144,1152]{2,1,0:T(8,128)(2,1)}, u32[]{:S(2)}, u32[]{:S(2)}) %collective-permute-start.31) | collective-permute-done | bytes 663584 | tf_op jit(solution)/shard_map/ppermute | solution.py:655
  707.1 2.3 collective-permute-start.35
  710.7 1.6 copy.88
  713.1 11.4 %collective-permute-done.35 = bf16[1,144,1152]{2,1,0:T(8,128)(2,1)S(1)} collective-permute-done((bf16[1,144,1152]{2,1,0:T(8,128)(2,1)S(1)}, bf16[1,144,1152]{2,1,0:T(8,128)(2,1)S(1)}, u32[]{:S(2)}, u32[]{:S(2)}) %collective-permute-start.35) | collective-permute-done | bytes 331808 | tf_op jit(solution)/shard_map/ppermute | solution.py:655
  728.2 5.7 gather_fusion.9
  733.9 3.3 copy.111
  (302 shorter events, 87.6 us)
Async XLA Ops:
  7.2 21.1 %copy-start = (bf16[1152,3,288]{0,2,1:T(8,128)(2,1)S(1)}, bf16[1152,3,288]{0,2,1:T(8,128)(2,1)}, u32[]{:S(2)}) copy-start(bf16[1152,3,288]{0,2,1:T(8,128)(2,1)} %param.36) | copy-start | bytes 5971972
  7.2 201.0 %all-gather.3.cloned.1.call-start = ((), (), s32[]{:S(2)}) async-start(), calls=%async_computation.6 | async-start | bytes 10948608 | tf_op jit(solution)/shard_map/all_gather | solution.py:641
  8.1 7.1 collective-permute-start
  11.9 18.7 %copy-start.20 = (s32[8]{0:T(128)}, s32[8]{0:T(128)S(1)}, u32[]{:S(2)}) copy-start(s32[8]{0:T(128)S(1)} %bitcast_subtract_fusion.2) | copy-start | bytes 100
  15.2 4.1 collective-permute-start.1
  19.3 8.5 %collective-permute-start.2 = (s32[4,2,32]{2,1,0:T(2,128)S(1)}, s32[4,2,32]{2,1,0:T(2,128)S(1)}, u32[]{:S(2)}, u32[]{:S(2)}) collective-permute-start(s32[4,2,32]{2,1,0:T(2,128)S(1)} %pad_add_fusion.1), channel_id=1, source_target_pairs={{0,16},{4,20},{8,24},{12,28},{16,0},{20,4},{24,8},{28,12},{1,17},{... | collective-permute-start | bytes 3080 | tf_op jit(solution)/shard_map/ppermute | solution.py:655
  35.6 38.2 %collective-permute-start.3 = (bf16[1,3,96,1152]{3,2,1,0:T(8,128)(2,1)S(1)}, bf16[1,3,96,1152]{3,2,1,0:T(8,128)(2,1)S(1)}, u32[]{:S(2)}, u32[]{:S(2)}) collective-permute-start(bf16[1,3,96,1152]{3,2,1,0:T(8,128)(2,1)S(1)} %maximum_bitcast_fusion), channel_id=1, source_target_pairs={{0,2},{1,3},{2,0},{3,1},{4,6},{5,7},{6,4},{7,5},{8,10},{9,11},{10,... | collective-permute-start | bytes 1990664 | tf_op jit(solution)/shard_map/ppermute | solution.py:655
  38.6 8.9 %copy-start.38 = (s32[128]{0:T(128)}, s32[128]{0:T(128)S(1)}, u32[]{:S(2)}) copy-start(s32[128]{0:T(128)S(1)} %get-tuple-element.239) | copy-start | bytes 1540
  42.8 68.8 %all-to-all-start = ((bf16[32,64,1152]{2,1,0:T(8,128)(2,1)}), bf16[32,64,1152]{2,1,0:T(8,128)(2,1)}, u32[]{:S(2)}, u32[]{:S(2)}) async-start(bf16[32,64,1152]{2,1,0:T(8,128)(2,1)} %gather_fusion.1), calls=%async_computation | async-start | bytes 9437184 | tf_op jit(solution)/shard_map/all_to_all | solution.py:819
  73.8 9.2 %copy-start.28 = (bf16[1,3,96,1152]{3,2,1,0:T(8,128)(2,1)}, bf16[1,3,96,1152]{3,2,1,0:T(8,128)(2,1)S(1)}, u32[]{:S(2)}) copy-start(bf16[1,3,96,1152]{3,2,1,0:T(8,128)(2,1)S(1)} %collective-permute-done.3) | copy-start | bytes 1990660
  74.0 46.9 %collective-permute-start.4 = (bf16[2,3,96,1152]{3,2,1,0:T(8,128)(2,1)S(1)}, bf16[2,3,96,1152]{3,2,1,0:T(8,128)(2,1)}, u32[]{:S(2)}, u32[]{:S(2)}) collective-permute-start(bf16[2,3,96,1152]{3,2,1,0:T(8,128)(2,1)S(1)} %pad_maximum_fusion.1), channel_id=1, source_target_pairs={{0,1},{1,0},{2,3},{3,2},{4,5},{5,4},{6,7},{7,6},{8,9},{9,8},{10,11... | collective-permute-start | bytes 3981320 | tf_op jit(solution)/shard_map/ppermute | solution.py:655
  116.1 84.1 %all-to-all-start.1 = ((bf16[4,4,64,1152]{3,2,1,0:T(8,128)(2,1)}), bf16[4,4,64,1152]{3,2,1,0:T(8,128)(2,1)}, u32[]{:S(2)}, u32[]{:S(2)}) async-start(bf16[4,4,64,1152]{3,2,1,0:T(8,128)(2,1)} %bitcast.23), calls=%async_computation.1 | async-start | bytes 4718592 | tf_op jit(solution)/shard_map/all_to_all | solution.py:770
  122.7 74.1 %collective-permute-start.7 = (bf16[4,3,96,1152]{3,2,1,0:T(8,128)(2,1)S(1)}, bf16[4,3,96,1152]{3,2,1,0:T(8,128)(2,1)}, u32[]{:S(2)}, u32[]{:S(2)}) collective-permute-start(bf16[4,3,96,1152]{3,2,1,0:T(8,128)(2,1)S(1)} %pad_maximum_fusion.refs_0_), channel_id=1, source_target_pairs={{0,4},{4,0},{8,12},{12,8},{16,20},{20,16},{24,28},{28,24},{1,5},{5... | collective-permute-start | bytes 7962632 | tf_op jit(solution)/shard_map/ppermute | solution.py:655
  122.8 6.7 copy-start.42
  122.8 9.1 %copy-start.40 = (f32[2]{0:T(128)S(1)}, f32[2]{0:T(128)}, u32[]{:S(2)}) copy-start(f32[2]{0:T(128)} %constant.218) | copy-start | bytes 28
  125.0 71.8 %collective-permute-start.5 = (bf16[4,3,48,1152]{3,2,1,0:T(8,128)(2,1)}, bf16[4,3,48,1152]{3,2,1,0:T(8,128)(2,1)}, u32[]{:S(2)}, u32[]{:S(2)}) collective-permute-start(bf16[4,3,48,1152]{3,2,1,0:T(8,128)(2,1)} %get-tuple-element.247), channel_id=1, source_target_pairs={{0,8},{4,12},{8,0},{12,4},{16,24},{20,28},{24,16},{28,20},{1,9},{5... | collective-permute-start | bytes 3981320 | tf_op jit(solution)/shard_map/ppermute | solution.py:655
  125.0 43.6 %collective-permute-start.9 = (bf16[4,3,48,1152]{3,2,1,0:T(8,128)(2,1)}, bf16[4,3,48,1152]{3,2,1,0:T(8,128)(2,1)}, u32[]{:S(2)}, u32[]{:S(2)}) collective-permute-start(bf16[4,3,48,1152]{3,2,1,0:T(8,128)(2,1)} %get-tuple-element.247), channel_id=1, source_target_pairs={{0,16},{4,20},{8,24},{12,28},{16,0},{20,4},{24,8},{28,12},{1,17},{... | collective-permute-start | bytes 3981320 | tf_op jit(solution)/shard_map/ppermute | solution.py:655
  126.5 70.2 %collective-permute-start.6 = (bf16[4,3,48,1152]{3,2,1,0:T(8,128)(2,1)}, bf16[4,3,48,1152]{3,2,1,0:T(8,128)(2,1)}, u32[]{:S(2)}, u32[]{:S(2)}) collective-permute-start(bf16[4,3,48,1152]{3,2,1,0:T(8,128)(2,1)} %get-tuple-element.246), channel_id=1, source_target_pairs={{0,16},{4,20},{8,24},{12,28},{16,0},{20,4},{24,8},{28,12},{1,17},{... | collective-permute-start | bytes 3981320 | tf_op jit(solution)/shard_map/ppermute | solution.py:655
  127.0 69.7 %collective-permute-start.15 = (bf16[4,3,48,1152]{3,2,1,0:T(8,128)(2,1)}, bf16[4,3,48,1152]{3,2,1,0:T(8,128)(2,1)}, u32[]{:S(2)}, u32[]{:S(2)}) collective-permute-start(bf16[4,3,48,1152]{3,2,1,0:T(8,128)(2,1)} %get-tuple-element.246), channel_id=1, source_target_pairs={{0,8},{4,12},{8,0},{12,4},{16,24},{20,28},{24,16},{28,20},{1,9},{5... | collective-permute-start | bytes 3981320 | tf_op jit(solution)/shard_map/ppermute | solution.py:655
  168.6 76.2 %collective-permute-start.10 = (bf16[4,3,48,1152]{3,2,1,0:T(8,128)(2,1)}, bf16[4,3,48,1152]{3,2,1,0:T(8,128)(2,1)}, u32[]{:S(2)}, u32[]{:S(2)}) collective-permute-start(bf16[4,3,48,1152]{3,2,1,0:T(8,128)(2,1)} %collective-permute-done.9.refs_4_), channel_id=1, source_target_pairs={{0,4},{4,0},{8,12},{12,8},{16,20},{20,16},{24,28},{28,24},{1,5},{5... | collective-permute-start | bytes 3981320 | tf_op jit(solution)/shard_map/ppermute | solution.py:655
  196.7 50.0 %collective-permute-start.16 = (bf16[4,3,48,1152]{3,2,1,0:T(8,128)(2,1)}, bf16[4,3,48,1152]{3,2,1,0:T(8,128)(2,1)}, u32[]{:S(2)}, u32[]{:S(2)}) collective-permute-start(bf16[4,3,48,1152]{3,2,1,0:T(8,128)(2,1)} %collective-permute-done.15.refs_10_), channel_id=1, source_target_pairs={{0,4},{4,0},{8,12},{12,8},{16,20},{20,16},{24,28},{28,24},{1,5},{5... | collective-permute-start | bytes 3981320 | tf_op jit(solution)/shard_map/ppermute | solution.py:655
  200.3 44.2 %collective-permute-start.12 = (bf16[4,3,48,1152]{3,2,1,0:T(8,128)(2,1)}, bf16[4,3,48,1152]{3,2,1,0:T(8,128)(2,1)}, u32[]{:S(2)}, u32[]{:S(2)}) collective-permute-start(bf16[4,3,48,1152]{3,2,1,0:T(8,128)(2,1)} %collective-permute-done.6.refs_8_), channel_id=1, source_target_pairs={{0,8},{4,12},{8,0},{12,4},{16,24},{20,28},{24,16},{28,20},{1,9},{5... | collective-permute-start | bytes 3981320 | tf_op jit(solution)/shard_map/ppermute | solution.py:655
  201.7 45.1 %collective-permute-start.14 = (bf16[4,3,48,1152]{3,2,1,0:T(8,128)(2,1)}, bf16[4,3,48,1152]{3,2,1,0:T(8,128)(2,1)}, u32[]{:S(2)}, u32[]{:S(2)}) collective-permute-start(bf16[4,3,48,1152]{3,2,1,0:T(8,128)(2,1)} %collective-permute-done.6.refs_8_), channel_id=1, source_target_pairs={{0,4},{4,0},{8,12},{12,8},{16,20},{20,16},{24,28},{28,24},{1,5},{5... | collective-permute-start | bytes 3981320 | tf_op jit(solution)/shard_map/ppermute | solution.py:655
  201.7 42.5 %collective-permute-start.11 = (bf16[4,3,48,1152]{3,2,1,0:T(8,128)(2,1)}, bf16[4,3,48,1152]{3,2,1,0:T(8,128)(2,1)}, u32[]{:S(2)}, u32[]{:S(2)}) collective-permute-start(bf16[4,3,48,1152]{3,2,1,0:T(8,128)(2,1)} %collective-permute-done.5.refs_2_), channel_id=1, source_target_pairs={{0,16},{4,20},{8,24},{12,28},{16,0},{20,4},{24,8},{28,12},{1,17},{... | collective-permute-start | bytes 3981320 | tf_op jit(solution)/shard_map/ppermute | solution.py:655
  203.2 87.2 %all-to-all-start.2 = ((bf16[4,4,64,1152]{3,2,1,0:T(8,128)(2,1)}), bf16[4,4,64,1152]{3,2,1,0:T(8,128)(2,1)}, u32[]{:S(2)}, u32[]{:S(2)}) async-start(bf16[4,4,64,1152]{3,2,1,0:T(8,128)(2,1)} %bitcast.180), calls=%async_computation.2 | async-start | bytes 4718592 | tf_op jit(solution)/shard_map/all_to_all | solution.py:770
  208.2 37.5 %copy-start.49 = (s32[8]{0:T(128)S(1)}, s32[8]{0:T(128)}, u32[]{:S(2)}) copy-start(s32[8]{0:T(128)} %constant.206.clone) | copy-start | bytes 100
  208.2 38.0 %copy-start.48 = (s32[8]{0:T(128)S(1)}, s32[8]{0:T(128)}, u32[]{:S(2)}) copy-start(s32[8]{0:T(128)} %constant.207.clone) | copy-start | bytes 100
  244.2 3.3 collective-permute-start.8
  244.5 6.8 collective-permute-start.13
  244.8 6.7 collective-permute-start.17
  252.4 38.0 %copy-start.10 = (f32[4,8,1152]{2,1,0:T(8,128)S(1)}, f32[4,8,1152]{2,1,0:T(8,128)}, u32[]{:S(2)}) copy-start(f32[4,8,1152]{2,1,0:T(8,128)} %maximum_maximum_fusion.mods_ref) | copy-start | bytes 442372
  336.1 43.3 %collective-permute-start.19 = (bf16[2,3,576,768]{3,2,1,0:T(8,128)(2,1)}, bf16[2,3,576,768]{3,2,1,0:T(8,128)(2,1)}, u32[]{:S(2)}, u32[]{:S(2)}) collective-permute-start(bf16[2,3,576,768]{3,2,1,0:T(8,128)(2,1)} %get-tuple-element.138), channel_id=1, source_target_pairs={{0,4},{4,0},{8,12},{12,8},{16,20},{20,16},{24,28},{28,24},{1,5},{5... | collective-permute-start | bytes 15925256 | tf_op jit(solution)/shard_map/ppermute | solution.py:655
  372.3 16.0 %collective-permute-start.18 = (bf16[2,3,576,768]{3,2,1,0:T(8,128)(2,1)}, bf16[2,3,576,768]{3,2,1,0:T(8,128)(2,1)}, u32[]{:S(2)}, u32[]{:S(2)}) collective-permute-start(bf16[2,3,576,768]{3,2,1,0:T(8,128)(2,1)} %get-tuple-element.135), channel_id=1, source_target_pairs={{0,4},{4,0},{8,12},{12,8},{16,20},{20,16},{24,28},{28,24},{1,5},{5... | collective-permute-start | bytes 15925256 | tf_op jit(solution)/shard_map/ppermute | solution.py:655
  372.6 59.8 %all-to-all-start.3 = ((bf16[4,4,64,1152]{3,2,1,0:T(8,128)(2,1)}), bf16[4,4,64,1152]{3,2,1,0:T(8,128)(2,1)}, u32[]{:S(2)}, u32[]{:S(2)}) async-start(bf16[4,4,64,1152]{3,2,1,0:T(8,128)(2,1)} %get-tuple-element.140), calls=%async_computation.3 | async-start | bytes 4718592 | tf_op jit(solution)/shard_map/all_to_all | solution.py:770
  379.4 10.4 %slice-start = ((s8[5308416]{0:T(1024)(128)(4,1)}), s8[4194304]{0:T(1024)(128)(4,1)S(1)}, s32[]{:S(2)}) async-start(s8[5308416]{0:T(1024)(128)(4,1)} %bitcast.161), calls=%async_computation.7 | async-start | bytes 8388608
  382.1 7.8 %slice-start.1 = ((s8[5308416]{0:T(1024)(128)(4,1)}), s8[1114112]{0:T(1024)(128)(4,1)S(1)}, s32[]{:S(2)}) async-start(s8[5308416]{0:T(1024)(128)(4,1)} %bitcast.161), calls=%async_computation.8 | async-start | bytes 2228224
  432.4 58.9 %collective-permute-start.21 = (bf16[2,3,288,768]{3,2,1,0:T(8,128)(2,1)}, bf16[2,3,288,768]{3,2,1,0:T(8,128)(2,1)}, u32[]{:S(2)}, u32[]{:S(2)}) collective-permute-start(bf16[2,3,288,768]{3,2,1,0:T(8,128)(2,1)} %bitcast.168), channel_id=1, source_target_pairs={{0,8},{4,12},{8,0},{12,4},{16,24},{20,28},{24,16},{28,20},{1,9},{5... | collective-permute-start | bytes 7962632 | tf_op jit(solution)/shard_map/ppermute | solution.py:655
  433.0 58.6 %collective-permute-start.20 = (bf16[2,3,288,768]{3,2,1,0:T(8,128)(2,1)}, bf16[2,3,288,768]{3,2,1,0:T(8,128)(2,1)}, u32[]{:S(2)}, u32[]{:S(2)}) collective-permute-start(bf16[2,3,288,768]{3,2,1,0:T(8,128)(2,1)} %bitcast.169), channel_id=1, source_target_pairs={{0,16},{4,20},{8,24},{12,28},{16,0},{20,4},{24,8},{28,12},{1,17},{... | collective-permute-start | bytes 7962632 | tf_op jit(solution)/shard_map/ppermute | solution.py:655
  524.4 43.3 %collective-permute-start.25 = (bf16[4,576,1152]{2,1,0:T(8,128)(2,1)}, bf16[4,576,1152]{2,1,0:T(8,128)(2,1)}, u32[]{:S(2)}, u32[]{:S(2)}) collective-permute-start(bf16[4,576,1152]{2,1,0:T(8,128)(2,1)} %get-tuple-element.172), channel_id=1, source_target_pairs={{0,4},{4,0},{8,12},{12,8},{16,20},{20,16},{24,28},{28,24},{1,5},{5... | collective-permute-start | bytes 15925256 | tf_op jit(solution)/shard_map/ppermute | solution.py:655
  524.4 10.0 %copy-start.33 = (f32[2,72,256]{2,1,0:T(8,128)S(1)}, f32[2,72,256]{2,1,0:T(8,128)}, u32[]{:S(2)}) copy-start(f32[2,72,256]{2,1,0:T(8,128)} %get-tuple-element.167) | copy-start | bytes 442372
  524.4 10.2 %copy-start.41 = (f32[2]{0:T(128)S(1)}, f32[2]{0:T(128)}, u32[]{:S(2)}) copy-start(f32[2]{0:T(128)} %constant.218) | copy-start | bytes 28
  524.4 10.3 %copy-start.34 = (f32[4,8,1152]{2,1,0:T(8,128)S(1)}, f32[4,8,1152]{2,1,0:T(8,128)}, u32[]{:S(2)}) copy-start(f32[4,8,1152]{2,1,0:T(8,128)} %get-tuple-element.170) | copy-start | bytes 442372
  524.4 59.5 %all-to-all-start.4 = ((bf16[4,4,64,1152]{3,2,1,0:T(8,128)(2,1)}), bf16[4,4,64,1152]{3,2,1,0:T(8,128)(2,1)}, u32[]{:S(2)}, u32[]{:S(2)}) async-start(bf16[4,4,64,1152]{3,2,1,0:T(8,128)(2,1)} %get-tuple-element.148), calls=%async_computation.4 | async-start | bytes 4718592 | tf_op jit(solution)/shard_map/all_to_all | solution.py:770
  530.8 31.7 %collective-permute-start.23 = (bf16[2,3,144,768]{3,2,1,0:T(8,128)(2,1)S(1)}, bf16[2,3,144,768]{3,2,1,0:T(8,128)(2,1)}, u32[]{:S(2)}, u32[]{:S(2)}) collective-permute-start(bf16[2,3,144,768]{3,2,1,0:T(8,128)(2,1)S(1)} %bitcast.172), channel_id=1, source_target_pairs={{0,16},{4,20},{8,24},{12,28},{16,0},{20,4},{24,8},{28,12},{1,17},{... | collective-permute-start | bytes 3981320 | tf_op jit(solution)/shard_map/ppermute | solution.py:655
  531.8 31.5 %collective-permute-start.22 = (bf16[2,3,144,768]{3,2,1,0:T(8,128)(2,1)}, bf16[2,3,144,768]{3,2,1,0:T(8,128)(2,1)}, u32[]{:S(2)}, u32[]{:S(2)}) collective-permute-start(bf16[2,3,144,768]{3,2,1,0:T(8,128)(2,1)} %bitcast.173), channel_id=1, source_target_pairs={{0,8},{4,12},{8,0},{12,4},{16,24},{20,28},{24,16},{28,20},{1,9},{5... | collective-permute-start | bytes 3981320 | tf_op jit(solution)/shard_map/ppermute | solution.py:655
  535.4 27.9 %collective-permute-start.24 = (bf16[1,4,8,1152]{3,2,1,0:T(8,128)(2,1)S(1)}, bf16[1,4,8,1152]{3,2,1,0:T(8,128)(2,1)S(1)}, u32[]{:S(2)}, u32[]{:S(2)}) collective-permute-start(bf16[1,4,8,1152]{3,2,1,0:T(8,128)(2,1)S(1)} %get-tuple-element.241), channel_id=1, source_target_pairs={{0,4},{4,0},{8,12},{12,8},{16,20},{20,16},{24,28},{28,24},{1,5},{5... | collective-permute-start | bytes 221192 | tf_op jit(solution)/shard_map/ppermute | solution.py:655
  563.4 28.9 %collective-permute-start.26 = (bf16[2,4,8,1152]{3,2,1,0:T(8,128)(2,1)S(1)}, bf16[2,4,8,1152]{3,2,1,0:T(8,128)(2,1)S(1)}, u32[]{:S(2)}, u32[]{:S(2)}) collective-permute-start(bf16[2,4,8,1152]{3,2,1,0:T(8,128)(2,1)S(1)} %pad_maximum_fusion.4), channel_id=1, source_target_pairs={{0,8},{4,12},{8,0},{12,4},{16,24},{20,28},{24,16},{28,20},{1,9},{5... | collective-permute-start | bytes 442376 | tf_op jit(solution)/shard_map/ppermute | solution.py:655
  592.4 10.0 %collective-permute-start.27 = (bf16[4,4,8,1152]{3,2,1,0:T(8,128)(2,1)S(1)}, bf16[4,4,8,1152]{3,2,1,0:T(8,128)(2,1)S(1)}, u32[]{:S(2)}, u32[]{:S(2)}) collective-permute-start(bf16[4,4,8,1152]{3,2,1,0:T(8,128)(2,1)S(1)} %pad_maximum_fusion.3), channel_id=1, source_target_pairs={{0,16},{4,20},{8,24},{12,28},{16,0},{20,4},{24,8},{28,12},{1,17},{... | collective-permute-start | bytes 884744 | tf_op jit(solution)/shard_map/ppermute | solution.py:655
  596.5 33.0 %collective-permute-start.32 = (bf16[2,288,1152]{2,1,0:T(8,128)(2,1)S(1)}, bf16[2,288,1152]{2,1,0:T(8,128)(2,1)S(1)}, u32[]{:S(2)}, u32[]{:S(2)}) collective-permute-start(bf16[2,288,1152]{2,1,0:T(8,128)(2,1)S(1)} %get-tuple-element.243), channel_id=1, source_target_pairs={{0,16},{4,20},{8,24},{12,28},{16,0},{20,4},{24,8},{28,12},{1,17},{... | collective-permute-start | bytes 3981320 | tf_op jit(solution)/shard_map/ppermute | solution.py:655
  602.4 25.3 %collective-permute-start.28 = (bf16[8,4,8,1152]{3,2,1,0:T(8,128)(2,1)S(1)}, bf16[8,4,8,1152]{3,2,1,0:T(8,128)(2,1)S(1)}, u32[]{:S(2)}, u32[]{:S(2)}) collective-permute-start(bf16[8,4,8,1152]{3,2,1,0:T(8,128)(2,1)S(1)} %pad_maximum_fusion.2), channel_id=1, source_target_pairs={{0,2},{1,3},{2,0},{3,1},{4,6},{5,7},{6,4},{7,5},{8,10},{9,11},{10,... | collective-permute-start | bytes 1769480 | tf_op jit(solution)/shard_map/ppermute | solution.py:655
  603.2 77.3 %collective-permute-start.36 = (bf16[2,3,144,768]{3,2,1,0:T(8,128)(2,1)}, bf16[2,3,144,768]{3,2,1,0:T(8,128)(2,1)}, u32[]{:S(2)}, u32[]{:S(2)}) collective-permute-start(bf16[2,3,144,768]{3,2,1,0:T(8,128)(2,1)} %add_convert_fusion.2), channel_id=1, source_target_pairs={{0,1},{1,0},{2,3},{3,2},{4,5},{5,4},{6,7},{7,6},{8,9},{9,8},{10,11... | collective-permute-start | bytes 3981320 | tf_op jit(solution)/shard_map/ppermute | solution.py:655
  605.2 32.4 %collective-permute-start.30 = (bf16[2,288,1152]{2,1,0:T(8,128)(2,1)}, bf16[2,288,1152]{2,1,0:T(8,128)(2,1)}, u32[]{:S(2)}, u32[]{:S(2)}) collective-permute-start(bf16[2,288,1152]{2,1,0:T(8,128)(2,1)} %get-tuple-element.242), channel_id=1, source_target_pairs={{0,8},{4,12},{8,0},{12,4},{16,24},{20,28},{24,16},{28,20},{1,9},{5... | collective-permute-start | bytes 3981320 | tf_op jit(solution)/shard_map/ppermute | solution.py:655
  608.2 23.7 %copy-start.24 = (s32[8]{0:T(128)S(1)}, s32[8]{0:T(128)}, u32[]{:S(2)}) copy-start(s32[8]{0:T(128)} %param.32) | copy-start | bytes 100
  628.8 51.7 %collective-permute-start.29 = (bf16[16,4,8,1152]{3,2,1,0:T(8,128)(2,1)}, bf16[16,4,8,1152]{3,2,1,0:T(8,128)(2,1)}, u32[]{:S(2)}, u32[]{:S(2)}) collective-permute-start(bf16[16,4,8,1152]{3,2,1,0:T(8,128)(2,1)} %get-tuple-element.248), channel_id=1, source_target_pairs={{0,1},{1,0},{2,3},{3,2},{4,5},{5,4},{6,7},{7,6},{8,9},{9,8},{10,11... | collective-permute-start | bytes 3538952 | tf_op jit(solution)/shard_map/ppermute | solution.py:655
  630.5 18.2 %collective-permute-start.33 = (bf16[2,144,1152]{2,1,0:T(8,128)(2,1)}, bf16[2,144,1152]{2,1,0:T(8,128)(2,1)}, u32[]{:S(2)}, u32[]{:S(2)}) collective-permute-start(bf16[2,144,1152]{2,1,0:T(8,128)(2,1)} %get-tuple-element.193), channel_id=1, source_target_pairs={{0,8},{4,12},{8,0},{12,4},{16,24},{20,28},{24,16},{28,20},{1,9},{5... | collective-permute-start | bytes 1990664 | tf_op jit(solution)/shard_map/ppermute | solution.py:655
  632.7 95.5 %all-to-all-start.5 = ((bf16[32,64,1152]{2,1,0:T(8,128)(2,1)}), bf16[32,64,1152]{2,1,0:T(8,128)(2,1)}, u32[]{:S(2)}, u32[]{:S(2)}) async-start(bf16[32,64,1152]{2,1,0:T(8,128)(2,1)} %gather_fusion.7), calls=%async_computation.5 | async-start | bytes 9437184 | tf_op jit(solution)/shard_map/all_to_all | solution.py:999
  637.5 43.0 %copy-start.26 = (bf16[2,3,144,768]{3,2,1,0:T(8,128)(2,1)S(1)}, bf16[2,3,144,768]{3,2,1,0:T(8,128)(2,1)}, u32[]{:S(2)}) copy-start(bf16[2,3,144,768]{3,2,1,0:T(8,128)(2,1)} %add_convert_fusion.1) | copy-start | bytes 3981316
  639.1 66.4 %collective-permute-start.31 = (bf16[2,144,1152]{2,1,0:T(8,128)(2,1)S(1)}, bf16[2,144,1152]{2,1,0:T(8,128)(2,1)}, u32[]{:S(2)}, u32[]{:S(2)}) collective-permute-start(bf16[2,144,1152]{2,1,0:T(8,128)(2,1)S(1)} %get-tuple-element.190), channel_id=1, source_target_pairs={{0,16},{4,20},{8,24},{12,28},{16,0},{20,4},{24,8},{28,12},{1,17},{... | collective-permute-start | bytes 1990664 | tf_op jit(solution)/shard_map/ppermute | solution.py:655
  650.7 32.0 %copy-start.29 = (bf16[32,4,8,1152]{3,2,1,0:T(8,128)(2,1)S(1)}, bf16[32,4,8,1152]{3,2,1,0:T(8,128)(2,1)}, u32[]{:S(2)}) copy-start(bf16[32,4,8,1152]{3,2,1,0:T(8,128)(2,1)} %get-tuple-element.249) | copy-start | bytes 7077892
  650.7 54.8 %collective-permute-start.34 = (bf16[2,144,1152]{2,1,0:T(8,128)(2,1)}, bf16[2,144,1152]{2,1,0:T(8,128)(2,1)}, u32[]{:S(2)}, u32[]{:S(2)}) collective-permute-start(bf16[2,144,1152]{2,1,0:T(8,128)(2,1)} %add_convert_fusion.5), channel_id=1, source_target_pairs={{0,1},{1,0},{2,3},{3,2},{4,5},{5,4},{6,7},{7,6},{8,9},{9,8},{10,11... | collective-permute-start | bytes 1990664 | tf_op jit(solution)/shard_map/ppermute | solution.py:655
  682.2 27.2 %collective-permute-start.37 = (bf16[1,3,144,768]{3,2,1,0:T(8,128)(2,1)S(1)}, bf16[1,3,144,768]{3,2,1,0:T(8,128)(2,1)}, u32[]{:S(2)}, u32[]{:S(2)}) collective-permute-start(bf16[1,3,144,768]{3,2,1,0:T(8,128)(2,1)S(1)} %slice.161), channel_id=1, source_target_pairs={{0,2},{1,3},{2,0},{3,1},{4,6},{5,7},{6,4},{7,5},{8,10},{9,11},{10,... | collective-permute-start | bytes 1990664 | tf_op jit(solution)/shard_map/ppermute | solution.py:655
  707.1 17.4 %collective-permute-start.35 = (bf16[1,144,1152]{2,1,0:T(8,128)(2,1)S(1)}, bf16[1,144,1152]{2,1,0:T(8,128)(2,1)S(1)}, u32[]{:S(2)}, u32[]{:S(2)}) collective-permute-start(bf16[1,144,1152]{2,1,0:T(8,128)(2,1)S(1)} %slice.156), channel_id=1, source_target_pairs={{0,2},{1,3},{2,0},{3,1},{4,6},{5,7},{6,4},{7,5},{8,10},{9,11},{10,... | collective-permute-start | bytes 995336 | tf_op jit(solution)/shard_map/ppermute | solution.py:655
  710.6 13.9 %copy-start.27 = (f32[864,864]{1,0:T(8,128)S(1)}, f32[864,864]{1,0:T(8,128)}, u32[]{:S(2)}) copy-start(f32[864,864]{1,0:T(8,128)} %constant.210.clone) | copy-start | bytes 8957956
  728.2 9.0 %copy-start.1 = (bf16[1152,3,288]{0,2,1:T(8,128)(2,1)S(1)}, bf16[1152,3,288]{0,2,1:T(8,128)(2,1)}, u32[]{:S(2)}) copy-start(bf16[1152,3,288]{0,2,1:T(8,128)(2,1)} %param.36) | copy-start | bytes 5971972
  (37 other events, 118.5 us)
Sparse Core Ops, SparseCore 0:
  29.7 161.6 all-gather.2

commit v10 on v9

--- a/solution.py
+++ b/solution.py
@@ -412,7 +412,7 @@
         in_specs=[block] * len(rows) + [chunk, whole],
         out_specs=specs + [whole],
         out_shape=shapes + [jax.ShapeDtypeStruct(mods.shape, f32)],
-        compiler_params=pltpu.CompilerParams(vmem_limit_bytes=48 << 20),
+        compiler_params=pltpu.CompilerParams(vmem_limit_bytes=60 << 20),
         cost_estimate=lasting(microseconds),
         name=name,
     )(*rows, chunks, mods)
@@ -433,7 +433,7 @@
         ],
         out_specs=pl.BlockSpec((1,) + silu.shape, lambda k: (k, 0, 0)),
         out_shape=jax.ShapeDtypeStruct((kinds,) + silu.shape, f32),
-        compiler_params=pltpu.CompilerParams(vmem_limit_bytes=32 << 20),
+        compiler_params=pltpu.CompilerParams(vmem_limit_bytes=60 << 20),
         cost_estimate=lasting(60),
         name="modulate",
     )(silu, ada)
@@ -624,7 +624,7 @@
         ),
         out_shape=[half, half],
         compiler_params=pltpu.CompilerParams(vmem_limit_bytes=56 << 20),
-        cost_estimate=lasting(200),
+        cost_estimate=lasting(0),
         name="attend_grads",
     )(m_order, e_orders, xt, lowt, proj, att)
 
@@ -643,7 +643,80 @@
 
 
 def take_rows(values, index):
-    return jnp.take(values, index, axis=0, mode="clip")
+    return values.at[index].get(mode="promise_in_bounds")
+
+
+def sum_quarters_kernel(kept_ref, got_ref, *out_refs):
+    total = (kept_ref[0].astype(f32) + got_ref[0].astype(f32)).astype(bf16)
+    half = total.shape[0] // 2
+    later = pl.program_id(0) >= pl.num_programs(0) // 2
+
+    @pl.when(jnp.logical_not(later))
+    def _():
+        out_refs[0][0] = total[:half]
+        out_refs[1][0] = total[half:]
+
+    @pl.when(later)
+    def _():
+        out_refs[2][0] = total[:half]
+        out_refs[3][0] = total[half:]
+
+
+def sum_quarters(kept, got):
+    groups, rows, columns = kept.shape
+    if rows % 32:
+        halves = split(add_low(kept, got), 0)
+        return split(halves[0], 1) + split(halves[1], 1)
+    part = groups // 2
+    whole = pl.BlockSpec((1, rows, columns), lambda i: (i, 0, 0))
+    block = (1, rows // 2, columns)
+    early = pl.BlockSpec(block, lambda i: (jnp.minimum(i, part - 1), 0, 0))
+    late = pl.BlockSpec(block, lambda i: (jnp.maximum(i - part, 0), 0, 0))
+    return pl.pallas_call(
+        sum_quarters_kernel,
+        grid=(groups,),
+        in_specs=[whole, whole],
+        out_specs=[early, early, late, late],
+        out_shape=[jax.ShapeDtypeStruct((part, rows // 2, columns), bf16)] * 4,
+        compiler_params=pltpu.CompilerParams(vmem_limit_bytes=60 << 20),
+        cost_estimate=lasting(0),
+        name="sum_quarters",
+    )(kept, got)
+
+
+def whole_arrays(kernel, name, microseconds, shape, *arrays):
+    specs = [pl.BlockSpec(array.shape, functools.partial(lambda n: (0,) * n, array.ndim)) for array in arrays]
+    return pl.pallas_call(
+        kernel,
+        in_specs=specs,
+        out_specs=pl.BlockSpec(shape, lambda: (0,) * len(shape)),
+        out_shape=jax.ShapeDtypeStruct(shape, bf16),
+        compiler_params=pltpu.CompilerParams(vmem_limit_bytes=60 << 20),
+        cost_estimate=lasting(microseconds),
+        name=name,
+    )(*arrays)
+
+
+def append_zero_kernel(value_ref, out_ref):
+    count = value_ref.shape[0]
+    out_ref[:count] = value_ref[...]
+    out_ref[count:] = jnp.zeros_like(out_ref[count:])
+
+
+def append_zero(values, microseconds):
+    shape = (values.shape[0] + 1,) + values.shape[1:]
+    return whole_arrays(append_zero_kernel, "append_zero", microseconds, shape, values)
+
+
+def append_kernel(one_ref, other_ref, out_ref):
+    count = one_ref.shape[0]
+    out_ref[:count] = one_ref[...]
+    out_ref[count:] = other_ref[...]
+
+
+def append(one, other, microseconds):
+    shape = (2 * one.shape[0],) + one.shape[1:]
+    return whole_arrays(append_kernel, "append", microseconds, shape, one, other)
 
 
 def bits_of(size):
@@ -683,7 +756,7 @@
     second_ref[0] = total[half:]
 
 
-def sum_halves(kept, got):
+def sum_halves(kept, got, microseconds=0):
     rows, columns = kept.shape[-2:]
     if rows % 32:
         return split(add_low(kept, got), kept.ndim - 2)
@@ -697,8 +770,8 @@
         in_specs=[whole, whole],
         out_specs=[half, half],
         out_shape=[jax.ShapeDtypeStruct((kept.shape[0], rows // 2, columns), bf16)] * 2,
-        compiler_params=pltpu.CompilerParams(vmem_limit_bytes=32 << 20),
-        cost_estimate=lasting(0),
+        compiler_params=pltpu.CompilerParams(vmem_limit_bytes=60 << 20),
+        cost_estimate=lasting(microseconds),
         name="sum_halves",
     )(kept, got)
     return halves[0].reshape(shape), halves[1].reshape(shape)
@@ -786,9 +859,7 @@
     info, info_places = xor_gather(
         jnp.stack([time_bins, labels]), [("dp", bit) for bit in bits_of(dp_size)]
     )
-    qkv_weight, out_weight, expand_weight, down_weight, send_patches, info = tie(
-        qkv_weight, out_weight, expand_weight, down_weight, send_patches, info
-    )
+    send_patches, info = tie(send_patches, info)
     share = 4 * local_dim // dp_size
     spots = lax.dynamic_slice_in_dim(jnp.array(places), dp_index * share, share, 0)
     take_qkv = (spots[:, None] == jnp.arange(3 * local_dim)[None, :]).astype(bf16)
@@ -827,8 +898,8 @@
     bin_totals = jnp.sum(
         ((info[0][:, None] == jnp.arange(NBINS)[None, :]) & live_all[:, None]).astype(f32), axis=0
     )
-    gather_bits = [("dp", bit) for bit in bits_of(dp_size)]
-    gather_bits = gather_bits + [("mp", bit) for bit in bits_of(mp_size)[::-1]]
+    gather_bits = [("mp", bit) for bit in mp_bits[::-1]]
+    gather_bits = gather_bits + [("dp", bit) for bit in dp_bits[0][1:] + dp_bits[0][:1]]
     spread = {"dp": [0], "mp": [0]}
     for axis, bit in gather_bits:
         spread = {
@@ -874,7 +945,14 @@
         ],
         axis=1,
     )
-    recv_patches, mods = tie(recv_patches, mods)
+    back_within = pair_slot * dp_size + jnp.mod(my_place - starts[pair_peer], dp_size)
+    back_valid = back_within < image_counts[pair_peer]
+    back_slot = jnp.clip((starts[pair_peer] + back_within - my_place) // dp_size, 0, images - 1)
+    back_slot = jnp.where(back_valid, back_slot, images)
+    slot_ids = jnp.arange(capacity)
+    home_peer = dest_perm[jnp.mod(my_start + slot_ids, dp_size)]
+    home_index = home_peer * slot_count + jnp.minimum(slot_ids // dp_size, slot_count - 1)
+    recv_patches, mods, back_slot, home_index = tie(recv_patches, mods, back_slot, home_index)
 
     rank_ids = jnp.arange(images) * dp_size + my_place
     source = jnp.sum((finish[None, :] <= rank_ids[:, None]).astype(jnp.int32), axis=1)
@@ -931,7 +1009,7 @@
     got_zero = swap(sent_zero, "dp", dp_bits[0][0])
     kept_one, sent_one = sum_halves(kept_one, got_one)
     kept_zero, sent_zero = sum_halves(kept_zero, got_zero)
-    two_zero, kept_one, kept_zero, result = tie(two_zero, kept_one, kept_zero, result)
+    two_zero, kept_one, kept_zero = tie(two_zero, kept_one, kept_zero)
     got_one = swap(sent_one, "dp", dp_bits[1][1])
     got_zero = swap(sent_zero, "dp", dp_bits[0][1])
     middle_grad, branch_low, branch_t, sums_middle = by_image(
@@ -948,65 +1026,60 @@
     )
     gains_grad = jnp.sum(gains_grad, axis=2) * jnp.array([[head_dim ** (-0.5)], [1.0]], f32)
     projected_low, got_one, got_zero = tie(projected_low, got_one, got_zero)
-    kept_one, sent_one = sum_halves(kept_one, got_one)
-    kept_zero, sent_zero = sum_halves(kept_zero, got_zero)
-    normed_t, kept_one, kept_zero = tie(normed_t, kept_one, kept_zero)
-    got_one = swap(sent_one, "dp", dp_bits[1][2])
-    got_zero = swap(sent_zero, "dp", dp_bits[0][2])
-    latent_back = turn(latent_back)
-
-    normed_t, branch_t = by_owner(normed_t), by_owner(branch_t)
-
-    attend_kept, attend_sent = attend_grads(
-        m_order, jnp.concatenate(e_orders), normed_t, branch_t, projected_low, attended
-    )
-    attend_got = swap(attend_sent, "dp", dp_bits[0][0])
-    attend_kept, got_one, got_zero = tie(attend_kept, got_one, got_zero)
-
     packed = sums_finish + sums_middle + sums_entry
     gains_row = jnp.pad(gains_grad.reshape(1, 1, -1), ((0, own - 1), (7, 0), (0, model_width - 2 * head_dim)))
     packed = jnp.where(jnp.arange(8)[:, None] == 7, gains_row, packed).astype(bf16)
     packed = packed[None]
-    got_packed = swap(packed, *gather_bits[0])
-
-    def more(after):
+    stage, got_packed = 0, swap(packed, *gather_bits[0])
+
+    def more(after, microseconds=0):
         nonlocal packed, got_packed, stage
         after, got_packed = tie(after, got_packed)
-        packed = jnp.concatenate([packed, got_packed], axis=0)
+        packed = append(packed, got_packed, microseconds)
         stage += 1
         if stage < len(gather_bits):
             got_packed = swap(packed, *gather_bits[stage])
         return after
 
-    stage = 0
-    attend_kept = more(attend_kept)
-    halves = sum_halves(attend_kept, attend_got)
-    (attend_zero, attend_one), (sent_zero, sent_one) = split(halves[0], 0), split(halves[1], 0)
+    kept_one, sent_one = sum_halves(kept_one, got_one, 200)
+    kept_one = more(kept_one)
+    latent_back, packed = tie(latent_back, packed)
+    kept_zero, sent_zero = sum_halves(kept_zero, got_zero, 200)
+    normed_t, kept_one, kept_zero, result = tie(normed_t, kept_one, kept_zero, result)
+    got_one = swap(sent_one, "dp", dp_bits[1][2])
+    got_zero = swap(sent_zero, "dp", dp_bits[0][2])
+    latent_back = turn(latent_back)
+
+    normed_t, branch_t = by_owner(normed_t), by_owner(branch_t)
+
+    attend_kept, attend_sent = attend_grads(
+        m_order, jnp.concatenate(e_orders), normed_t, branch_t, projected_low, attended
+    )
+    attend_got = swap(attend_sent, "dp", dp_bits[0][0])
+
+    attend_kept, got_one, got_zero, latent_back, got_packed = tie(
+        attend_kept, got_one, got_zero, latent_back, got_packed
+    )
+    attend_kept = more(attend_kept, 200)
+    attend_got, packed = tie(attend_got, packed)
+    attend_zero, sent_zero, attend_one, sent_one = sum_quarters(attend_kept, attend_got)
+    mlp_one = halve(add_low(kept_one, got_one), "dp", dp_bits[1][3:], 2)
+    mlp_zero = halve(add_low(kept_zero, got_zero), "dp", dp_bits[0][3:], 2)
+    mlp_got = swap(mlp_one, "mp", mp_bits[0])
+
+    latent_back, attend_zero, attend_one = tie(latent_back, attend_zero, attend_one)
+    latent_back = append_zero(latent_back.reshape(images, local_len, model_width), 200)
+    back_patches = take_rows(latent_back, back_slot)
     attend_got_one = swap(sent_one, "dp", dp_bits[1][1])
     attend_got_zero = swap(sent_zero, "dp", dp_bits[0][1])
-    latent_back, attend_one, attend_zero = tie(latent_back, attend_one, attend_zero)
-
-    back_within = pair_slot * dp_size + jnp.mod(my_place - starts[pair_peer], dp_size)
-    back_valid = back_within < image_counts[pair_peer]
-    back_slot = jnp.clip((starts[pair_peer] + back_within - my_place) // dp_size, 0, images - 1)
-    back_slot = jnp.where(back_valid, back_slot, images)
-    empty = jnp.zeros((1, local_len, model_width), bf16)
-    latent_back = latent_back.reshape(images, local_len, model_width)
-    latent_back = jnp.concatenate([latent_back, empty], axis=0)
-    back_patches = take_rows(latent_back, back_slot)
-
-    got_packed, _ = tie(got_packed, back_patches)
-    got_patches = lax.all_to_all(back_patches, "dp", split_axis=0, concat_axis=0, tiled=True)
-    slot_ids = jnp.arange(capacity)
-    home_peer = dest_perm[jnp.mod(my_start + slot_ids, dp_size)]
-    home_index = home_peer * slot_count + jnp.minimum(slot_ids // dp_size, slot_count - 1)
-    patch_grad = take_rows(got_patches, home_index)
-
-    mlp_one = more(halve(add_low(kept_one, got_one), "dp", dp_bits[1][3:], 2))
-    mlp_zero = more(halve(add_low(kept_zero, got_zero), "dp", dp_bits[0][3:], 2))
-    mlp_got = swap(mlp_one, "mp", mp_bits[0])
+    attend_zero = more(attend_zero)
+    back_patches, attend_zero, attend_one = tie(back_patches, attend_zero, attend_one)
+    attend_zero = more(attend_zero)
     attend_one, sent_one = sum_halves(attend_one, attend_got_one)
     attend_zero, sent_zero = sum_halves(attend_zero, attend_got_zero)
+    back_patches, sent_one, sent_zero = tie(back_patches, sent_one, sent_zero)
+    got_patches = lax.all_to_all(back_patches, "dp", split_axis=0, concat_axis=0, tiled=True)
+    patch_grad = take_rows(got_patches, home_index)
     attend_got_one = swap(sent_one, "dp", dp_bits[1][2])
     attend_got_zero = swap(sent_zero, "dp", dp_bits[0][2])
     while stage < len(gather_bits):

time: 752 us -> 690 us (0.918)
  waiting for transfers between devices: 280 us -> 212 us
  Pallas kernels: 255 us -> 293 us
  local copies, waits for them, and re-layouts: 84.6 us -> 52.9 us
    ppermute x38, waiting for transfers between devices: 206 us -> 138 us  [swap(): return lax.ppermute(values, axis, [(i, i ^ bit) for i in range(size)])]
    all_to_all x4, waiting for transfers between devices: 46.8 us -> 12.6 us  [turn(): return lax.all_to_all(chunks, 'mp', split_axis=0, concat_axis=0, tiled=True)]
    all_to_all x1, waiting for transfers between devices: 27.7 us -> 60.9 us  [shards(): lax.all_to_all(send_patches, 'dp', split_axis=0, concat_axis=0, tiled=True)]
    unnamed x121 -> x85, local copies, waits for them, and re-layouts: 39.9 us -> 9.48 us
    pallas_call x0 -> x7, Pallas kernels: none -> 21.9 us  [the longest x6 14.2 us: whole_arrays(): pl.pallas_call(kernel, in_specs=specs, out_specs=pl.BlockSpec(shape, lamb...]
    pallas_call x7 -> x6, Pallas kernels: 22.9 us -> 31.7 us  [sum_halves(): pl.pallas_call(sum_halves_kernel, grid=(kept.shape[0],), in_specs=[whole,...]
  transfers between devices with their start and end apart: 45 -> 45, of which waited for: 22 -> 16; matrix products, arithmetic and copies ran while one was open for 12% -> 12% of each run, Pallas kernels for 25% -> 37%
where the time goes in v10:
time: 690 us; the launch traced here: 681 us
  Pallas kernels  293 us (42%)
  waiting for transfers between devices  212 us (31%)
  starting transfers between devices  63.2 us (9%)
  local copies, waits for them, and re-layouts  52.9 us (8%)
  other arithmetic  28.9 us (4%)
  matrix products  15.6 us (2%)
  between operations  15.4 us (2%)
    ppermute x38, waiting for transfers between devices, swap(): return lax.ppermute(values, axis, [(i, i ^ bit) for i in range(size)])  138 us
    pallas_call x2, Pallas kernels, mlp_back(): pl.pallas_call(mlp_back_kernel, grid_spec=pltpu.PrefetchScalarGridSpec(nu...  72.1 us
    all_to_all x1, waiting for transfers between devices, shards(): lax.all_to_all(send_patches, 'dp', split_axis=0, concat_axis=0, tiled=True)  60.9 us
    pallas_call x1, Pallas kernels, attend_back(): pl.pallas_call(attend_back_kernel, grid=(groups,), in_specs=[whole_spec(l...  44.9 us
    pallas_call x1, Pallas kernels, mlp(): pl.pallas_call(functools.partial(mlp_kernel, len(pieces)), grid_spec=pltp...  37.9 us
    pallas_call x1, Pallas kernels, attend(): pl.pallas_call(attend_kernel, grid=(groups,), in_specs=[whole_spec(latent...  35.9 us
    ppermute x38, starting transfers between devices, swap(): return lax.ppermute(values, axis, [(i, i ^ bit) for i in range(size)])  33.8 us
    pallas_call x6, Pallas kernels, sum_halves(): pl.pallas_call(sum_halves_kernel, grid=(kept.shape[0],), in_specs=[whole,...  31.7 us
  transfers between devices with their start and end apart: 45, of which 16 were waited for; matrix products, arithmetic and copies ran while one was open for 12% of the time, Pallas kernels for 37%

profile of v10, /device:TPU:0, one launch (start us, length us, event | category | flops | bytes accessed | tf_op | source)
XLA Modules:
  0.0 680.9 jit_solution(16978919273366078187)
XLA Ops:
  11.6 7.9 %fusion.58 = (bf16[1152,1,768]{2,1,0:T(2,128)(2,1)S(1)}, bf16[1152,1,768]{2,1,0:T(2,128)(2,1)S(1)}) fusion(bf16[1152,2,768]{2,1,0:T(2,128)(2,1)} %param.39), kind=kLoop, calls=%fused_computation.194 | loop fusion | bytes 7077888 | tf_op jit(solution)/shard_map/slice | solution.py:874
  22.0 3.7 collective-permute-start.3
  37.2 2.1 collective-permute-done.1
  40.9 5.6 gather_fusion.1
  47.3 3.1 multiply_convert_fusion
  51.0 4.6 all-to-all-start
  55.9 10.4 %collective-permute-done.3 = bf16[1,3,96,1152]{3,2,1,0:T(8,128)(2,1)S(1)} collective-permute-done((bf16[1,3,96,1152]{3,2,1,0:T(8,128)(2,1)S(1)}, bf16[1,3,96,1152]{3,2,1,0:T(8,128)(2,1)S(1)}, u32[]{:S(2)}, u32[]{:S(2)}) %collective-permute-start.3) | collective-permute-done | bytes 663584 | tf_op jit(solution)/shard_map/ppermute | solution.py:728
  67.2 8.5 %modulate.1 = f32[6,16,1152]{2,1,0:T(8,128)} custom-call(bf16[16,1152]{1,0:T(8,128)(2,1)} %pad.8.silu_ref, bf16[6,1152,1152]{2,1,0:T(8,128)(2,1)} %bitcast.159), custom_call_target="tpu_custom_call" | custom-call | flops 65999998976 | bytes 1024 | tf_op jit(solution)/shard_map/modulate/pallas_call | solution.py:427
  77.6 60.9 %all-to-all-done = bf16[32,64,1152]{2,1,0:T(8,128)(2,1)} async-done(((bf16[32,64,1152]{2,1,0:T(8,128)(2,1)}), bf16[32,64,1152]{2,1,0:T(8,128)(2,1)}, u32[]{:S(2)}, u32[]{:S(2)}) %all-to-all-start) | async-done | bytes 4718624 | tf_op jit(solution)/shard_map/all_to_all | solution.py:890
  138.5 4.8 gather_fusion.6
  143.3 4.5 all-to-all-start.1
  147.8 1.8 pad_maximum_fusion.refs_0_
  149.8 1.9 fusion.59
  153.9 2.0 collective-permute-start.15
  159.6 24.6 %collective-permute-done.9.refs_4_ = bf16[4,3,48,1152]{3,2,1,0:T(8,128)(2,1)} collective-permute-done((bf16[4,3,48,1152]{3,2,1,0:T(8,128)(2,1)}, bf16[4,3,48,1152]{3,2,1,0:T(8,128)(2,1)}, u32[]{:S(2)}, u32[]{:S(2)}) %collective-permute-start.9) | collective-permute-done | bytes 1327136 | tf_op jit(solution)/shard_map/ppermute | solution.py:728
  184.2 27.6 %collective-permute-done.15.refs_10_ = bf16[4,3,48,1152]{3,2,1,0:T(8,128)(2,1)} collective-permute-done((bf16[4,3,48,1152]{3,2,1,0:T(8,128)(2,1)}, bf16[4,3,48,1152]{3,2,1,0:T(8,128)(2,1)}, u32[]{:S(2)}, u32[]{:S(2)}) %collective-permute-start.15) | collective-permute-done | bytes 1327136 | tf_op jit(solution)/shard_map/ppermute | solution.py:728
  211.8 1.7 collective-permute-start.12
  214.1 5.3 all-to-all-start.2
  219.4 35.9 %attend.1 = (f32[4,864,1024]{2,1,0:T(8,128)}, bf16[4,288,1024]{2,1,0:T(8,128)(2,1)}, bf16[1024,1152]{1,0:T(8,128)(2,1)}, bf16[1152,1024]{1,0:T(8,128)(2,1)}, f32...) custom-call(bf16[4,4,64,1152]{3,2,1,0:T(8,128)(2,1)} %all-to-all-done.1.latent_ref, ...), custom_call_target="tpu_custom_call" | custom-call | flops 176000008192 | bytes 1024 | tf_op jit(solution)/shard_map/attend/pallas_call | solution.py:286
  257.6 2.0 collective-permute-done.8.refs_3_
  260.7 1.9 collective-permute-done.17.refs_13_
  262.6 37.9 %mlp.1 = (bf16[4,2,1024,768]{3,2,1,0:T(8,128)(2,1)}, f32[1024,1152]{1,0:T(8,128)}, bf16[4,3,768,1152]{3,2,1,0:T(8,128)(2,1)}) custom-call(s32[14]{0:T(128)} %stack.93.e_ref, bf16[1024,1152]{1,0:T(8,128)(2,1)} %get-tuple-element.125.x_ref, bf16[4,3,96,1152]{3,2,1,0:T(8,128)(2,1)} %copy-done.4, bf16[4,3,96,1152]{3,2,1,0:T(8,128)(2,1)} %collective-permute-done.7.refs_1_, ...), custom_call_target="tpu_custom_call" | custom-call | flops 1100000000 | bytes 1024 | tf_op jit(solution)/shard_map/mlp/pallas_call | solution.py:479
  300.5 7.7 %finish.1 = (bf16[1024,1152]{1,0:T(8,128)(2,1)}, bf16[1152,1024]{1,0:T(8,128)(2,1)}, bf16[4,4,64,1152]{3,2,1,0:T(8,128)(2,1)}, f32[4,8,1152]{2,1,0:T(8,128)}) custom-call(f32[1024,1152]{1,0:T(8,128)} %get-tuple-element.134.branch_ref, f32[1024,1152]{1,0:T(8,128)} %get-tuple-element.135.middle_ref, bf16[4,4,64,1152]{3,2,1,0:T(8,128)(2,1)} %all-to-all-done.2.cot_ref, ...), custom_call_target="tpu_custom_call" | custom-call | flops 1100000000 | bytes 1024 | tf_op jit(solution)/shard_map/finish/pallas_call | solution.py:409
  308.2 36.2 %mlp_back.2 = (bf16[2,3,576,768]{3,2,1,0:T(8,128)(2,1)}, bf16[2,3,576,768]{3,2,1,0:T(8,128)(2,1)}, f32[1024,1152]{1,0:T(8,128)}) custom-call(s32[8]{0:T(128)} %broadcast_xor_fusion.2.e_ref, bf16[8,144,1024]{2,1,0:T(8,128)(2,1)} %bitcast.166, bf16[8,144,1024]{2,1,0:T(8,128)(2,1)} %bitcast.162, bf16[1024,1152]{1,0:T(8,128)(2,1)} %get-tuple-element.138.low_ref, ...), custom_call_target="tpu_custom_call" | custom-call | flops 165000003584 | bytes 1024 | tf_op jit(solution)/shard_map/mlp_back/pallas_call | solution.py:555
  344.5 35.9 %mlp_back.3 = (bf16[2,3,576,768]{3,2,1,0:T(8,128)(2,1)}, bf16[2,3,576,768]{3,2,1,0:T(8,128)(2,1)}, f32[1024,1152]{1,0:T(8,128)}) custom-call(s32[8]{0:T(128)} %broadcast_xor_fusion.1.e_ref, bf16[8,144,1024]{2,1,0:T(8,128)(2,1)} %bitcast.167, bf16[8,144,1024]{2,1,0:T(8,128)(2,1)} %bitcast.163, bf16[1024,1152]{1,0:T(8,128)(2,1)} %get-tuple-element.138.low_ref, ...), custom_call_target="tpu_custom_call" | custom-call | flops 165000003584 | bytes 1024 | tf_op jit(solution)/shard_map/mlp_back/pallas_call | solution.py:555
  380.9 5.3 all-to-all-start.3
  386.2 7.6 %sum_halves.7 = (bf16[6,288,768]{2,1,0:T(8,128)(2,1)}, bf16[6,288,768]{2,1,0:T(8,128)(2,1)}) custom-call(bf16[6,576,768]{2,1,0:T(8,128)(2,1)} %bitcast.147, bf16[6,576,768]{2,1,0:T(8,128)(2,1)} %bitcast.51.got_ref), custom_call_target="tpu_custom_call" | custom-call | bytes 1024 | tf_op jit(solution)/shard_map/sum_halves/pallas_call | solution.py:767
  393.8 7.6 %sum_halves.6 = (bf16[6,288,768]{2,1,0:T(8,128)(2,1)}, bf16[6,288,768]{2,1,0:T(8,128)(2,1)}) custom-call(bf16[6,576,768]{2,1,0:T(8,128)(2,1)} %bitcast.146, bf16[6,576,768]{2,1,0:T(8,128)(2,1)} %bitcast.48.got_ref), custom_call_target="tpu_custom_call" | custom-call | bytes 1024 | tf_op jit(solution)/shard_map/sum_halves/pallas_call | solution.py:767
  403.6 11.1 %middle.1 = (f32[1024,1152]{1,0:T(8,128)}, bf16[1024,1152]{1,0:T(8,128)(2,1)}, bf16[1152,1024]{1,0:T(8,128)(2,1)}, f32[4,8,1152]{2,1,0:T(8,128)}) custom-call(f32[1024,1152]{1,0:T(8,128)} %get-tuple-element.150.one_ref, f32[1024,1152]{1,0:T(8,128)} %get-tuple-element.151.other_ref, f32[1024,1152]{1,0:T(8,128)} %get-tuple-element.135.middle_ref, ...), custom_call_target="tpu_custom_call" | custom-call | flops 109999996928 | bytes 1024 | tf_op jit(solution)/shard_map/middle/pallas_call | solution.py:409
  414.7 44.9 %attend_back.1 = (bf16[4,864,1024]{2,1,0:T(8,128)(2,1)}, f32[2,72,256]{2,1,0:T(8,128)}, f32[4,8,1152]{2,1,0:T(8,128)}, bf16[4,4,64,1152]{3,2,1,0:T(8,128)(2,1)}) custom-call(bf16[4,4,64,1152]{3,2,1,0:T(8,128)(2,1)} %all-to-all-done.1.latent_ref, f32[4,864,1024]{2,1,0:T(8,128)} %get-tuple-element.149.proj_ref, bf16[1024,1152]{1,0:T(8,128)(2,1)} %get-tuple-element.153.low_ref, ...), custom_call_target="tpu_custom_call" | custom-call | flops 1100000000 | bytes 1024 | tf_op jit(solution)/shard_map/attend_back/pallas_call | solution.py:330
  460.7 1.6 fusion.32.one_ref
  462.4 3.0 collective-permute-start.22
  465.3 5.6 sum_halves.8
  472.5 4.7 all-to-all-start.4
  477.3 5.7 sum_halves.9
  486.0 2.0 collective-permute-start.25
  488.6 21.4 %attend_grads.1 = (bf16[4,576,1152]{2,1,0:T(8,128)(2,1)}, bf16[4,576,1152]{2,1,0:T(8,128)(2,1)}) custom-call(s32[4]{0:T(128)} %broadcast_xor_fusion.m_ref, s32[16]{0:T(128)} %pad_add_fusion.3.e_ref, bf16[8,144,1024]{2,1,0:T(8,128)(2,1)} %bitcast.148, bf16[8,144,1024]{2,1,0:T(8,128)(2,1)} %bitcast.149, bf16[4,864,1024]{2,1,0:T(8,128)(2,1)} %get-tuple-element.172.proj_ref, ...), custom_call_target="tpu_custom_call" | custom-call | bytes 1024 | tf_op jit(solution)/shard_map/attend_grads/pallas_call | solution.py:608
  510.1 7.6 %collective-permute-done.25.other_ref = bf16[2,4,8,1152]{3,2,1,0:T(8,128)(2,1)S(1)} collective-permute-done((bf16[2,4,8,1152]{3,2,1,0:T(8,128)(2,1)S(1)}, bf16[2,4,8,1152]{3,2,1,0:T(8,128)(2,1)S(1)}, u32[]{:S(2)}, u32[]{:S(2)}) %collective-permute-start.25) | collective-permute-done | bytes 147488 | tf_op jit(solution)/shard_map/ppermute | solution.py:728
  517.7 12.6 %all-to-all-done.4 = bf16[4,4,64,1152]{3,2,1,0:T(8,128)(2,1)} async-done(((bf16[4,4,64,1152]{3,2,1,0:T(8,128)(2,1)}), bf16[4,4,64,1152]{3,2,1,0:T(8,128)(2,1)}, u32[]{:S(2)}, u32[]{:S(2)}) %all-to-all-start.4) | async-done | bytes 2359328 | tf_op jit(solution)/shard_map/all_to_all | solution.py:843
  530.3 1.8 append.6.one_ref
  533.5 2.7 add_convert_fusion.1
  536.3 7.7 %sum_quarters.1 = (bf16[2,288,1152]{2,1,0:T(8,128)(2,1)}, bf16[2,288,1152]{2,1,0:T(8,128)(2,1)}, bf16[2,288,1152]{2,1,0:T(8,128)(2,1)}, bf16[2,288,1152]{2,1,0:T(8,128)(2,1)}) custom-call(bf16[4,576,1152]{2,1,0:T(8,128)(2,1)} %get-tuple-element.183.kept_ref, bf16[4,576,1152]{2,1,0:T(8,128)(2,1)} %collective-permute-done.26.got_ref), custom_call_target="tpu_custom_call" | custom-call | bytes 1024 | tf_op jit(solution)/shard_map/sum_quarters/pallas_call | solution.py:675
  544.7 1.9 append.7.one_ref
  549.2 3.3 append_zero.1
  552.5 5.1 gather_fusion.8
  557.6 5.6 collective-permute-done.29.other_ref
  563.2 2.3 append.8.one_ref
  565.7 1.6 add_convert_fusion.2
  567.3 9.6 %collective-permute-done.30.got_ref = bf16[2,288,1152]{2,1,0:T(8,128)(2,1)} collective-permute-done((bf16[2,288,1152]{2,1,0:T(8,128)(2,1)}, bf16[2,288,1152]{2,1,0:T(8,128)(2,1)}, u32[]{:S(2)}, u32[]{:S(2)}) %collective-permute-start.30) | collective-permute-done | bytes 1327136 | tf_op jit(solution)/shard_map/ppermute | solution.py:728
  576.9 2.6 sum_halves.11
  579.6 9.8 %collective-permute-done.28.got_ref = bf16[2,288,1152]{2,1,0:T(8,128)(2,1)} collective-permute-done((bf16[2,288,1152]{2,1,0:T(8,128)(2,1)}, bf16[2,288,1152]{2,1,0:T(8,128)(2,1)}, u32[]{:S(2)}, u32[]{:S(2)}) %collective-permute-start.28) | collective-permute-done | bytes 1327136 | tf_op jit(solution)/shard_map/ppermute | solution.py:728
  589.4 2.6 sum_halves.10
  593.0 4.9 all-to-all-start.5
  598.0 1.6 add_convert_fusion
  601.0 3.2 append.9
  605.1 1.9 copy.100
  607.8 2.2 fusion.28
  613.5 2.4 fusion.12
  617.1 16.3 %collective-permute-done.37 = bf16[1,3,144,768]{3,2,1,0:T(8,128)(2,1)} collective-permute-done((bf16[1,3,144,768]{3,2,1,0:T(8,128)(2,1)}, bf16[1,3,144,768]{3,2,1,0:T(8,128)(2,1)}, u32[]{:S(2)}, u32[]{:S(2)}) %collective-permute-start.37) | collective-permute-done | bytes 663584 | tf_op jit(solution)/shard_map/ppermute | solution.py:728
  634.6 7.5 %collective-permute-done.34 = bf16[2,144,1152]{2,1,0:T(8,128)(2,1)S(1)} collective-permute-done((bf16[2,144,1152]{2,1,0:T(8,128)(2,1)S(1)}, bf16[2,144,1152]{2,1,0:T(8,128)(2,1)S(1)}, u32[]{:S(2)}, u32[]{:S(2)}) %collective-permute-start.34) | collective-permute-done | bytes 663584 | tf_op jit(solution)/shard_map/ppermute | solution.py:728
  643.5 3.0 collective-permute-start.35
  648.9 12.0 %collective-permute-done.35 = bf16[1,144,1152]{2,1,0:T(8,128)(2,1)S(1)} collective-permute-done((bf16[1,144,1152]{2,1,0:T(8,128)(2,1)S(1)}, bf16[1,144,1152]{2,1,0:T(8,128)(2,1)S(1)}, u32[]{:S(2)}, u32[]{:S(2)}) %collective-permute-start.35) | collective-permute-done | bytes 331808 | tf_op jit(solution)/shard_map/ppermute | solution.py:728
  664.6 5.7 gather_fusion.9
  670.3 3.3 copy.108
  (266 shorter events, 65.2 us)
Async XLA Ops:
  7.2 212.1 %all-gather.3.cloned.1.call-start = ((), (), s32[]{:S(2)}) async-start(), calls=%async_computation.6 | async-start | bytes 10948608 | tf_op jit(solution)/shard_map/all_gather | solution.py:641
  11.1 24.6 %collective-permute-start = (s32[1,2,32]{2,1,0:T(2,128)S(1)}, s32[1,2,32]{2,1,0:T(2,128)S(1)}, u32[]{:S(2)}, u32[]{:S(2)}) collective-permute-start(s32[1,2,32]{2,1,0:T(2,128)S(1)} %add_bitcast_fusion), channel_id=1, source_target_pairs={{0,4},{4,0},{8,12},{12,8},{16,20},{20,16},{24,28},{28,24},{1,5},{5... | collective-permute-start | bytes 776 | tf_op jit(solution)/shard_map/ppermute | solution.py:728
  20.2 9.1 %copy-start.39 = (s32[32]{0:T(128)S(1)}, s32[32]{0:T(128)}, u32[]{:S(2)}) copy-start(s32[32]{0:T(128)} %constant.210.clone) | copy-start | bytes 388
  20.2 9.3 %copy-start.38 = (s32[32]{0:T(128)S(1)}, s32[32]{0:T(128)}, u32[]{:S(2)}) copy-start(s32[32]{0:T(128)} %constant.211.clone) | copy-start | bytes 388
  22.0 44.3 %collective-permute-start.3 = (bf16[1,3,96,1152]{3,2,1,0:T(8,128)(2,1)S(1)}, bf16[1,3,96,1152]{3,2,1,0:T(8,128)(2,1)S(1)}, u32[]{:S(2)}, u32[]{:S(2)}) collective-permute-start(bf16[1,3,96,1152]{3,2,1,0:T(8,128)(2,1)S(1)} %maximum_bitcast_fusion), channel_id=1, source_target_pairs={{0,2},{1,3},{2,0},{3,1},{4,6},{5,7},{6,4},{7,5},{8,10},{9,11},{10,... | collective-permute-start | bytes 1990664 | tf_op jit(solution)/shard_map/ppermute | solution.py:728
  35.7 3.6 collective-permute-start.1
  39.3 7.2 %collective-permute-start.2 = (s32[4,2,32]{2,1,0:T(2,128)S(1)}, s32[4,2,32]{2,1,0:T(2,128)S(1)}, u32[]{:S(2)}, u32[]{:S(2)}) collective-permute-start(s32[4,2,32]{2,1,0:T(2,128)S(1)} %pad_add_fusion.1), channel_id=1, source_target_pairs={{0,16},{4,20},{8,24},{12,28},{16,0},{20,4},{24,8},{28,12},{1,17},{... | collective-permute-start | bytes 3080 | tf_op jit(solution)/shard_map/ppermute | solution.py:728
  46.9 8.9 %copy-start.18 = (s32[128]{0:T(128)}, s32[128]{0:T(128)S(1)}, u32[]{:S(2)}) copy-start(s32[128]{0:T(128)S(1)} %get-tuple-element.261) | copy-start | bytes 1540
  51.0 87.5 %all-to-all-start = ((bf16[32,64,1152]{2,1,0:T(8,128)(2,1)}), bf16[32,64,1152]{2,1,0:T(8,128)(2,1)}, u32[]{:S(2)}, u32[]{:S(2)}) async-start(bf16[32,64,1152]{2,1,0:T(8,128)(2,1)} %gather_fusion.1), calls=%async_computation | async-start | bytes 9437184 | tf_op jit(solution)/shard_map/all_to_all | solution.py:890
  66.3 9.5 %copy-start.6 = (bf16[1,3,96,1152]{3,2,1,0:T(8,128)(2,1)}, bf16[1,3,96,1152]{3,2,1,0:T(8,128)(2,1)S(1)}, u32[]{:S(2)}) copy-start(bf16[1,3,96,1152]{3,2,1,0:T(8,128)(2,1)S(1)} %collective-permute-done.3) | copy-start | bytes 1990660
  66.4 81.3 %collective-permute-start.4 = (bf16[2,3,96,1152]{3,2,1,0:T(8,128)(2,1)S(1)}, bf16[2,3,96,1152]{3,2,1,0:T(8,128)(2,1)}, u32[]{:S(2)}, u32[]{:S(2)}) collective-permute-start(bf16[2,3,96,1152]{3,2,1,0:T(8,128)(2,1)S(1)} %pad_maximum_fusion.1), channel_id=1, source_target_pairs={{0,1},{1,0},{2,3},{3,2},{4,5},{5,4},{6,7},{7,6},{8,9},{9,8},{10,11... | collective-permute-start | bytes 3981320 | tf_op jit(solution)/shard_map/ppermute | solution.py:728
  143.3 68.5 %all-to-all-start.1 = ((bf16[4,4,64,1152]{3,2,1,0:T(8,128)(2,1)}), bf16[4,4,64,1152]{3,2,1,0:T(8,128)(2,1)}, u32[]{:S(2)}, u32[]{:S(2)}) async-start(bf16[4,4,64,1152]{3,2,1,0:T(8,128)(2,1)} %bitcast.24), calls=%async_computation.1 | async-start | bytes 4718592 | tf_op jit(solution)/shard_map/all_to_all | solution.py:843
  149.6 62.2 %collective-permute-start.7 = (bf16[4,3,96,1152]{3,2,1,0:T(8,128)(2,1)S(1)}, bf16[4,3,96,1152]{3,2,1,0:T(8,128)(2,1)}, u32[]{:S(2)}, u32[]{:S(2)}) collective-permute-start(bf16[4,3,96,1152]{3,2,1,0:T(8,128)(2,1)S(1)} %pad_maximum_fusion.refs_0_), channel_id=1, source_target_pairs={{0,4},{4,0},{8,12},{12,8},{16,20},{20,16},{24,28},{28,24},{1,5},{5... | collective-permute-start | bytes 7962632 | tf_op jit(solution)/shard_map/ppermute | solution.py:728
  149.8 9.1 %copy-start.20 = (f32[2]{0:T(128)S(1)}, f32[2]{0:T(128)}, u32[]{:S(2)}) copy-start(f32[2]{0:T(128)} %constant.222) | copy-start | bytes 28
  151.9 59.9 %collective-permute-start.5 = (bf16[4,3,48,1152]{3,2,1,0:T(8,128)(2,1)}, bf16[4,3,48,1152]{3,2,1,0:T(8,128)(2,1)}, u32[]{:S(2)}, u32[]{:S(2)}) collective-permute-start(bf16[4,3,48,1152]{3,2,1,0:T(8,128)(2,1)} %get-tuple-element.265), channel_id=1, source_target_pairs={{0,8},{4,12},{8,0},{12,4},{16,24},{20,28},{24,16},{28,20},{1,9},{5... | collective-permute-start | bytes 3981320 | tf_op jit(solution)/shard_map/ppermute | solution.py:728
  151.9 32.3 %collective-permute-start.9 = (bf16[4,3,48,1152]{3,2,1,0:T(8,128)(2,1)}, bf16[4,3,48,1152]{3,2,1,0:T(8,128)(2,1)}, u32[]{:S(2)}, u32[]{:S(2)}) collective-permute-start(bf16[4,3,48,1152]{3,2,1,0:T(8,128)(2,1)} %get-tuple-element.265), channel_id=1, source_target_pairs={{0,16},{4,20},{8,24},{12,28},{16,0},{20,4},{24,8},{28,12},{1,17},{... | collective-permute-start | bytes 3981320 | tf_op jit(solution)/shard_map/ppermute | solution.py:728
  153.1 58.7 %collective-permute-start.6 = (bf16[4,3,48,1152]{3,2,1,0:T(8,128)(2,1)}, bf16[4,3,48,1152]{3,2,1,0:T(8,128)(2,1)}, u32[]{:S(2)}, u32[]{:S(2)}) collective-permute-start(bf16[4,3,48,1152]{3,2,1,0:T(8,128)(2,1)} %get-tuple-element.264), channel_id=1, source_target_pairs={{0,16},{4,20},{8,24},{12,28},{16,0},{20,4},{24,8},{28,12},{1,17},{... | collective-permute-start | bytes 3981320 | tf_op jit(solution)/shard_map/ppermute | solution.py:728
  153.9 57.9 %collective-permute-start.15 = (bf16[4,3,48,1152]{3,2,1,0:T(8,128)(2,1)}, bf16[4,3,48,1152]{3,2,1,0:T(8,128)(2,1)}, u32[]{:S(2)}, u32[]{:S(2)}) collective-permute-start(bf16[4,3,48,1152]{3,2,1,0:T(8,128)(2,1)} %get-tuple-element.264), channel_id=1, source_target_pairs={{0,8},{4,12},{8,0},{12,4},{16,24},{20,28},{24,16},{28,20},{1,9},{5... | collective-permute-start | bytes 3981320 | tf_op jit(solution)/shard_map/ppermute | solution.py:728
  184.2 71.7 %collective-permute-start.10 = (bf16[4,3,48,1152]{3,2,1,0:T(8,128)(2,1)}, bf16[4,3,48,1152]{3,2,1,0:T(8,128)(2,1)}, u32[]{:S(2)}, u32[]{:S(2)}) collective-permute-start(bf16[4,3,48,1152]{3,2,1,0:T(8,128)(2,1)} %collective-permute-done.9.refs_4_), channel_id=1, source_target_pairs={{0,4},{4,0},{8,12},{12,8},{16,20},{20,16},{24,28},{28,24},{1,5},{5... | collective-permute-start | bytes 3981320 | tf_op jit(solution)/shard_map/ppermute | solution.py:728
  211.8 45.8 %collective-permute-start.16 = (bf16[4,3,48,1152]{3,2,1,0:T(8,128)(2,1)}, bf16[4,3,48,1152]{3,2,1,0:T(8,128)(2,1)}, u32[]{:S(2)}, u32[]{:S(2)}) collective-permute-start(bf16[4,3,48,1152]{3,2,1,0:T(8,128)(2,1)} %collective-permute-done.15.refs_10_), channel_id=1, source_target_pairs={{0,4},{4,0},{8,12},{12,8},{16,20},{20,16},{24,28},{28,24},{1,5},{5... | collective-permute-start | bytes 3981320 | tf_op jit(solution)/shard_map/ppermute | solution.py:728
  211.8 43.6 %collective-permute-start.12 = (bf16[4,3,48,1152]{3,2,1,0:T(8,128)(2,1)}, bf16[4,3,48,1152]{3,2,1,0:T(8,128)(2,1)}, u32[]{:S(2)}, u32[]{:S(2)}) collective-permute-start(bf16[4,3,48,1152]{3,2,1,0:T(8,128)(2,1)} %collective-permute-done.6.refs_8_), channel_id=1, source_target_pairs={{0,8},{4,12},{8,0},{12,4},{16,24},{20,28},{24,16},{28,20},{1,9},{5... | collective-permute-start | bytes 3981320 | tf_op jit(solution)/shard_map/ppermute | solution.py:728
  213.5 44.1 %collective-permute-start.14 = (bf16[4,3,48,1152]{3,2,1,0:T(8,128)(2,1)}, bf16[4,3,48,1152]{3,2,1,0:T(8,128)(2,1)}, u32[]{:S(2)}, u32[]{:S(2)}) collective-permute-start(bf16[4,3,48,1152]{3,2,1,0:T(8,128)(2,1)} %collective-permute-done.6.refs_8_), channel_id=1, source_target_pairs={{0,4},{4,0},{8,12},{12,8},{16,20},{20,16},{24,28},{28,24},{1,5},{5... | collective-permute-start | bytes 3981320 | tf_op jit(solution)/shard_map/ppermute | solution.py:728
  213.5 41.8 %collective-permute-start.11 = (bf16[4,3,48,1152]{3,2,1,0:T(8,128)(2,1)}, bf16[4,3,48,1152]{3,2,1,0:T(8,128)(2,1)}, u32[]{:S(2)}, u32[]{:S(2)}) collective-permute-start(bf16[4,3,48,1152]{3,2,1,0:T(8,128)(2,1)} %collective-permute-done.5.refs_2_), channel_id=1, source_target_pairs={{0,16},{4,20},{8,24},{12,28},{16,0},{20,4},{24,8},{28,12},{1,17},{... | collective-permute-start | bytes 3981320 | tf_op jit(solution)/shard_map/ppermute | solution.py:728
  214.1 86.4 %all-to-all-start.2 = ((bf16[4,4,64,1152]{3,2,1,0:T(8,128)(2,1)}), bf16[4,4,64,1152]{3,2,1,0:T(8,128)(2,1)}, u32[]{:S(2)}, u32[]{:S(2)}) async-start(bf16[4,4,64,1152]{3,2,1,0:T(8,128)(2,1)} %bitcast.150), calls=%async_computation.2 | async-start | bytes 4718592 | tf_op jit(solution)/shard_map/all_to_all | solution.py:843
  219.3 37.2 %copy-start.35 = (s32[8]{0:T(128)S(1)}, s32[8]{0:T(128)}, u32[]{:S(2)}) copy-start(s32[8]{0:T(128)} %constant.212.clone) | copy-start | bytes 100
  219.4 37.7 %copy-start.34 = (s32[8]{0:T(128)S(1)}, s32[8]{0:T(128)}, u32[]{:S(2)}) copy-start(s32[8]{0:T(128)} %constant.213.clone) | copy-start | bytes 100
  255.3 4.3 collective-permute-start.8
  255.4 5.3 collective-permute-start.13
  255.9 6.7 collective-permute-start.17
  344.4 41.8 %collective-permute-start.19 = (bf16[2,3,576,768]{3,2,1,0:T(8,128)(2,1)}, bf16[2,3,576,768]{3,2,1,0:T(8,128)(2,1)}, u32[]{:S(2)}, u32[]{:S(2)}) collective-permute-start(bf16[2,3,576,768]{3,2,1,0:T(8,128)(2,1)} %get-tuple-element.146), channel_id=1, source_target_pairs={{0,4},{4,0},{8,12},{12,8},{16,20},{20,16},{24,28},{28,24},{1,5},{5... | collective-permute-start | bytes 15925256 | tf_op jit(solution)/shard_map/ppermute | solution.py:728
  380.5 13.3 %collective-permute-start.18 = (bf16[2,3,576,768]{3,2,1,0:T(8,128)(2,1)}, bf16[2,3,576,768]{3,2,1,0:T(8,128)(2,1)}, u32[]{:S(2)}, u32[]{:S(2)}) collective-permute-start(bf16[2,3,576,768]{3,2,1,0:T(8,128)(2,1)} %get-tuple-element.143), channel_id=1, source_target_pairs={{0,4},{4,0},{8,12},{12,8},{16,20},{20,16},{24,28},{28,24},{1,5},{5... | collective-permute-start | bytes 15925256 | tf_op jit(solution)/shard_map/ppermute | solution.py:728
  380.9 91.6 %all-to-all-start.3 = ((bf16[4,4,64,1152]{3,2,1,0:T(8,128)(2,1)}), bf16[4,4,64,1152]{3,2,1,0:T(8,128)(2,1)}, u32[]{:S(2)}, u32[]{:S(2)}) async-start(bf16[4,4,64,1152]{3,2,1,0:T(8,128)(2,1)} %get-tuple-element.168), calls=%async_computation.3 | async-start | bytes 4718592 | tf_op jit(solution)/shard_map/all_to_all | solution.py:843
  401.4 63.9 %collective-permute-start.21 = (bf16[2,3,288,768]{3,2,1,0:T(8,128)(2,1)}, bf16[2,3,288,768]{3,2,1,0:T(8,128)(2,1)}, u32[]{:S(2)}, u32[]{:S(2)}) collective-permute-start(bf16[2,3,288,768]{3,2,1,0:T(8,128)(2,1)} %bitcast.160), channel_id=1, source_target_pairs={{0,8},{4,12},{8,0},{12,4},{16,24},{20,28},{24,16},{28,20},{1,9},{5... | collective-permute-start | bytes 7962632 | tf_op jit(solution)/shard_map/ppermute | solution.py:728
  402.0 63.3 %collective-permute-start.20 = (bf16[2,3,288,768]{3,2,1,0:T(8,128)(2,1)}, bf16[2,3,288,768]{3,2,1,0:T(8,128)(2,1)}, u32[]{:S(2)}, u32[]{:S(2)}) collective-permute-start(bf16[2,3,288,768]{3,2,1,0:T(8,128)(2,1)} %bitcast.161), channel_id=1, source_target_pairs={{0,16},{4,20},{8,24},{12,28},{16,0},{20,4},{24,8},{28,12},{1,17},{... | collective-permute-start | bytes 7962632 | tf_op jit(solution)/shard_map/ppermute | solution.py:728
  414.6 45.9 %copy-start.21 = (f32[2]{0:T(128)S(1)}, f32[2]{0:T(128)}, u32[]{:S(2)}) copy-start(f32[2]{0:T(128)} %constant.222) | copy-start | bytes 28
  414.7 46.1 %copy-start.13 = (f32[4,8,1152]{2,1,0:T(8,128)S(1)}, f32[4,8,1152]{2,1,0:T(8,128)}, u32[]{:S(2)}) copy-start(f32[4,8,1152]{2,1,0:T(8,128)} %get-tuple-element.161) | copy-start | bytes 442372
  414.7 46.1 %copy-start.14 = (f32[4,8,1152]{2,1,0:T(8,128)S(1)}, f32[4,8,1152]{2,1,0:T(8,128)}, u32[]{:S(2)}) copy-start(f32[4,8,1152]{2,1,0:T(8,128)} %get-tuple-element.162) | copy-start | bytes 442372
  462.4 8.5 %collective-permute-start.22 = (bf16[1,4,8,1152]{3,2,1,0:T(8,128)(2,1)}, bf16[1,4,8,1152]{3,2,1,0:T(8,128)(2,1)}, u32[]{:S(2)}, u32[]{:S(2)}) collective-permute-start(bf16[1,4,8,1152]{3,2,1,0:T(8,128)(2,1)} %fusion.32.one_ref), channel_id=1, source_target_pairs={{0,2},{1,3},{2,0},{3,1},{4,6},{5,7},{6,4},{7,5},{8,10},{9,11},{10,... | collective-permute-start | bytes 221192 | tf_op jit(solution)/shard_map/ppermute | solution.py:728
  472.5 57.8 %all-to-all-start.4 = ((bf16[4,4,64,1152]{3,2,1,0:T(8,128)(2,1)}), bf16[4,4,64,1152]{3,2,1,0:T(8,128)(2,1)}, u32[]{:S(2)}, u32[]{:S(2)}) async-start(bf16[4,4,64,1152]{3,2,1,0:T(8,128)(2,1)} %get-tuple-element.179), calls=%async_computation.4 | async-start | bytes 4718592 | tf_op jit(solution)/shard_map/all_to_all | solution.py:843
  477.3 8.3 %copy-start.33 = (s32[4]{0:T(128)S(1)}, s32[4]{0:T(128)}, u32[]{:S(2)}) copy-start(s32[4]{0:T(128)} %constant.214.clone) | copy-start | bytes 52
  477.3 8.8 %copy-start.15 = (bf16[2,4,8,1152]{3,2,1,0:T(8,128)(2,1)S(1)}, bf16[2,4,8,1152]{3,2,1,0:T(8,128)(2,1)}, u32[]{:S(2)}) copy-start(bf16[2,4,8,1152]{3,2,1,0:T(8,128)(2,1)} %append.5.one_ref) | copy-start | bytes 442372
  477.3 10.7 %copy-start.30 = (s32[32]{0:T(128)S(1)}, s32[32]{0:T(128)}, u32[]{:S(2)}) copy-start(s32[32]{0:T(128)} %get-tuple-element.191) | copy-start | bytes 388
  483.0 34.7 %collective-permute-start.24 = (bf16[2,3,144,768]{3,2,1,0:T(8,128)(2,1)}, bf16[2,3,144,768]{3,2,1,0:T(8,128)(2,1)}, u32[]{:S(2)}, u32[]{:S(2)}) collective-permute-start(bf16[2,3,144,768]{3,2,1,0:T(8,128)(2,1)} %bitcast.165), channel_id=1, source_target_pairs={{0,16},{4,20},{8,24},{12,28},{16,0},{20,4},{24,8},{28,12},{1,17},{... | collective-permute-start | bytes 3981320 | tf_op jit(solution)/shard_map/ppermute | solution.py:728
  483.5 34.2 %collective-permute-start.23 = (bf16[2,3,144,768]{3,2,1,0:T(8,128)(2,1)S(1)}, bf16[2,3,144,768]{3,2,1,0:T(8,128)(2,1)}, u32[]{:S(2)}, u32[]{:S(2)}) collective-permute-start(bf16[2,3,144,768]{3,2,1,0:T(8,128)(2,1)S(1)} %bitcast.164), channel_id=1, source_target_pairs={{0,8},{4,12},{8,0},{12,4},{16,24},{20,28},{24,16},{28,20},{1,9},{5... | collective-permute-start | bytes 3981320 | tf_op jit(solution)/shard_map/ppermute | solution.py:728
  486.0 31.6 %collective-permute-start.25 = (bf16[2,4,8,1152]{3,2,1,0:T(8,128)(2,1)S(1)}, bf16[2,4,8,1152]{3,2,1,0:T(8,128)(2,1)S(1)}, u32[]{:S(2)}, u32[]{:S(2)}) collective-permute-start(bf16[2,4,8,1152]{3,2,1,0:T(8,128)(2,1)S(1)} %copy-done.15), channel_id=1, source_target_pairs={{0,1},{1,0},{2,3},{3,2},{4,5},{5,4},{6,7},{7,6},{8,9},{9,8},{10,11... | collective-permute-start | bytes 442376 | tf_op jit(solution)/shard_map/ppermute | solution.py:728
  510.1 26.2 %collective-permute-start.26 = (bf16[4,576,1152]{2,1,0:T(8,128)(2,1)}, bf16[4,576,1152]{2,1,0:T(8,128)(2,1)}, u32[]{:S(2)}, u32[]{:S(2)}) collective-permute-start(bf16[4,576,1152]{2,1,0:T(8,128)(2,1)} %get-tuple-element.184), channel_id=1, source_target_pairs={{0,4},{4,0},{8,12},{12,8},{16,20},{20,16},{24,28},{28,24},{1,5},{5... | collective-permute-start | bytes 15925256 | tf_op jit(solution)/shard_map/ppermute | solution.py:728
  517.7 12.6 %copy-start.32 = (bf16[2,4,8,1152]{3,2,1,0:T(8,128)(2,1)}, bf16[2,4,8,1152]{3,2,1,0:T(8,128)(2,1)S(1)}, u32[]{:S(2)}) copy-start(bf16[2,4,8,1152]{3,2,1,0:T(8,128)(2,1)S(1)} %collective-permute-done.25.other_ref) | copy-start | bytes 442372
  532.1 11.8 %collective-permute-start.27 = (bf16[4,4,8,1152]{3,2,1,0:T(8,128)(2,1)}, bf16[4,4,8,1152]{3,2,1,0:T(8,128)(2,1)S(1)}, u32[]{:S(2)}, u32[]{:S(2)}) collective-permute-start(bf16[4,4,8,1152]{3,2,1,0:T(8,128)(2,1)} %append.6.one_ref), channel_id=1, source_target_pairs={{0,8},{4,12},{8,0},{12,4},{16,24},{20,28},{24,16},{28,20},{1,9},{5... | collective-permute-start | bytes 884744 | tf_op jit(solution)/shard_map/ppermute | solution.py:728
  536.3 61.7 %collective-permute-start.36 = (bf16[2,3,144,768]{3,2,1,0:T(8,128)(2,1)}, bf16[2,3,144,768]{3,2,1,0:T(8,128)(2,1)}, u32[]{:S(2)}, u32[]{:S(2)}) collective-permute-start(bf16[2,3,144,768]{3,2,1,0:T(8,128)(2,1)} %add_convert_fusion.1), channel_id=1, source_target_pairs={{0,1},{1,0},{2,3},{3,2},{4,5},{5,4},{6,7},{7,6},{8,9},{9,8},{10,11... | collective-permute-start | bytes 3981320 | tf_op jit(solution)/shard_map/ppermute | solution.py:728
  546.6 16.6 %collective-permute-start.29 = (bf16[8,4,8,1152]{3,2,1,0:T(8,128)(2,1)}, bf16[8,4,8,1152]{3,2,1,0:T(8,128)(2,1)}, u32[]{:S(2)}, u32[]{:S(2)}) collective-permute-start(bf16[8,4,8,1152]{3,2,1,0:T(8,128)(2,1)} %append.7.one_ref), channel_id=1, source_target_pairs={{0,16},{4,20},{8,24},{12,28},{16,0},{20,4},{24,8},{28,12},{1,17},{... | collective-permute-start | bytes 1769480 | tf_op jit(solution)/shard_map/ppermute | solution.py:728
  547.1 29.8 %collective-permute-start.30 = (bf16[2,288,1152]{2,1,0:T(8,128)(2,1)}, bf16[2,288,1152]{2,1,0:T(8,128)(2,1)}, u32[]{:S(2)}, u32[]{:S(2)}) collective-permute-start(bf16[2,288,1152]{2,1,0:T(8,128)(2,1)} %get-tuple-element.203), channel_id=1, source_target_pairs={{0,8},{4,12},{8,0},{12,4},{16,24},{20,28},{24,16},{28,20},{1,9},{5... | collective-permute-start | bytes 3981320 | tf_op jit(solution)/shard_map/ppermute | solution.py:728
  547.7 41.7 %collective-permute-start.28 = (bf16[2,288,1152]{2,1,0:T(8,128)(2,1)}, bf16[2,288,1152]{2,1,0:T(8,128)(2,1)}, u32[]{:S(2)}, u32[]{:S(2)}) collective-permute-start(bf16[2,288,1152]{2,1,0:T(8,128)(2,1)} %get-tuple-element.197), channel_id=1, source_target_pairs={{0,16},{4,20},{8,24},{12,28},{16,0},{20,4},{24,8},{28,12},{1,17},{... | collective-permute-start | bytes 3981320 | tf_op jit(solution)/shard_map/ppermute | solution.py:728
  557.6 8.0 %copy-start.29 = (s32[32]{0:T(128)S(1)}, s32[32]{0:T(128)}, u32[]{:S(2)}) copy-start(s32[32]{0:T(128)} %get-tuple-element.206) | copy-start | bytes 388
  557.6 8.1 %copy-start.8 = (bf16[6,144,768]{2,1,0:T(8,128)(2,1)S(1)}, bf16[6,144,768]{2,1,0:T(8,128)(2,1)}, u32[]{:S(2)}) copy-start(bf16[6,144,768]{2,1,0:T(8,128)(2,1)} %get-tuple-element.167) | copy-start | bytes 3981316
  565.5 32.5 %collective-permute-start.31 = (bf16[16,4,8,1152]{3,2,1,0:T(8,128)(2,1)}, bf16[16,4,8,1152]{3,2,1,0:T(8,128)(2,1)}, u32[]{:S(2)}, u32[]{:S(2)}) collective-permute-start(bf16[16,4,8,1152]{3,2,1,0:T(8,128)(2,1)} %append.8.one_ref), channel_id=1, source_target_pairs={{0,4},{4,0},{8,12},{12,8},{16,20},{20,16},{24,28},{28,24},{1,5},{5... | collective-permute-start | bytes 3538952 | tf_op jit(solution)/shard_map/ppermute | solution.py:728
  592.0 18.9 %collective-permute-start.33 = (bf16[2,144,1152]{2,1,0:T(8,128)(2,1)}, bf16[2,144,1152]{2,1,0:T(8,128)(2,1)}, u32[]{:S(2)}, u32[]{:S(2)}) collective-permute-start(bf16[2,144,1152]{2,1,0:T(8,128)(2,1)} %get-tuple-element.214), channel_id=1, source_target_pairs={{0,8},{4,12},{8,0},{12,4},{16,24},{20,28},{24,16},{28,20},{1,9},{5... | collective-permute-start | bytes 1990664 | tf_op jit(solution)/shard_map/ppermute | solution.py:728
  592.6 42.0 %collective-permute-start.32 = (bf16[2,144,1152]{2,1,0:T(8,128)(2,1)}, bf16[2,144,1152]{2,1,0:T(8,128)(2,1)}, u32[]{:S(2)}, u32[]{:S(2)}) collective-permute-start(bf16[2,144,1152]{2,1,0:T(8,128)(2,1)} %get-tuple-element.212), channel_id=1, source_target_pairs={{0,16},{4,20},{8,24},{12,28},{16,0},{20,4},{24,8},{28,12},{1,17},{... | collective-permute-start | bytes 1990664 | tf_op jit(solution)/shard_map/ppermute | solution.py:728
  593.0 71.5 %all-to-all-start.5 = ((bf16[32,64,1152]{2,1,0:T(8,128)(2,1)}), bf16[32,64,1152]{2,1,0:T(8,128)(2,1)}, u32[]{:S(2)}, u32[]{:S(2)}) async-start(bf16[32,64,1152]{2,1,0:T(8,128)(2,1)} %gather_fusion.8), calls=%async_computation.5 | async-start | bytes 9437184 | tf_op jit(solution)/shard_map/all_to_all | solution.py:1081
  600.5 32.8 %collective-permute-start.37 = (bf16[1,3,144,768]{3,2,1,0:T(8,128)(2,1)}, bf16[1,3,144,768]{3,2,1,0:T(8,128)(2,1)}, u32[]{:S(2)}, u32[]{:S(2)}) collective-permute-start(bf16[1,3,144,768]{3,2,1,0:T(8,128)(2,1)} %slice.143), channel_id=1, source_target_pairs={{0,2},{1,3},{2,0},{3,1},{4,6},{5,7},{6,4},{7,5},{8,10},{9,11},{10,... | collective-permute-start | bytes 1990664 | tf_op jit(solution)/shard_map/ppermute | solution.py:728
  612.1 30.0 %copy-start.10 = (bf16[2,144,1152]{2,1,0:T(8,128)(2,1)S(1)}, bf16[2,144,1152]{2,1,0:T(8,128)(2,1)}, u32[]{:S(2)}) copy-start(bf16[2,144,1152]{2,1,0:T(8,128)(2,1)} %get-tuple-element.211) | copy-start | bytes 1990660
  612.1 30.0 %collective-permute-start.34 = (bf16[2,144,1152]{2,1,0:T(8,128)(2,1)S(1)}, bf16[2,144,1152]{2,1,0:T(8,128)(2,1)S(1)}, u32[]{:S(2)}, u32[]{:S(2)}) collective-permute-start(bf16[2,144,1152]{2,1,0:T(8,128)(2,1)S(1)} %add_convert_fusion.5), channel_id=1, source_target_pairs={{0,1},{1,0},{2,3},{3,2},{4,5},{5,4},{6,7},{7,6},{8,9},{9,8},{10,11... | collective-permute-start | bytes 1990664 | tf_op jit(solution)/shard_map/ppermute | solution.py:728
  643.5 17.5 %copy-start.5 = (f32[864,864]{1,0:T(8,128)S(1)}, f32[864,864]{1,0:T(8,128)}, u32[]{:S(2)}) copy-start(f32[864,864]{1,0:T(8,128)} %constant.216.clone) | copy-start | bytes 8957956
  643.5 17.4 %collective-permute-start.35 = (bf16[1,144,1152]{2,1,0:T(8,128)(2,1)S(1)}, bf16[1,144,1152]{2,1,0:T(8,128)(2,1)S(1)}, u32[]{:S(2)}, u32[]{:S(2)}) collective-permute-start(bf16[1,144,1152]{2,1,0:T(8,128)(2,1)S(1)} %slice.138), channel_id=1, source_target_pairs={{0,2},{1,3},{2,0},{3,1},{4,6},{5,7},{6,4},{7,5},{8,10},{9,11},{10,... | collective-permute-start | bytes 995336 | tf_op jit(solution)/shard_map/ppermute | solution.py:728
  664.6 9.0 %copy-start.1 = (bf16[1152,3,288]{0,2,1:T(8,128)(2,1)S(1)}, bf16[1152,3,288]{0,2,1:T(8,128)(2,1)}, u32[]{:S(2)}) copy-start(bf16[1152,3,288]{0,2,1:T(8,128)(2,1)} %param.36) | copy-start | bytes 5971972
  (21 other events, 96.6 us)
Sparse Core Ops, SparseCore 0:
  11.5 150.5 all-gather.2

commit v11 on v10

--- a/solution.py
+++ b/solution.py
@@ -434,7 +434,7 @@
         out_specs=pl.BlockSpec((1,) + silu.shape, lambda k: (k, 0, 0)),
         out_shape=jax.ShapeDtypeStruct((kinds,) + silu.shape, f32),
         compiler_params=pltpu.CompilerParams(vmem_limit_bytes=60 << 20),
-        cost_estimate=lasting(60),
+        cost_estimate=lasting(0),
         name="modulate",
     )(silu, ada)
 
@@ -690,7 +690,7 @@
         kernel,
         in_specs=specs,
         out_specs=pl.BlockSpec(shape, lambda: (0,) * len(shape)),
-        out_shape=jax.ShapeDtypeStruct(shape, bf16),
+        out_shape=jax.ShapeDtypeStruct(shape, arrays[0].dtype),
         compiler_params=pltpu.CompilerParams(vmem_limit_bytes=60 << 20),
         cost_estimate=lasting(microseconds),
         name=name,
@@ -726,16 +726,6 @@
 def swap(values, axis, bit):
     size = lax.axis_size(axis)
     return lax.ppermute(values, axis, [(i, i ^ bit) for i in range(size)])
-
-
-def xor_gather(values, axes_bits):
-    names = sorted({axis for axis, _ in axes_bits})
-    places = [{name: 0 for name in names}]
-    values = values[None]
-    for axis, bit in axes_bits:
-        values = jnp.concatenate([values, swap(values, axis, bit)], axis=0)
-        places = places + [dict(place, **{axis: place[axis] ^ bit}) for place in places]
-    return values, {name: [place[name] for place in places] for name in names}
 
 
 def halving_order(bits):
@@ -856,10 +846,6 @@
     send_index = pair_slot * dp_size + jnp.mod(inverse[pair_peer] - my_start, dp_size)
     send_index = jnp.minimum(send_index, capacity - 1)
     send_patches = take_rows(patches, send_index)
-    info, info_places = xor_gather(
-        jnp.stack([time_bins, labels]), [("dp", bit) for bit in bits_of(dp_size)]
-    )
-    send_patches, info = tie(send_patches, info)
     share = 4 * local_dim // dp_size
     spots = lax.dynamic_slice_in_dim(jnp.array(places), dp_index * share, share, 0)
     take_qkv = (spots[:, None] == jnp.arange(3 * local_dim)[None, :]).astype(bf16)
@@ -869,13 +855,22 @@
     share = unit_count // dp_size
     spots = dp_index * share + jnp.arange(share)
     take_units = (spots[:, None] == jnp.arange(unit_count)[None, :]).astype(bf16)
+    expand_kinds = tie(expand_weight.swapaxes(0, 1))[0]
     mlp_piece = jnp.stack(
         [
-            ein("rf,df->rd", take_units, expand_weight[:, 0]).astype(bf16),
-            ein("rf,df->rd", take_units, expand_weight[:, 1]).astype(bf16),
+            dot_11(take_units, expand_kinds[0]).astype(bf16),
+            dot_11(take_units, expand_kinds[1]).astype(bf16),
             lax.dynamic_slice_in_dim(down_weight, dp_index * share, share, 0),
         ]
     )
+    info = jnp.stack([time_bins, labels])[None]
+    info_places = [0]
+    for bit in bits_of(dp_size):
+        got_info = swap(info, "dp", bit)
+        if bit * 2 == dp_size:
+            send_patches, got_info, attend_piece = tie(send_patches, got_info, attend_piece)
+        info = append(info, got_info, 200)
+        info_places = info_places + [place ^ bit for place in info_places]
     attend_full = gather_pieces(attend_piece, mp_size).reshape(mp_size, 4 * local_dim, -1)
     by_permutes = share % 32 == 0 and dp_size == 8 and mp_size == 4
     if by_permutes:
@@ -889,7 +884,7 @@
 
     recv_patches = lax.all_to_all(send_patches, "dp", split_axis=0, concat_axis=0, tiled=True)
     info = info.swapaxes(0, 1).reshape(2, -1)
-    info_owner = jnp.repeat(dp_index ^ jnp.array(info_places["dp"]), capacity)
+    info_owner = jnp.repeat(dp_index ^ jnp.array(info_places), capacity)
     info_slot = jnp.tile(jnp.arange(capacity), dp_size)
     info_count = jnp.sum(
         jnp.where(info_owner[:, None] == device_ids[None, :], image_counts[None, :], 0), axis=1
@@ -945,6 +940,7 @@
         ],
         axis=1,
     )
+    mods, starts, image_counts, dest_perm, my_place = tie(mods, starts, image_counts, dest_perm, my_place)
     back_within = pair_slot * dp_size + jnp.mod(my_place - starts[pair_peer], dp_size)
     back_valid = back_within < image_counts[pair_peer]
     back_slot = jnp.clip((starts[pair_peer] + back_within - my_place) // dp_size, 0, images - 1)
@@ -1043,8 +1039,8 @@
 
     kept_one, sent_one = sum_halves(kept_one, got_one, 200)
     kept_one = more(kept_one)
-    latent_back, packed = tie(latent_back, packed)
-    kept_zero, sent_zero = sum_halves(kept_zero, got_zero, 200)
+    kept_one, kept_zero = tie(kept_one, kept_zero)
+    kept_zero, sent_zero = sum_halves(kept_zero, got_zero)
     normed_t, kept_one, kept_zero, result = tie(normed_t, kept_one, kept_zero, result)
     got_one = swap(sent_one, "dp", dp_bits[1][2])
     got_zero = swap(sent_zero, "dp", dp_bits[0][2])
@@ -1072,12 +1068,11 @@
     back_patches = take_rows(latent_back, back_slot)
     attend_got_one = swap(sent_one, "dp", dp_bits[1][1])
     attend_got_zero = swap(sent_zero, "dp", dp_bits[0][1])
-    attend_zero = more(attend_zero)
     back_patches, attend_zero, attend_one = tie(back_patches, attend_zero, attend_one)
     attend_zero = more(attend_zero)
     attend_one, sent_one = sum_halves(attend_one, attend_got_one)
     attend_zero, sent_zero = sum_halves(attend_zero, attend_got_zero)
-    back_patches, sent_one, sent_zero = tie(back_patches, sent_one, sent_zero)
+    back_patches, sent_one, sent_zero, mlp_zero = tie(back_patches, sent_one, sent_zero, mlp_zero)
     got_patches = lax.all_to_all(back_patches, "dp", split_axis=0, concat_axis=0, tiled=True)
     patch_grad = take_rows(got_patches, home_index)
     attend_got_one = swap(sent_one, "dp", dp_bits[1][2])

time: 690 us -> 667 us (0.967)
  waiting for transfers between devices: 212 us -> 178 us
  other arithmetic: 28.9 us -> 37 us
    all_to_all x1, waiting for transfers between devices: 60.9 us -> 39.9 us  [shards(): lax.all_to_all(send_patches, 'dp', split_axis=0, concat_axis=0, tiled=True)]
    ppermute x38, waiting for transfers between devices: 138 us -> 123 us  [swap(): return lax.ppermute(values, axis, [(i, i ^ bit) for i in range(size)])]
    slice x1 -> x0, local copies, waits for them, and re-layouts: 7.91 us -> none  [shards(): expand_weight[:, 0]]
    unnamed x85 -> x126, local copies, waits for them, and re-layouts: 9.48 us -> 16.8 us
    pallas_call x6 -> x9, Pallas kernels: 14.2 us -> 18.6 us  [whole_arrays(): pl.pallas_call(kernel, in_specs=specs, out_specs=pl.BlockSpec(shape, lamb...]
  transfers between devices with their start and end apart: 45 -> 45, of which waited for: 16 -> 15; matrix products, arithmetic and copies ran while one was open for 12% -> 14% of each run, Pallas kernels for 37% -> 39%
where the time goes in v11:
time: 667 us; the launch traced here: 658 us
  Pallas kernels  298 us (45%)
  waiting for transfers between devices  178 us (27%)
  starting transfers between devices  62.1 us (9%)
  local copies, waits for them, and re-layouts  54.1 us (8%)
  other arithmetic  37 us (6%)
  between operations  15.4 us (2%)
  matrix products  13.7 us (2%)
    ppermute x38, waiting for transfers between devices, swap(): return lax.ppermute(values, axis, [(i, i ^ bit) for i in range(size)])  123 us
    pallas_call x2, Pallas kernels, mlp_back(): pl.pallas_call(mlp_back_kernel, grid_spec=pltpu.PrefetchScalarGridSpec(nu...  72.2 us
    pallas_call x1, Pallas kernels, attend_back(): pl.pallas_call(attend_back_kernel, grid=(groups,), in_specs=[whole_spec(l...  44.9 us
    all_to_all x1, waiting for transfers between devices, shards(): lax.all_to_all(send_patches, 'dp', split_axis=0, concat_axis=0, tiled=True)  39.9 us
    pallas_call x1, Pallas kernels, mlp(): pl.pallas_call(functools.partial(mlp_kernel, len(pieces)), grid_spec=pltp...  37.8 us
    pallas_call x1, Pallas kernels, attend(): pl.pallas_call(attend_kernel, grid=(groups,), in_specs=[whole_spec(latent...  36 us
    ppermute x38, starting transfers between devices, swap(): return lax.ppermute(values, axis, [(i, i ^ bit) for i in range(size)])  33.1 us
    pallas_call x6, Pallas kernels, sum_halves(): pl.pallas_call(sum_halves_kernel, grid=(kept.shape[0],), in_specs=[whole,...  31.7 us
  transfers between devices with their start and end apart: 45, of which 15 were waited for; matrix products, arithmetic and copies ran while one was open for 14% of the time, Pallas kernels for 39%

profile of v11, /device:TPU:0, one launch (start us, length us, event | category | flops | bytes accessed | tf_op | source)
XLA Modules:
  0.0 657.8 jit_solution(3513119213032273460)
XLA Ops:
  8.5 2.4 copy.98
  14.3 3.6 collective-permute-start.3
  33.6 1.5 collective-permute-start.2
  36.9 5.7 gather_fusion.1
  43.9 4.6 all-to-all-start
  55.8 1.6 collective-permute-start.4
  58.1 8.7 %modulate.1 = f32[6,16,1152]{2,1,0:T(8,128)} custom-call(bf16[16,1152]{1,0:T(8,128)(2,1)} %pad.8.silu_ref, bf16[6,1152,1152]{2,1,0:T(8,128)(2,1)} %bitcast.145), custom_call_target="tpu_custom_call" | custom-call | bytes 1024 | tf_op jit(solution)/shard_map/modulate/pallas_call | solution.py:427
  74.5 39.9 %all-to-all-done = bf16[32,64,1152]{2,1,0:T(8,128)(2,1)} async-done(((bf16[32,64,1152]{2,1,0:T(8,128)(2,1)}), bf16[32,64,1152]{2,1,0:T(8,128)(2,1)}, u32[]{:S(2)}, u32[]{:S(2)}) %all-to-all-start) | async-done | bytes 4718624 | tf_op jit(solution)/shard_map/all_to_all | solution.py:885
  114.4 4.6 gather_fusion.6
  119.1 4.5 all-to-all-start.1
  123.6 2.0 pad_maximum_fusion.refs_0_
  125.8 2.0 fusion.58
  129.2 1.7 collective-permute-start.6
  130.9 2.0 collective-permute-start.15
  136.5 40.3 %collective-permute-done.9.refs_4_ = bf16[4,3,48,1152]{3,2,1,0:T(8,128)(2,1)} collective-permute-done((bf16[4,3,48,1152]{3,2,1,0:T(8,128)(2,1)}, bf16[4,3,48,1152]{3,2,1,0:T(8,128)(2,1)}, u32[]{:S(2)}, u32[]{:S(2)}) %collective-permute-start.9) | collective-permute-done | bytes 1327136 | tf_op jit(solution)/shard_map/ppermute | solution.py:728
  176.8 27.9 %collective-permute-done.15.refs_10_ = bf16[4,3,48,1152]{3,2,1,0:T(8,128)(2,1)} collective-permute-done((bf16[4,3,48,1152]{3,2,1,0:T(8,128)(2,1)}, bf16[4,3,48,1152]{3,2,1,0:T(8,128)(2,1)}, u32[]{:S(2)}, u32[]{:S(2)}) %collective-permute-start.15) | collective-permute-done | bytes 1327136 | tf_op jit(solution)/shard_map/ppermute | solution.py:728
  207.1 4.8 all-to-all-start.2
  212.0 36.0 %attend.1 = (f32[4,864,1024]{2,1,0:T(8,128)}, bf16[4,288,1024]{2,1,0:T(8,128)(2,1)}, bf16[1024,1152]{1,0:T(8,128)(2,1)}, bf16[1152,1024]{1,0:T(8,128)(2,1)}, f32...) custom-call(bf16[4,4,64,1152]{3,2,1,0:T(8,128)(2,1)} %all-to-all-done.1.latent_ref, ...), custom_call_target="tpu_custom_call" | custom-call | flops 176000008192 | bytes 1024 | tf_op jit(solution)/shard_map/attend/pallas_call | solution.py:286
  250.3 1.9 collective-permute-done.8.refs_3_
  253.3 1.9 collective-permute-done.17.refs_13_
  255.2 37.8 %mlp.1 = (bf16[4,2,1024,768]{3,2,1,0:T(8,128)(2,1)}, f32[1024,1152]{1,0:T(8,128)}, bf16[4,3,768,1152]{3,2,1,0:T(8,128)(2,1)}) custom-call(s32[14]{0:T(128)} %stack.93.e_ref, bf16[1024,1152]{1,0:T(8,128)(2,1)} %get-tuple-element.138.x_ref, bf16[4,3,96,1152]{3,2,1,0:T(8,128)(2,1)} %copy-done.10, bf16[4,3,96,1152]{3,2,1,0:T(8,128)(2,1)} %collective-permute-done.7.refs_1_, ...), custom_call_target="tpu_custom_call" | custom-call | flops 1100000000 | bytes 1024 | tf_op jit(solution)/shard_map/mlp/pallas_call | solution.py:479
  293.0 7.7 %finish.1 = (bf16[1024,1152]{1,0:T(8,128)(2,1)}, bf16[1152,1024]{1,0:T(8,128)(2,1)}, bf16[4,4,64,1152]{3,2,1,0:T(8,128)(2,1)}, f32[4,8,1152]{2,1,0:T(8,128)}) custom-call(f32[1024,1152]{1,0:T(8,128)} %get-tuple-element.147.branch_ref, f32[1024,1152]{1,0:T(8,128)} %get-tuple-element.148.middle_ref, bf16[4,4,64,1152]{3,2,1,0:T(8,128)(2,1)} %all-to-all-done.2.cot_ref, ...), custom_call_target="tpu_custom_call" | custom-call | flops 1100000000 | bytes 1024 | tf_op jit(solution)/shard_map/finish/pallas_call | solution.py:409
  300.8 36.2 %mlp_back.2 = (bf16[2,3,576,768]{3,2,1,0:T(8,128)(2,1)}, bf16[2,3,576,768]{3,2,1,0:T(8,128)(2,1)}, f32[1024,1152]{1,0:T(8,128)}) custom-call(s32[8]{0:T(128)} %broadcast_xor_fusion.2.e_ref, bf16[8,144,1024]{2,1,0:T(8,128)(2,1)} %bitcast.171, bf16[8,144,1024]{2,1,0:T(8,128)(2,1)} %bitcast.167, bf16[1024,1152]{1,0:T(8,128)(2,1)} %get-tuple-element.151.low_ref, ...), custom_call_target="tpu_custom_call" | custom-call | flops 165000003584 | bytes 1024 | tf_op jit(solution)/shard_map/mlp_back/pallas_call | solution.py:555
  337.1 36.0 %mlp_back.3 = (bf16[2,3,576,768]{3,2,1,0:T(8,128)(2,1)}, bf16[2,3,576,768]{3,2,1,0:T(8,128)(2,1)}, f32[1024,1152]{1,0:T(8,128)}) custom-call(s32[8]{0:T(128)} %broadcast_xor_fusion.1.e_ref, bf16[8,144,1024]{2,1,0:T(8,128)(2,1)} %bitcast.172, bf16[8,144,1024]{2,1,0:T(8,128)(2,1)} %bitcast.168, bf16[1024,1152]{1,0:T(8,128)(2,1)} %get-tuple-element.151.low_ref, ...), custom_call_target="tpu_custom_call" | custom-call | flops 165000003584 | bytes 1024 | tf_op jit(solution)/shard_map/mlp_back/pallas_call | solution.py:555
  373.5 5.3 all-to-all-start.3
  378.8 7.6 %sum_halves.7 = (bf16[6,288,768]{2,1,0:T(8,128)(2,1)}, bf16[6,288,768]{2,1,0:T(8,128)(2,1)}) custom-call(bf16[6,576,768]{2,1,0:T(8,128)(2,1)} %bitcast.151, bf16[6,576,768]{2,1,0:T(8,128)(2,1)} %bitcast.52.got_ref), custom_call_target="tpu_custom_call" | custom-call | bytes 1024 | tf_op jit(solution)/shard_map/sum_halves/pallas_call | solution.py:757
  386.4 7.6 %sum_halves.6 = (bf16[6,288,768]{2,1,0:T(8,128)(2,1)}, bf16[6,288,768]{2,1,0:T(8,128)(2,1)}) custom-call(bf16[6,576,768]{2,1,0:T(8,128)(2,1)} %bitcast.150, bf16[6,576,768]{2,1,0:T(8,128)(2,1)} %bitcast.49.got_ref), custom_call_target="tpu_custom_call" | custom-call | bytes 1024 | tf_op jit(solution)/shard_map/sum_halves/pallas_call | solution.py:757
  396.1 11.1 %middle.1 = (f32[1024,1152]{1,0:T(8,128)}, bf16[1024,1152]{1,0:T(8,128)(2,1)}, bf16[1152,1024]{1,0:T(8,128)(2,1)}, f32[4,8,1152]{2,1,0:T(8,128)}) custom-call(f32[1024,1152]{1,0:T(8,128)} %get-tuple-element.163.one_ref, f32[1024,1152]{1,0:T(8,128)} %get-tuple-element.164.other_ref, f32[1024,1152]{1,0:T(8,128)} %get-tuple-element.148.middle_ref, ...), custom_call_target="tpu_custom_call" | custom-call | flops 109999996928 | bytes 1024 | tf_op jit(solution)/shard_map/middle/pallas_call | solution.py:409
  407.2 44.9 %attend_back.1 = (bf16[4,864,1024]{2,1,0:T(8,128)(2,1)}, f32[2,72,256]{2,1,0:T(8,128)}, f32[4,8,1152]{2,1,0:T(8,128)}, bf16[4,4,64,1152]{3,2,1,0:T(8,128)(2,1)}) custom-call(bf16[4,4,64,1152]{3,2,1,0:T(8,128)(2,1)} %all-to-all-done.1.latent_ref, f32[4,864,1024]{2,1,0:T(8,128)} %get-tuple-element.162.proj_ref, bf16[1024,1152]{1,0:T(8,128)(2,1)} %get-tuple-element.166.low_ref, ...), custom_call_target="tpu_custom_call" | custom-call | flops 1100000000 | bytes 1024 | tf_op jit(solution)/shard_map/attend_back/pallas_call | solution.py:330
  453.3 1.6 fusion.32.one_ref
  454.9 3.0 collective-permute-start.22
  457.9 4.8 all-to-all-start.4
  462.7 5.6 sum_halves.8
  468.3 5.6 sum_halves.9
  477.0 1.6 append.11.one_ref
  478.6 2.0 collective-permute-start.25
  481.2 21.4 %attend_grads.1 = (bf16[4,576,1152]{2,1,0:T(8,128)(2,1)}, bf16[4,576,1152]{2,1,0:T(8,128)(2,1)}) custom-call(s32[4]{0:T(128)} %broadcast_xor_fusion.m_ref, s32[16]{0:T(128)} %pad_add_fusion.e_ref, bf16[8,144,1024]{2,1,0:T(8,128)(2,1)} %bitcast.154, bf16[8,144,1024]{2,1,0:T(8,128)(2,1)} %bitcast.155, bf16[4,864,1024]{2,1,0:T(8,128)(2,1)} %get-tuple-element.187.proj_ref, ...), custom_call_target="tpu_custom_call" | custom-call | bytes 1024 | tf_op jit(solution)/shard_map/attend_grads/pallas_call | solution.py:608
  503.1 12.5 %all-to-all-done.4 = bf16[4,4,64,1152]{3,2,1,0:T(8,128)(2,1)} async-done(((bf16[4,4,64,1152]{3,2,1,0:T(8,128)(2,1)}), bf16[4,4,64,1152]{3,2,1,0:T(8,128)(2,1)}, u32[]{:S(2)}, u32[]{:S(2)}) %all-to-all-start.4) | async-done | bytes 2359328 | tf_op jit(solution)/shard_map/all_to_all | solution.py:833
  515.7 2.1 append.12.one_ref
  518.9 7.7 %sum_quarters.1 = (bf16[2,288,1152]{2,1,0:T(8,128)(2,1)}, bf16[2,288,1152]{2,1,0:T(8,128)(2,1)}, bf16[2,288,1152]{2,1,0:T(8,128)(2,1)}, bf16[2,288,1152]{2,1,0:T(8,128)(2,1)}) custom-call(bf16[4,576,1152]{2,1,0:T(8,128)(2,1)} %get-tuple-element.197.kept_ref, bf16[4,576,1152]{2,1,0:T(8,128)(2,1)} %collective-permute-done.26.got_ref), custom_call_target="tpu_custom_call" | custom-call | bytes 1024 | tf_op jit(solution)/shard_map/sum_quarters/pallas_call | solution.py:675
  529.0 3.3 append_zero.1
  532.2 5.2 gather_fusion.8
  537.4 2.1 append.13.one_ref
  540.0 2.7 add_convert_fusion.1
  542.7 1.6 add_convert_fusion.2
  544.4 12.4 %collective-permute-done.29.got_ref = bf16[2,288,1152]{2,1,0:T(8,128)(2,1)} collective-permute-done((bf16[2,288,1152]{2,1,0:T(8,128)(2,1)}, bf16[2,288,1152]{2,1,0:T(8,128)(2,1)}, u32[]{:S(2)}, u32[]{:S(2)}) %collective-permute-start.29) | collective-permute-done | bytes 1327136 | tf_op jit(solution)/shard_map/ppermute | solution.py:728
  556.8 2.7 sum_halves.11
  559.9 2.6 sum_halves.10
  563.7 6.2 collective-permute-done.30.other_ref
  570.7 2.3 append.14.one_ref
  573.2 1.5 collective-permute-start.32
  574.7 4.9 all-to-all-start.5
  579.7 2.3 add_convert_fusion.5
  583.0 1.6 add_convert_fusion
  586.3 3.2 append.15
  590.5 3.1 copy.95
  593.7 2.7 fusion.12
  596.4 2.8 fusion.28
  600.0 8.3 %collective-permute-done.34 = bf16[2,144,1152]{2,1,0:T(8,128)(2,1)} collective-permute-done((bf16[2,144,1152]{2,1,0:T(8,128)(2,1)}, bf16[2,144,1152]{2,1,0:T(8,128)(2,1)}, u32[]{:S(2)}, u32[]{:S(2)}) %collective-permute-start.34) | collective-permute-done | bytes 663584 | tf_op jit(solution)/shard_map/ppermute | solution.py:728
  611.7 20.7 %collective-permute-done.35 = bf16[1,144,1152]{2,1,0:T(8,128)(2,1)S(1)} collective-permute-done((bf16[1,144,1152]{2,1,0:T(8,128)(2,1)S(1)}, bf16[1,144,1152]{2,1,0:T(8,128)(2,1)S(1)}, u32[]{:S(2)}, u32[]{:S(2)}) %collective-permute-start.35) | collective-permute-done | bytes 331808 | tf_op jit(solution)/shard_map/ppermute | solution.py:728
  637.4 1.6 copy.85
  639.7 1.7 all-to-all-done.5
  641.4 5.7 gather_fusion.9
  647.1 3.3 copy.101
  (306 shorter events, 77.7 us)
Async XLA Ops:
  7.2 17.0 %copy-start = (bf16[1152,3,288]{0,2,1:T(8,128)(2,1)S(1)}, bf16[1152,3,288]{0,2,1:T(8,128)(2,1)}, u32[]{:S(2)}) copy-start(bf16[1152,3,288]{0,2,1:T(8,128)(2,1)} %param.36) | copy-start | bytes 5971972
  8.0 18.1 %collective-permute-start = (s32[1,2,32]{2,1,0:T(2,128)S(1)}, s32[1,2,32]{2,1,0:T(2,128)S(1)}, u32[]{:S(2)}, u32[]{:S(2)}) collective-permute-start(s32[1,2,32]{2,1,0:T(2,128)S(1)} %add_bitcast_fusion.one_ref), channel_id=1, source_target_pairs={{0,4},{4,0},{8,12},{12,8},{16,20},{20,16},{24,28},{28,24},{1,5},{5... | collective-permute-start | bytes 776 | tf_op jit(solution)/shard_map/ppermute | solution.py:728
  11.7 11.3 %copy-start.18 = (bf16[288,1152]{1,0:T(8,128)(2,1)S(1)}, bf16[288,1152]{1,0:T(8,128)(2,1)}, u32[]{:S(2)}) copy-start(bf16[288,1152]{1,0:T(8,128)(2,1)} %param.38) | copy-start | bytes 1990660
  14.3 40.1 %collective-permute-start.3 = (bf16[1,3,96,1152]{3,2,1,0:T(8,128)(2,1)}, bf16[1,3,96,1152]{3,2,1,0:T(8,128)(2,1)}, u32[]{:S(2)}, u32[]{:S(2)}) collective-permute-start(bf16[1,3,96,1152]{3,2,1,0:T(8,128)(2,1)} %maximum_bitcast_fusion), channel_id=1, source_target_pairs={{0,2},{1,3},{2,0},{3,1},{4,6},{5,7},{6,4},{7,5},{8,10},{9,11},{10,... | collective-permute-start | bytes 1990664 | tf_op jit(solution)/shard_map/ppermute | solution.py:728
  27.9 3.8 collective-permute-start.1
  33.6 9.7 %collective-permute-start.2 = (s32[4,2,32]{2,1,0:T(2,128)}, s32[4,2,32]{2,1,0:T(2,128)S(1)}, u32[]{:S(2)}, u32[]{:S(2)}) collective-permute-start(s32[4,2,32]{2,1,0:T(2,128)} %append.9.one_ref), channel_id=1, source_target_pairs={{0,16},{4,20},{8,24},{12,28},{16,0},{20,4},{24,8},{28,12},{1,17},{... | collective-permute-start | bytes 3080 | tf_op jit(solution)/shard_map/ppermute | solution.py:728
  43.9 70.5 %all-to-all-start = ((bf16[32,64,1152]{2,1,0:T(8,128)(2,1)}), bf16[32,64,1152]{2,1,0:T(8,128)(2,1)}, u32[]{:S(2)}, u32[]{:S(2)}) async-start(bf16[32,64,1152]{2,1,0:T(8,128)(2,1)} %gather_fusion.1), calls=%async_computation | async-start | bytes 9437184 | tf_op jit(solution)/shard_map/all_to_all | solution.py:885
  48.5 163.4 %all-gather.3.cloned.1.call-start = ((), (), s32[]{:S(2)}) async-start(), calls=%async_computation.6 | async-start | bytes 10948608 | tf_op jit(solution)/shard_map/all_gather | solution.py:641
  55.8 67.8 %collective-permute-start.4 = (bf16[2,3,96,1152]{3,2,1,0:T(8,128)(2,1)S(1)}, bf16[2,3,96,1152]{3,2,1,0:T(8,128)(2,1)}, u32[]{:S(2)}, u32[]{:S(2)}) collective-permute-start(bf16[2,3,96,1152]{3,2,1,0:T(8,128)(2,1)S(1)} %pad_maximum_fusion.1), channel_id=1, source_target_pairs={{0,1},{1,0},{2,3},{3,2},{4,5},{5,4},{6,7},{7,6},{8,9},{9,8},{10,11... | collective-permute-start | bytes 3981320 | tf_op jit(solution)/shard_map/ppermute | solution.py:728
  58.1 9.8 %copy-start.42 = (f32[8]{0:T(128)S(1)}, f32[8]{0:T(128)}, u32[]{:S(2)}) copy-start(f32[8]{0:T(128)} %pad.28.clone) | copy-start | bytes 100
  58.1 10.6 %copy-start.3 = (s32[8]{0:T(128)S(1)}, s32[8]{0:T(128)}, u32[]{:S(2)}) copy-start(s32[8]{0:T(128)} %copy-done.2) | copy-start | bytes 100
  58.1 12.0 %copy-start.57 = (s32[8,1]{0,1:T(1,128)S(1)}, s32[8,1]{0,1:T(1,128)}, u32[]{:S(2)}) copy-start(s32[8,1]{0,1:T(1,128)} %copy-done.56) | copy-start | bytes 100
  58.1 12.8 %copy-start.5 = (s32[8]{0:T(128)S(1)}, s32[8]{0:T(128)}, u32[]{:S(2)}) copy-start(s32[8]{0:T(128)} %param.31) | copy-start | bytes 100
  119.1 85.7 %all-to-all-start.1 = ((bf16[4,4,64,1152]{3,2,1,0:T(8,128)(2,1)}), bf16[4,4,64,1152]{3,2,1,0:T(8,128)(2,1)}, u32[]{:S(2)}, u32[]{:S(2)}) async-start(bf16[4,4,64,1152]{3,2,1,0:T(8,128)(2,1)} %bitcast.27), calls=%async_computation.1 | async-start | bytes 4718592 | tf_op jit(solution)/shard_map/all_to_all | solution.py:833
  125.6 79.1 %collective-permute-start.7 = (bf16[4,3,96,1152]{3,2,1,0:T(8,128)(2,1)S(1)}, bf16[4,3,96,1152]{3,2,1,0:T(8,128)(2,1)}, u32[]{:S(2)}, u32[]{:S(2)}) collective-permute-start(bf16[4,3,96,1152]{3,2,1,0:T(8,128)(2,1)S(1)} %pad_maximum_fusion.refs_0_), channel_id=1, source_target_pairs={{0,4},{4,0},{8,12},{12,8},{16,20},{20,16},{24,28},{28,24},{1,5},{5... | collective-permute-start | bytes 7962632 | tf_op jit(solution)/shard_map/ppermute | solution.py:728
  125.8 10.1 %copy-start.32 = (f32[2]{0:T(128)S(1)}, f32[2]{0:T(128)}, u32[]{:S(2)}) copy-start(f32[2]{0:T(128)} %constant.222) | copy-start | bytes 28
  128.9 75.9 %collective-permute-start.5 = (bf16[4,3,48,1152]{3,2,1,0:T(8,128)(2,1)}, bf16[4,3,48,1152]{3,2,1,0:T(8,128)(2,1)}, u32[]{:S(2)}, u32[]{:S(2)}) collective-permute-start(bf16[4,3,48,1152]{3,2,1,0:T(8,128)(2,1)} %get-tuple-element.277), channel_id=1, source_target_pairs={{0,8},{4,12},{8,0},{12,4},{16,24},{20,28},{24,16},{28,20},{1,9},{5... | collective-permute-start | bytes 3981320 | tf_op jit(solution)/shard_map/ppermute | solution.py:728
  128.9 48.0 %collective-permute-start.9 = (bf16[4,3,48,1152]{3,2,1,0:T(8,128)(2,1)}, bf16[4,3,48,1152]{3,2,1,0:T(8,128)(2,1)}, u32[]{:S(2)}, u32[]{:S(2)}) collective-permute-start(bf16[4,3,48,1152]{3,2,1,0:T(8,128)(2,1)} %get-tuple-element.277), channel_id=1, source_target_pairs={{0,16},{4,20},{8,24},{12,28},{16,0},{20,4},{24,8},{28,12},{1,17},{... | collective-permute-start | bytes 3981320 | tf_op jit(solution)/shard_map/ppermute | solution.py:728
  129.2 75.6 %collective-permute-start.6 = (bf16[4,3,48,1152]{3,2,1,0:T(8,128)(2,1)}, bf16[4,3,48,1152]{3,2,1,0:T(8,128)(2,1)}, u32[]{:S(2)}, u32[]{:S(2)}) collective-permute-start(bf16[4,3,48,1152]{3,2,1,0:T(8,128)(2,1)} %get-tuple-element.276), channel_id=1, source_target_pairs={{0,16},{4,20},{8,24},{12,28},{16,0},{20,4},{24,8},{28,12},{1,17},{... | collective-permute-start | bytes 3981320 | tf_op jit(solution)/shard_map/ppermute | solution.py:728
  130.9 73.8 %collective-permute-start.15 = (bf16[4,3,48,1152]{3,2,1,0:T(8,128)(2,1)}, bf16[4,3,48,1152]{3,2,1,0:T(8,128)(2,1)}, u32[]{:S(2)}, u32[]{:S(2)}) collective-permute-start(bf16[4,3,48,1152]{3,2,1,0:T(8,128)(2,1)} %get-tuple-element.276), channel_id=1, source_target_pairs={{0,8},{4,12},{8,0},{12,4},{16,24},{20,28},{24,16},{28,20},{1,9},{5... | collective-permute-start | bytes 3981320 | tf_op jit(solution)/shard_map/ppermute | solution.py:728
  176.8 71.7 %collective-permute-start.10 = (bf16[4,3,48,1152]{3,2,1,0:T(8,128)(2,1)}, bf16[4,3,48,1152]{3,2,1,0:T(8,128)(2,1)}, u32[]{:S(2)}, u32[]{:S(2)}) collective-permute-start(bf16[4,3,48,1152]{3,2,1,0:T(8,128)(2,1)} %collective-permute-done.9.refs_4_), channel_id=1, source_target_pairs={{0,4},{4,0},{8,12},{12,8},{16,20},{20,16},{24,28},{28,24},{1,5},{5... | collective-permute-start | bytes 3981320 | tf_op jit(solution)/shard_map/ppermute | solution.py:728
  204.7 45.6 %collective-permute-start.16 = (bf16[4,3,48,1152]{3,2,1,0:T(8,128)(2,1)}, bf16[4,3,48,1152]{3,2,1,0:T(8,128)(2,1)}, u32[]{:S(2)}, u32[]{:S(2)}) collective-permute-start(bf16[4,3,48,1152]{3,2,1,0:T(8,128)(2,1)} %collective-permute-done.15.refs_10_), channel_id=1, source_target_pairs={{0,4},{4,0},{8,12},{12,8},{16,20},{20,16},{24,28},{28,24},{1,5},{5... | collective-permute-start | bytes 3981320 | tf_op jit(solution)/shard_map/ppermute | solution.py:728
  204.8 43.2 %collective-permute-start.12 = (bf16[4,3,48,1152]{3,2,1,0:T(8,128)(2,1)}, bf16[4,3,48,1152]{3,2,1,0:T(8,128)(2,1)}, u32[]{:S(2)}, u32[]{:S(2)}) collective-permute-start(bf16[4,3,48,1152]{3,2,1,0:T(8,128)(2,1)} %collective-permute-done.6.refs_8_), channel_id=1, source_target_pairs={{0,8},{4,12},{8,0},{12,4},{16,24},{20,28},{24,16},{28,20},{1,9},{5... | collective-permute-start | bytes 3981320 | tf_op jit(solution)/shard_map/ppermute | solution.py:728
  206.2 44.1 %collective-permute-start.14 = (bf16[4,3,48,1152]{3,2,1,0:T(8,128)(2,1)}, bf16[4,3,48,1152]{3,2,1,0:T(8,128)(2,1)}, u32[]{:S(2)}, u32[]{:S(2)}) collective-permute-start(bf16[4,3,48,1152]{3,2,1,0:T(8,128)(2,1)} %collective-permute-done.6.refs_8_), channel_id=1, source_target_pairs={{0,4},{4,0},{8,12},{12,8},{16,20},{20,16},{24,28},{28,24},{1,5},{5... | collective-permute-start | bytes 3981320 | tf_op jit(solution)/shard_map/ppermute | solution.py:728
  206.2 41.7 %collective-permute-start.11 = (bf16[4,3,48,1152]{3,2,1,0:T(8,128)(2,1)}, bf16[4,3,48,1152]{3,2,1,0:T(8,128)(2,1)}, u32[]{:S(2)}, u32[]{:S(2)}) collective-permute-start(bf16[4,3,48,1152]{3,2,1,0:T(8,128)(2,1)} %collective-permute-done.5.refs_2_), channel_id=1, source_target_pairs={{0,16},{4,20},{8,24},{12,28},{16,0},{20,4},{24,8},{28,12},{1,17},{... | collective-permute-start | bytes 3981320 | tf_op jit(solution)/shard_map/ppermute | solution.py:728
  207.1 86.0 %all-to-all-start.2 = ((bf16[4,4,64,1152]{3,2,1,0:T(8,128)(2,1)}), bf16[4,4,64,1152]{3,2,1,0:T(8,128)(2,1)}, u32[]{:S(2)}, u32[]{:S(2)}) async-start(bf16[4,4,64,1152]{3,2,1,0:T(8,128)(2,1)} %bitcast.156), calls=%async_computation.2 | async-start | bytes 4718592 | tf_op jit(solution)/shard_map/all_to_all | solution.py:833
  211.9 37.3 %copy-start.53 = (s32[8]{0:T(128)S(1)}, s32[8]{0:T(128)}, u32[]{:S(2)}) copy-start(s32[8]{0:T(128)} %constant.212.clone) | copy-start | bytes 100
  211.9 37.9 %copy-start.52 = (s32[8]{0:T(128)S(1)}, s32[8]{0:T(128)}, u32[]{:S(2)}) copy-start(s32[8]{0:T(128)} %constant.213.clone) | copy-start | bytes 100
  247.9 4.3 collective-permute-start.8
  248.0 5.3 collective-permute-start.13
  248.5 6.7 %collective-permute-start.17 = (bf16[4,3,48,1152]{3,2,1,0:T(8,128)(2,1)}, bf16[4,3,48,1152]{3,2,1,0:T(8,128)(2,1)}, u32[]{:S(2)}, u32[]{:S(2)}) collective-permute-start(bf16[4,3,48,1152]{3,2,1,0:T(8,128)(2,1)} %collective-permute-done.12.refs_12_), channel_id=1, source_target_pairs={{0,4},{4,0},{8,12},{12,8},{16,20},{20,16},{24,28},{28,24},{1,5},{5... | collective-permute-start | bytes 3981320 | tf_op jit(solution)/shard_map/ppermute | solution.py:728
  337.0 41.8 %collective-permute-start.19 = (bf16[2,3,576,768]{3,2,1,0:T(8,128)(2,1)}, bf16[2,3,576,768]{3,2,1,0:T(8,128)(2,1)}, u32[]{:S(2)}, u32[]{:S(2)}) collective-permute-start(bf16[2,3,576,768]{3,2,1,0:T(8,128)(2,1)} %get-tuple-element.159), channel_id=1, source_target_pairs={{0,4},{4,0},{8,12},{12,8},{16,20},{20,16},{24,28},{28,24},{1,5},{5... | collective-permute-start | bytes 15925256 | tf_op jit(solution)/shard_map/ppermute | solution.py:728
  373.1 13.3 %collective-permute-start.18 = (bf16[2,3,576,768]{3,2,1,0:T(8,128)(2,1)}, bf16[2,3,576,768]{3,2,1,0:T(8,128)(2,1)}, u32[]{:S(2)}, u32[]{:S(2)}) collective-permute-start(bf16[2,3,576,768]{3,2,1,0:T(8,128)(2,1)} %get-tuple-element.156), channel_id=1, source_target_pairs={{0,4},{4,0},{8,12},{12,8},{16,20},{20,16},{24,28},{28,24},{1,5},{5... | collective-permute-start | bytes 15925256 | tf_op jit(solution)/shard_map/ppermute | solution.py:728
  373.5 84.4 %all-to-all-start.3 = ((bf16[4,4,64,1152]{3,2,1,0:T(8,128)(2,1)}), bf16[4,4,64,1152]{3,2,1,0:T(8,128)(2,1)}, u32[]{:S(2)}, u32[]{:S(2)}) async-start(bf16[4,4,64,1152]{3,2,1,0:T(8,128)(2,1)} %get-tuple-element.183), calls=%async_computation.3 | async-start | bytes 4718592 | tf_op jit(solution)/shard_map/all_to_all | solution.py:833
  394.1 63.8 %collective-permute-start.21 = (bf16[2,3,288,768]{3,2,1,0:T(8,128)(2,1)}, bf16[2,3,288,768]{3,2,1,0:T(8,128)(2,1)}, u32[]{:S(2)}, u32[]{:S(2)}) collective-permute-start(bf16[2,3,288,768]{3,2,1,0:T(8,128)(2,1)} %bitcast.165), channel_id=1, source_target_pairs={{0,8},{4,12},{8,0},{12,4},{16,24},{20,28},{24,16},{28,20},{1,9},{5... | collective-permute-start | bytes 7962632 | tf_op jit(solution)/shard_map/ppermute | solution.py:728
  395.5 62.4 %collective-permute-start.20 = (bf16[2,3,288,768]{3,2,1,0:T(8,128)(2,1)}, bf16[2,3,288,768]{3,2,1,0:T(8,128)(2,1)}, u32[]{:S(2)}, u32[]{:S(2)}) collective-permute-start(bf16[2,3,288,768]{3,2,1,0:T(8,128)(2,1)} %bitcast.166), channel_id=1, source_target_pairs={{0,16},{4,20},{8,24},{12,28},{16,0},{20,4},{24,8},{28,12},{1,17},{... | collective-permute-start | bytes 7962632 | tf_op jit(solution)/shard_map/ppermute | solution.py:728
  407.2 45.9 %copy-start.33 = (f32[2]{0:T(128)S(1)}, f32[2]{0:T(128)}, u32[]{:S(2)}) copy-start(f32[2]{0:T(128)} %constant.222) | copy-start | bytes 28
  407.2 46.1 %copy-start.21 = (f32[4,8,1152]{2,1,0:T(8,128)S(1)}, f32[4,8,1152]{2,1,0:T(8,128)}, u32[]{:S(2)}) copy-start(f32[4,8,1152]{2,1,0:T(8,128)} %get-tuple-element.174) | copy-start | bytes 442372
  407.2 46.1 %copy-start.22 = (f32[4,8,1152]{2,1,0:T(8,128)S(1)}, f32[4,8,1152]{2,1,0:T(8,128)}, u32[]{:S(2)}) copy-start(f32[4,8,1152]{2,1,0:T(8,128)} %get-tuple-element.175) | copy-start | bytes 442372
  454.9 13.3 %collective-permute-start.22 = (bf16[1,4,8,1152]{3,2,1,0:T(8,128)(2,1)}, bf16[1,4,8,1152]{3,2,1,0:T(8,128)(2,1)}, u32[]{:S(2)}, u32[]{:S(2)}) collective-permute-start(bf16[1,4,8,1152]{3,2,1,0:T(8,128)(2,1)} %fusion.32.one_ref), channel_id=1, source_target_pairs={{0,2},{1,3},{2,0},{3,1},{4,6},{5,7},{6,4},{7,5},{8,10},{9,11},{10,... | collective-permute-start | bytes 221192 | tf_op jit(solution)/shard_map/ppermute | solution.py:728
  457.9 57.8 %all-to-all-start.4 = ((bf16[4,4,64,1152]{3,2,1,0:T(8,128)(2,1)}), bf16[4,4,64,1152]{3,2,1,0:T(8,128)(2,1)}, u32[]{:S(2)}, u32[]{:S(2)}) async-start(bf16[4,4,64,1152]{3,2,1,0:T(8,128)(2,1)} %get-tuple-element.192), calls=%async_computation.4 | async-start | bytes 4718592 | tf_op jit(solution)/shard_map/all_to_all | solution.py:833
  468.2 12.4 %copy-start.45 = (s32[32]{0:T(128)S(1)}, s32[32]{0:T(128)}, u32[]{:S(2)}) copy-start(s32[32]{0:T(128)} %get-tuple-element.204) | copy-start | bytes 388
  473.9 41.8 %collective-permute-start.24 = (bf16[2,3,144,768]{3,2,1,0:T(8,128)(2,1)}, bf16[2,3,144,768]{3,2,1,0:T(8,128)(2,1)S(1)}, u32[]{:S(2)}, u32[]{:S(2)}) collective-permute-start(bf16[2,3,144,768]{3,2,1,0:T(8,128)(2,1)} %bitcast.170), channel_id=1, source_target_pairs={{0,16},{4,20},{8,24},{12,28},{16,0},{20,4},{24,8},{28,12},{1,17},{... | collective-permute-start | bytes 3981320 | tf_op jit(solution)/shard_map/ppermute | solution.py:728
  475.3 40.3 %collective-permute-start.23 = (bf16[2,3,144,768]{3,2,1,0:T(8,128)(2,1)}, bf16[2,3,144,768]{3,2,1,0:T(8,128)(2,1)S(1)}, u32[]{:S(2)}, u32[]{:S(2)}) collective-permute-start(bf16[2,3,144,768]{3,2,1,0:T(8,128)(2,1)} %bitcast.169), channel_id=1, source_target_pairs={{0,8},{4,12},{8,0},{12,4},{16,24},{20,28},{24,16},{28,20},{1,9},{5... | collective-permute-start | bytes 3981320 | tf_op jit(solution)/shard_map/ppermute | solution.py:728
  478.6 24.5 %collective-permute-start.25 = (bf16[2,4,8,1152]{3,2,1,0:T(8,128)(2,1)}, bf16[2,4,8,1152]{3,2,1,0:T(8,128)(2,1)S(1)}, u32[]{:S(2)}, u32[]{:S(2)}) collective-permute-start(bf16[2,4,8,1152]{3,2,1,0:T(8,128)(2,1)} %append.11.one_ref), channel_id=1, source_target_pairs={{0,1},{1,0},{2,3},{3,2},{4,5},{5,4},{6,7},{7,6},{8,9},{9,8},{10,11... | collective-permute-start | bytes 442376 | tf_op jit(solution)/shard_map/ppermute | solution.py:728
  502.6 16.3 %collective-permute-start.26 = (bf16[4,576,1152]{2,1,0:T(8,128)(2,1)}, bf16[4,576,1152]{2,1,0:T(8,128)(2,1)}, u32[]{:S(2)}, u32[]{:S(2)}) collective-permute-start(bf16[4,576,1152]{2,1,0:T(8,128)(2,1)} %get-tuple-element.198), channel_id=1, source_target_pairs={{0,4},{4,0},{8,12},{12,8},{16,20},{20,16},{24,28},{28,24},{1,5},{5... | collective-permute-start | bytes 15925256 | tf_op jit(solution)/shard_map/ppermute | solution.py:728
  503.1 12.5 %copy-start.47 = (bf16[2,4,8,1152]{3,2,1,0:T(8,128)(2,1)}, bf16[2,4,8,1152]{3,2,1,0:T(8,128)(2,1)S(1)}, u32[]{:S(2)}) copy-start(bf16[2,4,8,1152]{3,2,1,0:T(8,128)(2,1)S(1)} %collective-permute-done.25.other_ref) | copy-start | bytes 442372
  517.7 19.7 %collective-permute-start.28 = (bf16[4,4,8,1152]{3,2,1,0:T(8,128)(2,1)}, bf16[4,4,8,1152]{3,2,1,0:T(8,128)(2,1)}, u32[]{:S(2)}, u32[]{:S(2)}) collective-permute-start(bf16[4,4,8,1152]{3,2,1,0:T(8,128)(2,1)} %append.12.one_ref), channel_id=1, source_target_pairs={{0,8},{4,12},{8,0},{12,4},{16,24},{20,28},{24,16},{28,20},{1,9},{5... | collective-permute-start | bytes 884744 | tf_op jit(solution)/shard_map/ppermute | solution.py:728
  526.7 30.1 %collective-permute-start.29 = (bf16[2,288,1152]{2,1,0:T(8,128)(2,1)}, bf16[2,288,1152]{2,1,0:T(8,128)(2,1)}, u32[]{:S(2)}, u32[]{:S(2)}) collective-permute-start(bf16[2,288,1152]{2,1,0:T(8,128)(2,1)} %get-tuple-element.213), channel_id=1, source_target_pairs={{0,8},{4,12},{8,0},{12,4},{16,24},{20,28},{24,16},{28,20},{1,9},{5... | collective-permute-start | bytes 3981320 | tf_op jit(solution)/shard_map/ppermute | solution.py:728
  527.5 32.4 %collective-permute-start.27 = (bf16[2,288,1152]{2,1,0:T(8,128)(2,1)}, bf16[2,288,1152]{2,1,0:T(8,128)(2,1)}, u32[]{:S(2)}, u32[]{:S(2)}) collective-permute-start(bf16[2,288,1152]{2,1,0:T(8,128)(2,1)} %get-tuple-element.209), channel_id=1, source_target_pairs={{0,16},{4,20},{8,24},{12,28},{16,0},{20,4},{24,8},{28,12},{1,17},{... | collective-permute-start | bytes 3981320 | tf_op jit(solution)/shard_map/ppermute | solution.py:728
  539.5 30.4 %collective-permute-start.30 = (bf16[8,4,8,1152]{3,2,1,0:T(8,128)(2,1)}, bf16[8,4,8,1152]{3,2,1,0:T(8,128)(2,1)S(1)}, u32[]{:S(2)}, u32[]{:S(2)}) collective-permute-start(bf16[8,4,8,1152]{3,2,1,0:T(8,128)(2,1)} %append.13.one_ref), channel_id=1, source_target_pairs={{0,16},{4,20},{8,24},{12,28},{16,0},{20,4},{24,8},{28,12},{1,17},{... | collective-permute-start | bytes 1769480 | tf_op jit(solution)/shard_map/ppermute | solution.py:728
  542.7 40.3 %collective-permute-start.36 = (bf16[2,3,144,768]{3,2,1,0:T(8,128)(2,1)}, bf16[2,3,144,768]{3,2,1,0:T(8,128)(2,1)}, u32[]{:S(2)}, u32[]{:S(2)}) collective-permute-start(bf16[2,3,144,768]{3,2,1,0:T(8,128)(2,1)} %add_convert_fusion.1), channel_id=1, source_target_pairs={{0,1},{1,0},{2,3},{3,2},{4,5},{5,4},{6,7},{7,6},{8,9},{9,8},{10,11... | collective-permute-start | bytes 3981320 | tf_op jit(solution)/shard_map/ppermute | solution.py:728
  559.5 13.5 %copy-start.35 = (s32[72]{0:T(128)S(1)}, s32[72]{0:T(128)}, u32[]{:S(2)}) copy-start(s32[72]{0:T(128)} %constant.223) | copy-start | bytes 868
  559.5 13.6 %copy-start.44 = (s32[32]{0:T(128)S(1)}, s32[32]{0:T(128)}, u32[]{:S(2)}) copy-start(s32[32]{0:T(128)} %get-tuple-element.218) | copy-start | bytes 388
  562.5 17.2 %collective-permute-start.33 = (bf16[2,144,1152]{2,1,0:T(8,128)(2,1)}, bf16[2,144,1152]{2,1,0:T(8,128)(2,1)}, u32[]{:S(2)}, u32[]{:S(2)}) collective-permute-start(bf16[2,144,1152]{2,1,0:T(8,128)(2,1)} %get-tuple-element.228), channel_id=1, source_target_pairs={{0,8},{4,12},{8,0},{12,4},{16,24},{20,28},{24,16},{28,20},{1,9},{5... | collective-permute-start | bytes 1990664 | tf_op jit(solution)/shard_map/ppermute | solution.py:728
  573.0 8.9 %collective-permute-start.31 = (bf16[16,4,8,1152]{3,2,1,0:T(8,128)(2,1)}, bf16[16,4,8,1152]{3,2,1,0:T(8,128)(2,1)S(1)}, u32[]{:S(2)}, u32[]{:S(2)}) collective-permute-start(bf16[16,4,8,1152]{3,2,1,0:T(8,128)(2,1)} %append.14.one_ref), channel_id=1, source_target_pairs={{0,4},{4,0},{8,12},{12,8},{16,20},{20,16},{24,28},{28,24},{1,5},{5... | collective-permute-start | bytes 3538952 | tf_op jit(solution)/shard_map/ppermute | solution.py:728
  573.2 26.9 %collective-permute-start.32 = (bf16[2,144,1152]{2,1,0:T(8,128)(2,1)}, bf16[2,144,1152]{2,1,0:T(8,128)(2,1)S(1)}, u32[]{:S(2)}, u32[]{:S(2)}) collective-permute-start(bf16[2,144,1152]{2,1,0:T(8,128)(2,1)} %get-tuple-element.226), channel_id=1, source_target_pairs={{0,16},{4,20},{8,24},{12,28},{16,0},{20,4},{24,8},{28,12},{1,17},{... | collective-permute-start | bytes 1990664 | tf_op jit(solution)/shard_map/ppermute | solution.py:728
  574.7 66.7 %all-to-all-start.5 = ((bf16[32,64,1152]{2,1,0:T(8,128)(2,1)}), bf16[32,64,1152]{2,1,0:T(8,128)(2,1)}, u32[]{:S(2)}, u32[]{:S(2)}) async-start(bf16[32,64,1152]{2,1,0:T(8,128)(2,1)} %gather_fusion.8), calls=%async_computation.5 | async-start | bytes 9437184 | tf_op jit(solution)/shard_map/all_to_all | solution.py:1076
  581.9 26.3 %collective-permute-start.34 = (bf16[2,144,1152]{2,1,0:T(8,128)(2,1)}, bf16[2,144,1152]{2,1,0:T(8,128)(2,1)}, u32[]{:S(2)}, u32[]{:S(2)}) collective-permute-start(bf16[2,144,1152]{2,1,0:T(8,128)(2,1)} %add_convert_fusion.5), channel_id=1, source_target_pairs={{0,1},{1,0},{2,3},{3,2},{4,5},{5,4},{6,7},{7,6},{8,9},{9,8},{10,11... | collective-permute-start | bytes 1990664 | tf_op jit(solution)/shard_map/ppermute | solution.py:728
  585.5 50.5 %collective-permute-start.37 = (bf16[1,3,144,768]{3,2,1,0:T(8,128)(2,1)}, bf16[1,3,144,768]{3,2,1,0:T(8,128)(2,1)}, u32[]{:S(2)}, u32[]{:S(2)}) collective-permute-start(bf16[1,3,144,768]{3,2,1,0:T(8,128)(2,1)} %slice.145), channel_id=1, source_target_pairs={{0,2},{1,3},{2,0},{3,1},{4,6},{5,7},{6,4},{7,5},{8,10},{9,11},{10,... | collective-permute-start | bytes 1990664 | tf_op jit(solution)/shard_map/ppermute | solution.py:728
  596.4 11.9 %copy-start.19 = (bf16[2,144,1152]{2,1,0:T(8,128)(2,1)S(1)}, bf16[2,144,1152]{2,1,0:T(8,128)(2,1)}, u32[]{:S(2)}) copy-start(bf16[2,144,1152]{2,1,0:T(8,128)(2,1)} %get-tuple-element.225) | copy-start | bytes 1990660
  599.3 11.3 %copy-start.39 = (s32[128]{0:T(128)S(1)}, s32[128]{0:T(128)}, u32[]{:S(2)}) copy-start(s32[128]{0:T(128)} %copy-done.38) | copy-start | bytes 1540
  608.3 24.2 %copy-start.11 = (f32[864,864]{1,0:T(8,128)S(1)}, f32[864,864]{1,0:T(8,128)}, u32[]{:S(2)}) copy-start(f32[864,864]{1,0:T(8,128)} %constant.216.clone) | copy-start | bytes 8957956
  609.8 22.6 %collective-permute-start.35 = (bf16[1,144,1152]{2,1,0:T(8,128)(2,1)S(1)}, bf16[1,144,1152]{2,1,0:T(8,128)(2,1)S(1)}, u32[]{:S(2)}, u32[]{:S(2)}) collective-permute-start(bf16[1,144,1152]{2,1,0:T(8,128)(2,1)S(1)} %slice.140), channel_id=1, source_target_pairs={{0,2},{1,3},{2,0},{3,1},{4,6},{5,7},{6,4},{7,5},{8,10},{9,11},{10,... | collective-permute-start | bytes 995336 | tf_op jit(solution)/shard_map/ppermute | solution.py:728
  (41 other events, 179.3 us)
Sparse Core Ops, SparseCore 0:
  52.9 141.9 all-gather.2

commit v12 on v11

--- a/solution.py
+++ b/solution.py
@@ -642,8 +642,52 @@
     return whole.reshape((mp_size, -1) + piece.shape)
 
 
-def take_rows(values, index):
+def pick_rows(values, index):
     return values.at[index].get(mode="promise_in_bounds")
+
+
+def take_rows_kernel(index_ref, *refs):
+    out_ref = refs[-1]
+    count = len(refs) - 1
+    base = pl.program_id(0) * count
+    for place, ref in enumerate(refs[:-1]):
+        live = index_ref[base + place] >= 0
+
+        @pl.when(live)
+        def _():
+            out_ref[place] = ref[0]
+
+        @pl.when(jnp.logical_not(live))
+        def _():
+            out_ref[place] = jnp.zeros_like(ref[0])
+
+
+def take_rows(values, index, microseconds=0):
+    number = index.shape[0]
+    count = math.gcd(number, 4)
+    block = values.shape[1:]
+    specs = [
+        pl.BlockSpec(
+            (1,) + block,
+            functools.partial(
+                lambda place, i, index: (jnp.maximum(index[i * count + place], 0), 0, 0), place
+            ),
+        )
+        for place in range(count)
+    ]
+    return pl.pallas_call(
+        take_rows_kernel,
+        grid_spec=pltpu.PrefetchScalarGridSpec(
+            num_scalar_prefetch=1,
+            grid=(number // count,),
+            in_specs=specs,
+            out_specs=pl.BlockSpec((count,) + block, lambda i, index: (i, 0, 0)),
+        ),
+        out_shape=jax.ShapeDtypeStruct((number,) + block, values.dtype),
+        compiler_params=pltpu.CompilerParams(vmem_limit_bytes=60 << 20),
+        cost_estimate=lasting(microseconds),
+        name="take_rows",
+    )(index.astype(jnp.int32), *([values] * count))
 
 
 def sum_quarters_kernel(kept_ref, got_ref, *out_refs):
@@ -697,15 +741,8 @@
     )(*arrays)
 
 
-def append_zero_kernel(value_ref, out_ref):
-    count = value_ref.shape[0]
-    out_ref[:count] = value_ref[...]
-    out_ref[count:] = jnp.zeros_like(out_ref[count:])
-
-
-def append_zero(values, microseconds):
-    shape = (values.shape[0] + 1,) + values.shape[1:]
-    return whole_arrays(append_zero_kernel, "append_zero", microseconds, shape, values)
+def copy_kernel(value_ref, out_ref):
+    out_ref[...] = value_ref[...]
 
 
 def append_kernel(one_ref, other_ref, out_ref):
@@ -773,10 +810,10 @@
 
 def split(values, dim):
     size = values.shape[dim] // 2
-    return (
+    return [
         lax.slice_in_dim(values, 0, size, axis=dim),
         lax.slice_in_dim(values, size, 2 * size, axis=dim),
-    )
+    ]
 
 
 def halve(values, axis, bits, dim):
@@ -845,7 +882,14 @@
     pair_slot = pair_ids % slot_count
     send_index = pair_slot * dp_size + jnp.mod(inverse[pair_peer] - my_start, dp_size)
     send_index = jnp.minimum(send_index, capacity - 1)
-    send_patches = take_rows(patches, send_index)
+    send_patches = pick_rows(patches, send_index)
+    qkv_weight, out_weight, expand_weight, down_weight, send_patches = tie(
+        qkv_weight, out_weight, expand_weight, down_weight, send_patches
+    )
+    recv_patches = lax.all_to_all(send_patches, "dp", split_axis=0, concat_axis=0, tiled=True)
+    info = jnp.stack([time_bins, labels])[None]
+    got_info = swap(info, "dp", dp_bits[0][0])
+
     share = 4 * local_dim // dp_size
     spots = lax.dynamic_slice_in_dim(jnp.array(places), dp_index * share, share, 0)
     take_qkv = (spots[:, None] == jnp.arange(3 * local_dim)[None, :]).astype(bf16)
@@ -863,14 +907,6 @@
             lax.dynamic_slice_in_dim(down_weight, dp_index * share, share, 0),
         ]
     )
-    info = jnp.stack([time_bins, labels])[None]
-    info_places = [0]
-    for bit in bits_of(dp_size):
-        got_info = swap(info, "dp", bit)
-        if bit * 2 == dp_size:
-            send_patches, got_info, attend_piece = tie(send_patches, got_info, attend_piece)
-        info = append(info, got_info, 200)
-        info_places = info_places + [place ^ bit for place in info_places]
     attend_full = gather_pieces(attend_piece, mp_size).reshape(mp_size, 4 * local_dim, -1)
     by_permutes = share % 32 == 0 and dp_size == 8 and mp_size == 4
     if by_permutes:
@@ -882,7 +918,30 @@
         mlp_pieces = [mlp_full[mp_index ^ jnp.array(halving_order(mp_bits))]]
         mlp_order = jnp.zeros((1,), jnp.int32)
 
-    recv_patches = lax.all_to_all(send_patches, "dp", split_axis=0, concat_axis=0, tiled=True)
+    rank_ids = jnp.arange(images) * dp_size + my_place
+    source = jnp.sum((finish[None, :] <= rank_ids[:, None]).astype(jnp.int32), axis=1)
+    within = rank_ids - starts[source]
+    recv_index = source * slot_count + within // dp_size
+
+    info_places = [0]
+    for step, bit in enumerate(dp_bits[0]):
+        info = append(info, got_info, 200 if step < 2 else 0)
+        info_places = info_places + [place ^ bit for place in info_places]
+        if by_permutes and step == 0:
+            mlp_near = jnp.concatenate([mlp_near, far_near], axis=0)
+            far_near = swap(mlp_near, "mp", 1)
+            info, mlp_near = tie(info, mlp_near)
+        if by_permutes and step == 1:
+            latent = pick_rows(recv_patches, recv_index)
+            far_near, info, _ = tie(far_near, info, latent)
+            mlp_near = append(mlp_near, far_near, 200)
+            halves = split(mlp_near, 2)
+        if step + 1 < len(dp_bits[0]):
+            got_info = swap(info, "dp", dp_bits[0][step + 1])
+    if not by_permutes:
+        latent = pick_rows(recv_patches, recv_index)
+    latent = turn(latent.reshape(mp_size, own, local_len, model_width))
+
     info = info.swapaxes(0, 1).reshape(2, -1)
     info_owner = jnp.repeat(dp_index ^ jnp.array(info_places), capacity)
     info_slot = jnp.tile(jnp.arange(capacity), dp_size)
@@ -926,10 +985,6 @@
     silu_cond = silu_all[:own]
     weights = weights_all[:own]
 
-    if by_permutes:
-        silu_cond, far_near = tie(silu_cond, far_near)
-        mlp_near = jnp.concatenate([mlp_near, far_near], axis=0)
-        far_near = swap(mlp_near, "mp", 1)
     ada_kinds = ada_weight.swapaxes(0, 1)
     modulation = modulate(jnp.pad(silu_cond, ((0, -own % 16), (0, 0))), ada_kinds)[:, :own]
     mods = jnp.concatenate(
@@ -944,23 +999,13 @@
     back_within = pair_slot * dp_size + jnp.mod(my_place - starts[pair_peer], dp_size)
     back_valid = back_within < image_counts[pair_peer]
     back_slot = jnp.clip((starts[pair_peer] + back_within - my_place) // dp_size, 0, images - 1)
-    back_slot = jnp.where(back_valid, back_slot, images)
+    back_slot = jnp.where(back_valid, back_slot, -1)
     slot_ids = jnp.arange(capacity)
     home_peer = dest_perm[jnp.mod(my_start + slot_ids, dp_size)]
     home_index = home_peer * slot_count + jnp.minimum(slot_ids // dp_size, slot_count - 1)
-    recv_patches, mods, back_slot, home_index = tie(recv_patches, mods, back_slot, home_index)
-
-    rank_ids = jnp.arange(images) * dp_size + my_place
-    source = jnp.sum((finish[None, :] <= rank_ids[:, None]).astype(jnp.int32), axis=1)
-    within = rank_ids - starts[source]
-    recv_index = source * slot_count + within // dp_size
-    latent = take_rows(recv_patches, recv_index).reshape(mp_size, own, local_len, model_width)
+    mods, back_slot, home_index = tie(mods, back_slot, home_index)
+
     if by_permutes:
-        far_near, _ = tie(far_near, latent)
-    latent = turn(latent)
-    if by_permutes:
-        mlp_near = jnp.concatenate([mlp_near, far_near], axis=0)
-        halves = split(mlp_near, 2)
         orders = ((2, 4), (4, 2))
         parts = [{bit: swap(halves[half], "dp", bit) for bit in orders[half]} for half in range(2)]
         cored = swap(mlp_near, "dp", 1)
@@ -1064,17 +1109,21 @@
     mlp_got = swap(mlp_one, "mp", mp_bits[0])
 
     latent_back, attend_zero, attend_one = tie(latent_back, attend_zero, attend_one)
-    latent_back = append_zero(latent_back.reshape(images, local_len, model_width), 200)
-    back_patches = take_rows(latent_back, back_slot)
+    latent_back = latent_back.reshape(images, local_len, model_width)
+    back_patches = take_rows(latent_back, back_slot, 200)
     attend_got_one = swap(sent_one, "dp", dp_bits[1][1])
     attend_got_zero = swap(sent_zero, "dp", dp_bits[0][1])
-    back_patches, attend_zero, attend_one = tie(back_patches, attend_zero, attend_one)
+    back_patches, attend_zero, attend_one, result = tie(
+        back_patches, attend_zero, attend_one, result
+    )
+    result = whole_arrays(copy_kernel, "copy_result", 0, result.shape, result)
+    attend_zero, attend_one, result = tie(attend_zero, attend_one, result)
     attend_zero = more(attend_zero)
     attend_one, sent_one = sum_halves(attend_one, attend_got_one)
     attend_zero, sent_zero = sum_halves(attend_zero, attend_got_zero)
     back_patches, sent_one, sent_zero, mlp_zero = tie(back_patches, sent_one, sent_zero, mlp_zero)
     got_patches = lax.all_to_all(back_patches, "dp", split_axis=0, concat_axis=0, tiled=True)
-    patch_grad = take_rows(got_patches, home_index)
+    patch_grad = pick_rows(got_patches, home_index)
     attend_got_one = swap(sent_one, "dp", dp_bits[1][2])
     attend_got_zero = swap(sent_zero, "dp", dp_bits[0][2])
     while stage < len(gather_bits):

time: 667 us -> 654 us (0.981)
  waiting for transfers between devices: 178 us -> 160 us
  local copies, waits for them, and re-layouts: 54.1 us -> 42 us
  Pallas kernels: 298 us -> 309 us
    all_to_all x1, waiting for transfers between devices: 39.9 us -> 0.01 us  [shards(): lax.all_to_all(send_patches, 'dp', split_axis=0, concat_axis=0, tiled=True)]
    ppermute x38, waiting for transfers between devices: 123 us -> 142 us  [swap(): return lax.ppermute(values, axis, [(i, i ^ bit) for i in range(size)])]
    unnamed x126 -> x120, local copies, waits for them, and re-layouts: 16.8 us -> 8.21 us
    pallas_call x0 -> x1, Pallas kernels: none -> 7.78 us  [take_rows(): pl.pallas_call(take_rows_kernel, grid_spec=pltpu.PrefetchScalarGridSpec(n...]
    gather x4 -> x3, local copies, waits for them, and re-layouts: 21.2 us -> 16 us  [pick_rows(): return values.at[index].get(mode='promise_in_bounds')]
    pallas_call x9 -> x10, Pallas kernels: 18.6 us -> 21.9 us  [whole_arrays(): pl.pallas_call(kernel, in_specs=specs, out_specs=pl.BlockSpec(shape, lamb...]
  transfers between devices with their start and end apart: 45 -> 45, of which waited for: 15 -> 18; matrix products, arithmetic and copies ran while one was open for 14% -> 11% of each run, Pallas kernels for 39% -> 41%
where the time goes in v12:
time: 654 us; the launch traced here: 645 us
  Pallas kernels  309 us (47%)
  waiting for transfers between devices  160 us (24%)
  starting transfers between devices  66.8 us (10%)
  local copies, waits for them, and re-layouts  42 us (6%)
  other arithmetic  37.2 us (6%)
  between operations  15.4 us (2%)
  matrix products  14.5 us (2%)
    ppermute x38, waiting for transfers between devices, swap(): return lax.ppermute(values, axis, [(i, i ^ bit) for i in range(size)])  142 us
    pallas_call x2, Pallas kernels, mlp_back(): pl.pallas_call(mlp_back_kernel, grid_spec=pltpu.PrefetchScalarGridSpec(nu...  72.2 us
    pallas_call x1, Pallas kernels, attend_back(): pl.pallas_call(attend_back_kernel, grid=(groups,), in_specs=[whole_spec(l...  45 us
    pallas_call x1, Pallas kernels, mlp(): pl.pallas_call(functools.partial(mlp_kernel, len(pieces)), grid_spec=pltp...  37.8 us
    ppermute x38, starting transfers between devices, swap(): return lax.ppermute(values, axis, [(i, i ^ bit) for i in range(size)])  37.4 us
    pallas_call x1, Pallas kernels, attend(): pl.pallas_call(attend_kernel, grid=(groups,), in_specs=[whole_spec(latent...  36.1 us
    pallas_call x6, Pallas kernels, sum_halves(): pl.pallas_call(sum_halves_kernel, grid=(kept.shape[0],), in_specs=[whole,...  31.6 us
    pallas_call x10, Pallas kernels, whole_arrays(): pl.pallas_call(kernel, in_specs=specs, out_specs=pl.BlockSpec(shape, lamb...  21.9 us
  transfers between devices with their start and end apart: 45, of which 18 were waited for; matrix products, arithmetic and copies ran while one was open for 11% of the time, Pallas kernels for 41%

profile of v12, /device:TPU:0, one launch (start us, length us, event | category | flops | bytes accessed | tf_op | source)
XLA Modules:
  0.0 645.1 jit_solution(15152605555769524467)
XLA Ops:
  11.6 5.6 gather_fusion.1
  17.2 2.4 copy.98
  22.9 4.0 collective-permute-start
  27.5 4.6 all-to-all-start
  47.3 12.1 %collective-permute-done = bf16[1,3,96,1152]{3,2,1,0:T(8,128)(2,1)} collective-permute-done((bf16[1,3,96,1152]{3,2,1,0:T(8,128)(2,1)}, bf16[1,3,96,1152]{3,2,1,0:T(8,128)(2,1)}, u32[]{:S(2)}, u32[]{:S(2)}) %collective-permute-start) | collective-permute-done | bytes 663584 | tf_op jit(solution)/shard_map/ppermute | solution.py:765
  59.4 2.5 pad_maximum_fusion.one_ref
  61.9 5.6 collective-permute-start.3
  69.9 27.8 %collective-permute-done.3.other_ref = s32[2,2,32]{2,1,0:T(2,128)S(1)} collective-permute-done((s32[2,2,32]{2,1,0:T(2,128)S(1)}, s32[2,2,32]{2,1,0:T(2,128)S(1)}, u32[]{:S(2)}, u32[]{:S(2)}) %collective-permute-start.3) | collective-permute-done | bytes 544 | tf_op jit(solution)/shard_map/ppermute | solution.py:765
  99.6 4.7 gather_fusion.3
  104.2 10.2 %collective-permute-done.1.other_ref = bf16[2,3,96,1152]{3,2,1,0:T(8,128)(2,1)} collective-permute-done((bf16[2,3,96,1152]{3,2,1,0:T(8,128)(2,1)}, bf16[2,3,96,1152]{3,2,1,0:T(8,128)(2,1)}, u32[]{:S(2)}, u32[]{:S(2)}) %collective-permute-start.1) | collective-permute-done | bytes 1327136 | tf_op jit(solution)/shard_map/ppermute | solution.py:765
  114.4 5.0 all-to-all-start.1
  119.5 3.4 append.12.refs_0_
  122.9 1.8 collective-permute-start.4
  124.7 1.9 fusion.58
  127.2 1.7 collective-permute-start.6
  128.9 1.9 collective-permute-start.15
  133.6 3.1 multiply_convert_fusion
  137.4 8.6 %modulate.1 = f32[6,16,1152]{2,1,0:T(8,128)} custom-call(bf16[16,1152]{1,0:T(8,128)(2,1)} %slice_select_fusion.silu_ref, bf16[6,1152,1152]{2,1,0:T(8,128)(2,1)} %bitcast.145), custom_call_target="tpu_custom_call" | custom-call | bytes 1024 | tf_op jit(solution)/shard_map/modulate/pallas_call | solution.py:427
  151.7 11.6 %collective-permute-done.9.refs_4_ = bf16[4,3,48,1152]{3,2,1,0:T(8,128)(2,1)} collective-permute-done((bf16[4,3,48,1152]{3,2,1,0:T(8,128)(2,1)S(1)}, bf16[4,3,48,1152]{3,2,1,0:T(8,128)(2,1)}, u32[]{:S(2)}, u32[]{:S(2)}) %collective-permute-start.9) | collective-permute-done | bytes 1327136 | tf_op jit(solution)/shard_map/ppermute | solution.py:765
  163.2 28.1 %collective-permute-done.15.refs_10_ = bf16[4,3,48,1152]{3,2,1,0:T(8,128)(2,1)} collective-permute-done((bf16[4,3,48,1152]{3,2,1,0:T(8,128)(2,1)S(1)}, bf16[4,3,48,1152]{3,2,1,0:T(8,128)(2,1)}, u32[]{:S(2)}, u32[]{:S(2)}) %collective-permute-start.15) | collective-permute-done | bytes 1327136 | tf_op jit(solution)/shard_map/ppermute | solution.py:765
  191.4 4.0 all-to-all-done.1.latent_ref
  198.3 4.7 all-to-all-start.2
  203.1 36.1 %attend.1 = (f32[4,864,1024]{2,1,0:T(8,128)}, bf16[4,288,1024]{2,1,0:T(8,128)(2,1)}, bf16[1024,1152]{1,0:T(8,128)(2,1)}, bf16[1152,1024]{1,0:T(8,128)(2,1)}, f32...) custom-call(bf16[4,4,64,1152]{3,2,1,0:T(8,128)(2,1)} %all-to-all-done.1.latent_ref, ...), custom_call_target="tpu_custom_call" | custom-call | flops 176000008192 | bytes 1024 | tf_op jit(solution)/shard_map/attend/pallas_call | solution.py:286
  242.6 2.0 collective-permute-done.13.refs_7_
  244.6 1.9 collective-permute-done.17.refs_13_
  246.5 37.8 %mlp.1 = (bf16[4,2,1024,768]{3,2,1,0:T(8,128)(2,1)}, f32[1024,1152]{1,0:T(8,128)}, bf16[4,3,768,1152]{3,2,1,0:T(8,128)(2,1)}) custom-call(s32[14]{0:T(128)} %stack.93.e_ref, bf16[1024,1152]{1,0:T(8,128)(2,1)} %get-tuple-element.147.x_ref, bf16[4,3,96,1152]{3,2,1,0:T(8,128)(2,1)} %append.12.refs_0_, bf16[4,3,96,1152]{3,2,1,0:T(8,128)(2,1)} %collective-permute-done.7.refs_1_, ...), custom_call_target="tpu_custom_call" | custom-call | flops 1100000000 | bytes 1024 | tf_op jit(solution)/shard_map/mlp/pallas_call | solution.py:479
  284.4 7.8 %finish.1 = (bf16[1024,1152]{1,0:T(8,128)(2,1)}, bf16[1152,1024]{1,0:T(8,128)(2,1)}, bf16[4,4,64,1152]{3,2,1,0:T(8,128)(2,1)}, f32[4,8,1152]{2,1,0:T(8,128)}) custom-call(f32[1024,1152]{1,0:T(8,128)} %get-tuple-element.156.branch_ref, f32[1024,1152]{1,0:T(8,128)} %get-tuple-element.157.middle_ref, bf16[4,4,64,1152]{3,2,1,0:T(8,128)(2,1)} %all-to-all-done.2.cot_ref, ...), custom_call_target="tpu_custom_call" | custom-call | flops 1100000000 | bytes 1024 | tf_op jit(solution)/shard_map/finish/pallas_call | solution.py:409
  292.1 36.2 %mlp_back.2 = (bf16[2,3,576,768]{3,2,1,0:T(8,128)(2,1)}, bf16[2,3,576,768]{3,2,1,0:T(8,128)(2,1)}, f32[1024,1152]{1,0:T(8,128)}) custom-call(s32[8]{0:T(128)} %broadcast_xor_fusion.2.e_ref, bf16[8,144,1024]{2,1,0:T(8,128)(2,1)} %bitcast.173, bf16[8,144,1024]{2,1,0:T(8,128)(2,1)} %bitcast.169, bf16[1024,1152]{1,0:T(8,128)(2,1)} %get-tuple-element.160.low_ref, ...), custom_call_target="tpu_custom_call" | custom-call | flops 165000003584 | bytes 1024 | tf_op jit(solution)/shard_map/mlp_back/pallas_call | solution.py:555
  328.6 36.0 %mlp_back.3 = (bf16[2,3,576,768]{3,2,1,0:T(8,128)(2,1)}, bf16[2,3,576,768]{3,2,1,0:T(8,128)(2,1)}, f32[1024,1152]{1,0:T(8,128)}) custom-call(s32[8]{0:T(128)} %broadcast_xor_fusion.1.e_ref, bf16[8,144,1024]{2,1,0:T(8,128)(2,1)} %bitcast.174, bf16[8,144,1024]{2,1,0:T(8,128)(2,1)} %bitcast.170, bf16[1024,1152]{1,0:T(8,128)(2,1)} %get-tuple-element.160.low_ref, ...), custom_call_target="tpu_custom_call" | custom-call | flops 165000003584 | bytes 1024 | tf_op jit(solution)/shard_map/mlp_back/pallas_call | solution.py:555
  364.8 5.3 all-to-all-start.3
  370.2 7.6 %sum_halves.7 = (bf16[6,288,768]{2,1,0:T(8,128)(2,1)}, bf16[6,288,768]{2,1,0:T(8,128)(2,1)}) custom-call(bf16[6,576,768]{2,1,0:T(8,128)(2,1)} %bitcast.152, bf16[6,576,768]{2,1,0:T(8,128)(2,1)} %bitcast.52.got_ref), custom_call_target="tpu_custom_call" | custom-call | bytes 1024 | tf_op jit(solution)/shard_map/sum_halves/pallas_call | solution.py:794
  377.8 7.6 %sum_halves.6 = (bf16[6,288,768]{2,1,0:T(8,128)(2,1)}, bf16[6,288,768]{2,1,0:T(8,128)(2,1)}) custom-call(bf16[6,576,768]{2,1,0:T(8,128)(2,1)} %bitcast.151, bf16[6,576,768]{2,1,0:T(8,128)(2,1)} %bitcast.49.got_ref), custom_call_target="tpu_custom_call" | custom-call | bytes 1024 | tf_op jit(solution)/shard_map/sum_halves/pallas_call | solution.py:794
  386.5 11.1 %middle.1 = (f32[1024,1152]{1,0:T(8,128)}, bf16[1024,1152]{1,0:T(8,128)(2,1)}, bf16[1152,1024]{1,0:T(8,128)(2,1)}, f32[4,8,1152]{2,1,0:T(8,128)}) custom-call(f32[1024,1152]{1,0:T(8,128)} %get-tuple-element.172.one_ref, f32[1024,1152]{1,0:T(8,128)} %get-tuple-element.173.other_ref, f32[1024,1152]{1,0:T(8,128)} %get-tuple-element.157.middle_ref, ...), custom_call_target="tpu_custom_call" | custom-call | flops 109999996928 | bytes 1024 | tf_op jit(solution)/shard_map/middle/pallas_call | solution.py:409
  397.6 45.0 %attend_back.1 = (bf16[4,864,1024]{2,1,0:T(8,128)(2,1)}, f32[2,72,256]{2,1,0:T(8,128)}, f32[4,8,1152]{2,1,0:T(8,128)}, bf16[4,4,64,1152]{3,2,1,0:T(8,128)(2,1)}) custom-call(bf16[4,4,64,1152]{3,2,1,0:T(8,128)(2,1)} %all-to-all-done.1.latent_ref, f32[4,864,1024]{2,1,0:T(8,128)} %get-tuple-element.171.proj_ref, bf16[1024,1152]{1,0:T(8,128)(2,1)} %get-tuple-element.175.low_ref, ...), custom_call_target="tpu_custom_call" | custom-call | flops 1100000000 | bytes 1024 | tf_op jit(solution)/shard_map/attend_back/pallas_call | solution.py:330
  445.4 2.9 collective-permute-start.22
  448.4 4.8 all-to-all-start.4
  453.2 5.6 sum_halves.8
  458.8 5.6 sum_halves.9
  468.9 2.0 collective-permute-start.25
  472.0 21.4 %attend_grads.1 = (bf16[4,576,1152]{2,1,0:T(8,128)(2,1)}, bf16[4,576,1152]{2,1,0:T(8,128)(2,1)}) custom-call(s32[4]{0:T(128)} %broadcast_xor_fusion.m_ref, s32[16]{0:T(128)} %pad_add_fusion.e_ref, bf16[8,144,1024]{2,1,0:T(8,128)(2,1)} %bitcast.155, bf16[8,144,1024]{2,1,0:T(8,128)(2,1)} %bitcast.156, bf16[4,864,1024]{2,1,0:T(8,128)(2,1)} %get-tuple-element.195.proj_ref, ...), custom_call_target="tpu_custom_call" | custom-call | bytes 1024 | tf_op jit(solution)/shard_map/attend_grads/pallas_call | solution.py:608
  493.7 12.5 %all-to-all-done.4 = bf16[4,4,64,1152]{3,2,1,0:T(8,128)(2,1)} async-done(((bf16[4,4,64,1152]{3,2,1,0:T(8,128)(2,1)}), bf16[4,4,64,1152]{3,2,1,0:T(8,128)(2,1)}, u32[]{:S(2)}, u32[]{:S(2)}) %all-to-all-start.4) | async-done | bytes 2359328 | tf_op jit(solution)/shard_map/all_to_all | solution.py:870
  506.3 2.1 append.14.one_ref
  509.8 7.6 %sum_quarters.1 = (bf16[2,288,1152]{2,1,0:T(8,128)(2,1)}, bf16[2,288,1152]{2,1,0:T(8,128)(2,1)}, bf16[2,288,1152]{2,1,0:T(8,128)(2,1)}, bf16[2,288,1152]{2,1,0:T(8,128)(2,1)}) custom-call(bf16[4,576,1152]{2,1,0:T(8,128)(2,1)} %get-tuple-element.205.kept_ref, bf16[4,576,1152]{2,1,0:T(8,128)(2,1)} %collective-permute-done.26.got_ref), custom_call_target="tpu_custom_call" | custom-call | bytes 1024 | tf_op jit(solution)/shard_map/sum_quarters/pallas_call | solution.py:719
  519.5 7.8 %take_rows.1 = bf16[32,64,1152]{2,1,0:T(8,128)(2,1)} custom-call(s32[32]{0:T(128)} %get-tuple-element.137.index_ref, bf16[16,64,1152]{2,1,0:T(8,128)(2,1)} %bitcast.67.refs_0_.refs_1_.refs_2_.refs_3_, bf16[16,64,1152]{2,1,0:T(8,128)(2,1)} %bitcast.67.refs_0_.refs_1_.refs_2_.refs_3_, bf16[16,64,1152]{2,1,0:T(8,128)(2,1)} %bitcast.67.refs_0_.refs_1_.refs_2_.refs_3_, ...), custom_call_target="tpu_custom_call" | custom-call | flops 219999993856 | bytes 1024 | tf_op jit(solution)/shard_map/take_rows/pallas_call | solution.py:678
  527.2 3.3 copy_result.1
  530.6 2.0 append.15.one_ref
  533.3 2.7 add_convert_fusion.1
  536.0 1.6 add_convert_fusion.2
  537.7 9.9 %collective-permute-done.29.got_ref = bf16[2,288,1152]{2,1,0:T(8,128)(2,1)} collective-permute-done((bf16[2,288,1152]{2,1,0:T(8,128)(2,1)}, bf16[2,288,1152]{2,1,0:T(8,128)(2,1)}, u32[]{:S(2)}, u32[]{:S(2)}) %collective-permute-start.29) | collective-permute-done | bytes 1327136 | tf_op jit(solution)/shard_map/ppermute | solution.py:765
  547.6 2.6 sum_halves.11
  550.4 2.6 sum_halves.10
  554.5 5.9 collective-permute-done.30.other_ref
  561.2 2.3 append.16.one_ref
  565.2 4.9 all-to-all-start.5
  570.2 2.1 add_convert_fusion.5
  576.6 3.2 append.17
  580.8 1.9 copy.95
  582.8 2.4 fusion.12
  585.3 2.3 fusion.28
  588.3 10.2 %collective-permute-done.34 = bf16[2,144,1152]{2,1,0:T(8,128)(2,1)} collective-permute-done((bf16[2,144,1152]{2,1,0:T(8,128)(2,1)}, bf16[2,144,1152]{2,1,0:T(8,128)(2,1)}, u32[]{:S(2)}, u32[]{:S(2)}) %collective-permute-start.34) | collective-permute-done | bytes 663584 | tf_op jit(solution)/shard_map/ppermute | solution.py:765
  598.5 1.7 add_convert_fusion.4
  602.2 20.6 %collective-permute-done.35 = bf16[1,144,1152]{2,1,0:T(8,128)(2,1)S(1)} collective-permute-done((bf16[1,144,1152]{2,1,0:T(8,128)(2,1)S(1)}, bf16[1,144,1152]{2,1,0:T(8,128)(2,1)S(1)}, u32[]{:S(2)}, u32[]{:S(2)}) %collective-permute-start.35) | collective-permute-done | bytes 331808 | tf_op jit(solution)/shard_map/ppermute | solution.py:765
  630.1 1.9 all-to-all-done.5
  632.0 5.7 gather_fusion.8
  (298 shorter events, 77.6 us)
Async XLA Ops:
  7.2 26.2 %copy-start = (bf16[1152,3,288]{0,2,1:T(8,128)(2,1)S(1)}, bf16[1152,3,288]{0,2,1:T(8,128)(2,1)}, u32[]{:S(2)}) copy-start(bf16[1152,3,288]{0,2,1:T(8,128)(2,1)} %param.36) | copy-start | bytes 5971972
  8.9 30.1 %copy-start.2 = (s32[8]{0:T(128)}, s32[8]{0:T(128)S(1)}, u32[]{:S(2)}) copy-start(s32[8]{0:T(128)S(1)} %bitcast_subtract_fusion.1) | copy-start | bytes 100
  22.9 36.5 %collective-permute-start = (bf16[1,3,96,1152]{3,2,1,0:T(8,128)(2,1)}, bf16[1,3,96,1152]{3,2,1,0:T(8,128)(2,1)}, u32[]{:S(2)}, u32[]{:S(2)}) collective-permute-start(bf16[1,3,96,1152]{3,2,1,0:T(8,128)(2,1)} %maximum_bitcast_fusion), channel_id=1, source_target_pairs={{0,2},{1,3},{2,0},{3,1},{4,6},{5,7},{6,4},{7,5},{8,10},{9,11},{10,... | collective-permute-start | bytes 1990664 | tf_op jit(solution)/shard_map/ppermute | solution.py:765
  27.0 18.5 %collective-permute-start.2 = (s32[1,2,32]{2,1,0:T(2,128)S(1)}, s32[1,2,32]{2,1,0:T(2,128)S(1)}, u32[]{:S(2)}, u32[]{:S(2)}) collective-permute-start(s32[1,2,32]{2,1,0:T(2,128)S(1)} %add_bitcast_fusion.one_ref), channel_id=1, source_target_pairs={{0,4},{4,0},{8,12},{12,8},{16,20},{20,16},{24,28},{28,24},{1,5},{5... | collective-permute-start | bytes 776 | tf_op jit(solution)/shard_map/ppermute | solution.py:765
  27.5 72.1 %all-to-all-start = ((bf16[32,64,1152]{2,1,0:T(8,128)(2,1)}), bf16[32,64,1152]{2,1,0:T(8,128)(2,1)}, u32[]{:S(2)}, u32[]{:S(2)}) async-start(bf16[32,64,1152]{2,1,0:T(8,128)(2,1)} %gather_fusion.1), calls=%async_computation | async-start | bytes 9437184 | tf_op jit(solution)/shard_map/all_to_all | solution.py:889
  32.1 171.0 %all-gather.3.cloned.1.call-start = ((), (), s32[]{:S(2)}) async-start(), calls=%async_computation.6 | async-start | bytes 10948608 | tf_op jit(solution)/shard_map/all_gather | solution.py:641
  47.3 14.6 %copy-start.48 = (s32[2,2,32]{2,1,0:T(2,128)S(1)}, s32[2,2,32]{2,1,0:T(2,128)}, u32[]{:S(2)}) copy-start(s32[2,2,32]{2,1,0:T(2,128)} %append.9.one_ref) | copy-start | bytes 1540
  47.3 20.3 %copy-start.43 = (s32[32]{0:T(128)S(1)}, s32[32]{0:T(128)}, u32[]{:S(2)}) copy-start(s32[32]{0:T(128)} %fusion.56) | copy-start | bytes 388
  47.3 20.9 %copy-start.28 = (s32[256]{0:T(256)S(1)}, s32[256]{0:T(256)}, u32[]{:S(2)}) copy-start(s32[256]{0:T(256)} %select_reduce_fusion.2) | copy-start | bytes 3076
  61.9 35.8 %collective-permute-start.3 = (s32[2,2,32]{2,1,0:T(2,128)S(1)}, s32[2,2,32]{2,1,0:T(2,128)S(1)}, u32[]{:S(2)}, u32[]{:S(2)}) collective-permute-start(s32[2,2,32]{2,1,0:T(2,128)S(1)} %copy-done.48), channel_id=1, source_target_pairs={{0,8},{4,12},{8,0},{12,4},{16,24},{20,28},{24,16},{28,20},{1,9},{5... | collective-permute-start | bytes 1544 | tf_op jit(solution)/shard_map/ppermute | solution.py:765
  69.3 45.2 %collective-permute-start.1 = (bf16[2,3,96,1152]{3,2,1,0:T(8,128)(2,1)}, bf16[2,3,96,1152]{3,2,1,0:T(8,128)(2,1)}, u32[]{:S(2)}, u32[]{:S(2)}) collective-permute-start(bf16[2,3,96,1152]{3,2,1,0:T(8,128)(2,1)} %pad_maximum_fusion.one_ref), channel_id=1, source_target_pairs={{0,1},{1,0},{2,3},{3,2},{4,5},{5,4},{6,7},{7,6},{8,9},{9,8},{10,11... | collective-permute-start | bytes 3981320 | tf_op jit(solution)/shard_map/ppermute | solution.py:765
  114.4 80.9 %all-to-all-start.1 = ((bf16[4,4,64,1152]{3,2,1,0:T(8,128)(2,1)}), bf16[4,4,64,1152]{3,2,1,0:T(8,128)(2,1)}, u32[]{:S(2)}, u32[]{:S(2)}) async-start(bf16[4,4,64,1152]{3,2,1,0:T(8,128)(2,1)} %bitcast.150), calls=%async_computation.1 | async-start | bytes 4718592 | tf_op jit(solution)/shard_map/all_to_all | solution.py:870
  122.9 68.5 %collective-permute-start.7 = (bf16[4,3,96,1152]{3,2,1,0:T(8,128)(2,1)}, bf16[4,3,96,1152]{3,2,1,0:T(8,128)(2,1)}, u32[]{:S(2)}, u32[]{:S(2)}) collective-permute-start(bf16[4,3,96,1152]{3,2,1,0:T(8,128)(2,1)} %append.12.refs_0_), channel_id=1, source_target_pairs={{0,4},{4,0},{8,12},{12,8},{16,20},{20,16},{24,28},{28,24},{1,5},{5... | collective-permute-start | bytes 7962632 | tf_op jit(solution)/shard_map/ppermute | solution.py:765
  122.9 5.9 collective-permute-start.4
  126.7 64.6 %collective-permute-start.5 = (bf16[4,3,48,1152]{3,2,1,0:T(8,128)(2,1)S(1)}, bf16[4,3,48,1152]{3,2,1,0:T(8,128)(2,1)}, u32[]{:S(2)}, u32[]{:S(2)}) collective-permute-start(bf16[4,3,48,1152]{3,2,1,0:T(8,128)(2,1)S(1)} %get-tuple-element.289), channel_id=1, source_target_pairs={{0,8},{4,12},{8,0},{12,4},{16,24},{20,28},{24,16},{28,20},{1,9},{5... | collective-permute-start | bytes 3981320 | tf_op jit(solution)/shard_map/ppermute | solution.py:765
  126.8 36.5 %collective-permute-start.9 = (bf16[4,3,48,1152]{3,2,1,0:T(8,128)(2,1)S(1)}, bf16[4,3,48,1152]{3,2,1,0:T(8,128)(2,1)}, u32[]{:S(2)}, u32[]{:S(2)}) collective-permute-start(bf16[4,3,48,1152]{3,2,1,0:T(8,128)(2,1)S(1)} %get-tuple-element.289), channel_id=1, source_target_pairs={{0,16},{4,20},{8,24},{12,28},{16,0},{20,4},{24,8},{28,12},{1,17},{... | collective-permute-start | bytes 3981320 | tf_op jit(solution)/shard_map/ppermute | solution.py:765
  127.2 64.3 %collective-permute-start.6 = (bf16[4,3,48,1152]{3,2,1,0:T(8,128)(2,1)S(1)}, bf16[4,3,48,1152]{3,2,1,0:T(8,128)(2,1)}, u32[]{:S(2)}, u32[]{:S(2)}) collective-permute-start(bf16[4,3,48,1152]{3,2,1,0:T(8,128)(2,1)S(1)} %get-tuple-element.288), channel_id=1, source_target_pairs={{0,16},{4,20},{8,24},{12,28},{16,0},{20,4},{24,8},{28,12},{1,17},{... | collective-permute-start | bytes 3981320 | tf_op jit(solution)/shard_map/ppermute | solution.py:765
  128.9 62.5 %collective-permute-start.15 = (bf16[4,3,48,1152]{3,2,1,0:T(8,128)(2,1)S(1)}, bf16[4,3,48,1152]{3,2,1,0:T(8,128)(2,1)}, u32[]{:S(2)}, u32[]{:S(2)}) collective-permute-start(bf16[4,3,48,1152]{3,2,1,0:T(8,128)(2,1)S(1)} %get-tuple-element.288), channel_id=1, source_target_pairs={{0,8},{4,12},{8,0},{12,4},{16,24},{20,28},{24,16},{28,20},{1,9},{5... | collective-permute-start | bytes 3981320 | tf_op jit(solution)/shard_map/ppermute | solution.py:765
  133.3 13.8 %copy-start.25 = (s32[128]{0:T(128)}, s32[128]{0:T(128)S(1)}, u32[]{:S(2)}) copy-start(s32[128]{0:T(128)S(1)} %get-tuple-element.287) | copy-start | bytes 1540
  163.2 76.6 %collective-permute-start.10 = (bf16[4,3,48,1152]{3,2,1,0:T(8,128)(2,1)}, bf16[4,3,48,1152]{3,2,1,0:T(8,128)(2,1)}, u32[]{:S(2)}, u32[]{:S(2)}) collective-permute-start(bf16[4,3,48,1152]{3,2,1,0:T(8,128)(2,1)} %collective-permute-done.9.refs_4_), channel_id=1, source_target_pairs={{0,4},{4,0},{8,12},{12,8},{16,20},{20,16},{24,28},{28,24},{1,5},{5... | collective-permute-start | bytes 3981320 | tf_op jit(solution)/shard_map/ppermute | solution.py:765
  191.3 50.5 %collective-permute-start.16 = (bf16[4,3,48,1152]{3,2,1,0:T(8,128)(2,1)}, bf16[4,3,48,1152]{3,2,1,0:T(8,128)(2,1)}, u32[]{:S(2)}, u32[]{:S(2)}) collective-permute-start(bf16[4,3,48,1152]{3,2,1,0:T(8,128)(2,1)} %collective-permute-done.15.refs_10_), channel_id=1, source_target_pairs={{0,4},{4,0},{8,12},{12,8},{16,20},{20,16},{24,28},{28,24},{1,5},{5... | collective-permute-start | bytes 3981320 | tf_op jit(solution)/shard_map/ppermute | solution.py:765
  195.4 44.2 %collective-permute-start.12 = (bf16[4,3,48,1152]{3,2,1,0:T(8,128)(2,1)}, bf16[4,3,48,1152]{3,2,1,0:T(8,128)(2,1)}, u32[]{:S(2)}, u32[]{:S(2)}) collective-permute-start(bf16[4,3,48,1152]{3,2,1,0:T(8,128)(2,1)} %collective-permute-done.6.refs_8_), channel_id=1, source_target_pairs={{0,8},{4,12},{8,0},{12,4},{16,24},{20,28},{24,16},{28,20},{1,9},{5... | collective-permute-start | bytes 3981320 | tf_op jit(solution)/shard_map/ppermute | solution.py:765
  196.9 45.0 %collective-permute-start.14 = (bf16[4,3,48,1152]{3,2,1,0:T(8,128)(2,1)}, bf16[4,3,48,1152]{3,2,1,0:T(8,128)(2,1)}, u32[]{:S(2)}, u32[]{:S(2)}) collective-permute-start(bf16[4,3,48,1152]{3,2,1,0:T(8,128)(2,1)} %collective-permute-done.6.refs_8_), channel_id=1, source_target_pairs={{0,4},{4,0},{8,12},{12,8},{16,20},{20,16},{24,28},{28,24},{1,5},{5... | collective-permute-start | bytes 3981320 | tf_op jit(solution)/shard_map/ppermute | solution.py:765
  196.9 42.4 %collective-permute-start.11 = (bf16[4,3,48,1152]{3,2,1,0:T(8,128)(2,1)}, bf16[4,3,48,1152]{3,2,1,0:T(8,128)(2,1)}, u32[]{:S(2)}, u32[]{:S(2)}) collective-permute-start(bf16[4,3,48,1152]{3,2,1,0:T(8,128)(2,1)} %collective-permute-done.5.refs_2_), channel_id=1, source_target_pairs={{0,16},{4,20},{8,24},{12,28},{16,0},{20,4},{24,8},{28,12},{1,17},{... | collective-permute-start | bytes 3981320 | tf_op jit(solution)/shard_map/ppermute | solution.py:765
  198.3 86.0 %all-to-all-start.2 = ((bf16[4,4,64,1152]{3,2,1,0:T(8,128)(2,1)}), bf16[4,4,64,1152]{3,2,1,0:T(8,128)(2,1)}, u32[]{:S(2)}, u32[]{:S(2)}) async-start(bf16[4,4,64,1152]{3,2,1,0:T(8,128)(2,1)} %bitcast.157), calls=%async_computation.2 | async-start | bytes 4718592 | tf_op jit(solution)/shard_map/all_to_all | solution.py:870
  203.1 37.7 %copy-start.53 = (s32[8]{0:T(128)S(1)}, s32[8]{0:T(128)}, u32[]{:S(2)}) copy-start(s32[8]{0:T(128)} %constant.213.clone) | copy-start | bytes 100
  203.1 38.2 %copy-start.52 = (s32[8]{0:T(128)S(1)}, s32[8]{0:T(128)}, u32[]{:S(2)}) copy-start(s32[8]{0:T(128)} %constant.214.clone) | copy-start | bytes 100
  239.3 3.3 collective-permute-start.8
  239.6 5.1 collective-permute-start.13
  239.9 6.7 %collective-permute-start.17 = (bf16[4,3,48,1152]{3,2,1,0:T(8,128)(2,1)}, bf16[4,3,48,1152]{3,2,1,0:T(8,128)(2,1)}, u32[]{:S(2)}, u32[]{:S(2)}) collective-permute-start(bf16[4,3,48,1152]{3,2,1,0:T(8,128)(2,1)} %collective-permute-done.12.refs_12_), channel_id=1, source_target_pairs={{0,4},{4,0},{8,12},{12,8},{16,20},{20,16},{24,28},{28,24},{1,5},{5... | collective-permute-start | bytes 3981320 | tf_op jit(solution)/shard_map/ppermute | solution.py:765
  328.3 41.8 %collective-permute-start.19 = (bf16[2,3,576,768]{3,2,1,0:T(8,128)(2,1)}, bf16[2,3,576,768]{3,2,1,0:T(8,128)(2,1)}, u32[]{:S(2)}, u32[]{:S(2)}) collective-permute-start(bf16[2,3,576,768]{3,2,1,0:T(8,128)(2,1)} %get-tuple-element.168), channel_id=1, source_target_pairs={{0,4},{4,0},{8,12},{12,8},{16,20},{20,16},{24,28},{28,24},{1,5},{5... | collective-permute-start | bytes 15925256 | tf_op jit(solution)/shard_map/ppermute | solution.py:765
  364.6 13.2 %collective-permute-start.18 = (bf16[2,3,576,768]{3,2,1,0:T(8,128)(2,1)}, bf16[2,3,576,768]{3,2,1,0:T(8,128)(2,1)}, u32[]{:S(2)}, u32[]{:S(2)}) collective-permute-start(bf16[2,3,576,768]{3,2,1,0:T(8,128)(2,1)} %get-tuple-element.165), channel_id=1, source_target_pairs={{0,4},{4,0},{8,12},{12,8},{16,20},{20,16},{24,28},{28,24},{1,5},{5... | collective-permute-start | bytes 15925256 | tf_op jit(solution)/shard_map/ppermute | solution.py:765
  364.8 83.5 %all-to-all-start.3 = ((bf16[4,4,64,1152]{3,2,1,0:T(8,128)(2,1)}), bf16[4,4,64,1152]{3,2,1,0:T(8,128)(2,1)}, u32[]{:S(2)}, u32[]{:S(2)}) async-start(bf16[4,4,64,1152]{3,2,1,0:T(8,128)(2,1)} %get-tuple-element.192), calls=%async_computation.3 | async-start | bytes 4718592 | tf_op jit(solution)/shard_map/all_to_all | solution.py:870
  385.4 63.0 %collective-permute-start.21 = (bf16[2,3,288,768]{3,2,1,0:T(8,128)(2,1)}, bf16[2,3,288,768]{3,2,1,0:T(8,128)(2,1)}, u32[]{:S(2)}, u32[]{:S(2)}) collective-permute-start(bf16[2,3,288,768]{3,2,1,0:T(8,128)(2,1)} %bitcast.167), channel_id=1, source_target_pairs={{0,8},{4,12},{8,0},{12,4},{16,24},{20,28},{24,16},{28,20},{1,9},{5... | collective-permute-start | bytes 7962632 | tf_op jit(solution)/shard_map/ppermute | solution.py:765
  386.0 62.4 %collective-permute-start.20 = (bf16[2,3,288,768]{3,2,1,0:T(8,128)(2,1)}, bf16[2,3,288,768]{3,2,1,0:T(8,128)(2,1)}, u32[]{:S(2)}, u32[]{:S(2)}) collective-permute-start(bf16[2,3,288,768]{3,2,1,0:T(8,128)(2,1)} %bitcast.168), channel_id=1, source_target_pairs={{0,16},{4,20},{8,24},{12,28},{16,0},{20,4},{24,8},{28,12},{1,17},{... | collective-permute-start | bytes 7962632 | tf_op jit(solution)/shard_map/ppermute | solution.py:765
  397.6 46.0 %copy-start.32 = (f32[2]{0:T(128)S(1)}, f32[2]{0:T(128)}, u32[]{:S(2)}) copy-start(f32[2]{0:T(128)} %constant.221) | copy-start | bytes 28
  397.6 46.2 %copy-start.18 = (f32[4,8,1152]{2,1,0:T(8,128)S(1)}, f32[4,8,1152]{2,1,0:T(8,128)}, u32[]{:S(2)}) copy-start(f32[4,8,1152]{2,1,0:T(8,128)} %get-tuple-element.183) | copy-start | bytes 442372
  397.6 46.2 %copy-start.19 = (f32[4,8,1152]{2,1,0:T(8,128)S(1)}, f32[4,8,1152]{2,1,0:T(8,128)}, u32[]{:S(2)}) copy-start(f32[4,8,1152]{2,1,0:T(8,128)} %get-tuple-element.184) | copy-start | bytes 442372
  445.4 13.3 %collective-permute-start.22 = (bf16[1,4,8,1152]{3,2,1,0:T(8,128)(2,1)}, bf16[1,4,8,1152]{3,2,1,0:T(8,128)(2,1)}, u32[]{:S(2)}, u32[]{:S(2)}) collective-permute-start(bf16[1,4,8,1152]{3,2,1,0:T(8,128)(2,1)} %fusion.32.one_ref), channel_id=1, source_target_pairs={{0,2},{1,3},{2,0},{3,1},{4,6},{5,7},{6,4},{7,5},{8,10},{9,11},{10,... | collective-permute-start | bytes 221192 | tf_op jit(solution)/shard_map/ppermute | solution.py:765
  448.4 57.9 %all-to-all-start.4 = ((bf16[4,4,64,1152]{3,2,1,0:T(8,128)(2,1)}), bf16[4,4,64,1152]{3,2,1,0:T(8,128)(2,1)}, u32[]{:S(2)}, u32[]{:S(2)}) async-start(bf16[4,4,64,1152]{3,2,1,0:T(8,128)(2,1)} %get-tuple-element.200), calls=%async_computation.4 | async-start | bytes 4718592 | tf_op jit(solution)/shard_map/all_to_all | solution.py:870
  458.7 12.7 %copy-start.54 = (s32[8]{0:T(128)S(1)}, s32[8]{0:T(128)}, u32[]{:S(2)}) copy-start(s32[8]{0:T(128)} %broadcast_xor_fusion.2.e_ref) | copy-start | bytes 100
  458.7 12.7 %copy-start.55 = (s32[8]{0:T(128)S(1)}, s32[8]{0:T(128)}, u32[]{:S(2)}) copy-start(s32[8]{0:T(128)} %broadcast_xor_fusion.1.e_ref) | copy-start | bytes 100
  464.3 41.9 %collective-permute-start.24 = (bf16[2,3,144,768]{3,2,1,0:T(8,128)(2,1)}, bf16[2,3,144,768]{3,2,1,0:T(8,128)(2,1)S(1)}, u32[]{:S(2)}, u32[]{:S(2)}) collective-permute-start(bf16[2,3,144,768]{3,2,1,0:T(8,128)(2,1)} %bitcast.172), channel_id=1, source_target_pairs={{0,16},{4,20},{8,24},{12,28},{16,0},{20,4},{24,8},{28,12},{1,17},{... | collective-permute-start | bytes 3981320 | tf_op jit(solution)/shard_map/ppermute | solution.py:765
  465.8 40.4 %collective-permute-start.23 = (bf16[2,3,144,768]{3,2,1,0:T(8,128)(2,1)}, bf16[2,3,144,768]{3,2,1,0:T(8,128)(2,1)S(1)}, u32[]{:S(2)}, u32[]{:S(2)}) collective-permute-start(bf16[2,3,144,768]{3,2,1,0:T(8,128)(2,1)} %bitcast.171), channel_id=1, source_target_pairs={{0,8},{4,12},{8,0},{12,4},{16,24},{20,28},{24,16},{28,20},{1,9},{5... | collective-permute-start | bytes 3981320 | tf_op jit(solution)/shard_map/ppermute | solution.py:765
  468.9 24.8 %collective-permute-start.25 = (bf16[2,4,8,1152]{3,2,1,0:T(8,128)(2,1)}, bf16[2,4,8,1152]{3,2,1,0:T(8,128)(2,1)S(1)}, u32[]{:S(2)}, u32[]{:S(2)}) collective-permute-start(bf16[2,4,8,1152]{3,2,1,0:T(8,128)(2,1)} %append.13.one_ref), channel_id=1, source_target_pairs={{0,1},{1,0},{2,3},{3,2},{4,5},{5,4},{6,7},{7,6},{8,9},{9,8},{10,11... | collective-permute-start | bytes 442376 | tf_op jit(solution)/shard_map/ppermute | solution.py:765
  493.4 16.4 %collective-permute-start.26 = (bf16[4,576,1152]{2,1,0:T(8,128)(2,1)}, bf16[4,576,1152]{2,1,0:T(8,128)(2,1)}, u32[]{:S(2)}, u32[]{:S(2)}) collective-permute-start(bf16[4,576,1152]{2,1,0:T(8,128)(2,1)} %get-tuple-element.206), channel_id=1, source_target_pairs={{0,4},{4,0},{8,12},{12,8},{16,20},{20,16},{24,28},{28,24},{1,5},{5... | collective-permute-start | bytes 15925256 | tf_op jit(solution)/shard_map/ppermute | solution.py:765
  493.7 12.5 %copy-start.47 = (bf16[2,4,8,1152]{3,2,1,0:T(8,128)(2,1)}, bf16[2,4,8,1152]{3,2,1,0:T(8,128)(2,1)S(1)}, u32[]{:S(2)}) copy-start(bf16[2,4,8,1152]{3,2,1,0:T(8,128)(2,1)S(1)} %collective-permute-done.25.other_ref) | copy-start | bytes 442372
  508.3 22.3 %collective-permute-start.28 = (bf16[4,4,8,1152]{3,2,1,0:T(8,128)(2,1)}, bf16[4,4,8,1152]{3,2,1,0:T(8,128)(2,1)}, u32[]{:S(2)}, u32[]{:S(2)}) collective-permute-start(bf16[4,4,8,1152]{3,2,1,0:T(8,128)(2,1)} %append.14.one_ref), channel_id=1, source_target_pairs={{0,8},{4,12},{8,0},{12,4},{16,24},{20,28},{24,16},{28,20},{1,9},{5... | collective-permute-start | bytes 884744 | tf_op jit(solution)/shard_map/ppermute | solution.py:765
  517.4 30.1 %collective-permute-start.29 = (bf16[2,288,1152]{2,1,0:T(8,128)(2,1)}, bf16[2,288,1152]{2,1,0:T(8,128)(2,1)}, u32[]{:S(2)}, u32[]{:S(2)}) collective-permute-start(bf16[2,288,1152]{2,1,0:T(8,128)(2,1)} %get-tuple-element.225), channel_id=1, source_target_pairs={{0,8},{4,12},{8,0},{12,4},{16,24},{20,28},{24,16},{28,20},{1,9},{5... | collective-permute-start | bytes 3981320 | tf_op jit(solution)/shard_map/ppermute | solution.py:765
  518.0 32.4 %collective-permute-start.27 = (bf16[2,288,1152]{2,1,0:T(8,128)(2,1)}, bf16[2,288,1152]{2,1,0:T(8,128)(2,1)}, u32[]{:S(2)}, u32[]{:S(2)}) collective-permute-start(bf16[2,288,1152]{2,1,0:T(8,128)(2,1)} %get-tuple-element.221), channel_id=1, source_target_pairs={{0,16},{4,20},{8,24},{12,28},{16,0},{20,4},{24,8},{28,12},{1,17},{... | collective-permute-start | bytes 3981320 | tf_op jit(solution)/shard_map/ppermute | solution.py:765
  532.6 27.8 %collective-permute-start.30 = (bf16[8,4,8,1152]{3,2,1,0:T(8,128)(2,1)}, bf16[8,4,8,1152]{3,2,1,0:T(8,128)(2,1)S(1)}, u32[]{:S(2)}, u32[]{:S(2)}) collective-permute-start(bf16[8,4,8,1152]{3,2,1,0:T(8,128)(2,1)} %append.15.one_ref), channel_id=1, source_target_pairs={{0,16},{4,20},{8,24},{12,28},{16,0},{20,4},{24,8},{28,12},{1,17},{... | collective-permute-start | bytes 1769480 | tf_op jit(solution)/shard_map/ppermute | solution.py:765
  536.0 37.3 %collective-permute-start.36 = (bf16[2,3,144,768]{3,2,1,0:T(8,128)(2,1)}, bf16[2,3,144,768]{3,2,1,0:T(8,128)(2,1)}, u32[]{:S(2)}, u32[]{:S(2)}) collective-permute-start(bf16[2,3,144,768]{3,2,1,0:T(8,128)(2,1)} %add_convert_fusion.1), channel_id=1, source_target_pairs={{0,1},{1,0},{2,3},{3,2},{4,5},{5,4},{6,7},{7,6},{8,9},{9,8},{10,11... | collective-permute-start | bytes 3981320 | tf_op jit(solution)/shard_map/ppermute | solution.py:765
  550.2 13.4 %copy-start.34 = (s32[72]{0:T(128)S(1)}, s32[72]{0:T(128)}, u32[]{:S(2)}) copy-start(s32[72]{0:T(128)} %constant.222) | copy-start | bytes 868
  550.2 13.5 %copy-start.46 = (s32[32]{0:T(128)S(1)}, s32[32]{0:T(128)}, u32[]{:S(2)}) copy-start(s32[32]{0:T(128)} %get-tuple-element.230) | copy-start | bytes 388
  553.0 17.1 %collective-permute-start.33 = (bf16[2,144,1152]{2,1,0:T(8,128)(2,1)}, bf16[2,144,1152]{2,1,0:T(8,128)(2,1)}, u32[]{:S(2)}, u32[]{:S(2)}) collective-permute-start(bf16[2,144,1152]{2,1,0:T(8,128)(2,1)} %get-tuple-element.240), channel_id=1, source_target_pairs={{0,8},{4,12},{8,0},{12,4},{16,24},{20,28},{24,16},{28,20},{1,9},{5... | collective-permute-start | bytes 1990664 | tf_op jit(solution)/shard_map/ppermute | solution.py:765
  563.6 8.7 %collective-permute-start.31 = (bf16[16,4,8,1152]{3,2,1,0:T(8,128)(2,1)}, bf16[16,4,8,1152]{3,2,1,0:T(8,128)(2,1)S(1)}, u32[]{:S(2)}, u32[]{:S(2)}) collective-permute-start(bf16[16,4,8,1152]{3,2,1,0:T(8,128)(2,1)} %append.16.one_ref), channel_id=1, source_target_pairs={{0,4},{4,0},{8,12},{12,8},{16,20},{20,16},{24,28},{28,24},{1,5},{5... | collective-permute-start | bytes 3538952 | tf_op jit(solution)/shard_map/ppermute | solution.py:765
  563.7 24.6 %collective-permute-start.32 = (bf16[2,144,1152]{2,1,0:T(8,128)(2,1)}, bf16[2,144,1152]{2,1,0:T(8,128)(2,1)}, u32[]{:S(2)}, u32[]{:S(2)}) collective-permute-start(bf16[2,144,1152]{2,1,0:T(8,128)(2,1)} %get-tuple-element.238), channel_id=1, source_target_pairs={{0,16},{4,20},{8,24},{12,28},{16,0},{20,4},{24,8},{28,12},{1,17},{... | collective-permute-start | bytes 1990664 | tf_op jit(solution)/shard_map/ppermute | solution.py:765
  565.2 66.8 %all-to-all-start.5 = ((bf16[32,64,1152]{2,1,0:T(8,128)(2,1)}), bf16[32,64,1152]{2,1,0:T(8,128)(2,1)}, u32[]{:S(2)}, u32[]{:S(2)}) async-start(bf16[32,64,1152]{2,1,0:T(8,128)(2,1)} %take_rows.1), calls=%async_computation.5 | async-start | bytes 9437184 | tf_op jit(solution)/shard_map/all_to_all | solution.py:1125
  572.2 26.3 %collective-permute-start.34 = (bf16[2,144,1152]{2,1,0:T(8,128)(2,1)}, bf16[2,144,1152]{2,1,0:T(8,128)(2,1)}, u32[]{:S(2)}, u32[]{:S(2)}) collective-permute-start(bf16[2,144,1152]{2,1,0:T(8,128)(2,1)} %add_convert_fusion.5), channel_id=1, source_target_pairs={{0,1},{1,0},{2,3},{3,2},{4,5},{5,4},{6,7},{7,6},{8,9},{9,8},{10,11... | collective-permute-start | bytes 1990664 | tf_op jit(solution)/shard_map/ppermute | solution.py:765
  575.9 50.5 %collective-permute-start.37 = (bf16[1,3,144,768]{3,2,1,0:T(8,128)(2,1)}, bf16[1,3,144,768]{3,2,1,0:T(8,128)(2,1)}, u32[]{:S(2)}, u32[]{:S(2)}) collective-permute-start(bf16[1,3,144,768]{3,2,1,0:T(8,128)(2,1)} %slice.144), channel_id=1, source_target_pairs={{0,2},{1,3},{2,0},{3,1},{4,6},{5,7},{6,4},{7,5},{8,10},{9,11},{10,... | collective-permute-start | bytes 1990664 | tf_op jit(solution)/shard_map/ppermute | solution.py:765
  585.3 13.3 %copy-start.15 = (bf16[2,144,1152]{2,1,0:T(8,128)(2,1)S(1)}, bf16[2,144,1152]{2,1,0:T(8,128)(2,1)}, u32[]{:S(2)}) copy-start(bf16[2,144,1152]{2,1,0:T(8,128)(2,1)} %get-tuple-element.237) | copy-start | bytes 1990660
  587.6 13.4 %copy-start.38 = (s32[128]{0:T(128)S(1)}, s32[128]{0:T(128)}, u32[]{:S(2)}) copy-start(s32[128]{0:T(128)} %copy-done.37) | copy-start | bytes 1540
  598.5 24.3 %copy-start.7 = (f32[864,864]{1,0:T(8,128)S(1)}, f32[864,864]{1,0:T(8,128)}, u32[]{:S(2)}) copy-start(f32[864,864]{1,0:T(8,128)} %constant.217.clone) | copy-start | bytes 8957956
  600.3 22.4 %collective-permute-start.35 = (bf16[1,144,1152]{2,1,0:T(8,128)(2,1)S(1)}, bf16[1,144,1152]{2,1,0:T(8,128)(2,1)S(1)}, u32[]{:S(2)}, u32[]{:S(2)}) collective-permute-start(bf16[1,144,1152]{2,1,0:T(8,128)(2,1)S(1)} %slice.139), channel_id=1, source_target_pairs={{0,2},{1,3},{2,0},{3,1},{4,6},{5,7},{6,4},{7,5},{8,10},{9,11},{10,... | collective-permute-start | bytes 995336 | tf_op jit(solution)/shard_map/ppermute | solution.py:765
  (39 other events, 232.3 us)
Sparse Core Ops, SparseCore 0:
  36.4 134.3 all-gather.2

commit v13 on v12

--- a/solution.py
+++ b/solution.py
@@ -883,11 +883,12 @@
     send_index = pair_slot * dp_size + jnp.mod(inverse[pair_peer] - my_start, dp_size)
     send_index = jnp.minimum(send_index, capacity - 1)
     send_patches = pick_rows(patches, send_index)
-    qkv_weight, out_weight, expand_weight, down_weight, send_patches = tie(
-        qkv_weight, out_weight, expand_weight, down_weight, send_patches
-    )
+    time_bins, labels, send_patches = tie(time_bins, labels, send_patches)
     recv_patches = lax.all_to_all(send_patches, "dp", split_axis=0, concat_axis=0, tiled=True)
-    info = jnp.stack([time_bins, labels])[None]
+    info = append(time_bins[None], labels[None], 200)[None]
+    qkv_weight, out_weight, expand_weight, down_weight, info = tie(
+        qkv_weight, out_weight, expand_weight, down_weight, info
+    )
     got_info = swap(info, "dp", dp_bits[0][0])
 
     share = 4 * local_dim // dp_size
@@ -925,7 +926,7 @@
 
     info_places = [0]
     for step, bit in enumerate(dp_bits[0]):
-        info = append(info, got_info, 200 if step < 2 else 0)
+        info = append(info, got_info, 200 if step == 1 else 0)
         info_places = info_places + [place ^ bit for place in info_places]
         if by_permutes and step == 0:
             mlp_near = jnp.concatenate([mlp_near, far_near], axis=0)

time: 654 us -> 655 us (level)
    pallas_call x10 -> x11, Pallas kernels: 21.9 us -> 23.1 us  [whole_arrays(): pl.pallas_call(kernel, in_specs=specs, out_specs=pl.BlockSpec(shape, lamb...]
where the time goes in v13:
time: 655 us; the launch traced here: 646 us
  Pallas kernels  310 us (47%)
  waiting for transfers between devices  161 us (25%)
  starting transfers between devices  67.1 us (10%)
  local copies, waits for them, and re-layouts  42.2 us (6%)
  other arithmetic  35.9 us (5%)
  between operations  15.4 us (2%)
  matrix products  14.6 us (2%)
    ppermute x38, waiting for transfers between devices, swap(): return lax.ppermute(values, axis, [(i, i ^ bit) for i in range(size)])  142 us
    pallas_call x2, Pallas kernels, mlp_back(): pl.pallas_call(mlp_back_kernel, grid_spec=pltpu.PrefetchScalarGridSpec(nu...  72.2 us
    pallas_call x1, Pallas kernels, attend_back(): pl.pallas_call(attend_back_kernel, grid=(groups,), in_specs=[whole_spec(l...  45 us
    pallas_call x1, Pallas kernels, mlp(): pl.pallas_call(functools.partial(mlp_kernel, len(pieces)), grid_spec=pltp...  37.8 us
    ppermute x38, starting transfers between devices, swap(): return lax.ppermute(values, axis, [(i, i ^ bit) for i in range(size)])  37.3 us
    pallas_call x1, Pallas kernels, attend(): pl.pallas_call(attend_kernel, grid=(groups,), in_specs=[whole_spec(latent...  36.1 us
    pallas_call x6, Pallas kernels, sum_halves(): pl.pallas_call(sum_halves_kernel, grid=(kept.shape[0],), in_specs=[whole,...  31.6 us
    pallas_call x11, Pallas kernels, whole_arrays(): pl.pallas_call(kernel, in_specs=specs, out_specs=pl.BlockSpec(shape, lamb...  23.1 us
  transfers between devices with their start and end apart: 45, of which 18 were waited for; matrix products, arithmetic and copies ran while one was open for 11% of the time, Pallas kernels for 41%

profile of v13, /device:TPU:0, one launch (start us, length us, event | category | flops | bytes accessed | tf_op | source)
XLA Modules:
  0.0 645.9 jit_solution(17209639526487897128)
XLA Ops:
  12.5 5.6 gather_fusion.1
  19.3 2.5 copy.98
  24.3 4.1 collective-permute-start
  28.4 4.6 all-to-all-start
  47.5 13.2 %collective-permute-done = bf16[1,3,96,1152]{3,2,1,0:T(8,128)(2,1)} collective-permute-done((bf16[1,3,96,1152]{3,2,1,0:T(8,128)(2,1)S(1)}, bf16[1,3,96,1152]{3,2,1,0:T(8,128)(2,1)}, u32[]{:S(2)}, u32[]{:S(2)}) %collective-permute-start) | collective-permute-done | bytes 663584 | tf_op jit(solution)/shard_map/ppermute | solution.py:765
  60.7 2.3 pad_maximum_fusion.one_ref
  63.0 5.6 collective-permute-start.3
  70.8 27.7 %collective-permute-done.3.other_ref = s32[2,2,32]{2,1,0:T(2,128)S(1)} collective-permute-done((s32[2,2,32]{2,1,0:T(2,128)S(1)}, s32[2,2,32]{2,1,0:T(2,128)S(1)}, u32[]{:S(2)}, u32[]{:S(2)}) %collective-permute-start.3) | collective-permute-done | bytes 544 | tf_op jit(solution)/shard_map/ppermute | solution.py:765
  100.4 4.7 gather_fusion.3
  105.1 10.2 %collective-permute-done.1.other_ref = bf16[2,3,96,1152]{3,2,1,0:T(8,128)(2,1)} collective-permute-done((bf16[2,3,96,1152]{3,2,1,0:T(8,128)(2,1)}, bf16[2,3,96,1152]{3,2,1,0:T(8,128)(2,1)}, u32[]{:S(2)}, u32[]{:S(2)}) %collective-permute-start.1) | collective-permute-done | bytes 1327136 | tf_op jit(solution)/shard_map/ppermute | solution.py:765
  115.4 5.6 all-to-all-start.1
  120.9 3.4 append.14.refs_0_
  124.4 1.7 collective-permute-start.4
  126.1 2.0 fusion.58
  128.5 1.7 collective-permute-start.6
  130.2 1.9 collective-permute-start.15
  135.0 3.1 multiply_convert_fusion
  138.8 8.7 %modulate.1 = f32[6,16,1152]{2,1,0:T(8,128)} custom-call(bf16[16,1152]{1,0:T(8,128)(2,1)} %slice_select_fusion.silu_ref, bf16[6,1152,1152]{2,1,0:T(8,128)(2,1)} %bitcast.144), custom_call_target="tpu_custom_call" | custom-call | bytes 1024 | tf_op jit(solution)/shard_map/modulate/pallas_call | solution.py:427
  153.3 10.8 %collective-permute-done.9.refs_4_ = bf16[4,3,48,1152]{3,2,1,0:T(8,128)(2,1)} collective-permute-done((bf16[4,3,48,1152]{3,2,1,0:T(8,128)(2,1)S(1)}, bf16[4,3,48,1152]{3,2,1,0:T(8,128)(2,1)}, u32[]{:S(2)}, u32[]{:S(2)}) %collective-permute-start.9) | collective-permute-done | bytes 1327136 | tf_op jit(solution)/shard_map/ppermute | solution.py:765
  164.1 28.0 %collective-permute-done.15.refs_10_ = bf16[4,3,48,1152]{3,2,1,0:T(8,128)(2,1)} collective-permute-done((bf16[4,3,48,1152]{3,2,1,0:T(8,128)(2,1)S(1)}, bf16[4,3,48,1152]{3,2,1,0:T(8,128)(2,1)}, u32[]{:S(2)}, u32[]{:S(2)}) %collective-permute-start.15) | collective-permute-done | bytes 1327136 | tf_op jit(solution)/shard_map/ppermute | solution.py:765
  192.3 4.0 all-to-all-done.1.latent_ref
  199.2 4.7 all-to-all-start.2
  204.0 36.1 %attend.1 = (f32[4,864,1024]{2,1,0:T(8,128)}, bf16[4,288,1024]{2,1,0:T(8,128)(2,1)}, bf16[1024,1152]{1,0:T(8,128)(2,1)}, bf16[1152,1024]{1,0:T(8,128)(2,1)}, f32...) custom-call(bf16[4,4,64,1152]{3,2,1,0:T(8,128)(2,1)} %all-to-all-done.1.latent_ref, ...), custom_call_target="tpu_custom_call" | custom-call | flops 176000008192 | bytes 1024 | tf_op jit(solution)/shard_map/attend/pallas_call | solution.py:286
  243.5 2.0 collective-permute-done.13.refs_7_
  245.5 1.9 collective-permute-done.17.refs_13_
  247.4 37.8 %mlp.1 = (bf16[4,2,1024,768]{3,2,1,0:T(8,128)(2,1)}, f32[1024,1152]{1,0:T(8,128)}, bf16[4,3,768,1152]{3,2,1,0:T(8,128)(2,1)}) custom-call(s32[14]{0:T(128)} %stack.81.e_ref, bf16[1024,1152]{1,0:T(8,128)(2,1)} %get-tuple-element.153.x_ref, bf16[4,3,96,1152]{3,2,1,0:T(8,128)(2,1)} %append.14.refs_0_, bf16[4,3,96,1152]{3,2,1,0:T(8,128)(2,1)} %collective-permute-done.7.refs_1_, ...), custom_call_target="tpu_custom_call" | custom-call | flops 1100000000 | bytes 1024 | tf_op jit(solution)/shard_map/mlp/pallas_call | solution.py:479
  285.3 7.8 %finish.1 = (bf16[1024,1152]{1,0:T(8,128)(2,1)}, bf16[1152,1024]{1,0:T(8,128)(2,1)}, bf16[4,4,64,1152]{3,2,1,0:T(8,128)(2,1)}, f32[4,8,1152]{2,1,0:T(8,128)}) custom-call(f32[1024,1152]{1,0:T(8,128)} %get-tuple-element.162.branch_ref, f32[1024,1152]{1,0:T(8,128)} %get-tuple-element.163.middle_ref, bf16[4,4,64,1152]{3,2,1,0:T(8,128)(2,1)} %all-to-all-done.2.cot_ref, ...), custom_call_target="tpu_custom_call" | custom-call | flops 1100000000 | bytes 1024 | tf_op jit(solution)/shard_map/finish/pallas_call | solution.py:409
  293.0 36.2 %mlp_back.2 = (bf16[2,3,576,768]{3,2,1,0:T(8,128)(2,1)}, bf16[2,3,576,768]{3,2,1,0:T(8,128)(2,1)}, f32[1024,1152]{1,0:T(8,128)}) custom-call(s32[8]{0:T(128)} %broadcast_xor_fusion.2.e_ref, bf16[8,144,1024]{2,1,0:T(8,128)(2,1)} %bitcast.174, bf16[8,144,1024]{2,1,0:T(8,128)(2,1)} %bitcast.168, bf16[1024,1152]{1,0:T(8,128)(2,1)} %get-tuple-element.166.low_ref, ...), custom_call_target="tpu_custom_call" | custom-call | flops 165000003584 | bytes 1024 | tf_op jit(solution)/shard_map/mlp_back/pallas_call | solution.py:555
  329.4 36.0 %mlp_back.3 = (bf16[2,3,576,768]{3,2,1,0:T(8,128)(2,1)}, bf16[2,3,576,768]{3,2,1,0:T(8,128)(2,1)}, f32[1024,1152]{1,0:T(8,128)}) custom-call(s32[8]{0:T(128)} %broadcast_xor_fusion.1.e_ref, bf16[8,144,1024]{2,1,0:T(8,128)(2,1)} %bitcast.175, bf16[8,144,1024]{2,1,0:T(8,128)(2,1)} %bitcast.169, bf16[1024,1152]{1,0:T(8,128)(2,1)} %get-tuple-element.166.low_ref, ...), custom_call_target="tpu_custom_call" | custom-call | flops 165000003584 | bytes 1024 | tf_op jit(solution)/shard_map/mlp_back/pallas_call | solution.py:555
  365.7 5.3 all-to-all-start.3
  371.0 7.6 %sum_halves.7 = (bf16[6,288,768]{2,1,0:T(8,128)(2,1)}, bf16[6,288,768]{2,1,0:T(8,128)(2,1)}) custom-call(bf16[6,576,768]{2,1,0:T(8,128)(2,1)} %bitcast.151, bf16[6,576,768]{2,1,0:T(8,128)(2,1)} %bitcast.52.got_ref), custom_call_target="tpu_custom_call" | custom-call | bytes 1024 | tf_op jit(solution)/shard_map/sum_halves/pallas_call | solution.py:794
  378.6 7.6 %sum_halves.6 = (bf16[6,288,768]{2,1,0:T(8,128)(2,1)}, bf16[6,288,768]{2,1,0:T(8,128)(2,1)}) custom-call(bf16[6,576,768]{2,1,0:T(8,128)(2,1)} %bitcast.150, bf16[6,576,768]{2,1,0:T(8,128)(2,1)} %bitcast.49.got_ref), custom_call_target="tpu_custom_call" | custom-call | bytes 1024 | tf_op jit(solution)/shard_map/sum_halves/pallas_call | solution.py:794
  387.4 11.1 %middle.1 = (f32[1024,1152]{1,0:T(8,128)}, bf16[1024,1152]{1,0:T(8,128)(2,1)}, bf16[1152,1024]{1,0:T(8,128)(2,1)}, f32[4,8,1152]{2,1,0:T(8,128)}) custom-call(f32[1024,1152]{1,0:T(8,128)} %get-tuple-element.178.one_ref, f32[1024,1152]{1,0:T(8,128)} %get-tuple-element.179.other_ref, f32[1024,1152]{1,0:T(8,128)} %get-tuple-element.163.middle_ref, ...), custom_call_target="tpu_custom_call" | custom-call | flops 109999996928 | bytes 1024 | tf_op jit(solution)/shard_map/middle/pallas_call | solution.py:409
  398.5 45.0 %attend_back.1 = (bf16[4,864,1024]{2,1,0:T(8,128)(2,1)}, f32[2,72,256]{2,1,0:T(8,128)}, f32[4,8,1152]{2,1,0:T(8,128)}, bf16[4,4,64,1152]{3,2,1,0:T(8,128)(2,1)}) custom-call(bf16[4,4,64,1152]{3,2,1,0:T(8,128)(2,1)} %all-to-all-done.1.latent_ref, f32[4,864,1024]{2,1,0:T(8,128)} %get-tuple-element.177.proj_ref, bf16[1024,1152]{1,0:T(8,128)(2,1)} %get-tuple-element.181.low_ref, ...), custom_call_target="tpu_custom_call" | custom-call | flops 1100000000 | bytes 1024 | tf_op jit(solution)/shard_map/attend_back/pallas_call | solution.py:330
  446.3 2.9 collective-permute-start.22
  449.3 4.8 all-to-all-start.4
  454.1 5.6 sum_halves.8
  459.7 5.6 sum_halves.9
  469.7 2.0 collective-permute-start.25
  472.8 21.4 %attend_grads.1 = (bf16[4,576,1152]{2,1,0:T(8,128)(2,1)}, bf16[4,576,1152]{2,1,0:T(8,128)(2,1)}) custom-call(s32[4]{0:T(128)} %broadcast_xor_fusion.m_ref, s32[16]{0:T(128)} %pad_add_fusion.e_ref, bf16[8,144,1024]{2,1,0:T(8,128)(2,1)} %bitcast.154, bf16[8,144,1024]{2,1,0:T(8,128)(2,1)} %bitcast.155, bf16[4,864,1024]{2,1,0:T(8,128)(2,1)} %get-tuple-element.201.proj_ref, ...), custom_call_target="tpu_custom_call" | custom-call | bytes 1024 | tf_op jit(solution)/shard_map/attend_grads/pallas_call | solution.py:608
  494.6 12.5 %all-to-all-done.4 = bf16[4,4,64,1152]{3,2,1,0:T(8,128)(2,1)} async-done(((bf16[4,4,64,1152]{3,2,1,0:T(8,128)(2,1)}), bf16[4,4,64,1152]{3,2,1,0:T(8,128)(2,1)}, u32[]{:S(2)}, u32[]{:S(2)}) %all-to-all-start.4) | async-done | bytes 2359328 | tf_op jit(solution)/shard_map/all_to_all | solution.py:870
  507.1 2.1 append.16.one_ref
  510.7 7.6 %sum_quarters.1 = (bf16[2,288,1152]{2,1,0:T(8,128)(2,1)}, bf16[2,288,1152]{2,1,0:T(8,128)(2,1)}, bf16[2,288,1152]{2,1,0:T(8,128)(2,1)}, bf16[2,288,1152]{2,1,0:T(8,128)(2,1)}) custom-call(bf16[4,576,1152]{2,1,0:T(8,128)(2,1)} %get-tuple-element.211.kept_ref, bf16[4,576,1152]{2,1,0:T(8,128)(2,1)} %collective-permute-done.26.got_ref), custom_call_target="tpu_custom_call" | custom-call | bytes 1024 | tf_op jit(solution)/shard_map/sum_quarters/pallas_call | solution.py:719
  520.4 7.7 %take_rows.1 = bf16[32,64,1152]{2,1,0:T(8,128)(2,1)} custom-call(s32[32]{0:T(128)} %get-tuple-element.143.index_ref, bf16[16,64,1152]{2,1,0:T(8,128)(2,1)} %bitcast.67.refs_0_.refs_1_.refs_2_.refs_3_, bf16[16,64,1152]{2,1,0:T(8,128)(2,1)} %bitcast.67.refs_0_.refs_1_.refs_2_.refs_3_, bf16[16,64,1152]{2,1,0:T(8,128)(2,1)} %bitcast.67.refs_0_.refs_1_.refs_2_.refs_3_, ...), custom_call_target="tpu_custom_call" | custom-call | flops 219999993856 | bytes 1024 | tf_op jit(solution)/shard_map/take_rows/pallas_call | solution.py:678
  528.1 3.3 copy_result.1
  531.4 2.0 append.17.one_ref
  533.9 2.7 add_convert_fusion.1
  536.6 1.6 add_convert_fusion.2
  538.2 10.2 %collective-permute-done.29.got_ref = bf16[2,288,1152]{2,1,0:T(8,128)(2,1)} collective-permute-done((bf16[2,288,1152]{2,1,0:T(8,128)(2,1)}, bf16[2,288,1152]{2,1,0:T(8,128)(2,1)}, u32[]{:S(2)}, u32[]{:S(2)}) %collective-permute-start.29) | collective-permute-done | bytes 1327136 | tf_op jit(solution)/shard_map/ppermute | solution.py:765
  548.5 2.6 sum_halves.11
  551.3 2.6 sum_halves.10
  555.4 5.9 collective-permute-done.30.other_ref
  562.1 2.3 append.18.one_ref
  566.1 4.9 all-to-all-start.5
  571.1 2.1 add_convert_fusion.5
  577.6 3.2 append.19
  581.8 1.9 copy.95
  583.8 2.4 fusion.12
  586.2 2.3 fusion.28
  589.3 10.1 %collective-permute-done.34 = bf16[2,144,1152]{2,1,0:T(8,128)(2,1)} collective-permute-done((bf16[2,144,1152]{2,1,0:T(8,128)(2,1)}, bf16[2,144,1152]{2,1,0:T(8,128)(2,1)}, u32[]{:S(2)}, u32[]{:S(2)}) %collective-permute-start.34) | collective-permute-done | bytes 663584 | tf_op jit(solution)/shard_map/ppermute | solution.py:765
  599.4 1.7 add_convert_fusion.4
  603.1 20.6 %collective-permute-done.35 = bf16[1,144,1152]{2,1,0:T(8,128)(2,1)S(1)} collective-permute-done((bf16[1,144,1152]{2,1,0:T(8,128)(2,1)S(1)}, bf16[1,144,1152]{2,1,0:T(8,128)(2,1)S(1)}, u32[]{:S(2)}, u32[]{:S(2)}) %collective-permute-start.35) | collective-permute-done | bytes 331808 | tf_op jit(solution)/shard_map/ppermute | solution.py:765
  631.0 1.8 all-to-all-done.5
  632.8 5.7 gather_fusion.8
  (298 shorter events, 77.6 us)
Async XLA Ops:
  7.2 27.1 %copy-start = (bf16[1152,3,288]{0,2,1:T(8,128)(2,1)S(1)}, bf16[1152,3,288]{0,2,1:T(8,128)(2,1)}, u32[]{:S(2)}) copy-start(bf16[1152,3,288]{0,2,1:T(8,128)(2,1)} %param.36) | copy-start | bytes 5971972
  24.3 36.4 %collective-permute-start = (bf16[1,3,96,1152]{3,2,1,0:T(8,128)(2,1)S(1)}, bf16[1,3,96,1152]{3,2,1,0:T(8,128)(2,1)}, u32[]{:S(2)}, u32[]{:S(2)}) collective-permute-start(bf16[1,3,96,1152]{3,2,1,0:T(8,128)(2,1)S(1)} %maximum_bitcast_fusion), channel_id=1, source_target_pairs={{0,2},{1,3},{2,0},{3,1},{4,6},{5,7},{6,4},{7,5},{8,10},{9,11},{10,... | collective-permute-start | bytes 1990664 | tf_op jit(solution)/shard_map/ppermute | solution.py:765
  28.4 17.3 %collective-permute-start.2 = (s32[1,2,32]{2,1,0:T(2,128)S(1)}, s32[1,2,32]{2,1,0:T(2,128)S(1)}, u32[]{:S(2)}, u32[]{:S(2)}) collective-permute-start(s32[1,2,32]{2,1,0:T(2,128)S(1)} %bitcast.164), channel_id=1, source_target_pairs={{0,4},{4,0},{8,12},{12,8},{16,20},{20,16},{24,28},{28,24},{1,5},{5... | collective-permute-start | bytes 776 | tf_op jit(solution)/shard_map/ppermute | solution.py:765
  28.4 72.1 %all-to-all-start = ((bf16[32,64,1152]{2,1,0:T(8,128)(2,1)}), bf16[32,64,1152]{2,1,0:T(8,128)(2,1)}, u32[]{:S(2)}, u32[]{:S(2)}) async-start(bf16[32,64,1152]{2,1,0:T(8,128)(2,1)} %gather_fusion.1), calls=%async_computation | async-start | bytes 9437184 | tf_op jit(solution)/shard_map/all_to_all | solution.py:887
  33.0 171.0 %all-gather.3.cloned.1.call-start = ((), (), s32[]{:S(2)}) async-start(), calls=%async_computation.6 | async-start | bytes 10948608 | tf_op jit(solution)/shard_map/all_gather | solution.py:641
  47.5 15.5 %copy-start.35 = (s32[2,2,32]{2,1,0:T(2,128)S(1)}, s32[2,2,32]{2,1,0:T(2,128)}, u32[]{:S(2)}) copy-start(s32[2,2,32]{2,1,0:T(2,128)} %append.11.one_ref) | copy-start | bytes 1540
  63.0 35.6 %collective-permute-start.3 = (s32[2,2,32]{2,1,0:T(2,128)S(1)}, s32[2,2,32]{2,1,0:T(2,128)S(1)}, u32[]{:S(2)}, u32[]{:S(2)}) collective-permute-start(s32[2,2,32]{2,1,0:T(2,128)S(1)} %copy-done.35), channel_id=1, source_target_pairs={{0,8},{4,12},{8,0},{12,4},{16,24},{20,28},{24,16},{28,20},{1,9},{5... | collective-permute-start | bytes 1544 | tf_op jit(solution)/shard_map/ppermute | solution.py:765
  70.3 45.1 %collective-permute-start.1 = (bf16[2,3,96,1152]{3,2,1,0:T(8,128)(2,1)}, bf16[2,3,96,1152]{3,2,1,0:T(8,128)(2,1)}, u32[]{:S(2)}, u32[]{:S(2)}) collective-permute-start(bf16[2,3,96,1152]{3,2,1,0:T(8,128)(2,1)} %pad_maximum_fusion.one_ref), channel_id=1, source_target_pairs={{0,1},{1,0},{2,3},{3,2},{4,5},{5,4},{6,7},{7,6},{8,9},{9,8},{10,11... | collective-permute-start | bytes 3981320 | tf_op jit(solution)/shard_map/ppermute | solution.py:765
  115.4 80.9 %all-to-all-start.1 = ((bf16[4,4,64,1152]{3,2,1,0:T(8,128)(2,1)}), bf16[4,4,64,1152]{3,2,1,0:T(8,128)(2,1)}, u32[]{:S(2)}, u32[]{:S(2)}) async-start(bf16[4,4,64,1152]{3,2,1,0:T(8,128)(2,1)} %bitcast.149), calls=%async_computation.1 | async-start | bytes 4718592 | tf_op jit(solution)/shard_map/all_to_all | solution.py:870
  124.3 68.0 %collective-permute-start.7 = (bf16[4,3,96,1152]{3,2,1,0:T(8,128)(2,1)}, bf16[4,3,96,1152]{3,2,1,0:T(8,128)(2,1)}, u32[]{:S(2)}, u32[]{:S(2)}) collective-permute-start(bf16[4,3,96,1152]{3,2,1,0:T(8,128)(2,1)} %append.14.refs_0_), channel_id=1, source_target_pairs={{0,4},{4,0},{8,12},{12,8},{16,20},{20,16},{24,28},{28,24},{1,5},{5... | collective-permute-start | bytes 7962632 | tf_op jit(solution)/shard_map/ppermute | solution.py:765
  124.4 5.9 collective-permute-start.4
  128.1 64.1 %collective-permute-start.5 = (bf16[4,3,48,1152]{3,2,1,0:T(8,128)(2,1)S(1)}, bf16[4,3,48,1152]{3,2,1,0:T(8,128)(2,1)}, u32[]{:S(2)}, u32[]{:S(2)}) collective-permute-start(bf16[4,3,48,1152]{3,2,1,0:T(8,128)(2,1)S(1)} %get-tuple-element.295), channel_id=1, source_target_pairs={{0,8},{4,12},{8,0},{12,4},{16,24},{20,28},{24,16},{28,20},{1,9},{5... | collective-permute-start | bytes 3981320 | tf_op jit(solution)/shard_map/ppermute | solution.py:765
  128.2 36.0 %collective-permute-start.9 = (bf16[4,3,48,1152]{3,2,1,0:T(8,128)(2,1)S(1)}, bf16[4,3,48,1152]{3,2,1,0:T(8,128)(2,1)}, u32[]{:S(2)}, u32[]{:S(2)}) collective-permute-start(bf16[4,3,48,1152]{3,2,1,0:T(8,128)(2,1)S(1)} %get-tuple-element.295), channel_id=1, source_target_pairs={{0,16},{4,20},{8,24},{12,28},{16,0},{20,4},{24,8},{28,12},{1,17},{... | collective-permute-start | bytes 3981320 | tf_op jit(solution)/shard_map/ppermute | solution.py:765
  128.5 63.8 %collective-permute-start.6 = (bf16[4,3,48,1152]{3,2,1,0:T(8,128)(2,1)S(1)}, bf16[4,3,48,1152]{3,2,1,0:T(8,128)(2,1)}, u32[]{:S(2)}, u32[]{:S(2)}) collective-permute-start(bf16[4,3,48,1152]{3,2,1,0:T(8,128)(2,1)S(1)} %get-tuple-element.294), channel_id=1, source_target_pairs={{0,16},{4,20},{8,24},{12,28},{16,0},{20,4},{24,8},{28,12},{1,17},{... | collective-permute-start | bytes 3981320 | tf_op jit(solution)/shard_map/ppermute | solution.py:765
  130.2 61.9 %collective-permute-start.15 = (bf16[4,3,48,1152]{3,2,1,0:T(8,128)(2,1)S(1)}, bf16[4,3,48,1152]{3,2,1,0:T(8,128)(2,1)}, u32[]{:S(2)}, u32[]{:S(2)}) collective-permute-start(bf16[4,3,48,1152]{3,2,1,0:T(8,128)(2,1)S(1)} %get-tuple-element.294), channel_id=1, source_target_pairs={{0,8},{4,12},{8,0},{12,4},{16,24},{20,28},{24,16},{28,20},{1,9},{5... | collective-permute-start | bytes 3981320 | tf_op jit(solution)/shard_map/ppermute | solution.py:765
  134.7 13.9 %copy-start.26 = (s32[128]{0:T(128)}, s32[128]{0:T(128)S(1)}, u32[]{:S(2)}) copy-start(s32[128]{0:T(128)S(1)} %get-tuple-element.293) | copy-start | bytes 1540
  138.8 11.6 %copy-start.6 = (s32[8]{0:T(128)S(1)}, s32[8]{0:T(128)}, u32[]{:S(2)}) copy-start(s32[8]{0:T(128)} %param.31) | copy-start | bytes 100
  138.8 12.4 %copy-start.7 = (s32[8]{0:T(128)S(1)}, s32[8]{0:T(128)}, u32[]{:S(2)}) copy-start(s32[8]{0:T(128)} %param.32) | copy-start | bytes 100
  164.1 76.6 %collective-permute-start.10 = (bf16[4,3,48,1152]{3,2,1,0:T(8,128)(2,1)}, bf16[4,3,48,1152]{3,2,1,0:T(8,128)(2,1)}, u32[]{:S(2)}, u32[]{:S(2)}) collective-permute-start(bf16[4,3,48,1152]{3,2,1,0:T(8,128)(2,1)} %collective-permute-done.9.refs_4_), channel_id=1, source_target_pairs={{0,4},{4,0},{8,12},{12,8},{16,20},{20,16},{24,28},{28,24},{1,5},{5... | collective-permute-start | bytes 3981320 | tf_op jit(solution)/shard_map/ppermute | solution.py:765
  192.2 50.5 %collective-permute-start.16 = (bf16[4,3,48,1152]{3,2,1,0:T(8,128)(2,1)}, bf16[4,3,48,1152]{3,2,1,0:T(8,128)(2,1)}, u32[]{:S(2)}, u32[]{:S(2)}) collective-permute-start(bf16[4,3,48,1152]{3,2,1,0:T(8,128)(2,1)} %collective-permute-done.15.refs_10_), channel_id=1, source_target_pairs={{0,4},{4,0},{8,12},{12,8},{16,20},{20,16},{24,28},{28,24},{1,5},{5... | collective-permute-start | bytes 3981320 | tf_op jit(solution)/shard_map/ppermute | solution.py:765
  196.3 44.2 %collective-permute-start.12 = (bf16[4,3,48,1152]{3,2,1,0:T(8,128)(2,1)}, bf16[4,3,48,1152]{3,2,1,0:T(8,128)(2,1)}, u32[]{:S(2)}, u32[]{:S(2)}) collective-permute-start(bf16[4,3,48,1152]{3,2,1,0:T(8,128)(2,1)} %collective-permute-done.6.refs_8_), channel_id=1, source_target_pairs={{0,8},{4,12},{8,0},{12,4},{16,24},{20,28},{24,16},{28,20},{1,9},{5... | collective-permute-start | bytes 3981320 | tf_op jit(solution)/shard_map/ppermute | solution.py:765
  197.7 45.0 %collective-permute-start.14 = (bf16[4,3,48,1152]{3,2,1,0:T(8,128)(2,1)}, bf16[4,3,48,1152]{3,2,1,0:T(8,128)(2,1)}, u32[]{:S(2)}, u32[]{:S(2)}) collective-permute-start(bf16[4,3,48,1152]{3,2,1,0:T(8,128)(2,1)} %collective-permute-done.6.refs_8_), channel_id=1, source_target_pairs={{0,4},{4,0},{8,12},{12,8},{16,20},{20,16},{24,28},{28,24},{1,5},{5... | collective-permute-start | bytes 3981320 | tf_op jit(solution)/shard_map/ppermute | solution.py:765
  197.7 42.4 %collective-permute-start.11 = (bf16[4,3,48,1152]{3,2,1,0:T(8,128)(2,1)}, bf16[4,3,48,1152]{3,2,1,0:T(8,128)(2,1)}, u32[]{:S(2)}, u32[]{:S(2)}) collective-permute-start(bf16[4,3,48,1152]{3,2,1,0:T(8,128)(2,1)} %collective-permute-done.5.refs_2_), channel_id=1, source_target_pairs={{0,16},{4,20},{8,24},{12,28},{16,0},{20,4},{24,8},{28,12},{1,17},{... | collective-permute-start | bytes 3981320 | tf_op jit(solution)/shard_map/ppermute | solution.py:765
  199.2 86.0 %all-to-all-start.2 = ((bf16[4,4,64,1152]{3,2,1,0:T(8,128)(2,1)}), bf16[4,4,64,1152]{3,2,1,0:T(8,128)(2,1)}, u32[]{:S(2)}, u32[]{:S(2)}) async-start(bf16[4,4,64,1152]{3,2,1,0:T(8,128)(2,1)} %bitcast.156), calls=%async_computation.2 | async-start | bytes 4718592 | tf_op jit(solution)/shard_map/all_to_all | solution.py:870
  204.0 37.7 %copy-start.50 = (s32[8]{0:T(128)S(1)}, s32[8]{0:T(128)}, u32[]{:S(2)}) copy-start(s32[8]{0:T(128)} %constant.213.clone) | copy-start | bytes 100
  204.0 38.2 %copy-start.49 = (s32[8]{0:T(128)S(1)}, s32[8]{0:T(128)}, u32[]{:S(2)}) copy-start(s32[8]{0:T(128)} %constant.214.clone) | copy-start | bytes 100
  240.2 3.3 collective-permute-start.8
  240.4 5.1 collective-permute-start.13
  240.7 6.7 %collective-permute-start.17 = (bf16[4,3,48,1152]{3,2,1,0:T(8,128)(2,1)}, bf16[4,3,48,1152]{3,2,1,0:T(8,128)(2,1)}, u32[]{:S(2)}, u32[]{:S(2)}) collective-permute-start(bf16[4,3,48,1152]{3,2,1,0:T(8,128)(2,1)} %collective-permute-done.12.refs_12_), channel_id=1, source_target_pairs={{0,4},{4,0},{8,12},{12,8},{16,20},{20,16},{24,28},{28,24},{1,5},{5... | collective-permute-start | bytes 3981320 | tf_op jit(solution)/shard_map/ppermute | solution.py:765
  329.2 41.8 %collective-permute-start.19 = (bf16[2,3,576,768]{3,2,1,0:T(8,128)(2,1)}, bf16[2,3,576,768]{3,2,1,0:T(8,128)(2,1)}, u32[]{:S(2)}, u32[]{:S(2)}) collective-permute-start(bf16[2,3,576,768]{3,2,1,0:T(8,128)(2,1)} %get-tuple-element.174), channel_id=1, source_target_pairs={{0,4},{4,0},{8,12},{12,8},{16,20},{20,16},{24,28},{28,24},{1,5},{5... | collective-permute-start | bytes 15925256 | tf_op jit(solution)/shard_map/ppermute | solution.py:765
  365.4 13.2 %collective-permute-start.18 = (bf16[2,3,576,768]{3,2,1,0:T(8,128)(2,1)}, bf16[2,3,576,768]{3,2,1,0:T(8,128)(2,1)}, u32[]{:S(2)}, u32[]{:S(2)}) collective-permute-start(bf16[2,3,576,768]{3,2,1,0:T(8,128)(2,1)} %get-tuple-element.171), channel_id=1, source_target_pairs={{0,4},{4,0},{8,12},{12,8},{16,20},{20,16},{24,28},{28,24},{1,5},{5... | collective-permute-start | bytes 15925256 | tf_op jit(solution)/shard_map/ppermute | solution.py:765
  365.7 83.5 %all-to-all-start.3 = ((bf16[4,4,64,1152]{3,2,1,0:T(8,128)(2,1)}), bf16[4,4,64,1152]{3,2,1,0:T(8,128)(2,1)}, u32[]{:S(2)}, u32[]{:S(2)}) async-start(bf16[4,4,64,1152]{3,2,1,0:T(8,128)(2,1)} %get-tuple-element.198), calls=%async_computation.3 | async-start | bytes 4718592 | tf_op jit(solution)/shard_map/all_to_all | solution.py:870
  386.3 63.0 %collective-permute-start.21 = (bf16[2,3,288,768]{3,2,1,0:T(8,128)(2,1)}, bf16[2,3,288,768]{3,2,1,0:T(8,128)(2,1)}, u32[]{:S(2)}, u32[]{:S(2)}) collective-permute-start(bf16[2,3,288,768]{3,2,1,0:T(8,128)(2,1)} %bitcast.166), channel_id=1, source_target_pairs={{0,8},{4,12},{8,0},{12,4},{16,24},{20,28},{24,16},{28,20},{1,9},{5... | collective-permute-start | bytes 7962632 | tf_op jit(solution)/shard_map/ppermute | solution.py:765
  386.8 62.5 %collective-permute-start.20 = (bf16[2,3,288,768]{3,2,1,0:T(8,128)(2,1)}, bf16[2,3,288,768]{3,2,1,0:T(8,128)(2,1)}, u32[]{:S(2)}, u32[]{:S(2)}) collective-permute-start(bf16[2,3,288,768]{3,2,1,0:T(8,128)(2,1)} %bitcast.167), channel_id=1, source_target_pairs={{0,16},{4,20},{8,24},{12,28},{16,0},{20,4},{24,8},{28,12},{1,17},{... | collective-permute-start | bytes 7962632 | tf_op jit(solution)/shard_map/ppermute | solution.py:765
  398.5 46.0 %copy-start.32 = (f32[2]{0:T(128)S(1)}, f32[2]{0:T(128)}, u32[]{:S(2)}) copy-start(f32[2]{0:T(128)} %constant.221) | copy-start | bytes 28
  398.5 46.2 %copy-start.21 = (f32[4,8,1152]{2,1,0:T(8,128)S(1)}, f32[4,8,1152]{2,1,0:T(8,128)}, u32[]{:S(2)}) copy-start(f32[4,8,1152]{2,1,0:T(8,128)} %get-tuple-element.189) | copy-start | bytes 442372
  398.5 46.2 %copy-start.22 = (f32[4,8,1152]{2,1,0:T(8,128)S(1)}, f32[4,8,1152]{2,1,0:T(8,128)}, u32[]{:S(2)}) copy-start(f32[4,8,1152]{2,1,0:T(8,128)} %get-tuple-element.190) | copy-start | bytes 442372
  446.3 13.3 %collective-permute-start.22 = (bf16[1,4,8,1152]{3,2,1,0:T(8,128)(2,1)}, bf16[1,4,8,1152]{3,2,1,0:T(8,128)(2,1)}, u32[]{:S(2)}, u32[]{:S(2)}) collective-permute-start(bf16[1,4,8,1152]{3,2,1,0:T(8,128)(2,1)} %fusion.32.one_ref), channel_id=1, source_target_pairs={{0,2},{1,3},{2,0},{3,1},{4,6},{5,7},{6,4},{7,5},{8,10},{9,11},{10,... | collective-permute-start | bytes 221192 | tf_op jit(solution)/shard_map/ppermute | solution.py:765
  449.3 57.8 %all-to-all-start.4 = ((bf16[4,4,64,1152]{3,2,1,0:T(8,128)(2,1)}), bf16[4,4,64,1152]{3,2,1,0:T(8,128)(2,1)}, u32[]{:S(2)}, u32[]{:S(2)}) async-start(bf16[4,4,64,1152]{3,2,1,0:T(8,128)(2,1)} %get-tuple-element.206), calls=%async_computation.4 | async-start | bytes 4718592 | tf_op jit(solution)/shard_map/all_to_all | solution.py:870
  459.6 12.1 %copy-start.48 = (s32[4]{0:T(128)S(1)}, s32[4]{0:T(128)}, u32[]{:S(2)}) copy-start(s32[4]{0:T(128)} %constant.215.clone) | copy-start | bytes 52
  459.6 12.6 %copy-start.51 = (s32[8]{0:T(128)S(1)}, s32[8]{0:T(128)}, u32[]{:S(2)}) copy-start(s32[8]{0:T(128)} %broadcast_xor_fusion.2.e_ref) | copy-start | bytes 100
  459.7 12.6 %copy-start.52 = (s32[8]{0:T(128)S(1)}, s32[8]{0:T(128)}, u32[]{:S(2)}) copy-start(s32[8]{0:T(128)} %broadcast_xor_fusion.1.e_ref) | copy-start | bytes 100
  465.3 41.8 %collective-permute-start.24 = (bf16[2,3,144,768]{3,2,1,0:T(8,128)(2,1)}, bf16[2,3,144,768]{3,2,1,0:T(8,128)(2,1)S(1)}, u32[]{:S(2)}, u32[]{:S(2)}) collective-permute-start(bf16[2,3,144,768]{3,2,1,0:T(8,128)(2,1)} %bitcast.171), channel_id=1, source_target_pairs={{0,16},{4,20},{8,24},{12,28},{16,0},{20,4},{24,8},{28,12},{1,17},{... | collective-permute-start | bytes 3981320 | tf_op jit(solution)/shard_map/ppermute | solution.py:765
  466.7 40.4 %collective-permute-start.23 = (bf16[2,3,144,768]{3,2,1,0:T(8,128)(2,1)}, bf16[2,3,144,768]{3,2,1,0:T(8,128)(2,1)S(1)}, u32[]{:S(2)}, u32[]{:S(2)}) collective-permute-start(bf16[2,3,144,768]{3,2,1,0:T(8,128)(2,1)} %bitcast.170), channel_id=1, source_target_pairs={{0,8},{4,12},{8,0},{12,4},{16,24},{20,28},{24,16},{28,20},{1,9},{5... | collective-permute-start | bytes 3981320 | tf_op jit(solution)/shard_map/ppermute | solution.py:765
  469.7 24.8 %collective-permute-start.25 = (bf16[2,4,8,1152]{3,2,1,0:T(8,128)(2,1)}, bf16[2,4,8,1152]{3,2,1,0:T(8,128)(2,1)S(1)}, u32[]{:S(2)}, u32[]{:S(2)}) collective-permute-start(bf16[2,4,8,1152]{3,2,1,0:T(8,128)(2,1)} %append.15.one_ref), channel_id=1, source_target_pairs={{0,1},{1,0},{2,3},{3,2},{4,5},{5,4},{6,7},{7,6},{8,9},{9,8},{10,11... | collective-permute-start | bytes 442376 | tf_op jit(solution)/shard_map/ppermute | solution.py:765
  494.2 16.5 %collective-permute-start.26 = (bf16[4,576,1152]{2,1,0:T(8,128)(2,1)}, bf16[4,576,1152]{2,1,0:T(8,128)(2,1)}, u32[]{:S(2)}, u32[]{:S(2)}) collective-permute-start(bf16[4,576,1152]{2,1,0:T(8,128)(2,1)} %get-tuple-element.212), channel_id=1, source_target_pairs={{0,4},{4,0},{8,12},{12,8},{16,20},{20,16},{24,28},{28,24},{1,5},{5... | collective-permute-start | bytes 15925256 | tf_op jit(solution)/shard_map/ppermute | solution.py:765
  494.6 12.5 %copy-start.46 = (bf16[2,4,8,1152]{3,2,1,0:T(8,128)(2,1)}, bf16[2,4,8,1152]{3,2,1,0:T(8,128)(2,1)S(1)}, u32[]{:S(2)}) copy-start(bf16[2,4,8,1152]{3,2,1,0:T(8,128)(2,1)S(1)} %collective-permute-done.25.other_ref) | copy-start | bytes 442372
  509.2 22.2 %collective-permute-start.28 = (bf16[4,4,8,1152]{3,2,1,0:T(8,128)(2,1)}, bf16[4,4,8,1152]{3,2,1,0:T(8,128)(2,1)}, u32[]{:S(2)}, u32[]{:S(2)}) collective-permute-start(bf16[4,4,8,1152]{3,2,1,0:T(8,128)(2,1)} %append.16.one_ref), channel_id=1, source_target_pairs={{0,8},{4,12},{8,0},{12,4},{16,24},{20,28},{24,16},{28,20},{1,9},{5... | collective-permute-start | bytes 884744 | tf_op jit(solution)/shard_map/ppermute | solution.py:765
  518.3 30.1 %collective-permute-start.29 = (bf16[2,288,1152]{2,1,0:T(8,128)(2,1)}, bf16[2,288,1152]{2,1,0:T(8,128)(2,1)}, u32[]{:S(2)}, u32[]{:S(2)}) collective-permute-start(bf16[2,288,1152]{2,1,0:T(8,128)(2,1)} %get-tuple-element.231), channel_id=1, source_target_pairs={{0,8},{4,12},{8,0},{12,4},{16,24},{20,28},{24,16},{28,20},{1,9},{5... | collective-permute-start | bytes 3981320 | tf_op jit(solution)/shard_map/ppermute | solution.py:765
  518.9 32.4 %collective-permute-start.27 = (bf16[2,288,1152]{2,1,0:T(8,128)(2,1)}, bf16[2,288,1152]{2,1,0:T(8,128)(2,1)}, u32[]{:S(2)}, u32[]{:S(2)}) collective-permute-start(bf16[2,288,1152]{2,1,0:T(8,128)(2,1)} %get-tuple-element.227), channel_id=1, source_target_pairs={{0,16},{4,20},{8,24},{12,28},{16,0},{20,4},{24,8},{28,12},{1,17},{... | collective-permute-start | bytes 3981320 | tf_op jit(solution)/shard_map/ppermute | solution.py:765
  533.4 27.8 %collective-permute-start.30 = (bf16[8,4,8,1152]{3,2,1,0:T(8,128)(2,1)}, bf16[8,4,8,1152]{3,2,1,0:T(8,128)(2,1)S(1)}, u32[]{:S(2)}, u32[]{:S(2)}) collective-permute-start(bf16[8,4,8,1152]{3,2,1,0:T(8,128)(2,1)} %append.17.one_ref), channel_id=1, source_target_pairs={{0,16},{4,20},{8,24},{12,28},{16,0},{20,4},{24,8},{28,12},{1,17},{... | collective-permute-start | bytes 1769480 | tf_op jit(solution)/shard_map/ppermute | solution.py:765
  536.6 37.7 %collective-permute-start.36 = (bf16[2,3,144,768]{3,2,1,0:T(8,128)(2,1)}, bf16[2,3,144,768]{3,2,1,0:T(8,128)(2,1)}, u32[]{:S(2)}, u32[]{:S(2)}) collective-permute-start(bf16[2,3,144,768]{3,2,1,0:T(8,128)(2,1)} %add_convert_fusion.1), channel_id=1, source_target_pairs={{0,1},{1,0},{2,3},{3,2},{4,5},{5,4},{6,7},{7,6},{8,9},{9,8},{10,11... | collective-permute-start | bytes 3981320 | tf_op jit(solution)/shard_map/ppermute | solution.py:765
  551.1 13.3 %copy-start.34 = (s32[72]{0:T(128)S(1)}, s32[72]{0:T(128)}, u32[]{:S(2)}) copy-start(s32[72]{0:T(128)} %constant.222) | copy-start | bytes 868
  551.1 13.4 %copy-start.45 = (s32[32]{0:T(128)S(1)}, s32[32]{0:T(128)}, u32[]{:S(2)}) copy-start(s32[32]{0:T(128)} %get-tuple-element.236) | copy-start | bytes 388
  553.9 17.2 %collective-permute-start.33 = (bf16[2,144,1152]{2,1,0:T(8,128)(2,1)}, bf16[2,144,1152]{2,1,0:T(8,128)(2,1)}, u32[]{:S(2)}, u32[]{:S(2)}) collective-permute-start(bf16[2,144,1152]{2,1,0:T(8,128)(2,1)} %get-tuple-element.246), channel_id=1, source_target_pairs={{0,8},{4,12},{8,0},{12,4},{16,24},{20,28},{24,16},{28,20},{1,9},{5... | collective-permute-start | bytes 1990664 | tf_op jit(solution)/shard_map/ppermute | solution.py:765
  564.4 8.7 %collective-permute-start.31 = (bf16[16,4,8,1152]{3,2,1,0:T(8,128)(2,1)}, bf16[16,4,8,1152]{3,2,1,0:T(8,128)(2,1)S(1)}, u32[]{:S(2)}, u32[]{:S(2)}) collective-permute-start(bf16[16,4,8,1152]{3,2,1,0:T(8,128)(2,1)} %append.18.one_ref), channel_id=1, source_target_pairs={{0,4},{4,0},{8,12},{12,8},{16,20},{20,16},{24,28},{28,24},{1,5},{5... | collective-permute-start | bytes 3538952 | tf_op jit(solution)/shard_map/ppermute | solution.py:765
  564.6 24.7 %collective-permute-start.32 = (bf16[2,144,1152]{2,1,0:T(8,128)(2,1)}, bf16[2,144,1152]{2,1,0:T(8,128)(2,1)}, u32[]{:S(2)}, u32[]{:S(2)}) collective-permute-start(bf16[2,144,1152]{2,1,0:T(8,128)(2,1)} %get-tuple-element.244), channel_id=1, source_target_pairs={{0,16},{4,20},{8,24},{12,28},{16,0},{20,4},{24,8},{28,12},{1,17},{... | collective-permute-start | bytes 1990664 | tf_op jit(solution)/shard_map/ppermute | solution.py:765
  566.1 66.7 %all-to-all-start.5 = ((bf16[32,64,1152]{2,1,0:T(8,128)(2,1)}), bf16[32,64,1152]{2,1,0:T(8,128)(2,1)}, u32[]{:S(2)}, u32[]{:S(2)}) async-start(bf16[32,64,1152]{2,1,0:T(8,128)(2,1)} %take_rows.1), calls=%async_computation.5 | async-start | bytes 9437184 | tf_op jit(solution)/shard_map/all_to_all | solution.py:1126
  573.1 26.3 %collective-permute-start.34 = (bf16[2,144,1152]{2,1,0:T(8,128)(2,1)}, bf16[2,144,1152]{2,1,0:T(8,128)(2,1)}, u32[]{:S(2)}, u32[]{:S(2)}) collective-permute-start(bf16[2,144,1152]{2,1,0:T(8,128)(2,1)} %add_convert_fusion.5), channel_id=1, source_target_pairs={{0,1},{1,0},{2,3},{3,2},{4,5},{5,4},{6,7},{7,6},{8,9},{9,8},{10,11... | collective-permute-start | bytes 1990664 | tf_op jit(solution)/shard_map/ppermute | solution.py:765
  576.8 50.5 %collective-permute-start.37 = (bf16[1,3,144,768]{3,2,1,0:T(8,128)(2,1)}, bf16[1,3,144,768]{3,2,1,0:T(8,128)(2,1)}, u32[]{:S(2)}, u32[]{:S(2)}) collective-permute-start(bf16[1,3,144,768]{3,2,1,0:T(8,128)(2,1)} %slice.144), channel_id=1, source_target_pairs={{0,2},{1,3},{2,0},{3,1},{4,6},{5,7},{6,4},{7,5},{8,10},{9,11},{10,... | collective-permute-start | bytes 1990664 | tf_op jit(solution)/shard_map/ppermute | solution.py:765
  586.2 13.2 %copy-start.18 = (bf16[2,144,1152]{2,1,0:T(8,128)(2,1)S(1)}, bf16[2,144,1152]{2,1,0:T(8,128)(2,1)}, u32[]{:S(2)}) copy-start(bf16[2,144,1152]{2,1,0:T(8,128)(2,1)} %get-tuple-element.243) | copy-start | bytes 1990660
  588.6 13.4 %copy-start.39 = (s32[128]{0:T(128)S(1)}, s32[128]{0:T(128)}, u32[]{:S(2)}) copy-start(s32[128]{0:T(128)} %copy-done.38) | copy-start | bytes 1540
  599.4 24.3 %copy-start.10 = (f32[864,864]{1,0:T(8,128)S(1)}, f32[864,864]{1,0:T(8,128)}, u32[]{:S(2)}) copy-start(f32[864,864]{1,0:T(8,128)} %constant.217.clone) | copy-start | bytes 8957956
  601.2 22.4 %collective-permute-start.35 = (bf16[1,144,1152]{2,1,0:T(8,128)(2,1)S(1)}, bf16[1,144,1152]{2,1,0:T(8,128)(2,1)S(1)}, u32[]{:S(2)}, u32[]{:S(2)}) collective-permute-start(bf16[1,144,1152]{2,1,0:T(8,128)(2,1)S(1)} %slice.139), channel_id=1, source_target_pairs={{0,2},{1,3},{2,0},{3,1},{4,6},{5,7},{6,4},{7,5},{8,10},{9,11},{10,... | collective-permute-start | bytes 995336 | tf_op jit(solution)/shard_map/ppermute | solution.py:765
  (39 other events, 200.8 us)
Sparse Core Ops, SparseCore 0:
  37.3 134.1 all-gather.2
